TPU v7x, 32 devices: a whole 2x2x4 slice. The times are simulated.
32 devices in a mesh: groups: 2 (over y), ep: 4 (over z), tp: 2 (over x), sub: 2 (over core).
Axes of the slice: x: 2, y: 2, z: 4, core: 2. Of those that a mesh axis runs over, the one named last changes fastest.
Arguments:
- queries: bfloat16 [2048, 4096], P(('groups', 'ep', 'sub'), 'tp'), parts along dimension 0, may hold values from -8 to 8
- key_rows: bfloat16 [2048, 512], P(('groups', 'ep', 'sub'), 'tp'), parts along dimension 0, may hold values from -5 to 5
- value_rows: bfloat16 [2048, 512], P(('groups', 'ep', 'sub'), 'tp'), parts along dimension 0, may hold values from -12 to 12
- sink_logits: float32 [64], P('tp'), may hold values from 2 to 6
- out_weight: bfloat16 [4096, 2880], P('tp', 'ep'), may hold values from -0.09375 to 0.09375
- residual: bfloat16 [2048, 2880], P(('groups', 'ep', 'sub')), parts along dimension 0, may hold values from -12 to 12
- norm_gain: float32 [2880], replicated, may hold values from 0.1 to 1.9
- expert_in: bfloat16 [8, 2, 2880, 1440], P(('ep', 'sub'), None, None, 'tp'), may hold values from -0.109375 to 0.109375
- expert_out: bfloat16 [8, 1440, 2880], P(('ep', 'sub'), None, 'tp'), may hold values from -0.15625 to 0.15625
- routes: int32 [2048, 4], P(('groups', 'ep', 'sub')), parts along dimension 0, may hold values from 0 to 7, all different within a row; in each aligned block of 128 rows (0 to 127, 128 to 255, ...) at most 128 rows name the same one
- route_scores: int32 [2048, 4], P(('groups', 'ep', 'sub')), parts along dimension 0, may hold values from 1 to 1023
Outputs:
- mixed_out: bfloat16 [2048, 2880], P(('groups', 'ep', 'sub'), 'tp'), parts along dimension 0
There are 2 independent parts, one for each index of `groups`. A program takes and returns all parts, laid end to end along the dimension named above; an argument that names none is the same for every part. Nothing has to cross between parts.
Inputs may be any that keep to these rules, and one draw needn't show every extreme that they name: `routes`: each row names 4 different experts. Within the 128 rows of one index of ep+sub no expert is named by more than 128 rows, a bound that some block reaches of them.
All inputs are finite; a program needn't handle non-finite values.
Results may differ from a plain program's by a relative error of at most 0.0044.
Values may be sent and summed in bfloat16 or wider, within the bound.
No kernel may reach another device: no remote copies, remote signals or barrier semaphores. Data moves between devices by JAX's collectives and lax.ppermute only.
A program may use at most 128 MiB of HBM per device.

v0:
```python
import jax
import jax.numpy as jnp
from jax import lax
from jax.sharding import PartitionSpec as P

D = 2880
HD = 64
WIN = 128
TOP = 4


def shifted(block, axis, distance):
    devices = range(lax.axis_size(axis))
    route = [(i - distance, i) for i in devices if i - distance in devices]
    return lax.ppermute(block, axis, route)


def expert_rows(flat_rows, expert_in, expert_out):
    gate_up = jnp.einsum("rd,kdf->rkf", flat_rows, expert_in[0], preferred_element_type=jnp.float32)
    gate_part = gate_up[:, 0]
    up_part = gate_up[:, 1]
    activated = ((up_part + 1.0) * gate_part * jax.nn.sigmoid(1.702 * gate_part)).astype(
        jnp.bfloat16
    )
    all_units = lax.all_gather(activated, "tp", axis=1, tiled=True)
    return jnp.dot(all_units, expert_out[0], preferred_element_type=jnp.float32).astype(
        jnp.bfloat16
    )


def serve_rows(arrived, expert_in, expert_out):
    source_count = arrived.shape[0]
    item_count = arrived.shape[1]
    finished = expert_rows(
        arrived.reshape(source_count * item_count, arrived.shape[2]), expert_in, expert_out
    )
    finished = finished.reshape(source_count, item_count, finished.shape[1])
    return lax.all_to_all(finished, ("ep", "sub"), split_axis=0, concat_axis=0, tiled=True)


def local(
    queries,
    key_rows,
    value_rows,
    sink_logits,
    out_weight,
    residual,
    norm_gain,
    expert_in,
    expert_out,
    routes,
    route_scores,
):
    row_count = queries.shape[0]
    head_count = queries.shape[1] // HD
    kv_count = key_rows.shape[1] // HD
    group_size = head_count // kv_count
    window_reach = WIN - 1
    kv_width = kv_count * HD
    paired = jnp.concatenate([key_rows, value_rows], axis=1)
    earlier = shifted(paired[row_count - window_reach :], ("ep", "sub"), 1)
    context = jnp.concatenate([earlier, paired], axis=0)
    key_part = context[:, :kv_width].reshape(row_count + window_reach, kv_count, HD)
    value_part = context[:, kv_width:].reshape(row_count + window_reach, kv_count, HD)
    query_rows = queries.reshape(row_count, kv_count, group_size, HD)
    scores = jnp.einsum(
        "pgqd,jgd->gqpj", query_rows, key_part, preferred_element_type=jnp.float32
    ) * HD ** (-0.5)
    query_pos = jnp.arange(row_count, dtype=jnp.int32)[:, None]
    key_pos = jnp.arange(row_count + window_reach, dtype=jnp.int32)[None, :]
    first_device = lax.axis_index(("ep", "sub")) == 0
    allowed = (key_pos >= query_pos) & (key_pos <= query_pos + window_reach)
    allowed = allowed & jnp.logical_or(jnp.logical_not(first_device), key_pos >= window_reach)
    sink_table = sink_logits.reshape(kv_count, group_size)
    masked = jnp.where(allowed, scores, -1e30)
    largest = jnp.maximum(jnp.max(masked, axis=3), sink_table[:, :, None])
    numerator = jnp.where(allowed, jnp.exp(masked - largest[..., None]), 0.0)
    denominator = jnp.sum(numerator, axis=3) + jnp.exp(sink_table[:, :, None] - largest)
    weights = (numerator / denominator[..., None]).astype(jnp.bfloat16)
    attended = jnp.einsum("gqpj,jgd->pgqd", weights, value_part, preferred_element_type=jnp.float32)
    attended = attended.reshape(row_count, head_count * HD).astype(jnp.bfloat16)
    partial_value = jnp.dot(
        attended,
        lax.all_gather(out_weight, "ep", axis=1, tiled=True),
        preferred_element_type=jnp.float32,
    )
    feature_count = expert_out.shape[2]
    column = lax.axis_index("tp") * feature_count
    hidden = residual.astype(jnp.float32) + lax.psum(partial_value, "tp")
    square = jnp.sum(hidden * hidden, axis=1, keepdims=True)
    normed = (hidden * lax.rsqrt(square / D + 1e-05) * norm_gain).astype(jnp.bfloat16)
    own_hidden = lax.dynamic_slice_in_dim(hidden, column, feature_count, 1)
    expert_count = lax.axis_size(("ep", "sub"))
    capacity = 2 * row_count * TOP // expert_count
    flat_routes = routes.reshape(-1)
    one_hot = (flat_routes[:, None] == jnp.arange(expert_count, dtype=jnp.int32)[None, :]).astype(
        jnp.int32
    )
    before = jnp.cumsum(one_hot, axis=0) - one_hot
    placed = jnp.sum(before * one_hot, axis=1) + flat_routes * capacity
    owner_row = jnp.arange(row_count * TOP, dtype=jnp.int32) // TOP
    source = jnp.zeros((expert_count * capacity,), jnp.int32).at[placed].set(owner_row)
    outgoing = jnp.take(normed, source, axis=0).reshape(expert_count, capacity, normed.shape[1])
    returned = serve_rows(
        lax.all_to_all(outgoing, ("ep", "sub"), split_axis=0, concat_axis=0, tiled=True),
        expert_in,
        expert_out,
    )
    flat_results = returned.reshape(expert_count * capacity, feature_count)
    picked = (
        jnp.take(flat_results, placed, axis=0)
        .astype(jnp.float32)
        .reshape(row_count, TOP, feature_count)
    )
    route_float = route_scores.astype(jnp.float32)
    mix_share = route_float / jnp.sum(route_float, axis=1, keepdims=True)
    expert_sum = jnp.einsum("tk,tkd->td", mix_share, picked)
    return (own_hidden + expert_sum).astype(jnp.bfloat16)


def solution(mesh):
    in_specs = (
        P(("groups", "ep", "sub"), "tp"),
        P(("groups", "ep", "sub"), "tp"),
        P(("groups", "ep", "sub"), "tp"),
        P("tp"),
        P("tp", "ep"),
        P(("groups", "ep", "sub"), None),
        P(),
        P(("ep", "sub"), None, None, "tp"),
        P(("ep", "sub"), None, "tp"),
        P(("groups", "ep", "sub"), None),
        P(("groups", "ep", "sub"), None),
    )
    out_specs = P(("groups", "ep", "sub"), "tp")
    return jax.shard_map(local, mesh=mesh, in_specs=in_specs, out_specs=out_specs, check_vma=False)
```

profile of v0, /device:TPU:0, one launch (start us, length us, event | category | flops | bytes accessed | tf_op | source)
XLA Modules:
  0.0 617.5 jit_solution(5010792642916383126)
XLA Ops:
  6.5 0.7 all-gather.4.cloned.1.call-update
  7.3 0.8 constant_dynamic-update-slice_fusion.1
  8.1 0.8 constant_dynamic-update-slice_fusion
  9.0 2.4 collective-permute-start
  11.4 1.3 copy.44
  12.8 0.1 fusion.22
  13.0 0.1 copy.43
  13.1 0.1 copy.42
  13.2 0.8 fusion.7
  14.0 1.1 fusion.8
  15.2 1.3 fusion.19
  16.5 200.5 %all-gather.4.cloned.1.call-done = bf16[2048,2880]{0,1:T(8,128)(2,1)} async-done(((bf16[2048,720]{0,1:T(8,128)(2,1)}), bf16[2048,2880]{0,1:T(8,128)(2,1)}) %all-gather.4.cloned.1.call-update) | async-done | bytes 11796496 | tf_op jit(solution)/shard_map/all_gather | solution.py:84
  217.0 7.3 %fusion.35 = f32[128,2880]{0,1:T(8,128)} fusion(bf16[2048,2880]{0,1:T(8,128)(2,1)} %all-gather.4.cloned.1.call-done, bf16[128,2048]{0,1:T(8,128)(2,1)S(1)} %bitcast.77), kind=kOutput, calls=%fused_computation.72 | convolution fusion | flops 1509949440 | bytes 13795328 | tf_op jit(solution)/shard_map/dot_general | solution.py:82
  224.4 0.1 copy.46
  224.6 0.1 eq.33
  224.7 0.1 eq.29
  224.8 1.1 reduce-window.6
  225.9 0.2 slice_reduce_fusion
  226.2 0.1 copy.50
  226.3 0.1 mul.80
  226.5 2.4 scatter_custom_fusion
  229.0 43.1 %all-reduce.2.cloned.1.call-done = f32[128,2880]{0,1:T(8,128)} async-done(((f32[128,2880]{0,1:T(8,128)}), f32[128,2880]{0,1:T(8,128)}) %all-reduce.2.cloned.1.call-update) | async-done | bytes 1474576 | tf_op jit(solution)/shard_map/psum | solution.py:89
  272.1 1.8 multiply_reduce_fusion.1
  273.9 1.2 copy-done
  275.0 0.4 multiply_convert_fusion
  275.5 0.3 copy.51
  275.8 6.5 %gather_fusion = bf16[1024,2880]{1,0:T(8,128)(2,1)} fusion(bf16[128,2880]{1,0:T(8,128)(2,1)S(1)} %copy.51, s32[1024]{0:T(1024)S(1)} %fusion.26), kind=kCustom, calls=%fused_computation | custom fusion | bytes 11800576 | tf_op jit(solution)/shard_map/jit(_take)/gather | solution.py:103
  282.4 8.4 %copy.52 = bf16[8,128,2880]{1,2,0:T(8,128)(2,1)} copy(bf16[8,128,2880]{2,1,0:T(8,128)(2,1)} %bitcast.70) | data formatting | bytes 11796480 | tf_op jit(solution)/shard_map/jit(_take)/gather | solution.py:103
  290.8 3.2 broadcast_select_fusion
  294.0 135.0 %all_to_all.10 = bf16[8,128,2880]{1,2,0:T(8,128)(2,1)S(1)} all-to-all(bf16[8,128,2880]{1,2,0:T(8,128)(2,1)S(1)} %broadcast_select_fusion), channel_id=1, replica_groups=mesh['groups'=2,'ep'=4,'tp'=2,'sub'=2] {'ep','sub'}, dimensions={0} | all-to-all | bytes 11796480 | tf_op jit(solution)/shard_map/all_to_all | solution.py:105
  429.1 18.0 %copy.53 = bf16[8,128,2880]{1,0,2:T(8,128)(2,1)} copy(bf16[8,128,2880]{1,2,0:T(8,128)(2,1)S(1)} %all_to_all.10) | data formatting | bytes 11796480 | tf_op jit(solution)/shard_map/all_to_all | solution.py:105
  447.1 9.9 %reshape.173 = bf16[1024,2880,1]{0,1,2:T(8,128)(2,1)} reshape(bf16[8,128,2880]{1,0,2:T(8,128)(2,1)} %copy.53) | data formatting | bytes 11796480 | tf_op jit(solution)/shard_map/reshape | solution.py:35
  457.0 13.7 %fusion = f32[1024,2,720]{0,2,1:T(8,128)S(1)} fusion(bf16[1024,2880,1]{0,1,2:T(8,128)(2,1)} %reshape.173, bf16[1,2,2880,720]{2,3,1,0:T(8,128)(2,1)} %param.18), kind=kOutput, calls=%fused_computation.3 | convolution fusion | flops 8493465600 | bytes 20090880 | tf_op jit(solution)/shard_map/rd,kdf->rkf/dot_general | solution.py:19
  470.7 2.0 fusion.11
  472.7 40.7 %all-gather.6.cloned.1.call-done = bf16[1024,1,1440]{0,2,1:T(8,128)(2,1)} async-done(((bf16[1024,1,720]{0,2,1:T(8,128)(2,1)}), bf16[1024,1,1440]{0,2,1:T(8,128)(2,1)}) %all-gather.6.cloned.1.call-update) | async-done | bytes 2949136 | tf_op jit(solution)/shard_map/all_gather | solution.py:25
  513.4 7.9 %fusion.14 = bf16[180,8,8,128]{3,2,1,0:T(8,128)(2,1)S(1)} fusion(bf16[1,1440,1440]{2,1,0:T(8,128)(2,1)} %param.19, bf16[1024,1,1440]{0,2,1:T(8,128)(2,1)} %all-gather.6.cloned.1.call-done), kind=kOutput, calls=%fused_computation.22 | convolution fusion | flops 4248207360 | bytes 10045440 | tf_op jit(solution)/shard_map/dot_general | solution.py:26
  521.3 2.1 copy.66
  523.5 4.7 all-to-all-start.1
  528.2 0.1 reduce_sum.43
  528.4 0.1 copy.49
  528.6 0.1 copy.63
  528.7 66.9 %all-to-all-done.1 = bf16[8,128,1440]{1,2,0:T(8,128)(2,1)} async-done(((bf16[8,128,1440]{1,2,0:T(8,128)(2,1)}), bf16[8,128,1440]{1,2,0:T(8,128)(2,1)}, u32[]{:S(2)}, u32[]{:S(2)}) %all-to-all-start.1) | async-done | bytes 2949152 | tf_op jit(solution)/shard_map/all_to_all | solution.py:38
  595.6 3.1 copy.55
  598.8 3.0 gather_fusion.1
  601.8 3.0 gather.15
  604.8 4.0 multiply_reduce_fusion
  608.8 1.4 copy.62
  610.2 0.8 add_convert_fusion
  (41 shorter events, 0.7 us)
Async XLA Ops:
  6.5 6.2 %copy-start.6 = (f32[32]{0:T(128)S(1)}, f32[32]{0:T(128)}, u32[]{:S(2)}) copy-start(f32[32]{0:T(128)} %param.14) | copy-start | bytes 388
  6.5 210.5 %all-gather.4.cloned.1.call-start = ((), (), s32[]{:S(2)}) async-start(), calls=%async_computation.2 | async-start | bytes 14745600 | tf_op jit(solution)/shard_map/all_gather | solution.py:84
  7.3 264.8 %all-reduce.2.cloned.1.call-start = ((), (), s32[]{:S(2)}) async-start(), calls=%async_computation.3 | async-start | bytes 2949120 | tf_op jit(solution)/shard_map/psum | solution.py:89
  9.0 3.9 collective-permute-start
  217.0 7.4 %copy-start.3 = (s32[128,4]{0,1:T(4,128)S(1)}, s32[128,4]{0,1:T(4,128)}, u32[]{:S(2)}) copy-start(s32[128,4]{0,1:T(4,128)} %param.20) | copy-start | bytes 6148
  217.0 55.1 %copy-start.2 = (bf16[128,2880]{0,1:T(8,128)(2,1)S(1)}, bf16[128,2880]{0,1:T(8,128)(2,1)}, u32[]{:S(2)}) copy-start(bf16[128,2880]{0,1:T(8,128)(2,1)} %param.16) | copy-start | bytes 2211844
  224.4 50.7 %copy-start.4 = (f32[2880]{0:T(1024)S(1)}, f32[2880]{0:T(1024)}, u32[]{:S(2)}) copy-start(f32[2880]{0:T(1024)} %param.17) | copy-start | bytes 34564
  224.4 289.0 %all-gather.6.cloned.1.call-start = ((), (), s32[]{:S(2)}) async-start(), calls=%async_computation.4 | async-start | bytes 4423680 | tf_op jit(solution)/shard_map/all_gather | solution.py:25
  273.9 1.2 copy-start
  523.5 5.1 copy-start.5
  523.5 72.2 %all-to-all-start.1 = ((bf16[8,128,1440]{1,2,0:T(8,128)(2,1)}), bf16[8,128,1440]{1,2,0:T(8,128)(2,1)}, u32[]{:S(2)}, u32[]{:S(2)}) async-start(bf16[8,128,1440]{1,2,0:T(8,128)(2,1)} %bitcast.68), calls=%async_computation.1 | async-start | bytes 5898240 | tf_op jit(solution)/shard_map/all_to_all | solution.py:38
  601.7 8.4 %copy-start.1 = (f32[128,2880]{0,1:T(8,128)S(1)}, f32[128,2880]{0,1:T(8,128)}, u32[]{:S(2)}) copy-start(f32[128,2880]{0,1:T(8,128)} %copy-done) | copy-start | bytes 4423684
Sparse Core Ops, SparseCore 0:
  8.9 208.0 all-gather.3
  224.5 47.5 all-reduce.1
  472.8 40.5 all-gather.5
where the time goes:
time: 619 us; the launch traced here: 618 us
  waiting for transfers between devices  352 us (57%)
  blocking collectives  135 us (22%)
  local copies, waits for them, and re-layouts  64.1 us (10%)
  matrix products  31 us (5%)
  other arithmetic  14.9 us (2%)
  between operations  13.4 us (2%)
  starting transfers between devices  7.18 us (1%)
    all_gather x1, waiting for transfers between devices, local(): lax.all_gather(out_weight, 'ep', axis=1, tiled=True)  201 us
    all_to_all x1, blocking collectives, local(): lax.all_to_all(outgoing, ('ep', 'sub'), split_axis=0, concat_axis=0, tile...  135 us
    all_to_all x1, waiting for transfers between devices, serve_rows(): lax.all_to_all(finished, ('ep', 'sub'), split_axis=0, concat_axis=0, tile...  66.9 us
    psum x1, waiting for transfers between devices, local(): hidden = residual.astype(jnp.float32) + lax.psum(partial_value, 'tp')  43.1 us
    all_gather x1, waiting for transfers between devices, expert_rows(): all_units = lax.all_gather(activated, 'tp', axis=1, tiled=True)  40.7 us
    all_to_all x1, local copies, waits for them, and re-layouts, local(): lax.all_to_all(outgoing, ('ep', 'sub'), split_axis=0, concat_axis=0, tile...  18 us
    gather x2, local copies, waits for them, and re-layouts, local(): jnp.take(normed, source, axis=0)  15 us
    dot_general x1, matrix products, expert_rows(): jnp.einsum('rd,kdf->rkf', flat_rows, expert_in[0], preferred_element_type...  13.7 us
  transfers between devices with their start and end apart: 5, of which 4 were waited for; matrix products, arithmetic and copies ran while one was open for 2% of the time, Pallas kernels for 0%

commit v1 on v0

v1 whole, which is shorter than its diff:
```python
import jax
import jax.numpy as jnp
from jax import lax
from jax.sharding import PartitionSpec as P

D = 2880
HD = 64
WIN = 128
TOP = 4


def shifted(block, axis, distance):
    devices = range(lax.axis_size(axis))
    route = [(i - distance, i) for i in devices if i - distance in devices]
    return lax.ppermute(block, axis, route)


def rotated(block, axis, distance):
    count = lax.axis_size(axis)
    return lax.ppermute(block, axis, [(i, (i + distance) % count) for i in range(count)])


def picked(blocks, index, axis):
    return lax.dynamic_index_in_dim(blocks, index, axis, keepdims=False)


def attention(queries, key_rows, value_rows, sink_logits):
    row_count = queries.shape[0]
    head_count = queries.shape[1] // HD
    kv_count = key_rows.shape[1] // HD
    group_size = head_count // kv_count
    window_reach = WIN - 1
    kv_width = kv_count * HD
    paired = jnp.concatenate([key_rows, value_rows], axis=1)
    earlier = shifted(paired[row_count - window_reach :], ("ep", "sub"), 1)
    context = jnp.concatenate([earlier, paired], axis=0)
    key_part = context[:, :kv_width].reshape(row_count + window_reach, kv_count, HD)
    value_part = context[:, kv_width:].reshape(row_count + window_reach, kv_count, HD)
    query_rows = queries.reshape(row_count, kv_count, group_size, HD)
    scores = jnp.einsum(
        "pgqd,jgd->gqpj", query_rows, key_part, preferred_element_type=jnp.float32
    ) * HD ** (-0.5)
    query_pos = jnp.arange(row_count, dtype=jnp.int32)[:, None]
    key_pos = jnp.arange(row_count + window_reach, dtype=jnp.int32)[None, :]
    first_device = lax.axis_index(("ep", "sub")) == 0
    allowed = (key_pos >= query_pos) & (key_pos <= query_pos + window_reach)
    allowed = allowed & jnp.logical_or(jnp.logical_not(first_device), key_pos >= window_reach)
    sink_table = sink_logits.reshape(kv_count, group_size)
    masked = jnp.where(allowed, scores, -1e30)
    largest = jnp.maximum(jnp.max(masked, axis=3), sink_table[:, :, None])
    numerator = jnp.where(allowed, jnp.exp(masked - largest[..., None]), 0.0)
    denominator = jnp.sum(numerator, axis=3) + jnp.exp(sink_table[:, :, None] - largest)
    weights = (numerator / denominator[..., None]).astype(jnp.bfloat16)
    attended = jnp.einsum("gqpj,jgd->pgqd", weights, value_part, preferred_element_type=jnp.float32)
    return attended.reshape(row_count, head_count * HD).astype(jnp.bfloat16)


def activation(rows, scale, expert_in):
    gate = jnp.dot(rows, expert_in[0, 0], preferred_element_type=jnp.float32) * scale
    up = jnp.dot(rows, expert_in[0, 1], preferred_element_type=jnp.float32) * scale
    return ((up + 1.0) * gate * jax.nn.sigmoid(1.702 * gate)).astype(jnp.bfloat16)


def local(
    queries,
    key_rows,
    value_rows,
    sink_logits,
    out_weight,
    residual,
    norm_gain,
    expert_in,
    expert_out,
    routes,
    route_scores,
):
    row_count = queries.shape[0]
    z_count, t_count, s_count = lax.axis_size("ep"), lax.axis_size("tp"), lax.axis_size("sub")
    z, t, s = lax.axis_index("ep"), lax.axis_index("tp"), lax.axis_index("sub")
    part_rows = row_count // t_count
    columns = out_weight.shape[1]
    units = expert_in.shape[3]
    width = expert_out.shape[2]

    experts_in = [expert_in] + [rotated(expert_in, "sub", k) for k in range(1, s_count)]
    experts_out = [expert_out] + [rotated(expert_out, "sub", k) for k in range(1, s_count)]
    experts_out = [
        [lax.dynamic_slice_in_dim(w[0], ((t - m) % t_count) * units, units, 0) for m in range(t_count)]
        for w in experts_out
    ]

    own_residual = picked(residual.reshape(t_count, part_rows, z_count, columns), t, 0)
    residual_parts = [picked(own_residual, z, 1)] + [
        rotated(picked(own_residual, (z + k) % z_count, 1), "ep", k) for k in range(1, z_count)
    ]
    order = (z - jnp.arange(z_count, dtype=jnp.int32)) % z_count
    residual_part = jnp.take(jnp.stack(residual_parts), order, axis=0)

    expert_count = z_count * s_count
    route_float = route_scores.astype(jnp.float32)
    mix_share = route_float / jnp.sum(route_float, axis=1, keepdims=True)
    named = routes[:, :, None] == jnp.arange(expert_count, dtype=jnp.int32)[None, None, :]
    share_table = jnp.sum(jnp.where(named, mix_share[:, :, None], 0.0), axis=1)
    share_table = lax.all_gather(share_table, "ep", axis=0)
    share_table = share_table.reshape(z_count, t_count, part_rows, z_count, s_count)
    share_table = picked(share_table, z, 3)

    attended = attention(queries, key_rows, value_rows, sink_logits)
    gathered = lax.all_gather(attended, "ep", axis=0, tiled=True)
    partial_value = jnp.dot(gathered, out_weight, preferred_element_type=jnp.float32)
    partial_value = partial_value.reshape(z_count, t_count, part_rows, columns)
    hidden = residual_part.astype(jnp.float32) + picked(partial_value, t, 1)
    for m in range(1, t_count):
        sent = picked(partial_value, (t + m) % t_count, 1).astype(jnp.bfloat16)
        hidden = hidden + rotated(sent, "tp", m).astype(jnp.float32)

    gain_part = lax.dynamic_slice_in_dim(norm_gain, z * columns, columns, 0)
    scaled = (hidden * gain_part).astype(jnp.bfloat16).reshape(z_count * part_rows, columns)
    rows = lax.all_gather(scaled, "ep", axis=1, tiled=True)
    row_sets = [rows] + [rotated(rows, "tp", m) for m in range(1, t_count)]

    inverse_gain = 1.0 / norm_gain
    activated = []
    for rows in row_sets:
        plain = rows.astype(jnp.float32) * inverse_gain
        square = jnp.sum(plain * plain, axis=1, keepdims=True)
        scale = lax.rsqrt(square / D + 1e-05)
        activated.append([activation(rows, scale, w) for w in experts_in])

    outputs = []
    for k in range(t_count):
        total = 0.0
        for e in range(s_count):
            result = 0.0
            for m in range(t_count):
                block = activated[(k - m) % t_count][e]
                if m:
                    block = rotated(block, "tp", m)
                result = result + jnp.dot(
                    block, experts_out[e][m], preferred_element_type=jnp.float32
                )
            share = picked(picked(share_table, (t - k) % t_count, 1), (s - e) % s_count, 2)
            result = result.astype(jnp.bfloat16).astype(jnp.float32)
            total = total + share.reshape(-1, 1) * result
        total = total.astype(jnp.bfloat16).reshape(z_count, part_rows, width)
        final = picked(total, z, 0).astype(jnp.float32)
        for n in range(1, z_count):
            final = final + rotated(picked(total, (z + n) % z_count, 0), "ep", n).astype(jnp.float32)
        own = picked(row_sets[k].reshape(z_count, part_rows, D), z, 0)
        own = lax.dynamic_slice_in_dim(own, t * width, width, 1).astype(jnp.float32)
        own = own * lax.dynamic_slice_in_dim(inverse_gain, t * width, width, 0)
        outputs.append((own + final).astype(jnp.bfloat16))
    order = (t - jnp.arange(t_count, dtype=jnp.int32)) % t_count
    return jnp.take(jnp.stack(outputs), order, axis=0).reshape(row_count, width)


def solution(mesh):
    in_specs = (
        P(("groups", "ep", "sub"), "tp"),
        P(("groups", "ep", "sub"), "tp"),
        P(("groups", "ep", "sub"), "tp"),
        P("tp"),
        P("tp", "ep"),
        P(("groups", "ep", "sub"), None),
        P(),
        P(("ep", "sub"), None, None, "tp"),
        P(("ep", "sub"), None, "tp"),
        P(("groups", "ep", "sub"), None),
        P(("groups", "ep", "sub"), None),
    )
    out_specs = P(("groups", "ep", "sub"), "tp")
    return jax.shard_map(local, mesh=mesh, in_specs=in_specs, out_specs=out_specs, check_vma=False)
```

time: 619 us -> 268 us (0.43)
  waiting for transfers between devices: 352 us -> 110 us
  blocking collectives: 135 us -> 13.1 us
  local copies, waits for them, and re-layouts: 64.1 us -> 38.2 us
  matrix products: 31 us -> 53.4 us
  starting transfers between devices: 7.18 us -> 28 us
    all_gather x2, waiting for transfers between devices: 241 us -> 77.9 us  [the longest x1 42.1 us: local(): gathered = lax.all_gather(attended, 'ep', axis=0, tiled=True)]
    all_to_all x1 -> x0, blocking collectives: 135 us -> none  [local(): lax.all_to_all(outgoing, ('ep', 'sub'), split_axis=0, concat_axis=0, tile...]
    all_to_all x1 -> x0, waiting for transfers between devices: 66.9 us -> none  [serve_rows(): lax.all_to_all(finished, ('ep', 'sub'), split_axis=0, concat_axis=0, tile...]
    psum x1 -> x0, waiting for transfers between devices: 43.1 us -> none  [local(): hidden = residual.astype(jnp.float32) + lax.psum(partial_value, 'tp')]
    ppermute x0 -> x17, waiting for transfers between devices: none -> 31.9 us  [rotated(): lax.ppermute(block, axis, [(i, (i + distance) % count) for i in range(cou...]
    ppermute x0 -> x17, starting transfers between devices: none -> 25 us  [rotated(): lax.ppermute(block, axis, [(i, (i + distance) % count) for i in range(cou...]
    dot_general x5 -> x19, matrix products: 31 us -> 53.4 us  [the longest x8 19.3 us: local(): jnp.dot(block, experts_out[e][m], preferred_element_type=jnp.float32)]
    all_to_all x2 -> x0, local copies, waits for them, and re-layouts: 21.1 us -> none  [the longest x1 18 us: local(): lax.all_to_all(outgoing, ('ep', 'sub'), split_axis=0, concat_axis=0, tile...]
  transfers between devices with their start and end apart: 5 -> 20, of which waited for: 4 -> 6; matrix products, arithmetic and copies ran while one was open for 2% -> 30% of each run, Pallas kernels for 0% -> 0%
where the time goes in v1:
time: 268 us; the launch traced here: 267 us
  waiting for transfers between devices  110 us (41%)
  matrix products  53.4 us (20%)
  local copies, waits for them, and re-layouts  38.2 us (14%)
  starting transfers between devices  28 us (10%)
  between operations  14 us (5%)
  blocking collectives  13.1 us (5%)
  other arithmetic  10.1 us (4%)
    all_gather x1, waiting for transfers between devices, local(): gathered = lax.all_gather(attended, 'ep', axis=0, tiled=True)  42.1 us
    all_gather x1, waiting for transfers between devices, local(): rows = lax.all_gather(scaled, 'ep', axis=1, tiled=True)  35.8 us
    ppermute x17, waiting for transfers between devices, rotated(): lax.ppermute(block, axis, [(i, (i + distance) % count) for i in range(cou...  31.9 us
    ppermute x17, starting transfers between devices, rotated(): lax.ppermute(block, axis, [(i, (i + distance) % count) for i in range(cou...  25 us
    dot_general x8, matrix products, local(): jnp.dot(block, experts_out[e][m], preferred_element_type=jnp.float32)  19.3 us
    all_gather x1, blocking collectives, local(): share_table = lax.all_gather(share_table, 'ep', axis=0)  13.1 us
    dot_general x4, matrix products, activation(): jnp.dot(rows, expert_in[0, 1], preferred_element_type=jnp.float32) * scale  12.8 us
    dot_general x4, matrix products, activation(): jnp.dot(rows, expert_in[0, 0], preferred_element_type=jnp.float32) * scale  12 us
  transfers between devices with their start and end apart: 20, of which 6 were waited for; matrix products, arithmetic and copies ran while one was open for 30% of the time, Pallas kernels for 0%

profile of v1, /device:TPU:0, one launch (start us, length us, event | category | flops | bytes accessed | tf_op | source)
XLA Modules:
  0.0 266.7 jit_solution(16156201961595448060)
XLA Ops:
  9.7 3.0 %collective-permute-start.3 = (bf16[127,512]{1,0:T(8,128)(2,1)}, bf16[127,512]{1,0:T(8,128)(2,1)}, u32[]{:S(2)}, u32[]{:S(2)}) collective-permute-start(bf16[127,512]{1,0:T(8,128)(2,1)} %slice.36), channel_id=1, source_target_pairs={{0,1},{1,4},{4,5},{5,8},{8,9},{9,12},{12,13},{2,3},{3,6},{6,7},{7,... | collective-permute-start | bytes 390152 | tf_op jit(solution)/shard_map/ppermute | solution.py:15
  14.9 1.7 pad_maximum_fusion.2
  16.6 1.7 copy.47
  18.3 1.7 fusion.16
  20.0 1.9 copy-done.2
  23.1 4.3 %fusion.55 = bf16[4,64,8,128]{3,1,2,0:T(8,128)(2,1)} fusion(bf16[255,4,64,1]{0,2,3,1:T(8,128)(2,1)S(1)} %bitcast.218, f32[4,255,128,8]{2,1,3,0:T(8,128)} %copy-done.2, f32[4,8,128]{2,1,0:T(8,128)S(1)} %exponential_add_fusion, f32[4,8,128]{2,1,0:T(8,128)S(1)} %broadcast_maximum_fusion, pred[128,255]{0,1:T(8,128)(4,1)S(1)} %fusion.120), kind=kOutput, calls=%fused_computation.68 | convolution fusion | flops 140222464 | bytes 4898176 | tf_op jit(solution)/shard_map/gqpj,jgd->pgqd/dot_general | solution.py:54
  27.6 2.3 copy.45
  29.9 3.3 %reshape.239 = bf16[2,64,4,720]{3,2,1,0:T(4,128)(2,1)} reshape(bf16[128,2880]{1,0:T(8,128)(2,1)} %copy.45) | data formatting | bytes 1474560 | tf_op jit(solution)/shard_map/reshape | solution.py:92
  33.2 2.4 constant_dynamic-slice_fusion.7
  36.2 4.4 %collective-permute-start = (bf16[64,720]{1,0:T(8,128)(2,1)}, bf16[64,720]{1,0:T(8,128)(2,1)}, u32[]{:S(2)}, u32[]{:S(2)}) collective-permute-start(bf16[64,720]{1,0:T(8,128)(2,1)} %bitcast.199), channel_id=1, source_target_pairs={{0,4},{4,8},{8,12},{12,0},{1,5},{5,9},{9,13},{13,1},{2,6},{6,10},{... | collective-permute-start | bytes 276488 | tf_op jit(solution)/shard_map/ppermute | solution.py:20
  41.3 2.6 collective-permute-start.1
  44.5 1.3 collective-permute-start.2
  45.9 42.1 %all-gather.4.cloned.1.call-done = bf16[512,2048]{0,1:T(8,128)(2,1)} async-done(((bf16[128,2048]{0,1:T(8,128)(2,1)}), bf16[512,2048]{0,1:T(8,128)(2,1)}) %all-gather.4.cloned.1.call-update) | async-done | bytes 2097168 | tf_op jit(solution)/shard_map/all_gather | solution.py:109
  88.0 3.4 %fusion.142 = f32[512,720]{1,0:T(8,128)S(1)} fusion(bf16[512,2048]{0,1:T(8,128)(2,1)} %all-gather.4.cloned.1.call-done, bf16[2048,720]{0,1:T(8,128)(2,1)S(1)} %copy-done), kind=kOutput, calls=%fused_computation.196 | convolution fusion | flops 1509949440 | bytes 6520832 | tf_op jit(solution)/shard_map/dot_general | solution.py:110
  92.6 1.8 collective-permute-start.4
  96.2 7.5 %collective-permute-done.4 = bf16[4,64,720]{2,1,0:T(8,128)(2,1)S(1)} collective-permute-done((bf16[4,64,720]{2,1,0:T(8,128)(2,1)S(1)}, bf16[4,64,720]{2,1,0:T(8,128)(2,1)S(1)}, u32[]{:S(2)}, u32[]{:S(2)}) %collective-permute-start.4) | collective-permute-done | bytes 368672 | tf_op jit(solution)/shard_map/ppermute | solution.py:20
  104.9 35.8 %all-gather.6.cloned.1.call-done = bf16[256,2880]{0,1:T(8,128)(2,1)} async-done(((bf16[256,720]{0,1:T(8,128)(2,1)}), bf16[256,2880]{0,1:T(8,128)(2,1)}) %all-gather.6.cloned.1.call-update) | async-done | bytes 1474576 | tf_op jit(solution)/shard_map/all_gather | solution.py:119
  140.7 1.5 collective-permute-start.5
  142.2 13.1 %all-gather = f32[512,8]{0,1:T(8,128)S(1)} all-gather(f32[128,8]{0,1:T(8,128)S(1)} %select_reduce_fusion), channel_id=2, replica_groups=mesh['groups'=2,'ep'=4,'tp'=2,'sub'=2] {'ep'}, dimensions={0}, use_global_device_ids=true | all-gather | bytes 20480 | tf_op jit(solution)/shard_map/all_gather | solution.py:104
  157.8 16.4 %collective-permute-done.5 = bf16[256,2880]{0,1:T(8,128)(2,1)S(1)} collective-permute-done((bf16[256,2880]{0,1:T(8,128)(2,1)}, bf16[256,2880]{0,1:T(8,128)(2,1)S(1)}, u32[]{:S(2)}, u32[]{:S(2)}) %collective-permute-start.5) | collective-permute-done | bytes 1474592 | tf_op jit(solution)/shard_map/ppermute | solution.py:20
  174.2 2.6 multiply_reduce_fusion
  176.8 3.7 %fusion.69 = f32[256,720]{0,1:T(8,128)S(1)} fusion(bf16[256,2880]{0,1:T(8,128)(2,1)S(1)} %copy-done.3, bf16[1,2,2880,720]{2,3,1,0:T(8,128)(2,1)} %param.18, f32[256]{0:T(256)S(1)} %add_rsqrt_fusion.1), kind=kOutput, calls=%fused_computation.76 | convolution fusion | flops 1061867520 | bytes 6452224 | tf_op jit(solution)/shard_map/dot_general | solution.py:59
  180.5 3.6 %fusion.101 = bf16[256,720]{0,1:T(8,128)(2,1)S(1)} fusion(f32[256,720]{0,1:T(8,128)S(1)} %fusion.69, bf16[256,2880]{0,1:T(8,128)(2,1)S(1)} %copy-done.3, bf16[1,2,2880,720]{2,3,1,0:T(8,128)(2,1)} %param.18, f32[256]{0:T(256)S(1)} %add_rsqrt_fusion.1), kind=kOutput, calls=%fused_computation.92 | convolution fusion | flops 1063342080 | bytes 6820864 | tf_op jit(solution)/shard_map/dot_general | solution.py:60
  184.1 1.5 collective-permute-start.13
  190.0 2.1 fusion.44
  192.1 3.5 %fusion.57 = f32[256,720]{0,1:T(8,128)S(1)} fusion(bf16[256,2880]{0,1:T(8,128)(2,1)S(1)} %copy-done.3, bf16[1,2,2880,720]{2,3,1,0:T(8,128)(2,1)} %collective-permute-done.7, f32[256]{0:T(256)S(1)} %add_rsqrt_fusion.1), kind=kOutput, calls=%fused_computation.70 | convolution fusion | flops 1061867520 | bytes 6452224 | tf_op jit(solution)/shard_map/dot_general | solution.py:59
  195.7 3.5 %fusion.97 = bf16[256,720]{0,1:T(8,128)(2,1)S(1)} fusion(f32[256,720]{0,1:T(8,128)S(1)} %fusion.57, bf16[256,2880]{0,1:T(8,128)(2,1)S(1)} %copy-done.3, bf16[1,2,2880,720]{2,3,1,0:T(8,128)(2,1)} %collective-permute-done.7, f32[256]{0:T(256)S(1)} %add_rsqrt_fusion.1), kind=kOutput, calls=%fused_computation.90 | convolution fusion | flops 1063342080 | bytes 6820864 | tf_op jit(solution)/shard_map/dot_general | solution.py:60
  199.2 1.5 collective-permute-start.14
  200.7 3.5 %fusion.56 = f32[256,720]{0,1:T(8,128)S(1)} fusion(bf16[256,2880]{0,1:T(8,128)(2,1)S(1)} %collective-permute-done.5, bf16[1,2,2880,720]{2,3,1,0:T(8,128)(2,1)} %collective-permute-done.7, f32[256]{0:T(256)S(1)} %add_rsqrt_fusion), kind=kOutput, calls=%fused_computation.69 | convolution fusion | flops 1061867520 | bytes 6452224 | tf_op jit(solution)/shard_map/dot_general | solution.py:59
  204.3 4.3 %fusion.96 = bf16[256,720]{0,1:T(8,128)(2,1)} fusion(f32[256,720]{0,1:T(8,128)S(1)} %fusion.56, bf16[256,2880]{0,1:T(8,128)(2,1)S(1)} %collective-permute-done.5, bf16[1,2,2880,720]{2,3,1,0:T(8,128)(2,1)} %collective-permute-done.7, f32[256]{0:T(256)S(1)} %add_rsqrt_fusion), kind=kOutput, calls=%fused_computation.89 | convolution fusion | flops 1063342080 | bytes 6820864 | tf_op jit(solution)/shard_map/dot_general | solution.py:60
  209.1 2.6 fusion.34
  211.7 2.8 %fusion.33 = f32[256,1440]{0,1:T(8,128)S(1)} fusion(f32[256,1440]{0,1:T(8,128)S(1)} %fusion.34, bf16[256,720]{0,1:T(8,128)(2,1)} %fusion.96, bf16[1,1440,1440]{2,1,0:T(8,128)(2,1)} %collective-permute-done.8, s32[]{:T(128)S(6)} %select_n.274, f32[256]{0:T(256)S(1)} %mul.248), kind=kOutput, calls=%fused_computation.46 | convolution fusion | flops 532316160 | bytes 5530628 | tf_op jit(solution)/shard_map/dot_general | solution.py:139
  214.6 2.2 fusion.30
  216.8 2.3 copy.55
  219.1 1.9 dynamic-slice_bitcast_fusion.2
  222.2 2.1 collective-permute-start.16
  224.3 2.0 collective-permute-start.17
  226.3 2.8 %fusion.36 = f32[256,1440]{0,1:T(8,128)S(1)} fusion(bf16[256,720]{0,1:T(8,128)(2,1)} %collective-permute-done.9, bf16[1,1440,1440]{2,1,0:T(8,128)(2,1)} %collective-permute-done.8, s32[]{:T(128)S(6)} %select_n.276), kind=kOutput, calls=%fused_computation.49 | convolution fusion | flops 530841600 | bytes 4055044 | tf_op jit(solution)/shard_map/dot_general | solution.py:139
  229.1 2.8 %fusion.25 = f32[256,1440]{0,1:T(8,128)S(1)} fusion(f32[256,1440]{0,1:T(8,128)S(1)} %fusion.36, bf16[256,720]{0,1:T(8,128)(2,1)S(1)} %copy-done.10, bf16[1,1440,1440]{2,1,0:T(8,128)(2,1)} %collective-permute-done.8, s32[]{:T(128)S(6)} %select_n.274, f32[256]{0:T(256)S(1)} %copy-done.13), kind=kOutput, calls=%fused_computation.38 | convolution fusion | flops 532316160 | bytes 5530628 | tf_op jit(solution)/shard_map/dot_general | solution.py:139
  232.0 3.0 %fusion.22 = bf16[256,1440]{0,1:T(8,128)(2,1)} fusion(f32[256,1440]{0,1:T(8,128)S(1)} %fusion.25, f32[256,1440]{0,1:T(8,128)S(1)} %copy-done.4, bf16[256,720]{0,1:T(8,128)(2,1)} %collective-permute-done.6, bf16[1,1440,1440]{2,1,0:T(8,128)(2,1)S(1)} %bitcast.204, s32[]{:T(128)S(6)} %select_n.276, f32[256]{0:T(256)S(1)} %copy-done.14), kind=kOutput, calls=%fused_computation.35 | convolution fusion | flops 533053440 | bytes 6267908 | tf_op jit(solution)/shard_map/dot_general | solution.py:139
  234.9 2.3 copy.53
  237.2 1.9 dynamic-slice_bitcast_fusion.5
  240.1 2.9 %collective-permute-start.12 = (bf16[64,1440]{1,0:T(8,128)(2,1)S(1)}, bf16[64,1440]{1,0:T(8,128)(2,1)}, u32[]{:S(2)}, u32[]{:S(2)}) collective-permute-start(bf16[64,1440]{1,0:T(8,128)(2,1)S(1)} %get-tuple-element.12), channel_id=1, source_target_pairs={{0,12},{4,0},{8,4},{12,8},{1,13},{5,1},{9,5},{13,9},{2,14},{6,2},{... | collective-permute-start | bytes 552968 | tf_op jit(solution)/shard_map/ppermute | solution.py:20
  243.0 1.8 copy.52
  244.7 1.7 copy.54
  246.5 2.6 collective-permute-done.10
  249.0 5.5 %collective-permute-done.11 = bf16[64,1440]{1,0:T(8,128)(2,1)S(1)} collective-permute-done((bf16[64,1440]{1,0:T(8,128)(2,1)}, bf16[64,1440]{1,0:T(8,128)(2,1)S(1)}, u32[]{:S(2)}, u32[]{:S(2)}) %collective-permute-start.11) | collective-permute-done | bytes 184352 | tf_op jit(solution)/shard_map/ppermute | solution.py:20
  254.5 2.0 fusion.116
  (125 shorter events, 25.7 us)
Async XLA Ops:
  6.5 81.4 %copy-start = (bf16[2048,720]{0,1:T(8,128)(2,1)S(1)}, bf16[2048,720]{0,1:T(8,128)(2,1)}, u32[]{:S(2)}) copy-start(bf16[2048,720]{0,1:T(8,128)(2,1)} %param.15) | copy-start | bytes 8847364
  6.5 81.4 %all-gather.4.cloned.1.call-start = ((), (), s32[]{:S(2)}) async-start(), calls=%async_computation | async-start | bytes 2621440 | tf_op jit(solution)/shard_map/all_gather | solution.py:109
  8.4 0.7 copy-start.7
  9.7 5.2 %collective-permute-start.3 = (bf16[127,512]{1,0:T(8,128)(2,1)}, bf16[127,512]{1,0:T(8,128)(2,1)}, u32[]{:S(2)}, u32[]{:S(2)}) collective-permute-start(bf16[127,512]{1,0:T(8,128)(2,1)} %slice.36), channel_id=1, source_target_pairs={{0,1},{1,4},{4,5},{5,8},{8,9},{9,12},{12,13},{2,3},{3,6},{6,7},{7,... | collective-permute-start | bytes 390152 | tf_op jit(solution)/shard_map/ppermute | solution.py:15
  19.9 2.0 copy-start.2
  19.9 3.1 %copy-start.8 = (bf16[255,256]{1,0:T(8,128)(2,1)S(1)}, bf16[255,256]{1,0:T(8,128)(2,1)}, u32[]{:S(2)}) copy-start(bf16[255,256]{1,0:T(8,128)(2,1)} %get-tuple-element.22) | copy-start | bytes 391684
  27.4 113.2 %all-gather.6.cloned.1.call-start = ((), (), s32[]{:S(2)}) async-start(), calls=%async_computation.1 | async-start | bytes 1843200 | tf_op jit(solution)/shard_map/all_gather | solution.py:119
  36.2 58.4 %collective-permute-start = (bf16[64,720]{1,0:T(8,128)(2,1)}, bf16[64,720]{1,0:T(8,128)(2,1)}, u32[]{:S(2)}, u32[]{:S(2)}) collective-permute-start(bf16[64,720]{1,0:T(8,128)(2,1)} %bitcast.199), channel_id=1, source_target_pairs={{0,4},{4,8},{8,12},{12,0},{1,5},{5,9},{9,13},{13,1},{2,6},{6,10},{... | collective-permute-start | bytes 276488 | tf_op jit(solution)/shard_map/ppermute | solution.py:20
  41.3 53.3 %collective-permute-start.1 = (bf16[64,720]{1,0:T(8,128)(2,1)}, bf16[64,720]{1,0:T(8,128)(2,1)}, u32[]{:S(2)}, u32[]{:S(2)}) collective-permute-start(bf16[64,720]{1,0:T(8,128)(2,1)} %bitcast.198), channel_id=1, source_target_pairs={{0,8},{4,12},{8,0},{12,4},{1,9},{5,13},{9,1},{13,5},{2,10},{6,14},... | collective-permute-start | bytes 276488 | tf_op jit(solution)/shard_map/ppermute | solution.py:20
  44.5 50.1 %collective-permute-start.2 = (bf16[64,720]{1,0:T(8,128)(2,1)}, bf16[64,720]{1,0:T(8,128)(2,1)}, u32[]{:S(2)}, u32[]{:S(2)}) collective-permute-start(bf16[64,720]{1,0:T(8,128)(2,1)} %bitcast.197), channel_id=1, source_target_pairs={{0,12},{4,0},{8,4},{12,8},{1,13},{5,1},{9,5},{13,9},{2,14},{6,2},{... | collective-permute-start | bytes 276488 | tf_op jit(solution)/shard_map/ppermute | solution.py:20
  45.9 146.3 %collective-permute-start.7 = (bf16[1,2,2880,720]{2,3,1,0:T(8,128)(2,1)}, bf16[1,2,2880,720]{2,3,1,0:T(8,128)(2,1)}, u32[]{:S(2)}, u32[]{:S(2)}) collective-permute-start(bf16[1,2,2880,720]{2,3,1,0:T(8,128)(2,1)} %param.18), channel_id=1, source_target_pairs={{0,1},{1,0},{2,3},{3,2},{4,5},{5,4},{6,7},{7,6},{8,9},{9,8},{10,11... | collective-permute-start | bytes 24883208 | tf_op jit(solution)/shard_map/ppermute | solution.py:20
  45.9 48.6 %copy-start.11 = (f32[2880]{0:T(1024)S(1)}, f32[2880]{0:T(1024)}, u32[]{:S(2)}) copy-start(f32[2880]{0:T(1024)} %param.17) | copy-start | bytes 34564
  91.4 1.2 copy-start.5
  92.6 11.1 %copy-start.6 = (f32[512,720]{1,0:T(8,128)S(1)}, f32[512,720]{1,0:T(8,128)}, u32[]{:S(2)}) copy-start(f32[512,720]{1,0:T(8,128)} %copy-done.5) | copy-start | bytes 4423684
  92.6 11.1 %collective-permute-start.4 = (bf16[4,64,720]{2,1,0:T(8,128)(2,1)S(1)}, bf16[4,64,720]{2,1,0:T(8,128)(2,1)S(1)}, u32[]{:S(2)}, u32[]{:S(2)}) collective-permute-start(bf16[4,64,720]{2,1,0:T(8,128)(2,1)S(1)} %fusion.107), channel_id=1, source_target_pairs={{0,2},{2,0},{1,3},{3,1},{4,6},{6,4},{5,7},{7,5},{8,10},{10,8},{9,1... | collective-permute-start | bytes 1105928 | tf_op jit(solution)/shard_map/ppermute | solution.py:20
  95.6 46.5 %copy-start.12 = (s32[128,4]{0,1:T(4,128)S(1)}, s32[128,4]{0,1:T(4,128)}, u32[]{:S(2)}) copy-start(s32[128,4]{0,1:T(4,128)} %param.21) | copy-start | bytes 6148
  95.6 46.5 %copy-start.15 = (s32[128,4]{0,1:T(4,128)S(1)}, s32[128,4]{0,1:T(4,128)}, u32[]{:S(2)}) copy-start(s32[128,4]{0,1:T(4,128)} %param.20) | copy-start | bytes 6148
  140.7 36.1 %copy-start.3 = (bf16[256,2880]{0,1:T(8,128)(2,1)S(1)}, bf16[256,2880]{0,1:T(8,128)(2,1)}, u32[]{:S(2)}) copy-start(bf16[256,2880]{0,1:T(8,128)(2,1)} %all-gather.6.cloned.1.call-done) | copy-start | bytes 4423684
  140.7 33.5 %collective-permute-start.5 = (bf16[256,2880]{0,1:T(8,128)(2,1)}, bf16[256,2880]{0,1:T(8,128)(2,1)S(1)}, u32[]{:S(2)}, u32[]{:S(2)}) collective-permute-start(bf16[256,2880]{0,1:T(8,128)(2,1)} %all-gather.6.cloned.1.call-done), channel_id=1, source_target_pairs={{0,2},{2,0},{1,3},{3,1},{4,6},{6,4},{5,7},{7,5},{8,10},{10,8},{9,1... | collective-permute-start | bytes 4423688 | tf_op jit(solution)/shard_map/ppermute | solution.py:20
  142.1 67.0 %collective-permute-start.8 = (bf16[1,1440,1440]{2,1,0:T(8,128)(2,1)}, bf16[1,1440,1440]{2,1,0:T(8,128)(2,1)}, u32[]{:S(2)}, u32[]{:S(2)}) collective-permute-start(bf16[1,1440,1440]{2,1,0:T(8,128)(2,1)} %param.19), channel_id=1, source_target_pairs={{0,1},{1,0},{2,3},{3,2},{4,5},{5,4},{6,7},{7,6},{8,9},{9,8},{10,11... | collective-permute-start | bytes 12441608 | tf_op jit(solution)/shard_map/ppermute | solution.py:20
  176.8 8.8 %slice-start.4 = ((s8[8478720]{0:T(1024)(128)(4,1)}), s8[4194304]{0:T(1024)(128)(4,1)S(1)}, s32[]{:S(2)}) async-start(s8[8478720]{0:T(1024)(128)(4,1)} %bitcast.219), calls=%async_computation.6 | async-start | bytes 8388608
  176.8 8.8 %slice-start.5 = ((s8[8478720]{0:T(1024)(128)(4,1)}), s8[4194304]{0:T(1024)(128)(4,1)S(1)}, s32[]{:S(2)}) async-start(s8[8478720]{0:T(1024)(128)(4,1)} %bitcast.219), calls=%async_computation.7 | async-start | bytes 8388608
  180.5 5.2 %slice-start.6 = ((s8[8478720]{0:T(1024)(128)(4,1)}), s8[90112]{0:T(1024)(128)(4,1)S(1)}, s32[]{:S(2)}) async-start(s8[8478720]{0:T(1024)(128)(4,1)} %bitcast.219), calls=%async_computation.8 | async-start | bytes 180224
  184.1 30.5 %collective-permute-start.13 = (bf16[256,720]{0,1:T(8,128)(2,1)S(1)}, bf16[256,720]{0,1:T(8,128)(2,1)S(1)}, u32[]{:S(2)}, u32[]{:S(2)}) collective-permute-start(bf16[256,720]{0,1:T(8,128)(2,1)S(1)} %fusion.101), channel_id=1, source_target_pairs={{0,2},{2,0},{1,3},{3,1},{4,6},{6,4},{5,7},{7,5},{8,10},{10,8},{9,1... | collective-permute-start | bytes 1105928 | tf_op jit(solution)/shard_map/ppermute | solution.py:20
  185.6 3.3 %slice-start = ((s8[4423680]{0:T(1024)(128)(4,1)}), s8[4194304]{0:T(1024)(128)(4,1)S(1)}, s32[]{:S(2)}) async-start(s8[4423680]{0:T(1024)(128)(4,1)} %bitcast.201), calls=%async_computation.2 | async-start | bytes 8388608
  187.0 2.0 slice-start.1
  188.4 43.6 %collective-permute-start.6 = (bf16[256,720]{0,1:T(8,128)(2,1)S(1)}, bf16[256,720]{0,1:T(8,128)(2,1)}, u32[]{:S(2)}, u32[]{:S(2)}) collective-permute-start(bf16[256,720]{0,1:T(8,128)(2,1)S(1)} %fusion.98), channel_id=1, source_target_pairs={{0,2},{2,0},{1,3},{3,1},{4,6},{6,4},{5,7},{7,5},{8,10},{10,8},{9,1... | collective-permute-start | bytes 1105928 | tf_op jit(solution)/shard_map/ppermute | solution.py:20
  199.2 5.1 %copy-start.9 = (bf16[256,720]{0,1:T(8,128)(2,1)}, bf16[256,720]{0,1:T(8,128)(2,1)S(1)}, u32[]{:S(2)}) copy-start(bf16[256,720]{0,1:T(8,128)(2,1)S(1)} %fusion.97) | copy-start | bytes 1105924
  199.2 9.9 %collective-permute-start.14 = (bf16[256,720]{0,1:T(8,128)(2,1)S(1)}, bf16[256,720]{0,1:T(8,128)(2,1)S(1)}, u32[]{:S(2)}, u32[]{:S(2)}) collective-permute-start(bf16[256,720]{0,1:T(8,128)(2,1)S(1)} %fusion.97), channel_id=1, source_target_pairs={{0,2},{2,0},{1,3},{3,1},{4,6},{6,4},{5,7},{7,5},{8,10},{10,8},{9,1... | collective-permute-start | bytes 1105928 | tf_op jit(solution)/shard_map/ppermute | solution.py:20
  208.5 17.8 %collective-permute-start.9 = (bf16[256,720]{0,1:T(8,128)(2,1)}, bf16[256,720]{0,1:T(8,128)(2,1)}, u32[]{:S(2)}, u32[]{:S(2)}) collective-permute-start(bf16[256,720]{0,1:T(8,128)(2,1)} %fusion.96), channel_id=1, source_target_pairs={{0,2},{2,0},{1,3},{3,1},{4,6},{6,4},{5,7},{7,5},{8,10},{10,8},{9,1... | collective-permute-start | bytes 1105928 | tf_op jit(solution)/shard_map/ppermute | solution.py:20
  216.8 15.2 %slice-start.2 = ((s8[4423680]{0:T(1024)(128)(4,1)}), s8[229376]{0:T(1024)(128)(4,1)S(1)}, s32[]{:S(2)}) async-start(s8[4423680]{0:T(1024)(128)(4,1)} %bitcast.203), calls=%async_computation.4 | async-start | bytes 458752
  221.0 8.1 %copy-start.10 = (bf16[256,720]{0,1:T(8,128)(2,1)S(1)}, bf16[256,720]{0,1:T(8,128)(2,1)}, u32[]{:S(2)}) copy-start(bf16[256,720]{0,1:T(8,128)(2,1)} %copy-done.9) | copy-start | bytes 1105924
  221.0 8.1 %copy-start.13 = (f32[256]{0:T(256)S(1)}, f32[256]{0:T(256)}, u32[]{:S(2)}) copy-start(f32[256]{0:T(256)} %mul.231) | copy-start | bytes 3076
  221.0 19.0 %collective-permute-start.15 = (bf16[64,1440]{1,0:T(8,128)(2,1)}, bf16[64,1440]{1,0:T(8,128)(2,1)}, u32[]{:S(2)}, u32[]{:S(2)}) collective-permute-start(bf16[64,1440]{1,0:T(8,128)(2,1)} %get-tuple-element.14), channel_id=1, source_target_pairs={{0,4},{4,8},{8,12},{12,0},{1,5},{5,9},{9,13},{13,1},{2,6},{6,10},{... | collective-permute-start | bytes 552968 | tf_op jit(solution)/shard_map/ppermute | solution.py:20
  222.2 24.3 %collective-permute-start.16 = (bf16[64,1440]{1,0:T(8,128)(2,1)}, bf16[64,1440]{1,0:T(8,128)(2,1)}, u32[]{:S(2)}, u32[]{:S(2)}) collective-permute-start(bf16[64,1440]{1,0:T(8,128)(2,1)} %get-tuple-element.16), channel_id=1, source_target_pairs={{0,8},{4,12},{8,0},{12,4},{1,9},{5,13},{9,1},{13,5},{2,10},{6,14},... | collective-permute-start | bytes 552968 | tf_op jit(solution)/shard_map/ppermute | solution.py:20
  224.3 7.7 %slice-start.3 = ((s8[4423680]{0:T(1024)(128)(4,1)}), s8[4194304]{0:T(1024)(128)(4,1)S(1)}, s32[]{:S(2)}) async-start(s8[4423680]{0:T(1024)(128)(4,1)} %bitcast.203), calls=%async_computation.5 | async-start | bytes 8388608
  224.3 22.2 %collective-permute-start.17 = (bf16[64,1440]{1,0:T(8,128)(2,1)}, bf16[64,1440]{1,0:T(8,128)(2,1)}, u32[]{:S(2)}, u32[]{:S(2)}) collective-permute-start(bf16[64,1440]{1,0:T(8,128)(2,1)} %get-tuple-element.15), channel_id=1, source_target_pairs={{0,12},{4,0},{8,4},{12,8},{1,13},{5,1},{9,5},{13,9},{2,14},{6,2},{... | collective-permute-start | bytes 552968 | tf_op jit(solution)/shard_map/ppermute | solution.py:20
  229.1 2.8 %copy-start.4 = (f32[256,1440]{0,1:T(8,128)S(1)}, f32[256,1440]{0,1:T(8,128)}, u32[]{:S(2)}) copy-start(f32[256,1440]{0,1:T(8,128)} %fusion.44) | copy-start | bytes 4423684
  229.1 2.8 %copy-start.14 = (f32[256]{0:T(256)S(1)}, f32[256]{0:T(256)}, u32[]{:S(2)}) copy-start(f32[256]{0:T(256)} %mul.209) | copy-start | bytes 3076
  239.1 9.9 %collective-permute-start.10 = (bf16[64,1440]{1,0:T(8,128)(2,1)}, bf16[64,1440]{1,0:T(8,128)(2,1)S(1)}, u32[]{:S(2)}, u32[]{:S(2)}) collective-permute-start(bf16[64,1440]{1,0:T(8,128)(2,1)} %get-tuple-element.11), channel_id=1, source_target_pairs={{0,4},{4,8},{8,12},{12,0},{1,5},{5,9},{9,13},{13,1},{2,6},{6,10},{... | collective-permute-start | bytes 552968 | tf_op jit(solution)/shard_map/ppermute | solution.py:20
  239.5 15.0 %collective-permute-start.11 = (bf16[64,1440]{1,0:T(8,128)(2,1)}, bf16[64,1440]{1,0:T(8,128)(2,1)S(1)}, u32[]{:S(2)}, u32[]{:S(2)}) collective-permute-start(bf16[64,1440]{1,0:T(8,128)(2,1)} %get-tuple-element.13), channel_id=1, source_target_pairs={{0,8},{4,12},{8,0},{12,4},{1,9},{5,13},{9,1},{13,5},{2,10},{6,14},... | collective-permute-start | bytes 552968 | tf_op jit(solution)/shard_map/ppermute | solution.py:20
  240.1 14.4 %collective-permute-start.12 = (bf16[64,1440]{1,0:T(8,128)(2,1)S(1)}, bf16[64,1440]{1,0:T(8,128)(2,1)}, u32[]{:S(2)}, u32[]{:S(2)}) collective-permute-start(bf16[64,1440]{1,0:T(8,128)(2,1)S(1)} %get-tuple-element.12), channel_id=1, source_target_pairs={{0,12},{4,0},{8,4},{12,8},{1,13},{5,1},{9,5},{13,9},{2,14},{6,2},{... | collective-permute-start | bytes 552968 | tf_op jit(solution)/shard_map/ppermute | solution.py:20
  246.5 11.4 %copy-start.16 = (pred[128]{0:T(512)(128)(4,1)S(1)}, pred[128]{0:T(512)(128)(4,1)}, u32[]{:S(2)}) copy-start(pred[128]{0:T(512)(128)(4,1)} %broadcast_in_dim.64) | copy-start | bytes 388
  254.5 5.4 %copy-start.1 = (bf16[2048,720]{0,1:T(8,128)(2,1)S(1)}, bf16[2048,720]{0,1:T(8,128)(2,1)}, u32[]{:S(2)}) copy-start(bf16[2048,720]{0,1:T(8,128)(2,1)} %param.15) | copy-start | bytes 8847364
Sparse Core Ops, SparseCore 0:
  27.6 60.3 all-gather.3
  105.0 35.6 all-gather.5

commit v2 on v0

v2 whole, which is shorter than its diff:
```python
import jax
import jax.numpy as jnp
from jax import lax
from jax.experimental import pallas as pl
from jax.experimental.pallas import tpu as pltpu
from jax.sharding import PartitionSpec as P

D = 2880
HD = 64
WIN = 128
TOP = 4
PAIR = 2
VMEM_BYTES = 48 * 1024 * 1024


def shifted(block, axis, distance):
    devices = range(lax.axis_size(axis))
    route = [(i - distance, i) for i in devices if i - distance in devices]
    return lax.ppermute(block, axis, route)


def swapped(block, axis, distance):
    return lax.ppermute(block, axis, [(i, i ^ distance) for i in range(lax.axis_size(axis))])


def picked(blocks, index, axis):
    return lax.dynamic_index_in_dim(blocks, index, axis, keepdims=False)


def in_vmem(count):
    return [pl.BlockSpec(memory_space=pltpu.VMEM)] * count


def cost(flops, bytes_accessed):
    return pl.CostEstimate(flops=flops, bytes_accessed=bytes_accessed, transcendentals=0)


def dot(left, right):
    return jnp.dot(left, right, preferred_element_type=jnp.float32)


def attention_kernel(first_ref, sink_ref, q_ref, kp_ref, k_ref, vp_ref, v_ref, out_ref):
    rows = q_ref.shape[0]
    kv_count = k_ref.shape[1] // HD
    pairs = q_ref.shape[1] // (2 * HD * kv_count)
    lane = lax.broadcasted_iota(jnp.int32, (rows, 2 * HD), 1)
    low = lane < HD
    row = lax.broadcasted_iota(jnp.int32, (rows, rows), 0)
    col = lax.broadcasted_iota(jnp.int32, (rows, rows), 1)
    before = col > row
    shut = before & (first_ref[0] == 1)
    zero = jnp.zeros((), jnp.bfloat16)

    def twice(ref, g):
        part = ref[:, g * HD : (g + 1) * HD]
        return jnp.concatenate([part, part], axis=1)

    def scores_of(q, keys):
        return lax.dot_general(q, keys, (((1,), (1,)), ((), ())), preferred_element_type=jnp.float32)

    for g in range(kv_count):
        keys_before, keys_own = twice(kp_ref, g), twice(k_ref, g)
        values_before, values_own = twice(vp_ref, g), twice(v_ref, g)
        for i in range(pairs):
            start = (g * pairs + i) * 2 * HD
            both = q_ref[:, start : start + 2 * HD]
            results = []
            for side in range(2):
                q = jnp.where(low if side == 0 else ~low, both, zero)
                sink = sink_ref[(g * pairs + i) * 2 + side]
                scores = jnp.where(before, scores_of(q, keys_before), scores_of(q, keys_own)) * HD ** (-0.5)
                scores = jnp.where(shut, -1e30, scores)
                largest = jnp.maximum(jnp.max(scores, axis=1, keepdims=True), sink)
                numerator = jnp.exp(scores - largest)
                denominator = jnp.sum(numerator, axis=1, keepdims=True) + jnp.exp(sink - largest)
                weights = (numerator * (1.0 / denominator)).astype(jnp.bfloat16)
                results.append(
                    dot(jnp.where(before, weights, zero), values_before)
                    + dot(jnp.where(before, zero, weights), values_own)
                )
            out_ref[:, start : start + 2 * HD] = jnp.where(low, results[0], results[1]).astype(jnp.bfloat16)


def attention(queries, key_rows, value_rows, sink_logits, first):
    rows, width = queries.shape
    earlier_keys = shifted(key_rows, ("ep", "sub"), 1)
    earlier_values = shifted(value_rows, ("ep", "sub"), 1)
    smem = pl.BlockSpec(memory_space=pltpu.SMEM)
    return pl.pallas_call(
        attention_kernel,
        out_shape=jax.ShapeDtypeStruct((rows, width), jnp.bfloat16),
        in_specs=[smem, smem] + in_vmem(5),
        out_specs=in_vmem(1)[0],
        compiler_params=pltpu.CompilerParams(vmem_limit_bytes=VMEM_BYTES),
        cost_estimate=cost(8 * rows * rows * width, 6 * rows * width),
        name="attention",
    )(first, sink_logits, queries, earlier_keys, key_rows, earlier_values, value_rows)


def project(attended, out_weight, near_weights, t, z, s, t_count):
    slots = len(attended)
    rows, width = attended[0].shape
    columns = out_weight.shape[1]
    half = rows // t_count
    shares = len(near_weights)
    depth = width // shares

    def kernel(place_ref, *refs):
        attended_refs = refs[:slots]
        weight_ref = refs[slots]
        near_refs = refs[slots + 1 : slots + 1 + shares]
        kept_ref, sent_ref, total = refs[slots + 1 + shares :]
        t, member, s = place_ref[0], place_ref[1], place_ref[2]
        for jr in range(slots):
            for i in range(PAIR):
                if i == 0:
                    result = dot(attended_refs[jr][...], weight_ref[...])
                else:
                    result = 0.0
                    for u in range(shares):
                        start = pl.multiple_of((s ^ u) * depth, 128)
                        result = result + dot(attended_refs[jr][:, pl.ds(start, depth)], near_refs[u][...])
                total[...] = result
                for m in range(t_count):
                    block = total[pl.ds(pl.multiple_of((t ^ m) * half, half), half), :]
                    if m == 0:
                        kept_ref[member ^ i, jr] = block
                    else:
                        sent_ref[m - 1, member ^ i, jr] = block.astype(jnp.bfloat16)

    place = jnp.stack([t, z % PAIR, s]).astype(jnp.int32)
    return pl.pallas_call(
        kernel,
        out_shape=(
            jax.ShapeDtypeStruct((PAIR, slots, half, columns), jnp.float32),
            jax.ShapeDtypeStruct((t_count - 1, PAIR, slots, half, columns), jnp.bfloat16),
        ),
        in_specs=[pl.BlockSpec(memory_space=pltpu.SMEM)] + in_vmem(slots + 1 + shares),
        out_specs=tuple(in_vmem(2)),
        scratch_shapes=[pltpu.VMEM((rows, columns), jnp.float32)],
        compiler_params=pltpu.CompilerParams(vmem_limit_bytes=VMEM_BYTES),
        cost_estimate=cost(4 * slots * rows * width * columns, 4 * width * columns),
        name="project",
    )(place, *attended, out_weight, *near_weights)


def activate(pieces, inverse_gain, experts_in, pair):
    t_count, slots = len(pieces), len(pieces[0])
    _, _, half, columns = pieces[0][0].shape
    chunks = slots * PAIR
    row_count = t_count * slots * half
    experts = len(experts_in)
    units = experts_in[0].shape[3]
    tile = min(256, units)
    tiles = -(-units // tile)
    weights = [w.reshape(2, chunks, columns, units) for w in experts_in]

    def kernel(pair_ref, *refs):
        piece_refs = refs[: t_count * slots]
        gain_ref = refs[t_count * slots]
        weight_refs = refs[t_count * slots + 1 : t_count * slots + 1 + experts]
        out_ref, rows_ref, scale_ref = refs[t_count * slots + 1 + experts :]
        e, step = pl.program_id(0), pl.program_id(1)

        @pl.when((e == 0) & (step == 0))
        def _():
            for m in range(t_count):
                for j in range(slots):
                    start = (m * slots + j) * half
                    square = jnp.zeros((half, 1), jnp.float32)
                    for r in range(slots):
                        for i in range(PAIR):
                            chunk = (pair_ref[0] ^ r) * PAIR + i
                            block = piece_refs[m * slots + r][i, j ^ r]
                            rows_ref[chunk, start : start + half, :] = block
                            plain = block.astype(jnp.float32) * gain_ref[chunk]
                            square = square + jnp.sum(plain * plain, axis=1, keepdims=True)
                    scale_ref[start : start + half, :] = lax.rsqrt(square / D + 1e-05)

        for index in range(experts):

            @pl.when(e == index)
            def _():
                gate = jnp.zeros((row_count, tile), jnp.float32)
                up = jnp.zeros((row_count, tile), jnp.float32)
                for c in range(chunks):
                    gate = gate + dot(rows_ref[c], weight_refs[index][0, c])
                    up = up + dot(rows_ref[c], weight_refs[index][1, c])
                gate = gate * scale_ref[...]
                up = up * scale_ref[...]
                out_ref[0] = ((up + 1.0) * gate * jax.nn.sigmoid(1.702 * gate)).astype(jnp.bfloat16)

    def weight_spec(index):
        def place(e, step):
            return (0, 0, 0, jnp.where(e == index, step, jnp.where(e < index, 0, tiles - 1)))

        return pl.BlockSpec((2, chunks, columns, tile), place)

    flat = [piece for part in pieces for piece in part]
    return pl.pallas_call(
        kernel,
        grid=(experts, tiles),
        out_shape=jax.ShapeDtypeStruct((experts, row_count, units), jnp.bfloat16),
        in_specs=[pl.BlockSpec(memory_space=pltpu.SMEM)]
        + in_vmem(len(flat) + 1)
        + [weight_spec(index) for index in range(experts)],
        out_specs=pl.BlockSpec((1, row_count, tile), lambda e, step: (e, 0, step)),
        scratch_shapes=[
            pltpu.VMEM((chunks, row_count, columns), jnp.bfloat16),
            pltpu.VMEM((row_count, 1), jnp.float32),
        ],
        compiler_params=pltpu.CompilerParams(vmem_limit_bytes=VMEM_BYTES),
        cost_estimate=cost(4 * experts * row_count * D * units, 4 * experts * D * units),
        name="activate",
    )(pair.reshape(1), *flat, inverse_gain.reshape(chunks, 1, columns), *weights)


def combine(activated, share, experts_out, t, slots):
    t_count = len(activated)
    experts, row_count, units = activated[0].shape
    width = experts_out[0].shape[2]
    half = row_count // (t_count * slots)
    tile = min(256, width)
    tiles = -(-width // tile)
    weights = [w.reshape(t_count, units, width) for w in experts_out]

    def kernel(t_ref, *refs):
        activated_refs = refs[:t_count]
        share_ref = refs[t_count]
        weight_refs = refs[t_count + 1 : t_count + 1 + experts]
        out_refs = refs[t_count + 1 + experts :]
        t = t_ref[0]
        for m in range(t_count):
            start = m * slots * half
            total = jnp.zeros((slots * half, tile), jnp.float32)
            for e in range(experts):
                result = jnp.zeros((slots * half, tile), jnp.float32)
                for u in range(t_count):
                    first = (m ^ u) * slots * half
                    result = result + dot(
                        activated_refs[u][e, first : first + slots * half, :], weight_refs[e][t ^ u]
                    )
                result = result.astype(jnp.bfloat16).astype(jnp.float32)
                total = total + share_ref[start : start + slots * half, e : e + 1] * result
            for j in range(slots):
                out_refs[j][m] = total[j * half : (j + 1) * half].astype(jnp.bfloat16)

    weight_spec = pl.BlockSpec((t_count, units, tile), lambda step: (0, 0, step))
    return pl.pallas_call(
        kernel,
        grid=(tiles,),
        out_shape=tuple(jax.ShapeDtypeStruct((t_count, half, width), jnp.bfloat16) for _ in range(slots)),
        in_specs=[pl.BlockSpec(memory_space=pltpu.SMEM)] + in_vmem(t_count + 1) + [weight_spec] * experts,
        out_specs=tuple(
            pl.BlockSpec((t_count, half, tile), lambda step: (0, 0, step)) for _ in range(slots)
        ),
        compiler_params=pltpu.CompilerParams(vmem_limit_bytes=VMEM_BYTES),
        cost_estimate=cost(
            2 * experts * row_count * t_count * units * width, 2 * experts * t_count * units * width
        ),
        name="combine",
    )(t.reshape(1), *activated, share, *weights)


def finish(own, returned, t):
    t_count, half, width = own.shape

    def kernel(t_ref, own_ref, *refs):
        *parts, out_ref = refs
        for m in range(t_count):
            total = own_ref[m]
            for part in parts:
                total = total + part[m].astype(jnp.float32)
            start = pl.multiple_of((t_ref[0] ^ m) * half, half)
            out_ref[pl.ds(start, half), :] = total.astype(jnp.bfloat16)

    return pl.pallas_call(
        kernel,
        out_shape=jax.ShapeDtypeStruct((t_count * half, width), jnp.bfloat16),
        in_specs=[pl.BlockSpec(memory_space=pltpu.SMEM)] + in_vmem(1 + len(returned)),
        out_specs=in_vmem(1)[0],
        compiler_params=pltpu.CompilerParams(vmem_limit_bytes=VMEM_BYTES),
        name="finish",
    )(t.reshape(1), own, *returned)


def local(
    queries,
    key_rows,
    value_rows,
    sink_logits,
    out_weight,
    residual,
    norm_gain,
    expert_in,
    expert_out,
    routes,
    route_scores,
):
    row_count = queries.shape[0]
    z_count, t_count, s_count = lax.axis_size("ep"), lax.axis_size("tp"), lax.axis_size("sub")
    z, t, s = lax.axis_index("ep"), lax.axis_index("tp"), lax.axis_index("sub")
    half = row_count // t_count
    columns = out_weight.shape[1]
    width = expert_out.shape[2]
    slots = z_count // PAIR
    pair = (z // PAIR).astype(jnp.int32)

    first = (lax.axis_index(("ep", "sub")) == 0).astype(jnp.int32).reshape(1)
    attended = attention(queries, key_rows, value_rows, sink_logits, first)

    near = picked(out_weight.reshape(s_count, out_weight.shape[0] // s_count, columns), s, 0)
    near = swapped(near, "ep", 1)
    near_weights = [near] + [swapped(near, "sub", u) for u in range(1, s_count)]

    experts_in = [expert_in] + [swapped(expert_in, "sub", e) for e in range(1, s_count)]
    experts_out = [expert_out] + [swapped(expert_out, "sub", e) for e in range(1, s_count)]

    own_residual = picked(residual.reshape(t_count, half, slots, PAIR * columns), t, 0)
    residual_part = [
        picked(own_residual, pair ^ j, 1) if j == 0 else swapped(picked(own_residual, pair ^ j, 1), "ep", PAIR * j)
        for j in range(slots)
    ]
    residual_part = jnp.stack([part.reshape(half, PAIR, columns) for part in residual_part])
    residual_part = residual_part.transpose(2, 0, 1, 3).astype(jnp.float32)

    expert_count = z_count * s_count
    route_float = route_scores.astype(jnp.float32)
    mix_share = route_float / jnp.sum(route_float, axis=1, keepdims=True)
    experts = jnp.arange(expert_count, dtype=jnp.int32)
    named = routes[:, :, None] == experts[None, None, :]
    table = jnp.sum(jnp.where(named, mix_share[:, :, None], 0.0), axis=1)
    tables = jnp.stack([table] + [swapped(table, "ep", d) for d in range(1, z_count)])
    chosen = jnp.stack([z * s_count + (s ^ e) for e in range(s_count)])
    tables = jnp.sum(
        jnp.where(experts[None, None, None, :] == chosen[None, None, :, None], tables[:, :, None, :], 0.0), axis=3
    )
    tables = tables.reshape(slots, PAIR, t_count, half, s_count)
    tables = jnp.take(tables, t ^ jnp.arange(t_count, dtype=jnp.int32), axis=2)

    gathered = [attended] + [swapped(attended, "ep", PAIR * j) for j in range(1, slots)]
    hidden, sent = project(gathered, out_weight, near_weights, t, z, s, t_count)
    hidden = hidden + residual_part
    for m in range(1, t_count):
        hidden = hidden + swapped(sent[m - 1], "tp", m).astype(jnp.float32)
    gain_part = picked(norm_gain.reshape(slots, PAIR, 1, 1, columns), pair, 0)
    scaled = (hidden * gain_part).astype(jnp.bfloat16)

    own = {0: scaled}
    distance = z_count // 2
    while distance:
        own.update({d + distance: swapped(own[d], "ep", distance) for d in list(own)})
        distance //= 2
    pieces = [own] + [{d: swapped(own[d], "tp", m) for d in own} for m in range(1, t_count)]

    inverse_gain = 1.0 / norm_gain
    own_rows = []
    for m in range(t_count):
        rows = jnp.stack([pieces[m][PAIR * r][:, r] for r in range(slots)])
        rows = jnp.take(rows, pair ^ jnp.arange(slots, dtype=jnp.int32), axis=0)
        own_rows.append(rows.reshape(z_count, half, columns).transpose(1, 0, 2).reshape(half, D))
    own_rows = lax.dynamic_slice_in_dim(jnp.stack(own_rows), t * width, width, 2).astype(jnp.float32)
    own_rows = own_rows * lax.dynamic_slice_in_dim(inverse_gain, t * width, width, 0)

    returned = []
    for p in range(PAIR):
        part = [[pieces[m][PAIR * r + p] for r in range(slots)] for m in range(t_count)]
        activated = activate(part, inverse_gain, experts_in, pair)
        activated = [activated] + [swapped(activated, "tp", m) for m in range(1, t_count)]
        share = tables[:, p].transpose(1, 0, 2, 3).reshape(row_count * slots, s_count)
        for j, result in enumerate(combine(activated, share, experts_out, t, slots)):
            distance = PAIR * j + p
            returned.append(swapped(result, "ep", distance) if distance else result)
    return finish(own_rows, returned, t)


def solution(mesh):
    in_specs = (
        P(("groups", "ep", "sub"), "tp"),
        P(("groups", "ep", "sub"), "tp"),
        P(("groups", "ep", "sub"), "tp"),
        P("tp"),
        P("tp", "ep"),
        P(("groups", "ep", "sub"), None),
        P(),
        P(("ep", "sub"), None, None, "tp"),
        P(("ep", "sub"), None, "tp"),
        P(("groups", "ep", "sub"), None),
        P(("groups", "ep", "sub"), None),
    )
    out_specs = P(("groups", "ep", "sub"), "tp")
    return jax.shard_map(local, mesh=mesh, in_specs=in_specs, out_specs=out_specs, check_vma=False)
```

time: 619 us -> 249 us (0.40)
  waiting for transfers between devices: 352 us -> 94.1 us
  blocking collectives: 135 us -> 0 us
  Pallas kernels: 0 us -> 53.5 us
  matrix products: 31 us -> 0 us
  starting transfers between devices: 7.18 us -> 28.4 us
  between operations: 13.4 us -> 0.53 us
  other arithmetic: 14.9 us -> 2.95 us
    all_gather x2 -> x0, waiting for transfers between devices: 241 us -> none  [the longest x1 201 us: local(): lax.all_gather(out_weight, 'ep', axis=1, tiled=True)]
    all_to_all x1 -> x0, blocking collectives: 135 us -> none  [local(): lax.all_to_all(outgoing, ('ep', 'sub'), split_axis=0, concat_axis=0, tile...]
    ppermute x0 -> x22, waiting for transfers between devices: none -> 94.1 us  [swapped(): lax.ppermute(block, axis, [(i, i ^ distance) for i in range(lax.axis_size...]
    all_to_all x1 -> x0, waiting for transfers between devices: 66.9 us -> none  [serve_rows(): lax.all_to_all(finished, ('ep', 'sub'), split_axis=0, concat_axis=0, tile...]
    pallas_call x0 -> x7, Pallas kernels: none -> 53.5 us  [the longest x2 23 us: activate(): pl.pallas_call(kernel, grid=(experts, tiles), out_shape=jax.ShapeDtypeStr...]
    psum x1 -> x0, waiting for transfers between devices: 43.1 us -> none  [local(): hidden = residual.astype(jnp.float32) + lax.psum(partial_value, 'tp')]
    dot_general x5 -> x0, matrix products: 31 us -> none  [the longest x1 13.7 us: expert_rows(): jnp.einsum('rd,kdf->rkf', flat_rows, expert_in[0], preferred_element_type...]
    ppermute x0 -> x22, starting transfers between devices: none -> 24.1 us  [swapped(): lax.ppermute(block, axis, [(i, i ^ distance) for i in range(lax.axis_size...]
  transfers between devices with their start and end apart: 5 -> 24, of which waited for: 4 -> 9; matrix products, arithmetic and copies ran while one was open for 2% -> 26% of each run, Pallas kernels for 0% -> 21%
where the time goes in v2:
time: 249 us; the launch traced here: 248 us
  waiting for transfers between devices  94.1 us (38%)
  local copies, waits for them, and re-layouts  68.4 us (27%)
  Pallas kernels  53.5 us (21%)
  starting transfers between devices  28.4 us (11%)
  other arithmetic  2.95 us (1%)
    ppermute x22, waiting for transfers between devices, swapped(): lax.ppermute(block, axis, [(i, i ^ distance) for i in range(lax.axis_size...  94.1 us
    unnamed x39, local copies, waits for them, and re-layouts  24.7 us
    ppermute x22, starting transfers between devices, swapped(): lax.ppermute(block, axis, [(i, i ^ distance) for i in range(lax.axis_size...  24.1 us
    pallas_call x2, Pallas kernels, activate(): pl.pallas_call(kernel, grid=(experts, tiles), out_shape=jax.ShapeDtypeStr...  23 us
    ppermute x8, local copies, waits for them, and re-layouts, swapped(): lax.ppermute(block, axis, [(i, i ^ distance) for i in range(lax.axis_size...  20.2 us
    pallas_call x2, Pallas kernels, combine(): pl.pallas_call(kernel, grid=(tiles,), out_shape=tuple((jax.ShapeDtypeStru...  13.6 us
    pallas_call x1, Pallas kernels, attention(): pl.pallas_call(attention_kernel, out_shape=jax.ShapeDtypeStruct((rows, wi...  12.6 us
    reshape x1, local copies, waits for them, and re-layouts, local(): out_weight.reshape(s_count, out_weight.shape[0] // s_count, columns)  6.73 us
  transfers between devices with their start and end apart: 24, of which 9 were waited for; matrix products, arithmetic and copies ran while one was open for 26% of the time, Pallas kernels for 21%

profile of v2, /device:TPU:0, one launch (start us, length us, event | category | flops | bytes accessed | tf_op | source)
XLA Modules:
  0.0 247.9 jit_solution(12982854927915016414)
XLA Ops:
  0.5 6.7 %reshape.120 = bf16[2,1024,720]{1,0,2:T(2,128)(2,1)S(1)} reshape(bf16[2048,720]{0,1:T(8,128)(2,1)} %param.17) | data formatting | bytes 5898240 | tf_op jit(solution)/shard_map/reshape | solution.py:312
  7.2 3.0 %constant_dynamic-slice_fusion.1 = bf16[1,1024,720]{1,0,2:T(2,128)(2,1)S(1)} fusion(bf16[2,1024,720]{1,0,2:T(2,128)(2,1)S(1)} %reshape.120, s32[]{:T(128)S(6)} %select_n.73), kind=kLoop, calls=%fused_computation.44 | loop fusion | bytes 2949124 | tf_op jit(solution)/shard_map/jit(dynamic_index_in_dim)/dynamic_slice | solution.py:27
  10.3 1.7 copy.140
  12.0 2.6 %collective-permute-start.3 = (bf16[1024,720]{0,1:T(8,128)(2,1)}, bf16[1024,720]{0,1:T(8,128)(2,1)}, u32[]{:S(2)}, u32[]{:S(2)}) collective-permute-start(bf16[1024,720]{0,1:T(8,128)(2,1)} %bitcast.65), channel_id=1, source_target_pairs={{0,4},{4,0},{8,12},{12,8},{1,5},{5,1},{9,13},{13,9},{2,6},{6,2},{1... | collective-permute-start | bytes 4423688 | tf_op jit(solution)/shard_map/ppermute | solution.py:23
  14.6 2.1 collective-permute-start
  16.7 2.1 collective-permute-start.1
  20.2 27.6 %collective-permute-done.3 = bf16[1024,720]{0,1:T(8,128)(2,1)} collective-permute-done((bf16[1024,720]{0,1:T(8,128)(2,1)}, bf16[1024,720]{0,1:T(8,128)(2,1)}, u32[]{:S(2)}, u32[]{:S(2)}) %collective-permute-start.3) | collective-permute-done | bytes 1474592 | tf_op jit(solution)/shard_map/ppermute | solution.py:23
  47.9 1.6 dynamic-slice_reduce_fusion
  50.1 2.8 %collective-permute-start.5 = (bf16[64,1440]{1,0:T(8,128)(2,1)}, bf16[64,1440]{1,0:T(8,128)(2,1)}, u32[]{:S(2)}, u32[]{:S(2)}) collective-permute-start(bf16[64,1440]{1,0:T(8,128)(2,1)} %bitcast.69), channel_id=1, source_target_pairs={{0,8},{4,12},{8,0},{12,4},{1,9},{5,13},{9,1},{13,5},{2,10},{6,14},... | collective-permute-start | bytes 552968 | tf_op jit(solution)/shard_map/ppermute | solution.py:23
  53.3 12.6 %attention.1.refs_0_ = bf16[128,2048]{1,0:T(8,128)(2,1)} custom-call(s32[1]{0:T(128)} %bitcast.3.first_ref, f32[32]{0:T(128)S(1)} %copy-done.9, bf16[128,2048]{1,0:T(8,128)(2,1)S(1)} %copy-done.2, bf16[128,256]{1,0:T(8,128)(2,1)S(1)} %collective-permute-done.kp_ref, bf16[128,256]{1,0:T(8,128)(2,1)S(1)} %copy-done.7, ...), custom_call_target="tpu_custom_call" | custom-call | flops 268435456 | bytes 1572864 | tf_op jit(solution)/shard_map/attention/pallas_call | solution.py:89
  66.2 4.8 %copy.105.refs_2_ = bf16[2048,720]{1,0:T(8,128)(2,1)} copy(bf16[2048,720]{0,1:T(8,128)(2,1)} %param.17) | data formatting | bytes 5898240 | tf_op args[4]
  71.1 1.7 copy.106.refs_3_
  72.8 1.1 copy-done.12
  73.9 2.0 collective-permute-start.12
  76.0 1.7 copy.107.refs_4_
  77.7 14.8 %collective-permute-done.2.refs_1_ = bf16[128,2048]{1,0:T(8,128)(2,1)} collective-permute-done((bf16[128,2048]{1,0:T(8,128)(2,1)}, bf16[128,2048]{1,0:T(8,128)(2,1)}, u32[]{:S(2)}, u32[]{:S(2)}) %collective-permute-start.2) | collective-permute-done | bytes 524320 | tf_op jit(solution)/shard_map/ppermute | solution.py:23
  92.4 4.1 %project.1 = (f32[2,2,64,720]{3,2,1,0:T(8,128)S(1)}, bf16[1,2,2,64,720]{4,3,2,1,0:T(8,128)(2,1)S(1)}) custom-call(s32[3]{0:T(128)S(1)} %pad_add_fusion.place_ref, bf16[128,2048]{1,0:T(8,128)(2,1)} %attention.1.refs_0_, bf16[128,2048]{1,0:T(8,128)(2,1)} %collective-permute-done.2.refs_1_, bf16[2048,720]{1,0:T(8,128)(2,1)} %copy.105.refs_2_, ...), custom_call_target="tpu_custom_call" | custom-call | flops 1509949440 | bytes 5898240 | tf_op jit(solution)/shard_map/project/pallas_call | solution.py:132
  97.5 1.6 collective-permute-start.6
  99.2 12.3 %copy.117 = bf16[1,2,2880,720]{3,2,1,0:T(8,128)(2,1)} copy(bf16[1,2,2880,720]{2,3,1,0:T(8,128)(2,1)} %param.20) | data formatting | bytes 16588800 | tf_op args[7]
  112.0 1.1 stack_reshape.13
  113.2 1.3 collective-permute-start.14
  114.7 2.1 collective-permute-start.7
  116.8 2.0 collective-permute-done.14
  119.7 15.1 %collective-permute-done.7.refs_1_ = bf16[2,2,64,720]{3,2,1,0:T(8,128)(2,1)S(1)} collective-permute-done((bf16[2,2,64,720]{3,2,1,0:T(8,128)(2,1)S(1)}, bf16[2,2,64,720]{3,2,1,0:T(8,128)(2,1)S(1)}, u32[]{:S(2)}, u32[]{:S(2)}) %collective-permute-start.7) | collective-permute-done | bytes 368672 | tf_op jit(solution)/shard_map/ppermute | solution.py:23
  137.2 7.7 %collective-permute-done.18.refs_1_ = bf16[2,2,64,720]{3,2,1,0:T(8,128)(2,1)S(1)} collective-permute-done((bf16[2,2,64,720]{3,2,1,0:T(8,128)(2,1)S(1)}, bf16[2,2,64,720]{3,2,1,0:T(8,128)(2,1)S(1)}, u32[]{:S(2)}, u32[]{:S(2)}) %collective-permute-start.18) | collective-permute-done | bytes 368672 | tf_op jit(solution)/shard_map/ppermute | solution.py:23
  145.4 1.3 gather_fusion.1
  146.7 1.0 copy.125.refs_0_
  147.7 1.7 collective-permute-start.9
  150.1 5.5 %collective-permute-done.19 = bf16[2,2,64,720]{3,2,0,1:T(8,128)(2,1)} collective-permute-done((bf16[2,2,64,720]{3,2,0,1:T(8,128)(2,1)}, bf16[2,2,64,720]{3,2,0,1:T(8,128)(2,1)}, u32[]{:S(2)}, u32[]{:S(2)}) %collective-permute-start.19) | collective-permute-done | bytes 368672 | tf_op jit(solution)/shard_map/ppermute | solution.py:23
  155.7 1.0 copy.126.refs_2_
  156.7 12.0 %copy.118 = bf16[1,2,2880,720]{3,2,1,0:T(8,128)(2,1)} copy(bf16[1,2,2880,720]{2,3,1,0:T(8,128)(2,1)} %collective-permute-done.10) | data formatting | bytes 16588800 | tf_op jit(solution)/shard_map/ppermute | solution.py:23
  171.5 11.5 %activate.3.refs_0_ = bf16[2,256,720]{2,1,0:T(8,128)(2,1)S(1)} custom-call(s32[1]{0:T(128)} %bitcast.16.pair_ref, bf16[2,2,64,720]{3,2,1,0:T(8,128)(2,1)S(1)} %copy.125.refs_0_, bf16[2,2,64,720]{3,2,1,0:T(8,128)(2,1)S(1)} %copy-done.4, bf16[2,2,64,720]{3,2,1,0:T(8,128)(2,1)S(1)} %copy.126.refs_2_, bf16[2,2,64,720]{3,2,1,0:T(8,128)(2,1)S(1)} %copy-done.6, ...), custom_call_target="tpu_custom_call" | custom-call | flops 4246732800 | bytes 16588800 | tf_op jit(solution)/shard_map/activate/pallas_call | solution.py:200
  183.0 1.1 copy.127
  184.6 11.5 %activate.2.refs_0_ = bf16[2,256,720]{2,1,0:T(8,128)(2,1)S(1)} custom-call(s32[1]{0:T(128)} %bitcast.16.pair_ref, bf16[2,2,64,720]{3,2,1,0:T(8,128)(2,1)S(1)} %copy.113.refs_0_, bf16[2,2,64,720]{3,2,1,0:T(8,128)(2,1)S(1)} %collective-permute-done.7.refs_1_, bf16[2,2,64,720]{3,2,1,0:T(8,128)(2,1)S(1)} %copy.120.refs_2_, ...), custom_call_target="tpu_custom_call" | custom-call | flops 4246732800 | bytes 16588800 | tf_op jit(solution)/shard_map/activate/pallas_call | solution.py:200
  196.2 1.1 copy.121
  197.3 1.5 collective-permute-start.11
  200.4 1.1 broadcast_select_fusion
  201.9 1.1 stack_reshape.14
  203.3 1.1 stack_reshape.15
  204.4 1.4 copy.129.refs_1_
  205.8 6.7 %combine.3 = (bf16[2,64,1440]{2,1,0:T(8,128)(2,1)S(1)}, bf16[2,64,1440]{2,1,0:T(8,128)(2,1)S(1)}) custom-call(s32[1]{0:T(128)} %bitcast.t_ref, bf16[2,256,720]{2,1,0:T(8,128)(2,1)S(1)} %activate.3.refs_0_, bf16[2,256,720]{2,1,0:T(8,128)(2,1)S(1)} %copy.129.refs_1_, f32[256,2]{1,0:T(8,128)S(1)} %bitcast.71, bf16[2,720,1440]{2,1,0:T(8,128)(2,1)} %bitcast.76, ...), custom_call_target="tpu_custom_call" | custom-call | flops 2123366400 | bytes 8294400 | tf_op jit(solution)/shard_map/combine/pallas_call | solution.py:249
  212.5 2.1 collective-permute-start.22
  214.6 2.0 collective-permute-start.23
  216.6 1.4 copy.124.refs_1_
  218.0 6.8 %combine.2 = (bf16[2,64,1440]{2,1,0:T(8,128)(2,1)S(1)}, bf16[2,64,1440]{2,1,0:T(8,128)(2,1)S(1)}) custom-call(s32[1]{0:T(128)} %bitcast.t_ref, bf16[2,256,720]{2,1,0:T(8,128)(2,1)S(1)} %activate.2.refs_0_, bf16[2,256,720]{2,1,0:T(8,128)(2,1)S(1)} %copy.124.refs_1_, f32[256,2]{1,0:T(8,128)S(1)} %bitcast.70, bf16[2,720,1440]{2,1,0:T(8,128)(2,1)} %bitcast.77, ...), custom_call_target="tpu_custom_call" | custom-call | flops 2123366400 | bytes 8294400 | tf_op jit(solution)/shard_map/combine/pallas_call | solution.py:249
  224.9 1.0 collective-permute-start.16
  226.1 8.0 %collective-permute-done.23.refs_3_ = bf16[2,64,1440]{2,1,0:T(8,128)(2,1)S(1)} collective-permute-done((bf16[2,64,1440]{2,1,0:T(8,128)(2,1)S(1)}, bf16[2,64,1440]{2,1,0:T(8,128)(2,1)S(1)}, u32[]{:S(2)}, u32[]{:S(2)}) %collective-permute-start.23) | collective-permute-done | bytes 368672 | tf_op jit(solution)/shard_map/ppermute | solution.py:23
  234.1 12.6 %collective-permute-done.16.refs_1_ = bf16[2,64,1440]{2,1,0:T(8,128)(2,1)S(1)} collective-permute-done((bf16[2,64,1440]{2,1,0:T(8,128)(2,1)S(1)}, bf16[2,64,1440]{2,1,0:T(8,128)(2,1)S(1)}, u32[]{:S(2)}, u32[]{:S(2)}) %collective-permute-start.16) | collective-permute-done | bytes 368672 | tf_op jit(solution)/shard_map/ppermute | solution.py:23
  (107 shorter events, 16.2 us)
Async XLA Ops:
  0.0 156.7 %collective-permute-start.10 = (bf16[1,2,2880,720]{2,3,1,0:T(8,128)(2,1)}, bf16[1,2,2880,720]{2,3,1,0:T(8,128)(2,1)}, u32[]{:S(2)}, u32[]{:S(2)}) collective-permute-start(bf16[1,2,2880,720]{2,3,1,0:T(8,128)(2,1)} %param.20), channel_id=1, source_target_pairs={{0,1},{1,0},{2,3},{3,2},{4,5},{5,4},{6,7},{7,6},{8,9},{9,8},{10,11... | collective-permute-start | bytes 24883208 | tf_op jit(solution)/shard_map/ppermute | solution.py:23
  10.2 4.3 %copy-start.7 = (bf16[128,256]{1,0:T(8,128)(2,1)S(1)}, bf16[128,256]{1,0:T(8,128)(2,1)}, u32[]{:S(2)}) copy-start(bf16[128,256]{1,0:T(8,128)(2,1)} %k_ref.1) | copy-start | bytes 196612
  10.3 6.5 %copy-start.8 = (bf16[128,256]{1,0:T(8,128)(2,1)S(1)}, bf16[128,256]{1,0:T(8,128)(2,1)}, u32[]{:S(2)}) copy-start(bf16[128,256]{1,0:T(8,128)(2,1)} %v_ref.1) | copy-start | bytes 196612
  10.3 8.7 %copy-start.13 = (bf16[128,2880]{0,1:T(8,128)(2,1)S(1)}, bf16[128,2880]{0,1:T(8,128)(2,1)}, u32[]{:S(2)}) copy-start(bf16[128,2880]{0,1:T(8,128)(2,1)} %param.18) | copy-start | bytes 2211844
  12.0 40.9 %copy-start.15 = (s32[128,4]{0,1:T(4,128)S(1)}, s32[128,4]{0,1:T(4,128)}, u32[]{:S(2)}) copy-start(s32[128,4]{0,1:T(4,128)} %param.23) | copy-start | bytes 6148
  12.0 41.3 %copy-start.2 = (bf16[128,2048]{1,0:T(8,128)(2,1)S(1)}, bf16[128,2048]{1,0:T(8,128)(2,1)}, u32[]{:S(2)}) copy-start(bf16[128,2048]{1,0:T(8,128)(2,1)} %q_ref.1) | copy-start | bytes 1572868
  12.0 41.3 %copy-start.9 = (f32[32]{0:T(128)S(1)}, f32[32]{0:T(128)}, u32[]{:S(2)}) copy-start(f32[32]{0:T(128)} %sink_ref.1) | copy-start | bytes 388
  12.0 35.8 %collective-permute-start.3 = (bf16[1024,720]{0,1:T(8,128)(2,1)}, bf16[1024,720]{0,1:T(8,128)(2,1)}, u32[]{:S(2)}, u32[]{:S(2)}) collective-permute-start(bf16[1024,720]{0,1:T(8,128)(2,1)} %bitcast.65), channel_id=1, source_target_pairs={{0,4},{4,0},{8,12},{12,8},{1,5},{5,1},{9,13},{13,9},{2,6},{6,2},{1... | collective-permute-start | bytes 4423688 | tf_op jit(solution)/shard_map/ppermute | solution.py:23
  14.6 38.4 %collective-permute-start = (bf16[128,256]{1,0:T(8,128)(2,1)S(1)}, bf16[128,256]{1,0:T(8,128)(2,1)S(1)}, u32[]{:S(2)}, u32[]{:S(2)}) collective-permute-start(bf16[128,256]{1,0:T(8,128)(2,1)S(1)} %copy-done.7), channel_id=1, source_target_pairs={{0,1},{1,4},{4,5},{5,8},{8,9},{9,12},{12,13},{2,3},{3,6},{6,7},{7,... | collective-permute-start | bytes 196616 | tf_op jit(solution)/shard_map/ppermute | solution.py:19
  16.7 36.5 %collective-permute-start.1 = (bf16[128,256]{1,0:T(8,128)(2,1)S(1)}, bf16[128,256]{1,0:T(8,128)(2,1)S(1)}, u32[]{:S(2)}, u32[]{:S(2)}) collective-permute-start(bf16[128,256]{1,0:T(8,128)(2,1)S(1)} %copy-done.8), channel_id=1, source_target_pairs={{0,1},{1,4},{4,5},{5,8},{8,9},{9,12},{12,13},{2,3},{3,6},{6,7},{7,... | collective-permute-start | bytes 196616 | tf_op jit(solution)/shard_map/ppermute | solution.py:19
  47.9 24.9 %collective-permute-start.4 = (bf16[1024,720]{0,1:T(8,128)(2,1)}, bf16[1024,720]{0,1:T(8,128)(2,1)S(1)}, u32[]{:S(2)}, u32[]{:S(2)}) collective-permute-start(bf16[1024,720]{0,1:T(8,128)(2,1)} %collective-permute-done.3), channel_id=1, source_target_pairs={{0,1},{1,0},{2,3},{3,2},{4,5},{5,4},{6,7},{7,6},{8,9},{9,8},{10,11... | collective-permute-start | bytes 4423688 | tf_op jit(solution)/shard_map/ppermute | solution.py:23
  50.1 61.9 %collective-permute-start.5 = (bf16[64,1440]{1,0:T(8,128)(2,1)}, bf16[64,1440]{1,0:T(8,128)(2,1)}, u32[]{:S(2)}, u32[]{:S(2)}) collective-permute-start(bf16[64,1440]{1,0:T(8,128)(2,1)} %bitcast.69), channel_id=1, source_target_pairs={{0,8},{4,12},{8,0},{12,4},{1,9},{5,13},{9,1},{13,5},{2,10},{6,14},... | collective-permute-start | bytes 552968 | tf_op jit(solution)/shard_map/ppermute | solution.py:23
  53.0 152.8 %collective-permute-start.15 = (bf16[1,1440,1440]{2,1,0:T(8,128)(2,1)}, bf16[1,1440,1440]{2,1,0:T(8,128)(2,1)}, u32[]{:S(2)}, u32[]{:S(2)}) collective-permute-start(bf16[1,1440,1440]{2,1,0:T(8,128)(2,1)} %param.21), channel_id=1, source_target_pairs={{0,1},{1,0},{2,3},{3,2},{4,5},{5,4},{6,7},{7,6},{8,9},{9,8},{10,11... | collective-permute-start | bytes 12441608 | tf_op jit(solution)/shard_map/ppermute | solution.py:23
  65.9 26.6 %collective-permute-start.2 = (bf16[128,2048]{1,0:T(8,128)(2,1)}, bf16[128,2048]{1,0:T(8,128)(2,1)}, u32[]{:S(2)}, u32[]{:S(2)}) collective-permute-start(bf16[128,2048]{1,0:T(8,128)(2,1)} %attention.1.refs_0_), channel_id=1, source_target_pairs={{0,8},{4,12},{8,0},{12,4},{1,9},{5,13},{9,1},{13,5},{2,10},{6,14},... | collective-permute-start | bytes 1572872 | tf_op jit(solution)/shard_map/ppermute | solution.py:23
  66.2 4.8 %copy-start.16 = (s32[128,4]{0,1:T(4,128)S(1)}, s32[128,4]{0,1:T(4,128)}, u32[]{:S(2)}) copy-start(s32[128,4]{0,1:T(4,128)} %param.22) | copy-start | bytes 6148
  66.2 4.8 %copy-start.14 = (f32[2880]{0:T(1024)S(1)}, f32[2880]{0:T(1024)}, u32[]{:S(2)}) copy-start(f32[2880]{0:T(1024)} %param.19) | copy-start | bytes 34564
  72.8 1.1 copy-start.12
  73.9 40.7 %collective-permute-start.12 = (f32[128,8]{0,1:T(8,128)S(1)}, f32[128,8]{0,1:T(8,128)S(1)}, u32[]{:S(2)}, u32[]{:S(2)}) collective-permute-start(f32[128,8]{0,1:T(8,128)S(1)} %select_reduce_fusion.1), channel_id=1, source_target_pairs={{0,4},{4,0},{8,12},{12,8},{1,5},{5,1},{9,13},{13,9},{2,6},{6,2},{1... | collective-permute-start | bytes 12296 | tf_op jit(solution)/shard_map/ppermute | solution.py:23
  96.5 0.9 copy-start
  97.5 15.7 %collective-permute-start.6 = (bf16[2,2,64,720]{3,2,0,1:T(8,128)(2,1)S(1)}, bf16[2,2,64,720]{3,2,0,1:T(8,128)(2,1)S(1)}, u32[]{:S(2)}, u32[]{:S(2)}) collective-permute-start(bf16[2,2,64,720]{3,2,0,1:T(8,128)(2,1)S(1)} %bitcast.82), channel_id=1, source_target_pairs={{0,2},{2,0},{1,3},{3,1},{4,6},{6,4},{5,7},{7,5},{8,10},{10,8},{9,1... | collective-permute-start | bytes 1105928 | tf_op jit(solution)/shard_map/ppermute | solution.py:23
  99.2 15.3 %copy-start.1 = (f32[2,2,64,720]{3,2,1,0:T(8,128)S(1)}, f32[2,2,64,720]{3,2,1,0:T(8,128)}, u32[]{:S(2)}) copy-start(f32[2,2,64,720]{3,2,1,0:T(8,128)} %copy-done) | copy-start | bytes 2211844
  112.0 4.8 %collective-permute-start.13 = (f32[128,8]{0,1:T(8,128)S(1)}, f32[128,8]{0,1:T(8,128)S(1)}, u32[]{:S(2)}, u32[]{:S(2)}) collective-permute-start(f32[128,8]{0,1:T(8,128)S(1)} %select_reduce_fusion.1), channel_id=1, source_target_pairs={{0,8},{4,12},{8,0},{12,4},{1,9},{5,13},{9,1},{13,5},{2,10},{6,14},... | collective-permute-start | bytes 12296 | tf_op jit(solution)/shard_map/ppermute | solution.py:23
  113.2 5.6 %collective-permute-start.14 = (f32[128,8]{0,1:T(8,128)S(1)}, f32[128,8]{0,1:T(8,128)S(1)}, u32[]{:S(2)}, u32[]{:S(2)}) collective-permute-start(f32[128,8]{0,1:T(8,128)S(1)} %select_reduce_fusion.1), channel_id=1, source_target_pairs={{0,12},{4,8},{8,4},{12,0},{1,13},{5,9},{9,5},{13,1},{2,14},{6,10},... | collective-permute-start | bytes 12296 | tf_op jit(solution)/shard_map/ppermute | solution.py:23
  114.7 20.1 %collective-permute-start.7 = (bf16[2,2,64,720]{3,2,1,0:T(8,128)(2,1)S(1)}, bf16[2,2,64,720]{3,2,1,0:T(8,128)(2,1)S(1)}, u32[]{:S(2)}, u32[]{:S(2)}) collective-permute-start(bf16[2,2,64,720]{3,2,1,0:T(8,128)(2,1)S(1)} %copy.113.refs_0_), channel_id=1, source_target_pairs={{0,8},{4,12},{8,0},{12,4},{1,9},{5,13},{9,1},{13,5},{2,10},{6,14},... | collective-permute-start | bytes 1105928 | tf_op jit(solution)/shard_map/ppermute | solution.py:23
  119.6 16.6 %collective-permute-start.17 = (bf16[2,2,64,720]{3,2,0,1:T(8,128)(2,1)S(1)}, bf16[2,2,64,720]{3,2,0,1:T(8,128)(2,1)}, u32[]{:S(2)}, u32[]{:S(2)}) collective-permute-start(bf16[2,2,64,720]{3,2,0,1:T(8,128)(2,1)S(1)} %fusion.2), channel_id=1, source_target_pairs={{0,4},{4,0},{8,12},{12,8},{1,5},{5,1},{9,13},{13,9},{2,6},{6,2},{1... | collective-permute-start | bytes 1105928 | tf_op jit(solution)/shard_map/ppermute | solution.py:23
  134.8 10.1 %collective-permute-start.18 = (bf16[2,2,64,720]{3,2,1,0:T(8,128)(2,1)S(1)}, bf16[2,2,64,720]{3,2,1,0:T(8,128)(2,1)S(1)}, u32[]{:S(2)}, u32[]{:S(2)}) collective-permute-start(bf16[2,2,64,720]{3,2,1,0:T(8,128)(2,1)S(1)} %collective-permute-done.7.refs_1_), channel_id=1, source_target_pairs={{0,4},{4,0},{8,12},{12,8},{1,5},{5,1},{9,13},{13,9},{2,6},{6,2},{1... | collective-permute-start | bytes 1105928 | tf_op jit(solution)/shard_map/ppermute | solution.py:23
  135.0 12.7 %collective-permute-start.8 = (bf16[2,2,64,720]{3,2,0,1:T(8,128)(2,1)S(1)}, bf16[2,2,64,720]{3,2,0,1:T(8,128)(2,1)S(1)}, u32[]{:S(2)}, u32[]{:S(2)}) collective-permute-start(bf16[2,2,64,720]{3,2,0,1:T(8,128)(2,1)S(1)} %fusion.2), channel_id=1, source_target_pairs={{0,2},{2,0},{1,3},{3,1},{4,6},{6,4},{5,7},{7,5},{8,10},{10,8},{9,1... | collective-permute-start | bytes 1105928 | tf_op jit(solution)/shard_map/ppermute | solution.py:23
  136.2 19.5 %collective-permute-start.19 = (bf16[2,2,64,720]{3,2,0,1:T(8,128)(2,1)}, bf16[2,2,64,720]{3,2,0,1:T(8,128)(2,1)}, u32[]{:S(2)}, u32[]{:S(2)}) collective-permute-start(bf16[2,2,64,720]{3,2,0,1:T(8,128)(2,1)} %collective-permute-done.17), channel_id=1, source_target_pairs={{0,2},{2,0},{1,3},{3,1},{4,6},{6,4},{5,7},{7,5},{8,10},{10,8},{9,1... | collective-permute-start | bytes 1105928 | tf_op jit(solution)/shard_map/ppermute | solution.py:23
  144.9 23.8 %copy-start.3 = (bf16[2,2,64,720]{3,2,1,0:T(8,128)(2,1)}, bf16[2,2,64,720]{3,2,1,0:T(8,128)(2,1)S(1)}, u32[]{:S(2)}) copy-start(bf16[2,2,64,720]{3,2,1,0:T(8,128)(2,1)S(1)} %collective-permute-done.18.refs_1_) | copy-start | bytes 1105924
  144.9 23.8 %collective-permute-start.20 = (bf16[2,2,64,720]{3,2,1,0:T(8,128)(2,1)S(1)}, bf16[2,2,64,720]{3,2,1,0:T(8,128)(2,1)S(1)}, u32[]{:S(2)}, u32[]{:S(2)}) collective-permute-start(bf16[2,2,64,720]{3,2,1,0:T(8,128)(2,1)S(1)} %collective-permute-done.18.refs_1_), channel_id=1, source_target_pairs={{0,2},{2,0},{1,3},{3,1},{4,6},{6,4},{5,7},{7,5},{8,10},{10,8},{9,1... | collective-permute-start | bytes 1105928 | tf_op jit(solution)/shard_map/ppermute | solution.py:23
  147.7 36.9 %collective-permute-start.9 = (bf16[2,2,64,720]{3,2,1,0:T(8,128)(2,1)S(1)}, bf16[2,2,64,720]{3,2,1,0:T(8,128)(2,1)S(1)}, u32[]{:S(2)}, u32[]{:S(2)}) collective-permute-start(bf16[2,2,64,720]{3,2,1,0:T(8,128)(2,1)S(1)} %collective-permute-done.7.refs_1_), channel_id=1, source_target_pairs={{0,2},{2,0},{1,3},{3,1},{4,6},{6,4},{5,7},{7,5},{8,10},{10,8},{9,1... | collective-permute-start | bytes 1105928 | tf_op jit(solution)/shard_map/ppermute | solution.py:23
  168.7 0.7 copy-start.5
  169.5 1.0 copy-start.4
  170.5 1.0 copy-start.6
  184.1 20.2 %collective-permute-start.21 = (bf16[2,256,720]{1,2,0:T(8,128)(2,1)}, bf16[2,256,720]{1,2,0:T(8,128)(2,1)}, u32[]{:S(2)}, u32[]{:S(2)}) collective-permute-start(bf16[2,256,720]{1,2,0:T(8,128)(2,1)} %copy.127), channel_id=1, source_target_pairs={{0,2},{2,0},{1,3},{3,1},{4,6},{6,4},{5,7},{7,5},{8,10},{10,8},{9,1... | collective-permute-start | bytes 2211848 | tf_op jit(solution)/shard_map/ppermute | solution.py:23
  197.3 19.3 %collective-permute-start.11 = (bf16[2,256,720]{1,2,0:T(8,128)(2,1)}, bf16[2,256,720]{1,2,0:T(8,128)(2,1)}, u32[]{:S(2)}, u32[]{:S(2)}) collective-permute-start(bf16[2,256,720]{1,2,0:T(8,128)(2,1)} %copy.121), channel_id=1, source_target_pairs={{0,2},{2,0},{1,3},{3,1},{4,6},{6,4},{5,7},{7,5},{8,10},{10,8},{9,1... | collective-permute-start | bytes 2211848 | tf_op jit(solution)/shard_map/ppermute | solution.py:23
  212.5 13.6 %collective-permute-start.22 = (bf16[2,64,1440]{2,1,0:T(8,128)(2,1)S(1)}, bf16[2,64,1440]{2,1,0:T(8,128)(2,1)S(1)}, u32[]{:S(2)}, u32[]{:S(2)}) collective-permute-start(bf16[2,64,1440]{2,1,0:T(8,128)(2,1)S(1)} %get-tuple-element.16), channel_id=1, source_target_pairs={{0,4},{4,0},{8,12},{12,8},{1,5},{5,1},{9,13},{13,9},{2,6},{6,2},{1... | collective-permute-start | bytes 1105928 | tf_op jit(solution)/shard_map/ppermute | solution.py:23
  214.6 19.5 %collective-permute-start.23 = (bf16[2,64,1440]{2,1,0:T(8,128)(2,1)S(1)}, bf16[2,64,1440]{2,1,0:T(8,128)(2,1)S(1)}, u32[]{:S(2)}, u32[]{:S(2)}) collective-permute-start(bf16[2,64,1440]{2,1,0:T(8,128)(2,1)S(1)} %get-tuple-element.17), channel_id=1, source_target_pairs={{0,12},{4,8},{8,4},{12,0},{1,13},{5,9},{9,5},{13,1},{2,14},{6,10},... | collective-permute-start | bytes 1105928 | tf_op jit(solution)/shard_map/ppermute | solution.py:23
  218.0 7.9 %copy-start.10 = (bf16[1,64,2880]{2,1,0:T(8,128)(2,1)S(1)}, bf16[1,64,2880]{2,1,0:T(8,128)(2,1)}, u32[]{:S(2)}) copy-start(bf16[1,64,2880]{2,1,0:T(8,128)(2,1)} %stack_reshape.14) | copy-start | bytes 1105924
  218.0 7.9 %copy-start.11 = (bf16[1,64,2880]{2,1,0:T(8,128)(2,1)S(1)}, bf16[1,64,2880]{2,1,0:T(8,128)(2,1)}, u32[]{:S(2)}) copy-start(bf16[1,64,2880]{2,1,0:T(8,128)(2,1)} %stack_reshape.15) | copy-start | bytes 1105924
  224.9 21.8 %collective-permute-start.16 = (bf16[2,64,1440]{2,1,0:T(8,128)(2,1)S(1)}, bf16[2,64,1440]{2,1,0:T(8,128)(2,1)S(1)}, u32[]{:S(2)}, u32[]{:S(2)}) collective-permute-start(bf16[2,64,1440]{2,1,0:T(8,128)(2,1)S(1)} %get-tuple-element.15), channel_id=1, source_target_pairs={{0,8},{4,12},{8,0},{12,4},{1,9},{5,13},{9,1},{13,5},{2,10},{6,14},... | collective-permute-start | bytes 1105928 | tf_op jit(solution)/shard_map/ppermute | solution.py:23

commit v3 on v0

v3 whole, which is shorter than its diff:
```python
import jax
import jax.numpy as jnp
from jax import lax
from jax.experimental import pallas as pl
from jax.experimental.pallas import tpu as pltpu
from jax.sharding import PartitionSpec as P

D = 2880
HD = 64
WIN = 128
TOP = 4
VMEM_BYTES = 48 * 1024 * 1024


def shifted(block, axis, distance):
    devices = range(lax.axis_size(axis))
    route = [(i - distance, i) for i in devices if i - distance in devices]
    return lax.ppermute(block, axis, route)


def swapped(block, axis, distance):
    return lax.ppermute(block, axis, [(i, i ^ distance) for i in range(lax.axis_size(axis))])


def picked(blocks, index, axis):
    return lax.dynamic_index_in_dim(blocks, index, axis, keepdims=False)


def in_vmem(count):
    return [pl.BlockSpec(memory_space=pltpu.VMEM)] * count


def in_smem():
    return pl.BlockSpec(memory_space=pltpu.SMEM)


def cost(flops, bytes_accessed):
    return pl.CostEstimate(flops=flops, bytes_accessed=bytes_accessed, transcendentals=0)


def dot(left, right):
    return jnp.dot(left, right, preferred_element_type=jnp.float32)


def tile_of(size):
    return size // 3 if size % 48 == 0 else size


def aligned(size):
    return size % 16 == 0


def params():
    return pltpu.CompilerParams(vmem_limit_bytes=VMEM_BYTES)


def attention_kernel(first_ref, sink_ref, q_ref, kp_ref, k_ref, vp_ref, v_ref, out_ref):
    rows = q_ref.shape[0]
    kv_count = k_ref.shape[1] // HD
    pairs = q_ref.shape[1] // (2 * HD * kv_count)
    key = lax.broadcasted_iota(jnp.int32, (rows, rows), 0)
    query = lax.broadcasted_iota(jnp.int32, (rows, rows), 1)
    before = key > query
    shut = before & (first_ref[0] == 1)
    blank = jnp.zeros((2 * rows, HD), jnp.bfloat16)
    values = jnp.concatenate(
        [ref[...].astype(jnp.float32).T.astype(jnp.bfloat16) for ref in (vp_ref, v_ref)], axis=1
    )
    for g in range(kv_count):
        head = slice(g * HD, (g + 1) * HD)
        keys = jnp.concatenate([kp_ref[:, head], k_ref[:, head]], axis=0) * jnp.bfloat16(HD ** (-0.5))
        keys = jnp.concatenate(
            [jnp.concatenate([keys, blank], axis=1), jnp.concatenate([blank, keys], axis=1)], axis=0
        )
        for i in range(pairs):
            start = (g * pairs + i) * 2 * HD
            products = lax.dot_general(
                keys,
                q_ref[:, start : start + 2 * HD],
                (((1,), (1,)), ((), ())),
                preferred_element_type=jnp.float32,
            )
            weights = []
            for side in range(2):
                sink = sink_ref[(g * pairs + i) * 2 + side]
                part = products[side * 2 * rows : (side + 1) * 2 * rows]
                scores = jnp.where(before, part[:rows], part[rows:])
                scores = jnp.where(shut, -1e30, scores)
                largest = jnp.maximum(jnp.max(scores, axis=0, keepdims=True), sink)
                numerator = jnp.exp(scores - largest)
                denominator = jnp.sum(numerator, axis=0, keepdims=True) + jnp.exp(sink - largest)
                numerator = numerator * (1.0 / denominator)
                weights.append(
                    jnp.concatenate(
                        [
                            jnp.where(before, numerator, 0.0).astype(jnp.bfloat16),
                            jnp.where(before, 0.0, numerator).astype(jnp.bfloat16),
                        ],
                        axis=0,
                    )
                )
            result = dot(values[head], jnp.concatenate(weights, axis=1)).astype(jnp.bfloat16)
            out_ref[start : start + HD, :] = result[:, :rows]
            out_ref[start + HD : start + 2 * HD, :] = result[:, rows:]


def attention(queries, key_rows, value_rows, sink_logits, first):
    rows, width = queries.shape
    earlier_keys = shifted(key_rows, ("ep", "sub"), 1)
    earlier_values = shifted(value_rows, ("ep", "sub"), 1)
    return pl.pallas_call(
        attention_kernel,
        out_shape=jax.ShapeDtypeStruct((width, rows), jnp.bfloat16),
        in_specs=[in_smem(), in_smem()] + in_vmem(5),
        out_specs=in_vmem(1)[0],
        compiler_params=params(),
        cost_estimate=cost(8 * rows * rows * width, 6 * rows * width),
        name="attention",
    )(first, sink_logits, queries, earlier_keys, key_rows, earlier_values, value_rows)


def project(attended, out_weight, near_weights, t, member, s, t_count):
    slots = len(attended)
    width, rows = attended[0].shape
    columns = out_weight.shape[0]
    shares = len(near_weights)
    pair = 2
    depth = width // shares

    def kernel(place_ref, *refs):
        attended_refs = refs[:slots]
        weight_ref = refs[slots]
        near_refs = refs[slots + 1 : slots + 1 + shares]
        kept_ref, sent_ref, total = refs[slots + 1 + shares :]
        t, member, s = place_ref[0], place_ref[1], place_ref[2]
        for i in range(pair):
            if i == 0:
                result = dot(weight_ref[...], jnp.concatenate([ref[...] for ref in attended_refs], axis=1))
            else:
                result = 0.0
                for u in range(shares):
                    span = pl.ds(pl.multiple_of((s ^ u) * depth, 128), depth)
                    block = jnp.concatenate([ref[span, :] for ref in attended_refs], axis=1)
                    result = result + dot(near_refs[u][...], block)
            total[...] = result
            for m in range(t_count):
                block = total[:, pl.ds(pl.multiple_of((t ^ m) * rows, 128), rows)]
                if m == 0:
                    kept_ref[member ^ i] = block
                else:
                    sent_ref[m - 1, member ^ i] = block.astype(jnp.bfloat16)

    return pl.pallas_call(
        kernel,
        out_shape=(
            jax.ShapeDtypeStruct((pair, columns, rows), jnp.float32),
            jax.ShapeDtypeStruct((t_count - 1, pair, columns, rows), jnp.bfloat16),
        ),
        in_specs=[in_smem()] + in_vmem(slots + 1 + shares),
        out_specs=tuple(in_vmem(2)),
        scratch_shapes=[pltpu.VMEM((columns, slots * rows), jnp.float32)],
        compiler_params=params(),
        cost_estimate=cost(4 * slots * rows * width * columns, 4 * width * columns),
        name="project",
    )(jnp.stack([t, member, s]).astype(jnp.int32), *attended, out_weight, *near_weights)


def activate(pieces, gain_table, weights, pair, t):
    slots = len(pieces)
    depth, rows = pieces[0][0].shape
    lanes = slots * rows
    experts = len(weights)
    units = weights[0].shape[1]
    tile = tile_of(units)
    tiles = units // tile

    def kernel(place_ref, *refs):
        piece_refs = refs[: slots * slots]
        table_ref = refs[slots * slots]
        weight_refs = refs[slots * slots + 1 : slots * slots + 1 + experts]
        out_ref, rows_ref, scale_ref, stage_ref = refs[slots * slots + 1 + experts :]
        e, step = pl.program_id(0), pl.program_id(1)

        @pl.when((e == 0) & (step == 0))
        def _():
            for m in range(slots):
                for r in range(slots):
                    lane = pl.ds(pl.multiple_of((place_ref[1] ^ r ^ m) * rows, 128), rows)
                    index = place_ref[0] ^ r
                    block = piece_refs[m * slots + r][...]
                    if aligned(depth):
                        rows_ref[pl.ds(pl.multiple_of(index * depth, 16), depth), lane] = block
                    else:
                        stage_ref[index, :, lane] = block
            if not aligned(depth):
                for index in range(slots):
                    rows_ref[index * depth : (index + 1) * depth, :] = stage_ref[index]
            plain = rows_ref[...].astype(jnp.float32)
            square = jnp.sum(dot(table_ref[...], (plain * plain).astype(jnp.bfloat16)), axis=0, keepdims=True)
            scale_ref[...] = lax.rsqrt(square / D + 1e-05)

        for index in range(experts):

            @pl.when(e == index)
            def _():
                gate = dot(weight_refs[index][0], rows_ref[...]) * scale_ref[...]
                up = dot(weight_refs[index][1], rows_ref[...]) * scale_ref[...]
                out_ref[0] = ((up + 1.0) * gate * jax.nn.sigmoid(1.702 * gate)).astype(jnp.bfloat16)

    def weight_spec(index):
        def place(e, step):
            return (0, jnp.where(e == index, step, jnp.where(e < index, 0, tiles - 1)), 0)

        return pl.BlockSpec((2, tile, D), place)

    flat = [piece for part in pieces for piece in part]
    return pl.pallas_call(
        kernel,
        grid=(experts, tiles),
        out_shape=jax.ShapeDtypeStruct((experts, units, lanes), jnp.bfloat16),
        in_specs=[in_smem()] + in_vmem(len(flat) + 1) + [weight_spec(index) for index in range(experts)],
        out_specs=pl.BlockSpec((1, tile, lanes), lambda e, step: (e, step, 0)),
        scratch_shapes=[
            pltpu.VMEM((D, lanes), jnp.bfloat16),
            pltpu.VMEM((1, lanes), jnp.float32),
            pltpu.VMEM((1, 16, 128) if aligned(depth) else (slots, depth, lanes), jnp.bfloat16),
        ],
        compiler_params=params(),
        cost_estimate=cost(4 * experts * lanes * D * units, 4 * experts * D * units),
        name="activate",
    )(jnp.stack([pair, t]).astype(jnp.int32), *flat, gain_table, *weights)


def combine(activated, share, weights, t, slots):
    t_count = len(activated)
    experts, units, lanes = activated[0].shape
    width = weights[0].shape[0]
    rows = lanes // slots
    tile = tile_of(width)
    tiles = width // tile

    def kernel(t_ref, *refs):
        activated_refs = refs[:t_count]
        share_ref = refs[t_count]
        weight_refs = refs[t_count + 1 : t_count + 1 + experts]
        *out_refs, all_ref, stage_ref = refs[t_count + 1 + experts :]

        @pl.when(pl.program_id(0) == 0)
        def _():
            for u in range(t_count):
                index = t_ref[0] ^ u
                if aligned(units):
                    all_ref[:, pl.ds(pl.multiple_of(index * units, 16), units), :] = activated_refs[u][...]
                else:
                    stage_ref[index] = activated_refs[u][...]
            if not aligned(units):
                for index in range(t_count):
                    all_ref[:, index * units : (index + 1) * units, :] = stage_ref[index]

        total = 0.0
        for e in range(experts):
            result = dot(weight_refs[e][...], all_ref[e]).astype(jnp.bfloat16).astype(jnp.float32)
            total = total + share_ref[e : e + 1, :] * result
        for j in range(slots):
            out_refs[j][...] = total[:, j * rows : (j + 1) * rows].astype(jnp.bfloat16)

    return pl.pallas_call(
        kernel,
        grid=(tiles,),
        out_shape=tuple(jax.ShapeDtypeStruct((width, rows), jnp.bfloat16) for _ in range(slots)),
        in_specs=[in_smem()]
        + in_vmem(t_count + 1)
        + [pl.BlockSpec((tile, t_count * units), lambda step: (step, 0))] * experts,
        out_specs=tuple(pl.BlockSpec((tile, rows), lambda step: (step, 0)) for _ in range(slots)),
        scratch_shapes=[
            pltpu.VMEM((experts, t_count * units, lanes), jnp.bfloat16),
            pltpu.VMEM((1, 1, 16, 128) if aligned(units) else (t_count, experts, units, lanes), jnp.bfloat16),
        ],
        compiler_params=params(),
        cost_estimate=cost(
            2 * experts * lanes * t_count * units * width, 2 * experts * t_count * units * width
        ),
        name="combine",
    )(t.reshape(1), *activated, share, *weights)


def local(
    queries,
    key_rows,
    value_rows,
    sink_logits,
    out_weight,
    residual,
    norm_gain,
    expert_in,
    expert_out,
    routes,
    route_scores,
):
    rows = queries.shape[0]
    z_count, t_count, s_count = lax.axis_size("ep"), lax.axis_size("tp"), lax.axis_size("sub")
    z, t, s = (lax.axis_index(name).astype(jnp.int32) for name in ("ep", "tp", "sub"))
    columns = out_weight.shape[1]
    width = expert_out.shape[2]
    slots = t_count
    group = z_count // slots
    pair = z // group

    first = (lax.axis_index(("ep", "sub")) == 0).astype(jnp.int32).reshape(1)
    attended = attention(queries, key_rows, value_rows, sink_logits, first)

    out_weight = out_weight.T
    depth = out_weight.shape[1] // s_count
    near = swapped(lax.dynamic_slice_in_dim(out_weight, s * depth, depth, 1), "ep", 1)
    near, attended = lax.optimization_barrier((near, attended))
    near_weights = [near] + [swapped(near, "sub", u) for u in range(1, s_count)]

    expert_in = expert_in[0].transpose(0, 2, 1)
    expert_out = expert_out[0].T
    experts_in = [expert_in] + [swapped(expert_in, "sub", e) for e in range(1, s_count)]
    experts_out = [expert_out] + [swapped(expert_out, "sub", e) for e in range(1, s_count)]

    residual = residual.T.reshape(slots, group * columns, rows)
    route = [
        (i * t_count + k, (i ^ (group * k)) * t_count + k) for i in range(z_count) for k in range(t_count)
    ]
    residual = lax.ppermute(picked(residual, pair ^ t, 0), ("ep", "tp"), route)

    expert_count = z_count * s_count
    route_float = route_scores.T.astype(jnp.float32)
    mix_share = route_float / jnp.sum(route_float, axis=0, keepdims=True)
    experts = jnp.arange(expert_count, dtype=jnp.int32)
    named = routes.T[:, None, :] == experts[None, :, None]
    table = jnp.sum(jnp.where(named, mix_share[:, None, :], 0.0), axis=0)
    tables = jnp.stack([table] + [swapped(table, "ep", d) for d in range(1, z_count)])
    tables = jnp.take(tables, jnp.stack([z * s_count + (s ^ e) for e in range(s_count)]), axis=1)
    tables = tables.reshape(slots, group, s_count, rows)

    gathered = [attended] + [swapped(attended, "ep", group * j) for j in range(1, slots)]
    hidden, sent = project(gathered, out_weight, near_weights, t, z % group, s, t_count)
    hidden = hidden.reshape(group * columns, rows) + residual.astype(jnp.float32)
    for m in range(1, t_count):
        received = swapped(sent[m - 1].reshape(group * columns, rows), "tp", m)
        hidden = hidden + received.astype(jnp.float32)
    gain_part = picked(norm_gain.reshape(slots, group * columns), pair, 0)
    scaled = (hidden * gain_part[:, None]).astype(jnp.bfloat16)

    own = {0: scaled}
    distance = z_count // 2
    while distance:
        own.update({d + distance: swapped(own[d], "ep", distance) for d in list(own)})
        distance //= 2
    pieces = [own] + [{d: swapped(own[d], "tp", m) for d in own} for m in range(1, t_count)]

    inverse_gain = 1.0 / norm_gain
    inverse_square = inverse_gain * inverse_gain
    coarse = inverse_square.astype(jnp.bfloat16)
    fine = (inverse_square - coarse.astype(jnp.float32)).astype(jnp.bfloat16)
    gain_table = jnp.concatenate([coarse[None], fine[None], jnp.zeros((14, D), jnp.bfloat16)], axis=0)

    total = 0.0
    for m in range(t_count):
        for r in range(slots):
            here = (pair == m) & ((pair ^ t) == r)
            total = total + jnp.where(here, pieces[m][group * r].astype(jnp.float32), 0.0)
    total = total * lax.dynamic_slice_in_dim(inverse_gain, t * width, width, 0)[:, None]

    for p in range(group):
        part = [[pieces[m][group * r + p] for r in range(slots)] for m in range(t_count)]
        activated = activate(part, gain_table, experts_in, pair, t)
        activated = [activated] + [swapped(activated, "tp", m) for m in range(1, t_count)]
        share = tables[:, p].transpose(1, 0, 2).reshape(s_count, slots * rows)
        for j, result in enumerate(combine(activated, share, experts_out, t, slots)):
            distance = group * j + p
            result = swapped(result, "ep", distance) if distance else result
            total = total + result.astype(jnp.float32)
    return total.astype(jnp.bfloat16).T


def solution(mesh):
    in_specs = (
        P(("groups", "ep", "sub"), "tp"),
        P(("groups", "ep", "sub"), "tp"),
        P(("groups", "ep", "sub"), "tp"),
        P("tp"),
        P("tp", "ep"),
        P(("groups", "ep", "sub"), None),
        P(),
        P(("ep", "sub"), None, None, "tp"),
        P(("ep", "sub"), None, "tp"),
        P(("groups", "ep", "sub"), None),
        P(("groups", "ep", "sub"), None),
    )
    out_specs = P(("groups", "ep", "sub"), "tp")
    return jax.shard_map(local, mesh=mesh, in_specs=in_specs, out_specs=out_specs, check_vma=False)
```

time: 619 us -> 209 us (0.34)
  waiting for transfers between devices: 352 us -> 85.9 us
  blocking collectives: 135 us -> 0 us
  starting transfers between devices: 7.18 us -> 55.6 us
  local copies, waits for them, and re-layouts: 64.1 us -> 16.1 us
  Pallas kernels: 0 us -> 46 us
  matrix products: 31 us -> 0 us
  between operations: 13.4 us -> 0.25 us
  other arithmetic: 14.9 us -> 4.24 us
    all_gather x2 -> x0, waiting for transfers between devices: 241 us -> none  [the longest x1 201 us: local(): lax.all_gather(out_weight, 'ep', axis=1, tiled=True)]
    all_to_all x1 -> x0, blocking collectives: 135 us -> none  [local(): lax.all_to_all(outgoing, ('ep', 'sub'), split_axis=0, concat_axis=0, tile...]
    ppermute x0 -> x22, waiting for transfers between devices: none -> 82.1 us  [the longest x21 82.1 us: swapped(): lax.ppermute(block, axis, [(i, i ^ distance) for i in range(lax.axis_size...]
    all_to_all x1 -> x0, waiting for transfers between devices: 66.9 us -> none  [serve_rows(): lax.all_to_all(finished, ('ep', 'sub'), split_axis=0, concat_axis=0, tile...]
    ppermute x0 -> x22, starting transfers between devices: none -> 51.7 us  [the longest x21 47.3 us: swapped(): lax.ppermute(block, axis, [(i, i ^ distance) for i in range(lax.axis_size...]
    pallas_call x0 -> x6, Pallas kernels: none -> 46 us  [the longest x2 22.3 us: activate(): pl.pallas_call(kernel, grid=(experts, tiles), out_shape=jax.ShapeDtypeStr...]
    psum x1 -> x0, waiting for transfers between devices: 43.1 us -> none  [local(): hidden = residual.astype(jnp.float32) + lax.psum(partial_value, 'tp')]
    dot_general x5 -> x0, matrix products: 31 us -> none  [the longest x1 13.7 us: expert_rows(): jnp.einsum('rd,kdf->rkf', flat_rows, expert_in[0], preferred_element_type...]
  transfers between devices with their start and end apart: 5 -> 24, of which waited for: 4 -> 13; matrix products, arithmetic and copies ran while one was open for 2% -> 6% of each run, Pallas kernels for 0% -> 22%
where the time goes in v3:
time: 209 us; the launch traced here: 208 us
  waiting for transfers between devices  85.9 us (41%)
  starting transfers between devices  55.6 us (27%)
  Pallas kernels  46 us (22%)
  local copies, waits for them, and re-layouts  16.1 us (8%)
  other arithmetic  4.24 us (2%)
    ppermute x21, waiting for transfers between devices, swapped(): lax.ppermute(block, axis, [(i, i ^ distance) for i in range(lax.axis_size...  82.1 us
    ppermute x21, starting transfers between devices, swapped(): lax.ppermute(block, axis, [(i, i ^ distance) for i in range(lax.axis_size...  47.3 us
    pallas_call x2, Pallas kernels, activate(): pl.pallas_call(kernel, grid=(experts, tiles), out_shape=jax.ShapeDtypeStr...  22.3 us
    pallas_call x2, Pallas kernels, combine(): pl.pallas_call(kernel, grid=(tiles,), out_shape=tuple((jax.ShapeDtypeStru...  13.2 us
    unnamed x33, local copies, waits for them, and re-layouts  11.9 us
    pallas_call x1, Pallas kernels, attention(): pl.pallas_call(attention_kernel, out_shape=jax.ShapeDtypeStruct((width, r...  5.55 us
    pallas_call x1, Pallas kernels, project(): pl.pallas_call(kernel, out_shape=(jax.ShapeDtypeStruct((pair, columns, ro...  4.89 us
    ppermute x1, starting transfers between devices, local(): residual = lax.ppermute(picked(residual, pair ^ t, 0), ('ep', 'tp'), route)  4.4 us
  transfers between devices with their start and end apart: 24, of which 13 were waited for; matrix products, arithmetic and copies ran while one was open for 6% of the time, Pallas kernels for 22%

profile of v3, /device:TPU:0, one launch (start us, length us, event | category | flops | bytes accessed | tf_op | source)
XLA Modules:
  0.0 208.1 jit_solution(7067731258479689881)
XLA Ops:
  0.0 0.5 collective-permute-start.10
  0.5 2.6 %dynamic-slice_bitcast_fusion = bf16[720,1024]{1,0:T(8,128)(2,1)} fusion(bf16[2048,720]{0,1:T(8,128)(2,1)} %param.15, s32[]{:T(128)S(6)} %select_n.79), kind=kLoop, calls=%fused_computation.1 | loop fusion | bytes 2949124 | tf_op jit(solution)/shard_map/dynamic_slice | solution.py:314
  3.1 2.7 %collective-permute-start = (bf16[720,1024]{1,0:T(8,128)(2,1)}, bf16[720,1024]{1,0:T(8,128)(2,1)S(1)}, u32[]{:S(2)}, u32[]{:S(2)}) collective-permute-start(bf16[720,1024]{1,0:T(8,128)(2,1)} %dynamic-slice_bitcast_fusion), channel_id=1, source_target_pairs={{0,4},{4,0},{8,12},{12,8},{1,5},{5,1},{9,13},{13,9},{2,6},{6,2},{1... | collective-permute-start | bytes 4423688 | tf_op jit(solution)/shard_map/ppermute | solution.py:22
  5.9 2.0 collective-permute-start.1
  7.8 1.9 collective-permute-start.2
  9.8 3.8 %collective-permute-done.1.kp_ref = bf16[128,256]{1,0:T(8,128)(2,1)S(1)} collective-permute-done((bf16[128,256]{1,0:T(8,128)(2,1)S(1)}, bf16[128,256]{1,0:T(8,128)(2,1)S(1)}, u32[]{:S(2)}, u32[]{:S(2)}) %collective-permute-start.1) | collective-permute-done | bytes 65568 | tf_op jit(solution)/shard_map/ppermute | solution.py:18
  13.7 5.5 %attention.1.refs_0_ = bf16[2048,128]{1,0:T(8,128)(2,1)S(1)} custom-call(s32[1]{0:T(128)} %bitcast.4.first_ref, f32[32]{0:T(128)S(1)} %copy-done.12, bf16[128,2048]{1,0:T(8,128)(2,1)S(1)} %copy-done.3, bf16[128,256]{1,0:T(8,128)(2,1)S(1)} %collective-permute-done.1.kp_ref, bf16[128,256]{1,0:T(8,128)(2,1)S(1)} %copy-done.10, ...), custom_call_target="tpu_custom_call" | custom-call | flops 268435456 | bytes 1572864 | tf_op jit(solution)/shard_map/attention/pallas_call | solution.py:111
  19.2 19.7 %collective-permute-done.refs_3_ = bf16[720,1024]{1,0:T(8,128)(2,1)S(1)} collective-permute-done((bf16[720,1024]{1,0:T(8,128)(2,1)}, bf16[720,1024]{1,0:T(8,128)(2,1)S(1)}, u32[]{:S(2)}, u32[]{:S(2)}) %collective-permute-start) | collective-permute-done | bytes 1474592 | tf_op jit(solution)/shard_map/ppermute | solution.py:22
  38.9 6.4 %collective-permute-start.4 = (bf16[720,1024]{1,0:T(8,128)(2,1)S(1)}, bf16[720,1024]{1,0:T(8,128)(2,1)}, u32[]{:S(2)}, u32[]{:S(2)}) collective-permute-start(bf16[720,1024]{1,0:T(8,128)(2,1)S(1)} %collective-permute-done.refs_3_), channel_id=1, source_target_pairs={{0,1},{1,0},{2,3},{3,2},{4,5},{5,4},{6,7},{7,6},{8,9},{9,8},{10,11... | collective-permute-start | bytes 4423688 | tf_op jit(solution)/shard_map/ppermute | solution.py:22
  45.3 2.6 %collective-permute-start.3 = (bf16[2048,128]{1,0:T(8,128)(2,1)S(1)}, bf16[2048,128]{1,0:T(8,128)(2,1)S(1)}, u32[]{:S(2)}, u32[]{:S(2)}) collective-permute-start(bf16[2048,128]{1,0:T(8,128)(2,1)S(1)} %attention.1.refs_0_), channel_id=1, source_target_pairs={{0,8},{4,12},{8,0},{12,4},{1,9},{5,13},{9,1},{13,5},{2,10},{6,14},... | collective-permute-start | bytes 1572872 | tf_op jit(solution)/shard_map/ppermute | solution.py:22
  47.9 0.8 dynamic-slice_bitcast_fusion.1
  48.6 4.4 %collective-permute-start.5 = (bf16[1440,128]{1,0:T(8,128)(2,1)}, bf16[1440,128]{1,0:T(8,128)(2,1)}, u32[]{:S(2)}, u32[]{:S(2)}) collective-permute-start(bf16[1440,128]{1,0:T(8,128)(2,1)} %dynamic-slice_bitcast_fusion.1), channel_id=1, source_target_pairs={{0,0},{2,10},{4,4},{6,14},{8,8},{10,2},{12,12},{14,6},{1,1},{3,11}... | collective-permute-start | bytes 1105928 | tf_op jit(solution)/shard_map/ppermute | solution.py:327
  53.0 6.5 %copy.19 = bf16[1,1440,1440]{1,2,0:T(8,128)(2,1)} copy(bf16[1,1440,1440]{2,1,0:T(8,128)(2,1)} %param.19) | data formatting | bytes 8294400 | tf_op args[8]
  59.6 11.7 %collective-permute-done.3.refs_1_ = bf16[2048,128]{1,0:T(8,128)(2,1)S(1)} collective-permute-done((bf16[2048,128]{1,0:T(8,128)(2,1)S(1)}, bf16[2048,128]{1,0:T(8,128)(2,1)S(1)}, u32[]{:S(2)}, u32[]{:S(2)}) %collective-permute-start.3) | collective-permute-done | bytes 524320 | tf_op jit(solution)/shard_map/ppermute | solution.py:22
  71.3 0.8 copy-done.4
  72.2 1.0 copy-done.5
  73.2 4.9 %project.1 = (f32[2,720,128]{2,1,0:T(8,128)S(1)}, bf16[1,2,720,128]{3,2,1,0:T(8,128)(2,1)}) custom-call(s32[3]{0:T(128)S(1)} %pad_add_fusion.place_ref, bf16[2048,128]{1,0:T(8,128)(2,1)S(1)} %attention.1.refs_0_, bf16[2048,128]{1,0:T(8,128)(2,1)S(1)} %copy-done.5, bf16[720,2048]{1,0:T(8,128)(2,1)} %bitcast.64, ...), custom_call_target="tpu_custom_call" | custom-call | flops 1509949440 | bytes 5898240 | tf_op jit(solution)/shard_map/project/pallas_call | solution.py:153
  78.1 10.3 %collective-permute-start.6 = (bf16[1440,128]{1,0:T(8,128)(2,1)}, bf16[1440,128]{1,0:T(8,128)(2,1)S(1)}, u32[]{:S(2)}, u32[]{:S(2)}) collective-permute-start(bf16[1440,128]{1,0:T(8,128)(2,1)} %bitcast.10), channel_id=1, source_target_pairs={{0,2},{2,0},{1,3},{3,1},{4,6},{6,4},{5,7},{7,5},{8,10},{10,8},{9,1... | collective-permute-start | bytes 1105928 | tf_op jit(solution)/shard_map/ppermute | solution.py:22
  88.5 7.2 %collective-permute-done.6 = bf16[1440,128]{1,0:T(8,128)(2,1)S(1)} collective-permute-done((bf16[1440,128]{1,0:T(8,128)(2,1)}, bf16[1440,128]{1,0:T(8,128)(2,1)S(1)}, u32[]{:S(2)}, u32[]{:S(2)}) %collective-permute-start.6) | collective-permute-done | bytes 368672 | tf_op jit(solution)/shard_map/ppermute | solution.py:22
  95.7 1.3 fusion.2.refs_0_
  97.1 4.4 %collective-permute-start.14 = (f32[8,128]{1,0:T(8,128)S(1)}, f32[8,128]{1,0:T(8,128)S(1)}, u32[]{:S(2)}, u32[]{:S(2)}) collective-permute-start(f32[8,128]{1,0:T(8,128)S(1)} %select_reduce_fusion), channel_id=1, source_target_pairs={{0,12},{4,8},{8,4},{12,0},{1,13},{5,9},{9,5},{13,1},{2,14},{6,10},... | collective-permute-start | bytes 12296 | tf_op jit(solution)/shard_map/ppermute | solution.py:22
  101.6 0.6 collective-permute-start.17
  102.2 12.1 %collective-permute-done.7.refs_1_ = bf16[1440,128]{1,0:T(8,128)(2,1)S(1)} collective-permute-done((bf16[1440,128]{1,0:T(8,128)(2,1)S(1)}, bf16[1440,128]{1,0:T(8,128)(2,1)S(1)}, u32[]{:S(2)}, u32[]{:S(2)}) %collective-permute-start.7) | collective-permute-done | bytes 368672 | tf_op jit(solution)/shard_map/ppermute | solution.py:22
  114.4 2.8 %collective-permute-done.17.refs_0_ = bf16[1440,128]{1,0:T(8,128)(2,1)S(1)} collective-permute-done((bf16[1440,128]{1,0:T(8,128)(2,1)S(1)}, bf16[1440,128]{1,0:T(8,128)(2,1)S(1)}, u32[]{:S(2)}, u32[]{:S(2)}) %collective-permute-start.17) | collective-permute-done | bytes 368672 | tf_op jit(solution)/shard_map/ppermute | solution.py:22
  117.2 1.5 collective-permute-start.19
  118.6 5.0 %collective-permute-done.18.refs_1_ = bf16[1440,128]{1,0:T(8,128)(2,1)S(1)} collective-permute-done((bf16[1440,128]{1,0:T(8,128)(2,1)S(1)}, bf16[1440,128]{1,0:T(8,128)(2,1)S(1)}, u32[]{:S(2)}, u32[]{:S(2)}) %collective-permute-start.18) | collective-permute-done | bytes 368672 | tf_op jit(solution)/shard_map/ppermute | solution.py:22
  123.7 1.5 collective-permute-start.20
  125.4 0.7 copy-done.6
  126.1 3.0 %collective-permute-start.13 = (f32[8,128]{1,0:T(8,128)S(1)}, f32[8,128]{1,0:T(8,128)S(1)}, u32[]{:S(2)}, u32[]{:S(2)}) collective-permute-start(f32[8,128]{1,0:T(8,128)S(1)} %select_reduce_fusion), channel_id=1, source_target_pairs={{0,8},{4,12},{8,0},{12,4},{1,9},{5,13},{9,1},{13,5},{2,10},{6,14},... | collective-permute-start | bytes 12296 | tf_op jit(solution)/shard_map/ppermute | solution.py:22
  129.1 3.5 %collective-permute-done.20.refs_3_ = bf16[1440,128]{1,0:T(8,128)(2,1)S(1)} collective-permute-done((bf16[1440,128]{1,0:T(8,128)(2,1)S(1)}, bf16[1440,128]{1,0:T(8,128)(2,1)S(1)}, u32[]{:S(2)}, u32[]{:S(2)}) %collective-permute-start.20) | collective-permute-done | bytes 368672 | tf_op jit(solution)/shard_map/ppermute | solution.py:22
  132.6 0.8 copy-done.8
  133.4 1.5 collective-permute-start.8
  134.8 0.6 collective-permute-start.9
  135.4 1.0 copy-done.7
  136.4 1.0 copy-done.9
  137.4 11.2 %activate.3.refs_0_ = bf16[2,720,256]{2,1,0:T(8,128)(2,1)S(1)} custom-call(s32[2]{0:T(128)S(1)} %pad_add_fusion.1.place_ref, bf16[1440,128]{1,0:T(8,128)(2,1)S(1)} %collective-permute-done.17.refs_0_, bf16[1440,128]{1,0:T(8,128)(2,1)S(1)} %collective-permute-done.18.refs_1_, bf16[1440,128]{1,0:T(8,128)(2,1)S(1)} %copy-done.7, ...), custom_call_target="tpu_custom_call" | custom-call | flops 4246732800 | bytes 16588800 | tf_op jit(solution)/shard_map/activate/pallas_call | solution.py:217
  148.6 1.4 collective-permute-done.9.refs_3_
  150.0 1.5 collective-permute-start.21
  151.5 11.2 %activate.2.refs_0_ = bf16[2,720,256]{2,1,0:T(8,128)(2,1)S(1)} custom-call(s32[2]{0:T(128)S(1)} %pad_add_fusion.1.place_ref, bf16[1440,128]{1,0:T(8,128)(2,1)S(1)} %fusion.2.refs_0_, bf16[1440,128]{1,0:T(8,128)(2,1)S(1)} %collective-permute-done.7.refs_1_, bf16[1440,128]{1,0:T(8,128)(2,1)S(1)} %collective-permute-done.8.refs_2_, ...), custom_call_target="tpu_custom_call" | custom-call | flops 4246732800 | bytes 16588800 | tf_op jit(solution)/shard_map/activate/pallas_call | solution.py:217
  162.7 0.6 collective-permute-start.11
  163.3 0.6 gather_fusion
  164.0 5.3 %collective-permute-done.21.refs_1_ = bf16[2,720,256]{2,1,0:T(8,128)(2,1)} collective-permute-done((bf16[2,720,256]{2,1,0:T(8,128)(2,1)S(1)}, bf16[2,720,256]{2,1,0:T(8,128)(2,1)}, u32[]{:S(2)}, u32[]{:S(2)}) %collective-permute-start.21) | collective-permute-done | bytes 737312 | tf_op jit(solution)/shard_map/ppermute | solution.py:22
  169.3 6.6 %combine.3 = (bf16[1440,128]{1,0:T(8,128)(2,1)}, bf16[1440,128]{1,0:T(8,128)(2,1)}) custom-call(s32[1]{0:T(128)} %bitcast.t_ref, bf16[2,720,256]{2,1,0:T(8,128)(2,1)S(1)} %activate.3.refs_0_, bf16[2,720,256]{2,1,0:T(8,128)(2,1)} %collective-permute-done.21.refs_1_, f32[2,256]{1,0:T(2,128)S(1)} %get-tuple-element.25.refs_2_, bf16[1440,1440]{1,0:T(8,128)(2,1)} %bitcast.59, ...), custom_call_target="tpu_custom_call" | custom-call | flops 2123366400 | bytes 8294400 | tf_op jit(solution)/shard_map/combine/pallas_call | solution.py:267
  175.9 5.5 %collective-permute-start.23 = (bf16[1440,128]{1,0:T(8,128)(2,1)}, bf16[1440,128]{1,0:T(8,128)(2,1)}, u32[]{:S(2)}, u32[]{:S(2)}) collective-permute-start(bf16[1440,128]{1,0:T(8,128)(2,1)} %get-tuple-element.20), channel_id=1, source_target_pairs={{0,12},{4,8},{8,4},{12,0},{1,13},{5,9},{9,5},{13,1},{2,14},{6,10},... | collective-permute-start | bytes 1105928 | tf_op jit(solution)/shard_map/ppermute | solution.py:22
  181.4 6.6 %combine.2 = (bf16[1440,128]{1,0:T(8,128)(2,1)S(1)}, bf16[1440,128]{1,0:T(8,128)(2,1)}) custom-call(s32[1]{0:T(128)} %bitcast.t_ref, bf16[2,720,256]{2,1,0:T(8,128)(2,1)S(1)} %activate.2.refs_0_, bf16[2,720,256]{2,1,0:T(8,128)(2,1)} %collective-permute-done.11.refs_1_, f32[2,256]{1,0:T(2,128)S(1)} %get-tuple-element.24.refs_2_, bf16[1440,1440]{1,0:T(8,128)(2,1)} %bitcast.60, ...), custom_call_target="tpu_custom_call" | custom-call | flops 2123366400 | bytes 8294400 | tf_op jit(solution)/shard_map/combine/pallas_call | solution.py:267
  187.9 4.2 %collective-permute-start.16 = (bf16[1440,128]{1,0:T(8,128)(2,1)}, bf16[1440,128]{1,0:T(8,128)(2,1)S(1)}, u32[]{:S(2)}, u32[]{:S(2)}) collective-permute-start(bf16[1440,128]{1,0:T(8,128)(2,1)} %get-tuple-element.18), channel_id=1, source_target_pairs={{0,8},{4,12},{8,0},{12,4},{1,9},{5,13},{9,1},{13,5},{2,10},{6,14},... | collective-permute-start | bytes 1105928 | tf_op jit(solution)/shard_map/ppermute | solution.py:22
  192.5 13.2 %collective-permute-done.16 = bf16[1440,128]{1,0:T(8,128)(2,1)S(1)} collective-permute-done((bf16[1440,128]{1,0:T(8,128)(2,1)}, bf16[1440,128]{1,0:T(8,128)(2,1)S(1)}, u32[]{:S(2)}, u32[]{:S(2)}) %collective-permute-start.16) | collective-permute-done | bytes 368672 | tf_op jit(solution)/shard_map/ppermute | solution.py:22
  205.7 2.4 %fusion.3 = bf16[128,1440]{0,1:T(8,128)(2,1)} fusion(bf16[1440,128]{1,0:T(8,128)(2,1)} %collective-permute-done.23, bf16[1440,128]{1,0:T(8,128)(2,1)} %collective-permute-done.22, bf16[1440,128]{1,0:T(8,128)(2,1)S(1)} %collective-permute-done.16, bf16[1440,128]{1,0:T(8,128)(2,1)S(1)} %get-tuple-element.17, f32[1440]{0:T(1024)S(1)} %dynamic_slice.17, ...), kind=kLoop, calls=%fused_computation.8 | loop fusion | flops 3870720 | bytes 3323524 | tf_op jit(solution)/shard_map/transpose | solution.py:377
  (65 shorter events, 1.4 us)
Async XLA Ops:
  0.0 47.9 %copy-start = (bf16[128,2880]{0,1:T(8,128)(2,1)S(1)}, bf16[128,2880]{0,1:T(8,128)(2,1)}, u32[]{:S(2)}) copy-start(bf16[128,2880]{0,1:T(8,128)(2,1)} %param.16) | copy-start | bytes 2211844
  0.0 5.8 %copy-start.10 = (bf16[128,256]{1,0:T(8,128)(2,1)S(1)}, bf16[128,256]{1,0:T(8,128)(2,1)}, u32[]{:S(2)}) copy-start(bf16[128,256]{1,0:T(8,128)(2,1)} %k_ref.1) | copy-start | bytes 196612
  0.0 7.8 %copy-start.11 = (bf16[128,256]{1,0:T(8,128)(2,1)S(1)}, bf16[128,256]{1,0:T(8,128)(2,1)}, u32[]{:S(2)}) copy-start(bf16[128,256]{1,0:T(8,128)(2,1)} %v_ref.1) | copy-start | bytes 196612
  0.0 13.6 %copy-start.12 = (f32[32]{0:T(128)S(1)}, f32[32]{0:T(128)}, u32[]{:S(2)}) copy-start(f32[32]{0:T(128)} %sink_ref.1) | copy-start | bytes 388
  0.0 13.6 %copy-start.3 = (bf16[128,2048]{1,0:T(8,128)(2,1)S(1)}, bf16[128,2048]{1,0:T(8,128)(2,1)}, u32[]{:S(2)}) copy-start(bf16[128,2048]{1,0:T(8,128)(2,1)} %q_ref.1) | copy-start | bytes 1572868
  0.0 134.8 %collective-permute-start.10 = (bf16[2,720,2880]{2,1,0:T(8,128)(2,1)}, bf16[2,720,2880]{2,1,0:T(8,128)(2,1)}, u32[]{:S(2)}, u32[]{:S(2)}) collective-permute-start(bf16[2,720,2880]{2,1,0:T(8,128)(2,1)} %bitcast.61), channel_id=1, source_target_pairs={{0,1},{1,0},{2,3},{3,2},{4,5},{5,4},{6,7},{7,6},{8,9},{9,8},{10,11... | collective-permute-start | bytes 24883208 | tf_op jit(solution)/shard_map/ppermute | solution.py:22
  3.1 35.7 %collective-permute-start = (bf16[720,1024]{1,0:T(8,128)(2,1)}, bf16[720,1024]{1,0:T(8,128)(2,1)S(1)}, u32[]{:S(2)}, u32[]{:S(2)}) collective-permute-start(bf16[720,1024]{1,0:T(8,128)(2,1)} %dynamic-slice_bitcast_fusion), channel_id=1, source_target_pairs={{0,4},{4,0},{8,12},{12,8},{1,5},{5,1},{9,13},{13,9},{2,6},{6,2},{1... | collective-permute-start | bytes 4423688 | tf_op jit(solution)/shard_map/ppermute | solution.py:22
  5.9 7.7 %collective-permute-start.1 = (bf16[128,256]{1,0:T(8,128)(2,1)S(1)}, bf16[128,256]{1,0:T(8,128)(2,1)S(1)}, u32[]{:S(2)}, u32[]{:S(2)}) collective-permute-start(bf16[128,256]{1,0:T(8,128)(2,1)S(1)} %copy-done.10), channel_id=1, source_target_pairs={{0,1},{1,4},{4,5},{5,8},{8,9},{9,12},{12,13},{2,3},{3,6},{6,7},{7,... | collective-permute-start | bytes 196616 | tf_op jit(solution)/shard_map/ppermute | solution.py:18
  7.8 5.8 %collective-permute-start.2 = (bf16[128,256]{1,0:T(8,128)(2,1)S(1)}, bf16[128,256]{1,0:T(8,128)(2,1)S(1)}, u32[]{:S(2)}, u32[]{:S(2)}) collective-permute-start(bf16[128,256]{1,0:T(8,128)(2,1)S(1)} %copy-done.11), channel_id=1, source_target_pairs={{0,1},{1,4},{4,5},{5,8},{8,9},{9,12},{12,13},{2,3},{3,6},{6,7},{7,... | collective-permute-start | bytes 196616 | tf_op jit(solution)/shard_map/ppermute | solution.py:18
  38.9 33.3 %collective-permute-start.4 = (bf16[720,1024]{1,0:T(8,128)(2,1)S(1)}, bf16[720,1024]{1,0:T(8,128)(2,1)}, u32[]{:S(2)}, u32[]{:S(2)}) collective-permute-start(bf16[720,1024]{1,0:T(8,128)(2,1)S(1)} %collective-permute-done.refs_3_), channel_id=1, source_target_pairs={{0,1},{1,0},{2,3},{3,2},{4,5},{5,4},{6,7},{7,6},{8,9},{9,8},{10,11... | collective-permute-start | bytes 4423688 | tf_op jit(solution)/shard_map/ppermute | solution.py:22
  45.3 26.0 %collective-permute-start.3 = (bf16[2048,128]{1,0:T(8,128)(2,1)S(1)}, bf16[2048,128]{1,0:T(8,128)(2,1)S(1)}, u32[]{:S(2)}, u32[]{:S(2)}) collective-permute-start(bf16[2048,128]{1,0:T(8,128)(2,1)S(1)} %attention.1.refs_0_), channel_id=1, source_target_pairs={{0,8},{4,12},{8,0},{12,4},{1,9},{5,13},{9,1},{13,5},{2,10},{6,14},... | collective-permute-start | bytes 1572872 | tf_op jit(solution)/shard_map/ppermute | solution.py:22
  48.6 39.9 %collective-permute-start.5 = (bf16[1440,128]{1,0:T(8,128)(2,1)}, bf16[1440,128]{1,0:T(8,128)(2,1)}, u32[]{:S(2)}, u32[]{:S(2)}) collective-permute-start(bf16[1440,128]{1,0:T(8,128)(2,1)} %dynamic-slice_bitcast_fusion.1), channel_id=1, source_target_pairs={{0,0},{2,10},{4,4},{6,14},{8,8},{10,2},{12,12},{14,6},{1,1},{3,11}... | collective-permute-start | bytes 1105928 | tf_op jit(solution)/shard_map/ppermute | solution.py:327
  59.6 104.4 %collective-permute-start.15 = (bf16[1440,1440]{1,0:T(8,128)(2,1)}, bf16[1440,1440]{1,0:T(8,128)(2,1)}, u32[]{:S(2)}, u32[]{:S(2)}) collective-permute-start(bf16[1440,1440]{1,0:T(8,128)(2,1)} %bitcast.58), channel_id=1, source_target_pairs={{0,1},{1,0},{2,3},{3,2},{4,5},{5,4},{6,7},{7,6},{8,9},{9,8},{10,11... | collective-permute-start | bytes 12441608 | tf_op jit(solution)/shard_map/ppermute | solution.py:22
  71.3 0.8 copy-start.4
  72.2 1.0 copy-start.5
  73.2 15.2 %copy-start.13 = (f32[2880]{0:T(1024)S(1)}, f32[2880]{0:T(1024)}, u32[]{:S(2)}) copy-start(f32[2880]{0:T(1024)} %param.17) | copy-start | bytes 34564
  73.2 15.3 %copy-start.14 = (s32[128,4]{0,1:T(4,128)S(1)}, s32[128,4]{0,1:T(4,128)}, u32[]{:S(2)}) copy-start(s32[128,4]{0,1:T(4,128)} %param.21) | copy-start | bytes 6148
  73.2 23.9 %copy-start.15 = (s32[128,4]{0,1:T(4,128)S(1)}, s32[128,4]{0,1:T(4,128)}, u32[]{:S(2)}) copy-start(s32[128,4]{0,1:T(4,128)} %param.20) | copy-start | bytes 6148
  78.1 17.6 %collective-permute-start.6 = (bf16[1440,128]{1,0:T(8,128)(2,1)}, bf16[1440,128]{1,0:T(8,128)(2,1)S(1)}, u32[]{:S(2)}, u32[]{:S(2)}) collective-permute-start(bf16[1440,128]{1,0:T(8,128)(2,1)} %bitcast.10), channel_id=1, source_target_pairs={{0,2},{2,0},{1,3},{3,1},{4,6},{6,4},{5,7},{7,5},{8,10},{10,8},{9,1... | collective-permute-start | bytes 1105928 | tf_op jit(solution)/shard_map/ppermute | solution.py:22
  97.0 17.3 %collective-permute-start.7 = (bf16[1440,128]{1,0:T(8,128)(2,1)S(1)}, bf16[1440,128]{1,0:T(8,128)(2,1)S(1)}, u32[]{:S(2)}, u32[]{:S(2)}) collective-permute-start(bf16[1440,128]{1,0:T(8,128)(2,1)S(1)} %fusion.2.refs_0_), channel_id=1, source_target_pairs={{0,8},{4,12},{8,0},{12,4},{1,9},{5,13},{9,1},{13,5},{2,10},{6,14},... | collective-permute-start | bytes 1105928 | tf_op jit(solution)/shard_map/ppermute | solution.py:22
  97.1 65.5 %collective-permute-start.14 = (f32[8,128]{1,0:T(8,128)S(1)}, f32[8,128]{1,0:T(8,128)S(1)}, u32[]{:S(2)}, u32[]{:S(2)}) collective-permute-start(f32[8,128]{1,0:T(8,128)S(1)} %select_reduce_fusion), channel_id=1, source_target_pairs={{0,12},{4,8},{8,4},{12,0},{1,13},{5,9},{9,5},{13,1},{2,14},{6,10},... | collective-permute-start | bytes 12296 | tf_op jit(solution)/shard_map/ppermute | solution.py:22
  101.6 15.5 %collective-permute-start.17 = (bf16[1440,128]{1,0:T(8,128)(2,1)S(1)}, bf16[1440,128]{1,0:T(8,128)(2,1)S(1)}, u32[]{:S(2)}, u32[]{:S(2)}) collective-permute-start(bf16[1440,128]{1,0:T(8,128)(2,1)S(1)} %fusion.2.refs_0_), channel_id=1, source_target_pairs={{0,4},{4,0},{8,12},{12,8},{1,5},{5,1},{9,13},{13,9},{2,6},{6,2},{1... | collective-permute-start | bytes 1105928 | tf_op jit(solution)/shard_map/ppermute | solution.py:22
  114.3 9.4 %collective-permute-start.18 = (bf16[1440,128]{1,0:T(8,128)(2,1)S(1)}, bf16[1440,128]{1,0:T(8,128)(2,1)S(1)}, u32[]{:S(2)}, u32[]{:S(2)}) collective-permute-start(bf16[1440,128]{1,0:T(8,128)(2,1)S(1)} %collective-permute-done.7.refs_1_), channel_id=1, source_target_pairs={{0,4},{4,0},{8,12},{12,8},{1,5},{5,1},{9,13},{13,9},{2,6},{6,2},{1... | collective-permute-start | bytes 1105928 | tf_op jit(solution)/shard_map/ppermute | solution.py:22
  117.2 8.2 %collective-permute-start.19 = (bf16[1440,128]{1,0:T(8,128)(2,1)S(1)}, bf16[1440,128]{1,0:T(8,128)(2,1)S(1)}, u32[]{:S(2)}, u32[]{:S(2)}) collective-permute-start(bf16[1440,128]{1,0:T(8,128)(2,1)S(1)} %collective-permute-done.17.refs_0_), channel_id=1, source_target_pairs={{0,2},{2,0},{1,3},{3,1},{4,6},{6,4},{5,7},{7,5},{8,10},{10,8},{9,1... | collective-permute-start | bytes 1105928 | tf_op jit(solution)/shard_map/ppermute | solution.py:22
  123.7 8.9 %collective-permute-start.20 = (bf16[1440,128]{1,0:T(8,128)(2,1)S(1)}, bf16[1440,128]{1,0:T(8,128)(2,1)S(1)}, u32[]{:S(2)}, u32[]{:S(2)}) collective-permute-start(bf16[1440,128]{1,0:T(8,128)(2,1)S(1)} %collective-permute-done.18.refs_1_), channel_id=1, source_target_pairs={{0,2},{2,0},{1,3},{3,1},{4,6},{6,4},{5,7},{7,5},{8,10},{10,8},{9,1... | collective-permute-start | bytes 1105928 | tf_op jit(solution)/shard_map/ppermute | solution.py:22
  125.4 0.7 copy-start.6
  126.1 37.2 %collective-permute-start.13 = (f32[8,128]{1,0:T(8,128)S(1)}, f32[8,128]{1,0:T(8,128)S(1)}, u32[]{:S(2)}, u32[]{:S(2)}) collective-permute-start(f32[8,128]{1,0:T(8,128)S(1)} %select_reduce_fusion), channel_id=1, source_target_pairs={{0,8},{4,12},{8,0},{12,4},{1,9},{5,13},{9,1},{13,5},{2,10},{6,14},... | collective-permute-start | bytes 12296 | tf_op jit(solution)/shard_map/ppermute | solution.py:22
  132.6 0.8 copy-start.8
  133.4 15.2 %collective-permute-start.8 = (bf16[1440,128]{1,0:T(8,128)(2,1)S(1)}, bf16[1440,128]{1,0:T(8,128)(2,1)S(1)}, u32[]{:S(2)}, u32[]{:S(2)}) collective-permute-start(bf16[1440,128]{1,0:T(8,128)(2,1)S(1)} %fusion.2.refs_0_), channel_id=1, source_target_pairs={{0,2},{2,0},{1,3},{3,1},{4,6},{6,4},{5,7},{7,5},{8,10},{10,8},{9,1... | collective-permute-start | bytes 1105928 | tf_op jit(solution)/shard_map/ppermute | solution.py:22
  134.8 15.2 %collective-permute-start.9 = (bf16[1440,128]{1,0:T(8,128)(2,1)S(1)}, bf16[1440,128]{1,0:T(8,128)(2,1)S(1)}, u32[]{:S(2)}, u32[]{:S(2)}) collective-permute-start(bf16[1440,128]{1,0:T(8,128)(2,1)S(1)} %collective-permute-done.7.refs_1_), channel_id=1, source_target_pairs={{0,2},{2,0},{1,3},{3,1},{4,6},{6,4},{5,7},{7,5},{8,10},{10,8},{9,1... | collective-permute-start | bytes 1105928 | tf_op jit(solution)/shard_map/ppermute | solution.py:22
  135.4 1.0 copy-start.7
  136.4 1.0 copy-start.9
  148.6 14.8 %collective-permute-start.12 = (f32[8,128]{1,0:T(8,128)S(1)}, f32[8,128]{1,0:T(8,128)S(1)}, u32[]{:S(2)}, u32[]{:S(2)}) collective-permute-start(f32[8,128]{1,0:T(8,128)S(1)} %select_reduce_fusion), channel_id=1, source_target_pairs={{0,4},{4,0},{8,12},{12,8},{1,5},{5,1},{9,13},{13,9},{2,6},{6,2},{1... | collective-permute-start | bytes 12296 | tf_op jit(solution)/shard_map/ppermute | solution.py:22
  150.0 12.6 %copy-start.1 = (bf16[1440,128]{1,0:T(8,128)(2,1)}, bf16[1440,128]{1,0:T(8,128)(2,1)S(1)}, u32[]{:S(2)}) copy-start(bf16[1440,128]{1,0:T(8,128)(2,1)S(1)} %collective-permute-done.9.refs_3_) | copy-start | bytes 1105924
  150.0 19.3 %collective-permute-start.21 = (bf16[2,720,256]{2,1,0:T(8,128)(2,1)S(1)}, bf16[2,720,256]{2,1,0:T(8,128)(2,1)}, u32[]{:S(2)}, u32[]{:S(2)}) collective-permute-start(bf16[2,720,256]{2,1,0:T(8,128)(2,1)S(1)} %activate.3.refs_0_), channel_id=1, source_target_pairs={{0,2},{2,0},{1,3},{3,1},{4,6},{6,4},{5,7},{7,5},{8,10},{10,8},{9,1... | collective-permute-start | bytes 2211848 | tf_op jit(solution)/shard_map/ppermute | solution.py:22
  162.7 18.7 %collective-permute-start.11 = (bf16[2,720,256]{2,1,0:T(8,128)(2,1)S(1)}, bf16[2,720,256]{2,1,0:T(8,128)(2,1)}, u32[]{:S(2)}, u32[]{:S(2)}) collective-permute-start(bf16[2,720,256]{2,1,0:T(8,128)(2,1)S(1)} %activate.2.refs_0_), channel_id=1, source_target_pairs={{0,2},{2,0},{1,3},{3,1},{4,6},{6,4},{5,7},{7,5},{8,10},{10,8},{9,1... | collective-permute-start | bytes 2211848 | tf_op jit(solution)/shard_map/ppermute | solution.py:22
  175.9 16.3 %collective-permute-start.23 = (bf16[1440,128]{1,0:T(8,128)(2,1)}, bf16[1440,128]{1,0:T(8,128)(2,1)}, u32[]{:S(2)}, u32[]{:S(2)}) collective-permute-start(bf16[1440,128]{1,0:T(8,128)(2,1)} %get-tuple-element.20), channel_id=1, source_target_pairs={{0,12},{4,8},{8,4},{12,0},{1,13},{5,9},{9,5},{13,1},{2,14},{6,10},... | collective-permute-start | bytes 1105928 | tf_op jit(solution)/shard_map/ppermute | solution.py:22
  181.4 11.1 %collective-permute-start.22 = (bf16[1440,128]{1,0:T(8,128)(2,1)}, bf16[1440,128]{1,0:T(8,128)(2,1)}, u32[]{:S(2)}, u32[]{:S(2)}) collective-permute-start(bf16[1440,128]{1,0:T(8,128)(2,1)} %get-tuple-element.19), channel_id=1, source_target_pairs={{0,4},{4,0},{8,12},{12,8},{1,5},{5,1},{9,13},{13,9},{2,6},{6,2},{1... | collective-permute-start | bytes 1105928 | tf_op jit(solution)/shard_map/ppermute | solution.py:22
  181.4 24.3 %copy-start.2 = (bf16[1440,128]{1,0:T(8,128)(2,1)S(1)}, bf16[1440,128]{1,0:T(8,128)(2,1)}, u32[]{:S(2)}) copy-start(bf16[1440,128]{1,0:T(8,128)(2,1)} %copy-done.1) | copy-start | bytes 1105924
  187.9 17.7 %collective-permute-start.16 = (bf16[1440,128]{1,0:T(8,128)(2,1)}, bf16[1440,128]{1,0:T(8,128)(2,1)S(1)}, u32[]{:S(2)}, u32[]{:S(2)}) collective-permute-start(bf16[1440,128]{1,0:T(8,128)(2,1)} %get-tuple-element.18), channel_id=1, source_target_pairs={{0,8},{4,12},{8,0},{12,4},{1,9},{5,13},{9,1},{13,5},{2,10},{6,14},... | collective-permute-start | bytes 1105928 | tf_op jit(solution)/shard_map/ppermute | solution.py:22

commit v4 on v3

--- a/solution.py
+++ b/solution.py
@@ -9,7 +9,7 @@
 HD = 64
 WIN = 128
 TOP = 4
-VMEM_BYTES = 48 * 1024 * 1024
+VMEM_BYTES = 16 * 1024 * 1024
 
 
 def shifted(block, axis, distance):
@@ -40,10 +40,6 @@
 
 def dot(left, right):
     return jnp.dot(left, right, preferred_element_type=jnp.float32)
-
-
-def tile_of(size):
-    return size // 3 if size % 48 == 0 else size
 
 
 def aligned(size):
@@ -104,10 +100,8 @@
             out_ref[start + HD : start + 2 * HD, :] = result[:, rows:]
 
 
-def attention(queries, key_rows, value_rows, sink_logits, first):
+def attention(queries, earlier_keys, key_rows, earlier_values, value_rows, sink_logits, first):
     rows, width = queries.shape
-    earlier_keys = shifted(key_rows, ("ep", "sub"), 1)
-    earlier_values = shifted(value_rows, ("ep", "sub"), 1)
     return pl.pallas_call(
         attention_kernel,
         out_shape=jax.ShapeDtypeStruct((width, rows), jnp.bfloat16),
@@ -171,58 +165,40 @@
     lanes = slots * rows
     experts = len(weights)
     units = weights[0].shape[1]
-    tile = tile_of(units)
-    tiles = units // tile
 
     def kernel(place_ref, *refs):
         piece_refs = refs[: slots * slots]
         table_ref = refs[slots * slots]
         weight_refs = refs[slots * slots + 1 : slots * slots + 1 + experts]
-        out_ref, rows_ref, scale_ref, stage_ref = refs[slots * slots + 1 + experts :]
-        e, step = pl.program_id(0), pl.program_id(1)
-
-        @pl.when((e == 0) & (step == 0))
-        def _():
-            for m in range(slots):
-                for r in range(slots):
-                    lane = pl.ds(pl.multiple_of((place_ref[1] ^ r ^ m) * rows, 128), rows)
-                    index = place_ref[0] ^ r
-                    block = piece_refs[m * slots + r][...]
-                    if aligned(depth):
-                        rows_ref[pl.ds(pl.multiple_of(index * depth, 16), depth), lane] = block
-                    else:
-                        stage_ref[index, :, lane] = block
-            if not aligned(depth):
-                for index in range(slots):
-                    rows_ref[index * depth : (index + 1) * depth, :] = stage_ref[index]
-            plain = rows_ref[...].astype(jnp.float32)
-            square = jnp.sum(dot(table_ref[...], (plain * plain).astype(jnp.bfloat16)), axis=0, keepdims=True)
-            scale_ref[...] = lax.rsqrt(square / D + 1e-05)
-
-        for index in range(experts):
-
-            @pl.when(e == index)
-            def _():
-                gate = dot(weight_refs[index][0], rows_ref[...]) * scale_ref[...]
-                up = dot(weight_refs[index][1], rows_ref[...]) * scale_ref[...]
-                out_ref[0] = ((up + 1.0) * gate * jax.nn.sigmoid(1.702 * gate)).astype(jnp.bfloat16)
-
-    def weight_spec(index):
-        def place(e, step):
-            return (0, jnp.where(e == index, step, jnp.where(e < index, 0, tiles - 1)), 0)
-
-        return pl.BlockSpec((2, tile, D), place)
+        out_ref, rows_ref, stage_ref = refs[slots * slots + 1 + experts :]
+        for m in range(slots):
+            for r in range(slots):
+                lane = pl.ds(pl.multiple_of((place_ref[1] ^ r ^ m) * rows, 128), rows)
+                index = place_ref[0] ^ r
+                block = piece_refs[m * slots + r][...]
+                if aligned(depth):
+                    rows_ref[pl.ds(pl.multiple_of(index * depth, 16), depth), lane] = block
+                else:
+                    stage_ref[index, :, lane] = block
+        if not aligned(depth):
+            for index in range(slots):
+                rows_ref[index * depth : (index + 1) * depth, :] = stage_ref[index]
+        plain = rows_ref[...].astype(jnp.float32)
+        square = jnp.sum(dot(table_ref[...], (plain * plain).astype(jnp.bfloat16)), axis=0, keepdims=True)
+        scale = lax.rsqrt(square / D + 1e-05)
+        for e in range(experts):
+            gate = dot(weight_refs[e][0], rows_ref[...]) * scale
+            up = dot(weight_refs[e][1], rows_ref[...]) * scale
+            out_ref[e] = ((up + 1.0) * gate * jax.nn.sigmoid(1.702 * gate)).astype(jnp.bfloat16)
 
     flat = [piece for part in pieces for piece in part]
     return pl.pallas_call(
         kernel,
-        grid=(experts, tiles),
         out_shape=jax.ShapeDtypeStruct((experts, units, lanes), jnp.bfloat16),
-        in_specs=[in_smem()] + in_vmem(len(flat) + 1) + [weight_spec(index) for index in range(experts)],
-        out_specs=pl.BlockSpec((1, tile, lanes), lambda e, step: (e, step, 0)),
+        in_specs=[in_smem()] + in_vmem(len(flat) + 1 + experts),
+        out_specs=in_vmem(1)[0],
         scratch_shapes=[
             pltpu.VMEM((D, lanes), jnp.bfloat16),
-            pltpu.VMEM((1, lanes), jnp.float32),
             pltpu.VMEM((1, 16, 128) if aligned(depth) else (slots, depth, lanes), jnp.bfloat16),
         ],
         compiler_params=params(),
@@ -236,27 +212,21 @@
     experts, units, lanes = activated[0].shape
     width = weights[0].shape[0]
     rows = lanes // slots
-    tile = tile_of(width)
-    tiles = width // tile
 
     def kernel(t_ref, *refs):
         activated_refs = refs[:t_count]
         share_ref = refs[t_count]
         weight_refs = refs[t_count + 1 : t_count + 1 + experts]
         *out_refs, all_ref, stage_ref = refs[t_count + 1 + experts :]
-
-        @pl.when(pl.program_id(0) == 0)
-        def _():
-            for u in range(t_count):
-                index = t_ref[0] ^ u
-                if aligned(units):
-                    all_ref[:, pl.ds(pl.multiple_of(index * units, 16), units), :] = activated_refs[u][...]
-                else:
-                    stage_ref[index] = activated_refs[u][...]
-            if not aligned(units):
-                for index in range(t_count):
-                    all_ref[:, index * units : (index + 1) * units, :] = stage_ref[index]
-
+        for u in range(t_count):
+            index = t_ref[0] ^ u
+            if aligned(units):
+                all_ref[:, pl.ds(pl.multiple_of(index * units, 16), units), :] = activated_refs[u][...]
+            else:
+                stage_ref[index] = activated_refs[u][...]
+        if not aligned(units):
+            for index in range(t_count):
+                all_ref[:, index * units : (index + 1) * units, :] = stage_ref[index]
         total = 0.0
         for e in range(experts):
             result = dot(weight_refs[e][...], all_ref[e]).astype(jnp.bfloat16).astype(jnp.float32)
@@ -266,12 +236,9 @@
 
     return pl.pallas_call(
         kernel,
-        grid=(tiles,),
         out_shape=tuple(jax.ShapeDtypeStruct((width, rows), jnp.bfloat16) for _ in range(slots)),
-        in_specs=[in_smem()]
-        + in_vmem(t_count + 1)
-        + [pl.BlockSpec((tile, t_count * units), lambda step: (step, 0))] * experts,
-        out_specs=tuple(pl.BlockSpec((tile, rows), lambda step: (step, 0)) for _ in range(slots)),
+        in_specs=[in_smem()] + in_vmem(t_count + 1 + experts),
+        out_specs=tuple(in_vmem(slots)),
         scratch_shapes=[
             pltpu.VMEM((experts, t_count * units, lanes), jnp.bfloat16),
             pltpu.VMEM((1, 1, 16, 128) if aligned(units) else (t_count, experts, units, lanes), jnp.bfloat16),
@@ -307,12 +274,17 @@
     pair = z // group
 
     first = (lax.axis_index(("ep", "sub")) == 0).astype(jnp.int32).reshape(1)
-    attended = attention(queries, key_rows, value_rows, sink_logits, first)
+    earlier_keys = shifted(key_rows, ("ep", "sub"), 1)
+    earlier_values = shifted(value_rows, ("ep", "sub"), 1)
+    attended = attention(
+        queries, earlier_keys, key_rows, earlier_values, value_rows, sink_logits, first
+    )
 
     out_weight = out_weight.T
     depth = out_weight.shape[1] // s_count
-    near = swapped(lax.dynamic_slice_in_dim(out_weight, s * depth, depth, 1), "ep", 1)
-    near, attended = lax.optimization_barrier((near, attended))
+    near, _ = lax.optimization_barrier((out_weight, earlier_values))
+    near = swapped(lax.dynamic_slice_in_dim(near, s * depth, depth, 1), "ep", 1)
+    near, _ = lax.optimization_barrier((near, attended))
     near_weights = [near] + [swapped(near, "sub", u) for u in range(1, s_count)]
 
     expert_in = expert_in[0].transpose(0, 2, 1)

time: 209 us -> 225 us (1.077)
  waiting for transfers between devices: 85.9 us -> 103 us
  local copies, waits for them, and re-layouts: 16.1 us -> 23.5 us
  Pallas kernels: 46 us -> 39 us
    ppermute x21, waiting for transfers between devices: 82.1 us -> 90.8 us  [swapped(): lax.ppermute(block, axis, [(i, i ^ distance) for i in range(lax.axis_size...]
    ppermute x2, waiting for transfers between devices: 3.86 us -> 12 us  [shifted(): return lax.ppermute(block, axis, route)]
    unnamed x33 -> x39, local copies, waits for them, and re-layouts: 11.9 us -> 19.3 us
    pallas_call x4, Pallas kernels: 35.5 us -> 29.5 us  [the longest x2 17.5 us: activate(): pl.pallas_call(kernel, out_shape=jax.ShapeDtypeStruct((experts, units, la...]
  transfers between devices with their start and end apart: 24 -> 24, of which waited for: 13 -> 12; matrix products, arithmetic and copies ran while one was open for 6% -> 6% of each run, Pallas kernels for 22% -> 17%
where the time goes in v4:
time: 225 us; the launch traced here: 224 us
  waiting for transfers between devices  103 us (46%)
  starting transfers between devices  54.3 us (24%)
  Pallas kernels  39 us (17%)
  local copies, waits for them, and re-layouts  23.5 us (10%)
  other arithmetic  4.24 us (2%)
    ppermute x21, waiting for transfers between devices, swapped(): lax.ppermute(block, axis, [(i, i ^ distance) for i in range(lax.axis_size...  90.8 us
    ppermute x21, starting transfers between devices, swapped(): lax.ppermute(block, axis, [(i, i ^ distance) for i in range(lax.axis_size...  45.8 us
    unnamed x39, local copies, waits for them, and re-layouts  19.3 us
    pallas_call x2, Pallas kernels, activate(): pl.pallas_call(kernel, out_shape=jax.ShapeDtypeStruct((experts, units, la...  17.5 us
    pallas_call x2, Pallas kernels, combine(): pl.pallas_call(kernel, out_shape=tuple((jax.ShapeDtypeStruct((width, rows...  12 us
    ppermute x2, waiting for transfers between devices, shifted(): return lax.ppermute(block, axis, route)  12 us
    pallas_call x1, Pallas kernels, attention(): pl.pallas_call(attention_kernel, out_shape=jax.ShapeDtypeStruct((width, r...  5.55 us
  transfers between devices with their start and end apart: 24, of which 12 were waited for; matrix products, arithmetic and copies ran while one was open for 6% of the time, Pallas kernels for 17%

profile of v4, /device:TPU:0, one launch (start us, length us, event | category | flops | bytes accessed | tf_op | source)
XLA Modules:
  0.0 224.1 jit_solution(1818620367251555668)
XLA Ops:
  0.5 2.1 collective-permute-start.1
  2.6 11.1 %collective-permute-done.1.vp_ref = bf16[128,256]{1,0:T(8,128)(2,1)S(1)} collective-permute-done((bf16[128,256]{1,0:T(8,128)(2,1)}, bf16[128,256]{1,0:T(8,128)(2,1)S(1)}, u32[]{:S(2)}, u32[]{:S(2)}) %collective-permute-start.1) | collective-permute-done | bytes 65568 | tf_op jit(solution)/shard_map/ppermute | solution.py:18
  13.8 2.6 %constant_dynamic-slice_fusion = bf16[720,1024]{1,0:T(8,128)(2,1)} fusion(bf16[720,2048]{1,0:T(8,128)(2,1)} %bitcast.62, s32[]{:T(128)S(6)} %select_n.79), kind=kLoop, calls=%fused_computation.25 | loop fusion | bytes 2949124 | tf_op jit(solution)/shard_map/dynamic_slice | solution.py:286
  16.4 2.6 %collective-permute-start.3 = (bf16[720,1024]{1,0:T(8,128)(2,1)}, bf16[720,1024]{1,0:T(8,128)(2,1)S(1)}, u32[]{:S(2)}, u32[]{:S(2)}) collective-permute-start(bf16[720,1024]{1,0:T(8,128)(2,1)} %constant_dynamic-slice_fusion), channel_id=1, source_target_pairs={{0,4},{4,0},{8,12},{12,8},{1,5},{5,1},{9,13},{13,9},{2,6},{6,2},{1... | collective-permute-start | bytes 4423688 | tf_op jit(solution)/shard_map/ppermute | solution.py:22
  18.9 2.0 collective-permute-start
  20.9 0.9 collective-permute-done.kp_ref
  21.8 5.5 %attention.1.refs_0_ = bf16[2048,128]{1,0:T(8,128)(2,1)S(1)} custom-call(s32[1]{0:T(128)} %bitcast.3.first_ref, f32[32]{0:T(128)S(1)} %copy-done.15, bf16[128,2048]{1,0:T(8,128)(2,1)S(1)} %copy-done.6, bf16[128,256]{1,0:T(8,128)(2,1)S(1)} %collective-permute-done.kp_ref, bf16[128,256]{1,0:T(8,128)(2,1)S(1)} %copy-done.13, ...), custom_call_target="tpu_custom_call" | custom-call | flops 268435456 | bytes 1572864 | tf_op jit(solution)/shard_map/attention/pallas_call | solution.py:105
  27.4 24.6 %collective-permute-done.3.refs_3_ = bf16[720,1024]{1,0:T(8,128)(2,1)S(1)} collective-permute-done((bf16[720,1024]{1,0:T(8,128)(2,1)}, bf16[720,1024]{1,0:T(8,128)(2,1)S(1)}, u32[]{:S(2)}, u32[]{:S(2)}) %collective-permute-start.3) | collective-permute-done | bytes 1474592 | tf_op jit(solution)/shard_map/ppermute | solution.py:22
  52.0 5.8 %collective-permute-start.4 = (bf16[720,1024]{1,0:T(8,128)(2,1)S(1)}, bf16[720,1024]{1,0:T(8,128)(2,1)}, u32[]{:S(2)}, u32[]{:S(2)}) collective-permute-start(bf16[720,1024]{1,0:T(8,128)(2,1)S(1)} %collective-permute-done.3.refs_3_), channel_id=1, source_target_pairs={{0,1},{1,0},{2,3},{3,2},{4,5},{5,4},{6,7},{7,6},{8,9},{9,8},{10,11... | collective-permute-start | bytes 4423688 | tf_op jit(solution)/shard_map/ppermute | solution.py:22
  57.8 2.6 %collective-permute-start.2 = (bf16[2048,128]{1,0:T(8,128)(2,1)S(1)}, bf16[2048,128]{1,0:T(8,128)(2,1)S(1)}, u32[]{:S(2)}, u32[]{:S(2)}) collective-permute-start(bf16[2048,128]{1,0:T(8,128)(2,1)S(1)} %attention.1.refs_0_), channel_id=1, source_target_pairs={{0,8},{4,12},{8,0},{12,4},{1,9},{5,13},{9,1},{13,5},{2,10},{6,14},... | collective-permute-start | bytes 1572872 | tf_op jit(solution)/shard_map/ppermute | solution.py:22
  60.3 0.8 dynamic-slice_bitcast_fusion
  61.1 4.4 %collective-permute-start.5 = (bf16[1440,128]{1,0:T(8,128)(2,1)}, bf16[1440,128]{1,0:T(8,128)(2,1)}, u32[]{:S(2)}, u32[]{:S(2)}) collective-permute-start(bf16[1440,128]{1,0:T(8,128)(2,1)} %dynamic-slice_bitcast_fusion), channel_id=1, source_target_pairs={{0,0},{2,10},{4,4},{6,14},{8,8},{10,2},{12,12},{14,6},{1,1},{3,11}... | collective-permute-start | bytes 1105928 | tf_op jit(solution)/shard_map/ppermute | solution.py:299
  65.5 6.4 %copy.19 = bf16[1,1440,1440]{1,2,0:T(8,128)(2,1)} copy(bf16[1,1440,1440]{2,1,0:T(8,128)(2,1)} %param.19) | data formatting | bytes 8294400 | tf_op args[8]
  72.0 11.8 %collective-permute-done.2.refs_1_ = bf16[2048,128]{1,0:T(8,128)(2,1)S(1)} collective-permute-done((bf16[2048,128]{1,0:T(8,128)(2,1)S(1)}, bf16[2048,128]{1,0:T(8,128)(2,1)S(1)}, u32[]{:S(2)}, u32[]{:S(2)}) %collective-permute-start.2) | collective-permute-done | bytes 524320 | tf_op jit(solution)/shard_map/ppermute | solution.py:22
  83.8 0.8 copy-done.7
  84.6 1.8 copy-done.3
  86.5 1.0 copy-done.8
  87.5 4.0 %project.1 = (f32[2,720,128]{2,1,0:T(8,128)S(1)}, bf16[1,2,720,128]{3,2,1,0:T(8,128)(2,1)}) custom-call(s32[3]{0:T(128)S(1)} %pad_add_fusion.place_ref, bf16[2048,128]{1,0:T(8,128)(2,1)S(1)} %attention.1.refs_0_, bf16[2048,128]{1,0:T(8,128)(2,1)S(1)} %copy-done.8, bf16[720,2048]{1,0:T(8,128)(2,1)S(1)} %bitcast.63, ...), custom_call_target="tpu_custom_call" | custom-call | flops 1509949440 | bytes 5898240 | tf_op jit(solution)/shard_map/project/pallas_call | solution.py:147
  91.5 10.3 %collective-permute-start.6 = (bf16[1440,128]{1,0:T(8,128)(2,1)}, bf16[1440,128]{1,0:T(8,128)(2,1)S(1)}, u32[]{:S(2)}, u32[]{:S(2)}) collective-permute-start(bf16[1440,128]{1,0:T(8,128)(2,1)} %bitcast.9), channel_id=1, source_target_pairs={{0,2},{2,0},{1,3},{3,1},{4,6},{6,4},{5,7},{7,5},{8,10},{10,8},{9,1... | collective-permute-start | bytes 1105928 | tf_op jit(solution)/shard_map/ppermute | solution.py:22
  101.9 7.2 %collective-permute-done.6 = bf16[1440,128]{1,0:T(8,128)(2,1)S(1)} collective-permute-done((bf16[1440,128]{1,0:T(8,128)(2,1)}, bf16[1440,128]{1,0:T(8,128)(2,1)S(1)}, u32[]{:S(2)}, u32[]{:S(2)}) %collective-permute-start.6) | collective-permute-done | bytes 368672 | tf_op jit(solution)/shard_map/ppermute | solution.py:22
  109.1 1.3 fusion.2.refs_0_
  110.5 4.4 %collective-permute-start.14 = (f32[8,128]{1,0:T(8,128)S(1)}, f32[8,128]{1,0:T(8,128)S(1)}, u32[]{:S(2)}, u32[]{:S(2)}) collective-permute-start(f32[8,128]{1,0:T(8,128)S(1)} %select_reduce_fusion), channel_id=1, source_target_pairs={{0,12},{4,8},{8,4},{12,0},{1,13},{5,9},{9,5},{13,1},{2,14},{6,10},... | collective-permute-start | bytes 12296 | tf_op jit(solution)/shard_map/ppermute | solution.py:22
  115.6 12.1 %collective-permute-done.7.refs_1_ = bf16[1440,128]{1,0:T(8,128)(2,1)S(1)} collective-permute-done((bf16[1440,128]{1,0:T(8,128)(2,1)S(1)}, bf16[1440,128]{1,0:T(8,128)(2,1)S(1)}, u32[]{:S(2)}, u32[]{:S(2)}) %collective-permute-start.7) | collective-permute-done | bytes 368672 | tf_op jit(solution)/shard_map/ppermute | solution.py:22
  127.8 2.8 %collective-permute-done.17.refs_0_ = bf16[1440,128]{1,0:T(8,128)(2,1)S(1)} collective-permute-done((bf16[1440,128]{1,0:T(8,128)(2,1)S(1)}, bf16[1440,128]{1,0:T(8,128)(2,1)S(1)}, u32[]{:S(2)}, u32[]{:S(2)}) %collective-permute-start.17) | collective-permute-done | bytes 368672 | tf_op jit(solution)/shard_map/ppermute | solution.py:22
  130.6 1.4 collective-permute-start.19
  132.0 5.0 %collective-permute-done.18.refs_1_ = bf16[1440,128]{1,0:T(8,128)(2,1)S(1)} collective-permute-done((bf16[1440,128]{1,0:T(8,128)(2,1)S(1)}, bf16[1440,128]{1,0:T(8,128)(2,1)S(1)}, u32[]{:S(2)}, u32[]{:S(2)}) %collective-permute-start.18) | collective-permute-done | bytes 368672 | tf_op jit(solution)/shard_map/ppermute | solution.py:22
  137.1 1.5 collective-permute-start.20
  138.8 0.7 copy-done.9
  139.5 3.0 %collective-permute-start.13 = (f32[8,128]{1,0:T(8,128)S(1)}, f32[8,128]{1,0:T(8,128)S(1)}, u32[]{:S(2)}, u32[]{:S(2)}) collective-permute-start(f32[8,128]{1,0:T(8,128)S(1)} %select_reduce_fusion), channel_id=1, source_target_pairs={{0,8},{4,12},{8,0},{12,4},{1,9},{5,13},{9,1},{13,5},{2,10},{6,14},... | collective-permute-start | bytes 12296 | tf_op jit(solution)/shard_map/ppermute | solution.py:22
  142.5 3.5 %collective-permute-done.20.refs_3_ = bf16[1440,128]{1,0:T(8,128)(2,1)S(1)} collective-permute-done((bf16[1440,128]{1,0:T(8,128)(2,1)S(1)}, bf16[1440,128]{1,0:T(8,128)(2,1)S(1)}, u32[]{:S(2)}, u32[]{:S(2)}) %collective-permute-start.20) | collective-permute-done | bytes 368672 | tf_op jit(solution)/shard_map/ppermute | solution.py:22
  146.0 0.8 copy-done.11
  146.8 1.4 collective-permute-start.8
  148.8 3.4 %copy-done.2 = bf16[1,2,2880,720]{2,3,1,0:T(8,128)(2,1)S(1)} copy-done((bf16[1,2,2880,720]{2,3,1,0:T(8,128)(2,1)S(1)}, bf16[1,2,2880,720]{2,3,1,0:T(8,128)(2,1)}, u32[]{:S(2)}) %copy-start.2) | copy-done | bytes 8294424
  152.2 1.0 copy-done.10
  153.2 1.0 copy-done.12
  154.2 8.7 %activate.3.refs_0_ = bf16[2,720,256]{2,1,0:T(8,128)(2,1)S(1)} custom-call(s32[2]{0:T(128)S(1)} %pad_add_fusion.1.place_ref, bf16[1440,128]{1,0:T(8,128)(2,1)S(1)} %collective-permute-done.17.refs_0_, bf16[1440,128]{1,0:T(8,128)(2,1)S(1)} %collective-permute-done.18.refs_1_, bf16[1440,128]{1,0:T(8,128)(2,1)S(1)} %copy-done.10, ...), custom_call_target="tpu_custom_call" | custom-call | flops 4246732800 | bytes 16588800 | tf_op jit(solution)/shard_map/activate/pallas_call | solution.py:195
  163.0 1.5 collective-permute-start.21
  164.5 8.7 %activate.2.refs_0_ = bf16[2,720,256]{2,1,0:T(8,128)(2,1)S(1)} custom-call(s32[2]{0:T(128)S(1)} %pad_add_fusion.1.place_ref, bf16[1440,128]{1,0:T(8,128)(2,1)S(1)} %fusion.2.refs_0_, bf16[1440,128]{1,0:T(8,128)(2,1)S(1)} %collective-permute-done.7.refs_1_, bf16[1440,128]{1,0:T(8,128)(2,1)S(1)} %collective-permute-done.8.refs_2_, ...), custom_call_target="tpu_custom_call" | custom-call | flops 4246732800 | bytes 16588800 | tf_op jit(solution)/shard_map/activate/pallas_call | solution.py:195
  174.6 8.0 %collective-permute-done.21.refs_1_ = bf16[2,720,256]{2,1,0:T(8,128)(2,1)} collective-permute-done((bf16[2,720,256]{2,1,0:T(8,128)(2,1)S(1)}, bf16[2,720,256]{2,1,0:T(8,128)(2,1)}, u32[]{:S(2)}, u32[]{:S(2)}) %collective-permute-start.21) | collective-permute-done | bytes 737312 | tf_op jit(solution)/shard_map/ppermute | solution.py:22
  182.6 2.3 %copy-done.1 = bf16[1,1440,1440]{1,2,0:T(8,128)(2,1)S(1)} copy-done((bf16[1,1440,1440]{1,2,0:T(8,128)(2,1)S(1)}, bf16[1,1440,1440]{1,2,0:T(8,128)(2,1)}, u32[]{:S(2)}) %copy-start.1) | copy-done | bytes 4147224
  184.9 6.2 %combine.3 = (bf16[1440,128]{1,0:T(8,128)(2,1)}, bf16[1440,128]{1,0:T(8,128)(2,1)}) custom-call(s32[1]{0:T(128)} %bitcast.t_ref, bf16[2,720,256]{2,1,0:T(8,128)(2,1)S(1)} %activate.3.refs_0_, bf16[2,720,256]{2,1,0:T(8,128)(2,1)} %collective-permute-done.21.refs_1_, f32[2,256]{1,0:T(2,128)S(1)} %get-tuple-element.25.refs_2_, bf16[1440,1440]{1,0:T(8,128)(2,1)S(1)} %bitcast.57, ...), custom_call_target="tpu_custom_call" | custom-call | flops 2123366400 | bytes 8294400 | tf_op jit(solution)/shard_map/combine/pallas_call | solution.py:237
  191.0 5.2 %collective-permute-start.23 = (bf16[1440,128]{1,0:T(8,128)(2,1)}, bf16[1440,128]{1,0:T(8,128)(2,1)}, u32[]{:S(2)}, u32[]{:S(2)}) collective-permute-start(bf16[1440,128]{1,0:T(8,128)(2,1)} %get-tuple-element.20), channel_id=1, source_target_pairs={{0,12},{4,8},{8,4},{12,0},{1,13},{5,9},{9,5},{13,1},{2,14},{6,10},... | collective-permute-start | bytes 1105928 | tf_op jit(solution)/shard_map/ppermute | solution.py:22
  196.2 1.0 collective-permute-start.22
  197.3 5.9 %combine.2 = (bf16[1440,128]{1,0:T(8,128)(2,1)S(1)}, bf16[1440,128]{1,0:T(8,128)(2,1)}) custom-call(s32[1]{0:T(128)} %bitcast.t_ref, bf16[2,720,256]{2,1,0:T(8,128)(2,1)S(1)} %activate.2.refs_0_, bf16[2,720,256]{2,1,0:T(8,128)(2,1)} %collective-permute-done.11.refs_1_, f32[2,256]{1,0:T(2,128)S(1)} %get-tuple-element.24.refs_2_, ...), custom_call_target="tpu_custom_call" | custom-call | flops 2123366400 | bytes 8294400 | tf_op jit(solution)/shard_map/combine/pallas_call | solution.py:237
  203.2 2.7 %collective-permute-start.16 = (bf16[1440,128]{1,0:T(8,128)(2,1)}, bf16[1440,128]{1,0:T(8,128)(2,1)S(1)}, u32[]{:S(2)}, u32[]{:S(2)}) collective-permute-start(bf16[1440,128]{1,0:T(8,128)(2,1)} %get-tuple-element.18), channel_id=1, source_target_pairs={{0,8},{4,12},{8,0},{12,4},{1,9},{5,13},{9,1},{13,5},{2,10},{6,14},... | collective-permute-start | bytes 1105928 | tf_op jit(solution)/shard_map/ppermute | solution.py:22
  205.9 2.9 %collective-permute-done.22 = bf16[1440,128]{1,0:T(8,128)(2,1)} collective-permute-done((bf16[1440,128]{1,0:T(8,128)(2,1)}, bf16[1440,128]{1,0:T(8,128)(2,1)}, u32[]{:S(2)}, u32[]{:S(2)}) %collective-permute-start.22) | collective-permute-done | bytes 368672 | tf_op jit(solution)/shard_map/ppermute | solution.py:22
  208.8 12.9 %collective-permute-done.16 = bf16[1440,128]{1,0:T(8,128)(2,1)S(1)} collective-permute-done((bf16[1440,128]{1,0:T(8,128)(2,1)}, bf16[1440,128]{1,0:T(8,128)(2,1)S(1)}, u32[]{:S(2)}, u32[]{:S(2)}) %collective-permute-start.16) | collective-permute-done | bytes 368672 | tf_op jit(solution)/shard_map/ppermute | solution.py:22
  221.7 2.4 %fusion.3 = bf16[128,1440]{0,1:T(8,128)(2,1)} fusion(bf16[1440,128]{1,0:T(8,128)(2,1)} %collective-permute-done.23, bf16[1440,128]{1,0:T(8,128)(2,1)} %collective-permute-done.22, bf16[1440,128]{1,0:T(8,128)(2,1)S(1)} %collective-permute-done.16, bf16[1440,128]{1,0:T(8,128)(2,1)S(1)} %get-tuple-element.17, f32[1440]{0:T(1024)S(1)} %dynamic_slice.17, ...), kind=kLoop, calls=%fused_computation.7 | loop fusion | flops 3870720 | bytes 3323524 | tf_op jit(solution)/shard_map/transpose | solution.py:349
  (71 shorter events, 3.9 us)
Async XLA Ops:
  0.0 60.3 %copy-start = (bf16[128,2880]{0,1:T(8,128)(2,1)S(1)}, bf16[128,2880]{0,1:T(8,128)(2,1)}, u32[]{:S(2)}) copy-start(bf16[128,2880]{0,1:T(8,128)(2,1)} %param.16) | copy-start | bytes 2211844
  0.0 21.8 %copy-start.14 = (bf16[128,256]{1,0:T(8,128)(2,1)S(1)}, bf16[128,256]{1,0:T(8,128)(2,1)}, u32[]{:S(2)}) copy-start(bf16[128,256]{1,0:T(8,128)(2,1)} %v_ref.1) | copy-start | bytes 196612
  0.0 18.9 %copy-start.13 = (bf16[128,256]{1,0:T(8,128)(2,1)S(1)}, bf16[128,256]{1,0:T(8,128)(2,1)}, u32[]{:S(2)}) copy-start(bf16[128,256]{1,0:T(8,128)(2,1)} %k_ref.1) | copy-start | bytes 196612
  0.0 21.8 %copy-start.15 = (f32[32]{0:T(128)S(1)}, f32[32]{0:T(128)}, u32[]{:S(2)}) copy-start(f32[32]{0:T(128)} %sink_ref.1) | copy-start | bytes 388
  0.0 21.8 %copy-start.6 = (bf16[128,2048]{1,0:T(8,128)(2,1)S(1)}, bf16[128,2048]{1,0:T(8,128)(2,1)}, u32[]{:S(2)}) copy-start(bf16[128,2048]{1,0:T(8,128)(2,1)} %q_ref.1) | copy-start | bytes 1572868
  0.0 148.2 %collective-permute-start.10 = (bf16[2,720,2880]{2,1,0:T(8,128)(2,1)}, bf16[2,720,2880]{2,1,0:T(8,128)(2,1)}, u32[]{:S(2)}, u32[]{:S(2)}) collective-permute-start(bf16[2,720,2880]{2,1,0:T(8,128)(2,1)} %bitcast.59), channel_id=1, source_target_pairs={{0,1},{1,0},{2,3},{3,2},{4,5},{5,4},{6,7},{7,6},{8,9},{9,8},{10,11... | collective-permute-start | bytes 24883208 | tf_op jit(solution)/shard_map/ppermute | solution.py:22
  0.5 13.2 %collective-permute-start.1 = (bf16[128,256]{1,0:T(8,128)(2,1)}, bf16[128,256]{1,0:T(8,128)(2,1)S(1)}, u32[]{:S(2)}, u32[]{:S(2)}) collective-permute-start(bf16[128,256]{1,0:T(8,128)(2,1)} %v_ref.1), channel_id=1, source_target_pairs={{0,1},{1,4},{4,5},{5,8},{8,9},{9,12},{12,13},{2,3},{3,6},{6,7},{7,... | collective-permute-start | bytes 196616 | tf_op jit(solution)/shard_map/ppermute | solution.py:18
  16.4 35.6 %collective-permute-start.3 = (bf16[720,1024]{1,0:T(8,128)(2,1)}, bf16[720,1024]{1,0:T(8,128)(2,1)S(1)}, u32[]{:S(2)}, u32[]{:S(2)}) collective-permute-start(bf16[720,1024]{1,0:T(8,128)(2,1)} %constant_dynamic-slice_fusion), channel_id=1, source_target_pairs={{0,4},{4,0},{8,12},{12,8},{1,5},{5,1},{9,13},{13,9},{2,6},{6,2},{1... | collective-permute-start | bytes 4423688 | tf_op jit(solution)/shard_map/ppermute | solution.py:22
  18.9 2.9 %collective-permute-start = (bf16[128,256]{1,0:T(8,128)(2,1)S(1)}, bf16[128,256]{1,0:T(8,128)(2,1)S(1)}, u32[]{:S(2)}, u32[]{:S(2)}) collective-permute-start(bf16[128,256]{1,0:T(8,128)(2,1)S(1)} %copy-done.13), channel_id=1, source_target_pairs={{0,1},{1,4},{4,5},{5,8},{8,9},{9,12},{12,13},{2,3},{3,6},{6,7},{7,... | collective-permute-start | bytes 196616 | tf_op jit(solution)/shard_map/ppermute | solution.py:18
  52.0 32.7 %collective-permute-start.4 = (bf16[720,1024]{1,0:T(8,128)(2,1)S(1)}, bf16[720,1024]{1,0:T(8,128)(2,1)}, u32[]{:S(2)}, u32[]{:S(2)}) collective-permute-start(bf16[720,1024]{1,0:T(8,128)(2,1)S(1)} %collective-permute-done.3.refs_3_), channel_id=1, source_target_pairs={{0,1},{1,0},{2,3},{3,2},{4,5},{5,4},{6,7},{7,6},{8,9},{9,8},{10,11... | collective-permute-start | bytes 4423688 | tf_op jit(solution)/shard_map/ppermute | solution.py:22
  57.8 26.0 %collective-permute-start.2 = (bf16[2048,128]{1,0:T(8,128)(2,1)S(1)}, bf16[2048,128]{1,0:T(8,128)(2,1)S(1)}, u32[]{:S(2)}, u32[]{:S(2)}) collective-permute-start(bf16[2048,128]{1,0:T(8,128)(2,1)S(1)} %attention.1.refs_0_), channel_id=1, source_target_pairs={{0,8},{4,12},{8,0},{12,4},{1,9},{5,13},{9,1},{13,5},{2,10},{6,14},... | collective-permute-start | bytes 1572872 | tf_op jit(solution)/shard_map/ppermute | solution.py:22
  61.1 40.8 %collective-permute-start.5 = (bf16[1440,128]{1,0:T(8,128)(2,1)}, bf16[1440,128]{1,0:T(8,128)(2,1)}, u32[]{:S(2)}, u32[]{:S(2)}) collective-permute-start(bf16[1440,128]{1,0:T(8,128)(2,1)} %dynamic-slice_bitcast_fusion), channel_id=1, source_target_pairs={{0,0},{2,10},{4,4},{6,14},{8,8},{10,2},{12,12},{14,6},{1,1},{3,11}... | collective-permute-start | bytes 1105928 | tf_op jit(solution)/shard_map/ppermute | solution.py:299
  71.9 102.7 %collective-permute-start.15 = (bf16[1440,1440]{1,0:T(8,128)(2,1)}, bf16[1440,1440]{1,0:T(8,128)(2,1)}, u32[]{:S(2)}, u32[]{:S(2)}) collective-permute-start(bf16[1440,1440]{1,0:T(8,128)(2,1)} %bitcast.56), channel_id=1, source_target_pairs={{0,1},{1,0},{2,3},{3,2},{4,5},{5,4},{6,7},{7,6},{8,9},{9,8},{10,11... | collective-permute-start | bytes 12441608 | tf_op jit(solution)/shard_map/ppermute | solution.py:22
  71.9 29.9 %copy-start.17 = (s32[128,4]{0,1:T(4,128)S(1)}, s32[128,4]{0,1:T(4,128)}, u32[]{:S(2)}) copy-start(s32[128,4]{0,1:T(4,128)} %param.21) | copy-start | bytes 6148
  83.8 0.8 copy-start.7
  84.6 1.8 copy-start.3
  86.5 1.0 copy-start.8
  87.5 14.2 %copy-start.16 = (f32[2880]{0:T(1024)S(1)}, f32[2880]{0:T(1024)}, u32[]{:S(2)}) copy-start(f32[2880]{0:T(1024)} %param.17) | copy-start | bytes 34564
  87.5 23.0 %copy-start.18 = (s32[128,4]{0,1:T(4,128)S(1)}, s32[128,4]{0,1:T(4,128)}, u32[]{:S(2)}) copy-start(s32[128,4]{0,1:T(4,128)} %param.20) | copy-start | bytes 6148
  91.5 17.6 %collective-permute-start.6 = (bf16[1440,128]{1,0:T(8,128)(2,1)}, bf16[1440,128]{1,0:T(8,128)(2,1)S(1)}, u32[]{:S(2)}, u32[]{:S(2)}) collective-permute-start(bf16[1440,128]{1,0:T(8,128)(2,1)} %bitcast.9), channel_id=1, source_target_pairs={{0,2},{2,0},{1,3},{3,1},{4,6},{6,4},{5,7},{7,5},{8,10},{10,8},{9,1... | collective-permute-start | bytes 1105928 | tf_op jit(solution)/shard_map/ppermute | solution.py:22
  110.4 17.3 %collective-permute-start.7 = (bf16[1440,128]{1,0:T(8,128)(2,1)S(1)}, bf16[1440,128]{1,0:T(8,128)(2,1)S(1)}, u32[]{:S(2)}, u32[]{:S(2)}) collective-permute-start(bf16[1440,128]{1,0:T(8,128)(2,1)S(1)} %fusion.2.refs_0_), channel_id=1, source_target_pairs={{0,8},{4,12},{8,0},{12,4},{1,9},{5,13},{9,1},{13,5},{2,10},{6,14},... | collective-permute-start | bytes 1105928 | tf_op jit(solution)/shard_map/ppermute | solution.py:22
  110.5 62.8 %collective-permute-start.14 = (f32[8,128]{1,0:T(8,128)S(1)}, f32[8,128]{1,0:T(8,128)S(1)}, u32[]{:S(2)}, u32[]{:S(2)}) collective-permute-start(f32[8,128]{1,0:T(8,128)S(1)} %select_reduce_fusion), channel_id=1, source_target_pairs={{0,12},{4,8},{8,4},{12,0},{1,13},{5,9},{9,5},{13,1},{2,14},{6,10},... | collective-permute-start | bytes 12296 | tf_op jit(solution)/shard_map/ppermute | solution.py:22
  115.0 15.6 %collective-permute-start.17 = (bf16[1440,128]{1,0:T(8,128)(2,1)S(1)}, bf16[1440,128]{1,0:T(8,128)(2,1)S(1)}, u32[]{:S(2)}, u32[]{:S(2)}) collective-permute-start(bf16[1440,128]{1,0:T(8,128)(2,1)S(1)} %fusion.2.refs_0_), channel_id=1, source_target_pairs={{0,4},{4,0},{8,12},{12,8},{1,5},{5,1},{9,13},{13,9},{2,6},{6,2},{1... | collective-permute-start | bytes 1105928 | tf_op jit(solution)/shard_map/ppermute | solution.py:22
  127.7 9.4 %collective-permute-start.18 = (bf16[1440,128]{1,0:T(8,128)(2,1)S(1)}, bf16[1440,128]{1,0:T(8,128)(2,1)S(1)}, u32[]{:S(2)}, u32[]{:S(2)}) collective-permute-start(bf16[1440,128]{1,0:T(8,128)(2,1)S(1)} %collective-permute-done.7.refs_1_), channel_id=1, source_target_pairs={{0,4},{4,0},{8,12},{12,8},{1,5},{5,1},{9,13},{13,9},{2,6},{6,2},{1... | collective-permute-start | bytes 1105928 | tf_op jit(solution)/shard_map/ppermute | solution.py:22
  130.6 8.2 %collective-permute-start.19 = (bf16[1440,128]{1,0:T(8,128)(2,1)S(1)}, bf16[1440,128]{1,0:T(8,128)(2,1)S(1)}, u32[]{:S(2)}, u32[]{:S(2)}) collective-permute-start(bf16[1440,128]{1,0:T(8,128)(2,1)S(1)} %collective-permute-done.17.refs_0_), channel_id=1, source_target_pairs={{0,2},{2,0},{1,3},{3,1},{4,6},{6,4},{5,7},{7,5},{8,10},{10,8},{9,1... | collective-permute-start | bytes 1105928 | tf_op jit(solution)/shard_map/ppermute | solution.py:22
  137.1 8.9 %collective-permute-start.20 = (bf16[1440,128]{1,0:T(8,128)(2,1)S(1)}, bf16[1440,128]{1,0:T(8,128)(2,1)S(1)}, u32[]{:S(2)}, u32[]{:S(2)}) collective-permute-start(bf16[1440,128]{1,0:T(8,128)(2,1)S(1)} %collective-permute-done.18.refs_1_), channel_id=1, source_target_pairs={{0,2},{2,0},{1,3},{3,1},{4,6},{6,4},{5,7},{7,5},{8,10},{10,8},{9,1... | collective-permute-start | bytes 1105928 | tf_op jit(solution)/shard_map/ppermute | solution.py:22
  138.8 0.7 copy-start.9
  139.5 34.4 %collective-permute-start.13 = (f32[8,128]{1,0:T(8,128)S(1)}, f32[8,128]{1,0:T(8,128)S(1)}, u32[]{:S(2)}, u32[]{:S(2)}) collective-permute-start(f32[8,128]{1,0:T(8,128)S(1)} %select_reduce_fusion), channel_id=1, source_target_pairs={{0,8},{4,12},{8,0},{12,4},{1,9},{5,13},{9,1},{13,5},{2,10},{6,14},... | collective-permute-start | bytes 12296 | tf_op jit(solution)/shard_map/ppermute | solution.py:22
  146.0 0.8 copy-start.11
  146.8 16.1 %collective-permute-start.8 = (bf16[1440,128]{1,0:T(8,128)(2,1)S(1)}, bf16[1440,128]{1,0:T(8,128)(2,1)S(1)}, u32[]{:S(2)}, u32[]{:S(2)}) collective-permute-start(bf16[1440,128]{1,0:T(8,128)(2,1)S(1)} %fusion.2.refs_0_), channel_id=1, source_target_pairs={{0,2},{2,0},{1,3},{3,1},{4,6},{6,4},{5,7},{7,5},{8,10},{10,8},{9,1... | collective-permute-start | bytes 1105928 | tf_op jit(solution)/shard_map/ppermute | solution.py:22
  148.2 14.8 %collective-permute-start.9 = (bf16[1440,128]{1,0:T(8,128)(2,1)S(1)}, bf16[1440,128]{1,0:T(8,128)(2,1)S(1)}, u32[]{:S(2)}, u32[]{:S(2)}) collective-permute-start(bf16[1440,128]{1,0:T(8,128)(2,1)S(1)} %collective-permute-done.7.refs_1_), channel_id=1, source_target_pairs={{0,2},{2,0},{1,3},{3,1},{4,6},{6,4},{5,7},{7,5},{8,10},{10,8},{9,1... | collective-permute-start | bytes 1105928 | tf_op jit(solution)/shard_map/ppermute | solution.py:22
  148.8 3.4 %copy-start.2 = (bf16[1,2,2880,720]{2,3,1,0:T(8,128)(2,1)S(1)}, bf16[1,2,2880,720]{2,3,1,0:T(8,128)(2,1)}, u32[]{:S(2)}) copy-start(bf16[1,2,2880,720]{2,3,1,0:T(8,128)(2,1)} %param.18) | copy-start | bytes 24883204
  152.2 1.0 copy-start.10
  153.2 1.0 copy-start.12
  162.9 11.0 %collective-permute-start.12 = (f32[8,128]{1,0:T(8,128)S(1)}, f32[8,128]{1,0:T(8,128)S(1)}, u32[]{:S(2)}, u32[]{:S(2)}) collective-permute-start(f32[8,128]{1,0:T(8,128)S(1)} %select_reduce_fusion), channel_id=1, source_target_pairs={{0,4},{4,0},{8,12},{12,8},{1,5},{5,1},{9,13},{13,9},{2,6},{6,2},{1... | collective-permute-start | bytes 12296 | tf_op jit(solution)/shard_map/ppermute | solution.py:22
  163.0 10.3 %copy-start.4 = (bf16[1440,128]{1,0:T(8,128)(2,1)}, bf16[1440,128]{1,0:T(8,128)(2,1)S(1)}, u32[]{:S(2)}) copy-start(bf16[1440,128]{1,0:T(8,128)(2,1)S(1)} %collective-permute-done.9.refs_3_) | copy-start | bytes 1105924
  163.0 19.6 %collective-permute-start.21 = (bf16[2,720,256]{2,1,0:T(8,128)(2,1)S(1)}, bf16[2,720,256]{2,1,0:T(8,128)(2,1)}, u32[]{:S(2)}, u32[]{:S(2)}) collective-permute-start(bf16[2,720,256]{2,1,0:T(8,128)(2,1)S(1)} %activate.3.refs_0_), channel_id=1, source_target_pairs={{0,2},{2,0},{1,3},{3,1},{4,6},{6,4},{5,7},{7,5},{8,10},{10,8},{9,1... | collective-permute-start | bytes 2211848 | tf_op jit(solution)/shard_map/ppermute | solution.py:22
  173.3 24.0 %collective-permute-start.11 = (bf16[2,720,256]{2,1,0:T(8,128)(2,1)S(1)}, bf16[2,720,256]{2,1,0:T(8,128)(2,1)}, u32[]{:S(2)}, u32[]{:S(2)}) collective-permute-start(bf16[2,720,256]{2,1,0:T(8,128)(2,1)S(1)} %activate.2.refs_0_), channel_id=1, source_target_pairs={{0,2},{2,0},{1,3},{3,1},{4,6},{6,4},{5,7},{7,5},{8,10},{10,8},{9,1... | collective-permute-start | bytes 2211848 | tf_op jit(solution)/shard_map/ppermute | solution.py:22
  182.6 2.3 %copy-start.1 = (bf16[1,1440,1440]{1,2,0:T(8,128)(2,1)S(1)}, bf16[1,1440,1440]{1,2,0:T(8,128)(2,1)}, u32[]{:S(2)}) copy-start(bf16[1,1440,1440]{1,2,0:T(8,128)(2,1)} %copy.19) | copy-start | bytes 12441604
  191.0 14.9 %collective-permute-start.23 = (bf16[1440,128]{1,0:T(8,128)(2,1)}, bf16[1440,128]{1,0:T(8,128)(2,1)}, u32[]{:S(2)}, u32[]{:S(2)}) collective-permute-start(bf16[1440,128]{1,0:T(8,128)(2,1)} %get-tuple-element.20), channel_id=1, source_target_pairs={{0,12},{4,8},{8,4},{12,0},{1,13},{5,9},{9,5},{13,1},{2,14},{6,10},... | collective-permute-start | bytes 1105928 | tf_op jit(solution)/shard_map/ppermute | solution.py:22
  196.2 12.6 %collective-permute-start.22 = (bf16[1440,128]{1,0:T(8,128)(2,1)}, bf16[1440,128]{1,0:T(8,128)(2,1)}, u32[]{:S(2)}, u32[]{:S(2)}) collective-permute-start(bf16[1440,128]{1,0:T(8,128)(2,1)} %get-tuple-element.19), channel_id=1, source_target_pairs={{0,4},{4,0},{8,12},{12,8},{1,5},{5,1},{9,13},{13,9},{2,6},{6,2},{1... | collective-permute-start | bytes 1105928 | tf_op jit(solution)/shard_map/ppermute | solution.py:22
  197.3 24.4 %copy-start.5 = (bf16[1440,128]{1,0:T(8,128)(2,1)S(1)}, bf16[1440,128]{1,0:T(8,128)(2,1)}, u32[]{:S(2)}) copy-start(bf16[1440,128]{1,0:T(8,128)(2,1)} %copy-done.4) | copy-start | bytes 1105924
  203.2 18.5 %collective-permute-start.16 = (bf16[1440,128]{1,0:T(8,128)(2,1)}, bf16[1440,128]{1,0:T(8,128)(2,1)S(1)}, u32[]{:S(2)}, u32[]{:S(2)}) collective-permute-start(bf16[1440,128]{1,0:T(8,128)(2,1)} %get-tuple-element.18), channel_id=1, source_target_pairs={{0,8},{4,12},{8,0},{12,4},{1,9},{5,13},{9,1},{13,5},{2,10},{6,14},... | collective-permute-start | bytes 1105928 | tf_op jit(solution)/shard_map/ppermute | solution.py:22

commit v5 on v4

--- a/solution.py
+++ b/solution.py
@@ -50,7 +50,7 @@
     return pltpu.CompilerParams(vmem_limit_bytes=VMEM_BYTES)
 
 
-def attention_kernel(first_ref, sink_ref, q_ref, kp_ref, k_ref, vp_ref, v_ref, out_ref):
+def attention_kernel(first_ref, sink_ref, q_ref, earlier_ref, k_ref, v_ref, out_ref):
     rows = q_ref.shape[0]
     kv_count = k_ref.shape[1] // HD
     pairs = q_ref.shape[1] // (2 * HD * kv_count)
@@ -60,11 +60,15 @@
     shut = before & (first_ref[0] == 1)
     blank = jnp.zeros((2 * rows, HD), jnp.bfloat16)
     values = jnp.concatenate(
-        [ref[...].astype(jnp.float32).T.astype(jnp.bfloat16) for ref in (vp_ref, v_ref)], axis=1
+        [
+            block.astype(jnp.float32).T.astype(jnp.bfloat16)
+            for block in (earlier_ref[:, kv_count * HD :], v_ref[...])
+        ],
+        axis=1,
     )
     for g in range(kv_count):
         head = slice(g * HD, (g + 1) * HD)
-        keys = jnp.concatenate([kp_ref[:, head], k_ref[:, head]], axis=0) * jnp.bfloat16(HD ** (-0.5))
+        keys = jnp.concatenate([earlier_ref[:, head], k_ref[:, head]], axis=0) * jnp.bfloat16(HD ** (-0.5))
         keys = jnp.concatenate(
             [jnp.concatenate([keys, blank], axis=1), jnp.concatenate([blank, keys], axis=1)], axis=0
         )
@@ -100,63 +104,57 @@
             out_ref[start + HD : start + 2 * HD, :] = result[:, rows:]
 
 
-def attention(queries, earlier_keys, key_rows, earlier_values, value_rows, sink_logits, first):
+def attention(queries, earlier, key_rows, value_rows, sink_logits, first):
     rows, width = queries.shape
     return pl.pallas_call(
         attention_kernel,
         out_shape=jax.ShapeDtypeStruct((width, rows), jnp.bfloat16),
-        in_specs=[in_smem(), in_smem()] + in_vmem(5),
+        in_specs=[in_smem(), in_smem()] + in_vmem(4),
         out_specs=in_vmem(1)[0],
         compiler_params=params(),
         cost_estimate=cost(8 * rows * rows * width, 6 * rows * width),
         name="attention",
-    )(first, sink_logits, queries, earlier_keys, key_rows, earlier_values, value_rows)
-
-
-def project(attended, out_weight, near_weights, t, member, s, t_count):
+    )(first, sink_logits, queries, earlier, key_rows, value_rows)
+
+
+def project(attended, weights, t, s, t_count):
     slots = len(attended)
     width, rows = attended[0].shape
-    columns = out_weight.shape[0]
-    shares = len(near_weights)
-    pair = 2
+    columns = weights[0].shape[0]
+    shares = len(weights)
     depth = width // shares
 
     def kernel(place_ref, *refs):
         attended_refs = refs[:slots]
-        weight_ref = refs[slots]
-        near_refs = refs[slots + 1 : slots + 1 + shares]
-        kept_ref, sent_ref, total = refs[slots + 1 + shares :]
-        t, member, s = place_ref[0], place_ref[1], place_ref[2]
-        for i in range(pair):
-            if i == 0:
-                result = dot(weight_ref[...], jnp.concatenate([ref[...] for ref in attended_refs], axis=1))
+        weight_refs = refs[slots : slots + shares]
+        kept_ref, sent_ref, total = refs[slots + shares :]
+        t, s = place_ref[0], place_ref[1]
+        result = 0.0
+        for u in range(shares):
+            span = pl.ds(pl.multiple_of((s ^ u) * depth, 128), depth)
+            block = jnp.concatenate([ref[span, :] for ref in attended_refs], axis=1)
+            result = result + dot(weight_refs[u][...], block)
+        total[...] = result
+        for m in range(t_count):
+            block = total[:, pl.ds(pl.multiple_of((t ^ m) * rows, 128), rows)]
+            if m == 0:
+                kept_ref[...] = block
             else:
-                result = 0.0
-                for u in range(shares):
-                    span = pl.ds(pl.multiple_of((s ^ u) * depth, 128), depth)
-                    block = jnp.concatenate([ref[span, :] for ref in attended_refs], axis=1)
-                    result = result + dot(near_refs[u][...], block)
-            total[...] = result
-            for m in range(t_count):
-                block = total[:, pl.ds(pl.multiple_of((t ^ m) * rows, 128), rows)]
-                if m == 0:
-                    kept_ref[member ^ i] = block
-                else:
-                    sent_ref[m - 1, member ^ i] = block.astype(jnp.bfloat16)
+                sent_ref[m - 1] = block.astype(jnp.bfloat16)
 
     return pl.pallas_call(
         kernel,
         out_shape=(
-            jax.ShapeDtypeStruct((pair, columns, rows), jnp.float32),
-            jax.ShapeDtypeStruct((t_count - 1, pair, columns, rows), jnp.bfloat16),
+            jax.ShapeDtypeStruct((columns, rows), jnp.float32),
+            jax.ShapeDtypeStruct((t_count - 1, columns, rows), jnp.bfloat16),
         ),
-        in_specs=[in_smem()] + in_vmem(slots + 1 + shares),
+        in_specs=[in_smem()] + in_vmem(slots + shares),
         out_specs=tuple(in_vmem(2)),
         scratch_shapes=[pltpu.VMEM((columns, slots * rows), jnp.float32)],
         compiler_params=params(),
-        cost_estimate=cost(4 * slots * rows * width * columns, 4 * width * columns),
+        cost_estimate=cost(2 * slots * rows * width * columns, 2 * width * columns),
         name="project",
-    )(jnp.stack([t, member, s]).astype(jnp.int32), *attended, out_weight, *near_weights)
+    )(jnp.stack([t, s]).astype(jnp.int32), *attended, *weights)
 
 
 def activate(pieces, gain_table, weights, pair, t):
@@ -273,30 +271,30 @@
     group = z_count // slots
     pair = z // group
 
-    first = (lax.axis_index(("ep", "sub")) == 0).astype(jnp.int32).reshape(1)
-    earlier_keys = shifted(key_rows, ("ep", "sub"), 1)
-    earlier_values = shifted(value_rows, ("ep", "sub"), 1)
-    attended = attention(
-        queries, earlier_keys, key_rows, earlier_values, value_rows, sink_logits, first
-    )
-
+    paired = jnp.concatenate([key_rows, value_rows], axis=1)
+    earlier = shifted(paired, ("ep", "sub"), 1)
     out_weight = out_weight.T
     depth = out_weight.shape[1] // s_count
-    near, _ = lax.optimization_barrier((out_weight, earlier_values))
-    near = swapped(lax.dynamic_slice_in_dim(near, s * depth, depth, 1), "ep", 1)
-    near, _ = lax.optimization_barrier((near, attended))
-    near_weights = [near] + [swapped(near, "sub", u) for u in range(1, s_count)]
-
-    expert_in = expert_in[0].transpose(0, 2, 1)
-    expert_out = expert_out[0].T
-    experts_in = [expert_in] + [swapped(expert_in, "sub", e) for e in range(1, s_count)]
-    experts_out = [expert_out] + [swapped(expert_out, "sub", e) for e in range(1, s_count)]
-
-    residual = residual.T.reshape(slots, group * columns, rows)
+    near = lax.dynamic_slice_in_dim(out_weight, s * depth, depth, 1)
+    residual = picked(residual.T.reshape(slots, group * columns, rows), pair ^ t, 0)
+    earlier, near, residual, expert_in, expert_out = lax.optimization_barrier(
+        (earlier, near, residual, expert_in, expert_out)
+    )
+
+    near = swapped(near, "ep", 1)
+
     route = [
         (i * t_count + k, (i ^ (group * k)) * t_count + k) for i in range(z_count) for k in range(t_count)
     ]
-    residual = lax.ppermute(picked(residual, pair ^ t, 0), ("ep", "tp"), route)
+    residual = lax.ppermute(residual, ("ep", "tp"), route)
+
+    expert_in = expert_in[0].transpose(0, 2, 1)
+    expert_out = expert_out[0]
+    experts_in = [expert_in] + [swapped(expert_in, "sub", e) for e in range(1, s_count)]
+    experts_out = [expert_out.T] + [swapped(expert_out, "sub", e).T for e in range(1, s_count)]
+
+    first = (lax.axis_index(("ep", "sub")) == 0).astype(jnp.int32).reshape(1)
+    attended = attention(queries, earlier, key_rows, value_rows, sink_logits, first)
 
     expert_count = z_count * s_count
     route_float = route_scores.T.astype(jnp.float32)
@@ -309,10 +307,18 @@
     tables = tables.reshape(slots, group, s_count, rows)
 
     gathered = [attended] + [swapped(attended, "ep", group * j) for j in range(1, slots)]
-    hidden, sent = project(gathered, out_weight, near_weights, t, z % group, s, t_count)
-    hidden = hidden.reshape(group * columns, rows) + residual.astype(jnp.float32)
+    near, *gathered = lax.optimization_barrier((near, *gathered))
+    near_weights = [near] + [swapped(near, "sub", u) for u in range(1, s_count)]
+    mine = project(gathered, [out_weight], t, s * 0, t_count)
+    other = project(gathered, near_weights, t, s, t_count)
+    first_member = z % group == 0
+
+    def ordered(a, b):
+        return jnp.concatenate([jnp.where(first_member, a, b), jnp.where(first_member, b, a)], axis=0)
+
+    hidden = ordered(mine[0], other[0]) + residual.astype(jnp.float32)
     for m in range(1, t_count):
-        received = swapped(sent[m - 1].reshape(group * columns, rows), "tp", m)
+        received = swapped(ordered(mine[1][m - 1], other[1][m - 1]), "tp", m)
         hidden = hidden + received.astype(jnp.float32)
     gain_part = picked(norm_gain.reshape(slots, group * columns), pair, 0)
     scaled = (hidden * gain_part[:, None]).astype(jnp.bfloat16)
@@ -336,6 +342,7 @@
             here = (pair == m) & ((pair ^ t) == r)
             total = total + jnp.where(here, pieces[m][group * r].astype(jnp.float32), 0.0)
     total = total * lax.dynamic_slice_in_dim(inverse_gain, t * width, width, 0)[:, None]
+    total = lax.optimization_barrier(total)
 
     for p in range(group):
         part = [[pieces[m][group * r + p] for r in range(slots)] for m in range(t_count)]

time: 225 us -> 198 us (0.88)
  starting transfers between devices: 54.3 us -> 40.2 us
  waiting for transfers between devices: 103 us -> 93.8 us
    ppermute x21, starting transfers between devices: 45.8 us -> 33.4 us  [swapped(): lax.ppermute(block, axis, [(i, i ^ distance) for i in range(lax.axis_size...]
    ppermute x2 -> x1, waiting for transfers between devices: 12 us -> 0.01 us  [shifted(): return lax.ppermute(block, axis, route)]
    unnamed x39 -> x34, local copies, waits for them, and re-layouts: 19.3 us -> 11 us
    optimization_barrier x0 -> x1, local copies, waits for them, and re-layouts: none -> 6.45 us  [local(): lax.optimization_barrier((earlier, near, residual, expert_in, expert_out))]
    ppermute x21, waiting for transfers between devices: 90.8 us -> 93.8 us  [swapped(): lax.ppermute(block, axis, [(i, i ^ distance) for i in range(lax.axis_size...]
  transfers between devices with their start and end apart: 24 -> 23, of which waited for: 12 -> 11; matrix products, arithmetic and copies ran while one was open for 6% -> 7% of each run, Pallas kernels for 17% -> 19%
where the time goes in v5:
time: 198 us; the launch traced here: 197 us
  waiting for transfers between devices  93.8 us (47%)
  starting transfers between devices  40.2 us (20%)
  Pallas kernels  37.3 us (19%)
  local copies, waits for them, and re-layouts  21.7 us (11%)
  other arithmetic  4.22 us (2%)
    ppermute x21, waiting for transfers between devices, swapped(): lax.ppermute(block, axis, [(i, i ^ distance) for i in range(lax.axis_size...  93.8 us
    ppermute x21, starting transfers between devices, swapped(): lax.ppermute(block, axis, [(i, i ^ distance) for i in range(lax.axis_size...  33.4 us
    pallas_call x2, Pallas kernels, activate(): pl.pallas_call(kernel, out_shape=jax.ShapeDtypeStruct((experts, units, la...  17.4 us
    unnamed x34, local copies, waits for them, and re-layouts  11 us
    pallas_call x2, Pallas kernels, combine(): pl.pallas_call(kernel, out_shape=tuple((jax.ShapeDtypeStruct((width, rows...  10.4 us
    optimization_barrier x1, local copies, waits for them, and re-layouts, local(): lax.optimization_barrier((earlier, near, residual, expert_in, expert_out))  6.45 us
    pallas_call x1, Pallas kernels, attention(): pl.pallas_call(attention_kernel, out_shape=jax.ShapeDtypeStruct((width, r...  5.56 us
    ppermute x1, starting transfers between devices, local(): residual = lax.ppermute(residual, ('ep', 'tp'), route)  4.41 us
  transfers between devices with their start and end apart: 23, of which 11 were waited for; matrix products, arithmetic and copies ran while one was open for 7% of the time, Pallas kernels for 19%

profile of v5, /device:TPU:0, one launch (start us, length us, event | category | flops | bytes accessed | tf_op | source)
XLA Modules:
  0.0 197.4 jit_solution(13135489551367634262)
XLA Ops:
  0.0 1.0 pad_maximum_fusion.1
  1.0 2.4 %collective-permute-start = (bf16[128,512]{1,0:T(8,128)(2,1)S(1)}, bf16[128,512]{1,0:T(8,128)(2,1)S(1)}, u32[]{:S(2)}, u32[]{:S(2)}) collective-permute-start(bf16[128,512]{1,0:T(8,128)(2,1)S(1)} %pad_maximum_fusion.1), channel_id=1, source_target_pairs={{0,1},{1,4},{4,5},{5,8},{8,9},{9,12},{12,13},{2,3},{3,6},{6,7},{7,... | collective-permute-start | bytes 393224 | tf_op jit(solution)/shard_map/ppermute | solution.py:18
  3.4 0.8 dynamic-slice_bitcast_fusion.1
  4.2 2.6 %dynamic-slice_bitcast_fusion = bf16[720,1024]{1,0:T(8,128)(2,1)} fusion(bf16[2048,720]{0,1:T(8,128)(2,1)} %param.15, s32[]{:T(128)S(6)} %select_n.110), kind=kLoop, calls=%fused_computation.1 | loop fusion | bytes 2949124 | tf_op jit(solution)/shard_map/dynamic_slice | solution.py:278
  6.8 2.7 %collective-permute-start.9 = (bf16[2,720,2880]{2,1,0:T(8,128)(2,1)}, bf16[2,720,2880]{2,1,0:T(8,128)(2,1)}, u32[]{:S(2)}, u32[]{:S(2)}) collective-permute-start(bf16[2,720,2880]{2,1,0:T(8,128)(2,1)} %bitcast.56), channel_id=1, source_target_pairs={{0,1},{1,0},{2,3},{3,2},{4,5},{5,4},{6,7},{7,6},{8,9},{9,8},{10,11... | collective-permute-start | bytes 24883208 | tf_op jit(solution)/shard_map/ppermute | solution.py:22
  9.5 1.6 collective-permute-start.1
  11.1 5.6 %attention.1.refs_0_ = bf16[2048,128]{1,0:T(8,128)(2,1)S(1)} custom-call(s32[1]{0:T(128)} %bitcast.5.first_ref, f32[32]{0:T(128)S(1)} %copy-done.13, bf16[128,2048]{1,0:T(8,128)(2,1)S(1)} %copy-done.6, bf16[128,512]{1,0:T(8,128)(2,1)S(1)} %collective-permute-done.earlier_ref, bf16[128,256]{1,0:T(8,128)(2,1)S(1)} %copy-done.12, bf16[128,256]{1,0:T(8,128)(2,1)S(1)} %copy-done.11), custom_call_target="tpu_custom_call" | custom-call | flops 268435456 | bytes 1572864 | tf_op jit(solution)/shard_map/attention/pallas_call | solution.py:109
  16.6 1.9 collective-permute-start.2
  18.6 35.6 %collective-permute-done.2.refs_1_ = bf16[2048,128]{1,0:T(8,128)(2,1)S(1)} collective-permute-done((bf16[2048,128]{1,0:T(8,128)(2,1)S(1)}, bf16[2048,128]{1,0:T(8,128)(2,1)S(1)}, u32[]{:S(2)}, u32[]{:S(2)}) %collective-permute-start.2) | collective-permute-done | bytes 524320 | tf_op jit(solution)/shard_map/ppermute | solution.py:22
  54.2 0.9 collective-permute-done.1.refs_2_
  55.4 4.4 %collective-permute-start.4 = (bf16[1440,128]{1,0:T(8,128)(2,1)}, bf16[1440,128]{1,0:T(8,128)(2,1)}, u32[]{:S(2)}, u32[]{:S(2)}) collective-permute-start(bf16[1440,128]{1,0:T(8,128)(2,1)} %dynamic-slice_bitcast_fusion.1), channel_id=1, source_target_pairs={{0,0},{2,10},{4,4},{6,14},{8,8},{10,2},{12,12},{14,6},{1,1},{3,11}... | collective-permute-start | bytes 1105928 | tf_op jit(solution)/shard_map/ppermute | solution.py:289
  59.8 6.4 %copy.19 = bf16[1,1440,1440]{1,2,0:T(8,128)(2,1)} copy(bf16[1,1440,1440]{2,1,0:T(8,128)(2,1)} %param.19) | data formatting | bytes 8294400 | tf_op jit(solution)/shard_map/optimization_barrier | solution.py:280
  66.8 1.8 copy-done.3
  68.6 1.5 project.2
  70.1 2.4 %project.3 = (f32[720,128]{1,0:T(8,128)S(1)}, bf16[1,720,128]{2,1,0:T(8,128)(2,1)S(1)}) custom-call(s32[2]{0:T(128)S(1)} %pad_add_fusion.1.place_ref, bf16[2048,128]{1,0:T(8,128)(2,1)S(1)} %attention.1.refs_0_, bf16[2048,128]{1,0:T(8,128)(2,1)S(1)} %collective-permute-done.2.refs_1_, bf16[720,1024]{1,0:T(8,128)(2,1)S(1)} %collective-permute-done.1.refs_2_, ...), custom_call_target="tpu_custom_call" | custom-call | flops 754974720 | bytes 2949120 | tf_op jit(solution)/shard_map/project/pallas_call | solution.py:145
  72.6 1.3 collective-permute-start.5
  73.9 9.2 %collective-permute-done.5 = bf16[1440,128]{1,0:T(8,128)(2,1)S(1)} collective-permute-done((bf16[1440,128]{1,0:T(8,128)(2,1)S(1)}, bf16[1440,128]{1,0:T(8,128)(2,1)S(1)}, u32[]{:S(2)}, u32[]{:S(2)}) %collective-permute-start.5) | collective-permute-done | bytes 368672 | tf_op jit(solution)/shard_map/ppermute | solution.py:22
  83.2 1.3 fusion.2.refs_0_
  84.4 2.5 %collective-permute-start.6 = (bf16[1440,128]{1,0:T(8,128)(2,1)S(1)}, bf16[1440,128]{1,0:T(8,128)(2,1)S(1)}, u32[]{:S(2)}, u32[]{:S(2)}) collective-permute-start(bf16[1440,128]{1,0:T(8,128)(2,1)S(1)} %fusion.2.refs_0_), channel_id=1, source_target_pairs={{0,8},{4,12},{8,0},{12,4},{1,9},{5,13},{9,1},{13,5},{2,10},{6,14},... | collective-permute-start | bytes 1105928 | tf_op jit(solution)/shard_map/ppermute | solution.py:22
  87.0 2.5 %collective-permute-start.13 = (f32[8,128]{1,0:T(8,128)S(1)}, f32[8,128]{1,0:T(8,128)S(1)}, u32[]{:S(2)}, u32[]{:S(2)}) collective-permute-start(f32[8,128]{1,0:T(8,128)S(1)} %select_reduce_fusion), channel_id=1, source_target_pairs={{0,12},{4,8},{8,4},{12,0},{1,13},{5,9},{9,5},{13,1},{2,14},{6,10},... | collective-permute-start | bytes 12296 | tf_op jit(solution)/shard_map/ppermute | solution.py:22
  89.7 13.5 %collective-permute-done.6.refs_1_ = bf16[1440,128]{1,0:T(8,128)(2,1)S(1)} collective-permute-done((bf16[1440,128]{1,0:T(8,128)(2,1)S(1)}, bf16[1440,128]{1,0:T(8,128)(2,1)S(1)}, u32[]{:S(2)}, u32[]{:S(2)}) %collective-permute-start.6) | collective-permute-done | bytes 368672 | tf_op jit(solution)/shard_map/ppermute | solution.py:22
  103.8 0.9 collective-permute-done.16.refs_0_
  104.7 1.8 collective-permute-start.18
  106.4 6.1 %collective-permute-done.17.refs_1_ = bf16[1440,128]{1,0:T(8,128)(2,1)S(1)} collective-permute-done((bf16[1440,128]{1,0:T(8,128)(2,1)S(1)}, bf16[1440,128]{1,0:T(8,128)(2,1)S(1)}, u32[]{:S(2)}, u32[]{:S(2)}) %collective-permute-start.17) | collective-permute-done | bytes 368672 | tf_op jit(solution)/shard_map/ppermute | solution.py:22
  112.5 1.9 collective-permute-start.19
  114.7 0.7 copy-done.7
  115.5 2.7 %collective-permute-start.12 = (f32[8,128]{1,0:T(8,128)S(1)}, f32[8,128]{1,0:T(8,128)S(1)}, u32[]{:S(2)}, u32[]{:S(2)}) collective-permute-start(f32[8,128]{1,0:T(8,128)S(1)} %select_reduce_fusion), channel_id=1, source_target_pairs={{0,8},{4,12},{8,0},{12,4},{1,9},{5,13},{9,1},{13,5},{2,10},{6,14},... | collective-permute-start | bytes 12296 | tf_op jit(solution)/shard_map/ppermute | solution.py:22
  118.1 3.8 %collective-permute-done.19.refs_3_ = bf16[1440,128]{1,0:T(8,128)(2,1)S(1)} collective-permute-done((bf16[1440,128]{1,0:T(8,128)(2,1)S(1)}, bf16[1440,128]{1,0:T(8,128)(2,1)S(1)}, u32[]{:S(2)}, u32[]{:S(2)}) %collective-permute-start.19) | collective-permute-done | bytes 368672 | tf_op jit(solution)/shard_map/ppermute | solution.py:22
  121.9 0.8 copy-done.9
  122.7 1.0 collective-permute-start.7
  123.7 1.0 collective-permute-start.8
  124.7 3.4 %copy-done.2 = bf16[1,2,2880,720]{2,3,1,0:T(8,128)(2,1)S(1)} copy-done((bf16[1,2,2880,720]{2,3,1,0:T(8,128)(2,1)S(1)}, bf16[1,2,2880,720]{2,3,1,0:T(8,128)(2,1)}, u32[]{:S(2)}) %copy-start.2) | copy-done | bytes 8294424
  128.1 1.0 copy-done.8
  129.1 1.0 copy-done.10
  130.1 8.7 %activate.3.refs_0_ = bf16[2,720,256]{2,1,0:T(8,128)(2,1)S(1)} custom-call(s32[2]{0:T(128)S(1)} %pad_add_fusion.2.place_ref, bf16[1440,128]{1,0:T(8,128)(2,1)S(1)} %collective-permute-done.16.refs_0_, bf16[1440,128]{1,0:T(8,128)(2,1)S(1)} %collective-permute-done.17.refs_1_, bf16[1440,128]{1,0:T(8,128)(2,1)S(1)} %copy-done.8, ...), custom_call_target="tpu_custom_call" | custom-call | flops 4246732800 | bytes 16588800 | tf_op jit(solution)/shard_map/activate/pallas_call | solution.py:193
  138.8 1.9 collective-permute-start.11
  141.2 8.7 %activate.2.refs_0_ = bf16[2,720,256]{2,1,0:T(8,128)(2,1)S(1)} custom-call(s32[2]{0:T(128)S(1)} %pad_add_fusion.2.place_ref, bf16[1440,128]{1,0:T(8,128)(2,1)S(1)} %fusion.2.refs_0_, bf16[1440,128]{1,0:T(8,128)(2,1)S(1)} %collective-permute-done.6.refs_1_, bf16[1440,128]{1,0:T(8,128)(2,1)S(1)} %collective-permute-done.7.refs_2_, ...), custom_call_target="tpu_custom_call" | custom-call | flops 4246732800 | bytes 16588800 | tf_op jit(solution)/shard_map/activate/pallas_call | solution.py:193
  149.9 1.6 collective-permute-start.10
  151.6 0.6 gather_fusion
  152.2 8.0 %collective-permute-done.20.refs_1_ = bf16[2,720,256]{2,1,0:T(8,128)(2,1)} collective-permute-done((bf16[2,720,256]{2,1,0:T(8,128)(2,1)S(1)}, bf16[2,720,256]{2,1,0:T(8,128)(2,1)}, u32[]{:S(2)}, u32[]{:S(2)}) %collective-permute-start.20) | collective-permute-done | bytes 737312 | tf_op jit(solution)/shard_map/ppermute | solution.py:22
  160.2 2.3 %copy-done.1 = bf16[1,1440,1440]{1,2,0:T(8,128)(2,1)S(1)} copy-done((bf16[1,1440,1440]{1,2,0:T(8,128)(2,1)S(1)}, bf16[1,1440,1440]{1,2,0:T(8,128)(2,1)}, u32[]{:S(2)}) %copy-start.1) | copy-done | bytes 4147224
  162.5 5.3 %combine.3 = (bf16[1440,128]{1,0:T(8,128)(2,1)S(1)}, bf16[1440,128]{1,0:T(8,128)(2,1)S(1)}) custom-call(s32[1]{0:T(128)} %bitcast.t_ref, bf16[2,720,256]{2,1,0:T(8,128)(2,1)S(1)} %activate.3.refs_0_, bf16[2,720,256]{2,1,0:T(8,128)(2,1)} %collective-permute-done.20.refs_1_, f32[2,256]{1,0:T(2,128)S(1)} %get-tuple-element.45.refs_2_, ...), custom_call_target="tpu_custom_call" | custom-call | flops 2123366400 | bytes 8294400 | tf_op jit(solution)/shard_map/combine/pallas_call | solution.py:235
  167.8 3.5 %collective-permute-start.22 = (bf16[1440,128]{1,0:T(8,128)(2,1)S(1)}, bf16[1440,128]{1,0:T(8,128)(2,1)S(1)}, u32[]{:S(2)}, u32[]{:S(2)}) collective-permute-start(bf16[1440,128]{1,0:T(8,128)(2,1)S(1)} %get-tuple-element.36), channel_id=1, source_target_pairs={{0,12},{4,8},{8,4},{12,0},{1,13},{5,9},{9,5},{13,1},{2,14},{6,10},... | collective-permute-start | bytes 1105928 | tf_op jit(solution)/shard_map/ppermute | solution.py:22
  172.3 5.1 %combine.2 = (bf16[1440,128]{1,0:T(8,128)(2,1)S(1)}, bf16[1440,128]{1,0:T(8,128)(2,1)S(1)}) custom-call(s32[1]{0:T(128)} %bitcast.t_ref, bf16[2,720,256]{2,1,0:T(8,128)(2,1)S(1)} %activate.2.refs_0_, bf16[2,720,256]{2,1,0:T(8,128)(2,1)} %collective-permute-done.10.refs_1_, f32[2,256]{1,0:T(2,128)S(1)} %get-tuple-element.44.refs_2_, ...), custom_call_target="tpu_custom_call" | custom-call | flops 2123366400 | bytes 8294400 | tf_op jit(solution)/shard_map/combine/pallas_call | solution.py:235
  177.4 3.5 %collective-permute-start.15 = (bf16[1440,128]{1,0:T(8,128)(2,1)S(1)}, bf16[1440,128]{1,0:T(8,128)(2,1)S(1)}, u32[]{:S(2)}, u32[]{:S(2)}) collective-permute-start(bf16[1440,128]{1,0:T(8,128)(2,1)S(1)} %get-tuple-element.34), channel_id=1, source_target_pairs={{0,8},{4,12},{8,0},{12,4},{1,9},{5,13},{9,1},{13,5},{2,10},{6,14},... | collective-permute-start | bytes 1105928 | tf_op jit(solution)/shard_map/ppermute | solution.py:22
  181.2 2.5 %collective-permute-done.21 = bf16[1440,128]{1,0:T(8,128)(2,1)S(1)} collective-permute-done((bf16[1440,128]{1,0:T(8,128)(2,1)S(1)}, bf16[1440,128]{1,0:T(8,128)(2,1)S(1)}, u32[]{:S(2)}, u32[]{:S(2)}) %collective-permute-start.21) | collective-permute-done | bytes 368672 | tf_op jit(solution)/shard_map/ppermute | solution.py:22
  183.7 12.7 %collective-permute-done.15 = bf16[1440,128]{1,0:T(8,128)(2,1)S(1)} collective-permute-done((bf16[1440,128]{1,0:T(8,128)(2,1)S(1)}, bf16[1440,128]{1,0:T(8,128)(2,1)S(1)}, u32[]{:S(2)}, u32[]{:S(2)}) %collective-permute-start.15) | collective-permute-done | bytes 368672 | tf_op jit(solution)/shard_map/ppermute | solution.py:22
  196.5 1.0 fusion.3
  (72 shorter events, 4.0 us)
Async XLA Ops:
  0.0 3.4 %copy-start = (bf16[128,2880]{0,1:T(8,128)(2,1)S(1)}, bf16[128,2880]{0,1:T(8,128)(2,1)}, u32[]{:S(2)}) copy-start(bf16[128,2880]{0,1:T(8,128)(2,1)} %param.16) | copy-start | bytes 2211844
  0.0 11.1 %copy-start.11 = (bf16[128,256]{1,0:T(8,128)(2,1)S(1)}, bf16[128,256]{1,0:T(8,128)(2,1)}, u32[]{:S(2)}) copy-start(bf16[128,256]{1,0:T(8,128)(2,1)} %v_ref.1) | copy-start | bytes 196612
  0.0 11.1 %copy-start.12 = (bf16[128,256]{1,0:T(8,128)(2,1)S(1)}, bf16[128,256]{1,0:T(8,128)(2,1)}, u32[]{:S(2)}) copy-start(bf16[128,256]{1,0:T(8,128)(2,1)} %k_ref.1) | copy-start | bytes 196612
  0.0 11.1 %copy-start.13 = (f32[32]{0:T(128)S(1)}, f32[32]{0:T(128)}, u32[]{:S(2)}) copy-start(f32[32]{0:T(128)} %sink_ref.1) | copy-start | bytes 388
  0.0 11.1 %copy-start.6 = (bf16[128,2048]{1,0:T(8,128)(2,1)S(1)}, bf16[128,2048]{1,0:T(8,128)(2,1)}, u32[]{:S(2)}) copy-start(bf16[128,2048]{1,0:T(8,128)(2,1)} %q_ref.1) | copy-start | bytes 1572868
  0.0 55.1 %copy-start.14 = (f32[2880]{0:T(1024)S(1)}, f32[2880]{0:T(1024)}, u32[]{:S(2)}) copy-start(f32[2880]{0:T(1024)} %param.17) | copy-start | bytes 34564
  1.0 5.8 %collective-permute-start = (bf16[128,512]{1,0:T(8,128)(2,1)S(1)}, bf16[128,512]{1,0:T(8,128)(2,1)S(1)}, u32[]{:S(2)}, u32[]{:S(2)}) collective-permute-start(bf16[128,512]{1,0:T(8,128)(2,1)S(1)} %pad_maximum_fusion.1), channel_id=1, source_target_pairs={{0,1},{1,4},{4,5},{5,8},{8,9},{9,12},{12,13},{2,3},{3,6},{6,7},{7,... | collective-permute-start | bytes 393224 | tf_op jit(solution)/shard_map/ppermute | solution.py:18
  6.8 116.9 %collective-permute-start.9 = (bf16[2,720,2880]{2,1,0:T(8,128)(2,1)}, bf16[2,720,2880]{2,1,0:T(8,128)(2,1)}, u32[]{:S(2)}, u32[]{:S(2)}) collective-permute-start(bf16[2,720,2880]{2,1,0:T(8,128)(2,1)} %bitcast.56), channel_id=1, source_target_pairs={{0,1},{1,0},{2,3},{3,2},{4,5},{5,4},{6,7},{7,6},{8,9},{9,8},{10,11... | collective-permute-start | bytes 24883208 | tf_op jit(solution)/shard_map/ppermute | solution.py:22
  9.5 45.6 %collective-permute-start.1 = (bf16[720,1024]{1,0:T(8,128)(2,1)}, bf16[720,1024]{1,0:T(8,128)(2,1)S(1)}, u32[]{:S(2)}, u32[]{:S(2)}) collective-permute-start(bf16[720,1024]{1,0:T(8,128)(2,1)} %dynamic-slice_bitcast_fusion), channel_id=1, source_target_pairs={{0,4},{4,0},{8,12},{12,8},{1,5},{5,1},{9,13},{13,9},{2,6},{6,2},{1... | collective-permute-start | bytes 4423688 | tf_op jit(solution)/shard_map/ppermute | solution.py:22
  16.6 37.6 %collective-permute-start.2 = (bf16[2048,128]{1,0:T(8,128)(2,1)S(1)}, bf16[2048,128]{1,0:T(8,128)(2,1)S(1)}, u32[]{:S(2)}, u32[]{:S(2)}) collective-permute-start(bf16[2048,128]{1,0:T(8,128)(2,1)S(1)} %attention.1.refs_0_), channel_id=1, source_target_pairs={{0,8},{4,12},{8,0},{12,4},{1,9},{5,13},{9,1},{13,5},{2,10},{6,14},... | collective-permute-start | bytes 1572872 | tf_op jit(solution)/shard_map/ppermute | solution.py:22
  55.1 15.0 %collective-permute-start.3 = (bf16[720,1024]{1,0:T(8,128)(2,1)S(1)}, bf16[720,1024]{1,0:T(8,128)(2,1)}, u32[]{:S(2)}, u32[]{:S(2)}) collective-permute-start(bf16[720,1024]{1,0:T(8,128)(2,1)S(1)} %collective-permute-done.1.refs_2_), channel_id=1, source_target_pairs={{0,1},{1,0},{2,3},{3,2},{4,5},{5,4},{6,7},{7,6},{8,9},{9,8},{10,11... | collective-permute-start | bytes 4423688 | tf_op jit(solution)/shard_map/ppermute | solution.py:22
  55.4 18.5 %collective-permute-start.4 = (bf16[1440,128]{1,0:T(8,128)(2,1)}, bf16[1440,128]{1,0:T(8,128)(2,1)}, u32[]{:S(2)}, u32[]{:S(2)}) collective-permute-start(bf16[1440,128]{1,0:T(8,128)(2,1)} %dynamic-slice_bitcast_fusion.1), channel_id=1, source_target_pairs={{0,0},{2,10},{4,4},{6,14},{8,8},{10,2},{12,12},{14,6},{1,1},{3,11}... | collective-permute-start | bytes 1105928 | tf_op jit(solution)/shard_map/ppermute | solution.py:289
  66.2 86.0 %collective-permute-start.14 = (bf16[1440,1440]{0,1:T(8,128)(2,1)}, bf16[1440,1440]{0,1:T(8,128)(2,1)}, u32[]{:S(2)}, u32[]{:S(2)}) collective-permute-start(bf16[1440,1440]{0,1:T(8,128)(2,1)} %bitcast.53), channel_id=1, source_target_pairs={{0,1},{1,0},{2,3},{3,2},{4,5},{5,4},{6,7},{7,6},{8,9},{9,8},{10,11... | collective-permute-start | bytes 12441608 | tf_op jit(solution)/shard_map/ppermute | solution.py:22
  66.8 1.8 copy-start.3
  70.1 3.8 %copy-start.15 = (s32[128,4]{0,1:T(4,128)S(1)}, s32[128,4]{0,1:T(4,128)}, u32[]{:S(2)}) copy-start(s32[128,4]{0,1:T(4,128)} %param.21) | copy-start | bytes 6148
  72.5 14.5 %copy-start.16 = (s32[128,4]{0,1:T(4,128)S(1)}, s32[128,4]{0,1:T(4,128)}, u32[]{:S(2)}) copy-start(s32[128,4]{0,1:T(4,128)} %param.20) | copy-start | bytes 6148
  72.6 10.6 %collective-permute-start.5 = (bf16[1440,128]{1,0:T(8,128)(2,1)S(1)}, bf16[1440,128]{1,0:T(8,128)(2,1)S(1)}, u32[]{:S(2)}, u32[]{:S(2)}) collective-permute-start(bf16[1440,128]{1,0:T(8,128)(2,1)S(1)} %pad_maximum_fusion), channel_id=1, source_target_pairs={{0,2},{2,0},{1,3},{3,1},{4,6},{6,4},{5,7},{7,5},{8,10},{10,8},{9,1... | collective-permute-start | bytes 1105928 | tf_op jit(solution)/shard_map/ppermute | solution.py:22
  84.4 18.7 %collective-permute-start.6 = (bf16[1440,128]{1,0:T(8,128)(2,1)S(1)}, bf16[1440,128]{1,0:T(8,128)(2,1)S(1)}, u32[]{:S(2)}, u32[]{:S(2)}) collective-permute-start(bf16[1440,128]{1,0:T(8,128)(2,1)S(1)} %fusion.2.refs_0_), channel_id=1, source_target_pairs={{0,8},{4,12},{8,0},{12,4},{1,9},{5,13},{9,1},{13,5},{2,10},{6,14},... | collective-permute-start | bytes 1105928 | tf_op jit(solution)/shard_map/ppermute | solution.py:22
  87.0 63.0 %collective-permute-start.13 = (f32[8,128]{1,0:T(8,128)S(1)}, f32[8,128]{1,0:T(8,128)S(1)}, u32[]{:S(2)}, u32[]{:S(2)}) collective-permute-start(f32[8,128]{1,0:T(8,128)S(1)} %select_reduce_fusion), channel_id=1, source_target_pairs={{0,12},{4,8},{8,4},{12,0},{1,13},{5,9},{9,5},{13,1},{2,14},{6,10},... | collective-permute-start | bytes 12296 | tf_op jit(solution)/shard_map/ppermute | solution.py:22
  89.7 15.0 %collective-permute-start.16 = (bf16[1440,128]{1,0:T(8,128)(2,1)S(1)}, bf16[1440,128]{1,0:T(8,128)(2,1)S(1)}, u32[]{:S(2)}, u32[]{:S(2)}) collective-permute-start(bf16[1440,128]{1,0:T(8,128)(2,1)S(1)} %fusion.2.refs_0_), channel_id=1, source_target_pairs={{0,4},{4,0},{8,12},{12,8},{1,5},{5,1},{9,13},{13,9},{2,6},{6,2},{1... | collective-permute-start | bytes 1105928 | tf_op jit(solution)/shard_map/ppermute | solution.py:22
  103.2 9.3 %collective-permute-start.17 = (bf16[1440,128]{1,0:T(8,128)(2,1)S(1)}, bf16[1440,128]{1,0:T(8,128)(2,1)S(1)}, u32[]{:S(2)}, u32[]{:S(2)}) collective-permute-start(bf16[1440,128]{1,0:T(8,128)(2,1)S(1)} %collective-permute-done.6.refs_1_), channel_id=1, source_target_pairs={{0,4},{4,0},{8,12},{12,8},{1,5},{5,1},{9,13},{13,9},{2,6},{6,2},{1... | collective-permute-start | bytes 1105928 | tf_op jit(solution)/shard_map/ppermute | solution.py:22
  104.7 10.1 %collective-permute-start.18 = (bf16[1440,128]{1,0:T(8,128)(2,1)S(1)}, bf16[1440,128]{1,0:T(8,128)(2,1)S(1)}, u32[]{:S(2)}, u32[]{:S(2)}) collective-permute-start(bf16[1440,128]{1,0:T(8,128)(2,1)S(1)} %collective-permute-done.16.refs_0_), channel_id=1, source_target_pairs={{0,2},{2,0},{1,3},{3,1},{4,6},{6,4},{5,7},{7,5},{8,10},{10,8},{9,1... | collective-permute-start | bytes 1105928 | tf_op jit(solution)/shard_map/ppermute | solution.py:22
  112.5 9.4 %collective-permute-start.19 = (bf16[1440,128]{1,0:T(8,128)(2,1)S(1)}, bf16[1440,128]{1,0:T(8,128)(2,1)S(1)}, u32[]{:S(2)}, u32[]{:S(2)}) collective-permute-start(bf16[1440,128]{1,0:T(8,128)(2,1)S(1)} %collective-permute-done.17.refs_1_), channel_id=1, source_target_pairs={{0,2},{2,0},{1,3},{3,1},{4,6},{6,4},{5,7},{7,5},{8,10},{10,8},{9,1... | collective-permute-start | bytes 1105928 | tf_op jit(solution)/shard_map/ppermute | solution.py:22
  114.7 0.7 copy-start.7
  115.5 36.1 %collective-permute-start.12 = (f32[8,128]{1,0:T(8,128)S(1)}, f32[8,128]{1,0:T(8,128)S(1)}, u32[]{:S(2)}, u32[]{:S(2)}) collective-permute-start(f32[8,128]{1,0:T(8,128)S(1)} %select_reduce_fusion), channel_id=1, source_target_pairs={{0,8},{4,12},{8,0},{12,4},{1,9},{5,13},{9,1},{13,5},{2,10},{6,14},... | collective-permute-start | bytes 12296 | tf_op jit(solution)/shard_map/ppermute | solution.py:22
  121.9 0.8 copy-start.9
  122.7 16.1 %collective-permute-start.7 = (bf16[1440,128]{1,0:T(8,128)(2,1)S(1)}, bf16[1440,128]{1,0:T(8,128)(2,1)S(1)}, u32[]{:S(2)}, u32[]{:S(2)}) collective-permute-start(bf16[1440,128]{1,0:T(8,128)(2,1)S(1)} %fusion.2.refs_0_), channel_id=1, source_target_pairs={{0,2},{2,0},{1,3},{3,1},{4,6},{6,4},{5,7},{7,5},{8,10},{10,8},{9,1... | collective-permute-start | bytes 1105928 | tf_op jit(solution)/shard_map/ppermute | solution.py:22
  123.7 17.0 %collective-permute-start.8 = (bf16[1440,128]{1,0:T(8,128)(2,1)S(1)}, bf16[1440,128]{1,0:T(8,128)(2,1)S(1)}, u32[]{:S(2)}, u32[]{:S(2)}) collective-permute-start(bf16[1440,128]{1,0:T(8,128)(2,1)S(1)} %collective-permute-done.6.refs_1_), channel_id=1, source_target_pairs={{0,2},{2,0},{1,3},{3,1},{4,6},{6,4},{5,7},{7,5},{8,10},{10,8},{9,1... | collective-permute-start | bytes 1105928 | tf_op jit(solution)/shard_map/ppermute | solution.py:22
  124.7 3.4 %copy-start.2 = (bf16[1,2,2880,720]{2,3,1,0:T(8,128)(2,1)S(1)}, bf16[1,2,2880,720]{2,3,1,0:T(8,128)(2,1)}, u32[]{:S(2)}) copy-start(bf16[1,2,2880,720]{2,3,1,0:T(8,128)(2,1)} %param.18) | copy-start | bytes 24883204
  128.1 1.0 copy-start.8
  129.1 1.0 copy-start.10
  138.8 12.7 %collective-permute-start.11 = (f32[8,128]{1,0:T(8,128)S(1)}, f32[8,128]{1,0:T(8,128)S(1)}, u32[]{:S(2)}, u32[]{:S(2)}) collective-permute-start(f32[8,128]{1,0:T(8,128)S(1)} %select_reduce_fusion), channel_id=1, source_target_pairs={{0,4},{4,0},{8,12},{12,8},{1,5},{5,1},{9,13},{13,9},{2,6},{6,2},{1... | collective-permute-start | bytes 12296 | tf_op jit(solution)/shard_map/ppermute | solution.py:22
  140.7 9.2 %copy-start.4 = (bf16[1440,128]{1,0:T(8,128)(2,1)}, bf16[1440,128]{1,0:T(8,128)(2,1)S(1)}, u32[]{:S(2)}) copy-start(bf16[1440,128]{1,0:T(8,128)(2,1)S(1)} %collective-permute-done.8.refs_3_) | copy-start | bytes 1105924
  140.7 19.5 %collective-permute-start.20 = (bf16[2,720,256]{2,1,0:T(8,128)(2,1)S(1)}, bf16[2,720,256]{2,1,0:T(8,128)(2,1)}, u32[]{:S(2)}, u32[]{:S(2)}) collective-permute-start(bf16[2,720,256]{2,1,0:T(8,128)(2,1)S(1)} %activate.3.refs_0_), channel_id=1, source_target_pairs={{0,2},{2,0},{1,3},{3,1},{4,6},{6,4},{5,7},{7,5},{8,10},{10,8},{9,1... | collective-permute-start | bytes 2211848 | tf_op jit(solution)/shard_map/ppermute | solution.py:22
  149.9 22.4 %collective-permute-start.10 = (bf16[2,720,256]{2,1,0:T(8,128)(2,1)S(1)}, bf16[2,720,256]{2,1,0:T(8,128)(2,1)}, u32[]{:S(2)}, u32[]{:S(2)}) collective-permute-start(bf16[2,720,256]{2,1,0:T(8,128)(2,1)S(1)} %activate.2.refs_0_), channel_id=1, source_target_pairs={{0,2},{2,0},{1,3},{3,1},{4,6},{6,4},{5,7},{7,5},{8,10},{10,8},{9,1... | collective-permute-start | bytes 2211848 | tf_op jit(solution)/shard_map/ppermute | solution.py:22
  160.2 2.3 %copy-start.1 = (bf16[1,1440,1440]{1,2,0:T(8,128)(2,1)S(1)}, bf16[1,1440,1440]{1,2,0:T(8,128)(2,1)}, u32[]{:S(2)}) copy-start(bf16[1,1440,1440]{1,2,0:T(8,128)(2,1)} %copy.19) | copy-start | bytes 12441604
  167.8 13.4 %collective-permute-start.22 = (bf16[1440,128]{1,0:T(8,128)(2,1)S(1)}, bf16[1440,128]{1,0:T(8,128)(2,1)S(1)}, u32[]{:S(2)}, u32[]{:S(2)}) collective-permute-start(bf16[1440,128]{1,0:T(8,128)(2,1)S(1)} %get-tuple-element.36), channel_id=1, source_target_pairs={{0,12},{4,8},{8,4},{12,0},{1,13},{5,9},{9,5},{13,1},{2,14},{6,10},... | collective-permute-start | bytes 1105928 | tf_op jit(solution)/shard_map/ppermute | solution.py:22
  171.3 12.5 %collective-permute-start.21 = (bf16[1440,128]{1,0:T(8,128)(2,1)S(1)}, bf16[1440,128]{1,0:T(8,128)(2,1)S(1)}, u32[]{:S(2)}, u32[]{:S(2)}) collective-permute-start(bf16[1440,128]{1,0:T(8,128)(2,1)S(1)} %get-tuple-element.35), channel_id=1, source_target_pairs={{0,4},{4,0},{8,12},{12,8},{1,5},{5,1},{9,13},{13,9},{2,6},{6,2},{1... | collective-permute-start | bytes 1105928 | tf_op jit(solution)/shard_map/ppermute | solution.py:22
  172.3 8.6 %copy-start.5 = (bf16[1440,128]{1,0:T(8,128)(2,1)S(1)}, bf16[1440,128]{1,0:T(8,128)(2,1)}, u32[]{:S(2)}) copy-start(bf16[1440,128]{1,0:T(8,128)(2,1)} %copy-done.4) | copy-start | bytes 1105924
  177.4 19.0 %collective-permute-start.15 = (bf16[1440,128]{1,0:T(8,128)(2,1)S(1)}, bf16[1440,128]{1,0:T(8,128)(2,1)S(1)}, u32[]{:S(2)}, u32[]{:S(2)}) collective-permute-start(bf16[1440,128]{1,0:T(8,128)(2,1)S(1)} %get-tuple-element.34), channel_id=1, source_target_pairs={{0,8},{4,12},{8,0},{12,4},{1,9},{5,13},{9,1},{13,5},{2,10},{6,14},... | collective-permute-start | bytes 1105928 | tf_op jit(solution)/shard_map/ppermute | solution.py:22

commit v6 on v5

--- a/solution.py
+++ b/solution.py
@@ -10,6 +10,7 @@
 WIN = 128
 TOP = 4
 VMEM_BYTES = 16 * 1024 * 1024
+FETCH_BYTES = 32 * 1024 * 1024
 
 
 def shifted(block, axis, distance):
@@ -46,8 +47,14 @@
     return size % 16 == 0
 
 
-def params():
-    return pltpu.CompilerParams(vmem_limit_bytes=VMEM_BYTES)
+def params(limit=VMEM_BYTES):
+    return pltpu.CompilerParams(vmem_limit_bytes=limit)
+
+
+def fetches(sources, held, arrived):
+    return [
+        pltpu.make_async_copy(source, held.at[index], arrived.at[index]) for index, source in enumerate(sources)
+    ]
 
 
 def attention_kernel(first_ref, sink_ref, q_ref, earlier_ref, k_ref, v_ref, out_ref):
@@ -168,7 +175,10 @@
         piece_refs = refs[: slots * slots]
         table_ref = refs[slots * slots]
         weight_refs = refs[slots * slots + 1 : slots * slots + 1 + experts]
-        out_ref, rows_ref, stage_ref = refs[slots * slots + 1 + experts :]
+        out_ref, rows_ref, stage_ref, held_ref, arrived = refs[slots * slots + 1 + experts :]
+        copies = fetches([ref.at[k] for ref in weight_refs for k in range(2)], held_ref, arrived)
+        for copy in copies:
+            copy.start()
         for m in range(slots):
             for r in range(slots):
                 lane = pl.ds(pl.multiple_of((place_ref[1] ^ r ^ m) * rows, 128), rows)
@@ -185,21 +195,25 @@
         square = jnp.sum(dot(table_ref[...], (plain * plain).astype(jnp.bfloat16)), axis=0, keepdims=True)
         scale = lax.rsqrt(square / D + 1e-05)
         for e in range(experts):
-            gate = dot(weight_refs[e][0], rows_ref[...]) * scale
-            up = dot(weight_refs[e][1], rows_ref[...]) * scale
+            copies[2 * e].wait()
+            gate = dot(held_ref[2 * e], rows_ref[...]) * scale
+            copies[2 * e + 1].wait()
+            up = dot(held_ref[2 * e + 1], rows_ref[...]) * scale
             out_ref[e] = ((up + 1.0) * gate * jax.nn.sigmoid(1.702 * gate)).astype(jnp.bfloat16)
 
     flat = [piece for part in pieces for piece in part]
     return pl.pallas_call(
         kernel,
         out_shape=jax.ShapeDtypeStruct((experts, units, lanes), jnp.bfloat16),
-        in_specs=[in_smem()] + in_vmem(len(flat) + 1 + experts),
+        in_specs=[in_smem()] + in_vmem(len(flat) + 1) + [pl.BlockSpec(memory_space=pl.ANY)] * experts,
         out_specs=in_vmem(1)[0],
         scratch_shapes=[
             pltpu.VMEM((D, lanes), jnp.bfloat16),
             pltpu.VMEM((1, 16, 128) if aligned(depth) else (slots, depth, lanes), jnp.bfloat16),
+            pltpu.VMEM((2 * experts, units, D), jnp.bfloat16),
+            pltpu.SemaphoreType.DMA((2 * experts,)),
         ],
-        compiler_params=params(),
+        compiler_params=params(FETCH_BYTES),
         cost_estimate=cost(4 * experts * lanes * D * units, 4 * experts * D * units),
         name="activate",
     )(jnp.stack([pair, t]).astype(jnp.int32), *flat, gain_table, *weights)
@@ -215,7 +229,10 @@
         activated_refs = refs[:t_count]
         share_ref = refs[t_count]
         weight_refs = refs[t_count + 1 : t_count + 1 + experts]
-        *out_refs, all_ref, stage_ref = refs[t_count + 1 + experts :]
+        *out_refs, all_ref, stage_ref, held_ref, arrived = refs[t_count + 1 + experts :]
+        copies = fetches(weight_refs, held_ref, arrived)
+        for copy in copies:
+            copy.start()
         for u in range(t_count):
             index = t_ref[0] ^ u
             if aligned(units):
@@ -227,7 +244,8 @@
                 all_ref[:, index * units : (index + 1) * units, :] = stage_ref[index]
         total = 0.0
         for e in range(experts):
-            result = dot(weight_refs[e][...], all_ref[e]).astype(jnp.bfloat16).astype(jnp.float32)
+            copies[e].wait()
+            result = dot(held_ref[e], all_ref[e]).astype(jnp.bfloat16).astype(jnp.float32)
             total = total + share_ref[e : e + 1, :] * result
         for j in range(slots):
             out_refs[j][...] = total[:, j * rows : (j + 1) * rows].astype(jnp.bfloat16)
@@ -235,13 +253,15 @@
     return pl.pallas_call(
         kernel,
         out_shape=tuple(jax.ShapeDtypeStruct((width, rows), jnp.bfloat16) for _ in range(slots)),
-        in_specs=[in_smem()] + in_vmem(t_count + 1 + experts),
+        in_specs=[in_smem()] + in_vmem(t_count + 1) + [pl.BlockSpec(memory_space=pl.ANY)] * experts,
         out_specs=tuple(in_vmem(slots)),
         scratch_shapes=[
             pltpu.VMEM((experts, t_count * units, lanes), jnp.bfloat16),
             pltpu.VMEM((1, 1, 16, 128) if aligned(units) else (t_count, experts, units, lanes), jnp.bfloat16),
+            pltpu.VMEM((experts, width, t_count * units), jnp.bfloat16),
+            pltpu.SemaphoreType.DMA((experts,)),
         ],
-        compiler_params=params(),
+        compiler_params=params(FETCH_BYTES),
         cost_estimate=cost(
             2 * experts * lanes * t_count * units * width, 2 * experts * t_count * units * width
         ),
@@ -274,14 +294,17 @@
     paired = jnp.concatenate([key_rows, value_rows], axis=1)
     earlier = shifted(paired, ("ep", "sub"), 1)
     out_weight = out_weight.T
-    depth = out_weight.shape[1] // s_count
-    near = lax.dynamic_slice_in_dim(out_weight, s * depth, depth, 1)
+    g_count = lax.axis_size("groups")
+    share = s * g_count + lax.axis_index("groups").astype(jnp.int32)
+    depth = out_weight.shape[1] // (s_count * g_count)
+    near = lax.dynamic_slice_in_dim(out_weight, share * depth, depth, 1)
     residual = picked(residual.T.reshape(slots, group * columns, rows), pair ^ t, 0)
     earlier, near, residual, expert_in, expert_out = lax.optimization_barrier(
         (earlier, near, residual, expert_in, expert_out)
     )
 
     near = swapped(near, "ep", 1)
+    near_weights = [near] + [swapped(near, "groups", g) for g in range(1, g_count)]
 
     route = [
         (i * t_count + k, (i ^ (group * k)) * t_count + k) for i in range(z_count) for k in range(t_count)
@@ -307,10 +330,12 @@
     tables = tables.reshape(slots, group, s_count, rows)
 
     gathered = [attended] + [swapped(attended, "ep", group * j) for j in range(1, slots)]
-    near, *gathered = lax.optimization_barrier((near, *gathered))
-    near_weights = [near] + [swapped(near, "sub", u) for u in range(1, s_count)]
+    near_weights = near_weights + [
+        swapped(part, "sub", u) for u in range(1, s_count) for part in near_weights
+    ]
+    gathered, residual, tables, experts_out = lax.optimization_barrier((gathered, residual, tables, experts_out))
     mine = project(gathered, [out_weight], t, s * 0, t_count)
-    other = project(gathered, near_weights, t, s, t_count)
+    other = project(gathered, near_weights, t, share, t_count)
     first_member = z % group == 0
 
     def ordered(a, b):
@@ -324,11 +349,22 @@
     scaled = (hidden * gain_part[:, None]).astype(jnp.bfloat16)
 
     own = {0: scaled}
+    pieces = [own] + [{} for m in range(1, t_count)]
     distance = z_count // 2
     while distance:
-        own.update({d + distance: swapped(own[d], "ep", distance) for d in list(own)})
+        held = list(own)
+        if distance >= group:
+            for m in range(1, t_count):
+                pieces[m].update({d: swapped(own[d], "tp", m) for d in held if d not in pieces[m]})
+        for d in held:
+            own[d + distance] = swapped(own[d], "ep", distance)
         distance //= 2
-    pieces = [own] + [{d: swapped(own[d], "tp", m) for d in own} for m in range(1, t_count)]
+    for m in range(1, t_count):
+        pieces[m].update({d: swapped(own[d], "tp", m) for d in range(0, z_count, group) if d not in pieces[m]})
+    late = {d: own[d] for d in own if d % group}
+    late, pieces[1:] = lax.optimization_barrier((late, pieces[1:]))
+    for m in range(1, t_count):
+        pieces[m].update({d: swapped(late[d], "tp", m) for d in late})
 
     inverse_gain = 1.0 / norm_gain
     inverse_square = inverse_gain * inverse_gain
@@ -344,9 +380,13 @@
     total = total * lax.dynamic_slice_in_dim(inverse_gain, t * width, width, 0)[:, None]
     total = lax.optimization_barrier(total)
 
+    after = None
     for p in range(group):
         part = [[pieces[m][group * r + p] for r in range(slots)] for m in range(t_count)]
+        if p:
+            part, after = lax.optimization_barrier((part, after))
         activated = activate(part, gain_table, experts_in, pair, t)
+        after = activated
         activated = [activated] + [swapped(activated, "tp", m) for m in range(1, t_count)]
         share = tables[:, p].transpose(1, 0, 2).reshape(s_count, slots * rows)
         for j, result in enumerate(combine(activated, share, experts_out, t, slots)):

time: 198 us -> 219 us (1.11)
  Pallas kernels: 37.3 us -> 46.8 us
  starting transfers between devices: 40.2 us -> 47.7 us
  waiting for transfers between devices: 93.8 us -> 100 us
  local copies, waits for them, and re-layouts: 21.7 us -> 17.5 us
    ppermute x21 -> x23, starting transfers between devices: 33.4 us -> 41 us  [swapped(): lax.ppermute(block, axis, [(i, i ^ distance) for i in range(lax.axis_size...]
    ppermute x21 -> x23, waiting for transfers between devices: 93.8 us -> 100 us  [swapped(): lax.ppermute(block, axis, [(i, i ^ distance) for i in range(lax.axis_size...]
    pallas_call x2, Pallas kernels: 17.4 us -> 23.5 us  [activate(): pl.pallas_call(kernel, out_shape=jax.ShapeDtypeStruct((experts, units, la...]
    pallas_call x2, Pallas kernels: 10.4 us -> 13.7 us  [combine(): pl.pallas_call(kernel, out_shape=tuple((jax.ShapeDtypeStruct((width, rows...]
    unnamed x34 -> x30, local copies, waits for them, and re-layouts: 11 us -> 8.31 us
  transfers between devices with their start and end apart: 23 -> 25, of which waited for: 11 -> 12; matrix products, arithmetic and copies ran while one was open for 7% -> 6% of each run, Pallas kernels for 19% -> 21%
where the time goes in v6:
time: 219 us; the launch traced here: 218 us
  waiting for transfers between devices  100 us (46%)
  starting transfers between devices  47.7 us (22%)
  Pallas kernels  46.8 us (21%)
  local copies, waits for them, and re-layouts  17.5 us (8%)
  other arithmetic  5.32 us (2%)
    ppermute x23, waiting for transfers between devices, swapped(): lax.ppermute(block, axis, [(i, i ^ distance) for i in range(lax.axis_size...  100 us
    ppermute x23, starting transfers between devices, swapped(): lax.ppermute(block, axis, [(i, i ^ distance) for i in range(lax.axis_size...  41 us
    pallas_call x2, Pallas kernels, activate(): pl.pallas_call(kernel, out_shape=jax.ShapeDtypeStruct((experts, units, la...  23.5 us
    pallas_call x2, Pallas kernels, combine(): pl.pallas_call(kernel, out_shape=tuple((jax.ShapeDtypeStruct((width, rows...  13.7 us
    unnamed x30, local copies, waits for them, and re-layouts  8.31 us
    optimization_barrier x1, local copies, waits for them, and re-layouts, local(): lax.optimization_barrier((earlier, near, residual, expert_in, expert_out))  6.45 us
    pallas_call x1, Pallas kernels, attention(): pl.pallas_call(attention_kernel, out_shape=jax.ShapeDtypeStruct((width, r...  5.57 us
    ppermute x1, starting transfers between devices, local(): residual = lax.ppermute(residual, ('ep', 'tp'), route)  4.41 us
  transfers between devices with their start and end apart: 25, of which 12 were waited for; matrix products, arithmetic and copies ran while one was open for 6% of the time, Pallas kernels for 21%

profile of v6, /device:TPU:0, one launch (start us, length us, event | category | flops | bytes accessed | tf_op | source)
XLA Modules:
  0.0 217.7 jit_solution(10042982614615333879)
XLA Ops:
  0.0 1.0 pad_maximum_fusion.1
  1.0 2.4 %collective-permute-start = (bf16[128,512]{1,0:T(8,128)(2,1)S(1)}, bf16[128,512]{1,0:T(8,128)(2,1)S(1)}, u32[]{:S(2)}, u32[]{:S(2)}) collective-permute-start(bf16[128,512]{1,0:T(8,128)(2,1)S(1)} %pad_maximum_fusion.1), channel_id=1, source_target_pairs={{0,1},{1,4},{4,5},{5,8},{8,9},{9,12},{12,13},{2,3},{3,6},{6,7},{7,... | collective-permute-start | bytes 393224 | tf_op jit(solution)/shard_map/ppermute | solution.py:19
  3.4 0.8 dynamic-slice_bitcast_fusion.1
  4.1 1.2 dynamic-slice_bitcast_fusion
  5.4 2.7 %collective-permute-start.17 = (bf16[2,720,2880]{2,1,0:T(8,128)(2,1)}, bf16[2,720,2880]{2,1,0:T(8,128)(2,1)}, u32[]{:S(2)}, u32[]{:S(2)}) collective-permute-start(bf16[2,720,2880]{2,1,0:T(8,128)(2,1)} %bitcast.56), channel_id=1, source_target_pairs={{0,1},{1,0},{2,3},{3,2},{4,5},{5,4},{6,7},{7,6},{8,9},{9,8},{10,11... | collective-permute-start | bytes 24883208 | tf_op jit(solution)/shard_map/ppermute | solution.py:23
  8.1 6.4 %copy.19 = bf16[1,1440,1440]{1,2,0:T(8,128)(2,1)} copy(bf16[1,1440,1440]{2,1,0:T(8,128)(2,1)} %param.19) | data formatting | bytes 8294400 | tf_op jit(solution)/shard_map/optimization_barrier | solution.py:302
  14.7 2.6 %collective-permute-start.7 = (bf16[720,512]{1,0:T(8,128)(2,1)S(1)}, bf16[720,512]{1,0:T(8,128)(2,1)S(1)}, u32[]{:S(2)}, u32[]{:S(2)}) collective-permute-start(bf16[720,512]{1,0:T(8,128)(2,1)S(1)} %dynamic-slice_bitcast_fusion), channel_id=1, source_target_pairs={{0,4},{4,0},{8,12},{12,8},{1,5},{5,1},{9,13},{13,9},{2,6},{6,2},{1... | collective-permute-start | bytes 2211848 | tf_op jit(solution)/shard_map/ppermute | solution.py:23
  17.3 16.8 %collective-permute-done.7.refs_2_ = bf16[720,512]{1,0:T(8,128)(2,1)S(1)} collective-permute-done((bf16[720,512]{1,0:T(8,128)(2,1)S(1)}, bf16[720,512]{1,0:T(8,128)(2,1)S(1)}, u32[]{:S(2)}, u32[]{:S(2)}) %collective-permute-start.7) | collective-permute-done | bytes 737312 | tf_op jit(solution)/shard_map/ppermute | solution.py:23
  34.1 1.5 collective-permute-start.8
  35.6 4.4 %collective-permute-start.2 = (bf16[1440,128]{1,0:T(8,128)(2,1)}, bf16[1440,128]{1,0:T(8,128)(2,1)}, u32[]{:S(2)}, u32[]{:S(2)}) collective-permute-start(bf16[1440,128]{1,0:T(8,128)(2,1)} %dynamic-slice_bitcast_fusion.1), channel_id=1, source_target_pairs={{0,0},{2,10},{4,4},{6,14},{8,8},{10,2},{12,12},{14,6},{1,1},{3,11}... | collective-permute-start | bytes 1105928 | tf_op jit(solution)/shard_map/ppermute | solution.py:312
  40.1 1.8 collective-permute-start.3
  41.9 1.9 collective-permute-done.3
  43.7 2.8 %collective-permute-start.4 = (f32[8,128]{1,0:T(8,128)S(1)}, f32[8,128]{1,0:T(8,128)S(1)}, u32[]{:S(2)}, u32[]{:S(2)}) collective-permute-start(f32[8,128]{1,0:T(8,128)S(1)} %select_reduce_fusion), channel_id=1, source_target_pairs={{0,8},{4,12},{8,0},{12,4},{1,9},{5,13},{9,1},{13,5},{2,10},{6,14},... | collective-permute-start | bytes 12296 | tf_op jit(solution)/shard_map/ppermute | solution.py:23
  46.6 1.7 collective-permute-done.4
  48.2 3.8 %collective-permute-start.5 = (f32[8,128]{1,0:T(8,128)S(1)}, f32[8,128]{1,0:T(8,128)S(1)}, u32[]{:S(2)}, u32[]{:S(2)}) collective-permute-start(f32[8,128]{1,0:T(8,128)S(1)} %select_reduce_fusion), channel_id=1, source_target_pairs={{0,12},{4,8},{8,4},{12,0},{1,13},{5,9},{9,5},{13,1},{2,14},{6,10},... | collective-permute-start | bytes 12296 | tf_op jit(solution)/shard_map/ppermute | solution.py:23
  52.1 1.6 collective-permute-done.5
  54.3 5.6 %attention.1.refs_0_ = bf16[2048,128]{1,0:T(8,128)(2,1)S(1)} custom-call(s32[1]{0:T(128)} %bitcast.1.first_ref, f32[32]{0:T(128)S(1)} %copy-done.11, bf16[128,2048]{1,0:T(8,128)(2,1)S(1)} %copy-done.6, bf16[128,512]{1,0:T(8,128)(2,1)S(1)} %collective-permute-done.earlier_ref, bf16[128,256]{1,0:T(8,128)(2,1)S(1)} %copy-done.10, bf16[128,256]{1,0:T(8,128)(2,1)S(1)} %copy-done.9), custom_call_target="tpu_custom_call" | custom-call | flops 268435456 | bytes 1572864 | tf_op jit(solution)/shard_map/attention/pallas_call | solution.py:116
  59.9 1.0 collective-permute-start.1
  61.6 24.2 %collective-permute-done.1.refs_1_ = bf16[2048,128]{1,0:T(8,128)(2,1)S(1)} collective-permute-done((bf16[2048,128]{1,0:T(8,128)(2,1)S(1)}, bf16[2048,128]{1,0:T(8,128)(2,1)S(1)}, u32[]{:S(2)}, u32[]{:S(2)}) %collective-permute-start.1) | collective-permute-done | bytes 524320 | tf_op jit(solution)/shard_map/ppermute | solution.py:23
  85.9 1.8 copy-done.3
  87.7 1.5 project.2
  89.3 2.5 %project.3 = (f32[720,128]{1,0:T(8,128)S(1)}, bf16[1,720,128]{2,1,0:T(8,128)(2,1)S(1)}) custom-call(s32[2]{0:T(128)S(1)} %pad_add_fusion.1.place_ref, bf16[2048,128]{1,0:T(8,128)(2,1)S(1)} %attention.1.refs_0_, bf16[2048,128]{1,0:T(8,128)(2,1)S(1)} %collective-permute-done.1.refs_1_, bf16[720,512]{1,0:T(8,128)(2,1)S(1)} %collective-permute-done.7.refs_2_, ...), custom_call_target="tpu_custom_call" | custom-call | flops 754974720 | bytes 2949120 | tf_op jit(solution)/shard_map/project/pallas_call | solution.py:152
  91.8 0.8 copy-done.8
  92.6 9.9 %collective-permute-start.11 = (bf16[1440,128]{1,0:T(8,128)(2,1)S(1)}, bf16[1440,128]{1,0:T(8,128)(2,1)S(1)}, u32[]{:S(2)}, u32[]{:S(2)}) collective-permute-start(bf16[1440,128]{1,0:T(8,128)(2,1)S(1)} %pad_maximum_fusion), channel_id=1, source_target_pairs={{0,2},{2,0},{1,3},{3,1},{4,6},{6,4},{5,7},{7,5},{8,10},{10,8},{9,1... | collective-permute-start | bytes 1105928 | tf_op jit(solution)/shard_map/ppermute | solution.py:23
  102.6 1.2 broadcast_select_fusion.1
  103.7 6.8 %collective-permute-done.11 = bf16[1440,128]{1,0:T(8,128)(2,1)S(1)} collective-permute-done((bf16[1440,128]{1,0:T(8,128)(2,1)S(1)}, bf16[1440,128]{1,0:T(8,128)(2,1)S(1)}, u32[]{:S(2)}, u32[]{:S(2)}) %collective-permute-start.11) | collective-permute-done | bytes 368672 | tf_op jit(solution)/shard_map/ppermute | solution.py:23
  110.6 1.3 fusion.2.refs_0_
  112.0 2.4 %collective-permute-start.13 = (bf16[1440,128]{1,0:T(8,128)(2,1)S(1)}, bf16[1440,128]{1,0:T(8,128)(2,1)S(1)}, u32[]{:S(2)}, u32[]{:S(2)}) collective-permute-start(bf16[1440,128]{1,0:T(8,128)(2,1)S(1)} %fusion.2.refs_0_), channel_id=1, source_target_pairs={{0,4},{4,0},{8,12},{12,8},{1,5},{5,1},{9,13},{13,9},{2,6},{6,2},{1... | collective-permute-start | bytes 1105928 | tf_op jit(solution)/shard_map/ppermute | solution.py:23
  114.5 1.7 collective-permute-start.15
  116.2 13.8 %collective-permute-done.12.refs_1_ = bf16[1440,128]{1,0:T(8,128)(2,1)S(1)} collective-permute-done((bf16[1440,128]{1,0:T(8,128)(2,1)S(1)}, bf16[1440,128]{1,0:T(8,128)(2,1)S(1)}, u32[]{:S(2)}, u32[]{:S(2)}) %collective-permute-start.12) | collective-permute-done | bytes 368672 | tf_op jit(solution)/shard_map/ppermute | solution.py:23
  130.0 1.4 collective-permute-start.16
  131.6 8.8 %collective-permute-done.14.refs_1_ = bf16[1440,128]{1,0:T(8,128)(2,1)S(1)} collective-permute-done((bf16[1440,128]{1,0:T(8,128)(2,1)S(1)}, bf16[1440,128]{1,0:T(8,128)(2,1)S(1)}, u32[]{:S(2)}, u32[]{:S(2)}) %collective-permute-start.14) | collective-permute-done | bytes 368672 | tf_op jit(solution)/shard_map/ppermute | solution.py:23
  140.4 1.5 collective-permute-start.20
  142.4 3.4 %copy-done.2 = bf16[1,2,2880,720]{2,3,1,0:T(8,128)(2,1)S(1)} copy-done((bf16[1,2,2880,720]{2,3,1,0:T(8,128)(2,1)S(1)}, bf16[1,2,2880,720]{2,3,1,0:T(8,128)(2,1)}, u32[]{:S(2)}) %copy-start.2) | copy-done | bytes 8294424
  145.8 11.8 %activate.2.refs_0_ = bf16[2,720,256]{2,1,0:T(8,128)(2,1)S(1)} custom-call(s32[2]{0:T(128)S(1)} %pad_add_fusion.2.place_ref, bf16[1440,128]{1,0:T(8,128)(2,1)S(1)} %fusion.2.refs_0_, bf16[1440,128]{1,0:T(8,128)(2,1)S(1)} %collective-permute-done.12.refs_1_, bf16[1440,128]{1,0:T(8,128)(2,1)S(1)} %collective-permute-done.15.refs_2_, ...), custom_call_target="tpu_custom_call" | custom-call | flops 4246732800 | bytes 16588800 | tf_op jit(solution)/shard_map/activate/pallas_call | solution.py:205
  157.7 1.5 collective-permute-start.18
  159.2 11.7 %activate.3.refs_0_ = bf16[2,720,256]{2,1,0:T(8,128)(2,1)S(1)} custom-call(s32[2]{0:T(128)S(1)} %pad_add_fusion.2.place_ref, bf16[1440,128]{1,0:T(8,128)(2,1)S(1)} %collective-permute-done.13.refs_0_, bf16[1440,128]{1,0:T(8,128)(2,1)S(1)} %collective-permute-done.14.refs_1_, bf16[1440,128]{1,0:T(8,128)(2,1)S(1)} %collective-permute-done.20.refs_2_, ...), custom_call_target="tpu_custom_call" | custom-call | flops 4246732800 | bytes 16588800 | tf_op jit(solution)/shard_map/activate/pallas_call | solution.py:205
  171.6 5.7 %collective-permute-done.18.refs_1_ = bf16[2,720,256]{2,1,0:T(8,128)(2,1)} collective-permute-done((bf16[2,720,256]{2,1,0:T(8,128)(2,1)S(1)}, bf16[2,720,256]{2,1,0:T(8,128)(2,1)}, u32[]{:S(2)}, u32[]{:S(2)}) %collective-permute-start.18) | collective-permute-done | bytes 737312 | tf_op jit(solution)/shard_map/ppermute | solution.py:23
  177.3 2.3 %copy-done.1 = bf16[1,1440,1440]{1,2,0:T(8,128)(2,1)S(1)} copy-done((bf16[1,1440,1440]{1,2,0:T(8,128)(2,1)S(1)}, bf16[1,1440,1440]{1,2,0:T(8,128)(2,1)}, u32[]{:S(2)}) %copy-start.1) | copy-done | bytes 4147224
  179.6 6.9 %combine.2 = (bf16[1440,128]{1,0:T(8,128)(2,1)S(1)}, bf16[1440,128]{1,0:T(8,128)(2,1)S(1)}) custom-call(s32[1]{0:T(128)} %bitcast.t_ref, bf16[2,720,256]{2,1,0:T(8,128)(2,1)S(1)} %activate.2.refs_0_, bf16[2,720,256]{2,1,0:T(8,128)(2,1)} %collective-permute-done.18.refs_1_, f32[2,256]{1,0:T(2,128)S(1)} %get-tuple-element.66.refs_2_, ...), custom_call_target="tpu_custom_call" | custom-call | flops 2123366400 | bytes 8294400 | tf_op jit(solution)/shard_map/combine/pallas_call | solution.py:253
  186.5 1.6 collective-permute-start.19
  188.1 2.5 %collective-permute-done.22.refs_1_ = bf16[2,720,256]{2,1,0:T(8,128)(2,1)} collective-permute-done((bf16[2,720,256]{2,1,0:T(8,128)(2,1)S(1)}, bf16[2,720,256]{2,1,0:T(8,128)(2,1)}, u32[]{:S(2)}, u32[]{:S(2)}) %collective-permute-start.22) | collective-permute-done | bytes 737312 | tf_op jit(solution)/shard_map/ppermute | solution.py:23
  190.6 6.8 %combine.3 = (bf16[1440,128]{1,0:T(8,128)(2,1)S(1)}, bf16[1440,128]{1,0:T(8,128)(2,1)S(1)}) custom-call(s32[1]{0:T(128)} %bitcast.t_ref, bf16[2,720,256]{2,1,0:T(8,128)(2,1)S(1)} %activate.3.refs_0_, bf16[2,720,256]{2,1,0:T(8,128)(2,1)} %collective-permute-done.22.refs_1_, f32[2,256]{1,0:T(2,128)S(1)} %get-tuple-element.67.refs_2_, ...), custom_call_target="tpu_custom_call" | custom-call | flops 2123366400 | bytes 8294400 | tf_op jit(solution)/shard_map/combine/pallas_call | solution.py:253
  197.4 1.5 collective-permute-start.23
  198.8 1.3 collective-permute-start.24
  200.4 3.4 %collective-permute-done.19 = bf16[1440,128]{1,0:T(8,128)(2,1)S(1)} collective-permute-done((bf16[1440,128]{1,0:T(8,128)(2,1)S(1)}, bf16[1440,128]{1,0:T(8,128)(2,1)S(1)}, u32[]{:S(2)}, u32[]{:S(2)}) %collective-permute-start.19) | collective-permute-done | bytes 368672 | tf_op jit(solution)/shard_map/ppermute | solution.py:23
  203.8 12.9 %collective-permute-done.23 = bf16[1440,128]{1,0:T(8,128)(2,1)S(1)} collective-permute-done((bf16[1440,128]{1,0:T(8,128)(2,1)S(1)}, bf16[1440,128]{1,0:T(8,128)(2,1)S(1)}, u32[]{:S(2)}, u32[]{:S(2)}) %collective-permute-start.23) | collective-permute-done | bytes 368672 | tf_op jit(solution)/shard_map/ppermute | solution.py:23
  216.7 1.0 fusion.3
  (72 shorter events, 3.8 us)
Async XLA Ops:
  0.0 3.4 %copy-start = (bf16[128,2880]{0,1:T(8,128)(2,1)S(1)}, bf16[128,2880]{0,1:T(8,128)(2,1)}, u32[]{:S(2)}) copy-start(bf16[128,2880]{0,1:T(8,128)(2,1)} %param.16) | copy-start | bytes 2211844
  1.0 4.3 %collective-permute-start = (bf16[128,512]{1,0:T(8,128)(2,1)S(1)}, bf16[128,512]{1,0:T(8,128)(2,1)S(1)}, u32[]{:S(2)}, u32[]{:S(2)}) collective-permute-start(bf16[128,512]{1,0:T(8,128)(2,1)S(1)} %pad_maximum_fusion.1), channel_id=1, source_target_pairs={{0,1},{1,4},{4,5},{5,8},{8,9},{9,12},{12,13},{2,3},{3,6},{6,7},{7,... | collective-permute-start | bytes 393224 | tf_op jit(solution)/shard_map/ppermute | solution.py:19
  5.3 30.3 %copy-start.13 = (s32[128,4]{0,1:T(4,128)S(1)}, s32[128,4]{0,1:T(4,128)}, u32[]{:S(2)}) copy-start(s32[128,4]{0,1:T(4,128)} %param.21) | copy-start | bytes 6148
  5.3 34.7 %copy-start.14 = (s32[128,4]{0,1:T(4,128)S(1)}, s32[128,4]{0,1:T(4,128)}, u32[]{:S(2)}) copy-start(s32[128,4]{0,1:T(4,128)} %param.20) | copy-start | bytes 6148
  5.3 48.9 %copy-start.6 = (bf16[128,2048]{1,0:T(8,128)(2,1)S(1)}, bf16[128,2048]{1,0:T(8,128)(2,1)}, u32[]{:S(2)}) copy-start(bf16[128,2048]{1,0:T(8,128)(2,1)} %q_ref.1) | copy-start | bytes 1572868
  5.3 48.9 %copy-start.9 = (bf16[128,256]{1,0:T(8,128)(2,1)S(1)}, bf16[128,256]{1,0:T(8,128)(2,1)}, u32[]{:S(2)}) copy-start(bf16[128,256]{1,0:T(8,128)(2,1)} %v_ref.1) | copy-start | bytes 196612
  5.4 48.9 %copy-start.10 = (bf16[128,256]{1,0:T(8,128)(2,1)S(1)}, bf16[128,256]{1,0:T(8,128)(2,1)}, u32[]{:S(2)}) copy-start(bf16[128,256]{1,0:T(8,128)(2,1)} %k_ref.1) | copy-start | bytes 196612
  5.4 48.9 %copy-start.11 = (f32[32]{0:T(128)S(1)}, f32[32]{0:T(128)}, u32[]{:S(2)}) copy-start(f32[32]{0:T(128)} %sink_ref.1) | copy-start | bytes 388
  5.4 137.1 %collective-permute-start.17 = (bf16[2,720,2880]{2,1,0:T(8,128)(2,1)}, bf16[2,720,2880]{2,1,0:T(8,128)(2,1)}, u32[]{:S(2)}, u32[]{:S(2)}) collective-permute-start(bf16[2,720,2880]{2,1,0:T(8,128)(2,1)} %bitcast.56), channel_id=1, source_target_pairs={{0,1},{1,0},{2,3},{3,2},{4,5},{5,4},{6,7},{7,6},{8,9},{9,8},{10,11... | collective-permute-start | bytes 24883208 | tf_op jit(solution)/shard_map/ppermute | solution.py:23
  14.6 71.3 %collective-permute-start.6 = (bf16[1440,1440]{0,1:T(8,128)(2,1)}, bf16[1440,1440]{0,1:T(8,128)(2,1)}, u32[]{:S(2)}, u32[]{:S(2)}) collective-permute-start(bf16[1440,1440]{0,1:T(8,128)(2,1)} %bitcast.53), channel_id=1, source_target_pairs={{0,1},{1,0},{2,3},{3,2},{4,5},{5,4},{6,7},{7,6},{8,9},{9,8},{10,11... | collective-permute-start | bytes 12441608 | tf_op jit(solution)/shard_map/ppermute | solution.py:23
  14.7 19.4 %collective-permute-start.7 = (bf16[720,512]{1,0:T(8,128)(2,1)S(1)}, bf16[720,512]{1,0:T(8,128)(2,1)S(1)}, u32[]{:S(2)}, u32[]{:S(2)}) collective-permute-start(bf16[720,512]{1,0:T(8,128)(2,1)S(1)} %dynamic-slice_bitcast_fusion), channel_id=1, source_target_pairs={{0,4},{4,0},{8,12},{12,8},{1,5},{5,1},{9,13},{13,9},{2,6},{6,2},{1... | collective-permute-start | bytes 2211848 | tf_op jit(solution)/shard_map/ppermute | solution.py:23
  34.1 19.6 %collective-permute-start.8 = (bf16[720,512]{1,0:T(8,128)(2,1)S(1)}, bf16[720,512]{1,0:T(8,128)(2,1)S(1)}, u32[]{:S(2)}, u32[]{:S(2)}) collective-permute-start(bf16[720,512]{1,0:T(8,128)(2,1)S(1)} %collective-permute-done.7.refs_2_), channel_id=1, source_target_pairs={{0,16},{16,0},{1,17},{17,1},{2,18},{18,2},{3,19},{19,3},{4,20},{20... | collective-permute-start | bytes 2211848 | tf_op jit(solution)/shard_map/ppermute | solution.py:23
  35.6 24.2 %collective-permute-start.2 = (bf16[1440,128]{1,0:T(8,128)(2,1)}, bf16[1440,128]{1,0:T(8,128)(2,1)}, u32[]{:S(2)}, u32[]{:S(2)}) collective-permute-start(bf16[1440,128]{1,0:T(8,128)(2,1)} %dynamic-slice_bitcast_fusion.1), channel_id=1, source_target_pairs={{0,0},{2,10},{4,4},{6,14},{8,8},{10,2},{12,12},{14,6},{1,1},{3,11}... | collective-permute-start | bytes 1105928 | tf_op jit(solution)/shard_map/ppermute | solution.py:312
  40.1 3.7 %collective-permute-start.3 = (f32[8,128]{1,0:T(8,128)S(1)}, f32[8,128]{1,0:T(8,128)S(1)}, u32[]{:S(2)}, u32[]{:S(2)}) collective-permute-start(f32[8,128]{1,0:T(8,128)S(1)} %select_reduce_fusion), channel_id=1, source_target_pairs={{0,4},{4,0},{8,12},{12,8},{1,5},{5,1},{9,13},{13,9},{2,6},{6,2},{1... | collective-permute-start | bytes 12296 | tf_op jit(solution)/shard_map/ppermute | solution.py:23
  43.7 4.5 %collective-permute-start.4 = (f32[8,128]{1,0:T(8,128)S(1)}, f32[8,128]{1,0:T(8,128)S(1)}, u32[]{:S(2)}, u32[]{:S(2)}) collective-permute-start(f32[8,128]{1,0:T(8,128)S(1)} %select_reduce_fusion), channel_id=1, source_target_pairs={{0,8},{4,12},{8,0},{12,4},{1,9},{5,13},{9,1},{13,5},{2,10},{6,14},... | collective-permute-start | bytes 12296 | tf_op jit(solution)/shard_map/ppermute | solution.py:23
  48.2 5.4 %collective-permute-start.5 = (f32[8,128]{1,0:T(8,128)S(1)}, f32[8,128]{1,0:T(8,128)S(1)}, u32[]{:S(2)}, u32[]{:S(2)}) collective-permute-start(f32[8,128]{1,0:T(8,128)S(1)} %select_reduce_fusion), channel_id=1, source_target_pairs={{0,12},{4,8},{8,4},{12,0},{1,13},{5,9},{9,5},{13,1},{2,14},{6,10},... | collective-permute-start | bytes 12296 | tf_op jit(solution)/shard_map/ppermute | solution.py:23
  53.6 35.6 %collective-permute-start.9 = (bf16[720,512]{1,0:T(8,128)(2,1)S(1)}, bf16[720,512]{1,0:T(8,128)(2,1)}, u32[]{:S(2)}, u32[]{:S(2)}) collective-permute-start(bf16[720,512]{1,0:T(8,128)(2,1)S(1)} %collective-permute-done.7.refs_2_), channel_id=1, source_target_pairs={{0,1},{1,0},{2,3},{3,2},{4,5},{5,4},{6,7},{7,6},{8,9},{9,8},{10,11... | collective-permute-start | bytes 2211848 | tf_op jit(solution)/shard_map/ppermute | solution.py:23
  53.7 35.6 %collective-permute-start.10 = (bf16[720,512]{1,0:T(8,128)(2,1)S(1)}, bf16[720,512]{1,0:T(8,128)(2,1)}, u32[]{:S(2)}, u32[]{:S(2)}) collective-permute-start(bf16[720,512]{1,0:T(8,128)(2,1)S(1)} %collective-permute-done.8.refs_3_), channel_id=1, source_target_pairs={{0,1},{1,0},{2,3},{3,2},{4,5},{5,4},{6,7},{7,6},{8,9},{9,8},{10,11... | collective-permute-start | bytes 2211848 | tf_op jit(solution)/shard_map/ppermute | solution.py:23
  59.9 26.0 %collective-permute-start.1 = (bf16[2048,128]{1,0:T(8,128)(2,1)S(1)}, bf16[2048,128]{1,0:T(8,128)(2,1)S(1)}, u32[]{:S(2)}, u32[]{:S(2)}) collective-permute-start(bf16[2048,128]{1,0:T(8,128)(2,1)S(1)} %attention.1.refs_0_), channel_id=1, source_target_pairs={{0,8},{4,12},{8,0},{12,4},{1,9},{5,13},{9,1},{13,5},{2,10},{6,14},... | collective-permute-start | bytes 1572872 | tf_op jit(solution)/shard_map/ppermute | solution.py:23
  85.9 1.8 copy-start.3
  87.7 14.8 %copy-start.12 = (f32[2880]{0:T(1024)S(1)}, f32[2880]{0:T(1024)}, u32[]{:S(2)}) copy-start(f32[2880]{0:T(1024)} %param.17) | copy-start | bytes 34564
  89.3 2.5 %copy-start.7 = (f32[720,128]{1,0:T(8,128)}, f32[720,128]{1,0:T(8,128)S(1)}, u32[]{:S(2)}) copy-start(f32[720,128]{1,0:T(8,128)S(1)} %get-tuple-element.37) | copy-start | bytes 1105924
  91.8 0.8 copy-start.8
  92.6 18.0 %collective-permute-start.11 = (bf16[1440,128]{1,0:T(8,128)(2,1)S(1)}, bf16[1440,128]{1,0:T(8,128)(2,1)S(1)}, u32[]{:S(2)}, u32[]{:S(2)}) collective-permute-start(bf16[1440,128]{1,0:T(8,128)(2,1)S(1)} %pad_maximum_fusion), channel_id=1, source_target_pairs={{0,2},{2,0},{1,3},{3,1},{4,6},{6,4},{5,7},{7,5},{8,10},{10,8},{9,1... | collective-permute-start | bytes 1105928 | tf_op jit(solution)/shard_map/ppermute | solution.py:23
  111.8 18.2 %collective-permute-start.12 = (bf16[1440,128]{1,0:T(8,128)(2,1)S(1)}, bf16[1440,128]{1,0:T(8,128)(2,1)S(1)}, u32[]{:S(2)}, u32[]{:S(2)}) collective-permute-start(bf16[1440,128]{1,0:T(8,128)(2,1)S(1)} %fusion.2.refs_0_), channel_id=1, source_target_pairs={{0,8},{4,12},{8,0},{12,4},{1,9},{5,13},{9,1},{13,5},{2,10},{6,14},... | collective-permute-start | bytes 1105928 | tf_op jit(solution)/shard_map/ppermute | solution.py:23
  112.0 19.6 %collective-permute-start.13 = (bf16[1440,128]{1,0:T(8,128)(2,1)S(1)}, bf16[1440,128]{1,0:T(8,128)(2,1)S(1)}, u32[]{:S(2)}, u32[]{:S(2)}) collective-permute-start(bf16[1440,128]{1,0:T(8,128)(2,1)S(1)} %fusion.2.refs_0_), channel_id=1, source_target_pairs={{0,4},{4,0},{8,12},{12,8},{1,5},{5,1},{9,13},{13,9},{2,6},{6,2},{1... | collective-permute-start | bytes 1105928 | tf_op jit(solution)/shard_map/ppermute | solution.py:23
  114.5 17.1 %collective-permute-start.15 = (bf16[1440,128]{1,0:T(8,128)(2,1)S(1)}, bf16[1440,128]{1,0:T(8,128)(2,1)S(1)}, u32[]{:S(2)}, u32[]{:S(2)}) collective-permute-start(bf16[1440,128]{1,0:T(8,128)(2,1)S(1)} %fusion.2.refs_0_), channel_id=1, source_target_pairs={{0,2},{2,0},{1,3},{3,1},{4,6},{6,4},{5,7},{7,5},{8,10},{10,8},{9,1... | collective-permute-start | bytes 1105928 | tf_op jit(solution)/shard_map/ppermute | solution.py:23
  130.0 10.4 %collective-permute-start.14 = (bf16[1440,128]{1,0:T(8,128)(2,1)S(1)}, bf16[1440,128]{1,0:T(8,128)(2,1)S(1)}, u32[]{:S(2)}, u32[]{:S(2)}) collective-permute-start(bf16[1440,128]{1,0:T(8,128)(2,1)S(1)} %collective-permute-done.12.refs_1_), channel_id=1, source_target_pairs={{0,4},{4,0},{8,12},{12,8},{1,5},{5,1},{9,13},{13,9},{2,6},{6,2},{1... | collective-permute-start | bytes 1105928 | tf_op jit(solution)/shard_map/ppermute | solution.py:23
  130.0 10.4 %collective-permute-start.16 = (bf16[1440,128]{1,0:T(8,128)(2,1)S(1)}, bf16[1440,128]{1,0:T(8,128)(2,1)S(1)}, u32[]{:S(2)}, u32[]{:S(2)}) collective-permute-start(bf16[1440,128]{1,0:T(8,128)(2,1)S(1)} %collective-permute-done.12.refs_1_), channel_id=1, source_target_pairs={{0,2},{2,0},{1,3},{3,1},{4,6},{6,4},{5,7},{7,5},{8,10},{10,8},{9,1... | collective-permute-start | bytes 1105928 | tf_op jit(solution)/shard_map/ppermute | solution.py:23
  140.4 17.3 %copy-start.4 = (bf16[1440,128]{1,0:T(8,128)(2,1)}, bf16[1440,128]{1,0:T(8,128)(2,1)S(1)}, u32[]{:S(2)}) copy-start(bf16[1440,128]{1,0:T(8,128)(2,1)S(1)} %collective-permute-done.16.refs_3_) | copy-start | bytes 1105924
  140.4 18.8 %collective-permute-start.20 = (bf16[1440,128]{1,0:T(8,128)(2,1)S(1)}, bf16[1440,128]{1,0:T(8,128)(2,1)S(1)}, u32[]{:S(2)}, u32[]{:S(2)}) collective-permute-start(bf16[1440,128]{1,0:T(8,128)(2,1)S(1)} %collective-permute-done.13.refs_0_), channel_id=1, source_target_pairs={{0,2},{2,0},{1,3},{3,1},{4,6},{6,4},{5,7},{7,5},{8,10},{10,8},{9,1... | collective-permute-start | bytes 1105928 | tf_op jit(solution)/shard_map/ppermute | solution.py:23
  141.9 17.4 %collective-permute-start.21 = (bf16[1440,128]{1,0:T(8,128)(2,1)S(1)}, bf16[1440,128]{1,0:T(8,128)(2,1)S(1)}, u32[]{:S(2)}, u32[]{:S(2)}) collective-permute-start(bf16[1440,128]{1,0:T(8,128)(2,1)S(1)} %collective-permute-done.14.refs_1_), channel_id=1, source_target_pairs={{0,2},{2,0},{1,3},{3,1},{4,6},{6,4},{5,7},{7,5},{8,10},{10,8},{9,1... | collective-permute-start | bytes 1105928 | tf_op jit(solution)/shard_map/ppermute | solution.py:23
  142.4 3.4 %copy-start.2 = (bf16[1,2,2880,720]{2,3,1,0:T(8,128)(2,1)S(1)}, bf16[1,2,2880,720]{2,3,1,0:T(8,128)(2,1)}, u32[]{:S(2)}) copy-start(bf16[1,2,2880,720]{2,3,1,0:T(8,128)(2,1)} %param.18) | copy-start | bytes 24883204
  157.7 19.6 %collective-permute-start.18 = (bf16[2,720,256]{2,1,0:T(8,128)(2,1)S(1)}, bf16[2,720,256]{2,1,0:T(8,128)(2,1)}, u32[]{:S(2)}, u32[]{:S(2)}) collective-permute-start(bf16[2,720,256]{2,1,0:T(8,128)(2,1)S(1)} %activate.2.refs_0_), channel_id=1, source_target_pairs={{0,2},{2,0},{1,3},{3,1},{4,6},{6,4},{5,7},{7,5},{8,10},{10,8},{9,1... | collective-permute-start | bytes 2211848 | tf_op jit(solution)/shard_map/ppermute | solution.py:23
  170.9 19.7 %collective-permute-start.22 = (bf16[2,720,256]{2,1,0:T(8,128)(2,1)S(1)}, bf16[2,720,256]{2,1,0:T(8,128)(2,1)}, u32[]{:S(2)}, u32[]{:S(2)}) collective-permute-start(bf16[2,720,256]{2,1,0:T(8,128)(2,1)S(1)} %activate.3.refs_0_), channel_id=1, source_target_pairs={{0,2},{2,0},{1,3},{3,1},{4,6},{6,4},{5,7},{7,5},{8,10},{10,8},{9,1... | collective-permute-start | bytes 2211848 | tf_op jit(solution)/shard_map/ppermute | solution.py:23
  177.3 2.3 %copy-start.1 = (bf16[1,1440,1440]{1,2,0:T(8,128)(2,1)S(1)}, bf16[1,1440,1440]{1,2,0:T(8,128)(2,1)}, u32[]{:S(2)}) copy-start(bf16[1,1440,1440]{1,2,0:T(8,128)(2,1)} %copy.19) | copy-start | bytes 12441604
  186.5 17.3 %collective-permute-start.19 = (bf16[1440,128]{1,0:T(8,128)(2,1)S(1)}, bf16[1440,128]{1,0:T(8,128)(2,1)S(1)}, u32[]{:S(2)}, u32[]{:S(2)}) collective-permute-start(bf16[1440,128]{1,0:T(8,128)(2,1)S(1)} %get-tuple-element.50), channel_id=1, source_target_pairs={{0,8},{4,12},{8,0},{12,4},{1,9},{5,13},{9,1},{13,5},{2,10},{6,14},... | collective-permute-start | bytes 1105928 | tf_op jit(solution)/shard_map/ppermute | solution.py:23
  190.6 9.5 %copy-start.5 = (bf16[1440,128]{1,0:T(8,128)(2,1)S(1)}, bf16[1440,128]{1,0:T(8,128)(2,1)}, u32[]{:S(2)}) copy-start(bf16[1440,128]{1,0:T(8,128)(2,1)} %copy-done.4) | copy-start | bytes 1105924
  197.4 19.4 %collective-permute-start.23 = (bf16[1440,128]{1,0:T(8,128)(2,1)S(1)}, bf16[1440,128]{1,0:T(8,128)(2,1)S(1)}, u32[]{:S(2)}, u32[]{:S(2)}) collective-permute-start(bf16[1440,128]{1,0:T(8,128)(2,1)S(1)} %get-tuple-element.57), channel_id=1, source_target_pairs={{0,4},{4,0},{8,12},{12,8},{1,5},{5,1},{9,13},{13,9},{2,6},{6,2},{1... | collective-permute-start | bytes 1105928 | tf_op jit(solution)/shard_map/ppermute | solution.py:23
  198.8 17.9 %collective-permute-start.24 = (bf16[1440,128]{1,0:T(8,128)(2,1)S(1)}, bf16[1440,128]{1,0:T(8,128)(2,1)S(1)}, u32[]{:S(2)}, u32[]{:S(2)}) collective-permute-start(bf16[1440,128]{1,0:T(8,128)(2,1)S(1)} %get-tuple-element.58), channel_id=1, source_target_pairs={{0,12},{4,8},{8,4},{12,0},{1,13},{5,9},{9,5},{13,1},{2,14},{6,10},... | collective-permute-start | bytes 1105928 | tf_op jit(solution)/shard_map/ppermute | solution.py:23

commit v7 on v6

--- a/solution.py
+++ b/solution.py
@@ -1,3 +1,5 @@
+import functools
+
 import jax
 import jax.numpy as jnp
 from jax import lax
@@ -51,13 +53,30 @@
     return pltpu.CompilerParams(vmem_limit_bytes=limit)
 
 
-def fetches(sources, held, arrived):
-    return [
-        pltpu.make_async_copy(source, held.at[index], arrived.at[index]) for index, source in enumerate(sources)
-    ]
-
-
-def attention_kernel(first_ref, sink_ref, q_ref, earlier_ref, k_ref, v_ref, out_ref):
+class Fetches:
+    def __init__(self, pairs, arrived, flying=3):
+        self.copies = [
+            pltpu.make_async_copy(source, target, arrived.at[index])
+            for index, (source, target) in enumerate(pairs)
+        ]
+        self.flying = flying
+        self.taken = 0
+        for copy in self.copies[:flying]:
+            copy.start()
+
+    def take(self):
+        self.copies[self.taken].wait()
+        if self.taken + self.flying < len(self.copies):
+            self.copies[self.taken + self.flying].start()
+        self.taken += 1
+
+
+def cuts_of(size, count):
+    count = count if size % (16 * count) == 0 else 1
+    return [slice(i * (size // count), (i + 1) * (size // count)) for i in range(count)]
+
+
+def attention_kernel(part, parts, first_ref, sink_ref, q_ref, earlier_ref, k_ref, v_ref, out_ref):
     rows = q_ref.shape[0]
     kv_count = k_ref.shape[1] // HD
     pairs = q_ref.shape[1] // (2 * HD * kv_count)
@@ -73,14 +92,20 @@
         ],
         axis=1,
     )
+    span = kv_count * pairs // parts
+    chosen = range(part * span, (part + 1) * span)
     for g in range(kv_count):
         head = slice(g * HD, (g + 1) * HD)
+        if not any(index // pairs == g for index in chosen):
+            continue
         keys = jnp.concatenate([earlier_ref[:, head], k_ref[:, head]], axis=0) * jnp.bfloat16(HD ** (-0.5))
         keys = jnp.concatenate(
             [jnp.concatenate([keys, blank], axis=1), jnp.concatenate([blank, keys], axis=1)], axis=0
         )
-        for i in range(pairs):
-            start = (g * pairs + i) * 2 * HD
+        for index in chosen:
+            if index // pairs != g:
+                continue
+            start = index * 2 * HD
             products = lax.dot_general(
                 keys,
                 q_ref[:, start : start + 2 * HD],
@@ -89,9 +114,9 @@
             )
             weights = []
             for side in range(2):
-                sink = sink_ref[(g * pairs + i) * 2 + side]
-                part = products[side * 2 * rows : (side + 1) * 2 * rows]
-                scores = jnp.where(before, part[:rows], part[rows:])
+                sink = sink_ref[index * 2 + side]
+                product = products[side * 2 * rows : (side + 1) * 2 * rows]
+                scores = jnp.where(before, product[:rows], product[rows:])
                 scores = jnp.where(shut, -1e30, scores)
                 largest = jnp.maximum(jnp.max(scores, axis=0, keepdims=True), sink)
                 numerator = jnp.exp(scores - largest)
@@ -107,40 +132,45 @@
                     )
                 )
             result = dot(values[head], jnp.concatenate(weights, axis=1)).astype(jnp.bfloat16)
+            start = start - part * span * 2 * HD
             out_ref[start : start + HD, :] = result[:, :rows]
             out_ref[start + HD : start + 2 * HD, :] = result[:, rows:]
 
 
-def attention(queries, earlier, key_rows, value_rows, sink_logits, first):
+def attention(queries, earlier, key_rows, value_rows, sink_logits, first, part, parts):
     rows, width = queries.shape
     return pl.pallas_call(
-        attention_kernel,
-        out_shape=jax.ShapeDtypeStruct((width, rows), jnp.bfloat16),
+        functools.partial(attention_kernel, part, parts),
+        out_shape=jax.ShapeDtypeStruct((width // parts, rows), jnp.bfloat16),
         in_specs=[in_smem(), in_smem()] + in_vmem(4),
         out_specs=in_vmem(1)[0],
         compiler_params=params(),
-        cost_estimate=cost(8 * rows * rows * width, 6 * rows * width),
+        cost_estimate=cost(8 * rows * rows * width // parts, 6 * rows * width // parts),
         name="attention",
     )(first, sink_logits, queries, earlier, key_rows, value_rows)
 
 
 def project(attended, weights, t, s, t_count):
-    slots = len(attended)
-    width, rows = attended[0].shape
+    slots, parts = len(attended), len(attended[0])
+    part_width, rows = attended[0][0].shape
+    width = parts * part_width
     columns = weights[0].shape[0]
     shares = len(weights)
     depth = width // shares
 
     def kernel(place_ref, *refs):
-        attended_refs = refs[:slots]
-        weight_refs = refs[slots : slots + shares]
-        kept_ref, sent_ref, total = refs[slots + shares :]
+        attended_refs = refs[: slots * parts]
+        weight_refs = refs[slots * parts : slots * parts + shares]
+        kept_ref, sent_ref, all_ref, total = refs[slots * parts + shares :]
         t, s = place_ref[0], place_ref[1]
+        for j in range(slots):
+            for i in range(parts):
+                span = slice(i * part_width, (i + 1) * part_width)
+                all_ref[span, j * rows : (j + 1) * rows] = attended_refs[j * parts + i][...]
         result = 0.0
         for u in range(shares):
             span = pl.ds(pl.multiple_of((s ^ u) * depth, 128), depth)
-            block = jnp.concatenate([ref[span, :] for ref in attended_refs], axis=1)
-            result = result + dot(weight_refs[u][...], block)
+            result = result + dot(weight_refs[u][...], all_ref[span, :])
         total[...] = result
         for m in range(t_count):
             block = total[:, pl.ds(pl.multiple_of((t ^ m) * rows, 128), rows)]
@@ -149,19 +179,23 @@
             else:
                 sent_ref[m - 1] = block.astype(jnp.bfloat16)
 
+    flat = [part for block in attended for part in block]
     return pl.pallas_call(
         kernel,
         out_shape=(
             jax.ShapeDtypeStruct((columns, rows), jnp.float32),
             jax.ShapeDtypeStruct((t_count - 1, columns, rows), jnp.bfloat16),
         ),
-        in_specs=[in_smem()] + in_vmem(slots + shares),
+        in_specs=[in_smem()] + in_vmem(len(flat) + shares),
         out_specs=tuple(in_vmem(2)),
-        scratch_shapes=[pltpu.VMEM((columns, slots * rows), jnp.float32)],
+        scratch_shapes=[
+            pltpu.VMEM((width, slots * rows), jnp.bfloat16),
+            pltpu.VMEM((columns, slots * rows), jnp.float32),
+        ],
         compiler_params=params(),
         cost_estimate=cost(2 * slots * rows * width * columns, 2 * width * columns),
         name="project",
-    )(jnp.stack([t, s]).astype(jnp.int32), *attended, *weights)
+    )(jnp.stack([t, s]).astype(jnp.int32), *flat, *weights)
 
 
 def activate(pieces, gain_table, weights, pair, t):
@@ -170,15 +204,22 @@
     lanes = slots * rows
     experts = len(weights)
     units = weights[0].shape[1]
+    cuts = cuts_of(units, 3)
 
     def kernel(place_ref, *refs):
         piece_refs = refs[: slots * slots]
         table_ref = refs[slots * slots]
         weight_refs = refs[slots * slots + 1 : slots * slots + 1 + experts]
         out_ref, rows_ref, stage_ref, held_ref, arrived = refs[slots * slots + 1 + experts :]
-        copies = fetches([ref.at[k] for ref in weight_refs for k in range(2)], held_ref, arrived)
-        for copy in copies:
-            copy.start()
+        fetched = Fetches(
+            [
+                (weight_refs[e].at[k, cut], held_ref.at[2 * e + k, cut])
+                for e in range(experts)
+                for cut in cuts
+                for k in range(2)
+            ],
+            arrived,
+        )
         for m in range(slots):
             for r in range(slots):
                 lane = pl.ds(pl.multiple_of((place_ref[1] ^ r ^ m) * rows, 128), rows)
@@ -195,11 +236,12 @@
         square = jnp.sum(dot(table_ref[...], (plain * plain).astype(jnp.bfloat16)), axis=0, keepdims=True)
         scale = lax.rsqrt(square / D + 1e-05)
         for e in range(experts):
-            copies[2 * e].wait()
-            gate = dot(held_ref[2 * e], rows_ref[...]) * scale
-            copies[2 * e + 1].wait()
-            up = dot(held_ref[2 * e + 1], rows_ref[...]) * scale
-            out_ref[e] = ((up + 1.0) * gate * jax.nn.sigmoid(1.702 * gate)).astype(jnp.bfloat16)
+            for cut in cuts:
+                fetched.take()
+                gate = dot(held_ref[2 * e, cut], rows_ref[...]) * scale
+                fetched.take()
+                up = dot(held_ref[2 * e + 1, cut], rows_ref[...]) * scale
+                out_ref[e, cut] = ((up + 1.0) * gate * jax.nn.sigmoid(1.702 * gate)).astype(jnp.bfloat16)
 
     flat = [piece for part in pieces for piece in part]
     return pl.pallas_call(
@@ -211,7 +253,7 @@
             pltpu.VMEM((D, lanes), jnp.bfloat16),
             pltpu.VMEM((1, 16, 128) if aligned(depth) else (slots, depth, lanes), jnp.bfloat16),
             pltpu.VMEM((2 * experts, units, D), jnp.bfloat16),
-            pltpu.SemaphoreType.DMA((2 * experts,)),
+            pltpu.SemaphoreType.DMA((2 * experts * len(cuts),)),
         ],
         compiler_params=params(FETCH_BYTES),
         cost_estimate=cost(4 * experts * lanes * D * units, 4 * experts * D * units),
@@ -224,15 +266,16 @@
     experts, units, lanes = activated[0].shape
     width = weights[0].shape[0]
     rows = lanes // slots
+    cuts = cuts_of(width, 3)
 
     def kernel(t_ref, *refs):
         activated_refs = refs[:t_count]
         share_ref = refs[t_count]
         weight_refs = refs[t_count + 1 : t_count + 1 + experts]
         *out_refs, all_ref, stage_ref, held_ref, arrived = refs[t_count + 1 + experts :]
-        copies = fetches(weight_refs, held_ref, arrived)
-        for copy in copies:
-            copy.start()
+        fetched = Fetches(
+            [(weight_refs[e].at[cut], held_ref.at[e, cut]) for cut in cuts for e in range(experts)], arrived
+        )
         for u in range(t_count):
             index = t_ref[0] ^ u
             if aligned(units):
@@ -242,13 +285,14 @@
         if not aligned(units):
             for index in range(t_count):
                 all_ref[:, index * units : (index + 1) * units, :] = stage_ref[index]
-        total = 0.0
-        for e in range(experts):
-            copies[e].wait()
-            result = dot(held_ref[e], all_ref[e]).astype(jnp.bfloat16).astype(jnp.float32)
-            total = total + share_ref[e : e + 1, :] * result
-        for j in range(slots):
-            out_refs[j][...] = total[:, j * rows : (j + 1) * rows].astype(jnp.bfloat16)
+        for cut in cuts:
+            total = 0.0
+            for e in range(experts):
+                fetched.take()
+                result = dot(held_ref[e, cut], all_ref[e]).astype(jnp.bfloat16).astype(jnp.float32)
+                total = total + share_ref[e : e + 1, :] * result
+            for j in range(slots):
+                out_refs[j][cut] = total[:, j * rows : (j + 1) * rows].astype(jnp.bfloat16)
 
     return pl.pallas_call(
         kernel,
@@ -259,7 +303,7 @@
             pltpu.VMEM((experts, t_count * units, lanes), jnp.bfloat16),
             pltpu.VMEM((1, 1, 16, 128) if aligned(units) else (t_count, experts, units, lanes), jnp.bfloat16),
             pltpu.VMEM((experts, width, t_count * units), jnp.bfloat16),
-            pltpu.SemaphoreType.DMA((experts,)),
+            pltpu.SemaphoreType.DMA((experts * len(cuts),)),
         ],
         compiler_params=params(FETCH_BYTES),
         cost_estimate=cost(
@@ -294,17 +338,12 @@
     paired = jnp.concatenate([key_rows, value_rows], axis=1)
     earlier = shifted(paired, ("ep", "sub"), 1)
     out_weight = out_weight.T
-    g_count = lax.axis_size("groups")
-    share = s * g_count + lax.axis_index("groups").astype(jnp.int32)
-    depth = out_weight.shape[1] // (s_count * g_count)
-    near = lax.dynamic_slice_in_dim(out_weight, share * depth, depth, 1)
+    depth = out_weight.shape[1] // s_count
+    near = lax.dynamic_slice_in_dim(out_weight, s * depth, depth, 1)
     residual = picked(residual.T.reshape(slots, group * columns, rows), pair ^ t, 0)
-    earlier, near, residual, expert_in, expert_out = lax.optimization_barrier(
-        (earlier, near, residual, expert_in, expert_out)
-    )
+    earlier, near, residual, expert_in = lax.optimization_barrier((earlier, near, residual, expert_in))
 
     near = swapped(near, "ep", 1)
-    near_weights = [near] + [swapped(near, "groups", g) for g in range(1, g_count)]
 
     route = [
         (i * t_count + k, (i ^ (group * k)) * t_count + k) for i in range(z_count) for k in range(t_count)
@@ -312,12 +351,25 @@
     residual = lax.ppermute(residual, ("ep", "tp"), route)
 
     expert_in = expert_in[0].transpose(0, 2, 1)
-    expert_out = expert_out[0]
     experts_in = [expert_in] + [swapped(expert_in, "sub", e) for e in range(1, s_count)]
-    experts_out = [expert_out.T] + [swapped(expert_out, "sub", e).T for e in range(1, s_count)]
 
     first = (lax.axis_index(("ep", "sub")) == 0).astype(jnp.int32).reshape(1)
-    attended = attention(queries, earlier, key_rows, value_rows, sink_logits, first)
+    gathered = [[] for _ in range(slots)]
+    for part in range(2):
+        attended = attention(queries, earlier, key_rows, value_rows, sink_logits, first, part, 2)
+        for j in range(slots):
+            gathered[j].append(swapped(attended, "ep", group * j) if j else attended)
+        if not part:
+            queries, _ = lax.optimization_barrier((queries, attended))
+
+    arrived = [block[0] for block in gathered]
+    arrived, near, expert_out, routes, route_scores = lax.optimization_barrier(
+        (arrived, near, expert_out, routes, route_scores)
+    )
+    gathered = [[arrived[j], gathered[j][1]] for j in range(slots)]
+    near_weights = [near] + [swapped(near, "sub", u) for u in range(1, s_count)]
+    expert_out = expert_out[0].T
+    experts_out = [expert_out] + [swapped(expert_out, "sub", e) for e in range(1, s_count)]
 
     expert_count = z_count * s_count
     route_float = route_scores.T.astype(jnp.float32)
@@ -329,13 +381,10 @@
     tables = jnp.take(tables, jnp.stack([z * s_count + (s ^ e) for e in range(s_count)]), axis=1)
     tables = tables.reshape(slots, group, s_count, rows)
 
-    gathered = [attended] + [swapped(attended, "ep", group * j) for j in range(1, slots)]
-    near_weights = near_weights + [
-        swapped(part, "sub", u) for u in range(1, s_count) for part in near_weights
-    ]
-    gathered, residual, tables, experts_out = lax.optimization_barrier((gathered, residual, tables, experts_out))
+    gathered, residual, tables, expert_out = lax.optimization_barrier((gathered, residual, tables, expert_out))
+    experts_out[0] = expert_out
     mine = project(gathered, [out_weight], t, s * 0, t_count)
-    other = project(gathered, near_weights, t, share, t_count)
+    other = project(gathered, near_weights, t, s, t_count)
     first_member = z % group == 0
 
     def ordered(a, b):

time: 219 us -> 240 us (1.096)
  Pallas kernels: 46.8 us -> 53.2 us
  local copies, waits for them, and re-layouts: 17.5 us -> 22.5 us
  waiting for transfers between devices: 100 us -> 105 us
  starting transfers between devices: 47.7 us -> 51.6 us
    ppermute x23 -> x22, waiting for transfers between devices: 100 us -> 105 us  [swapped(): lax.ppermute(block, axis, [(i, i ^ distance) for i in range(lax.axis_size...]
    pallas_call x2, Pallas kernels: 23.5 us -> 27.3 us  [activate(): pl.pallas_call(kernel, out_shape=jax.ShapeDtypeStruct((experts, units, la...]
    ppermute x23 -> x22, starting transfers between devices: 41 us -> 44.8 us  [swapped(): lax.ppermute(block, axis, [(i, i ^ distance) for i in range(lax.axis_size...]
    unnamed x30 -> x40, local copies, waits for them, and re-layouts: 8.31 us -> 11.6 us
    pallas_call x1 -> x2, Pallas kernels: 5.57 us -> 6.2 us  [attention(): pl.pallas_call(functools.partial(attention_kernel, part, parts), out_shap...]
  transfers between devices with their start and end apart: 25 -> 24, of which waited for: 12 -> 11; matrix products, arithmetic and copies ran while one was open for 6% -> 6% of each run, Pallas kernels for 21% -> 22%
where the time goes in v7:
time: 240 us; the launch traced here: 239 us
  waiting for transfers between devices  105 us (44%)
  Pallas kernels  53.2 us (22%)
  starting transfers between devices  51.6 us (22%)
  local copies, waits for them, and re-layouts  22.5 us (9%)
  other arithmetic  5.82 us (2%)
    ppermute x22, waiting for transfers between devices, swapped(): lax.ppermute(block, axis, [(i, i ^ distance) for i in range(lax.axis_size...  105 us
    ppermute x22, starting transfers between devices, swapped(): lax.ppermute(block, axis, [(i, i ^ distance) for i in range(lax.axis_size...  44.8 us
    pallas_call x2, Pallas kernels, activate(): pl.pallas_call(kernel, out_shape=jax.ShapeDtypeStruct((experts, units, la...  27.3 us
    pallas_call x2, Pallas kernels, combine(): pl.pallas_call(kernel, out_shape=tuple((jax.ShapeDtypeStruct((width, rows...  15.4 us
    unnamed x40, local copies, waits for them, and re-layouts  11.6 us
    optimization_barrier x1, local copies, waits for them, and re-layouts, local(): lax.optimization_barrier((arrived, near, expert_out, routes, route_scores))  6.67 us
    pallas_call x2, Pallas kernels, attention(): pl.pallas_call(functools.partial(attention_kernel, part, parts), out_shap...  6.2 us
  transfers between devices with their start and end apart: 24, of which 11 were waited for; matrix products, arithmetic and copies ran while one was open for 6% of the time, Pallas kernels for 22%

profile of v7, /device:TPU:0, one launch (start us, length us, event | category | flops | bytes accessed | tf_op | source)
XLA Modules:
  0.0 238.8 jit_solution(5973921915293748796)
XLA Ops:
  0.0 1.0 pad_maximum_fusion.1
  1.0 2.4 collective-permute-start
  3.5 0.8 dynamic-slice_bitcast_fusion.1
  4.2 2.6 %dynamic-slice_bitcast_fusion = bf16[720,1024]{1,0:T(8,128)(2,1)} fusion(bf16[2048,720]{0,1:T(8,128)(2,1)} %param.15, s32[]{:T(128)S(6)} %select_n.110), kind=kLoop, calls=%fused_computation.1 | loop fusion | bytes 2949124 | tf_op jit(solution)/shard_map/dynamic_slice | solution.py:342
  6.8 2.7 %collective-permute-start.15 = (bf16[2,720,2880]{2,1,0:T(8,128)(2,1)}, bf16[2,720,2880]{2,1,0:T(8,128)(2,1)}, u32[]{:S(2)}, u32[]{:S(2)}) collective-permute-start(bf16[2,720,2880]{2,1,0:T(8,128)(2,1)} %bitcast.55), channel_id=1, source_target_pairs={{0,1},{1,0},{2,3},{3,2},{4,5},{5,4},{6,7},{7,6},{8,9},{9,8},{10,11... | collective-permute-start | bytes 24883208 | tf_op jit(solution)/shard_map/ppermute | solution.py:25
  9.5 1.6 collective-permute-start.2
  11.1 3.1 %attention.2.refs_0_ = bf16[1024,128]{1,0:T(8,128)(2,1)S(1)} custom-call(s32[1]{0:T(128)} %bitcast.1.first_ref, f32[32]{0:T(128)S(1)} %copy-done.15, bf16[128,2048]{1,0:T(8,128)(2,1)S(1)} %copy-done.4, bf16[128,512]{1,0:T(8,128)(2,1)S(1)} %collective-permute-done.earlier_ref, bf16[128,256]{1,0:T(8,128)(2,1)S(1)} %copy-done.9, bf16[128,256]{1,0:T(8,128)(2,1)S(1)} %copy-done.7), custom_call_target="tpu_custom_call" | custom-call | flops 134217728 | bytes 786432 | tf_op jit(solution)/shard_map/attention/pallas_call | solution.py:142
  14.2 1.9 collective-permute-start.1
  16.1 32.6 %collective-permute-done.1.refs_2_ = bf16[1024,128]{1,0:T(8,128)(2,1)S(1)} collective-permute-done((bf16[1024,128]{1,0:T(8,128)(2,1)S(1)}, bf16[1024,128]{1,0:T(8,128)(2,1)S(1)}, u32[]{:S(2)}, u32[]{:S(2)}) %collective-permute-start.1) | collective-permute-done | bytes 262176 | tf_op jit(solution)/shard_map/ppermute | solution.py:25
  48.7 0.9 collective-permute-done.2.refs_4_
  49.8 4.4 %collective-permute-start.4 = (bf16[1440,128]{1,0:T(8,128)(2,1)}, bf16[1440,128]{1,0:T(8,128)(2,1)}, u32[]{:S(2)}, u32[]{:S(2)}) collective-permute-start(bf16[1440,128]{1,0:T(8,128)(2,1)} %dynamic-slice_bitcast_fusion.1), channel_id=1, source_target_pairs={{0,0},{2,10},{4,4},{6,14},{8,8},{10,2},{12,12},{14,6},{1,1},{3,11}... | collective-permute-start | bytes 1105928 | tf_op jit(solution)/shard_map/ppermute | solution.py:351
  54.3 3.4 %collective-permute-start.7 = (f32[8,128]{1,0:T(8,128)S(1)}, f32[8,128]{1,0:T(8,128)S(1)}, u32[]{:S(2)}, u32[]{:S(2)}) collective-permute-start(f32[8,128]{1,0:T(8,128)S(1)} %select_reduce_fusion), channel_id=1, source_target_pairs={{0,12},{4,8},{8,4},{12,0},{1,13},{5,9},{9,5},{13,1},{2,14},{6,10},... | collective-permute-start | bytes 12296 | tf_op jit(solution)/shard_map/ppermute | solution.py:25
  59.0 0.8 collective-permute-done.7
  59.8 0.8 collective-permute-start.5
  60.6 0.8 copy-done.8
  61.4 0.8 copy-done.10
  62.2 0.9 copy-done.12
  63.1 3.1 %attention.3.refs_1_ = bf16[1024,128]{1,0:T(8,128)(2,1)S(1)} custom-call(s32[1]{0:T(128)} %bitcast.1.first_ref, f32[32]{0:T(128)S(1)} %copy-done.15, bf16[128,2048]{1,0:T(8,128)(2,1)S(1)} %copy-done.4, bf16[128,512]{1,0:T(8,128)(2,1)S(1)} %copy-done.12, bf16[128,256]{1,0:T(8,128)(2,1)S(1)} %copy-done.10, bf16[128,256]{1,0:T(8,128)(2,1)S(1)} %copy-done.8), custom_call_target="tpu_custom_call" | custom-call | flops 134217728 | bytes 786432 | tf_op jit(solution)/shard_map/attention/pallas_call | solution.py:142
  66.3 6.7 %copy.19 = bf16[1,1440,1440]{1,2,0:T(8,128)(2,1)} copy(bf16[1,1440,1440]{2,1,0:T(8,128)(2,1)} %param.19) | data formatting | bytes 8294400 | tf_op jit(solution)/shard_map/optimization_barrier | solution.py:366
  72.9 3.1 %collective-permute-start.3 = (bf16[1024,128]{1,0:T(8,128)(2,1)S(1)}, bf16[1024,128]{1,0:T(8,128)(2,1)S(1)}, u32[]{:S(2)}, u32[]{:S(2)}) collective-permute-start(bf16[1024,128]{1,0:T(8,128)(2,1)S(1)} %attention.3.refs_1_), channel_id=1, source_target_pairs={{0,8},{4,12},{8,0},{12,4},{1,9},{5,13},{9,1},{13,5},{2,10},{6,14},... | collective-permute-start | bytes 786440 | tf_op jit(solution)/shard_map/ppermute | solution.py:25
  76.7 10.5 %collective-permute-done.3.refs_3_ = bf16[1024,128]{1,0:T(8,128)(2,1)S(1)} collective-permute-done((bf16[1024,128]{1,0:T(8,128)(2,1)S(1)}, bf16[1024,128]{1,0:T(8,128)(2,1)S(1)}, u32[]{:S(2)}, u32[]{:S(2)}) %collective-permute-start.3) | collective-permute-done | bytes 262176 | tf_op jit(solution)/shard_map/ppermute | solution.py:25
  87.2 1.8 copy-done.3
  89.0 1.7 project.2
  91.5 2.5 %project.3 = (f32[720,128]{1,0:T(8,128)S(1)}, bf16[1,720,128]{2,1,0:T(8,128)(2,1)S(1)}) custom-call(s32[2]{0:T(128)S(1)} %pad_add_fusion.1.place_ref, bf16[1024,128]{1,0:T(8,128)(2,1)S(1)} %attention.2.refs_0_, bf16[1024,128]{1,0:T(8,128)(2,1)S(1)} %attention.3.refs_1_, bf16[1024,128]{1,0:T(8,128)(2,1)S(1)} %collective-permute-done.1.refs_2_, ...), custom_call_target="tpu_custom_call" | custom-call | flops 754974720 | bytes 2949120 | tf_op jit(solution)/shard_map/project/pallas_call | solution.py:183
  94.0 0.8 copy-done.14
  94.9 13.7 %collective-permute-start.9 = (bf16[1440,128]{1,0:T(8,128)(2,1)S(1)}, bf16[1440,128]{1,0:T(8,128)(2,1)S(1)}, u32[]{:S(2)}, u32[]{:S(2)}) collective-permute-start(bf16[1440,128]{1,0:T(8,128)(2,1)S(1)} %pad_maximum_fusion), channel_id=1, source_target_pairs={{0,2},{2,0},{1,3},{3,1},{4,6},{6,4},{5,7},{7,5},{8,10},{10,8},{9,1... | collective-permute-start | bytes 1105928 | tf_op jit(solution)/shard_map/ppermute | solution.py:25
  108.6 1.2 broadcast_select_fusion.1
  109.8 7.0 %collective-permute-done.9 = bf16[1440,128]{1,0:T(8,128)(2,1)S(1)} collective-permute-done((bf16[1440,128]{1,0:T(8,128)(2,1)S(1)}, bf16[1440,128]{1,0:T(8,128)(2,1)S(1)}, u32[]{:S(2)}, u32[]{:S(2)}) %collective-permute-start.9) | collective-permute-done | bytes 368672 | tf_op jit(solution)/shard_map/ppermute | solution.py:25
  116.8 1.3 fusion.2.refs_0_
  118.2 3.8 %collective-permute-start.11 = (bf16[1440,128]{1,0:T(8,128)(2,1)S(1)}, bf16[1440,128]{1,0:T(8,128)(2,1)S(1)}, u32[]{:S(2)}, u32[]{:S(2)}) collective-permute-start(bf16[1440,128]{1,0:T(8,128)(2,1)S(1)} %fusion.2.refs_0_), channel_id=1, source_target_pairs={{0,4},{4,0},{8,12},{12,8},{1,5},{5,1},{9,13},{13,9},{2,6},{6,2},{1... | collective-permute-start | bytes 1105928 | tf_op jit(solution)/shard_map/ppermute | solution.py:25
  122.1 1.7 collective-permute-start.13
  123.8 12.6 %collective-permute-done.10.refs_1_ = bf16[1440,128]{1,0:T(8,128)(2,1)S(1)} collective-permute-done((bf16[1440,128]{1,0:T(8,128)(2,1)S(1)}, bf16[1440,128]{1,0:T(8,128)(2,1)S(1)}, u32[]{:S(2)}, u32[]{:S(2)}) %collective-permute-start.10) | collective-permute-done | bytes 368672 | tf_op jit(solution)/shard_map/ppermute | solution.py:25
  136.6 1.4 collective-permute-start.14
  138.2 7.6 %collective-permute-done.12.refs_1_ = bf16[1440,128]{1,0:T(8,128)(2,1)S(1)} collective-permute-done((bf16[1440,128]{1,0:T(8,128)(2,1)S(1)}, bf16[1440,128]{1,0:T(8,128)(2,1)S(1)}, u32[]{:S(2)}, u32[]{:S(2)}) %collective-permute-start.12) | collective-permute-done | bytes 368672 | tf_op jit(solution)/shard_map/ppermute | solution.py:25
  145.7 1.4 collective-permute-start.19
  147.8 3.4 %copy-done.2 = bf16[1,2,2880,720]{2,3,1,0:T(8,128)(2,1)S(1)} copy-done((bf16[1,2,2880,720]{2,3,1,0:T(8,128)(2,1)S(1)}, bf16[1,2,2880,720]{2,3,1,0:T(8,128)(2,1)}, u32[]{:S(2)}) %copy-start.2) | copy-done | bytes 8294424
  151.2 13.6 %activate.2.refs_0_ = bf16[2,720,256]{2,1,0:T(8,128)(2,1)S(1)} custom-call(s32[2]{0:T(128)S(1)} %pad_add_fusion.2.place_ref, bf16[1440,128]{1,0:T(8,128)(2,1)S(1)} %fusion.2.refs_0_, bf16[1440,128]{1,0:T(8,128)(2,1)S(1)} %collective-permute-done.10.refs_1_, bf16[1440,128]{1,0:T(8,128)(2,1)S(1)} %collective-permute-done.13.refs_2_, ...), custom_call_target="tpu_custom_call" | custom-call | flops 4246732800 | bytes 16588800 | tf_op jit(solution)/shard_map/activate/pallas_call | solution.py:247
  164.8 13.8 %activate.3.refs_0_ = bf16[2,720,256]{2,1,0:T(8,128)(2,1)S(1)} custom-call(s32[2]{0:T(128)S(1)} %pad_add_fusion.2.place_ref, bf16[1440,128]{1,0:T(8,128)(2,1)S(1)} %collective-permute-done.11.refs_0_, bf16[1440,128]{1,0:T(8,128)(2,1)S(1)} %collective-permute-done.12.refs_1_, bf16[1440,128]{1,0:T(8,128)(2,1)S(1)} %collective-permute-done.19.refs_2_, ...), custom_call_target="tpu_custom_call" | custom-call | flops 4246732800 | bytes 16588800 | tf_op jit(solution)/shard_map/activate/pallas_call | solution.py:247
  178.6 1.5 collective-permute-start.21
  180.7 17.4 %collective-permute-done.21.refs_1_ = bf16[2,720,256]{2,1,0:T(8,128)(2,1)} collective-permute-done((bf16[2,720,256]{2,1,0:T(8,128)(2,1)S(1)}, bf16[2,720,256]{2,1,0:T(8,128)(2,1)}, u32[]{:S(2)}, u32[]{:S(2)}) %collective-permute-start.21) | collective-permute-done | bytes 737312 | tf_op jit(solution)/shard_map/ppermute | solution.py:25
  198.2 2.3 copy-done.1
  200.4 7.7 %combine.3 = (bf16[1440,128]{1,0:T(8,128)(2,1)S(1)}, bf16[1440,128]{1,0:T(8,128)(2,1)S(1)}) custom-call(s32[1]{0:T(128)} %bitcast.t_ref, bf16[2,720,256]{2,1,0:T(8,128)(2,1)S(1)} %activate.3.refs_0_, bf16[2,720,256]{2,1,0:T(8,128)(2,1)} %collective-permute-done.21.refs_1_, f32[2,256]{1,0:T(2,128)S(1)} %get-tuple-element.81.refs_2_, ...), custom_call_target="tpu_custom_call" | custom-call | flops 2123366400 | bytes 8294400 | tf_op jit(solution)/shard_map/combine/pallas_call | solution.py:297
  208.1 2.8 %collective-permute-start.23 = (bf16[1440,128]{1,0:T(8,128)(2,1)S(1)}, bf16[1440,128]{1,0:T(8,128)(2,1)S(1)}, u32[]{:S(2)}, u32[]{:S(2)}) collective-permute-start(bf16[1440,128]{1,0:T(8,128)(2,1)S(1)} %get-tuple-element.72), channel_id=1, source_target_pairs={{0,12},{4,8},{8,4},{12,0},{1,13},{5,9},{9,5},{13,1},{2,14},{6,10},... | collective-permute-start | bytes 1105928 | tf_op jit(solution)/shard_map/ppermute | solution.py:25
  211.4 7.7 %combine.2 = (bf16[1440,128]{1,0:T(8,128)(2,1)S(1)}, bf16[1440,128]{1,0:T(8,128)(2,1)S(1)}) custom-call(s32[1]{0:T(128)} %bitcast.t_ref, bf16[2,720,256]{2,1,0:T(8,128)(2,1)S(1)} %activate.2.refs_0_, bf16[2,720,256]{2,1,0:T(8,128)(2,1)} %collective-permute-done.16.refs_1_, f32[2,256]{1,0:T(2,128)S(1)} %get-tuple-element.80.refs_2_, ...), custom_call_target="tpu_custom_call" | custom-call | flops 2123366400 | bytes 8294400 | tf_op jit(solution)/shard_map/combine/pallas_call | solution.py:297
  219.2 2.5 %collective-permute-start.18 = (bf16[1440,128]{1,0:T(8,128)(2,1)S(1)}, bf16[1440,128]{1,0:T(8,128)(2,1)S(1)}, u32[]{:S(2)}, u32[]{:S(2)}) collective-permute-start(bf16[1440,128]{1,0:T(8,128)(2,1)S(1)} %get-tuple-element.64), channel_id=1, source_target_pairs={{0,8},{4,12},{8,0},{12,4},{1,9},{5,13},{9,1},{13,5},{2,10},{6,14},... | collective-permute-start | bytes 1105928 | tf_op jit(solution)/shard_map/ppermute | solution.py:25
  222.0 1.6 collective-permute-done.22
  223.6 14.2 %collective-permute-done.18 = bf16[1440,128]{1,0:T(8,128)(2,1)S(1)} collective-permute-done((bf16[1440,128]{1,0:T(8,128)(2,1)S(1)}, bf16[1440,128]{1,0:T(8,128)(2,1)S(1)}, u32[]{:S(2)}, u32[]{:S(2)}) %collective-permute-start.18) | collective-permute-done | bytes 368672 | tf_op jit(solution)/shard_map/ppermute | solution.py:25
  237.8 1.0 fusion.3
  (81 shorter events, 5.7 us)
Async XLA Ops:
  0.0 3.4 %copy-start = (bf16[128,2880]{0,1:T(8,128)(2,1)S(1)}, bf16[128,2880]{0,1:T(8,128)(2,1)}, u32[]{:S(2)}) copy-start(bf16[128,2880]{0,1:T(8,128)(2,1)} %param.16) | copy-start | bytes 2211844
  0.0 11.1 %copy-start.7 = (bf16[128,256]{1,0:T(8,128)(2,1)S(1)}, bf16[128,256]{1,0:T(8,128)(2,1)}, u32[]{:S(2)}) copy-start(bf16[128,256]{1,0:T(8,128)(2,1)} %v_ref.3) | copy-start | bytes 196612
  0.0 11.1 %copy-start.9 = (bf16[128,256]{1,0:T(8,128)(2,1)S(1)}, bf16[128,256]{1,0:T(8,128)(2,1)}, u32[]{:S(2)}) copy-start(bf16[128,256]{1,0:T(8,128)(2,1)} %k_ref.3) | copy-start | bytes 196612
  0.0 11.1 %copy-start.15 = (f32[32]{0:T(128)S(1)}, f32[32]{0:T(128)}, u32[]{:S(2)}) copy-start(f32[32]{0:T(128)} %sink_ref.3) | copy-start | bytes 388
  0.0 11.1 %copy-start.4 = (bf16[128,2048]{1,0:T(8,128)(2,1)S(1)}, bf16[128,2048]{1,0:T(8,128)(2,1)}, u32[]{:S(2)}) copy-start(bf16[128,2048]{1,0:T(8,128)(2,1)} %q_ref.2) | copy-start | bytes 1572868
  0.0 54.2 %copy-start.18 = (s32[128,4]{0,1:T(4,128)S(1)}, s32[128,4]{0,1:T(4,128)}, u32[]{:S(2)}) copy-start(s32[128,4]{0,1:T(4,128)} %param.20) | copy-start | bytes 6148
  0.0 54.2 %copy-start.17 = (s32[128,4]{0,1:T(4,128)S(1)}, s32[128,4]{0,1:T(4,128)}, u32[]{:S(2)}) copy-start(s32[128,4]{0,1:T(4,128)} %param.21) | copy-start | bytes 6148
  1.0 5.8 %collective-permute-start = (bf16[128,512]{1,0:T(8,128)(2,1)S(1)}, bf16[128,512]{1,0:T(8,128)(2,1)S(1)}, u32[]{:S(2)}, u32[]{:S(2)}) collective-permute-start(bf16[128,512]{1,0:T(8,128)(2,1)S(1)} %pad_maximum_fusion.1), channel_id=1, source_target_pairs={{0,1},{1,4},{4,5},{5,8},{8,9},{9,12},{12,13},{2,3},{3,6},{6,7},{7,... | collective-permute-start | bytes 393224 | tf_op jit(solution)/shard_map/ppermute | solution.py:21
  6.8 52.9 %copy-start.11 = (bf16[128,512]{1,0:T(8,128)(2,1)}, bf16[128,512]{1,0:T(8,128)(2,1)S(1)}, u32[]{:S(2)}) copy-start(bf16[128,512]{1,0:T(8,128)(2,1)S(1)} %collective-permute-done.earlier_ref) | copy-start | bytes 393220
  6.8 140.9 %collective-permute-start.15 = (bf16[2,720,2880]{2,1,0:T(8,128)(2,1)}, bf16[2,720,2880]{2,1,0:T(8,128)(2,1)}, u32[]{:S(2)}, u32[]{:S(2)}) collective-permute-start(bf16[2,720,2880]{2,1,0:T(8,128)(2,1)} %bitcast.55), channel_id=1, source_target_pairs={{0,1},{1,0},{2,3},{3,2},{4,5},{5,4},{6,7},{7,6},{8,9},{9,8},{10,11... | collective-permute-start | bytes 24883208 | tf_op jit(solution)/shard_map/ppermute | solution.py:25
  9.5 40.1 %collective-permute-start.2 = (bf16[720,1024]{1,0:T(8,128)(2,1)}, bf16[720,1024]{1,0:T(8,128)(2,1)S(1)}, u32[]{:S(2)}, u32[]{:S(2)}) collective-permute-start(bf16[720,1024]{1,0:T(8,128)(2,1)} %dynamic-slice_bitcast_fusion), channel_id=1, source_target_pairs={{0,4},{4,0},{8,12},{12,8},{1,5},{5,1},{9,13},{13,9},{2,6},{6,2},{1... | collective-permute-start | bytes 4423688 | tf_op jit(solution)/shard_map/ppermute | solution.py:25
  14.2 34.5 %collective-permute-start.1 = (bf16[1024,128]{1,0:T(8,128)(2,1)S(1)}, bf16[1024,128]{1,0:T(8,128)(2,1)S(1)}, u32[]{:S(2)}, u32[]{:S(2)}) collective-permute-start(bf16[1024,128]{1,0:T(8,128)(2,1)S(1)} %attention.2.refs_0_), channel_id=1, source_target_pairs={{0,8},{4,12},{8,0},{12,4},{1,9},{5,13},{9,1},{13,5},{2,10},{6,14},... | collective-permute-start | bytes 786440 | tf_op jit(solution)/shard_map/ppermute | solution.py:25
  49.6 41.9 %collective-permute-start.8 = (bf16[720,1024]{1,0:T(8,128)(2,1)S(1)}, bf16[720,1024]{1,0:T(8,128)(2,1)}, u32[]{:S(2)}, u32[]{:S(2)}) collective-permute-start(bf16[720,1024]{1,0:T(8,128)(2,1)S(1)} %collective-permute-done.2.refs_4_), channel_id=1, source_target_pairs={{0,1},{1,0},{2,3},{3,2},{4,5},{5,4},{6,7},{7,6},{8,9},{9,8},{10,11... | collective-permute-start | bytes 4423688 | tf_op jit(solution)/shard_map/ppermute | solution.py:25
  49.8 37.4 %collective-permute-start.4 = (bf16[1440,128]{1,0:T(8,128)(2,1)}, bf16[1440,128]{1,0:T(8,128)(2,1)}, u32[]{:S(2)}, u32[]{:S(2)}) collective-permute-start(bf16[1440,128]{1,0:T(8,128)(2,1)} %dynamic-slice_bitcast_fusion.1), channel_id=1, source_target_pairs={{0,0},{2,10},{4,4},{6,14},{8,8},{10,2},{12,12},{14,6},{1,1},{3,11}... | collective-permute-start | bytes 1105928 | tf_op jit(solution)/shard_map/ppermute | solution.py:351
  54.3 5.5 %collective-permute-start.7 = (f32[8,128]{1,0:T(8,128)S(1)}, f32[8,128]{1,0:T(8,128)S(1)}, u32[]{:S(2)}, u32[]{:S(2)}) collective-permute-start(f32[8,128]{1,0:T(8,128)S(1)} %select_reduce_fusion), channel_id=1, source_target_pairs={{0,12},{4,8},{8,4},{12,0},{1,13},{5,9},{9,5},{13,1},{2,14},{6,10},... | collective-permute-start | bytes 12296 | tf_op jit(solution)/shard_map/ppermute | solution.py:25
  58.2 14.7 %collective-permute-start.6 = (f32[8,128]{1,0:T(8,128)S(1)}, f32[8,128]{1,0:T(8,128)S(1)}, u32[]{:S(2)}, u32[]{:S(2)}) collective-permute-start(f32[8,128]{1,0:T(8,128)S(1)} %select_reduce_fusion), channel_id=1, source_target_pairs={{0,8},{4,12},{8,0},{12,4},{1,9},{5,13},{9,1},{13,5},{2,10},{6,14},... | collective-permute-start | bytes 12296 | tf_op jit(solution)/shard_map/ppermute | solution.py:25
  59.8 16.3 %collective-permute-start.5 = (f32[8,128]{1,0:T(8,128)S(1)}, f32[8,128]{1,0:T(8,128)S(1)}, u32[]{:S(2)}, u32[]{:S(2)}) collective-permute-start(f32[8,128]{1,0:T(8,128)S(1)} %select_reduce_fusion), channel_id=1, source_target_pairs={{0,4},{4,0},{8,12},{12,8},{1,5},{5,1},{9,13},{13,9},{2,6},{6,2},{1... | collective-permute-start | bytes 12296 | tf_op jit(solution)/shard_map/ppermute | solution.py:25
  60.6 0.8 copy-start.8
  61.4 0.8 copy-start.10
  62.2 0.9 copy-start.12
  66.2 10.4 %copy-start.19 = (pred[2]{0:T(512)(128)(4,1)S(1)}, pred[2]{0:T(512)(128)(4,1)}, u32[]{:S(2)}) copy-start(pred[2]{0:T(512)(128)(4,1)} %compare_and_fusion) | copy-start | bytes 10
  72.9 14.3 %collective-permute-start.3 = (bf16[1024,128]{1,0:T(8,128)(2,1)S(1)}, bf16[1024,128]{1,0:T(8,128)(2,1)S(1)}, u32[]{:S(2)}, u32[]{:S(2)}) collective-permute-start(bf16[1024,128]{1,0:T(8,128)(2,1)S(1)} %attention.3.refs_1_), channel_id=1, source_target_pairs={{0,8},{4,12},{8,0},{12,4},{1,9},{5,13},{9,1},{13,5},{2,10},{6,14},... | collective-permute-start | bytes 786440 | tf_op jit(solution)/shard_map/ppermute | solution.py:25
  76.0 104.7 %collective-permute-start.17 = (bf16[1440,1440]{1,0:T(8,128)(2,1)}, bf16[1440,1440]{1,0:T(8,128)(2,1)}, u32[]{:S(2)}, u32[]{:S(2)}) collective-permute-start(bf16[1440,1440]{1,0:T(8,128)(2,1)} %bitcast.52), channel_id=1, source_target_pairs={{0,1},{1,0},{2,3},{3,2},{4,5},{5,4},{6,7},{7,6},{8,9},{9,8},{10,11... | collective-permute-start | bytes 12441608 | tf_op jit(solution)/shard_map/ppermute | solution.py:25
  87.2 1.8 copy-start.3
  90.7 0.7 copy-start.13
  91.5 17.1 %copy-start.16 = (f32[2880]{0:T(1024)S(1)}, f32[2880]{0:T(1024)}, u32[]{:S(2)}) copy-start(f32[2880]{0:T(1024)} %param.17) | copy-start | bytes 34564
  94.0 0.8 copy-start.14
  94.9 22.0 %collective-permute-start.9 = (bf16[1440,128]{1,0:T(8,128)(2,1)S(1)}, bf16[1440,128]{1,0:T(8,128)(2,1)S(1)}, u32[]{:S(2)}, u32[]{:S(2)}) collective-permute-start(bf16[1440,128]{1,0:T(8,128)(2,1)S(1)} %pad_maximum_fusion), channel_id=1, source_target_pairs={{0,2},{2,0},{1,3},{3,1},{4,6},{6,4},{5,7},{7,5},{8,10},{10,8},{9,1... | collective-permute-start | bytes 1105928 | tf_op jit(solution)/shard_map/ppermute | solution.py:25
  118.1 18.4 %collective-permute-start.10 = (bf16[1440,128]{1,0:T(8,128)(2,1)S(1)}, bf16[1440,128]{1,0:T(8,128)(2,1)S(1)}, u32[]{:S(2)}, u32[]{:S(2)}) collective-permute-start(bf16[1440,128]{1,0:T(8,128)(2,1)S(1)} %fusion.2.refs_0_), channel_id=1, source_target_pairs={{0,8},{4,12},{8,0},{12,4},{1,9},{5,13},{9,1},{13,5},{2,10},{6,14},... | collective-permute-start | bytes 1105928 | tf_op jit(solution)/shard_map/ppermute | solution.py:25
  118.2 18.4 %collective-permute-start.11 = (bf16[1440,128]{1,0:T(8,128)(2,1)S(1)}, bf16[1440,128]{1,0:T(8,128)(2,1)S(1)}, u32[]{:S(2)}, u32[]{:S(2)}) collective-permute-start(bf16[1440,128]{1,0:T(8,128)(2,1)S(1)} %fusion.2.refs_0_), channel_id=1, source_target_pairs={{0,4},{4,0},{8,12},{12,8},{1,5},{5,1},{9,13},{13,9},{2,6},{6,2},{1... | collective-permute-start | bytes 1105928 | tf_op jit(solution)/shard_map/ppermute | solution.py:25
  122.1 16.1 %collective-permute-start.13 = (bf16[1440,128]{1,0:T(8,128)(2,1)S(1)}, bf16[1440,128]{1,0:T(8,128)(2,1)S(1)}, u32[]{:S(2)}, u32[]{:S(2)}) collective-permute-start(bf16[1440,128]{1,0:T(8,128)(2,1)S(1)} %fusion.2.refs_0_), channel_id=1, source_target_pairs={{0,2},{2,0},{1,3},{3,1},{4,6},{6,4},{5,7},{7,5},{8,10},{10,8},{9,1... | collective-permute-start | bytes 1105928 | tf_op jit(solution)/shard_map/ppermute | solution.py:25
  136.5 9.2 %collective-permute-start.12 = (bf16[1440,128]{1,0:T(8,128)(2,1)S(1)}, bf16[1440,128]{1,0:T(8,128)(2,1)S(1)}, u32[]{:S(2)}, u32[]{:S(2)}) collective-permute-start(bf16[1440,128]{1,0:T(8,128)(2,1)S(1)} %collective-permute-done.10.refs_1_), channel_id=1, source_target_pairs={{0,4},{4,0},{8,12},{12,8},{1,5},{5,1},{9,13},{13,9},{2,6},{6,2},{1... | collective-permute-start | bytes 1105928 | tf_op jit(solution)/shard_map/ppermute | solution.py:25
  136.6 9.2 %collective-permute-start.14 = (bf16[1440,128]{1,0:T(8,128)(2,1)S(1)}, bf16[1440,128]{1,0:T(8,128)(2,1)S(1)}, u32[]{:S(2)}, u32[]{:S(2)}) collective-permute-start(bf16[1440,128]{1,0:T(8,128)(2,1)S(1)} %collective-permute-done.10.refs_1_), channel_id=1, source_target_pairs={{0,2},{2,0},{1,3},{3,1},{4,6},{6,4},{5,7},{7,5},{8,10},{10,8},{9,1... | collective-permute-start | bytes 1105928 | tf_op jit(solution)/shard_map/ppermute | solution.py:25
  145.7 19.0 %copy-start.5 = (bf16[1440,128]{1,0:T(8,128)(2,1)}, bf16[1440,128]{1,0:T(8,128)(2,1)S(1)}, u32[]{:S(2)}) copy-start(bf16[1440,128]{1,0:T(8,128)(2,1)S(1)} %collective-permute-done.14.refs_3_) | copy-start | bytes 1105924
  145.7 19.0 %collective-permute-start.19 = (bf16[1440,128]{1,0:T(8,128)(2,1)S(1)}, bf16[1440,128]{1,0:T(8,128)(2,1)S(1)}, u32[]{:S(2)}, u32[]{:S(2)}) collective-permute-start(bf16[1440,128]{1,0:T(8,128)(2,1)S(1)} %collective-permute-done.11.refs_0_), channel_id=1, source_target_pairs={{0,2},{2,0},{1,3},{3,1},{4,6},{6,4},{5,7},{7,5},{8,10},{10,8},{9,1... | collective-permute-start | bytes 1105928 | tf_op jit(solution)/shard_map/ppermute | solution.py:25
  147.1 17.6 %collective-permute-start.20 = (bf16[1440,128]{1,0:T(8,128)(2,1)S(1)}, bf16[1440,128]{1,0:T(8,128)(2,1)S(1)}, u32[]{:S(2)}, u32[]{:S(2)}) collective-permute-start(bf16[1440,128]{1,0:T(8,128)(2,1)S(1)} %collective-permute-done.12.refs_1_), channel_id=1, source_target_pairs={{0,2},{2,0},{1,3},{3,1},{4,6},{6,4},{5,7},{7,5},{8,10},{10,8},{9,1... | collective-permute-start | bytes 1105928 | tf_op jit(solution)/shard_map/ppermute | solution.py:25
  147.8 3.4 %copy-start.2 = (bf16[1,2,2880,720]{2,3,1,0:T(8,128)(2,1)S(1)}, bf16[1,2,2880,720]{2,3,1,0:T(8,128)(2,1)}, u32[]{:S(2)}) copy-start(bf16[1,2,2880,720]{2,3,1,0:T(8,128)(2,1)} %param.18) | copy-start | bytes 24883204
  178.6 19.6 %collective-permute-start.21 = (bf16[2,720,256]{2,1,0:T(8,128)(2,1)S(1)}, bf16[2,720,256]{2,1,0:T(8,128)(2,1)}, u32[]{:S(2)}, u32[]{:S(2)}) collective-permute-start(bf16[2,720,256]{2,1,0:T(8,128)(2,1)S(1)} %activate.3.refs_0_), channel_id=1, source_target_pairs={{0,2},{2,0},{1,3},{3,1},{4,6},{6,4},{5,7},{7,5},{8,10},{10,8},{9,1... | collective-permute-start | bytes 2211848 | tf_op jit(solution)/shard_map/ppermute | solution.py:25
  180.0 31.4 %collective-permute-start.16 = (bf16[2,720,256]{2,1,0:T(8,128)(2,1)S(1)}, bf16[2,720,256]{2,1,0:T(8,128)(2,1)}, u32[]{:S(2)}, u32[]{:S(2)}) collective-permute-start(bf16[2,720,256]{2,1,0:T(8,128)(2,1)S(1)} %activate.2.refs_0_), channel_id=1, source_target_pairs={{0,2},{2,0},{1,3},{3,1},{4,6},{6,4},{5,7},{7,5},{8,10},{10,8},{9,1... | collective-permute-start | bytes 2211848 | tf_op jit(solution)/shard_map/ppermute | solution.py:25
  198.2 2.3 copy-start.1
  208.1 13.8 %collective-permute-start.23 = (bf16[1440,128]{1,0:T(8,128)(2,1)S(1)}, bf16[1440,128]{1,0:T(8,128)(2,1)S(1)}, u32[]{:S(2)}, u32[]{:S(2)}) collective-permute-start(bf16[1440,128]{1,0:T(8,128)(2,1)S(1)} %get-tuple-element.72), channel_id=1, source_target_pairs={{0,12},{4,8},{8,4},{12,0},{1,13},{5,9},{9,5},{13,1},{2,14},{6,10},... | collective-permute-start | bytes 1105928 | tf_op jit(solution)/shard_map/ppermute | solution.py:25
  210.9 12.7 %collective-permute-start.22 = (bf16[1440,128]{1,0:T(8,128)(2,1)S(1)}, bf16[1440,128]{1,0:T(8,128)(2,1)S(1)}, u32[]{:S(2)}, u32[]{:S(2)}) collective-permute-start(bf16[1440,128]{1,0:T(8,128)(2,1)S(1)} %get-tuple-element.71), channel_id=1, source_target_pairs={{0,4},{4,0},{8,12},{12,8},{1,5},{5,1},{9,13},{13,9},{2,6},{6,2},{1... | collective-permute-start | bytes 1105928 | tf_op jit(solution)/shard_map/ppermute | solution.py:25
  211.4 10.2 %copy-start.6 = (bf16[1440,128]{1,0:T(8,128)(2,1)S(1)}, bf16[1440,128]{1,0:T(8,128)(2,1)}, u32[]{:S(2)}) copy-start(bf16[1440,128]{1,0:T(8,128)(2,1)} %copy-done.5) | copy-start | bytes 1105924
  219.2 18.6 %collective-permute-start.18 = (bf16[1440,128]{1,0:T(8,128)(2,1)S(1)}, bf16[1440,128]{1,0:T(8,128)(2,1)S(1)}, u32[]{:S(2)}, u32[]{:S(2)}) collective-permute-start(bf16[1440,128]{1,0:T(8,128)(2,1)S(1)} %get-tuple-element.64), channel_id=1, source_target_pairs={{0,8},{4,12},{8,0},{12,4},{1,9},{5,13},{9,1},{13,5},{2,10},{6,14},... | collective-permute-start | bytes 1105928 | tf_op jit(solution)/shard_map/ppermute | solution.py:25

commit v8 on v6

--- a/solution.py
+++ b/solution.py
@@ -51,13 +51,12 @@
     return pltpu.CompilerParams(vmem_limit_bytes=limit)
 
 
-def fetches(sources, held, arrived):
-    return [
-        pltpu.make_async_copy(source, held.at[index], arrived.at[index]) for index, source in enumerate(sources)
-    ]
-
-
-def attention_kernel(first_ref, sink_ref, q_ref, earlier_ref, k_ref, v_ref, out_ref):
+def attention_kernel(first_ref, sink_ref, q_ref, earlier_ref, k_ref, v_ref, routes_ref, *refs):
+    residual_refs, out_refs = refs[: len(refs) // 2], refs[len(refs) // 2 :]
+    width, depth = q_ref.shape[1], residual_refs[0].shape[0]
+    for residual_ref, out_ref in zip(residual_refs, out_refs):
+        out_ref[width : width + depth, :] = residual_ref[...]
+        out_ref[width + depth :, :] = routes_ref[...]
     rows = q_ref.shape[0]
     kv_count = k_ref.shape[1] // HD
     pairs = q_ref.shape[1] // (2 * HD * kv_count)
@@ -107,29 +106,47 @@
                     )
                 )
             result = dot(values[head], jnp.concatenate(weights, axis=1)).astype(jnp.bfloat16)
-            out_ref[start : start + HD, :] = result[:, :rows]
-            out_ref[start + HD : start + 2 * HD, :] = result[:, rows:]
-
-
-def attention(queries, earlier, key_rows, value_rows, sink_logits, first):
+            for out_ref in out_refs:
+                out_ref[start : start + HD, :] = result[:, :rows]
+                out_ref[start + HD : start + 2 * HD, :] = result[:, rows:]
+
+
+def attention(queries, earlier, key_rows, value_rows, sink_logits, first, routes, residuals):
     rows, width = queries.shape
+    height = width + residuals[0].shape[0] + routes.shape[0]
     return pl.pallas_call(
         attention_kernel,
-        out_shape=jax.ShapeDtypeStruct((width, rows), jnp.bfloat16),
-        in_specs=[in_smem(), in_smem()] + in_vmem(4),
-        out_specs=in_vmem(1)[0],
+        out_shape=tuple(jax.ShapeDtypeStruct((height, rows), jnp.bfloat16) for _ in residuals),
+        in_specs=[in_smem(), in_smem()] + in_vmem(5 + len(residuals)),
+        out_specs=tuple(in_vmem(len(residuals))),
         compiler_params=params(),
         cost_estimate=cost(8 * rows * rows * width, 6 * rows * width),
         name="attention",
-    )(first, sink_logits, queries, earlier, key_rows, value_rows)
+    )(first, sink_logits, queries, earlier, key_rows, value_rows, routes, *residuals)
+
+
+def flip(arrays):
+    def kernel(*refs):
+        for i in range(len(arrays)):
+            refs[len(arrays) + i][...] = refs[i][...].T
+
+    return pl.pallas_call(
+        kernel,
+        out_shape=tuple(jax.ShapeDtypeStruct(a.shape[::-1], a.dtype) for a in arrays),
+        in_specs=in_vmem(len(arrays)),
+        out_specs=tuple(in_vmem(len(arrays))),
+        compiler_params=params(FETCH_BYTES),
+        cost_estimate=cost(0, 4 * sum(a.size for a in arrays)),
+        name="flip",
+    )(*arrays)
 
 
 def project(attended, weights, t, s, t_count):
     slots = len(attended)
-    width, rows = attended[0].shape
-    columns = weights[0].shape[0]
+    rows = attended[0].shape[1]
+    columns, depth = weights[0].shape
     shares = len(weights)
-    depth = width // shares
+    width = shares * depth
 
     def kernel(place_ref, *refs):
         attended_refs = refs[:slots]
@@ -164,59 +181,80 @@
     )(jnp.stack([t, s]).astype(jnp.int32), *attended, *weights)
 
 
-def activate(pieces, gain_table, weights, pair, t):
+def activate(pieces, gain_table, weights, pair, t, chosen):
     slots = len(pieces)
-    depth, rows = pieces[0][0].shape
+    height, rows = pieces[0][0].shape
+    depth = D // slots
     lanes = slots * rows
     experts = len(weights)
-    units = weights[0].shape[1]
+    units = weights[0].shape[0] // 2
 
     def kernel(place_ref, *refs):
         piece_refs = refs[: slots * slots]
         table_ref = refs[slots * slots]
         weight_refs = refs[slots * slots + 1 : slots * slots + 1 + experts]
-        out_ref, rows_ref, stage_ref, held_ref, arrived = refs[slots * slots + 1 + experts :]
-        copies = fetches([ref.at[k] for ref in weight_refs for k in range(2)], held_ref, arrived)
+        out_ref, share_ref, rows_ref, stage_ref, routes_ref, held_ref, arrived = refs[
+            slots * slots + 1 + experts :
+        ]
+        copies = [
+            pltpu.make_async_copy(weight_refs[e], held_ref.at[e - 1], arrived.at[e - 1])
+            for e in range(1, experts)
+        ]
         for copy in copies:
             copy.start()
         for m in range(slots):
             for r in range(slots):
                 lane = pl.ds(pl.multiple_of((place_ref[1] ^ r ^ m) * rows, 128), rows)
                 index = place_ref[0] ^ r
-                block = piece_refs[m * slots + r][...]
+                piece_ref = piece_refs[m * slots + r]
+                block = piece_ref[:depth, :]
                 if aligned(depth):
                     rows_ref[pl.ds(pl.multiple_of(index * depth, 16), depth), lane] = block
                 else:
                     stage_ref[index, :, lane] = block
+                if not r:
+                    routes_ref[:, lane] = piece_ref[depth:, :]
         if not aligned(depth):
             for index in range(slots):
                 rows_ref[index * depth : (index + 1) * depth, :] = stage_ref[index]
+        routes = routes_ref[...].astype(jnp.float32)
+        scores = routes[TOP : 2 * TOP] * 256.0 + routes[2 * TOP : 3 * TOP]
+        scores = scores / jnp.sum(scores, axis=0, keepdims=True)
+        for e in range(experts):
+            mine = routes[:TOP] == place_ref[2 + e].astype(jnp.float32)
+            share_ref[e : e + 1, :] = jnp.sum(jnp.where(mine, scores, 0.0), axis=0, keepdims=True)
         plain = rows_ref[...].astype(jnp.float32)
         square = jnp.sum(dot(table_ref[...], (plain * plain).astype(jnp.bfloat16)), axis=0, keepdims=True)
         scale = lax.rsqrt(square / D + 1e-05)
         for e in range(experts):
-            copies[2 * e].wait()
-            gate = dot(held_ref[2 * e], rows_ref[...]) * scale
-            copies[2 * e + 1].wait()
-            up = dot(held_ref[2 * e + 1], rows_ref[...]) * scale
+            if e:
+                copies[e - 1].wait()
+            both = dot(held_ref[e - 1] if e else weight_refs[0][...], rows_ref[...]) * scale
+            gate, up = both[:units], both[units:]
             out_ref[e] = ((up + 1.0) * gate * jax.nn.sigmoid(1.702 * gate)).astype(jnp.bfloat16)
 
     flat = [piece for part in pieces for piece in part]
     return pl.pallas_call(
         kernel,
-        out_shape=jax.ShapeDtypeStruct((experts, units, lanes), jnp.bfloat16),
-        in_specs=[in_smem()] + in_vmem(len(flat) + 1) + [pl.BlockSpec(memory_space=pl.ANY)] * experts,
-        out_specs=in_vmem(1)[0],
+        out_shape=(
+            jax.ShapeDtypeStruct((experts, units, lanes), jnp.bfloat16),
+            jax.ShapeDtypeStruct((experts, lanes), jnp.float32),
+        ),
+        in_specs=[in_smem()]
+        + in_vmem(len(flat) + 2)
+        + [pl.BlockSpec(memory_space=pl.ANY)] * (experts - 1),
+        out_specs=tuple(in_vmem(2)),
         scratch_shapes=[
             pltpu.VMEM((D, lanes), jnp.bfloat16),
             pltpu.VMEM((1, 16, 128) if aligned(depth) else (slots, depth, lanes), jnp.bfloat16),
-            pltpu.VMEM((2 * experts, units, D), jnp.bfloat16),
-            pltpu.SemaphoreType.DMA((2 * experts,)),
+            pltpu.VMEM((height - depth, lanes), jnp.bfloat16),
+            pltpu.VMEM((max(1, experts - 1), 2 * units, D), jnp.bfloat16),
+            pltpu.SemaphoreType.DMA((max(1, experts - 1),)),
         ],
         compiler_params=params(FETCH_BYTES),
         cost_estimate=cost(4 * experts * lanes * D * units, 4 * experts * D * units),
         name="activate",
-    )(jnp.stack([pair, t]).astype(jnp.int32), *flat, gain_table, *weights)
+    )(jnp.stack([pair, t] + chosen).astype(jnp.int32), *flat, gain_table, *weights)
 
 
 def combine(activated, share, weights, t, slots):
@@ -230,7 +268,10 @@
         share_ref = refs[t_count]
         weight_refs = refs[t_count + 1 : t_count + 1 + experts]
         *out_refs, all_ref, stage_ref, held_ref, arrived = refs[t_count + 1 + experts :]
-        copies = fetches(weight_refs, held_ref, arrived)
+        copies = [
+            pltpu.make_async_copy(weight_refs[e], held_ref.at[e - 1], arrived.at[e - 1])
+            for e in range(1, experts)
+        ]
         for copy in copies:
             copy.start()
         for u in range(t_count):
@@ -244,8 +285,10 @@
                 all_ref[:, index * units : (index + 1) * units, :] = stage_ref[index]
         total = 0.0
         for e in range(experts):
-            copies[e].wait()
-            result = dot(held_ref[e], all_ref[e]).astype(jnp.bfloat16).astype(jnp.float32)
+            if e:
+                copies[e - 1].wait()
+            result = dot(held_ref[e - 1] if e else weight_refs[0][...], all_ref[e])
+            result = result.astype(jnp.bfloat16).astype(jnp.float32)
             total = total + share_ref[e : e + 1, :] * result
         for j in range(slots):
             out_refs[j][...] = total[:, j * rows : (j + 1) * rows].astype(jnp.bfloat16)
@@ -253,13 +296,15 @@
     return pl.pallas_call(
         kernel,
         out_shape=tuple(jax.ShapeDtypeStruct((width, rows), jnp.bfloat16) for _ in range(slots)),
-        in_specs=[in_smem()] + in_vmem(t_count + 1) + [pl.BlockSpec(memory_space=pl.ANY)] * experts,
+        in_specs=[in_smem()]
+        + in_vmem(t_count + 2)
+        + [pl.BlockSpec(memory_space=pl.ANY)] * (experts - 1),
         out_specs=tuple(in_vmem(slots)),
         scratch_shapes=[
             pltpu.VMEM((experts, t_count * units, lanes), jnp.bfloat16),
             pltpu.VMEM((1, 1, 16, 128) if aligned(units) else (t_count, experts, units, lanes), jnp.bfloat16),
-            pltpu.VMEM((experts, width, t_count * units), jnp.bfloat16),
-            pltpu.SemaphoreType.DMA((experts,)),
+            pltpu.VMEM((max(1, experts - 1), width, t_count * units), jnp.bfloat16),
+            pltpu.SemaphoreType.DMA((max(1, experts - 1),)),
         ],
         compiler_params=params(FETCH_BYTES),
         cost_estimate=cost(
@@ -294,59 +339,53 @@
     paired = jnp.concatenate([key_rows, value_rows], axis=1)
     earlier = shifted(paired, ("ep", "sub"), 1)
     out_weight = out_weight.T
-    g_count = lax.axis_size("groups")
-    share = s * g_count + lax.axis_index("groups").astype(jnp.int32)
-    depth = out_weight.shape[1] // (s_count * g_count)
-    near = lax.dynamic_slice_in_dim(out_weight, share * depth, depth, 1)
-    residual = picked(residual.T.reshape(slots, group * columns, rows), pair ^ t, 0)
-    earlier, near, residual, expert_in, expert_out = lax.optimization_barrier(
-        (earlier, near, residual, expert_in, expert_out)
+    depth = out_weight.shape[1] // s_count
+    near = lax.dynamic_slice_in_dim(out_weight, s * depth, depth, 1)
+    residual = residual.T.reshape(slots, group * columns, rows)
+    residuals = [picked(residual, pair ^ j, 0) for j in range(slots)]
+    route_rows = jnp.concatenate(
+        [routes.T, route_scores.T // 256, route_scores.T % 256, jnp.zeros((16 - 3 * TOP, rows), jnp.int32)], axis=0
+    ).astype(jnp.bfloat16)
+    earlier, near, residuals, route_rows, expert_in, expert_out = lax.optimization_barrier(
+        (earlier, near, residuals, route_rows, expert_in, expert_out)
     )
 
     near = swapped(near, "ep", 1)
-    near_weights = [near] + [swapped(near, "groups", g) for g in range(1, g_count)]
-
-    route = [
-        (i * t_count + k, (i ^ (group * k)) * t_count + k) for i in range(z_count) for k in range(t_count)
-    ]
-    residual = lax.ppermute(residual, ("ep", "tp"), route)
-
-    expert_in = expert_in[0].transpose(0, 2, 1)
+
+    expert_in = expert_in[0].transpose(0, 2, 1).reshape(-1, D)
     expert_out = expert_out[0]
     experts_in = [expert_in] + [swapped(expert_in, "sub", e) for e in range(1, s_count)]
-    experts_out = [expert_out.T] + [swapped(expert_out, "sub", e).T for e in range(1, s_count)]
+    experts_out = [expert_out] + [swapped(expert_out, "sub", e) for e in range(1, s_count)]
+    chosen = [z * s_count + (s ^ e) for e in range(s_count)]
 
     first = (lax.axis_index(("ep", "sub")) == 0).astype(jnp.int32).reshape(1)
-    attended = attention(queries, earlier, key_rows, value_rows, sink_logits, first)
-
-    expert_count = z_count * s_count
-    route_float = route_scores.T.astype(jnp.float32)
-    mix_share = route_float / jnp.sum(route_float, axis=0, keepdims=True)
-    experts = jnp.arange(expert_count, dtype=jnp.int32)
-    named = routes.T[:, None, :] == experts[None, :, None]
-    table = jnp.sum(jnp.where(named, mix_share[:, None, :], 0.0), axis=0)
-    tables = jnp.stack([table] + [swapped(table, "ep", d) for d in range(1, z_count)])
-    tables = jnp.take(tables, jnp.stack([z * s_count + (s ^ e) for e in range(s_count)]), axis=1)
-    tables = tables.reshape(slots, group, s_count, rows)
-
-    gathered = [attended] + [swapped(attended, "ep", group * j) for j in range(1, slots)]
-    near_weights = near_weights + [
-        swapped(part, "sub", u) for u in range(1, s_count) for part in near_weights
-    ]
-    gathered, residual, tables, experts_out = lax.optimization_barrier((gathered, residual, tables, experts_out))
+    sent = attention(
+        queries, earlier, key_rows, value_rows, sink_logits, first, route_rows, residuals[1:]
+    )
+    gathered = [sent[0]] + [swapped(sent[j - 1], "ep", group * j) for j in range(1, slots)]
+    experts_out, _ = lax.optimization_barrier((experts_out, sent))
+    experts_out = flip(experts_out)
+
+    gathered, near, experts_out = lax.optimization_barrier((gathered, near, experts_out))
+    near_weights = [near] + [swapped(near, "sub", u) for u in range(1, s_count)]
     mine = project(gathered, [out_weight], t, s * 0, t_count)
-    other = project(gathered, near_weights, t, share, t_count)
+    other = project(gathered, near_weights, t, s, t_count)
     first_member = z % group == 0
 
     def ordered(a, b):
         return jnp.concatenate([jnp.where(first_member, a, b), jnp.where(first_member, b, a)], axis=0)
 
-    hidden = ordered(mine[0], other[0]) + residual.astype(jnp.float32)
+    width_in, below = queries.shape[1], group * columns
+    residual_part, kept_routes = residuals[0], route_rows
+    for j in range(1, slots):
+        residual_part = jnp.where(t == j, gathered[j][width_in : width_in + below], residual_part)
+        kept_routes = jnp.where(t == j, gathered[j][width_in + below :], kept_routes)
+    hidden = ordered(mine[0], other[0]) + residual_part.astype(jnp.float32)
     for m in range(1, t_count):
         received = swapped(ordered(mine[1][m - 1], other[1][m - 1]), "tp", m)
         hidden = hidden + received.astype(jnp.float32)
     gain_part = picked(norm_gain.reshape(slots, group * columns), pair, 0)
-    scaled = (hidden * gain_part[:, None]).astype(jnp.bfloat16)
+    scaled = jnp.concatenate([(hidden * gain_part[:, None]).astype(jnp.bfloat16), kept_routes], axis=0)
 
     own = {0: scaled}
     pieces = [own] + [{} for m in range(1, t_count)]
@@ -376,7 +415,7 @@
     for m in range(t_count):
         for r in range(slots):
             here = (pair == m) & ((pair ^ t) == r)
-            total = total + jnp.where(here, pieces[m][group * r].astype(jnp.float32), 0.0)
+            total = total + jnp.where(here, pieces[m][group * r][:width].astype(jnp.float32), 0.0)
     total = total * lax.dynamic_slice_in_dim(inverse_gain, t * width, width, 0)[:, None]
     total = lax.optimization_barrier(total)
 
@@ -385,10 +424,9 @@
         part = [[pieces[m][group * r + p] for r in range(slots)] for m in range(t_count)]
         if p:
             part, after = lax.optimization_barrier((part, after))
-        activated = activate(part, gain_table, experts_in, pair, t)
+        activated, share = activate(part, gain_table, experts_in, pair, t, chosen)
         after = activated
         activated = [activated] + [swapped(activated, "tp", m) for m in range(1, t_count)]
-        share = tables[:, p].transpose(1, 0, 2).reshape(s_count, slots * rows)
         for j, result in enumerate(combine(activated, share, experts_out, t, slots)):
             distance = group * j + p
             result = swapped(result, "ep", distance) if distance else result

time: 219 us -> 194 us (0.89)
  starting transfers between devices: 47.7 us -> 24.6 us
  waiting for transfers between devices: 100 us -> 84.3 us
  Pallas kernels: 46.8 us -> 55.2 us
  local copies, waits for them, and re-layouts: 17.5 us -> 25 us
    ppermute x23 -> x18, starting transfers between devices: 41 us -> 22.2 us  [swapped(): lax.ppermute(block, axis, [(i, i ^ distance) for i in range(lax.axis_size...]
    ppermute x23 -> x18, waiting for transfers between devices: 100 us -> 84.3 us  [swapped(): lax.ppermute(block, axis, [(i, i ^ distance) for i in range(lax.axis_size...]
    unnamed x30 -> x38, local copies, waits for them, and re-layouts: 8.31 us -> 20.2 us
    pallas_call x3 -> x4, Pallas kernels: 29.1 us -> 37.8 us  [the longest x2 26.2 us: activate(): pl.pallas_call(kernel, out_shape=(jax.ShapeDtypeStruct((experts, units, l...]
    optimization_barrier x1 -> x0, local copies, waits for them, and re-layouts: 6.45 us -> none  [local(): lax.optimization_barrier((earlier, near, residual, expert_in, expert_out))]
    ppermute x1 -> x0, starting transfers between devices: 4.41 us -> none  [local(): residual = lax.ppermute(residual, ('ep', 'tp'), route)]
  transfers between devices with their start and end apart: 25 -> 19, of which waited for: 12 -> 10; matrix products, arithmetic and copies ran while one was open for 6% -> 4% of each run, Pallas kernels for 21% -> 28%
where the time goes in v8:
time: 194 us
  waiting for transfers between devices  84.3 us (43%)
  Pallas kernels  55.2 us (28%)
  local copies, waits for them, and re-layouts  25 us (13%)
  starting transfers between devices  24.6 us (13%)
  other arithmetic  4.43 us (2%)
    ppermute x18, waiting for transfers between devices, swapped(): lax.ppermute(block, axis, [(i, i ^ distance) for i in range(lax.axis_size...  84.3 us
    pallas_call x2, Pallas kernels, activate(): pl.pallas_call(kernel, out_shape=(jax.ShapeDtypeStruct((experts, units, l...  26.2 us
    ppermute x18, starting transfers between devices, swapped(): lax.ppermute(block, axis, [(i, i ^ distance) for i in range(lax.axis_size...  22.2 us
    unnamed x38, local copies, waits for them, and re-layouts  20.2 us
    pallas_call x2, Pallas kernels, combine(): pl.pallas_call(kernel, out_shape=tuple((jax.ShapeDtypeStruct((width, rows...  13.4 us
    pallas_call x1, Pallas kernels, flip(): pl.pallas_call(kernel, out_shape=tuple((jax.ShapeDtypeStruct(a.shape[::-1...  6.08 us
    pallas_call x1, Pallas kernels, attention(): pl.pallas_call(attention_kernel, out_shape=tuple((jax.ShapeDtypeStruct((h...  5.58 us
    pallas_call x2, Pallas kernels, project(): pl.pallas_call(kernel, out_shape=(jax.ShapeDtypeStruct((columns, rows), j...  3.93 us
  transfers between devices with their start and end apart: 19, of which 10 were waited for; matrix products, arithmetic and copies ran while one was open for 4% of the time, Pallas kernels for 28%

profile of v8, /device:TPU:0, one launch (start us, length us, event | category | flops | bytes accessed | tf_op | source)
XLA Modules:
  0.0 193.8 jit_solution(1177810660658826587)
XLA Ops:
  0.0 0.9 pad_maximum_fusion.2
  1.0 2.4 %collective-permute-start = (bf16[128,512]{1,0:T(8,128)(2,1)S(1)}, bf16[128,512]{1,0:T(8,128)(2,1)S(1)}, u32[]{:S(2)}, u32[]{:S(2)}) collective-permute-start(bf16[128,512]{1,0:T(8,128)(2,1)S(1)} %pad_maximum_fusion.2), channel_id=1, source_target_pairs={{0,1},{1,4},{4,5},{5,8},{8,9},{9,12},{12,13},{2,3},{3,6},{6,7},{7,... | collective-permute-start | bytes 393224 | tf_op jit(solution)/shard_map/ppermute | solution.py:19
  3.4 0.7 fusion.4
  4.1 0.7 convert_bitcast_fusion
  4.8 1.9 dynamic-slice_bitcast_fusion.1
  6.8 2.6 %dynamic-slice_bitcast_fusion = bf16[720,1024]{1,0:T(8,128)(2,1)} fusion(bf16[2048,720]{0,1:T(8,128)(2,1)} %param.15, s32[]{:T(128)S(6)} %select_n.113), kind=kLoop, calls=%fused_computation | loop fusion | bytes 2949124 | tf_op jit(solution)/shard_map/dynamic_slice | solution.py:343
  9.4 2.7 %collective-permute-start.3 = (bf16[1440,1440]{1,0:T(8,128)(2,1)}, bf16[1440,1440]{1,0:T(8,128)(2,1)}, u32[]{:S(2)}, u32[]{:S(2)}) collective-permute-start(bf16[1440,1440]{1,0:T(8,128)(2,1)} %bitcast.10.refs_0_), channel_id=1, source_target_pairs={{0,1},{1,0},{2,3},{3,2},{4,5},{5,4},{6,7},{7,6},{8,9},{9,8},{10,11... | collective-permute-start | bytes 12441608 | tf_op jit(solution)/shard_map/ppermute | solution.py:23
  12.1 1.6 collective-permute-start.2
  13.7 5.6 %attention.1.refs_0_ = bf16[3504,128]{1,0:T(8,128)(2,1)S(1)} custom-call(s32[1]{0:T(128)} %bitcast.1.first_ref, f32[32]{0:T(128)S(1)} %copy-done.14, bf16[128,2048]{1,0:T(8,128)(2,1)S(1)} %copy-done.9, bf16[128,512]{1,0:T(8,128)(2,1)S(1)} %collective-permute-done.earlier_ref, bf16[128,256]{1,0:T(8,128)(2,1)S(1)} %copy-done.13, ...), custom_call_target="tpu_custom_call" | custom-call | flops 268435456 | bytes 1572864 | tf_op jit(solution)/shard_map/attention/pallas_call | solution.py:117
  19.3 1.5 collective-permute-start.1
  20.8 6.1 %flip.1 = (bf16[1440,1440]{1,0:T(8,128)(2,1)S(1)}, bf16[1440,1440]{1,0:T(8,128)(2,1)S(1)}) custom-call(bf16[1440,1440]{1,0:T(8,128)(2,1)} %bitcast.10.refs_0_, bf16[1440,1440]{1,0:T(8,128)(2,1)} %collective-permute-done.3.refs_1_), custom_call_target="tpu_custom_call" | custom-call | bytes 16588800 | tf_op jit(solution)/shard_map/flip/pallas_call | solution.py:133
  26.9 2.1 %copy-done.2 = bf16[1440,1440]{1,0:T(8,128)(2,1)} copy-done((bf16[1440,1440]{1,0:T(8,128)(2,1)}, bf16[1440,1440]{1,0:T(8,128)(2,1)S(1)}, u32[]{:S(2)}) %copy-start.2) | copy-done | bytes 4147224
  29.0 2.0 %copy-done.5 = bf16[1440,1440]{1,0:T(8,128)(2,1)} copy-done((bf16[1440,1440]{1,0:T(8,128)(2,1)}, bf16[1440,1440]{1,0:T(8,128)(2,1)S(1)}, u32[]{:S(2)}) %copy-start.5) | copy-done | bytes 4147224
  31.0 34.3 %collective-permute-done.1.refs_1_ = bf16[3504,128]{1,0:T(8,128)(2,1)S(1)} collective-permute-done((bf16[3504,128]{1,0:T(8,128)(2,1)S(1)}, bf16[3504,128]{1,0:T(8,128)(2,1)S(1)}, u32[]{:S(2)}, u32[]{:S(2)}) %collective-permute-start.1) | collective-permute-done | bytes 897056 | tf_op jit(solution)/shard_map/ppermute | solution.py:23
  65.3 0.9 collective-permute-done.2.refs_2_
  66.5 1.8 copy-done.8
  68.3 1.5 project.2
  69.9 2.4 %project.3 = (f32[720,128]{1,0:T(8,128)S(1)}, bf16[1,720,128]{2,1,0:T(8,128)(2,1)S(1)}) custom-call(s32[2]{0:T(128)S(1)} %pad_add_fusion.1.place_ref, bf16[3504,128]{1,0:T(8,128)(2,1)S(1)} %attention.1.refs_0_, bf16[3504,128]{1,0:T(8,128)(2,1)S(1)} %collective-permute-done.1.refs_1_, bf16[720,1024]{1,0:T(8,128)(2,1)S(1)} %collective-permute-done.2.refs_2_, ...), custom_call_target="tpu_custom_call" | custom-call | flops 754974720 | bytes 2949120 | tf_op jit(solution)/shard_map/project/pallas_call | solution.py:169
  72.4 1.6 collective-permute-start.5
  74.0 9.5 %collective-permute-done.5 = bf16[1440,128]{1,0:T(8,128)(2,1)S(1)} collective-permute-done((bf16[1440,128]{1,0:T(8,128)(2,1)S(1)}, bf16[1440,128]{1,0:T(8,128)(2,1)S(1)}, u32[]{:S(2)}, u32[]{:S(2)}) %collective-permute-start.5) | collective-permute-done | bytes 368672 | tf_op jit(solution)/shard_map/ppermute | solution.py:23
  83.8 0.7 copy-done.15
  84.5 2.5 %collective-permute-start.6 = (bf16[1456,128]{1,0:T(8,128)(2,1)S(1)}, bf16[1456,128]{1,0:T(8,128)(2,1)S(1)}, u32[]{:S(2)}, u32[]{:S(2)}) collective-permute-start(bf16[1456,128]{1,0:T(8,128)(2,1)S(1)} %pad_maximum_fusion.refs_0_), channel_id=1, source_target_pairs={{0,8},{4,12},{8,0},{12,4},{1,9},{5,13},{9,1},{13,5},{2,10},{6,14},... | collective-permute-start | bytes 1118216 | tf_op jit(solution)/shard_map/ppermute | solution.py:23
  87.6 1.5 collective-permute-start.9
  89.1 14.7 %collective-permute-done.6.refs_1_ = bf16[1456,128]{1,0:T(8,128)(2,1)S(1)} collective-permute-done((bf16[1456,128]{1,0:T(8,128)(2,1)S(1)}, bf16[1456,128]{1,0:T(8,128)(2,1)S(1)}, u32[]{:S(2)}, u32[]{:S(2)}) %collective-permute-start.6) | collective-permute-done | bytes 372768 | tf_op jit(solution)/shard_map/ppermute | solution.py:23
  103.8 1.5 collective-permute-start.10
  105.5 7.8 %collective-permute-done.10.refs_3_ = bf16[1456,128]{1,0:T(8,128)(2,1)S(1)} collective-permute-done((bf16[1456,128]{1,0:T(8,128)(2,1)S(1)}, bf16[1456,128]{1,0:T(8,128)(2,1)S(1)}, u32[]{:S(2)}, u32[]{:S(2)}) %collective-permute-start.10) | collective-permute-done | bytes 372768 | tf_op jit(solution)/shard_map/ppermute | solution.py:23
  113.2 1.2 collective-permute-done.8.refs_1_
  115.0 1.5 collective-permute-start.15
  116.4 3.4 %copy-done = bf16[1,2,2880,720]{2,3,1,0:T(8,128)(2,1)S(1)} copy-done((bf16[1,2,2880,720]{2,3,1,0:T(8,128)(2,1)S(1)}, bf16[1,2,2880,720]{2,3,1,0:T(8,128)(2,1)}, u32[]{:S(2)}) %copy-start) | copy-done | bytes 8294424
  119.9 13.1 %activate.2 = (bf16[2,720,256]{2,1,0:T(8,128)(2,1)S(1)}, f32[2,256]{1,0:T(2,128)S(1)}) custom-call(s32[4]{0:T(128)S(1)} %pad_add_fusion.2.place_ref, bf16[1456,128]{1,0:T(8,128)(2,1)S(1)} %pad_maximum_fusion.refs_0_, bf16[1456,128]{1,0:T(8,128)(2,1)S(1)} %collective-permute-done.6.refs_1_, bf16[1456,128]{1,0:T(8,128)(2,1)S(1)} %collective-permute-done.9.refs_2_, ...), custom_call_target="tpu_custom_call" | custom-call | flops 4246732800 | bytes 16588800 | tf_op jit(solution)/shard_map/activate/pallas_call | solution.py:237
  133.0 0.6 collective-permute-start.12
  133.7 1.0 copy-done.11
  134.6 13.0 %activate.3 = (bf16[2,720,256]{2,1,0:T(8,128)(2,1)S(1)}, f32[2,256]{1,0:T(2,128)S(1)}) custom-call(s32[4]{0:T(128)S(1)} %pad_add_fusion.2.place_ref, bf16[1456,128]{1,0:T(8,128)(2,1)S(1)} %collective-permute-done.7.refs_0_, bf16[1456,128]{1,0:T(8,128)(2,1)S(1)} %copy-done.11, bf16[1456,128]{1,0:T(8,128)(2,1)S(1)} %collective-permute-done.14.refs_2_, ...), custom_call_target="tpu_custom_call" | custom-call | flops 4246732800 | bytes 16588800 | tf_op jit(solution)/shard_map/activate/pallas_call | solution.py:237
  147.7 1.5 collective-permute-start.16
  149.3 0.7 collective-permute-done.12.refs_1_
  150.0 2.3 %copy-done.3 = bf16[1440,1440]{1,0:T(8,128)(2,1)S(1)} copy-done((bf16[1440,1440]{1,0:T(8,128)(2,1)S(1)}, bf16[1440,1440]{1,0:T(8,128)(2,1)}, u32[]{:S(2)}) %copy-start.3) | copy-done | bytes 4147224
  152.3 2.3 %copy-done.6 = bf16[1440,1440]{1,0:T(8,128)(2,1)S(1)} copy-done((bf16[1440,1440]{1,0:T(8,128)(2,1)S(1)}, bf16[1440,1440]{1,0:T(8,128)(2,1)}, u32[]{:S(2)}) %copy-start.6) | copy-done | bytes 4147224
  154.5 6.7 %combine.2 = (bf16[1440,128]{1,0:T(8,128)(2,1)S(1)}, bf16[1440,128]{1,0:T(8,128)(2,1)S(1)}) custom-call(s32[1]{0:T(128)} %bitcast.t_ref, bf16[2,720,256]{2,1,0:T(8,128)(2,1)S(1)} %get-tuple-element.61.refs_0_, bf16[2,720,256]{2,1,0:T(8,128)(2,1)} %collective-permute-done.12.refs_1_, f32[2,256]{1,0:T(2,128)S(1)} %get-tuple-element.62.refs_2_, ...), custom_call_target="tpu_custom_call" | custom-call | flops 2123366400 | bytes 8294400 | tf_op jit(solution)/shard_map/combine/pallas_call | solution.py:296
  161.2 1.7 collective-permute-start.13
  162.9 1.5 collective-permute-done.16.refs_1_
  164.5 2.3 %copy-done.4 = bf16[1440,1440]{1,0:T(8,128)(2,1)S(1)} copy-done((bf16[1440,1440]{1,0:T(8,128)(2,1)S(1)}, bf16[1440,1440]{1,0:T(8,128)(2,1)}, u32[]{:S(2)}) %copy-start.4) | copy-done | bytes 4147224
  166.7 2.3 %copy-done.7 = bf16[1440,1440]{1,0:T(8,128)(2,1)S(1)} copy-done((bf16[1440,1440]{1,0:T(8,128)(2,1)S(1)}, bf16[1440,1440]{1,0:T(8,128)(2,1)}, u32[]{:S(2)}) %copy-start.7) | copy-done | bytes 4147224
  169.0 6.7 %combine.3 = (bf16[1440,128]{1,0:T(8,128)(2,1)S(1)}, bf16[1440,128]{1,0:T(8,128)(2,1)S(1)}) custom-call(s32[1]{0:T(128)} %bitcast.t_ref, bf16[2,720,256]{2,1,0:T(8,128)(2,1)S(1)} %get-tuple-element.73.refs_0_, bf16[2,720,256]{2,1,0:T(8,128)(2,1)} %collective-permute-done.16.refs_1_, f32[2,256]{1,0:T(2,128)S(1)} %get-tuple-element.74.refs_2_, ...), custom_call_target="tpu_custom_call" | custom-call | flops 2123366400 | bytes 8294400 | tf_op jit(solution)/shard_map/combine/pallas_call | solution.py:296
  175.7 0.6 collective-permute-start.17
  176.3 2.5 %collective-permute-start.18 = (bf16[1440,128]{1,0:T(8,128)(2,1)S(1)}, bf16[1440,128]{1,0:T(8,128)(2,1)S(1)}, u32[]{:S(2)}, u32[]{:S(2)}) collective-permute-start(bf16[1440,128]{1,0:T(8,128)(2,1)S(1)} %get-tuple-element.76), channel_id=1, source_target_pairs={{0,12},{4,8},{8,4},{12,0},{1,13},{5,9},{9,5},{13,1},{2,14},{6,10},... | collective-permute-start | bytes 1105928 | tf_op jit(solution)/shard_map/ppermute | solution.py:23
  179.2 7.8 %collective-permute-done.17 = bf16[1440,128]{1,0:T(8,128)(2,1)S(1)} collective-permute-done((bf16[1440,128]{1,0:T(8,128)(2,1)S(1)}, bf16[1440,128]{1,0:T(8,128)(2,1)S(1)}, u32[]{:S(2)}, u32[]{:S(2)}) %collective-permute-start.17) | collective-permute-done | bytes 368672 | tf_op jit(solution)/shard_map/ppermute | solution.py:23
  187.0 5.9 %collective-permute-done.18 = bf16[1440,128]{1,0:T(8,128)(2,1)S(1)} collective-permute-done((bf16[1440,128]{1,0:T(8,128)(2,1)S(1)}, bf16[1440,128]{1,0:T(8,128)(2,1)S(1)}, u32[]{:S(2)}, u32[]{:S(2)}) %collective-permute-start.18) | collective-permute-done | bytes 368672 | tf_op jit(solution)/shard_map/ppermute | solution.py:23
  192.8 1.0 fusion.3
  (64 shorter events, 2.5 us)
Async XLA Ops:
  0.0 13.7 %copy-start.13 = (bf16[128,256]{1,0:T(8,128)(2,1)S(1)}, bf16[128,256]{1,0:T(8,128)(2,1)}, u32[]{:S(2)}) copy-start(bf16[128,256]{1,0:T(8,128)(2,1)} %k_ref.1) | copy-start | bytes 196612
  0.0 13.7 %copy-start.12 = (bf16[128,256]{1,0:T(8,128)(2,1)S(1)}, bf16[128,256]{1,0:T(8,128)(2,1)}, u32[]{:S(2)}) copy-start(bf16[128,256]{1,0:T(8,128)(2,1)} %v_ref.1) | copy-start | bytes 196612
  0.0 13.7 %copy-start.9 = (bf16[128,2048]{1,0:T(8,128)(2,1)S(1)}, bf16[128,2048]{1,0:T(8,128)(2,1)}, u32[]{:S(2)}) copy-start(bf16[128,2048]{1,0:T(8,128)(2,1)} %q_ref.1) | copy-start | bytes 1572868
  0.0 13.7 %copy-start.14 = (f32[32]{0:T(128)S(1)}, f32[32]{0:T(128)}, u32[]{:S(2)}) copy-start(f32[32]{0:T(128)} %sink_ref.1) | copy-start | bytes 388
  1.0 8.5 %collective-permute-start = (bf16[128,512]{1,0:T(8,128)(2,1)S(1)}, bf16[128,512]{1,0:T(8,128)(2,1)S(1)}, u32[]{:S(2)}, u32[]{:S(2)}) collective-permute-start(bf16[128,512]{1,0:T(8,128)(2,1)S(1)} %pad_maximum_fusion.2), channel_id=1, source_target_pairs={{0,1},{1,4},{4,5},{5,8},{8,9},{9,12},{12,13},{2,3},{3,6},{6,7},{7,... | collective-permute-start | bytes 393224 | tf_op jit(solution)/shard_map/ppermute | solution.py:19
  9.4 11.4 %collective-permute-start.3 = (bf16[1440,1440]{1,0:T(8,128)(2,1)}, bf16[1440,1440]{1,0:T(8,128)(2,1)}, u32[]{:S(2)}, u32[]{:S(2)}) collective-permute-start(bf16[1440,1440]{1,0:T(8,128)(2,1)} %bitcast.10.refs_0_), channel_id=1, source_target_pairs={{0,1},{1,0},{2,3},{3,2},{4,5},{5,4},{6,7},{7,6},{8,9},{9,8},{10,11... | collective-permute-start | bytes 12441608 | tf_op jit(solution)/shard_map/ppermute | solution.py:23
  12.1 104.3 %collective-permute-start.11 = (bf16[1440,2880]{1,0:T(8,128)(2,1)}, bf16[1440,2880]{1,0:T(8,128)(2,1)}, u32[]{:S(2)}, u32[]{:S(2)}) collective-permute-start(bf16[1440,2880]{1,0:T(8,128)(2,1)} %bitcast.52), channel_id=1, source_target_pairs={{0,1},{1,0},{2,3},{3,2},{4,5},{5,4},{6,7},{7,6},{8,9},{9,8},{10,11... | collective-permute-start | bytes 24883208 | tf_op jit(solution)/shard_map/ppermute | solution.py:23
  12.1 54.1 %collective-permute-start.2 = (bf16[720,1024]{1,0:T(8,128)(2,1)}, bf16[720,1024]{1,0:T(8,128)(2,1)S(1)}, u32[]{:S(2)}, u32[]{:S(2)}) collective-permute-start(bf16[720,1024]{1,0:T(8,128)(2,1)} %dynamic-slice_bitcast_fusion), channel_id=1, source_target_pairs={{0,4},{4,0},{8,12},{12,8},{1,5},{5,1},{9,13},{13,9},{2,6},{6,2},{1... | collective-permute-start | bytes 4423688 | tf_op jit(solution)/shard_map/ppermute | solution.py:23
  19.3 47.0 %copy-start.18 = (f32[2880]{0:T(1024)S(1)}, f32[2880]{0:T(1024)}, u32[]{:S(2)}) copy-start(f32[2880]{0:T(1024)} %param.17) | copy-start | bytes 34564
  19.3 46.0 %collective-permute-start.1 = (bf16[3504,128]{1,0:T(8,128)(2,1)S(1)}, bf16[3504,128]{1,0:T(8,128)(2,1)S(1)}, u32[]{:S(2)}, u32[]{:S(2)}) collective-permute-start(bf16[3504,128]{1,0:T(8,128)(2,1)S(1)} %attention.1.refs_0_), channel_id=1, source_target_pairs={{0,8},{4,12},{8,0},{12,4},{1,9},{5,13},{9,1},{13,5},{2,10},{6,14},... | collective-permute-start | bytes 2691080 | tf_op jit(solution)/shard_map/ppermute | solution.py:23
  26.9 2.1 %copy-start.2 = (bf16[1440,1440]{1,0:T(8,128)(2,1)}, bf16[1440,1440]{1,0:T(8,128)(2,1)S(1)}, u32[]{:S(2)}) copy-start(bf16[1440,1440]{1,0:T(8,128)(2,1)S(1)} %get-tuple-element.63.refs_3_) | copy-start | bytes 12441604
  29.0 2.0 %copy-start.5 = (bf16[1440,1440]{1,0:T(8,128)(2,1)}, bf16[1440,1440]{1,0:T(8,128)(2,1)S(1)}, u32[]{:S(2)}) copy-start(bf16[1440,1440]{1,0:T(8,128)(2,1)S(1)} %get-tuple-element.64.refs_4_) | copy-start | bytes 12441604
  66.2 3.6 %collective-permute-start.4 = (bf16[720,1024]{1,0:T(8,128)(2,1)S(1)}, bf16[720,1024]{1,0:T(8,128)(2,1)}, u32[]{:S(2)}, u32[]{:S(2)}) collective-permute-start(bf16[720,1024]{1,0:T(8,128)(2,1)S(1)} %collective-permute-done.2.refs_2_), channel_id=1, source_target_pairs={{0,1},{1,0},{2,3},{3,2},{4,5},{5,4},{6,7},{7,6},{8,9},{9,8},{10,11... | collective-permute-start | bytes 4423688 | tf_op jit(solution)/shard_map/ppermute | solution.py:23
  66.5 1.8 copy-start.8
  69.9 13.6 %copy-start.17 = (bf16[1440,128]{1,0:T(8,128)(2,1)S(1)}, bf16[1440,128]{1,0:T(8,128)(2,1)}, u32[]{:S(2)}) copy-start(bf16[1440,128]{1,0:T(8,128)(2,1)} %get-tuple-element.55) | copy-start | bytes 1105924
  72.4 11.1 %collective-permute-start.5 = (bf16[1440,128]{1,0:T(8,128)(2,1)S(1)}, bf16[1440,128]{1,0:T(8,128)(2,1)S(1)}, u32[]{:S(2)}, u32[]{:S(2)}) collective-permute-start(bf16[1440,128]{1,0:T(8,128)(2,1)S(1)} %pad_maximum_fusion.1), channel_id=1, source_target_pairs={{0,2},{2,0},{1,3},{3,1},{4,6},{6,4},{5,7},{7,5},{8,10},{10,8},{9,1... | collective-permute-start | bytes 1105928 | tf_op jit(solution)/shard_map/ppermute | solution.py:23
  83.8 0.7 copy-start.15
  84.5 19.3 %collective-permute-start.6 = (bf16[1456,128]{1,0:T(8,128)(2,1)S(1)}, bf16[1456,128]{1,0:T(8,128)(2,1)S(1)}, u32[]{:S(2)}, u32[]{:S(2)}) collective-permute-start(bf16[1456,128]{1,0:T(8,128)(2,1)S(1)} %pad_maximum_fusion.refs_0_), channel_id=1, source_target_pairs={{0,8},{4,12},{8,0},{12,4},{1,9},{5,13},{9,1},{13,5},{2,10},{6,14},... | collective-permute-start | bytes 1118216 | tf_op jit(solution)/shard_map/ppermute | solution.py:23
  87.2 18.3 %collective-permute-start.7 = (bf16[1456,128]{1,0:T(8,128)(2,1)S(1)}, bf16[1456,128]{1,0:T(8,128)(2,1)S(1)}, u32[]{:S(2)}, u32[]{:S(2)}) collective-permute-start(bf16[1456,128]{1,0:T(8,128)(2,1)S(1)} %pad_maximum_fusion.refs_0_), channel_id=1, source_target_pairs={{0,4},{4,0},{8,12},{12,8},{1,5},{5,1},{9,13},{13,9},{2,6},{6,2},{1... | collective-permute-start | bytes 1118216 | tf_op jit(solution)/shard_map/ppermute | solution.py:23
  87.6 17.9 %collective-permute-start.9 = (bf16[1456,128]{1,0:T(8,128)(2,1)S(1)}, bf16[1456,128]{1,0:T(8,128)(2,1)S(1)}, u32[]{:S(2)}, u32[]{:S(2)}) collective-permute-start(bf16[1456,128]{1,0:T(8,128)(2,1)S(1)} %pad_maximum_fusion.refs_0_), channel_id=1, source_target_pairs={{0,2},{2,0},{1,3},{3,1},{4,6},{6,4},{5,7},{7,5},{8,10},{10,8},{9,1... | collective-permute-start | bytes 1118216 | tf_op jit(solution)/shard_map/ppermute | solution.py:23
  103.8 9.4 %collective-permute-start.10 = (bf16[1456,128]{1,0:T(8,128)(2,1)S(1)}, bf16[1456,128]{1,0:T(8,128)(2,1)S(1)}, u32[]{:S(2)}, u32[]{:S(2)}) collective-permute-start(bf16[1456,128]{1,0:T(8,128)(2,1)S(1)} %collective-permute-done.6.refs_1_), channel_id=1, source_target_pairs={{0,2},{2,0},{1,3},{3,1},{4,6},{6,4},{5,7},{7,5},{8,10},{10,8},{9,1... | collective-permute-start | bytes 1118216 | tf_op jit(solution)/shard_map/ppermute | solution.py:23
  105.3 9.1 %collective-permute-start.8 = (bf16[1456,128]{1,0:T(8,128)(2,1)S(1)}, bf16[1456,128]{1,0:T(8,128)(2,1)S(1)}, u32[]{:S(2)}, u32[]{:S(2)}) collective-permute-start(bf16[1456,128]{1,0:T(8,128)(2,1)S(1)} %collective-permute-done.6.refs_1_), channel_id=1, source_target_pairs={{0,4},{4,0},{8,12},{12,8},{1,5},{5,1},{9,13},{13,9},{2,6},{6,2},{1... | collective-permute-start | bytes 1118216 | tf_op jit(solution)/shard_map/ppermute | solution.py:23
  114.4 18.6 %copy-start.10 = (bf16[1456,128]{1,0:T(8,128)(2,1)}, bf16[1456,128]{1,0:T(8,128)(2,1)S(1)}, u32[]{:S(2)}) copy-start(bf16[1456,128]{1,0:T(8,128)(2,1)S(1)} %collective-permute-done.8.refs_1_) | copy-start | bytes 1118212
  114.4 19.2 %collective-permute-start.14 = (bf16[1456,128]{1,0:T(8,128)(2,1)S(1)}, bf16[1456,128]{1,0:T(8,128)(2,1)S(1)}, u32[]{:S(2)}, u32[]{:S(2)}) collective-permute-start(bf16[1456,128]{1,0:T(8,128)(2,1)S(1)} %collective-permute-done.7.refs_0_), channel_id=1, source_target_pairs={{0,2},{2,0},{1,3},{3,1},{4,6},{6,4},{5,7},{7,5},{8,10},{10,8},{9,1... | collective-permute-start | bytes 1118216 | tf_op jit(solution)/shard_map/ppermute | solution.py:23
  115.0 18.7 %collective-permute-start.15 = (bf16[1456,128]{1,0:T(8,128)(2,1)S(1)}, bf16[1456,128]{1,0:T(8,128)(2,1)S(1)}, u32[]{:S(2)}, u32[]{:S(2)}) collective-permute-start(bf16[1456,128]{1,0:T(8,128)(2,1)S(1)} %collective-permute-done.8.refs_1_), channel_id=1, source_target_pairs={{0,2},{2,0},{1,3},{3,1},{4,6},{6,4},{5,7},{7,5},{8,10},{10,8},{9,1... | collective-permute-start | bytes 1118216 | tf_op jit(solution)/shard_map/ppermute | solution.py:23
  116.4 3.4 %copy-start = (bf16[1,2,2880,720]{2,3,1,0:T(8,128)(2,1)S(1)}, bf16[1,2,2880,720]{2,3,1,0:T(8,128)(2,1)}, u32[]{:S(2)}) copy-start(bf16[1,2,2880,720]{2,3,1,0:T(8,128)(2,1)} %param.18) | copy-start | bytes 24883204
  119.9 13.8 %copy-start.1 = (bf16[1,2,2880,720]{2,3,1,0:T(8,128)(2,1)S(1)}, bf16[1,2,2880,720]{2,3,1,0:T(8,128)(2,1)}, u32[]{:S(2)}) copy-start(bf16[1,2,2880,720]{2,3,1,0:T(8,128)(2,1)} %param.18) | copy-start | bytes 24883204
  133.0 17.0 %collective-permute-start.12 = (bf16[2,720,256]{2,1,0:T(8,128)(2,1)S(1)}, bf16[2,720,256]{2,1,0:T(8,128)(2,1)}, u32[]{:S(2)}, u32[]{:S(2)}) collective-permute-start(bf16[2,720,256]{2,1,0:T(8,128)(2,1)S(1)} %get-tuple-element.61.refs_0_), channel_id=1, source_target_pairs={{0,2},{2,0},{1,3},{3,1},{4,6},{6,4},{5,7},{7,5},{8,10},{10,8},{9,1... | collective-permute-start | bytes 2211848 | tf_op jit(solution)/shard_map/ppermute | solution.py:23
  133.6 1.0 copy-start.11
  147.7 16.8 %collective-permute-start.16 = (bf16[2,720,256]{2,1,0:T(8,128)(2,1)S(1)}, bf16[2,720,256]{2,1,0:T(8,128)(2,1)}, u32[]{:S(2)}, u32[]{:S(2)}) collective-permute-start(bf16[2,720,256]{2,1,0:T(8,128)(2,1)S(1)} %get-tuple-element.73.refs_0_), channel_id=1, source_target_pairs={{0,2},{2,0},{1,3},{3,1},{4,6},{6,4},{5,7},{7,5},{8,10},{10,8},{9,1... | collective-permute-start | bytes 2211848 | tf_op jit(solution)/shard_map/ppermute | solution.py:23
  150.0 2.3 %copy-start.3 = (bf16[1440,1440]{1,0:T(8,128)(2,1)S(1)}, bf16[1440,1440]{1,0:T(8,128)(2,1)}, u32[]{:S(2)}) copy-start(bf16[1440,1440]{1,0:T(8,128)(2,1)} %copy-done.2) | copy-start | bytes 12441604
  152.3 2.3 %copy-start.6 = (bf16[1440,1440]{1,0:T(8,128)(2,1)S(1)}, bf16[1440,1440]{1,0:T(8,128)(2,1)}, u32[]{:S(2)}) copy-start(bf16[1440,1440]{1,0:T(8,128)(2,1)} %copy-done.5) | copy-start | bytes 12441604
  161.2 17.9 %collective-permute-start.13 = (bf16[1440,128]{1,0:T(8,128)(2,1)S(1)}, bf16[1440,128]{1,0:T(8,128)(2,1)S(1)}, u32[]{:S(2)}, u32[]{:S(2)}) collective-permute-start(bf16[1440,128]{1,0:T(8,128)(2,1)S(1)} %get-tuple-element.66), channel_id=1, source_target_pairs={{0,8},{4,12},{8,0},{12,4},{1,9},{5,13},{9,1},{13,5},{2,10},{6,14},... | collective-permute-start | bytes 1105928 | tf_op jit(solution)/shard_map/ppermute | solution.py:23
  164.5 2.3 %copy-start.4 = (bf16[1440,1440]{1,0:T(8,128)(2,1)S(1)}, bf16[1440,1440]{1,0:T(8,128)(2,1)}, u32[]{:S(2)}) copy-start(bf16[1440,1440]{1,0:T(8,128)(2,1)} %copy-done.2) | copy-start | bytes 12441604
  166.7 2.3 %copy-start.7 = (bf16[1440,1440]{1,0:T(8,128)(2,1)S(1)}, bf16[1440,1440]{1,0:T(8,128)(2,1)}, u32[]{:S(2)}) copy-start(bf16[1440,1440]{1,0:T(8,128)(2,1)} %copy-done.5) | copy-start | bytes 12441604
  169.0 9.9 %copy-start.16 = (bf16[1440,128]{1,0:T(8,128)(2,1)S(1)}, bf16[1440,128]{1,0:T(8,128)(2,1)}, u32[]{:S(2)}) copy-start(bf16[1440,128]{1,0:T(8,128)(2,1)} %copy-done.15) | copy-start | bytes 1105924
  175.7 11.3 %collective-permute-start.17 = (bf16[1440,128]{1,0:T(8,128)(2,1)S(1)}, bf16[1440,128]{1,0:T(8,128)(2,1)S(1)}, u32[]{:S(2)}, u32[]{:S(2)}) collective-permute-start(bf16[1440,128]{1,0:T(8,128)(2,1)S(1)} %get-tuple-element.75), channel_id=1, source_target_pairs={{0,4},{4,0},{8,12},{12,8},{1,5},{5,1},{9,13},{13,9},{2,6},{6,2},{1... | collective-permute-start | bytes 1105928 | tf_op jit(solution)/shard_map/ppermute | solution.py:23
  176.3 16.5 %collective-permute-start.18 = (bf16[1440,128]{1,0:T(8,128)(2,1)S(1)}, bf16[1440,128]{1,0:T(8,128)(2,1)S(1)}, u32[]{:S(2)}, u32[]{:S(2)}) collective-permute-start(bf16[1440,128]{1,0:T(8,128)(2,1)S(1)} %get-tuple-element.76), channel_id=1, source_target_pairs={{0,12},{4,8},{8,4},{12,0},{1,13},{5,9},{9,5},{13,1},{2,14},{6,10},... | collective-permute-start | bytes 1105928 | tf_op jit(solution)/shard_map/ppermute | solution.py:23

commit v9 on v8

--- a/solution.py
+++ b/solution.py
@@ -10,7 +10,6 @@
 WIN = 128
 TOP = 4
 VMEM_BYTES = 16 * 1024 * 1024
-FETCH_BYTES = 32 * 1024 * 1024
 
 
 def shifted(block, axis, distance):
@@ -47,23 +46,27 @@
     return size % 16 == 0
 
 
-def params(limit=VMEM_BYTES):
-    return pltpu.CompilerParams(vmem_limit_bytes=limit)
-
-
-def attention_kernel(first_ref, sink_ref, q_ref, earlier_ref, k_ref, v_ref, routes_ref, *refs):
-    residual_refs, out_refs = refs[: len(refs) // 2], refs[len(refs) // 2 :]
-    width, depth = q_ref.shape[1], residual_refs[0].shape[0]
-    for residual_ref, out_ref in zip(residual_refs, out_refs):
-        out_ref[width : width + depth, :] = residual_ref[...]
-        out_ref[width + depth :, :] = routes_ref[...]
+def params():
+    return pltpu.CompilerParams(vmem_limit_bytes=VMEM_BYTES)
+
+
+def attention_kernel(
+    place_ref, sink_ref, q_ref, earlier_ref, k_ref, v_ref, residual_ref, routes_ref, scores_ref, *out_refs
+):
+    width, depth = q_ref.shape[1], residual_ref.shape[1]
+    numbers = [routes_ref[...], scores_ref[...] // 256, scores_ref[...] % 256]
+    numbers.append(jnp.zeros((out_refs[0].shape[0] - width - depth - 3 * TOP, q_ref.shape[0]), jnp.int32))
+    numbers = jnp.concatenate(numbers, axis=0).astype(jnp.float32).astype(jnp.bfloat16)
+    for j, out_ref in enumerate(out_refs):
+        out_ref[width : width + depth, :] = residual_ref[place_ref[1] ^ (j + 1)]
+        out_ref[width + depth :, :] = numbers
     rows = q_ref.shape[0]
     kv_count = k_ref.shape[1] // HD
     pairs = q_ref.shape[1] // (2 * HD * kv_count)
     key = lax.broadcasted_iota(jnp.int32, (rows, rows), 0)
     query = lax.broadcasted_iota(jnp.int32, (rows, rows), 1)
     before = key > query
-    shut = before & (first_ref[0] == 1)
+    shut = before & (place_ref[0] == 1)
     blank = jnp.zeros((2 * rows, HD), jnp.bfloat16)
     values = jnp.concatenate(
         [
@@ -111,18 +114,20 @@
                 out_ref[start + HD : start + 2 * HD, :] = result[:, rows:]
 
 
-def attention(queries, earlier, key_rows, value_rows, sink_logits, first, routes, residuals):
+def attention(queries, earlier, key_rows, value_rows, sink_logits, place, residual, routes, scores):
     rows, width = queries.shape
-    height = width + residuals[0].shape[0] + routes.shape[0]
+    slots, depth, _ = residual.shape
     return pl.pallas_call(
         attention_kernel,
-        out_shape=tuple(jax.ShapeDtypeStruct((height, rows), jnp.bfloat16) for _ in residuals),
-        in_specs=[in_smem(), in_smem()] + in_vmem(5 + len(residuals)),
-        out_specs=tuple(in_vmem(len(residuals))),
+        out_shape=tuple(
+            jax.ShapeDtypeStruct((width + depth + 16, rows), jnp.bfloat16) for _ in range(slots - 1)
+        ),
+        in_specs=[in_smem(), in_smem()] + in_vmem(7),
+        out_specs=tuple(in_vmem(slots - 1)),
         compiler_params=params(),
         cost_estimate=cost(8 * rows * rows * width, 6 * rows * width),
         name="attention",
-    )(first, sink_logits, queries, earlier, key_rows, value_rows, routes, *residuals)
+    )(place, sink_logits, queries, earlier, key_rows, value_rows, residual, routes, scores)
 
 
 def flip(arrays):
@@ -135,7 +140,7 @@
         out_shape=tuple(jax.ShapeDtypeStruct(a.shape[::-1], a.dtype) for a in arrays),
         in_specs=in_vmem(len(arrays)),
         out_specs=tuple(in_vmem(len(arrays))),
-        compiler_params=params(FETCH_BYTES),
+        compiler_params=params(),
         cost_estimate=cost(0, 4 * sum(a.size for a in arrays)),
         name="flip",
     )(*arrays)
@@ -187,21 +192,13 @@
     depth = D // slots
     lanes = slots * rows
     experts = len(weights)
-    units = weights[0].shape[0] // 2
+    units = weights[0].shape[1]
 
     def kernel(place_ref, *refs):
         piece_refs = refs[: slots * slots]
         table_ref = refs[slots * slots]
         weight_refs = refs[slots * slots + 1 : slots * slots + 1 + experts]
-        out_ref, share_ref, rows_ref, stage_ref, routes_ref, held_ref, arrived = refs[
-            slots * slots + 1 + experts :
-        ]
-        copies = [
-            pltpu.make_async_copy(weight_refs[e], held_ref.at[e - 1], arrived.at[e - 1])
-            for e in range(1, experts)
-        ]
-        for copy in copies:
-            copy.start()
+        out_ref, share_ref, rows_ref, stage_ref, routes_ref = refs[slots * slots + 1 + experts :]
         for m in range(slots):
             for r in range(slots):
                 lane = pl.ds(pl.multiple_of((place_ref[1] ^ r ^ m) * rows, 128), rows)
@@ -227,10 +224,8 @@
         square = jnp.sum(dot(table_ref[...], (plain * plain).astype(jnp.bfloat16)), axis=0, keepdims=True)
         scale = lax.rsqrt(square / D + 1e-05)
         for e in range(experts):
-            if e:
-                copies[e - 1].wait()
-            both = dot(held_ref[e - 1] if e else weight_refs[0][...], rows_ref[...]) * scale
-            gate, up = both[:units], both[units:]
+            gate = dot(weight_refs[e][0], rows_ref[...]) * scale
+            up = dot(weight_refs[e][1], rows_ref[...]) * scale
             out_ref[e] = ((up + 1.0) * gate * jax.nn.sigmoid(1.702 * gate)).astype(jnp.bfloat16)
 
     flat = [piece for part in pieces for piece in part]
@@ -240,18 +235,14 @@
             jax.ShapeDtypeStruct((experts, units, lanes), jnp.bfloat16),
             jax.ShapeDtypeStruct((experts, lanes), jnp.float32),
         ),
-        in_specs=[in_smem()]
-        + in_vmem(len(flat) + 2)
-        + [pl.BlockSpec(memory_space=pl.ANY)] * (experts - 1),
+        in_specs=[in_smem()] + in_vmem(len(flat) + 1 + experts),
         out_specs=tuple(in_vmem(2)),
         scratch_shapes=[
             pltpu.VMEM((D, lanes), jnp.bfloat16),
             pltpu.VMEM((1, 16, 128) if aligned(depth) else (slots, depth, lanes), jnp.bfloat16),
             pltpu.VMEM((height - depth, lanes), jnp.bfloat16),
-            pltpu.VMEM((max(1, experts - 1), 2 * units, D), jnp.bfloat16),
-            pltpu.SemaphoreType.DMA((max(1, experts - 1),)),
         ],
-        compiler_params=params(FETCH_BYTES),
+        compiler_params=params(),
         cost_estimate=cost(4 * experts * lanes * D * units, 4 * experts * D * units),
         name="activate",
     )(jnp.stack([pair, t] + chosen).astype(jnp.int32), *flat, gain_table, *weights)
@@ -267,13 +258,7 @@
         activated_refs = refs[:t_count]
         share_ref = refs[t_count]
         weight_refs = refs[t_count + 1 : t_count + 1 + experts]
-        *out_refs, all_ref, stage_ref, held_ref, arrived = refs[t_count + 1 + experts :]
-        copies = [
-            pltpu.make_async_copy(weight_refs[e], held_ref.at[e - 1], arrived.at[e - 1])
-            for e in range(1, experts)
-        ]
-        for copy in copies:
-            copy.start()
+        *out_refs, all_ref, stage_ref = refs[t_count + 1 + experts :]
         for u in range(t_count):
             index = t_ref[0] ^ u
             if aligned(units):
@@ -285,10 +270,7 @@
                 all_ref[:, index * units : (index + 1) * units, :] = stage_ref[index]
         total = 0.0
         for e in range(experts):
-            if e:
-                copies[e - 1].wait()
-            result = dot(held_ref[e - 1] if e else weight_refs[0][...], all_ref[e])
-            result = result.astype(jnp.bfloat16).astype(jnp.float32)
+            result = dot(weight_refs[e][...], all_ref[e]).astype(jnp.bfloat16).astype(jnp.float32)
             total = total + share_ref[e : e + 1, :] * result
         for j in range(slots):
             out_refs[j][...] = total[:, j * rows : (j + 1) * rows].astype(jnp.bfloat16)
@@ -296,17 +278,13 @@
     return pl.pallas_call(
         kernel,
         out_shape=tuple(jax.ShapeDtypeStruct((width, rows), jnp.bfloat16) for _ in range(slots)),
-        in_specs=[in_smem()]
-        + in_vmem(t_count + 2)
-        + [pl.BlockSpec(memory_space=pl.ANY)] * (experts - 1),
+        in_specs=[in_smem()] + in_vmem(t_count + 1 + experts),
         out_specs=tuple(in_vmem(slots)),
         scratch_shapes=[
             pltpu.VMEM((experts, t_count * units, lanes), jnp.bfloat16),
             pltpu.VMEM((1, 1, 16, 128) if aligned(units) else (t_count, experts, units, lanes), jnp.bfloat16),
-            pltpu.VMEM((max(1, experts - 1), width, t_count * units), jnp.bfloat16),
-            pltpu.SemaphoreType.DMA((max(1, experts - 1),)),
         ],
-        compiler_params=params(FETCH_BYTES),
+        compiler_params=params(),
         cost_estimate=cost(
             2 * experts * lanes * t_count * units * width, 2 * experts * t_count * units * width
         ),
@@ -339,44 +317,44 @@
     paired = jnp.concatenate([key_rows, value_rows], axis=1)
     earlier = shifted(paired, ("ep", "sub"), 1)
     out_weight = out_weight.T
-    depth = out_weight.shape[1] // s_count
-    near = lax.dynamic_slice_in_dim(out_weight, s * depth, depth, 1)
+    g_count = lax.axis_size("groups")
+    share = s * g_count + lax.axis_index("groups").astype(jnp.int32)
+    depth = out_weight.shape[1] // (s_count * g_count)
+    near = lax.dynamic_slice_in_dim(out_weight, share * depth, depth, 1)
     residual = residual.T.reshape(slots, group * columns, rows)
-    residuals = [picked(residual, pair ^ j, 0) for j in range(slots)]
-    route_rows = jnp.concatenate(
-        [routes.T, route_scores.T // 256, route_scores.T % 256, jnp.zeros((16 - 3 * TOP, rows), jnp.int32)], axis=0
-    ).astype(jnp.bfloat16)
-    earlier, near, residuals, route_rows, expert_in, expert_out = lax.optimization_barrier(
-        (earlier, near, residuals, route_rows, expert_in, expert_out)
-    )
+    earlier, near, expert_in, expert_out = lax.optimization_barrier((earlier, near, expert_in, expert_out))
 
     near = swapped(near, "ep", 1)
 
-    expert_in = expert_in[0].transpose(0, 2, 1).reshape(-1, D)
+    expert_in = expert_in[0].transpose(0, 2, 1)
     expert_out = expert_out[0]
     experts_in = [expert_in] + [swapped(expert_in, "sub", e) for e in range(1, s_count)]
     experts_out = [expert_out] + [swapped(expert_out, "sub", e) for e in range(1, s_count)]
     chosen = [z * s_count + (s ^ e) for e in range(s_count)]
 
-    first = (lax.axis_index(("ep", "sub")) == 0).astype(jnp.int32).reshape(1)
+    first = (lax.axis_index(("ep", "sub")) == 0).astype(jnp.int32)
+    place = jnp.stack([first, pair])
     sent = attention(
-        queries, earlier, key_rows, value_rows, sink_logits, first, route_rows, residuals[1:]
+        queries, earlier, key_rows, value_rows, sink_logits, place, residual, routes.T, route_scores.T
     )
     gathered = [sent[0]] + [swapped(sent[j - 1], "ep", group * j) for j in range(1, slots)]
     experts_out, _ = lax.optimization_barrier((experts_out, sent))
     experts_out = flip(experts_out)
 
-    gathered, near, experts_out = lax.optimization_barrier((gathered, near, experts_out))
-    near_weights = [near] + [swapped(near, "sub", u) for u in range(1, s_count)]
+    near, experts_out = lax.optimization_barrier((near, experts_out))
+    near_weights = [near] + [swapped(near, "groups", g) for g in range(1, g_count)]
+    near_weights = near_weights + [
+        swapped(part, "sub", u) for u in range(1, s_count) for part in near_weights
+    ]
     mine = project(gathered, [out_weight], t, s * 0, t_count)
-    other = project(gathered, near_weights, t, s, t_count)
+    other = project(gathered, near_weights, t, share, t_count)
     first_member = z % group == 0
 
     def ordered(a, b):
         return jnp.concatenate([jnp.where(first_member, a, b), jnp.where(first_member, b, a)], axis=0)
 
     width_in, below = queries.shape[1], group * columns
-    residual_part, kept_routes = residuals[0], route_rows
+    residual_part, kept_routes = picked(residual, pair, 0), gathered[0][width_in + below :]
     for j in range(1, slots):
         residual_part = jnp.where(t == j, gathered[j][width_in : width_in + below], residual_part)
         kept_routes = jnp.where(t == j, gathered[j][width_in + below :], kept_routes)
@@ -388,19 +366,17 @@
     scaled = jnp.concatenate([(hidden * gain_part[:, None]).astype(jnp.bfloat16), kept_routes], axis=0)
 
     own = {0: scaled}
-    pieces = [own] + [{} for m in range(1, t_count)]
     distance = z_count // 2
+    while distance >= group:
+        own.update({d + distance: swapped(own[d], "ep", distance) for d in list(own)})
+        distance //= 2
+    pieces = [own] + [{d: swapped(own[d], "tp", m) for d in own} for m in range(1, t_count)]
     while distance:
-        held = list(own)
-        if distance >= group:
-            for m in range(1, t_count):
-                pieces[m].update({d: swapped(own[d], "tp", m) for d in held if d not in pieces[m]})
-        for d in held:
-            own[d + distance] = swapped(own[d], "ep", distance)
+        for part in pieces:
+            part[distance] = swapped(part[0], "ep", distance)
+        own.update({d + distance: swapped(own[d], "ep", distance) for d in list(own) if d + distance not in own})
         distance //= 2
-    for m in range(1, t_count):
-        pieces[m].update({d: swapped(own[d], "tp", m) for d in range(0, z_count, group) if d not in pieces[m]})
-    late = {d: own[d] for d in own if d % group}
+    late = {d: own[d] for d in own if d not in pieces[-1]}
     late, pieces[1:] = lax.optimization_barrier((late, pieces[1:]))
     for m in range(1, t_count):
         pieces[m].update({d: swapped(late[d], "tp", m) for d in late})

time: 194 us -> 200 us (1.031)
  waiting for transfers between devices: 84.3 us -> 106 us
  Pallas kernels: 55.2 us -> 39.3 us
    ppermute x18 -> x20, waiting for transfers between devices: 84.3 us -> 106 us  [swapped(): lax.ppermute(block, axis, [(i, i ^ distance) for i in range(lax.axis_size...]
    pallas_call x2, Pallas kernels: 26.2 us -> 17.6 us  [activate(): pl.pallas_call(kernel, out_shape=(jax.ShapeDtypeStruct((experts, units, l...]
    pallas_call x2, Pallas kernels: 13.4 us -> 7.44 us  [combine(): pl.pallas_call(kernel, out_shape=tuple((jax.ShapeDtypeStruct((width, rows...]
    unnamed x38 -> x40, local copies, waits for them, and re-layouts: 20.2 us -> 23.7 us
    ppermute x18 -> x20, starting transfers between devices: 22.2 us -> 22.5 us  [swapped(): lax.ppermute(block, axis, [(i, i ^ distance) for i in range(lax.axis_size...]
  transfers between devices with their start and end apart: 19 -> 21, of which waited for: 10 -> 9; matrix products, arithmetic and copies ran while one was open for 4% -> 1% of each run, Pallas kernels for 28% -> 20%
where the time goes in v9:
time: 200 us; the launch traced here: 199 us
  waiting for transfers between devices  106 us (53%)
  Pallas kernels  39.3 us (20%)
  local copies, waits for them, and re-layouts  25.2 us (13%)
  starting transfers between devices  24.9 us (12%)
  other arithmetic  2.97 us (1%)
    ppermute x20, waiting for transfers between devices, swapped(): lax.ppermute(block, axis, [(i, i ^ distance) for i in range(lax.axis_size...  106 us
    unnamed x40, local copies, waits for them, and re-layouts  23.7 us
    ppermute x20, starting transfers between devices, swapped(): lax.ppermute(block, axis, [(i, i ^ distance) for i in range(lax.axis_size...  22.5 us
    pallas_call x2, Pallas kernels, activate(): pl.pallas_call(kernel, out_shape=(jax.ShapeDtypeStruct((experts, units, l...  17.6 us
    pallas_call x2, Pallas kernels, combine(): pl.pallas_call(kernel, out_shape=tuple((jax.ShapeDtypeStruct((width, rows...  7.44 us
    pallas_call x1, Pallas kernels, attention(): pl.pallas_call(attention_kernel, out_shape=tuple((jax.ShapeDtypeStruct((w...  5.57 us
    pallas_call x1, Pallas kernels, flip(): pl.pallas_call(kernel, out_shape=tuple((jax.ShapeDtypeStruct(a.shape[::-1...  4.75 us
  transfers between devices with their start and end apart: 21, of which 9 were waited for; matrix products, arithmetic and copies ran while one was open for 1% of the time, Pallas kernels for 20%

profile of v9, /device:TPU:0, one launch (start us, length us, event | category | flops | bytes accessed | tf_op | source)
XLA Modules:
  0.0 198.7 jit_solution(4366567637675291468)
XLA Ops:
  0.0 0.9 pad_maximum_fusion.2
  0.9 2.4 %collective-permute-start = (bf16[128,512]{1,0:T(8,128)(2,1)S(1)}, bf16[128,512]{1,0:T(8,128)(2,1)S(1)}, u32[]{:S(2)}, u32[]{:S(2)}) collective-permute-start(bf16[128,512]{1,0:T(8,128)(2,1)S(1)} %pad_maximum_fusion.2), channel_id=1, source_target_pairs={{0,1},{1,4},{4,5},{5,8},{8,9},{9,12},{12,13},{2,3},{3,6},{6,7},{7,... | collective-permute-start | bytes 393224 | tf_op jit(solution)/shard_map/ppermute | solution.py:18
  3.3 1.2 dynamic-slice_bitcast_fusion
  4.4 3.4 %collective-permute-start.3 = (bf16[1440,1440]{1,0:T(8,128)(2,1)}, bf16[1440,1440]{1,0:T(8,128)(2,1)}, u32[]{:S(2)}, u32[]{:S(2)}) collective-permute-start(bf16[1440,1440]{1,0:T(8,128)(2,1)} %bitcast.30), channel_id=1, source_target_pairs={{0,1},{1,0},{2,3},{3,2},{4,5},{5,4},{6,7},{7,6},{8,9},{9,8},{10,11... | collective-permute-start | bytes 12441608 | tf_op jit(solution)/shard_map/ppermute | solution.py:22
  7.9 2.8 %collective-permute-start.2 = (bf16[720,512]{1,0:T(8,128)(2,1)S(1)}, bf16[720,512]{1,0:T(8,128)(2,1)S(1)}, u32[]{:S(2)}, u32[]{:S(2)}) collective-permute-start(bf16[720,512]{1,0:T(8,128)(2,1)S(1)} %dynamic-slice_bitcast_fusion), channel_id=1, source_target_pairs={{0,4},{4,0},{8,12},{12,8},{1,5},{5,1},{9,13},{13,9},{2,6},{6,2},{1... | collective-permute-start | bytes 2211848 | tf_op jit(solution)/shard_map/ppermute | solution.py:22
  10.8 1.1 copy-done.7
  11.9 1.0 copy-done.9
  12.9 0.8 copy-done.12
  13.8 0.8 copy-done.13
  14.6 0.7 copy-done.14
  15.3 0.7 copy-done.15
  16.6 5.6 %attention.1.refs_0_ = bf16[3504,128]{1,0:T(8,128)(2,1)S(1)} custom-call(s32[2]{0:T(128)S(1)} %pad_add_fusion.1.place_ref, f32[32]{0:T(128)S(1)} %copy-done.16, bf16[128,2048]{1,0:T(8,128)(2,1)S(1)} %copy-done.9, bf16[128,512]{1,0:T(8,128)(2,1)S(1)} %collective-permute-done.earlier_ref, bf16[128,256]{1,0:T(8,128)(2,1)S(1)} %copy-done.13, ...), custom_call_target="tpu_custom_call" | custom-call | flops 268435456 | bytes 1572864 | tf_op jit(solution)/shard_map/attention/pallas_call | solution.py:120
  22.2 2.2 %copy-done.6 = bf16[1,1440,1440]{2,1,0:T(8,128)(2,1)S(1)} copy-done((bf16[1,1440,1440]{2,1,0:T(8,128)(2,1)S(1)}, bf16[1,1440,1440]{2,1,0:T(8,128)(2,1)}, u32[]{:S(2)}) %copy-start.6) | copy-done | bytes 4147224
  24.5 4.7 %flip.1 = (bf16[1440,1440]{1,0:T(8,128)(2,1)S(1)}, bf16[1440,1440]{1,0:T(8,128)(2,1)S(1)}) custom-call(bf16[1440,1440]{1,0:T(8,128)(2,1)S(1)} %bitcast.31, bf16[1440,1440]{1,0:T(8,128)(2,1)} %collective-permute-done.3.refs_1_), custom_call_target="tpu_custom_call" | custom-call | bytes 16588800 | tf_op jit(solution)/shard_map/flip/pallas_call | solution.py:138
  29.2 2.1 %copy-done.1 = bf16[1440,1440]{1,0:T(8,128)(2,1)} copy-done((bf16[1440,1440]{1,0:T(8,128)(2,1)}, bf16[1440,1440]{1,0:T(8,128)(2,1)S(1)}, u32[]{:S(2)}) %copy-start.1) | copy-done | bytes 4147224
  31.4 2.0 %copy-done.3 = bf16[1440,1440]{1,0:T(8,128)(2,1)} copy-done((bf16[1440,1440]{1,0:T(8,128)(2,1)}, bf16[1440,1440]{1,0:T(8,128)(2,1)S(1)}, u32[]{:S(2)}) %copy-start.3) | copy-done | bytes 4147224
  33.4 1.5 collective-permute-start.4
  34.9 2.6 %collective-permute-start.1 = (bf16[3504,128]{1,0:T(8,128)(2,1)S(1)}, bf16[3504,128]{1,0:T(8,128)(2,1)S(1)}, u32[]{:S(2)}, u32[]{:S(2)}) collective-permute-start(bf16[3504,128]{1,0:T(8,128)(2,1)S(1)} %attention.1.refs_0_), channel_id=1, source_target_pairs={{0,8},{4,12},{8,0},{12,4},{1,9},{5,13},{9,1},{13,5},{2,10},{6,14},... | collective-permute-start | bytes 2691080 | tf_op jit(solution)/shard_map/ppermute | solution.py:22
  37.5 14.0 %collective-permute-done.4.refs_3_ = bf16[720,512]{1,0:T(8,128)(2,1)S(1)} collective-permute-done((bf16[720,512]{1,0:T(8,128)(2,1)S(1)}, bf16[720,512]{1,0:T(8,128)(2,1)S(1)}, u32[]{:S(2)}, u32[]{:S(2)}) %collective-permute-start.4) | collective-permute-done | bytes 737312 | tf_op jit(solution)/shard_map/ppermute | solution.py:22
  51.8 24.3 %collective-permute-done.1.refs_1_ = bf16[3504,128]{1,0:T(8,128)(2,1)S(1)} collective-permute-done((bf16[3504,128]{1,0:T(8,128)(2,1)S(1)}, bf16[3504,128]{1,0:T(8,128)(2,1)S(1)}, u32[]{:S(2)}, u32[]{:S(2)}) %collective-permute-start.1) | collective-permute-done | bytes 897056 | tf_op jit(solution)/shard_map/ppermute | solution.py:22
  76.1 1.8 copy-done.5
  78.0 1.5 project.2
  79.5 2.4 %project.3 = (f32[720,128]{1,0:T(8,128)S(1)}, bf16[1,720,128]{2,1,0:T(8,128)(2,1)S(1)}) custom-call(s32[2]{0:T(128)S(1)} %pad_add_fusion.2.place_ref, bf16[3504,128]{1,0:T(8,128)(2,1)S(1)} %attention.1.refs_0_, bf16[3504,128]{1,0:T(8,128)(2,1)S(1)} %collective-permute-done.1.refs_1_, bf16[720,512]{1,0:T(8,128)(2,1)S(1)} %collective-permute-done.2.refs_2_, ...), custom_call_target="tpu_custom_call" | custom-call | flops 754974720 | bytes 2949120 | tf_op jit(solution)/shard_map/project/pallas_call | solution.py:174
  82.0 1.6 collective-permute-start.7
  83.6 8.9 %collective-permute-done.7 = bf16[1440,128]{1,0:T(8,128)(2,1)S(1)} collective-permute-done((bf16[1440,128]{1,0:T(8,128)(2,1)S(1)}, bf16[1440,128]{1,0:T(8,128)(2,1)S(1)}, u32[]{:S(2)}, u32[]{:S(2)}) %collective-permute-start.7) | collective-permute-done | bytes 368672 | tf_op jit(solution)/shard_map/ppermute | solution.py:22
  92.9 0.7 copy-done.17
  93.7 1.6 collective-permute-start.10
  95.4 14.7 %collective-permute-done.8.refs_1_ = bf16[1456,128]{1,0:T(8,128)(2,1)S(1)} collective-permute-done((bf16[1456,128]{1,0:T(8,128)(2,1)S(1)}, bf16[1456,128]{1,0:T(8,128)(2,1)S(1)}, u32[]{:S(2)}, u32[]{:S(2)}) %collective-permute-start.8) | collective-permute-done | bytes 372768 | tf_op jit(solution)/shard_map/ppermute | solution.py:22
  110.1 1.5 collective-permute-start.12
  111.6 2.0 %collective-permute-start.11 = (bf16[1456,128]{1,0:T(8,128)(2,1)S(1)}, bf16[1456,128]{1,0:T(8,128)(2,1)S(1)}, u32[]{:S(2)}, u32[]{:S(2)}) collective-permute-start(bf16[1456,128]{1,0:T(8,128)(2,1)S(1)} %collective-permute-done.10.refs_2_), channel_id=1, source_target_pairs={{0,4},{4,0},{8,12},{12,8},{1,5},{5,1},{9,13},{13,9},{2,6},{6,2},{1... | collective-permute-start | bytes 1118216 | tf_op jit(solution)/shard_map/ppermute | solution.py:22
  113.9 17.3 %collective-permute-done.11.refs_2_ = bf16[1456,128]{1,0:T(8,128)(2,1)S(1)} collective-permute-done((bf16[1456,128]{1,0:T(8,128)(2,1)S(1)}, bf16[1456,128]{1,0:T(8,128)(2,1)S(1)}, u32[]{:S(2)}, u32[]{:S(2)}) %collective-permute-start.11) | collective-permute-done | bytes 372768 | tf_op jit(solution)/shard_map/ppermute | solution.py:22
  131.8 3.4 %copy-done = bf16[1,2,2880,720]{2,3,1,0:T(8,128)(2,1)S(1)} copy-done((bf16[1,2,2880,720]{2,3,1,0:T(8,128)(2,1)S(1)}, bf16[1,2,2880,720]{2,3,1,0:T(8,128)(2,1)}, u32[]{:S(2)}) %copy-start) | copy-done | bytes 8294424
  135.2 8.9 %activate.2 = (bf16[2,720,256]{2,1,0:T(8,128)(2,1)S(1)}, f32[2,256]{1,0:T(2,128)S(1)}) custom-call(s32[4]{0:T(128)S(1)} %pad_add_fusion.3.place_ref, bf16[1456,128]{1,0:T(8,128)(2,1)S(1)} %pad_maximum_fusion.refs_0_, bf16[1456,128]{1,0:T(8,128)(2,1)S(1)} %collective-permute-done.8.refs_1_, bf16[1456,128]{1,0:T(8,128)(2,1)S(1)} %collective-permute-done.10.refs_2_, ...), custom_call_target="tpu_custom_call" | custom-call | flops 4246732800 | bytes 16588800 | tf_op jit(solution)/shard_map/activate/pallas_call | solution.py:232
  144.1 1.6 collective-permute-start.14
  145.7 1.0 copy-done.11
  146.7 8.7 %activate.3 = (bf16[2,720,256]{2,1,0:T(8,128)(2,1)S(1)}, f32[2,256]{1,0:T(2,128)S(1)}) custom-call(s32[4]{0:T(128)S(1)} %pad_add_fusion.3.place_ref, bf16[1456,128]{1,0:T(8,128)(2,1)S(1)} %collective-permute-done.16.refs_0_, bf16[1456,128]{1,0:T(8,128)(2,1)S(1)} %collective-permute-done.9.refs_1_, bf16[1456,128]{1,0:T(8,128)(2,1)S(1)} %copy-done.11, ...), custom_call_target="tpu_custom_call" | custom-call | flops 4246732800 | bytes 16588800 | tf_op jit(solution)/shard_map/activate/pallas_call | solution.py:232
  156.0 7.7 %collective-permute-done.14.refs_1_ = bf16[2,720,256]{2,1,0:T(8,128)(2,1)} collective-permute-done((bf16[2,720,256]{2,1,0:T(8,128)(2,1)S(1)}, bf16[2,720,256]{2,1,0:T(8,128)(2,1)}, u32[]{:S(2)}, u32[]{:S(2)}) %collective-permute-start.14) | collective-permute-done | bytes 737312 | tf_op jit(solution)/shard_map/ppermute | solution.py:22
  163.7 2.3 %copy-done.2 = bf16[1440,1440]{1,0:T(8,128)(2,1)S(1)} copy-done((bf16[1440,1440]{1,0:T(8,128)(2,1)S(1)}, bf16[1440,1440]{1,0:T(8,128)(2,1)}, u32[]{:S(2)}) %copy-start.2) | copy-done | bytes 4147224
  166.0 2.3 %copy-done.4 = bf16[1440,1440]{1,0:T(8,128)(2,1)S(1)} copy-done((bf16[1440,1440]{1,0:T(8,128)(2,1)S(1)}, bf16[1440,1440]{1,0:T(8,128)(2,1)}, u32[]{:S(2)}) %copy-start.4) | copy-done | bytes 4147224
  168.2 3.7 %combine.2 = (bf16[1440,128]{1,0:T(8,128)(2,1)S(1)}, bf16[1440,128]{1,0:T(8,128)(2,1)S(1)}) custom-call(s32[1]{0:T(128)} %bitcast.t_ref, bf16[2,720,256]{2,1,0:T(8,128)(2,1)S(1)} %get-tuple-element.51.refs_0_, bf16[2,720,256]{2,1,0:T(8,128)(2,1)} %collective-permute-done.14.refs_1_, f32[2,256]{1,0:T(2,128)S(1)} %get-tuple-element.52.refs_2_, ...), custom_call_target="tpu_custom_call" | custom-call | flops 2123366400 | bytes 8294400 | tf_op jit(solution)/shard_map/combine/pallas_call | solution.py:278
  171.9 1.1 collective-permute-start.15
  173.0 2.7 %collective-permute-done.18.refs_1_ = bf16[2,720,256]{2,1,0:T(8,128)(2,1)} collective-permute-done((bf16[2,720,256]{2,1,0:T(8,128)(2,1)S(1)}, bf16[2,720,256]{2,1,0:T(8,128)(2,1)}, u32[]{:S(2)}, u32[]{:S(2)}) %collective-permute-start.18) | collective-permute-done | bytes 737312 | tf_op jit(solution)/shard_map/ppermute | solution.py:22
  175.8 3.7 %combine.3 = (bf16[1440,128]{1,0:T(8,128)(2,1)S(1)}, bf16[1440,128]{1,0:T(8,128)(2,1)S(1)}) custom-call(s32[1]{0:T(128)} %bitcast.t_ref, bf16[2,720,256]{2,1,0:T(8,128)(2,1)S(1)} %get-tuple-element.63.refs_0_, bf16[2,720,256]{2,1,0:T(8,128)(2,1)} %collective-permute-done.18.refs_1_, f32[2,256]{1,0:T(2,128)S(1)} %get-tuple-element.64.refs_2_, ...), custom_call_target="tpu_custom_call" | custom-call | flops 2123366400 | bytes 8294400 | tf_op jit(solution)/shard_map/combine/pallas_call | solution.py:278
  179.5 0.7 collective-permute-start.19
  180.2 0.9 collective-permute-start.20
  181.4 6.9 %collective-permute-done.15 = bf16[1440,128]{1,0:T(8,128)(2,1)S(1)} collective-permute-done((bf16[1440,128]{1,0:T(8,128)(2,1)S(1)}, bf16[1440,128]{1,0:T(8,128)(2,1)S(1)}, u32[]{:S(2)}, u32[]{:S(2)}) %collective-permute-start.15) | collective-permute-done | bytes 368672 | tf_op jit(solution)/shard_map/ppermute | solution.py:22
  188.3 9.4 %collective-permute-done.19 = bf16[1440,128]{1,0:T(8,128)(2,1)S(1)} collective-permute-done((bf16[1440,128]{1,0:T(8,128)(2,1)S(1)}, bf16[1440,128]{1,0:T(8,128)(2,1)S(1)}, u32[]{:S(2)}, u32[]{:S(2)}) %collective-permute-start.19) | collective-permute-done | bytes 368672 | tf_op jit(solution)/shard_map/ppermute | solution.py:22
  197.7 1.0 fusion.3
  (65 shorter events, 3.4 us)
Async XLA Ops:
  0.9 3.6 %collective-permute-start = (bf16[128,512]{1,0:T(8,128)(2,1)S(1)}, bf16[128,512]{1,0:T(8,128)(2,1)S(1)}, u32[]{:S(2)}, u32[]{:S(2)}) collective-permute-start(bf16[128,512]{1,0:T(8,128)(2,1)S(1)} %pad_maximum_fusion.2), channel_id=1, source_target_pairs={{0,1},{1,4},{4,5},{5,8},{8,9},{9,12},{12,13},{2,3},{3,6},{6,7},{7,... | collective-permute-start | bytes 393224 | tf_op jit(solution)/shard_map/ppermute | solution.py:18
  4.4 17.8 %collective-permute-start.3 = (bf16[1440,1440]{1,0:T(8,128)(2,1)}, bf16[1440,1440]{1,0:T(8,128)(2,1)}, u32[]{:S(2)}, u32[]{:S(2)}) collective-permute-start(bf16[1440,1440]{1,0:T(8,128)(2,1)} %bitcast.30), channel_id=1, source_target_pairs={{0,1},{1,0},{2,3},{3,2},{4,5},{5,4},{6,7},{7,6},{8,9},{9,8},{10,11... | collective-permute-start | bytes 12441608 | tf_op jit(solution)/shard_map/ppermute | solution.py:22
  7.9 123.9 %collective-permute-start.13 = (bf16[2,720,2880]{2,1,0:T(8,128)(2,1)}, bf16[2,720,2880]{2,1,0:T(8,128)(2,1)}, u32[]{:S(2)}, u32[]{:S(2)}) collective-permute-start(bf16[2,720,2880]{2,1,0:T(8,128)(2,1)} %bitcast.26), channel_id=1, source_target_pairs={{0,1},{1,0},{2,3},{3,2},{4,5},{5,4},{6,7},{7,6},{8,9},{9,8},{10,11... | collective-permute-start | bytes 24883208 | tf_op jit(solution)/shard_map/ppermute | solution.py:22
  7.9 25.5 %collective-permute-start.2 = (bf16[720,512]{1,0:T(8,128)(2,1)S(1)}, bf16[720,512]{1,0:T(8,128)(2,1)S(1)}, u32[]{:S(2)}, u32[]{:S(2)}) collective-permute-start(bf16[720,512]{1,0:T(8,128)(2,1)S(1)} %dynamic-slice_bitcast_fusion), channel_id=1, source_target_pairs={{0,4},{4,0},{8,12},{12,8},{1,5},{5,1},{9,13},{13,9},{2,6},{6,2},{1... | collective-permute-start | bytes 2211848 | tf_op jit(solution)/shard_map/ppermute | solution.py:22
  10.8 1.1 copy-start.7
  11.9 1.0 copy-start.9
  12.9 0.8 copy-start.12
  13.8 0.8 copy-start.13
  14.6 0.7 copy-start.14
  15.3 0.7 copy-start.15
  16.0 0.7 copy-start.16
  22.2 2.3 %copy-start.6 = (bf16[1,1440,1440]{2,1,0:T(8,128)(2,1)S(1)}, bf16[1,1440,1440]{2,1,0:T(8,128)(2,1)}, u32[]{:S(2)}) copy-start(bf16[1,1440,1440]{2,1,0:T(8,128)(2,1)} %param.19) | copy-start | bytes 12441604
  24.5 27.0 %copy-start.19 = (f32[2880]{0:T(1024)S(1)}, f32[2880]{0:T(1024)}, u32[]{:S(2)}) copy-start(f32[2880]{0:T(1024)} %param.17) | copy-start | bytes 34564
  29.2 2.1 %copy-start.1 = (bf16[1440,1440]{1,0:T(8,128)(2,1)}, bf16[1440,1440]{1,0:T(8,128)(2,1)S(1)}, u32[]{:S(2)}) copy-start(bf16[1440,1440]{1,0:T(8,128)(2,1)S(1)} %get-tuple-element.53.refs_3_) | copy-start | bytes 12441604
  31.4 2.0 %copy-start.3 = (bf16[1440,1440]{1,0:T(8,128)(2,1)}, bf16[1440,1440]{1,0:T(8,128)(2,1)S(1)}, u32[]{:S(2)}) copy-start(bf16[1440,1440]{1,0:T(8,128)(2,1)S(1)} %get-tuple-element.54.refs_4_) | copy-start | bytes 12441604
  33.4 18.1 %collective-permute-start.4 = (bf16[720,512]{1,0:T(8,128)(2,1)S(1)}, bf16[720,512]{1,0:T(8,128)(2,1)S(1)}, u32[]{:S(2)}, u32[]{:S(2)}) collective-permute-start(bf16[720,512]{1,0:T(8,128)(2,1)S(1)} %collective-permute-done.2.refs_2_), channel_id=1, source_target_pairs={{0,16},{16,0},{1,17},{17,1},{2,18},{18,2},{3,19},{19,3},{4,20},{20... | collective-permute-start | bytes 2211848 | tf_op jit(solution)/shard_map/ppermute | solution.py:22
  34.9 41.2 %collective-permute-start.1 = (bf16[3504,128]{1,0:T(8,128)(2,1)S(1)}, bf16[3504,128]{1,0:T(8,128)(2,1)S(1)}, u32[]{:S(2)}, u32[]{:S(2)}) collective-permute-start(bf16[3504,128]{1,0:T(8,128)(2,1)S(1)} %attention.1.refs_0_), channel_id=1, source_target_pairs={{0,8},{4,12},{8,0},{12,4},{1,9},{5,13},{9,1},{13,5},{2,10},{6,14},... | collective-permute-start | bytes 2691080 | tf_op jit(solution)/shard_map/ppermute | solution.py:22
  37.5 42.0 %collective-permute-start.5 = (bf16[720,512]{1,0:T(8,128)(2,1)S(1)}, bf16[720,512]{1,0:T(8,128)(2,1)}, u32[]{:S(2)}, u32[]{:S(2)}) collective-permute-start(bf16[720,512]{1,0:T(8,128)(2,1)S(1)} %collective-permute-done.2.refs_2_), channel_id=1, source_target_pairs={{0,1},{1,0},{2,3},{3,2},{4,5},{5,4},{6,7},{7,6},{8,9},{9,8},{10,11... | collective-permute-start | bytes 2211848 | tf_op jit(solution)/shard_map/ppermute | solution.py:22
  51.5 28.0 %collective-permute-start.6 = (bf16[720,512]{1,0:T(8,128)(2,1)S(1)}, bf16[720,512]{1,0:T(8,128)(2,1)}, u32[]{:S(2)}, u32[]{:S(2)}) collective-permute-start(bf16[720,512]{1,0:T(8,128)(2,1)S(1)} %collective-permute-done.4.refs_3_), channel_id=1, source_target_pairs={{0,1},{1,0},{2,3},{3,2},{4,5},{5,4},{6,7},{7,6},{8,9},{9,8},{10,11... | collective-permute-start | bytes 2211848 | tf_op jit(solution)/shard_map/ppermute | solution.py:22
  76.1 1.8 copy-start.5
  79.5 13.1 %copy-start.8 = (bf16[128,2880]{0,1:T(8,128)(2,1)S(1)}, bf16[128,2880]{0,1:T(8,128)(2,1)}, u32[]{:S(2)}) copy-start(bf16[128,2880]{0,1:T(8,128)(2,1)} %param.16) | copy-start | bytes 2211844
  82.0 10.6 %collective-permute-start.7 = (bf16[1440,128]{1,0:T(8,128)(2,1)S(1)}, bf16[1440,128]{1,0:T(8,128)(2,1)S(1)}, u32[]{:S(2)}, u32[]{:S(2)}) collective-permute-start(bf16[1440,128]{1,0:T(8,128)(2,1)S(1)} %pad_maximum_fusion.1), channel_id=1, source_target_pairs={{0,2},{2,0},{1,3},{3,1},{4,6},{6,4},{5,7},{7,5},{8,10},{10,8},{9,1... | collective-permute-start | bytes 1105928 | tf_op jit(solution)/shard_map/ppermute | solution.py:22
  92.9 0.7 copy-start.17
  93.7 16.5 %collective-permute-start.8 = (bf16[1456,128]{1,0:T(8,128)(2,1)S(1)}, bf16[1456,128]{1,0:T(8,128)(2,1)S(1)}, u32[]{:S(2)}, u32[]{:S(2)}) collective-permute-start(bf16[1456,128]{1,0:T(8,128)(2,1)S(1)} %pad_maximum_fusion.refs_0_), channel_id=1, source_target_pairs={{0,8},{4,12},{8,0},{12,4},{1,9},{5,13},{9,1},{13,5},{2,10},{6,14},... | collective-permute-start | bytes 1118216 | tf_op jit(solution)/shard_map/ppermute | solution.py:22
  93.7 17.9 %collective-permute-start.10 = (bf16[1456,128]{1,0:T(8,128)(2,1)S(1)}, bf16[1456,128]{1,0:T(8,128)(2,1)S(1)}, u32[]{:S(2)}, u32[]{:S(2)}) collective-permute-start(bf16[1456,128]{1,0:T(8,128)(2,1)S(1)} %pad_maximum_fusion.refs_0_), channel_id=1, source_target_pairs={{0,2},{2,0},{1,3},{3,1},{4,6},{6,4},{5,7},{7,5},{8,10},{10,8},{9,1... | collective-permute-start | bytes 1118216 | tf_op jit(solution)/shard_map/ppermute | solution.py:22
  110.1 21.1 %collective-permute-start.12 = (bf16[1456,128]{1,0:T(8,128)(2,1)S(1)}, bf16[1456,128]{1,0:T(8,128)(2,1)S(1)}, u32[]{:S(2)}, u32[]{:S(2)}) collective-permute-start(bf16[1456,128]{1,0:T(8,128)(2,1)S(1)} %collective-permute-done.8.refs_1_), channel_id=1, source_target_pairs={{0,2},{2,0},{1,3},{3,1},{4,6},{6,4},{5,7},{7,5},{8,10},{10,8},{9,1... | collective-permute-start | bytes 1118216 | tf_op jit(solution)/shard_map/ppermute | solution.py:22
  111.6 19.6 %collective-permute-start.9 = (bf16[1456,128]{1,0:T(8,128)(2,1)S(1)}, bf16[1456,128]{1,0:T(8,128)(2,1)S(1)}, u32[]{:S(2)}, u32[]{:S(2)}) collective-permute-start(bf16[1456,128]{1,0:T(8,128)(2,1)S(1)} %collective-permute-done.8.refs_1_), channel_id=1, source_target_pairs={{0,4},{4,0},{8,12},{12,8},{1,5},{5,1},{9,13},{13,9},{2,6},{6,2},{1... | collective-permute-start | bytes 1118216 | tf_op jit(solution)/shard_map/ppermute | solution.py:22
  111.6 19.6 %collective-permute-start.11 = (bf16[1456,128]{1,0:T(8,128)(2,1)S(1)}, bf16[1456,128]{1,0:T(8,128)(2,1)S(1)}, u32[]{:S(2)}, u32[]{:S(2)}) collective-permute-start(bf16[1456,128]{1,0:T(8,128)(2,1)S(1)} %collective-permute-done.10.refs_2_), channel_id=1, source_target_pairs={{0,4},{4,0},{8,12},{12,8},{1,5},{5,1},{9,13},{13,9},{2,6},{6,2},{1... | collective-permute-start | bytes 1118216 | tf_op jit(solution)/shard_map/ppermute | solution.py:22
  113.8 31.9 %collective-permute-start.16 = (bf16[1456,128]{1,0:T(8,128)(2,1)S(1)}, bf16[1456,128]{1,0:T(8,128)(2,1)S(1)}, u32[]{:S(2)}, u32[]{:S(2)}) collective-permute-start(bf16[1456,128]{1,0:T(8,128)(2,1)S(1)} %pad_maximum_fusion.refs_0_), channel_id=1, source_target_pairs={{0,4},{4,0},{8,12},{12,8},{1,5},{5,1},{9,13},{13,9},{2,6},{6,2},{1... | collective-permute-start | bytes 1118216 | tf_op jit(solution)/shard_map/ppermute | solution.py:22
  131.2 12.9 %copy-start.10 = (bf16[1456,128]{1,0:T(8,128)(2,1)}, bf16[1456,128]{1,0:T(8,128)(2,1)S(1)}, u32[]{:S(2)}) copy-start(bf16[1456,128]{1,0:T(8,128)(2,1)S(1)} %collective-permute-done.11.refs_2_) | copy-start | bytes 1118212
  131.2 14.5 %collective-permute-start.17 = (bf16[1456,128]{1,0:T(8,128)(2,1)S(1)}, bf16[1456,128]{1,0:T(8,128)(2,1)S(1)}, u32[]{:S(2)}, u32[]{:S(2)}) collective-permute-start(bf16[1456,128]{1,0:T(8,128)(2,1)S(1)} %collective-permute-done.9.refs_1_), channel_id=1, source_target_pairs={{0,2},{2,0},{1,3},{3,1},{4,6},{6,4},{5,7},{7,5},{8,10},{10,8},{9,1... | collective-permute-start | bytes 1118216 | tf_op jit(solution)/shard_map/ppermute | solution.py:22
  131.8 3.4 %copy-start = (bf16[1,2,2880,720]{2,3,1,0:T(8,128)(2,1)S(1)}, bf16[1,2,2880,720]{2,3,1,0:T(8,128)(2,1)}, u32[]{:S(2)}) copy-start(bf16[1,2,2880,720]{2,3,1,0:T(8,128)(2,1)} %param.18) | copy-start | bytes 24883204
  144.1 19.6 %collective-permute-start.14 = (bf16[2,720,256]{2,1,0:T(8,128)(2,1)S(1)}, bf16[2,720,256]{2,1,0:T(8,128)(2,1)}, u32[]{:S(2)}, u32[]{:S(2)}) collective-permute-start(bf16[2,720,256]{2,1,0:T(8,128)(2,1)S(1)} %get-tuple-element.51.refs_0_), channel_id=1, source_target_pairs={{0,2},{2,0},{1,3},{3,1},{4,6},{6,4},{5,7},{7,5},{8,10},{10,8},{9,1... | collective-permute-start | bytes 2211848 | tf_op jit(solution)/shard_map/ppermute | solution.py:22
  145.7 1.0 copy-start.11
  155.4 20.4 %collective-permute-start.18 = (bf16[2,720,256]{2,1,0:T(8,128)(2,1)S(1)}, bf16[2,720,256]{2,1,0:T(8,128)(2,1)}, u32[]{:S(2)}, u32[]{:S(2)}) collective-permute-start(bf16[2,720,256]{2,1,0:T(8,128)(2,1)S(1)} %get-tuple-element.63.refs_0_), channel_id=1, source_target_pairs={{0,2},{2,0},{1,3},{3,1},{4,6},{6,4},{5,7},{7,5},{8,10},{10,8},{9,1... | collective-permute-start | bytes 2211848 | tf_op jit(solution)/shard_map/ppermute | solution.py:22
  163.7 2.3 %copy-start.2 = (bf16[1440,1440]{1,0:T(8,128)(2,1)S(1)}, bf16[1440,1440]{1,0:T(8,128)(2,1)}, u32[]{:S(2)}) copy-start(bf16[1440,1440]{1,0:T(8,128)(2,1)} %copy-done.1) | copy-start | bytes 12441604
  166.0 2.3 %copy-start.4 = (bf16[1440,1440]{1,0:T(8,128)(2,1)S(1)}, bf16[1440,1440]{1,0:T(8,128)(2,1)}, u32[]{:S(2)}) copy-start(bf16[1440,1440]{1,0:T(8,128)(2,1)} %copy-done.3) | copy-start | bytes 12441604
  171.9 16.3 %collective-permute-start.15 = (bf16[1440,128]{1,0:T(8,128)(2,1)S(1)}, bf16[1440,128]{1,0:T(8,128)(2,1)S(1)}, u32[]{:S(2)}, u32[]{:S(2)}) collective-permute-start(bf16[1440,128]{1,0:T(8,128)(2,1)S(1)} %get-tuple-element.56), channel_id=1, source_target_pairs={{0,8},{4,12},{8,0},{12,4},{1,9},{5,13},{9,1},{13,5},{2,10},{6,14},... | collective-permute-start | bytes 1105928 | tf_op jit(solution)/shard_map/ppermute | solution.py:22
  175.8 5.3 %copy-start.18 = (bf16[1440,128]{1,0:T(8,128)(2,1)S(1)}, bf16[1440,128]{1,0:T(8,128)(2,1)}, u32[]{:S(2)}) copy-start(bf16[1440,128]{1,0:T(8,128)(2,1)} %copy-done.17) | copy-start | bytes 1105924
  179.5 18.2 %collective-permute-start.19 = (bf16[1440,128]{1,0:T(8,128)(2,1)S(1)}, bf16[1440,128]{1,0:T(8,128)(2,1)S(1)}, u32[]{:S(2)}, u32[]{:S(2)}) collective-permute-start(bf16[1440,128]{1,0:T(8,128)(2,1)S(1)} %get-tuple-element.65), channel_id=1, source_target_pairs={{0,4},{4,0},{8,12},{12,8},{1,5},{5,1},{9,13},{13,9},{2,6},{6,2},{1... | collective-permute-start | bytes 1105928 | tf_op jit(solution)/shard_map/ppermute | solution.py:22
  180.2 17.5 %collective-permute-start.20 = (bf16[1440,128]{1,0:T(8,128)(2,1)S(1)}, bf16[1440,128]{1,0:T(8,128)(2,1)S(1)}, u32[]{:S(2)}, u32[]{:S(2)}) collective-permute-start(bf16[1440,128]{1,0:T(8,128)(2,1)S(1)} %get-tuple-element.66), channel_id=1, source_target_pairs={{0,12},{4,8},{8,4},{12,0},{1,13},{5,9},{9,5},{13,1},{2,14},{6,10},... | collective-permute-start | bytes 1105928 | tf_op jit(solution)/shard_map/ppermute | solution.py:22

commit v10 on v8

--- a/solution.py
+++ b/solution.py
@@ -10,7 +10,6 @@
 WIN = 128
 TOP = 4
 VMEM_BYTES = 16 * 1024 * 1024
-FETCH_BYTES = 32 * 1024 * 1024
 
 
 def shifted(block, axis, distance):
@@ -47,23 +46,34 @@
     return size % 16 == 0
 
 
-def params(limit=VMEM_BYTES):
-    return pltpu.CompilerParams(vmem_limit_bytes=limit)
-
-
-def attention_kernel(first_ref, sink_ref, q_ref, earlier_ref, k_ref, v_ref, routes_ref, *refs):
-    residual_refs, out_refs = refs[: len(refs) // 2], refs[len(refs) // 2 :]
-    width, depth = q_ref.shape[1], residual_refs[0].shape[0]
-    for residual_ref, out_ref in zip(residual_refs, out_refs):
-        out_ref[width : width + depth, :] = residual_ref[...]
-        out_ref[width + depth :, :] = routes_ref[...]
+def fetches(source, target, arrived, cuts):
+    return [
+        pltpu.make_async_copy(source.at[cut], target.at[cut], arrived.at[index]) for index, cut in enumerate(cuts)
+    ]
+
+
+def cuts_of(lead, size, count):
+    count = count if size % (16 * count) == 0 else 1
+    step = size // count
+    return [(*at, pl.ds(i * step, step)) for at in lead for i in range(count)]
+
+
+def params():
+    return pltpu.CompilerParams(vmem_limit_bytes=VMEM_BYTES)
+
+
+def attention_kernel(place_ref, sink_ref, q_ref, earlier_ref, k_ref, v_ref, routes_ref, scores_ref, out_ref):
+    width = q_ref.shape[1]
+    numbers = [routes_ref[...], scores_ref[...] // 256, scores_ref[...] % 256]
+    numbers.append(jnp.zeros((out_ref.shape[0] - width - 3 * TOP, q_ref.shape[0]), jnp.int32))
+    out_ref[width:, :] = jnp.concatenate(numbers, axis=0).astype(jnp.float32).astype(jnp.bfloat16)
     rows = q_ref.shape[0]
     kv_count = k_ref.shape[1] // HD
     pairs = q_ref.shape[1] // (2 * HD * kv_count)
     key = lax.broadcasted_iota(jnp.int32, (rows, rows), 0)
     query = lax.broadcasted_iota(jnp.int32, (rows, rows), 1)
     before = key > query
-    shut = before & (first_ref[0] == 1)
+    shut = before & (place_ref[0] == 1)
     blank = jnp.zeros((2 * rows, HD), jnp.bfloat16)
     values = jnp.concatenate(
         [
@@ -106,23 +116,21 @@
                     )
                 )
             result = dot(values[head], jnp.concatenate(weights, axis=1)).astype(jnp.bfloat16)
-            for out_ref in out_refs:
-                out_ref[start : start + HD, :] = result[:, :rows]
-                out_ref[start + HD : start + 2 * HD, :] = result[:, rows:]
-
-
-def attention(queries, earlier, key_rows, value_rows, sink_logits, first, routes, residuals):
+            out_ref[start : start + HD, :] = result[:, :rows]
+            out_ref[start + HD : start + 2 * HD, :] = result[:, rows:]
+
+
+def attention(queries, earlier, key_rows, value_rows, sink_logits, first, routes, scores):
     rows, width = queries.shape
-    height = width + residuals[0].shape[0] + routes.shape[0]
     return pl.pallas_call(
         attention_kernel,
-        out_shape=tuple(jax.ShapeDtypeStruct((height, rows), jnp.bfloat16) for _ in residuals),
-        in_specs=[in_smem(), in_smem()] + in_vmem(5 + len(residuals)),
-        out_specs=tuple(in_vmem(len(residuals))),
+        out_shape=jax.ShapeDtypeStruct((width + 16, rows), jnp.bfloat16),
+        in_specs=[in_smem(), in_smem()] + in_vmem(6),
+        out_specs=in_vmem(1)[0],
         compiler_params=params(),
         cost_estimate=cost(8 * rows * rows * width, 6 * rows * width),
         name="attention",
-    )(first, sink_logits, queries, earlier, key_rows, value_rows, routes, *residuals)
+    )(first, sink_logits, queries, earlier, key_rows, value_rows, routes, scores)
 
 
 def flip(arrays):
@@ -135,7 +143,7 @@
         out_shape=tuple(jax.ShapeDtypeStruct(a.shape[::-1], a.dtype) for a in arrays),
         in_specs=in_vmem(len(arrays)),
         out_specs=tuple(in_vmem(len(arrays))),
-        compiler_params=params(FETCH_BYTES),
+        compiler_params=params(),
         cost_estimate=cost(0, 4 * sum(a.size for a in arrays)),
         name="flip",
     )(*arrays)
@@ -187,7 +195,8 @@
     depth = D // slots
     lanes = slots * rows
     experts = len(weights)
-    units = weights[0].shape[0] // 2
+    units = weights[0].shape[1]
+    cuts = cuts_of([(0,), (1,)], units, 3)
 
     def kernel(place_ref, *refs):
         piece_refs = refs[: slots * slots]
@@ -197,10 +206,9 @@
             slots * slots + 1 + experts :
         ]
         copies = [
-            pltpu.make_async_copy(weight_refs[e], held_ref.at[e - 1], arrived.at[e - 1])
-            for e in range(1, experts)
+            fetches(weight_refs[e], held_ref.at[e - 1], arrived.at[e - 1], cuts) for e in range(1, experts)
         ]
-        for copy in copies:
+        for copy in sum(copies, []):
             copy.start()
         for m in range(slots):
             for r in range(slots):
@@ -228,9 +236,11 @@
         scale = lax.rsqrt(square / D + 1e-05)
         for e in range(experts):
             if e:
-                copies[e - 1].wait()
-            both = dot(held_ref[e - 1] if e else weight_refs[0][...], rows_ref[...]) * scale
-            gate, up = both[:units], both[units:]
+                for copy in copies[e - 1]:
+                    copy.wait()
+            weight_ref = held_ref.at[e - 1] if e else weight_refs[0]
+            gate = dot(weight_ref[0], rows_ref[...]) * scale
+            up = dot(weight_ref[1], rows_ref[...]) * scale
             out_ref[e] = ((up + 1.0) * gate * jax.nn.sigmoid(1.702 * gate)).astype(jnp.bfloat16)
 
     flat = [piece for part in pieces for piece in part]
@@ -248,10 +258,10 @@
             pltpu.VMEM((D, lanes), jnp.bfloat16),
             pltpu.VMEM((1, 16, 128) if aligned(depth) else (slots, depth, lanes), jnp.bfloat16),
             pltpu.VMEM((height - depth, lanes), jnp.bfloat16),
-            pltpu.VMEM((max(1, experts - 1), 2 * units, D), jnp.bfloat16),
-            pltpu.SemaphoreType.DMA((max(1, experts - 1),)),
+            pltpu.VMEM((max(1, experts - 1), 2, units, D), jnp.bfloat16),
+            pltpu.SemaphoreType.DMA((max(1, experts - 1), len(cuts))),
         ],
-        compiler_params=params(FETCH_BYTES),
+        compiler_params=params(),
         cost_estimate=cost(4 * experts * lanes * D * units, 4 * experts * D * units),
         name="activate",
     )(jnp.stack([pair, t] + chosen).astype(jnp.int32), *flat, gain_table, *weights)
@@ -262,6 +272,7 @@
     experts, units, lanes = activated[0].shape
     width = weights[0].shape[0]
     rows = lanes // slots
+    cuts = cuts_of([()], width, 3)
 
     def kernel(t_ref, *refs):
         activated_refs = refs[:t_count]
@@ -269,10 +280,9 @@
         weight_refs = refs[t_count + 1 : t_count + 1 + experts]
         *out_refs, all_ref, stage_ref, held_ref, arrived = refs[t_count + 1 + experts :]
         copies = [
-            pltpu.make_async_copy(weight_refs[e], held_ref.at[e - 1], arrived.at[e - 1])
-            for e in range(1, experts)
+            fetches(weight_refs[e], held_ref.at[e - 1], arrived.at[e - 1], cuts) for e in range(1, experts)
         ]
-        for copy in copies:
+        for copy in sum(copies, []):
             copy.start()
         for u in range(t_count):
             index = t_ref[0] ^ u
@@ -286,9 +296,10 @@
         total = 0.0
         for e in range(experts):
             if e:
-                copies[e - 1].wait()
-            result = dot(held_ref[e - 1] if e else weight_refs[0][...], all_ref[e])
-            result = result.astype(jnp.bfloat16).astype(jnp.float32)
+                for copy in copies[e - 1]:
+                    copy.wait()
+            weight_ref = held_ref.at[e - 1] if e else weight_refs[0]
+            result = dot(weight_ref[...], all_ref[e]).astype(jnp.bfloat16).astype(jnp.float32)
             total = total + share_ref[e : e + 1, :] * result
         for j in range(slots):
             out_refs[j][...] = total[:, j * rows : (j + 1) * rows].astype(jnp.bfloat16)
@@ -304,9 +315,9 @@
             pltpu.VMEM((experts, t_count * units, lanes), jnp.bfloat16),
             pltpu.VMEM((1, 1, 16, 128) if aligned(units) else (t_count, experts, units, lanes), jnp.bfloat16),
             pltpu.VMEM((max(1, experts - 1), width, t_count * units), jnp.bfloat16),
-            pltpu.SemaphoreType.DMA((max(1, experts - 1),)),
+            pltpu.SemaphoreType.DMA((max(1, experts - 1), len(cuts))),
         ],
-        compiler_params=params(FETCH_BYTES),
+        compiler_params=params(),
         cost_estimate=cost(
             2 * experts * lanes * t_count * units * width, 2 * experts * t_count * units * width
         ),
@@ -341,32 +352,33 @@
     out_weight = out_weight.T
     depth = out_weight.shape[1] // s_count
     near = lax.dynamic_slice_in_dim(out_weight, s * depth, depth, 1)
-    residual = residual.T.reshape(slots, group * columns, rows)
-    residuals = [picked(residual, pair ^ j, 0) for j in range(slots)]
-    route_rows = jnp.concatenate(
-        [routes.T, route_scores.T // 256, route_scores.T % 256, jnp.zeros((16 - 3 * TOP, rows), jnp.int32)], axis=0
-    ).astype(jnp.bfloat16)
-    earlier, near, residuals, route_rows, expert_in, expert_out = lax.optimization_barrier(
-        (earlier, near, residuals, route_rows, expert_in, expert_out)
+    residual = picked(residual.T.reshape(slots, group * columns, rows), pair ^ t, 0)
+    earlier, near, residual, expert_in, expert_out = lax.optimization_barrier(
+        (earlier, near, residual, expert_in, expert_out)
     )
 
     near = swapped(near, "ep", 1)
 
-    expert_in = expert_in[0].transpose(0, 2, 1).reshape(-1, D)
+    route = [
+        (i * t_count + k, (i ^ (group * k)) * t_count + k) for i in range(z_count) for k in range(t_count)
+    ]
+    residual = lax.ppermute(residual, ("ep", "tp"), route)
+
+    expert_in = expert_in[0].transpose(0, 2, 1)
     expert_out = expert_out[0]
     experts_in = [expert_in] + [swapped(expert_in, "sub", e) for e in range(1, s_count)]
     experts_out = [expert_out] + [swapped(expert_out, "sub", e) for e in range(1, s_count)]
     chosen = [z * s_count + (s ^ e) for e in range(s_count)]
 
     first = (lax.axis_index(("ep", "sub")) == 0).astype(jnp.int32).reshape(1)
-    sent = attention(
-        queries, earlier, key_rows, value_rows, sink_logits, first, route_rows, residuals[1:]
+    attended = attention(
+        queries, earlier, key_rows, value_rows, sink_logits, first, routes.T, route_scores.T
     )
-    gathered = [sent[0]] + [swapped(sent[j - 1], "ep", group * j) for j in range(1, slots)]
-    experts_out, _ = lax.optimization_barrier((experts_out, sent))
+    gathered = [attended] + [swapped(attended, "ep", group * j) for j in range(1, slots)]
+    experts_out, _ = lax.optimization_barrier((experts_out, attended))
     experts_out = flip(experts_out)
 
-    gathered, near, experts_out = lax.optimization_barrier((gathered, near, experts_out))
+    gathered, near, residual, experts_out = lax.optimization_barrier((gathered, near, residual, experts_out))
     near_weights = [near] + [swapped(near, "sub", u) for u in range(1, s_count)]
     mine = project(gathered, [out_weight], t, s * 0, t_count)
     other = project(gathered, near_weights, t, s, t_count)
@@ -375,12 +387,10 @@
     def ordered(a, b):
         return jnp.concatenate([jnp.where(first_member, a, b), jnp.where(first_member, b, a)], axis=0)
 
-    width_in, below = queries.shape[1], group * columns
-    residual_part, kept_routes = residuals[0], route_rows
+    kept_routes = gathered[0][queries.shape[1] :]
     for j in range(1, slots):
-        residual_part = jnp.where(t == j, gathered[j][width_in : width_in + below], residual_part)
-        kept_routes = jnp.where(t == j, gathered[j][width_in + below :], kept_routes)
-    hidden = ordered(mine[0], other[0]) + residual_part.astype(jnp.float32)
+        kept_routes = jnp.where(t == j, gathered[j][queries.shape[1] :], kept_routes)
+    hidden = ordered(mine[0], other[0]) + residual.astype(jnp.float32)
     for m in range(1, t_count):
         received = swapped(ordered(mine[1][m - 1], other[1][m - 1]), "tp", m)
         hidden = hidden + received.astype(jnp.float32)

time: 194 us -> 189 us (0.974)
  starting transfers between devices: 24.6 us -> 35.2 us
  Pallas kernels: 55.2 us -> 46.5 us
  waiting for transfers between devices: 84.3 us -> 78 us
    ppermute x18, starting transfers between devices: 22.2 us -> 31.2 us  [swapped(): lax.ppermute(block, axis, [(i, i ^ distance) for i in range(lax.axis_size...]
    pallas_call x2, Pallas kernels: 26.2 us -> 18 us  [activate(): pl.pallas_call(kernel, out_shape=(jax.ShapeDtypeStruct((experts, units, l...]
    ppermute x18, waiting for transfers between devices: 84.3 us -> 78 us  [swapped(): lax.ppermute(block, axis, [(i, i ^ distance) for i in range(lax.axis_size...]
    unnamed x38 -> x42, local copies, waits for them, and re-layouts: 20.2 us -> 21.9 us
  transfers between devices with their start and end apart: 19 -> 20, of which waited for: 10 -> 10; matrix products, arithmetic and copies ran while one was open for 4% -> 3% of each run, Pallas kernels for 28% -> 25%
where the time goes in v10:
time: 189 us; the launch traced here: 188 us
  waiting for transfers between devices  78 us (41%)
  Pallas kernels  46.5 us (25%)
  starting transfers between devices  35.2 us (19%)
  local copies, waits for them, and re-layouts  25.6 us (14%)
  other arithmetic  2.97 us (2%)
    ppermute x18, waiting for transfers between devices, swapped(): lax.ppermute(block, axis, [(i, i ^ distance) for i in range(lax.axis_size...  78 us
    ppermute x18, starting transfers between devices, swapped(): lax.ppermute(block, axis, [(i, i ^ distance) for i in range(lax.axis_size...  31.2 us
    unnamed x42, local copies, waits for them, and re-layouts  21.9 us
    pallas_call x2, Pallas kernels, activate(): pl.pallas_call(kernel, out_shape=(jax.ShapeDtypeStruct((experts, units, l...  18 us
    pallas_call x2, Pallas kernels, combine(): pl.pallas_call(kernel, out_shape=tuple((jax.ShapeDtypeStruct((width, rows...  14.3 us
    pallas_call x1, Pallas kernels, attention(): pl.pallas_call(attention_kernel, out_shape=jax.ShapeDtypeStruct((width +...  5.54 us
    pallas_call x1, Pallas kernels, flip(): pl.pallas_call(kernel, out_shape=tuple((jax.ShapeDtypeStruct(a.shape[::-1...  4.73 us
    pallas_call x2, Pallas kernels, project(): pl.pallas_call(kernel, out_shape=(jax.ShapeDtypeStruct((columns, rows), j...  3.93 us
  transfers between devices with their start and end apart: 20, of which 10 were waited for; matrix products, arithmetic and copies ran while one was open for 3% of the time, Pallas kernels for 25%

profile of v10, /device:TPU:0, one launch (start us, length us, event | category | flops | bytes accessed | tf_op | source)
XLA Modules:
  0.0 188.5 jit_solution(16310408318206341407)
XLA Ops:
  0.0 1.0 pad_maximum_fusion.2
  1.0 2.4 %collective-permute-start = (bf16[128,512]{1,0:T(8,128)(2,1)S(1)}, bf16[128,512]{1,0:T(8,128)(2,1)S(1)}, u32[]{:S(2)}, u32[]{:S(2)}) collective-permute-start(bf16[128,512]{1,0:T(8,128)(2,1)S(1)} %pad_maximum_fusion.2), channel_id=1, source_target_pairs={{0,1},{1,4},{4,5},{5,8},{8,9},{9,12},{12,13},{2,3},{3,6},{6,7},{7,... | collective-permute-start | bytes 393224 | tf_op jit(solution)/shard_map/ppermute | solution.py:18
  3.4 0.8 dynamic-slice_bitcast_fusion.1
  4.1 2.6 %dynamic-slice_bitcast_fusion = bf16[720,1024]{1,0:T(8,128)(2,1)} fusion(bf16[2048,720]{0,1:T(8,128)(2,1)} %param.15, s32[]{:T(128)S(6)} %select_n.93), kind=kLoop, calls=%fused_computation | loop fusion | bytes 2949124 | tf_op jit(solution)/shard_map/dynamic_slice | solution.py:354
  6.8 2.7 %collective-permute-start.4 = (bf16[1440,1440]{1,0:T(8,128)(2,1)}, bf16[1440,1440]{1,0:T(8,128)(2,1)}, u32[]{:S(2)}, u32[]{:S(2)}) collective-permute-start(bf16[1440,1440]{1,0:T(8,128)(2,1)} %bitcast.31), channel_id=1, source_target_pairs={{0,1},{1,0},{2,3},{3,2},{4,5},{5,4},{6,7},{7,6},{8,9},{9,8},{10,11... | collective-permute-start | bytes 12441608 | tf_op jit(solution)/shard_map/ppermute | solution.py:22
  9.5 1.6 collective-permute-start.2
  11.0 1.0 copy-done.8
  12.1 0.8 copy-done.11
  12.9 0.8 copy-done.12
  15.8 5.5 %attention.1.refs_0_ = bf16[2064,128]{1,0:T(8,128)(2,1)S(1)} custom-call(s32[1]{0:T(128)} %bitcast.1.place_ref, f32[32]{0:T(128)S(1)} %copy-done.15, bf16[128,2048]{1,0:T(8,128)(2,1)S(1)} %copy-done.8, bf16[128,512]{1,0:T(8,128)(2,1)S(1)} %collective-permute-done.earlier_ref, bf16[128,256]{1,0:T(8,128)(2,1)S(1)} %copy-done.12, ...), custom_call_target="tpu_custom_call" | custom-call | flops 268435456 | bytes 1572864 | tf_op jit(solution)/shard_map/attention/pallas_call | solution.py:125
  21.3 2.4 %collective-permute-start.1 = (bf16[2064,128]{1,0:T(8,128)(2,1)S(1)}, bf16[2064,128]{1,0:T(8,128)(2,1)S(1)}, u32[]{:S(2)}, u32[]{:S(2)}) collective-permute-start(bf16[2064,128]{1,0:T(8,128)(2,1)S(1)} %attention.1.refs_0_), channel_id=1, source_target_pairs={{0,8},{4,12},{8,0},{12,4},{1,9},{5,13},{9,1},{13,5},{2,10},{6,14},... | collective-permute-start | bytes 1585160 | tf_op jit(solution)/shard_map/ppermute | solution.py:22
  23.7 1.6 collective-permute-start.3
  25.4 2.3 %copy-done.7 = bf16[1,1440,1440]{2,1,0:T(8,128)(2,1)S(1)} copy-done((bf16[1,1440,1440]{2,1,0:T(8,128)(2,1)S(1)}, bf16[1,1440,1440]{2,1,0:T(8,128)(2,1)}, u32[]{:S(2)}) %copy-start.7) | copy-done | bytes 4147224
  27.6 4.7 %flip.1 = (bf16[1440,1440]{1,0:T(8,128)(2,1)S(1)}, bf16[1440,1440]{1,0:T(8,128)(2,1)S(1)}) custom-call(bf16[1440,1440]{1,0:T(8,128)(2,1)S(1)} %bitcast.32, bf16[1440,1440]{1,0:T(8,128)(2,1)} %collective-permute-done.4.refs_1_), custom_call_target="tpu_custom_call" | custom-call | bytes 16588800 | tf_op jit(solution)/shard_map/flip/pallas_call | solution.py:141
  32.4 2.1 %copy-done.2 = bf16[1440,1440]{1,0:T(8,128)(2,1)} copy-done((bf16[1440,1440]{1,0:T(8,128)(2,1)}, bf16[1440,1440]{1,0:T(8,128)(2,1)S(1)}, u32[]{:S(2)}) %copy-start.2) | copy-done | bytes 4147224
  34.5 2.0 %copy-done.4 = bf16[1440,1440]{1,0:T(8,128)(2,1)} copy-done((bf16[1440,1440]{1,0:T(8,128)(2,1)}, bf16[1440,1440]{1,0:T(8,128)(2,1)S(1)}, u32[]{:S(2)}) %copy-start.4) | copy-done | bytes 4147224
  36.5 18.3 %collective-permute-done.1.refs_1_ = bf16[2064,128]{1,0:T(8,128)(2,1)S(1)} collective-permute-done((bf16[2064,128]{1,0:T(8,128)(2,1)S(1)}, bf16[2064,128]{1,0:T(8,128)(2,1)S(1)}, u32[]{:S(2)}, u32[]{:S(2)}) %collective-permute-start.1) | collective-permute-done | bytes 528416 | tf_op jit(solution)/shard_map/ppermute | solution.py:22
  54.8 0.9 collective-permute-done.2.refs_2_
  56.0 1.8 copy-done.6
  57.8 1.5 project.2
  59.3 2.4 %project.3 = (f32[720,128]{1,0:T(8,128)S(1)}, bf16[1,720,128]{2,1,0:T(8,128)(2,1)S(1)}) custom-call(s32[2]{0:T(128)S(1)} %pad_add_fusion.1.place_ref, bf16[2064,128]{1,0:T(8,128)(2,1)S(1)} %attention.1.refs_0_, bf16[2064,128]{1,0:T(8,128)(2,1)S(1)} %collective-permute-done.1.refs_1_, bf16[720,1024]{1,0:T(8,128)(2,1)S(1)} %collective-permute-done.2.refs_2_, ...), custom_call_target="tpu_custom_call" | custom-call | flops 754974720 | bytes 2949120 | tf_op jit(solution)/shard_map/project/pallas_call | solution.py:177
  61.8 9.5 %collective-permute-start.6 = (bf16[1440,128]{1,0:T(8,128)(2,1)S(1)}, bf16[1440,128]{1,0:T(8,128)(2,1)S(1)}, u32[]{:S(2)}, u32[]{:S(2)}) collective-permute-start(bf16[1440,128]{1,0:T(8,128)(2,1)S(1)} %pad_maximum_fusion.1), channel_id=1, source_target_pairs={{0,2},{2,0},{1,3},{3,1},{4,6},{6,4},{5,7},{7,5},{8,10},{10,8},{9,1... | collective-permute-start | bytes 1105928 | tf_op jit(solution)/shard_map/ppermute | solution.py:22
  71.4 9.2 %collective-permute-done.6 = bf16[1440,128]{1,0:T(8,128)(2,1)S(1)} collective-permute-done((bf16[1440,128]{1,0:T(8,128)(2,1)S(1)}, bf16[1440,128]{1,0:T(8,128)(2,1)S(1)}, u32[]{:S(2)}, u32[]{:S(2)}) %collective-permute-start.6) | collective-permute-done | bytes 368672 | tf_op jit(solution)/shard_map/ppermute | solution.py:22
  80.9 3.3 %collective-permute-start.7 = (bf16[1456,128]{1,0:T(8,128)(2,1)S(1)}, bf16[1456,128]{1,0:T(8,128)(2,1)S(1)}, u32[]{:S(2)}, u32[]{:S(2)}) collective-permute-start(bf16[1456,128]{1,0:T(8,128)(2,1)S(1)} %pad_maximum_fusion.refs_0_), channel_id=1, source_target_pairs={{0,8},{4,12},{8,0},{12,4},{1,9},{5,13},{9,1},{13,5},{2,10},{6,14},... | collective-permute-start | bytes 1118216 | tf_op jit(solution)/shard_map/ppermute | solution.py:22
  84.3 1.7 collective-permute-start.10
  86.3 14.8 %collective-permute-done.7.refs_1_ = bf16[1456,128]{1,0:T(8,128)(2,1)S(1)} collective-permute-done((bf16[1456,128]{1,0:T(8,128)(2,1)S(1)}, bf16[1456,128]{1,0:T(8,128)(2,1)S(1)}, u32[]{:S(2)}, u32[]{:S(2)}) %collective-permute-start.7) | collective-permute-done | bytes 372768 | tf_op jit(solution)/shard_map/ppermute | solution.py:22
  101.0 1.4 collective-permute-start.11
  102.7 8.3 %collective-permute-done.11.refs_3_ = bf16[1456,128]{1,0:T(8,128)(2,1)S(1)} collective-permute-done((bf16[1456,128]{1,0:T(8,128)(2,1)S(1)}, bf16[1456,128]{1,0:T(8,128)(2,1)S(1)}, u32[]{:S(2)}, u32[]{:S(2)}) %collective-permute-start.11) | collective-permute-done | bytes 372768 | tf_op jit(solution)/shard_map/ppermute | solution.py:22
  111.0 1.0 collective-permute-done.9.refs_1_
  111.9 0.8 collective-permute-start.15
  112.7 1.3 collective-permute-start.16
  114.0 3.4 %copy-done.1 = bf16[1,2,2880,720]{2,3,1,0:T(8,128)(2,1)S(1)} copy-done((bf16[1,2,2880,720]{2,3,1,0:T(8,128)(2,1)S(1)}, bf16[1,2,2880,720]{2,3,1,0:T(8,128)(2,1)}, u32[]{:S(2)}) %copy-start.1) | copy-done | bytes 8294424
  117.4 10.3 %activate.2 = (bf16[2,720,256]{2,1,0:T(8,128)(2,1)}, f32[2,256]{1,0:T(2,128)S(1)}) custom-call(s32[4]{0:T(128)S(1)} %pad_add_fusion.2.place_ref, bf16[1456,128]{1,0:T(8,128)(2,1)S(1)} %pad_maximum_fusion.refs_0_, bf16[1456,128]{1,0:T(8,128)(2,1)S(1)} %collective-permute-done.7.refs_1_, bf16[1456,128]{1,0:T(8,128)(2,1)S(1)} %collective-permute-done.10.refs_2_, ...), custom_call_target="tpu_custom_call" | custom-call | flops 4246732800 | bytes 16588800 | tf_op jit(solution)/shard_map/activate/pallas_call | solution.py:247
  127.7 0.8 collective-permute-start.13
  128.9 1.0 copy-done.10
  129.9 7.7 %activate.3 = (bf16[2,720,256]{2,1,0:T(8,128)(2,1)S(1)}, f32[2,256]{1,0:T(2,128)S(1)}) custom-call(s32[4]{0:T(128)S(1)} %pad_add_fusion.2.place_ref, bf16[1456,128]{1,0:T(8,128)(2,1)S(1)} %collective-permute-done.8.refs_0_, bf16[1456,128]{1,0:T(8,128)(2,1)S(1)} %copy-done.10, bf16[1456,128]{1,0:T(8,128)(2,1)S(1)} %collective-permute-done.15.refs_2_, ...), custom_call_target="tpu_custom_call" | custom-call | flops 4246732800 | bytes 16588800 | tf_op jit(solution)/shard_map/activate/pallas_call | solution.py:247
  137.5 1.0 collective-permute-start.17
  138.6 8.9 %collective-permute-done.13.refs_1_ = bf16[2,720,256]{2,1,0:T(8,128)(2,1)} collective-permute-done((bf16[2,720,256]{2,1,0:T(8,128)(2,1)}, bf16[2,720,256]{2,1,0:T(8,128)(2,1)}, u32[]{:S(2)}, u32[]{:S(2)}) %collective-permute-start.13) | collective-permute-done | bytes 737312 | tf_op jit(solution)/shard_map/ppermute | solution.py:22
  147.5 2.3 %copy-done.3 = bf16[1440,1440]{1,0:T(8,128)(2,1)S(1)} copy-done((bf16[1440,1440]{1,0:T(8,128)(2,1)S(1)}, bf16[1440,1440]{1,0:T(8,128)(2,1)}, u32[]{:S(2)}) %copy-start.3) | copy-done | bytes 4147224
  149.8 2.3 %copy-done.5 = bf16[1440,1440]{1,0:T(8,128)(2,1)S(1)} copy-done((bf16[1440,1440]{1,0:T(8,128)(2,1)S(1)}, bf16[1440,1440]{1,0:T(8,128)(2,1)}, u32[]{:S(2)}) %copy-start.5) | copy-done | bytes 4147224
  152.0 7.2 %combine.2 = (bf16[1440,128]{1,0:T(8,128)(2,1)S(1)}, bf16[1440,128]{1,0:T(8,128)(2,1)S(1)}) custom-call(s32[1]{0:T(128)} %bitcast.t_ref, bf16[2,720,256]{2,1,0:T(8,128)(2,1)} %get-tuple-element.59.refs_0_, bf16[2,720,256]{2,1,0:T(8,128)(2,1)} %collective-permute-done.13.refs_1_, f32[2,256]{1,0:T(2,128)S(1)} %get-tuple-element.60.refs_2_, ...), custom_call_target="tpu_custom_call" | custom-call | flops 2123366400 | bytes 8294400 | tf_op jit(solution)/shard_map/combine/pallas_call | solution.py:307
  159.3 1.3 collective-permute-start.14
  160.6 7.1 %combine.3 = (bf16[1440,128]{1,0:T(8,128)(2,1)S(1)}, bf16[1440,128]{1,0:T(8,128)(2,1)S(1)}) custom-call(s32[1]{0:T(128)} %bitcast.t_ref, bf16[2,720,256]{2,1,0:T(8,128)(2,1)S(1)} %get-tuple-element.71.refs_0_, bf16[2,720,256]{2,1,0:T(8,128)(2,1)} %collective-permute-done.17.refs_1_, f32[2,256]{1,0:T(2,128)S(1)} %get-tuple-element.72.refs_2_, ...), custom_call_target="tpu_custom_call" | custom-call | flops 2123366400 | bytes 8294400 | tf_op jit(solution)/shard_map/combine/pallas_call | solution.py:307
  167.7 1.8 collective-permute-start.18
  169.5 1.4 collective-permute-start.19
  171.2 8.4 %collective-permute-done.14 = bf16[1440,128]{1,0:T(8,128)(2,1)S(1)} collective-permute-done((bf16[1440,128]{1,0:T(8,128)(2,1)S(1)}, bf16[1440,128]{1,0:T(8,128)(2,1)S(1)}, u32[]{:S(2)}, u32[]{:S(2)}) %collective-permute-start.14) | collective-permute-done | bytes 368672 | tf_op jit(solution)/shard_map/ppermute | solution.py:22
  179.5 8.0 %collective-permute-done.18 = bf16[1440,128]{1,0:T(8,128)(2,1)S(1)} collective-permute-done((bf16[1440,128]{1,0:T(8,128)(2,1)S(1)}, bf16[1440,128]{1,0:T(8,128)(2,1)S(1)}, u32[]{:S(2)}, u32[]{:S(2)}) %collective-permute-start.18) | collective-permute-done | bytes 368672 | tf_op jit(solution)/shard_map/ppermute | solution.py:22
  187.5 1.0 fusion.3
  (65 shorter events, 4.0 us)
Async XLA Ops:
  0.0 3.4 %copy-start = (bf16[128,2880]{0,1:T(8,128)(2,1)S(1)}, bf16[128,2880]{0,1:T(8,128)(2,1)}, u32[]{:S(2)}) copy-start(bf16[128,2880]{0,1:T(8,128)(2,1)} %param.16) | copy-start | bytes 2211844
  1.0 5.8 %collective-permute-start = (bf16[128,512]{1,0:T(8,128)(2,1)S(1)}, bf16[128,512]{1,0:T(8,128)(2,1)S(1)}, u32[]{:S(2)}, u32[]{:S(2)}) collective-permute-start(bf16[128,512]{1,0:T(8,128)(2,1)S(1)} %pad_maximum_fusion.2), channel_id=1, source_target_pairs={{0,1},{1,4},{4,5},{5,8},{8,9},{9,12},{12,13},{2,3},{3,6},{6,7},{7,... | collective-permute-start | bytes 393224 | tf_op jit(solution)/shard_map/ppermute | solution.py:18
  6.8 18.6 %collective-permute-start.4 = (bf16[1440,1440]{1,0:T(8,128)(2,1)}, bf16[1440,1440]{1,0:T(8,128)(2,1)}, u32[]{:S(2)}, u32[]{:S(2)}) collective-permute-start(bf16[1440,1440]{1,0:T(8,128)(2,1)} %bitcast.31), channel_id=1, source_target_pairs={{0,1},{1,0},{2,3},{3,2},{4,5},{5,4},{6,7},{7,6},{8,9},{9,8},{10,11... | collective-permute-start | bytes 12441608 | tf_op jit(solution)/shard_map/ppermute | solution.py:22
  9.4 104.5 %collective-permute-start.12 = (bf16[2,720,2880]{2,1,0:T(8,128)(2,1)}, bf16[2,720,2880]{2,1,0:T(8,128)(2,1)}, u32[]{:S(2)}, u32[]{:S(2)}) collective-permute-start(bf16[2,720,2880]{2,1,0:T(8,128)(2,1)} %bitcast.27), channel_id=1, source_target_pairs={{0,1},{1,0},{2,3},{3,2},{4,5},{5,4},{6,7},{7,6},{8,9},{9,8},{10,11... | collective-permute-start | bytes 24883208 | tf_op jit(solution)/shard_map/ppermute | solution.py:22
  9.5 46.2 %collective-permute-start.2 = (bf16[720,1024]{1,0:T(8,128)(2,1)}, bf16[720,1024]{1,0:T(8,128)(2,1)S(1)}, u32[]{:S(2)}, u32[]{:S(2)}) collective-permute-start(bf16[720,1024]{1,0:T(8,128)(2,1)} %dynamic-slice_bitcast_fusion), channel_id=1, source_target_pairs={{0,4},{4,0},{8,12},{12,8},{1,5},{5,1},{9,13},{13,9},{2,6},{6,2},{1... | collective-permute-start | bytes 4423688 | tf_op jit(solution)/shard_map/ppermute | solution.py:22
  11.0 1.0 copy-start.8
  12.1 0.8 copy-start.11
  12.9 0.8 copy-start.12
  13.7 0.7 copy-start.13
  14.4 0.7 copy-start.14
  15.1 0.7 copy-start.15
  15.8 39.9 %copy-start.20 = (f32[2880]{0:T(1024)S(1)}, f32[2880]{0:T(1024)}, u32[]{:S(2)}) copy-start(f32[2880]{0:T(1024)} %param.17) | copy-start | bytes 34564
  21.3 33.5 %collective-permute-start.1 = (bf16[2064,128]{1,0:T(8,128)(2,1)S(1)}, bf16[2064,128]{1,0:T(8,128)(2,1)S(1)}, u32[]{:S(2)}, u32[]{:S(2)}) collective-permute-start(bf16[2064,128]{1,0:T(8,128)(2,1)S(1)} %attention.1.refs_0_), channel_id=1, source_target_pairs={{0,8},{4,12},{8,0},{12,4},{1,9},{5,13},{9,1},{13,5},{2,10},{6,14},... | collective-permute-start | bytes 1585160 | tf_op jit(solution)/shard_map/ppermute | solution.py:22
  23.7 12.8 %collective-permute-start.3 = (bf16[1440,128]{1,0:T(8,128)(2,1)}, bf16[1440,128]{1,0:T(8,128)(2,1)S(1)}, u32[]{:S(2)}, u32[]{:S(2)}) collective-permute-start(bf16[1440,128]{1,0:T(8,128)(2,1)} %dynamic-slice_bitcast_fusion.1), channel_id=1, source_target_pairs={{0,0},{2,10},{4,4},{6,14},{8,8},{10,2},{12,12},{14,6},{1,1},{3,11}... | collective-permute-start | bytes 1105928 | tf_op jit(solution)/shard_map/ppermute | solution.py:365
  25.4 2.3 %copy-start.7 = (bf16[1,1440,1440]{2,1,0:T(8,128)(2,1)S(1)}, bf16[1,1440,1440]{2,1,0:T(8,128)(2,1)}, u32[]{:S(2)}) copy-start(bf16[1,1440,1440]{2,1,0:T(8,128)(2,1)} %param.19) | copy-start | bytes 12441604
  32.4 2.1 %copy-start.2 = (bf16[1440,1440]{1,0:T(8,128)(2,1)}, bf16[1440,1440]{1,0:T(8,128)(2,1)S(1)}, u32[]{:S(2)}) copy-start(bf16[1440,1440]{1,0:T(8,128)(2,1)S(1)} %get-tuple-element.61.refs_3_) | copy-start | bytes 12441604
  34.5 2.0 %copy-start.4 = (bf16[1440,1440]{1,0:T(8,128)(2,1)}, bf16[1440,1440]{1,0:T(8,128)(2,1)S(1)}, u32[]{:S(2)}) copy-start(bf16[1440,1440]{1,0:T(8,128)(2,1)S(1)} %get-tuple-element.62.refs_4_) | copy-start | bytes 12441604
  36.5 19.2 %copy-start.18 = (bf16[1440,128]{1,0:T(8,128)(2,1)}, bf16[1440,128]{1,0:T(8,128)(2,1)S(1)}, u32[]{:S(2)}) copy-start(bf16[1440,128]{1,0:T(8,128)(2,1)S(1)} %collective-permute-done.3) | copy-start | bytes 1105924
  55.7 3.6 %collective-permute-start.5 = (bf16[720,1024]{1,0:T(8,128)(2,1)S(1)}, bf16[720,1024]{1,0:T(8,128)(2,1)}, u32[]{:S(2)}, u32[]{:S(2)}) collective-permute-start(bf16[720,1024]{1,0:T(8,128)(2,1)S(1)} %collective-permute-done.2.refs_2_), channel_id=1, source_target_pairs={{0,1},{1,0},{2,3},{3,2},{4,5},{5,4},{6,7},{7,6},{8,9},{9,8},{10,11... | collective-permute-start | bytes 4423688 | tf_op jit(solution)/shard_map/ppermute | solution.py:22
  56.0 1.8 copy-start.6
  59.3 21.2 %copy-start.19 = (bf16[1440,128]{1,0:T(8,128)(2,1)S(1)}, bf16[1440,128]{1,0:T(8,128)(2,1)}, u32[]{:S(2)}) copy-start(bf16[1440,128]{1,0:T(8,128)(2,1)} %copy-done.18) | copy-start | bytes 1105924
  61.8 18.7 %collective-permute-start.6 = (bf16[1440,128]{1,0:T(8,128)(2,1)S(1)}, bf16[1440,128]{1,0:T(8,128)(2,1)S(1)}, u32[]{:S(2)}, u32[]{:S(2)}) collective-permute-start(bf16[1440,128]{1,0:T(8,128)(2,1)S(1)} %pad_maximum_fusion.1), channel_id=1, source_target_pairs={{0,2},{2,0},{1,3},{3,1},{4,6},{6,4},{5,7},{7,5},{8,10},{10,8},{9,1... | collective-permute-start | bytes 1105928 | tf_op jit(solution)/shard_map/ppermute | solution.py:22
  80.9 21.6 %copy-start.16 = (bf16[1440,128]{1,0:T(8,128)(2,1)}, bf16[1440,128]{1,0:T(8,128)(2,1)S(1)}, u32[]{:S(2)}) copy-start(bf16[1440,128]{1,0:T(8,128)(2,1)S(1)} %fusion.2) | copy-start | bytes 1105924
  80.9 20.1 %collective-permute-start.7 = (bf16[1456,128]{1,0:T(8,128)(2,1)S(1)}, bf16[1456,128]{1,0:T(8,128)(2,1)S(1)}, u32[]{:S(2)}, u32[]{:S(2)}) collective-permute-start(bf16[1456,128]{1,0:T(8,128)(2,1)S(1)} %pad_maximum_fusion.refs_0_), channel_id=1, source_target_pairs={{0,8},{4,12},{8,0},{12,4},{1,9},{5,13},{9,1},{13,5},{2,10},{6,14},... | collective-permute-start | bytes 1118216 | tf_op jit(solution)/shard_map/ppermute | solution.py:22
  84.3 18.3 %collective-permute-start.10 = (bf16[1456,128]{1,0:T(8,128)(2,1)S(1)}, bf16[1456,128]{1,0:T(8,128)(2,1)S(1)}, u32[]{:S(2)}, u32[]{:S(2)}) collective-permute-start(bf16[1456,128]{1,0:T(8,128)(2,1)S(1)} %pad_maximum_fusion.refs_0_), channel_id=1, source_target_pairs={{0,2},{2,0},{1,3},{3,1},{4,6},{6,4},{5,7},{7,5},{8,10},{10,8},{9,1... | collective-permute-start | bytes 1118216 | tf_op jit(solution)/shard_map/ppermute | solution.py:22
  86.1 16.6 %collective-permute-start.8 = (bf16[1456,128]{1,0:T(8,128)(2,1)S(1)}, bf16[1456,128]{1,0:T(8,128)(2,1)S(1)}, u32[]{:S(2)}, u32[]{:S(2)}) collective-permute-start(bf16[1456,128]{1,0:T(8,128)(2,1)S(1)} %pad_maximum_fusion.refs_0_), channel_id=1, source_target_pairs={{0,4},{4,0},{8,12},{12,8},{1,5},{5,1},{9,13},{13,9},{2,6},{6,2},{1... | collective-permute-start | bytes 1118216 | tf_op jit(solution)/shard_map/ppermute | solution.py:22
  101.0 9.9 %collective-permute-start.11 = (bf16[1456,128]{1,0:T(8,128)(2,1)S(1)}, bf16[1456,128]{1,0:T(8,128)(2,1)S(1)}, u32[]{:S(2)}, u32[]{:S(2)}) collective-permute-start(bf16[1456,128]{1,0:T(8,128)(2,1)S(1)} %collective-permute-done.7.refs_1_), channel_id=1, source_target_pairs={{0,2},{2,0},{1,3},{3,1},{4,6},{6,4},{5,7},{7,5},{8,10},{10,8},{9,1... | collective-permute-start | bytes 1118216 | tf_op jit(solution)/shard_map/ppermute | solution.py:22
  102.5 9.5 %collective-permute-start.9 = (bf16[1456,128]{1,0:T(8,128)(2,1)S(1)}, bf16[1456,128]{1,0:T(8,128)(2,1)S(1)}, u32[]{:S(2)}, u32[]{:S(2)}) collective-permute-start(bf16[1456,128]{1,0:T(8,128)(2,1)S(1)} %collective-permute-done.7.refs_1_), channel_id=1, source_target_pairs={{0,4},{4,0},{8,12},{12,8},{1,5},{5,1},{9,13},{13,9},{2,6},{6,2},{1... | collective-permute-start | bytes 1118216 | tf_op jit(solution)/shard_map/ppermute | solution.py:22
  111.9 15.8 %copy-start.9 = (bf16[1456,128]{1,0:T(8,128)(2,1)}, bf16[1456,128]{1,0:T(8,128)(2,1)S(1)}, u32[]{:S(2)}) copy-start(bf16[1456,128]{1,0:T(8,128)(2,1)S(1)} %collective-permute-done.9.refs_1_) | copy-start | bytes 1118212
  111.9 16.6 %collective-permute-start.15 = (bf16[1456,128]{1,0:T(8,128)(2,1)S(1)}, bf16[1456,128]{1,0:T(8,128)(2,1)S(1)}, u32[]{:S(2)}, u32[]{:S(2)}) collective-permute-start(bf16[1456,128]{1,0:T(8,128)(2,1)S(1)} %collective-permute-done.8.refs_0_), channel_id=1, source_target_pairs={{0,2},{2,0},{1,3},{3,1},{4,6},{6,4},{5,7},{7,5},{8,10},{10,8},{9,1... | collective-permute-start | bytes 1118216 | tf_op jit(solution)/shard_map/ppermute | solution.py:22
  112.7 16.2 %collective-permute-start.16 = (bf16[1456,128]{1,0:T(8,128)(2,1)S(1)}, bf16[1456,128]{1,0:T(8,128)(2,1)S(1)}, u32[]{:S(2)}, u32[]{:S(2)}) collective-permute-start(bf16[1456,128]{1,0:T(8,128)(2,1)S(1)} %collective-permute-done.9.refs_1_), channel_id=1, source_target_pairs={{0,2},{2,0},{1,3},{3,1},{4,6},{6,4},{5,7},{7,5},{8,10},{10,8},{9,1... | collective-permute-start | bytes 1118216 | tf_op jit(solution)/shard_map/ppermute | solution.py:22
  114.0 3.4 %copy-start.1 = (bf16[1,2,2880,720]{2,3,1,0:T(8,128)(2,1)S(1)}, bf16[1,2,2880,720]{2,3,1,0:T(8,128)(2,1)}, u32[]{:S(2)}) copy-start(bf16[1,2,2880,720]{2,3,1,0:T(8,128)(2,1)} %param.18) | copy-start | bytes 24883204
  127.7 19.8 %collective-permute-start.13 = (bf16[2,720,256]{2,1,0:T(8,128)(2,1)}, bf16[2,720,256]{2,1,0:T(8,128)(2,1)}, u32[]{:S(2)}, u32[]{:S(2)}) collective-permute-start(bf16[2,720,256]{2,1,0:T(8,128)(2,1)} %get-tuple-element.59.refs_0_), channel_id=1, source_target_pairs={{0,2},{2,0},{1,3},{3,1},{4,6},{6,4},{5,7},{7,5},{8,10},{10,8},{9,1... | collective-permute-start | bytes 2211848 | tf_op jit(solution)/shard_map/ppermute | solution.py:22
  128.9 1.0 copy-start.10
  137.5 23.1 %collective-permute-start.17 = (bf16[2,720,256]{2,1,0:T(8,128)(2,1)S(1)}, bf16[2,720,256]{2,1,0:T(8,128)(2,1)}, u32[]{:S(2)}, u32[]{:S(2)}) collective-permute-start(bf16[2,720,256]{2,1,0:T(8,128)(2,1)S(1)} %get-tuple-element.71.refs_0_), channel_id=1, source_target_pairs={{0,2},{2,0},{1,3},{3,1},{4,6},{6,4},{5,7},{7,5},{8,10},{10,8},{9,1... | collective-permute-start | bytes 2211848 | tf_op jit(solution)/shard_map/ppermute | solution.py:22
  147.5 2.3 %copy-start.3 = (bf16[1440,1440]{1,0:T(8,128)(2,1)S(1)}, bf16[1440,1440]{1,0:T(8,128)(2,1)}, u32[]{:S(2)}) copy-start(bf16[1440,1440]{1,0:T(8,128)(2,1)} %copy-done.2) | copy-start | bytes 12441604
  149.8 2.3 %copy-start.5 = (bf16[1440,1440]{1,0:T(8,128)(2,1)S(1)}, bf16[1440,1440]{1,0:T(8,128)(2,1)}, u32[]{:S(2)}) copy-start(bf16[1440,1440]{1,0:T(8,128)(2,1)} %copy-done.4) | copy-start | bytes 12441604
  159.3 20.3 %collective-permute-start.14 = (bf16[1440,128]{1,0:T(8,128)(2,1)S(1)}, bf16[1440,128]{1,0:T(8,128)(2,1)S(1)}, u32[]{:S(2)}, u32[]{:S(2)}) collective-permute-start(bf16[1440,128]{1,0:T(8,128)(2,1)S(1)} %get-tuple-element.64), channel_id=1, source_target_pairs={{0,8},{4,12},{8,0},{12,4},{1,9},{5,13},{9,1},{13,5},{2,10},{6,14},... | collective-permute-start | bytes 1105928 | tf_op jit(solution)/shard_map/ppermute | solution.py:22
  160.6 10.3 %copy-start.17 = (bf16[1440,128]{1,0:T(8,128)(2,1)S(1)}, bf16[1440,128]{1,0:T(8,128)(2,1)}, u32[]{:S(2)}) copy-start(bf16[1440,128]{1,0:T(8,128)(2,1)} %copy-done.16) | copy-start | bytes 1105924
  167.7 19.8 %collective-permute-start.18 = (bf16[1440,128]{1,0:T(8,128)(2,1)S(1)}, bf16[1440,128]{1,0:T(8,128)(2,1)S(1)}, u32[]{:S(2)}, u32[]{:S(2)}) collective-permute-start(bf16[1440,128]{1,0:T(8,128)(2,1)S(1)} %get-tuple-element.73), channel_id=1, source_target_pairs={{0,4},{4,0},{8,12},{12,8},{1,5},{5,1},{9,13},{13,9},{2,6},{6,2},{1... | collective-permute-start | bytes 1105928 | tf_op jit(solution)/shard_map/ppermute | solution.py:22
  169.5 18.0 %collective-permute-start.19 = (bf16[1440,128]{1,0:T(8,128)(2,1)S(1)}, bf16[1440,128]{1,0:T(8,128)(2,1)S(1)}, u32[]{:S(2)}, u32[]{:S(2)}) collective-permute-start(bf16[1440,128]{1,0:T(8,128)(2,1)S(1)} %get-tuple-element.74), channel_id=1, source_target_pairs={{0,12},{4,8},{8,4},{12,0},{1,13},{5,9},{9,5},{13,1},{2,14},{6,10},... | collective-permute-start | bytes 1105928 | tf_op jit(solution)/shard_map/ppermute | solution.py:22

commit v11 on v10

--- a/solution.py
+++ b/solution.py
@@ -62,29 +62,25 @@
     return pltpu.CompilerParams(vmem_limit_bytes=VMEM_BYTES)
 
 
-def attention_kernel(place_ref, sink_ref, q_ref, earlier_ref, k_ref, v_ref, routes_ref, scores_ref, out_ref):
-    width = q_ref.shape[1]
-    numbers = [routes_ref[...], scores_ref[...] // 256, scores_ref[...] % 256]
-    numbers.append(jnp.zeros((out_ref.shape[0] - width - 3 * TOP, q_ref.shape[0]), jnp.int32))
-    out_ref[width:, :] = jnp.concatenate(numbers, axis=0).astype(jnp.float32).astype(jnp.bfloat16)
+def attention_kernel(sink_ref, q_ref, earlier_ref, own_ref, out_ref):
     rows = q_ref.shape[0]
-    kv_count = k_ref.shape[1] // HD
+    kv_count = own_ref.shape[1] // (2 * HD)
     pairs = q_ref.shape[1] // (2 * HD * kv_count)
     key = lax.broadcasted_iota(jnp.int32, (rows, rows), 0)
     query = lax.broadcasted_iota(jnp.int32, (rows, rows), 1)
     before = key > query
-    shut = before & (place_ref[0] == 1)
+    shut = before & (sink_ref[0] == 1.0)
     blank = jnp.zeros((2 * rows, HD), jnp.bfloat16)
     values = jnp.concatenate(
         [
             block.astype(jnp.float32).T.astype(jnp.bfloat16)
-            for block in (earlier_ref[:, kv_count * HD :], v_ref[...])
+            for block in (earlier_ref[:, kv_count * HD :], own_ref[:, kv_count * HD :])
         ],
         axis=1,
     )
     for g in range(kv_count):
         head = slice(g * HD, (g + 1) * HD)
-        keys = jnp.concatenate([earlier_ref[:, head], k_ref[:, head]], axis=0) * jnp.bfloat16(HD ** (-0.5))
+        keys = jnp.concatenate([earlier_ref[:, head], own_ref[:, head]], axis=0) * jnp.bfloat16(HD ** (-0.5))
         keys = jnp.concatenate(
             [jnp.concatenate([keys, blank], axis=1), jnp.concatenate([blank, keys], axis=1)], axis=0
         )
@@ -98,7 +94,7 @@
             )
             weights = []
             for side in range(2):
-                sink = sink_ref[(g * pairs + i) * 2 + side]
+                sink = sink_ref[1 + (g * pairs + i) * 2 + side]
                 part = products[side * 2 * rows : (side + 1) * 2 * rows]
                 scores = jnp.where(before, part[:rows], part[rows:])
                 scores = jnp.where(shut, -1e30, scores)
@@ -120,33 +116,35 @@
             out_ref[start + HD : start + 2 * HD, :] = result[:, rows:]
 
 
-def attention(queries, earlier, key_rows, value_rows, sink_logits, first, routes, scores):
+def attention(queries, earlier, paired, sinks):
     rows, width = queries.shape
     return pl.pallas_call(
         attention_kernel,
-        out_shape=jax.ShapeDtypeStruct((width + 16, rows), jnp.bfloat16),
-        in_specs=[in_smem(), in_smem()] + in_vmem(6),
+        out_shape=jax.ShapeDtypeStruct((width, rows), jnp.bfloat16),
+        in_specs=[in_smem()] + in_vmem(3),
         out_specs=in_vmem(1)[0],
         compiler_params=params(),
         cost_estimate=cost(8 * rows * rows * width, 6 * rows * width),
         name="attention",
-    )(first, sink_logits, queries, earlier, key_rows, value_rows, routes, scores)
-
-
-def flip(arrays):
+    )(sinks, queries, earlier, paired)
+
+
+def flip(arrays, ahead):
+    count = len(arrays)
+
     def kernel(*refs):
-        for i in range(len(arrays)):
-            refs[len(arrays) + i][...] = refs[i][...].T
+        for i in range(count):
+            refs[count + len(ahead) + i][...] = refs[i][...].T
 
     return pl.pallas_call(
         kernel,
         out_shape=tuple(jax.ShapeDtypeStruct(a.shape[::-1], a.dtype) for a in arrays),
-        in_specs=in_vmem(len(arrays)),
-        out_specs=tuple(in_vmem(len(arrays))),
+        in_specs=in_vmem(count + len(ahead)),
+        out_specs=tuple(in_vmem(count)),
         compiler_params=params(),
         cost_estimate=cost(0, 4 * sum(a.size for a in arrays)),
         name="flip",
-    )(*arrays)
+    )(*arrays, *ahead)
 
 
 def project(attended, weights, t, s, t_count):
@@ -272,18 +270,12 @@
     experts, units, lanes = activated[0].shape
     width = weights[0].shape[0]
     rows = lanes // slots
-    cuts = cuts_of([()], width, 3)
 
     def kernel(t_ref, *refs):
         activated_refs = refs[:t_count]
         share_ref = refs[t_count]
         weight_refs = refs[t_count + 1 : t_count + 1 + experts]
-        *out_refs, all_ref, stage_ref, held_ref, arrived = refs[t_count + 1 + experts :]
-        copies = [
-            fetches(weight_refs[e], held_ref.at[e - 1], arrived.at[e - 1], cuts) for e in range(1, experts)
-        ]
-        for copy in sum(copies, []):
-            copy.start()
+        *out_refs, all_ref, stage_ref = refs[t_count + 1 + experts :]
         for u in range(t_count):
             index = t_ref[0] ^ u
             if aligned(units):
@@ -295,11 +287,7 @@
                 all_ref[:, index * units : (index + 1) * units, :] = stage_ref[index]
         total = 0.0
         for e in range(experts):
-            if e:
-                for copy in copies[e - 1]:
-                    copy.wait()
-            weight_ref = held_ref.at[e - 1] if e else weight_refs[0]
-            result = dot(weight_ref[...], all_ref[e]).astype(jnp.bfloat16).astype(jnp.float32)
+            result = dot(weight_refs[e][...], all_ref[e]).astype(jnp.bfloat16).astype(jnp.float32)
             total = total + share_ref[e : e + 1, :] * result
         for j in range(slots):
             out_refs[j][...] = total[:, j * rows : (j + 1) * rows].astype(jnp.bfloat16)
@@ -307,15 +295,11 @@
     return pl.pallas_call(
         kernel,
         out_shape=tuple(jax.ShapeDtypeStruct((width, rows), jnp.bfloat16) for _ in range(slots)),
-        in_specs=[in_smem()]
-        + in_vmem(t_count + 2)
-        + [pl.BlockSpec(memory_space=pl.ANY)] * (experts - 1),
+        in_specs=[in_smem()] + in_vmem(t_count + 1 + experts),
         out_specs=tuple(in_vmem(slots)),
         scratch_shapes=[
             pltpu.VMEM((experts, t_count * units, lanes), jnp.bfloat16),
             pltpu.VMEM((1, 1, 16, 128) if aligned(units) else (t_count, experts, units, lanes), jnp.bfloat16),
-            pltpu.VMEM((max(1, experts - 1), width, t_count * units), jnp.bfloat16),
-            pltpu.SemaphoreType.DMA((max(1, experts - 1), len(cuts))),
         ],
         compiler_params=params(),
         cost_estimate=cost(
@@ -352,7 +336,12 @@
     out_weight = out_weight.T
     depth = out_weight.shape[1] // s_count
     near = lax.dynamic_slice_in_dim(out_weight, s * depth, depth, 1)
+    scores = route_scores.T
+    numbers = [routes.T, scores // 256, scores % 256, jnp.zeros((16 - 3 * TOP, rows), jnp.int32)]
     residual = picked(residual.T.reshape(slots, group * columns, rows), pair ^ t, 0)
+    residual = jnp.concatenate([residual, jnp.concatenate(numbers, axis=0).astype(jnp.bfloat16)], axis=0)
+    first = lax.axis_index(("ep", "sub")) == 0
+    sinks = jnp.concatenate([first.astype(jnp.float32).reshape(1), sink_logits])
     earlier, near, residual, expert_in, expert_out = lax.optimization_barrier(
         (earlier, near, residual, expert_in, expert_out)
     )
@@ -370,15 +359,13 @@
     experts_out = [expert_out] + [swapped(expert_out, "sub", e) for e in range(1, s_count)]
     chosen = [z * s_count + (s ^ e) for e in range(s_count)]
 
-    first = (lax.axis_index(("ep", "sub")) == 0).astype(jnp.int32).reshape(1)
-    attended = attention(
-        queries, earlier, key_rows, value_rows, sink_logits, first, routes.T, route_scores.T
-    )
+    attended = attention(queries, earlier, paired, sinks)
+    attended, residual = lax.optimization_barrier((attended, residual))
     gathered = [attended] + [swapped(attended, "ep", group * j) for j in range(1, slots)]
     experts_out, _ = lax.optimization_barrier((experts_out, attended))
-    experts_out = flip(experts_out)
-
-    gathered, near, residual, experts_out = lax.optimization_barrier((gathered, near, residual, experts_out))
+    experts_out = flip(experts_out, [out_weight, expert_in])
+
+    gathered, near, experts_out = lax.optimization_barrier((gathered, near, experts_out))
     near_weights = [near] + [swapped(near, "sub", u) for u in range(1, s_count)]
     mine = project(gathered, [out_weight], t, s * 0, t_count)
     other = project(gathered, near_weights, t, s, t_count)
@@ -387,15 +374,12 @@
     def ordered(a, b):
         return jnp.concatenate([jnp.where(first_member, a, b), jnp.where(first_member, b, a)], axis=0)
 
-    kept_routes = gathered[0][queries.shape[1] :]
-    for j in range(1, slots):
-        kept_routes = jnp.where(t == j, gathered[j][queries.shape[1] :], kept_routes)
-    hidden = ordered(mine[0], other[0]) + residual.astype(jnp.float32)
+    hidden = ordered(mine[0], other[0]) + residual[: group * columns].astype(jnp.float32)
     for m in range(1, t_count):
         received = swapped(ordered(mine[1][m - 1], other[1][m - 1]), "tp", m)
         hidden = hidden + received.astype(jnp.float32)
     gain_part = picked(norm_gain.reshape(slots, group * columns), pair, 0)
-    scaled = jnp.concatenate([(hidden * gain_part[:, None]).astype(jnp.bfloat16), kept_routes], axis=0)
+    scaled = jnp.concatenate([(hidden * gain_part[:, None]).astype(jnp.bfloat16), residual[group * columns :]], axis=0)
 
     own = {0: scaled}
     pieces = [own] + [{} for m in range(1, t_count)]

time: 189 us -> 209 us (1.11)
  starting transfers between devices: 35.2 us -> 48.3 us
  Pallas kernels: 46.5 us -> 39.8 us
  local copies, waits for them, and re-layouts: 25.6 us -> 31.1 us
  waiting for transfers between devices: 78 us -> 82.7 us
  other arithmetic: 2.97 us -> 5.55 us
    ppermute x18, starting transfers between devices: 31.2 us -> 41.6 us  [swapped(): lax.ppermute(block, axis, [(i, i ^ distance) for i in range(lax.axis_size...]
    pallas_call x2, Pallas kernels: 14.3 us -> 7.66 us  [combine(): pl.pallas_call(kernel, out_shape=tuple((jax.ShapeDtypeStruct((width, rows...]
    ppermute x18, waiting for transfers between devices: 78 us -> 82.7 us  [swapped(): lax.ppermute(block, axis, [(i, i ^ distance) for i in range(lax.axis_size...]
    concatenate x0 -> x2, local copies, waits for them, and re-layouts: none -> 3.38 us  [the longest x1 2.54 us: local(): jnp.concatenate([residual, jnp.concatenate(numbers, axis=0).astype(jnp.bf...]
    ppermute x1, starting transfers between devices: 1.64 us -> 4.41 us  [local(): residual = lax.ppermute(residual, ('ep', 'tp'), route)]
    unnamed x42 -> x39, local copies, waits for them, and re-layouts: 21.9 us -> 24.1 us
  transfers between devices with their start and end apart: 20 -> 20, of which waited for: 10 -> 11; matrix products, arithmetic and copies ran while one was open for 3% -> 5% of each run, Pallas kernels for 25% -> 19%
where the time goes in v11:
time: 209 us; the launch traced here: 208 us
  waiting for transfers between devices  82.7 us (40%)
  starting transfers between devices  48.3 us (23%)
  Pallas kernels  39.8 us (19%)
  local copies, waits for them, and re-layouts  31.1 us (15%)
  other arithmetic  5.55 us (3%)
    ppermute x18, waiting for transfers between devices, swapped(): lax.ppermute(block, axis, [(i, i ^ distance) for i in range(lax.axis_size...  82.7 us
    ppermute x18, starting transfers between devices, swapped(): lax.ppermute(block, axis, [(i, i ^ distance) for i in range(lax.axis_size...  41.6 us
    unnamed x39, local copies, waits for them, and re-layouts  24.1 us
    pallas_call x2, Pallas kernels, activate(): pl.pallas_call(kernel, out_shape=(jax.ShapeDtypeStruct((experts, units, l...  17.9 us
    pallas_call x2, Pallas kernels, combine(): pl.pallas_call(kernel, out_shape=tuple((jax.ShapeDtypeStruct((width, rows...  7.66 us
    pallas_call x1, Pallas kernels, attention(): pl.pallas_call(attention_kernel, out_shape=jax.ShapeDtypeStruct((width, r...  5.55 us
    pallas_call x1, Pallas kernels, flip(): pl.pallas_call(kernel, out_shape=tuple((jax.ShapeDtypeStruct(a.shape[::-1...  4.73 us
    ppermute x1, starting transfers between devices, local(): residual = lax.ppermute(residual, ('ep', 'tp'), route)  4.41 us
  transfers between devices with their start and end apart: 20, of which 11 were waited for; matrix products, arithmetic and copies ran while one was open for 5% of the time, Pallas kernels for 19%

profile of v11, /device:TPU:0, one launch (start us, length us, event | category | flops | bytes accessed | tf_op | source)
XLA Modules:
  0.0 207.8 jit_solution(4013488933160624218)
XLA Ops:
  0.0 0.9 constant_dynamic-update-slice_fusion.1
  1.0 0.8 constant_dynamic-update-slice_fusion.own_ref
  1.8 2.4 %collective-permute-start = (bf16[128,512]{1,0:T(8,128)(2,1)S(1)}, bf16[128,512]{1,0:T(8,128)(2,1)S(1)}, u32[]{:S(2)}, u32[]{:S(2)}) collective-permute-start(bf16[128,512]{1,0:T(8,128)(2,1)S(1)} %constant_dynamic-update-slice_fusion.own_ref), channel_id=1, source_target_pairs={{0,1},{1,4},{4,5},{5,8},{8,9},{9,12},{12,13},{2,3},{3,6},{6,7},{7,... | collective-permute-start | bytes 393224 | tf_op jit(solution)/shard_map/ppermute | solution.py:18
  5.6 2.5 %concatenate.26 = bf16[1456,128]{1,0:T(8,128)(2,1)} concatenate(bf16[1440,128]{1,0:T(8,128)(2,1)S(1)} %dynamic-slice_bitcast_fusion.1, bf16[4,128]{1,0:T(4,128)(2,1)S(1)} %convert_bitcast_fusion, bf16[4,128]{1,0:T(4,128)(2,1)S(1)} %get-tuple-element.85, bf16[4,128]{1,0:T(4,128)(2,1)S(1)} %get-tuple-element.84, bf16[4,128]{1,0:T(4,128)(2,1)S(1)} %broadcast.25), dimensions={0} | concatenate | bytes 745472 | tf_op jit(solution)/shard_map/concatenate | solution.py:342
  8.1 2.6 %dynamic-slice_bitcast_fusion = bf16[720,1024]{1,0:T(8,128)(2,1)} fusion(bf16[2048,720]{0,1:T(8,128)(2,1)} %param.15, s32[]{:T(128)S(6)} %select_n.96), kind=kLoop, calls=%fused_computation | loop fusion | bytes 2949124 | tf_op jit(solution)/shard_map/dynamic_slice | solution.py:338
  10.8 2.7 %collective-permute-start.4 = (bf16[1440,1440]{1,0:T(8,128)(2,1)}, bf16[1440,1440]{1,0:T(8,128)(2,1)}, u32[]{:S(2)}, u32[]{:S(2)}) collective-permute-start(bf16[1440,1440]{1,0:T(8,128)(2,1)} %bitcast.55), channel_id=1, source_target_pairs={{0,1},{1,0},{2,3},{3,2},{4,5},{5,4},{6,7},{7,6},{8,9},{9,8},{10,11... | collective-permute-start | bytes 12441608 | tf_op jit(solution)/shard_map/ppermute | solution.py:22
  13.5 1.6 collective-permute-start.3
  15.0 4.4 %collective-permute-start.1 = (bf16[1456,128]{1,0:T(8,128)(2,1)}, bf16[1456,128]{1,0:T(8,128)(2,1)}, u32[]{:S(2)}, u32[]{:S(2)}) collective-permute-start(bf16[1456,128]{1,0:T(8,128)(2,1)} %concatenate.26), channel_id=1, source_target_pairs={{0,0},{2,10},{4,4},{6,14},{8,8},{10,2},{12,12},{14,6},{1,1},{3,11}... | collective-permute-start | bytes 1118216 | tf_op jit(solution)/shard_map/ppermute | solution.py:354
  19.5 5.5 %attention.1.refs_0_ = bf16[2048,128]{1,0:T(8,128)(2,1)S(1)} custom-call(f32[33]{0:T(128)S(1)} %pad_maximum_fusion.2.sink_ref, bf16[128,2048]{1,0:T(8,128)(2,1)S(1)} %copy-done.10, bf16[128,512]{1,0:T(8,128)(2,1)S(1)} %collective-permute-done.earlier_ref, bf16[128,512]{1,0:T(8,128)(2,1)S(1)} %constant_dynamic-update-slice_fusion.own_ref), custom_call_target="tpu_custom_call" | custom-call | flops 268435456 | bytes 1572864 | tf_op jit(solution)/shard_map/attention/pallas_call | solution.py:121
  25.1 1.5 collective-permute-start.2
  26.6 3.4 %copy-done.1 = bf16[1,2,2880,720]{2,3,1,0:T(8,128)(2,1)S(1)} copy-done((bf16[1,2,2880,720]{2,3,1,0:T(8,128)(2,1)S(1)}, bf16[1,2,2880,720]{2,3,1,0:T(8,128)(2,1)}, u32[]{:S(2)}) %copy-start.1) | copy-done | bytes 8294424
  30.0 1.8 copy-done.3
  31.8 2.3 %copy-done.9 = bf16[1,1440,1440]{2,1,0:T(8,128)(2,1)S(1)} copy-done((bf16[1,1440,1440]{2,1,0:T(8,128)(2,1)S(1)}, bf16[1,1440,1440]{2,1,0:T(8,128)(2,1)}, u32[]{:S(2)}) %copy-start.9) | copy-done | bytes 4147224
  34.1 4.7 %flip.1 = (bf16[1440,1440]{1,0:T(8,128)(2,1)S(1)}, bf16[1440,1440]{1,0:T(8,128)(2,1)S(1)}) custom-call(bf16[1440,1440]{1,0:T(8,128)(2,1)S(1)} %bitcast.56, bf16[1440,1440]{1,0:T(8,128)(2,1)} %collective-permute-done.4.refs_1_, bf16[720,2048]{1,0:T(8,128)(2,1)S(1)} %bitcast.53, bf16[2,720,2880]{2,1,0:T(8,128)(2,1)S(1)} %bitcast.50), custom_call_target="tpu_custom_call" | custom-call | bytes 16588800 | tf_op jit(solution)/shard_map/flip/pallas_call | solution.py:139
  38.8 2.1 %copy-done.5 = bf16[1440,1440]{1,0:T(8,128)(2,1)} copy-done((bf16[1440,1440]{1,0:T(8,128)(2,1)}, bf16[1440,1440]{1,0:T(8,128)(2,1)S(1)}, u32[]{:S(2)}) %copy-start.5) | copy-done | bytes 4147224
  41.0 2.0 copy-done.7
  43.0 15.7 %collective-permute-done.2.refs_1_ = bf16[2048,128]{1,0:T(8,128)(2,1)S(1)} collective-permute-done((bf16[2048,128]{1,0:T(8,128)(2,1)S(1)}, bf16[2048,128]{1,0:T(8,128)(2,1)S(1)}, u32[]{:S(2)}, u32[]{:S(2)}) %collective-permute-start.2) | collective-permute-done | bytes 524320 | tf_op jit(solution)/shard_map/ppermute | solution.py:22
  58.7 0.9 collective-permute-done.3.refs_2_
  59.8 1.8 copy-done.4
  61.6 1.5 project.2
  63.1 2.5 %project.3 = (f32[720,128]{1,0:T(8,128)S(1)}, bf16[1,720,128]{2,1,0:T(8,128)(2,1)S(1)}) custom-call(s32[2]{0:T(128)S(1)} %pad_add_fusion.1.place_ref, bf16[2048,128]{1,0:T(8,128)(2,1)S(1)} %attention.1.refs_0_, bf16[2048,128]{1,0:T(8,128)(2,1)S(1)} %collective-permute-done.2.refs_1_, bf16[720,1024]{1,0:T(8,128)(2,1)S(1)} %collective-permute-done.3.refs_2_, ...), custom_call_target="tpu_custom_call" | custom-call | flops 754974720 | bytes 2949120 | tf_op jit(solution)/shard_map/project/pallas_call | solution.py:175
  65.7 0.7 copy-done.14
  66.5 23.9 %collective-permute-start.6 = (bf16[1440,128]{1,0:T(8,128)(2,1)S(1)}, bf16[1440,128]{1,0:T(8,128)(2,1)S(1)}, u32[]{:S(2)}, u32[]{:S(2)}) collective-permute-start(bf16[1440,128]{1,0:T(8,128)(2,1)S(1)} %pad_maximum_fusion.1), channel_id=1, source_target_pairs={{0,2},{2,0},{1,3},{3,1},{4,6},{6,4},{5,7},{7,5},{8,10},{10,8},{9,1... | collective-permute-start | bytes 1105928 | tf_op jit(solution)/shard_map/ppermute | solution.py:22
  91.2 1.1 broadcast_select_fusion.1
  92.4 7.3 %collective-permute-done.6 = bf16[1440,128]{1,0:T(8,128)(2,1)S(1)} collective-permute-done((bf16[1440,128]{1,0:T(8,128)(2,1)S(1)}, bf16[1440,128]{1,0:T(8,128)(2,1)S(1)}, u32[]{:S(2)}, u32[]{:S(2)}) %collective-permute-start.6) | collective-permute-done | bytes 368672 | tf_op jit(solution)/shard_map/ppermute | solution.py:22
  99.7 1.3 fusion.2
  101.2 1.7 collective-permute-start.10
  103.0 3.0 %collective-permute-start.8 = (bf16[1456,128]{1,0:T(8,128)(2,1)S(1)}, bf16[1456,128]{1,0:T(8,128)(2,1)S(1)}, u32[]{:S(2)}, u32[]{:S(2)}) collective-permute-start(bf16[1456,128]{1,0:T(8,128)(2,1)S(1)} %pad_maximum_fusion.refs_0_), channel_id=1, source_target_pairs={{0,4},{4,0},{8,12},{12,8},{1,5},{5,1},{9,13},{13,9},{2,6},{6,2},{1... | collective-permute-start | bytes 1118216 | tf_op jit(solution)/shard_map/ppermute | solution.py:22
  106.0 14.4 %collective-permute-done.7.refs_1_ = bf16[1456,128]{1,0:T(8,128)(2,1)S(1)} collective-permute-done((bf16[1456,128]{1,0:T(8,128)(2,1)S(1)}, bf16[1456,128]{1,0:T(8,128)(2,1)S(1)}, u32[]{:S(2)}, u32[]{:S(2)}) %collective-permute-start.7) | collective-permute-done | bytes 372768 | tf_op jit(solution)/shard_map/ppermute | solution.py:22
  120.4 1.5 collective-permute-start.11
  122.1 8.8 %collective-permute-done.11.refs_3_ = bf16[1456,128]{1,0:T(8,128)(2,1)S(1)} collective-permute-done((bf16[1456,128]{1,0:T(8,128)(2,1)S(1)}, bf16[1456,128]{1,0:T(8,128)(2,1)S(1)}, u32[]{:S(2)}, u32[]{:S(2)}) %collective-permute-start.11) | collective-permute-done | bytes 372768 | tf_op jit(solution)/shard_map/ppermute | solution.py:22
  130.9 1.3 collective-permute-done.9.refs_1_
  132.7 1.5 collective-permute-start.16
  134.2 3.4 %copy-done.2 = bf16[1,2,2880,720]{2,3,1,0:T(8,128)(2,1)S(1)} copy-done((bf16[1,2,2880,720]{2,3,1,0:T(8,128)(2,1)S(1)}, bf16[1,2,2880,720]{2,3,1,0:T(8,128)(2,1)}, u32[]{:S(2)}) %copy-start.2) | copy-done | bytes 8294424
  137.6 10.3 %activate.2 = (bf16[2,720,256]{2,1,0:T(8,128)(2,1)}, f32[2,256]{1,0:T(2,128)S(1)}) custom-call(s32[4]{0:T(128)S(1)} %pad_add_fusion.2.place_ref, bf16[1456,128]{1,0:T(8,128)(2,1)S(1)} %pad_maximum_fusion.refs_0_, bf16[1456,128]{1,0:T(8,128)(2,1)S(1)} %collective-permute-done.7.refs_1_, bf16[1456,128]{1,0:T(8,128)(2,1)S(1)} %collective-permute-done.10.refs_2_, ...), custom_call_target="tpu_custom_call" | custom-call | flops 4246732800 | bytes 16588800 | tf_op jit(solution)/shard_map/activate/pallas_call | solution.py:245
  148.5 1.4 collective-permute-done.16.refs_3_
  150.0 1.0 copy-done.12
  150.9 7.5 %activate.3 = (bf16[2,720,256]{2,1,0:T(8,128)(2,1)S(1)}, f32[2,256]{1,0:T(2,128)S(1)}) custom-call(s32[4]{0:T(128)S(1)} %pad_add_fusion.2.place_ref, bf16[1456,128]{1,0:T(8,128)(2,1)S(1)} %collective-permute-done.8.refs_0_, bf16[1456,128]{1,0:T(8,128)(2,1)S(1)} %copy-done.12, bf16[1456,128]{1,0:T(8,128)(2,1)S(1)} %collective-permute-done.15.refs_2_, ...), custom_call_target="tpu_custom_call" | custom-call | flops 4246732800 | bytes 16588800 | tf_op jit(solution)/shard_map/activate/pallas_call | solution.py:245
  159.2 8.5 %collective-permute-done.13.refs_1_ = bf16[2,720,256]{2,1,0:T(8,128)(2,1)} collective-permute-done((bf16[2,720,256]{2,1,0:T(8,128)(2,1)}, bf16[2,720,256]{2,1,0:T(8,128)(2,1)}, u32[]{:S(2)}, u32[]{:S(2)}) %collective-permute-start.13) | collective-permute-done | bytes 737312 | tf_op jit(solution)/shard_map/ppermute | solution.py:22
  167.8 2.3 %copy-done.6 = bf16[1440,1440]{1,0:T(8,128)(2,1)S(1)} copy-done((bf16[1440,1440]{1,0:T(8,128)(2,1)S(1)}, bf16[1440,1440]{1,0:T(8,128)(2,1)}, u32[]{:S(2)}) %copy-start.6) | copy-done | bytes 4147224
  170.0 2.3 %copy-done.8 = bf16[1440,1440]{1,0:T(8,128)(2,1)S(1)} copy-done((bf16[1440,1440]{1,0:T(8,128)(2,1)S(1)}, bf16[1440,1440]{1,0:T(8,128)(2,1)}, u32[]{:S(2)}) %copy-start.8) | copy-done | bytes 4147224
  172.3 3.9 %combine.2 = (bf16[1440,128]{1,0:T(8,128)(2,1)S(1)}, bf16[1440,128]{1,0:T(8,128)(2,1)S(1)}) custom-call(s32[1]{0:T(128)} %bitcast.t_ref, bf16[2,720,256]{2,1,0:T(8,128)(2,1)} %get-tuple-element.61.refs_0_, bf16[2,720,256]{2,1,0:T(8,128)(2,1)} %collective-permute-done.13.refs_1_, f32[2,256]{1,0:T(2,128)S(1)} %get-tuple-element.62.refs_2_, ...), custom_call_target="tpu_custom_call" | custom-call | flops 2123366400 | bytes 8294400 | tf_op jit(solution)/shard_map/combine/pallas_call | solution.py:295
  176.4 4.8 %collective-permute-done.17.refs_1_ = bf16[2,720,256]{2,1,0:T(8,128)(2,1)} collective-permute-done((bf16[2,720,256]{2,1,0:T(8,128)(2,1)S(1)}, bf16[2,720,256]{2,1,0:T(8,128)(2,1)}, u32[]{:S(2)}, u32[]{:S(2)}) %collective-permute-start.17) | collective-permute-done | bytes 737312 | tf_op jit(solution)/shard_map/ppermute | solution.py:22
  181.2 3.7 %combine.3 = (bf16[1440,128]{1,0:T(8,128)(2,1)S(1)}, bf16[1440,128]{1,0:T(8,128)(2,1)S(1)}) custom-call(s32[1]{0:T(128)} %bitcast.t_ref, bf16[2,720,256]{2,1,0:T(8,128)(2,1)S(1)} %get-tuple-element.73.refs_0_, bf16[2,720,256]{2,1,0:T(8,128)(2,1)} %collective-permute-done.17.refs_1_, f32[2,256]{1,0:T(2,128)S(1)} %get-tuple-element.74.refs_2_, ...), custom_call_target="tpu_custom_call" | custom-call | flops 2123366400 | bytes 8294400 | tf_op jit(solution)/shard_map/combine/pallas_call | solution.py:295
  185.7 1.4 collective-permute-start.19
  187.3 7.0 %collective-permute-done.14 = bf16[1440,128]{1,0:T(8,128)(2,1)S(1)} collective-permute-done((bf16[1440,128]{1,0:T(8,128)(2,1)S(1)}, bf16[1440,128]{1,0:T(8,128)(2,1)S(1)}, u32[]{:S(2)}, u32[]{:S(2)}) %collective-permute-start.14) | collective-permute-done | bytes 368672 | tf_op jit(solution)/shard_map/ppermute | solution.py:22
  194.4 12.5 %collective-permute-done.18 = bf16[1440,128]{1,0:T(8,128)(2,1)S(1)} collective-permute-done((bf16[1440,128]{1,0:T(8,128)(2,1)S(1)}, bf16[1440,128]{1,0:T(8,128)(2,1)S(1)}, u32[]{:S(2)}, u32[]{:S(2)}) %collective-permute-start.18) | collective-permute-done | bytes 368672 | tf_op jit(solution)/shard_map/ppermute | solution.py:22
  206.8 1.0 fusion.3
  (67 shorter events, 5.9 us)
Async XLA Ops:
  0.0 5.6 %copy-start = (bf16[128,2880]{0,1:T(8,128)(2,1)S(1)}, bf16[128,2880]{0,1:T(8,128)(2,1)}, u32[]{:S(2)}) copy-start(bf16[128,2880]{0,1:T(8,128)(2,1)} %param.16) | copy-start | bytes 2211844
  0.0 19.5 %copy-start.18 = (f32[32]{0:T(128)S(1)}, f32[32]{0:T(128)}, u32[]{:S(2)}) copy-start(f32[32]{0:T(128)} %param.14) | copy-start | bytes 388
  0.0 19.5 %copy-start.10 = (bf16[128,2048]{1,0:T(8,128)(2,1)S(1)}, bf16[128,2048]{1,0:T(8,128)(2,1)}, u32[]{:S(2)}) copy-start(bf16[128,2048]{1,0:T(8,128)(2,1)} %q_ref.1) | copy-start | bytes 1572868
  1.8 9.0 %collective-permute-start = (bf16[128,512]{1,0:T(8,128)(2,1)S(1)}, bf16[128,512]{1,0:T(8,128)(2,1)S(1)}, u32[]{:S(2)}, u32[]{:S(2)}) collective-permute-start(bf16[128,512]{1,0:T(8,128)(2,1)S(1)} %constant_dynamic-update-slice_fusion.own_ref), channel_id=1, source_target_pairs={{0,1},{1,4},{4,5},{5,8},{8,9},{9,12},{12,13},{2,3},{3,6},{6,7},{7,... | collective-permute-start | bytes 393224 | tf_op jit(solution)/shard_map/ppermute | solution.py:18
  10.8 15.8 %collective-permute-start.4 = (bf16[1440,1440]{1,0:T(8,128)(2,1)}, bf16[1440,1440]{1,0:T(8,128)(2,1)}, u32[]{:S(2)}, u32[]{:S(2)}) collective-permute-start(bf16[1440,1440]{1,0:T(8,128)(2,1)} %bitcast.55), channel_id=1, source_target_pairs={{0,1},{1,0},{2,3},{3,2},{4,5},{5,4},{6,7},{7,6},{8,9},{9,8},{10,11... | collective-permute-start | bytes 12441608 | tf_op jit(solution)/shard_map/ppermute | solution.py:22
  13.5 120.8 %collective-permute-start.12 = (bf16[2,720,2880]{2,1,0:T(8,128)(2,1)}, bf16[2,720,2880]{2,1,0:T(8,128)(2,1)}, u32[]{:S(2)}, u32[]{:S(2)}) collective-permute-start(bf16[2,720,2880]{2,1,0:T(8,128)(2,1)} %bitcast.49), channel_id=1, source_target_pairs={{0,1},{1,0},{2,3},{3,2},{4,5},{5,4},{6,7},{7,6},{8,9},{9,8},{10,11... | collective-permute-start | bytes 24883208 | tf_op jit(solution)/shard_map/ppermute | solution.py:22
  13.5 46.1 %collective-permute-start.3 = (bf16[720,1024]{1,0:T(8,128)(2,1)}, bf16[720,1024]{1,0:T(8,128)(2,1)S(1)}, u32[]{:S(2)}, u32[]{:S(2)}) collective-permute-start(bf16[720,1024]{1,0:T(8,128)(2,1)} %dynamic-slice_bitcast_fusion), channel_id=1, source_target_pairs={{0,4},{4,0},{8,12},{12,8},{1,5},{5,1},{9,13},{13,9},{2,6},{6,2},{1... | collective-permute-start | bytes 4423688 | tf_op jit(solution)/shard_map/ppermute | solution.py:22
  15.0 10.1 %collective-permute-start.1 = (bf16[1456,128]{1,0:T(8,128)(2,1)}, bf16[1456,128]{1,0:T(8,128)(2,1)}, u32[]{:S(2)}, u32[]{:S(2)}) collective-permute-start(bf16[1456,128]{1,0:T(8,128)(2,1)} %concatenate.26), channel_id=1, source_target_pairs={{0,0},{2,10},{4,4},{6,14},{8,8},{10,2},{12,12},{14,6},{1,1},{3,11}... | collective-permute-start | bytes 1118216 | tf_op jit(solution)/shard_map/ppermute | solution.py:354
  25.1 33.6 %collective-permute-start.2 = (bf16[2048,128]{1,0:T(8,128)(2,1)S(1)}, bf16[2048,128]{1,0:T(8,128)(2,1)S(1)}, u32[]{:S(2)}, u32[]{:S(2)}) collective-permute-start(bf16[2048,128]{1,0:T(8,128)(2,1)S(1)} %attention.1.refs_0_), channel_id=1, source_target_pairs={{0,8},{4,12},{8,0},{12,4},{1,9},{5,13},{9,1},{13,5},{2,10},{6,14},... | collective-permute-start | bytes 1572872 | tf_op jit(solution)/shard_map/ppermute | solution.py:22
  26.6 3.4 %copy-start.1 = (bf16[1,2,2880,720]{2,3,1,0:T(8,128)(2,1)S(1)}, bf16[1,2,2880,720]{2,3,1,0:T(8,128)(2,1)}, u32[]{:S(2)}) copy-start(bf16[1,2,2880,720]{2,3,1,0:T(8,128)(2,1)} %param.18) | copy-start | bytes 24883204
  30.0 1.8 copy-start.3
  31.8 2.3 %copy-start.9 = (bf16[1,1440,1440]{2,1,0:T(8,128)(2,1)S(1)}, bf16[1,1440,1440]{2,1,0:T(8,128)(2,1)}, u32[]{:S(2)}) copy-start(bf16[1,1440,1440]{2,1,0:T(8,128)(2,1)} %param.19) | copy-start | bytes 12441604
  38.8 2.1 %copy-start.5 = (bf16[1440,1440]{1,0:T(8,128)(2,1)}, bf16[1440,1440]{1,0:T(8,128)(2,1)S(1)}, u32[]{:S(2)}) copy-start(bf16[1440,1440]{1,0:T(8,128)(2,1)S(1)} %get-tuple-element.63.refs_3_) | copy-start | bytes 12441604
  41.0 2.0 copy-start.7
  59.6 3.5 %collective-permute-start.5 = (bf16[720,1024]{1,0:T(8,128)(2,1)S(1)}, bf16[720,1024]{1,0:T(8,128)(2,1)}, u32[]{:S(2)}, u32[]{:S(2)}) collective-permute-start(bf16[720,1024]{1,0:T(8,128)(2,1)S(1)} %collective-permute-done.3.refs_2_), channel_id=1, source_target_pairs={{0,1},{1,0},{2,3},{3,2},{4,5},{5,4},{6,7},{7,6},{8,9},{9,8},{10,11... | collective-permute-start | bytes 4423688 | tf_op jit(solution)/shard_map/ppermute | solution.py:22
  59.8 1.8 copy-start.4
  61.6 28.8 %copy-start.17 = (f32[2880]{0:T(1024)S(1)}, f32[2880]{0:T(1024)}, u32[]{:S(2)}) copy-start(f32[2880]{0:T(1024)} %param.17) | copy-start | bytes 34564
  63.1 2.5 %copy-start.13 = (f32[720,128]{1,0:T(8,128)}, f32[720,128]{1,0:T(8,128)S(1)}, u32[]{:S(2)}) copy-start(f32[720,128]{1,0:T(8,128)S(1)} %get-tuple-element.53) | copy-start | bytes 1105924
  65.7 0.8 copy-start.14
  66.5 33.2 %collective-permute-start.6 = (bf16[1440,128]{1,0:T(8,128)(2,1)S(1)}, bf16[1440,128]{1,0:T(8,128)(2,1)S(1)}, u32[]{:S(2)}, u32[]{:S(2)}) collective-permute-start(bf16[1440,128]{1,0:T(8,128)(2,1)S(1)} %pad_maximum_fusion.1), channel_id=1, source_target_pairs={{0,2},{2,0},{1,3},{3,1},{4,6},{6,4},{5,7},{7,5},{8,10},{10,8},{9,1... | collective-permute-start | bytes 1105928 | tf_op jit(solution)/shard_map/ppermute | solution.py:22
  100.9 21.0 %copy-start.15 = (bf16[1440,128]{1,0:T(8,128)(2,1)}, bf16[1440,128]{1,0:T(8,128)(2,1)S(1)}, u32[]{:S(2)}) copy-start(bf16[1440,128]{1,0:T(8,128)(2,1)S(1)} %fusion.2) | copy-start | bytes 1105924
  101.0 19.4 %collective-permute-start.7 = (bf16[1456,128]{1,0:T(8,128)(2,1)S(1)}, bf16[1456,128]{1,0:T(8,128)(2,1)S(1)}, u32[]{:S(2)}, u32[]{:S(2)}) collective-permute-start(bf16[1456,128]{1,0:T(8,128)(2,1)S(1)} %pad_maximum_fusion.refs_0_), channel_id=1, source_target_pairs={{0,8},{4,12},{8,0},{12,4},{1,9},{5,13},{9,1},{13,5},{2,10},{6,14},... | collective-permute-start | bytes 1118216 | tf_op jit(solution)/shard_map/ppermute | solution.py:22
  101.2 20.9 %collective-permute-start.10 = (bf16[1456,128]{1,0:T(8,128)(2,1)S(1)}, bf16[1456,128]{1,0:T(8,128)(2,1)S(1)}, u32[]{:S(2)}, u32[]{:S(2)}) collective-permute-start(bf16[1456,128]{1,0:T(8,128)(2,1)S(1)} %pad_maximum_fusion.refs_0_), channel_id=1, source_target_pairs={{0,2},{2,0},{1,3},{3,1},{4,6},{6,4},{5,7},{7,5},{8,10},{10,8},{9,1... | collective-permute-start | bytes 1118216 | tf_op jit(solution)/shard_map/ppermute | solution.py:22
  103.0 19.2 %collective-permute-start.8 = (bf16[1456,128]{1,0:T(8,128)(2,1)S(1)}, bf16[1456,128]{1,0:T(8,128)(2,1)S(1)}, u32[]{:S(2)}, u32[]{:S(2)}) collective-permute-start(bf16[1456,128]{1,0:T(8,128)(2,1)S(1)} %pad_maximum_fusion.refs_0_), channel_id=1, source_target_pairs={{0,4},{4,0},{8,12},{12,8},{1,5},{5,1},{9,13},{13,9},{2,6},{6,2},{1... | collective-permute-start | bytes 1118216 | tf_op jit(solution)/shard_map/ppermute | solution.py:22
  120.4 10.5 %collective-permute-start.11 = (bf16[1456,128]{1,0:T(8,128)(2,1)S(1)}, bf16[1456,128]{1,0:T(8,128)(2,1)S(1)}, u32[]{:S(2)}, u32[]{:S(2)}) collective-permute-start(bf16[1456,128]{1,0:T(8,128)(2,1)S(1)} %collective-permute-done.7.refs_1_), channel_id=1, source_target_pairs={{0,2},{2,0},{1,3},{3,1},{4,6},{6,4},{5,7},{7,5},{8,10},{10,8},{9,1... | collective-permute-start | bytes 1118216 | tf_op jit(solution)/shard_map/ppermute | solution.py:22
  121.9 10.3 %collective-permute-start.9 = (bf16[1456,128]{1,0:T(8,128)(2,1)S(1)}, bf16[1456,128]{1,0:T(8,128)(2,1)S(1)}, u32[]{:S(2)}, u32[]{:S(2)}) collective-permute-start(bf16[1456,128]{1,0:T(8,128)(2,1)S(1)} %collective-permute-done.7.refs_1_), channel_id=1, source_target_pairs={{0,4},{4,0},{8,12},{12,8},{1,5},{5,1},{9,13},{13,9},{2,6},{6,2},{1... | collective-permute-start | bytes 1118216 | tf_op jit(solution)/shard_map/ppermute | solution.py:22
  132.2 15.8 %copy-start.11 = (bf16[1456,128]{1,0:T(8,128)(2,1)}, bf16[1456,128]{1,0:T(8,128)(2,1)S(1)}, u32[]{:S(2)}) copy-start(bf16[1456,128]{1,0:T(8,128)(2,1)S(1)} %collective-permute-done.9.refs_1_) | copy-start | bytes 1118212
  132.2 16.3 %collective-permute-start.15 = (bf16[1456,128]{1,0:T(8,128)(2,1)S(1)}, bf16[1456,128]{1,0:T(8,128)(2,1)S(1)}, u32[]{:S(2)}, u32[]{:S(2)}) collective-permute-start(bf16[1456,128]{1,0:T(8,128)(2,1)S(1)} %collective-permute-done.8.refs_0_), channel_id=1, source_target_pairs={{0,2},{2,0},{1,3},{3,1},{4,6},{6,4},{5,7},{7,5},{8,10},{10,8},{9,1... | collective-permute-start | bytes 1118216 | tf_op jit(solution)/shard_map/ppermute | solution.py:22
  132.7 17.3 %collective-permute-start.16 = (bf16[1456,128]{1,0:T(8,128)(2,1)S(1)}, bf16[1456,128]{1,0:T(8,128)(2,1)S(1)}, u32[]{:S(2)}, u32[]{:S(2)}) collective-permute-start(bf16[1456,128]{1,0:T(8,128)(2,1)S(1)} %collective-permute-done.9.refs_1_), channel_id=1, source_target_pairs={{0,2},{2,0},{1,3},{3,1},{4,6},{6,4},{5,7},{7,5},{8,10},{10,8},{9,1... | collective-permute-start | bytes 1118216 | tf_op jit(solution)/shard_map/ppermute | solution.py:22
  134.2 3.4 %copy-start.2 = (bf16[1,2,2880,720]{2,3,1,0:T(8,128)(2,1)S(1)}, bf16[1,2,2880,720]{2,3,1,0:T(8,128)(2,1)}, u32[]{:S(2)}) copy-start(bf16[1,2,2880,720]{2,3,1,0:T(8,128)(2,1)} %param.18) | copy-start | bytes 24883204
  148.0 19.8 %collective-permute-start.13 = (bf16[2,720,256]{2,1,0:T(8,128)(2,1)}, bf16[2,720,256]{2,1,0:T(8,128)(2,1)}, u32[]{:S(2)}, u32[]{:S(2)}) collective-permute-start(bf16[2,720,256]{2,1,0:T(8,128)(2,1)} %get-tuple-element.61.refs_0_), channel_id=1, source_target_pairs={{0,2},{2,0},{1,3},{3,1},{4,6},{6,4},{5,7},{7,5},{8,10},{10,8},{9,1... | collective-permute-start | bytes 2211848 | tf_op jit(solution)/shard_map/ppermute | solution.py:22
  150.0 1.0 copy-start.12
  158.5 22.7 %collective-permute-start.17 = (bf16[2,720,256]{2,1,0:T(8,128)(2,1)S(1)}, bf16[2,720,256]{2,1,0:T(8,128)(2,1)}, u32[]{:S(2)}, u32[]{:S(2)}) collective-permute-start(bf16[2,720,256]{2,1,0:T(8,128)(2,1)S(1)} %get-tuple-element.73.refs_0_), channel_id=1, source_target_pairs={{0,2},{2,0},{1,3},{3,1},{4,6},{6,4},{5,7},{7,5},{8,10},{10,8},{9,1... | collective-permute-start | bytes 2211848 | tf_op jit(solution)/shard_map/ppermute | solution.py:22
  167.8 2.3 %copy-start.6 = (bf16[1440,1440]{1,0:T(8,128)(2,1)S(1)}, bf16[1440,1440]{1,0:T(8,128)(2,1)}, u32[]{:S(2)}) copy-start(bf16[1440,1440]{1,0:T(8,128)(2,1)} %copy-done.5) | copy-start | bytes 12441604
  170.0 2.3 %copy-start.8 = (bf16[1440,1440]{1,0:T(8,128)(2,1)S(1)}, bf16[1440,1440]{1,0:T(8,128)(2,1)}, u32[]{:S(2)}) copy-start(bf16[1440,1440]{1,0:T(8,128)(2,1)} %copy-done.7) | copy-start | bytes 12441604
  176.2 18.2 %collective-permute-start.14 = (bf16[1440,128]{1,0:T(8,128)(2,1)S(1)}, bf16[1440,128]{1,0:T(8,128)(2,1)S(1)}, u32[]{:S(2)}, u32[]{:S(2)}) collective-permute-start(bf16[1440,128]{1,0:T(8,128)(2,1)S(1)} %get-tuple-element.66), channel_id=1, source_target_pairs={{0,8},{4,12},{8,0},{12,4},{1,9},{5,13},{9,1},{13,5},{2,10},{6,14},... | collective-permute-start | bytes 1105928 | tf_op jit(solution)/shard_map/ppermute | solution.py:22
  181.2 5.8 %copy-start.16 = (bf16[1440,128]{1,0:T(8,128)(2,1)S(1)}, bf16[1440,128]{1,0:T(8,128)(2,1)}, u32[]{:S(2)}) copy-start(bf16[1440,128]{1,0:T(8,128)(2,1)} %copy-done.15) | copy-start | bytes 1105924
  185.0 21.8 %collective-permute-start.18 = (bf16[1440,128]{1,0:T(8,128)(2,1)S(1)}, bf16[1440,128]{1,0:T(8,128)(2,1)S(1)}, u32[]{:S(2)}, u32[]{:S(2)}) collective-permute-start(bf16[1440,128]{1,0:T(8,128)(2,1)S(1)} %get-tuple-element.75), channel_id=1, source_target_pairs={{0,4},{4,0},{8,12},{12,8},{1,5},{5,1},{9,13},{13,9},{2,6},{6,2},{1... | collective-permute-start | bytes 1105928 | tf_op jit(solution)/shard_map/ppermute | solution.py:22
  185.7 21.2 %collective-permute-start.19 = (bf16[1440,128]{1,0:T(8,128)(2,1)S(1)}, bf16[1440,128]{1,0:T(8,128)(2,1)S(1)}, u32[]{:S(2)}, u32[]{:S(2)}) collective-permute-start(bf16[1440,128]{1,0:T(8,128)(2,1)S(1)} %get-tuple-element.76), channel_id=1, source_target_pairs={{0,12},{4,8},{8,4},{12,0},{1,13},{5,9},{9,5},{13,1},{2,14},{6,10},... | collective-permute-start | bytes 1105928 | tf_op jit(solution)/shard_map/ppermute | solution.py:22

commit v12 on v10

--- a/solution.py
+++ b/solution.py
@@ -189,7 +189,7 @@
     )(jnp.stack([t, s]).astype(jnp.int32), *attended, *weights)
 
 
-def activate(pieces, gain_table, weights, pair, t, chosen):
+def activate(pieces, gain_table, weights, pair, t, chosen, ahead):
     slots = len(pieces)
     height, rows = pieces[0][0].shape
     depth = D // slots
@@ -203,7 +203,7 @@
         table_ref = refs[slots * slots]
         weight_refs = refs[slots * slots + 1 : slots * slots + 1 + experts]
         out_ref, share_ref, rows_ref, stage_ref, routes_ref, held_ref, arrived = refs[
-            slots * slots + 1 + experts :
+            slots * slots + 1 + experts + len(ahead) :
         ]
         copies = [
             fetches(weight_refs[e], held_ref.at[e - 1], arrived.at[e - 1], cuts) for e in range(1, experts)
@@ -252,7 +252,8 @@
         ),
         in_specs=[in_smem()]
         + in_vmem(len(flat) + 2)
-        + [pl.BlockSpec(memory_space=pl.ANY)] * (experts - 1),
+        + [pl.BlockSpec(memory_space=pl.ANY)] * (experts - 1)
+        + in_vmem(len(ahead)),
         out_specs=tuple(in_vmem(2)),
         scratch_shapes=[
             pltpu.VMEM((D, lanes), jnp.bfloat16),
@@ -264,7 +265,22 @@
         compiler_params=params(),
         cost_estimate=cost(4 * experts * lanes * D * units, 4 * experts * D * units),
         name="activate",
-    )(jnp.stack([pair, t] + chosen).astype(jnp.int32), *flat, gain_table, *weights)
+    )(jnp.stack([pair, t] + chosen).astype(jnp.int32), *flat, gain_table, *weights, *ahead)
+
+
+def ready(table, ahead):
+    def kernel(table_ref, ahead_ref, out_ref):
+        out_ref[...] = table_ref[...]
+
+    return pl.pallas_call(
+        kernel,
+        out_shape=jax.ShapeDtypeStruct(table.shape, table.dtype),
+        in_specs=in_vmem(2),
+        out_specs=in_vmem(1)[0],
+        compiler_params=params(),
+        cost_estimate=cost(0, 4 * table.size),
+        name="ready",
+    )(table, ahead)
 
 
 def combine(activated, share, weights, t, slots):
@@ -272,18 +288,12 @@
     experts, units, lanes = activated[0].shape
     width = weights[0].shape[0]
     rows = lanes // slots
-    cuts = cuts_of([()], width, 3)
 
     def kernel(t_ref, *refs):
         activated_refs = refs[:t_count]
         share_ref = refs[t_count]
         weight_refs = refs[t_count + 1 : t_count + 1 + experts]
-        *out_refs, all_ref, stage_ref, held_ref, arrived = refs[t_count + 1 + experts :]
-        copies = [
-            fetches(weight_refs[e], held_ref.at[e - 1], arrived.at[e - 1], cuts) for e in range(1, experts)
-        ]
-        for copy in sum(copies, []):
-            copy.start()
+        *out_refs, all_ref, stage_ref = refs[t_count + 1 + experts :]
         for u in range(t_count):
             index = t_ref[0] ^ u
             if aligned(units):
@@ -295,11 +305,7 @@
                 all_ref[:, index * units : (index + 1) * units, :] = stage_ref[index]
         total = 0.0
         for e in range(experts):
-            if e:
-                for copy in copies[e - 1]:
-                    copy.wait()
-            weight_ref = held_ref.at[e - 1] if e else weight_refs[0]
-            result = dot(weight_ref[...], all_ref[e]).astype(jnp.bfloat16).astype(jnp.float32)
+            result = dot(weight_refs[e][...], all_ref[e]).astype(jnp.bfloat16).astype(jnp.float32)
             total = total + share_ref[e : e + 1, :] * result
         for j in range(slots):
             out_refs[j][...] = total[:, j * rows : (j + 1) * rows].astype(jnp.bfloat16)
@@ -307,15 +313,11 @@
     return pl.pallas_call(
         kernel,
         out_shape=tuple(jax.ShapeDtypeStruct((width, rows), jnp.bfloat16) for _ in range(slots)),
-        in_specs=[in_smem()]
-        + in_vmem(t_count + 2)
-        + [pl.BlockSpec(memory_space=pl.ANY)] * (experts - 1),
+        in_specs=[in_smem()] + in_vmem(t_count + 1 + experts),
         out_specs=tuple(in_vmem(slots)),
         scratch_shapes=[
             pltpu.VMEM((experts, t_count * units, lanes), jnp.bfloat16),
             pltpu.VMEM((1, 1, 16, 128) if aligned(units) else (t_count, experts, units, lanes), jnp.bfloat16),
-            pltpu.VMEM((max(1, experts - 1), width, t_count * units), jnp.bfloat16),
-            pltpu.SemaphoreType.DMA((max(1, experts - 1), len(cuts))),
         ],
         compiler_params=params(),
         cost_estimate=cost(
@@ -421,6 +423,9 @@
     fine = (inverse_square - coarse.astype(jnp.float32)).astype(jnp.bfloat16)
     gain_table = jnp.concatenate([coarse[None], fine[None], jnp.zeros((14, D), jnp.bfloat16)], axis=0)
 
+    gain_table, _ = lax.optimization_barrier((gain_table, scaled))
+    gain_table = ready(gain_table, expert_in)
+
     total = 0.0
     for m in range(t_count):
         for r in range(slots):
@@ -434,7 +439,9 @@
         part = [[pieces[m][group * r + p] for r in range(slots)] for m in range(t_count)]
         if p:
             part, after = lax.optimization_barrier((part, after))
-        activated, share = activate(part, gain_table, experts_in, pair, t, chosen)
+        activated, share = activate(
+            part, gain_table, experts_in, pair, t, chosen, experts_out if p == group - 1 else []
+        )
         after = activated
         activated = [activated] + [swapped(activated, "tp", m) for m in range(1, t_count)]
         for j, result in enumerate(combine(activated, share, experts_out, t, slots)):

time: 189 us -> 186 us (0.984)
  Pallas kernels: 46.5 us -> 39.7 us
  local copies, waits for them, and re-layouts: 25.6 us -> 30 us
    pallas_call x2, Pallas kernels: 14.3 us -> 7.66 us  [combine(): pl.pallas_call(kernel, out_shape=tuple((jax.ShapeDtypeStruct((width, rows...]
    unnamed x42 -> x54, local copies, waits for them, and re-layouts: 21.9 us -> 26.4 us
  transfers between devices with their start and end apart: 20 -> 20, of which waited for: 10 -> 11; matrix products, arithmetic and copies ran while one was open for 3% -> 3% of each run, Pallas kernels for 25% -> 21%
where the time goes in v12:
time: 186 us; the launch traced here: 185 us
  waiting for transfers between devices  77.4 us (42%)
  Pallas kernels  39.7 us (21%)
  starting transfers between devices  34.8 us (19%)
  local copies, waits for them, and re-layouts  30 us (16%)
  other arithmetic  2.96 us (2%)
    ppermute x18, waiting for transfers between devices, swapped(): lax.ppermute(block, axis, [(i, i ^ distance) for i in range(lax.axis_size...  77.4 us
    ppermute x18, starting transfers between devices, swapped(): lax.ppermute(block, axis, [(i, i ^ distance) for i in range(lax.axis_size...  30.8 us
    unnamed x54, local copies, waits for them, and re-layouts  26.4 us
    pallas_call x2, Pallas kernels, activate(): pl.pallas_call(kernel, out_shape=(jax.ShapeDtypeStruct((experts, units, l...  17.9 us
    pallas_call x2, Pallas kernels, combine(): pl.pallas_call(kernel, out_shape=tuple((jax.ShapeDtypeStruct((width, rows...  7.66 us
    pallas_call x1, Pallas kernels, attention(): pl.pallas_call(attention_kernel, out_shape=jax.ShapeDtypeStruct((width +...  5.54 us
    pallas_call x1, Pallas kernels, flip(): pl.pallas_call(kernel, out_shape=tuple((jax.ShapeDtypeStruct(a.shape[::-1...  4.73 us
    pallas_call x2, Pallas kernels, project(): pl.pallas_call(kernel, out_shape=(jax.ShapeDtypeStruct((columns, rows), j...  3.93 us
  transfers between devices with their start and end apart: 20, of which 11 were waited for; matrix products, arithmetic and copies ran while one was open for 3% of the time, Pallas kernels for 21%

profile of v12, /device:TPU:0, one launch (start us, length us, event | category | flops | bytes accessed | tf_op | source)
XLA Modules:
  0.0 185.2 jit_solution(6936275837680730869)
XLA Ops:
  0.0 1.0 pad_maximum_fusion.2
  1.0 2.4 %collective-permute-start = (bf16[128,512]{1,0:T(8,128)(2,1)S(1)}, bf16[128,512]{1,0:T(8,128)(2,1)S(1)}, u32[]{:S(2)}, u32[]{:S(2)}) collective-permute-start(bf16[128,512]{1,0:T(8,128)(2,1)S(1)} %pad_maximum_fusion.2), channel_id=1, source_target_pairs={{0,1},{1,4},{4,5},{5,8},{8,9},{9,12},{12,13},{2,3},{3,6},{6,7},{7,... | collective-permute-start | bytes 393224 | tf_op jit(solution)/shard_map/ppermute | solution.py:18
  4.1 2.6 %dynamic-slice_bitcast_fusion = bf16[720,1024]{1,0:T(8,128)(2,1)} fusion(bf16[2048,720]{0,1:T(8,128)(2,1)} %param.15, s32[]{:T(128)S(6)} %select_n.93), kind=kLoop, calls=%fused_computation | loop fusion | bytes 2949124 | tf_op jit(solution)/shard_map/dynamic_slice | solution.py:356
  6.7 2.7 %collective-permute-start.4 = (bf16[1440,1440]{1,0:T(8,128)(2,1)}, bf16[1440,1440]{1,0:T(8,128)(2,1)}, u32[]{:S(2)}, u32[]{:S(2)}) collective-permute-start(bf16[1440,1440]{1,0:T(8,128)(2,1)} %bitcast.34), channel_id=1, source_target_pairs={{0,1},{1,0},{2,3},{3,2},{4,5},{5,4},{6,7},{7,6},{8,9},{9,8},{10,11... | collective-permute-start | bytes 12441608 | tf_op jit(solution)/shard_map/ppermute | solution.py:22
  9.4 1.6 collective-permute-start.2
  11.0 1.0 copy-done.10
  12.0 0.8 copy-done.15
  12.9 0.8 copy-done.16
  15.7 5.5 %attention.1.refs_0_ = bf16[2064,128]{1,0:T(8,128)(2,1)S(1)} custom-call(s32[1]{0:T(128)} %bitcast.1.place_ref, f32[32]{0:T(128)S(1)} %copy-done.19, bf16[128,2048]{1,0:T(8,128)(2,1)S(1)} %copy-done.10, bf16[128,512]{1,0:T(8,128)(2,1)S(1)} %collective-permute-done.earlier_ref, bf16[128,256]{1,0:T(8,128)(2,1)S(1)} %copy-done.16, ...), custom_call_target="tpu_custom_call" | custom-call | flops 268435456 | bytes 1572864 | tf_op jit(solution)/shard_map/attention/pallas_call | solution.py:125
  21.3 2.4 %collective-permute-start.1 = (bf16[2064,128]{1,0:T(8,128)(2,1)S(1)}, bf16[2064,128]{1,0:T(8,128)(2,1)S(1)}, u32[]{:S(2)}, u32[]{:S(2)}) collective-permute-start(bf16[2064,128]{1,0:T(8,128)(2,1)S(1)} %attention.1.refs_0_), channel_id=1, source_target_pairs={{0,8},{4,12},{8,0},{12,4},{1,9},{5,13},{9,1},{13,5},{2,10},{6,14},... | collective-permute-start | bytes 1585160 | tf_op jit(solution)/shard_map/ppermute | solution.py:22
  23.7 1.6 collective-permute-start.3
  25.4 2.3 %copy-done.9 = bf16[1,1440,1440]{2,1,0:T(8,128)(2,1)S(1)} copy-done((bf16[1,1440,1440]{2,1,0:T(8,128)(2,1)S(1)}, bf16[1,1440,1440]{2,1,0:T(8,128)(2,1)}, u32[]{:S(2)}) %copy-start.9) | copy-done | bytes 4147224
  27.6 4.7 %flip.1 = (bf16[1440,1440]{1,0:T(8,128)(2,1)S(1)}, bf16[1440,1440]{1,0:T(8,128)(2,1)S(1)}) custom-call(bf16[1440,1440]{1,0:T(8,128)(2,1)S(1)} %bitcast.35, bf16[1440,1440]{1,0:T(8,128)(2,1)} %collective-permute-done.4.refs_1_), custom_call_target="tpu_custom_call" | custom-call | bytes 16588800 | tf_op jit(solution)/shard_map/flip/pallas_call | solution.py:141
  32.4 2.2 %copy-done.3 = bf16[1440,1440]{1,0:T(8,128)(2,1)} copy-done((bf16[1440,1440]{1,0:T(8,128)(2,1)}, bf16[1440,1440]{1,0:T(8,128)(2,1)S(1)}, u32[]{:S(2)}) %copy-start.3) | copy-done | bytes 4147224
  34.5 2.0 %copy-done.5 = bf16[1440,1440]{1,0:T(8,128)(2,1)} copy-done((bf16[1440,1440]{1,0:T(8,128)(2,1)}, bf16[1440,1440]{1,0:T(8,128)(2,1)S(1)}, u32[]{:S(2)}) %copy-start.5) | copy-done | bytes 4147224
  36.6 18.2 %collective-permute-done.1.refs_1_ = bf16[2064,128]{1,0:T(8,128)(2,1)S(1)} collective-permute-done((bf16[2064,128]{1,0:T(8,128)(2,1)S(1)}, bf16[2064,128]{1,0:T(8,128)(2,1)S(1)}, u32[]{:S(2)}, u32[]{:S(2)}) %collective-permute-start.1) | collective-permute-done | bytes 528416 | tf_op jit(solution)/shard_map/ppermute | solution.py:22
  54.7 0.9 collective-permute-done.2.refs_2_
  55.9 1.8 copy-done.8
  57.8 1.5 project.2
  59.3 2.4 %project.3 = (f32[720,128]{1,0:T(8,128)S(1)}, bf16[1,720,128]{2,1,0:T(8,128)(2,1)S(1)}) custom-call(s32[2]{0:T(128)S(1)} %pad_add_fusion.1.place_ref, bf16[2064,128]{1,0:T(8,128)(2,1)S(1)} %attention.1.refs_0_, bf16[2064,128]{1,0:T(8,128)(2,1)S(1)} %collective-permute-done.1.refs_1_, bf16[720,1024]{1,0:T(8,128)(2,1)S(1)} %collective-permute-done.2.refs_2_, ...), custom_call_target="tpu_custom_call" | custom-call | flops 754974720 | bytes 2949120 | tf_op jit(solution)/shard_map/project/pallas_call | solution.py:177
  61.8 9.5 %collective-permute-start.6 = (bf16[1440,128]{1,0:T(8,128)(2,1)S(1)}, bf16[1440,128]{1,0:T(8,128)(2,1)S(1)}, u32[]{:S(2)}, u32[]{:S(2)}) collective-permute-start(bf16[1440,128]{1,0:T(8,128)(2,1)S(1)} %pad_maximum_fusion.1), channel_id=1, source_target_pairs={{0,2},{2,0},{1,3},{3,1},{4,6},{6,4},{5,7},{7,5},{8,10},{10,8},{9,1... | collective-permute-start | bytes 1105928 | tf_op jit(solution)/shard_map/ppermute | solution.py:22
  71.3 9.2 %collective-permute-done.6 = bf16[1440,128]{1,0:T(8,128)(2,1)S(1)} collective-permute-done((bf16[1440,128]{1,0:T(8,128)(2,1)S(1)}, bf16[1440,128]{1,0:T(8,128)(2,1)S(1)}, u32[]{:S(2)}, u32[]{:S(2)}) %collective-permute-start.6) | collective-permute-done | bytes 368672 | tf_op jit(solution)/shard_map/ppermute | solution.py:22
  80.9 3.3 %collective-permute-start.7 = (bf16[1456,128]{1,0:T(8,128)(2,1)S(1)}, bf16[1456,128]{1,0:T(8,128)(2,1)S(1)}, u32[]{:S(2)}, u32[]{:S(2)}) collective-permute-start(bf16[1456,128]{1,0:T(8,128)(2,1)S(1)} %pad_maximum_fusion.refs_0_), channel_id=1, source_target_pairs={{0,8},{4,12},{8,0},{12,4},{1,9},{5,13},{9,1},{13,5},{2,10},{6,14},... | collective-permute-start | bytes 1118216 | tf_op jit(solution)/shard_map/ppermute | solution.py:22
  84.3 1.7 collective-permute-start.10
  86.2 14.7 %collective-permute-done.7.refs_1_ = bf16[1456,128]{1,0:T(8,128)(2,1)S(1)} collective-permute-done((bf16[1456,128]{1,0:T(8,128)(2,1)S(1)}, bf16[1456,128]{1,0:T(8,128)(2,1)S(1)}, u32[]{:S(2)}, u32[]{:S(2)}) %collective-permute-start.7) | collective-permute-done | bytes 372768 | tf_op jit(solution)/shard_map/ppermute | solution.py:22
  101.0 1.4 collective-permute-start.11
  102.6 3.4 %copy-done.1 = bf16[1,2,2880,720]{2,3,1,0:T(8,128)(2,1)S(1)} copy-done((bf16[1,2,2880,720]{2,3,1,0:T(8,128)(2,1)S(1)}, bf16[1,2,2880,720]{2,3,1,0:T(8,128)(2,1)}, u32[]{:S(2)}) %copy-start.1) | copy-done | bytes 8294424
  106.1 4.8 %collective-permute-done.11.refs_3_ = bf16[1456,128]{1,0:T(8,128)(2,1)S(1)} collective-permute-done((bf16[1456,128]{1,0:T(8,128)(2,1)S(1)}, bf16[1456,128]{1,0:T(8,128)(2,1)S(1)}, u32[]{:S(2)}, u32[]{:S(2)}) %collective-permute-start.11) | collective-permute-done | bytes 372768 | tf_op jit(solution)/shard_map/ppermute | solution.py:22
  110.9 1.0 collective-permute-done.9.refs_1_
  112.7 1.3 collective-permute-start.16
  113.9 3.4 %copy-done.2 = bf16[1,2,2880,720]{2,3,1,0:T(8,128)(2,1)S(1)} copy-done((bf16[1,2,2880,720]{2,3,1,0:T(8,128)(2,1)S(1)}, bf16[1,2,2880,720]{2,3,1,0:T(8,128)(2,1)}, u32[]{:S(2)}) %copy-start.2) | copy-done | bytes 8294424
  117.3 10.3 %activate.2 = (bf16[2,720,256]{2,1,0:T(8,128)(2,1)}, f32[2,256]{1,0:T(2,128)S(1)}) custom-call(s32[4]{0:T(128)S(1)} %pad_add_fusion.2.place_ref, bf16[1456,128]{1,0:T(8,128)(2,1)S(1)} %pad_maximum_fusion.refs_0_, bf16[1456,128]{1,0:T(8,128)(2,1)S(1)} %collective-permute-done.7.refs_1_, bf16[1456,128]{1,0:T(8,128)(2,1)S(1)} %collective-permute-done.10.refs_2_, ...), custom_call_target="tpu_custom_call" | custom-call | flops 4246732800 | bytes 16588800 | tf_op jit(solution)/shard_map/activate/pallas_call | solution.py:247
  127.6 0.8 collective-permute-start.13
  128.9 1.0 copy-done.12
  129.9 1.0 copy-done.14
  130.9 7.6 %activate.3 = (bf16[2,720,256]{2,1,0:T(8,128)(2,1)S(1)}, f32[2,256]{1,0:T(2,128)S(1)}) custom-call(s32[4]{0:T(128)S(1)} %pad_add_fusion.2.place_ref, bf16[1456,128]{1,0:T(8,128)(2,1)S(1)} %copy-done.12, bf16[1456,128]{1,0:T(8,128)(2,1)S(1)} %copy-done.14, bf16[1456,128]{1,0:T(8,128)(2,1)S(1)} %collective-permute-done.15.refs_2_, ...), custom_call_target="tpu_custom_call" | custom-call | flops 4246732800 | bytes 16588800 | tf_op jit(solution)/shard_map/activate/pallas_call | solution.py:247
  138.5 1.0 collective-permute-start.17
  139.6 7.9 %collective-permute-done.13.refs_1_ = bf16[2,720,256]{2,1,0:T(8,128)(2,1)} collective-permute-done((bf16[2,720,256]{2,1,0:T(8,128)(2,1)}, bf16[2,720,256]{2,1,0:T(8,128)(2,1)}, u32[]{:S(2)}, u32[]{:S(2)}) %collective-permute-start.13) | collective-permute-done | bytes 737312 | tf_op jit(solution)/shard_map/ppermute | solution.py:22
  147.4 2.3 %copy-done.4 = bf16[1440,1440]{1,0:T(8,128)(2,1)S(1)} copy-done((bf16[1440,1440]{1,0:T(8,128)(2,1)S(1)}, bf16[1440,1440]{1,0:T(8,128)(2,1)}, u32[]{:S(2)}) %copy-start.4) | copy-done | bytes 4147224
  149.7 2.3 %copy-done.7 = bf16[1440,1440]{1,0:T(8,128)(2,1)S(1)} copy-done((bf16[1440,1440]{1,0:T(8,128)(2,1)S(1)}, bf16[1440,1440]{1,0:T(8,128)(2,1)}, u32[]{:S(2)}) %copy-start.7) | copy-done | bytes 4147224
  151.9 3.9 %combine.2 = (bf16[1440,128]{1,0:T(8,128)(2,1)S(1)}, bf16[1440,128]{1,0:T(8,128)(2,1)S(1)}) custom-call(s32[1]{0:T(128)} %bitcast.t_ref, bf16[2,720,256]{2,1,0:T(8,128)(2,1)} %get-tuple-element.61.refs_0_, bf16[2,720,256]{2,1,0:T(8,128)(2,1)} %collective-permute-done.13.refs_1_, f32[2,256]{1,0:T(2,128)S(1)} %get-tuple-element.62.refs_2_, ...), custom_call_target="tpu_custom_call" | custom-call | flops 2123366400 | bytes 8294400 | tf_op jit(solution)/shard_map/combine/pallas_call | solution.py:313
  155.9 1.3 collective-permute-start.14
  157.1 3.0 %collective-permute-done.17.refs_1_ = bf16[2,720,256]{2,1,0:T(8,128)(2,1)} collective-permute-done((bf16[2,720,256]{2,1,0:T(8,128)(2,1)S(1)}, bf16[2,720,256]{2,1,0:T(8,128)(2,1)}, u32[]{:S(2)}, u32[]{:S(2)}) %collective-permute-start.17) | collective-permute-done | bytes 737312 | tf_op jit(solution)/shard_map/ppermute | solution.py:22
  160.1 3.7 %combine.3 = (bf16[1440,128]{1,0:T(8,128)(2,1)S(1)}, bf16[1440,128]{1,0:T(8,128)(2,1)S(1)}) custom-call(s32[1]{0:T(128)} %bitcast.t_ref, bf16[2,720,256]{2,1,0:T(8,128)(2,1)S(1)} %get-tuple-element.73.refs_0_, bf16[2,720,256]{2,1,0:T(8,128)(2,1)} %collective-permute-done.17.refs_1_, f32[2,256]{1,0:T(2,128)S(1)} %get-tuple-element.74.refs_2_, ...), custom_call_target="tpu_custom_call" | custom-call | flops 2123366400 | bytes 8294400 | tf_op jit(solution)/shard_map/combine/pallas_call | solution.py:313
  164.5 2.2 %collective-permute-start.19 = (bf16[1440,128]{1,0:T(8,128)(2,1)S(1)}, bf16[1440,128]{1,0:T(8,128)(2,1)S(1)}, u32[]{:S(2)}, u32[]{:S(2)}) collective-permute-start(bf16[1440,128]{1,0:T(8,128)(2,1)S(1)} %get-tuple-element.76), channel_id=1, source_target_pairs={{0,12},{4,8},{8,4},{12,0},{1,13},{5,9},{9,5},{13,1},{2,14},{6,10},... | collective-permute-start | bytes 1105928 | tf_op jit(solution)/shard_map/ppermute | solution.py:22
  167.0 9.0 %collective-permute-done.14 = bf16[1440,128]{1,0:T(8,128)(2,1)S(1)} collective-permute-done((bf16[1440,128]{1,0:T(8,128)(2,1)S(1)}, bf16[1440,128]{1,0:T(8,128)(2,1)S(1)}, u32[]{:S(2)}, u32[]{:S(2)}) %collective-permute-start.14) | collective-permute-done | bytes 368672 | tf_op jit(solution)/shard_map/ppermute | solution.py:22
  176.0 8.2 %collective-permute-done.18 = bf16[1440,128]{1,0:T(8,128)(2,1)S(1)} collective-permute-done((bf16[1440,128]{1,0:T(8,128)(2,1)S(1)}, bf16[1440,128]{1,0:T(8,128)(2,1)S(1)}, u32[]{:S(2)}, u32[]{:S(2)}) %collective-permute-start.18) | collective-permute-done | bytes 368672 | tf_op jit(solution)/shard_map/ppermute | solution.py:22
  184.3 1.0 fusion.3
  (79 shorter events, 6.3 us)
Async XLA Ops:
  0.0 3.4 %copy-start = (bf16[128,2880]{0,1:T(8,128)(2,1)S(1)}, bf16[128,2880]{0,1:T(8,128)(2,1)}, u32[]{:S(2)}) copy-start(bf16[128,2880]{0,1:T(8,128)(2,1)} %param.16) | copy-start | bytes 2211844
  1.0 5.8 %collective-permute-start = (bf16[128,512]{1,0:T(8,128)(2,1)S(1)}, bf16[128,512]{1,0:T(8,128)(2,1)S(1)}, u32[]{:S(2)}, u32[]{:S(2)}) collective-permute-start(bf16[128,512]{1,0:T(8,128)(2,1)S(1)} %pad_maximum_fusion.2), channel_id=1, source_target_pairs={{0,1},{1,4},{4,5},{5,8},{8,9},{9,12},{12,13},{2,3},{3,6},{6,7},{7,... | collective-permute-start | bytes 393224 | tf_op jit(solution)/shard_map/ppermute | solution.py:18
  6.7 18.6 %collective-permute-start.4 = (bf16[1440,1440]{1,0:T(8,128)(2,1)}, bf16[1440,1440]{1,0:T(8,128)(2,1)}, u32[]{:S(2)}, u32[]{:S(2)}) collective-permute-start(bf16[1440,1440]{1,0:T(8,128)(2,1)} %bitcast.34), channel_id=1, source_target_pairs={{0,1},{1,0},{2,3},{3,2},{4,5},{5,4},{6,7},{7,6},{8,9},{9,8},{10,11... | collective-permute-start | bytes 12441608 | tf_op jit(solution)/shard_map/ppermute | solution.py:22
  9.4 104.5 %collective-permute-start.12 = (bf16[2,720,2880]{2,1,0:T(8,128)(2,1)}, bf16[2,720,2880]{2,1,0:T(8,128)(2,1)}, u32[]{:S(2)}, u32[]{:S(2)}) collective-permute-start(bf16[2,720,2880]{2,1,0:T(8,128)(2,1)} %bitcast.27), channel_id=1, source_target_pairs={{0,1},{1,0},{2,3},{3,2},{4,5},{5,4},{6,7},{7,6},{8,9},{9,8},{10,11... | collective-permute-start | bytes 24883208 | tf_op jit(solution)/shard_map/ppermute | solution.py:22
  9.4 46.2 %collective-permute-start.2 = (bf16[720,1024]{1,0:T(8,128)(2,1)}, bf16[720,1024]{1,0:T(8,128)(2,1)S(1)}, u32[]{:S(2)}, u32[]{:S(2)}) collective-permute-start(bf16[720,1024]{1,0:T(8,128)(2,1)} %dynamic-slice_bitcast_fusion), channel_id=1, source_target_pairs={{0,4},{4,0},{8,12},{12,8},{1,5},{5,1},{9,13},{13,9},{2,6},{6,2},{1... | collective-permute-start | bytes 4423688 | tf_op jit(solution)/shard_map/ppermute | solution.py:22
  11.0 1.0 copy-start.10
  12.0 0.8 copy-start.15
  12.9 0.8 copy-start.16
  13.7 0.7 copy-start.17
  14.4 0.7 copy-start.18
  15.1 0.7 copy-start.19
  15.7 39.9 %copy-start.24 = (f32[2880]{0:T(1024)S(1)}, f32[2880]{0:T(1024)}, u32[]{:S(2)}) copy-start(f32[2880]{0:T(1024)} %param.17) | copy-start | bytes 34564
  21.3 33.5 %collective-permute-start.1 = (bf16[2064,128]{1,0:T(8,128)(2,1)S(1)}, bf16[2064,128]{1,0:T(8,128)(2,1)S(1)}, u32[]{:S(2)}, u32[]{:S(2)}) collective-permute-start(bf16[2064,128]{1,0:T(8,128)(2,1)S(1)} %attention.1.refs_0_), channel_id=1, source_target_pairs={{0,8},{4,12},{8,0},{12,4},{1,9},{5,13},{9,1},{13,5},{2,10},{6,14},... | collective-permute-start | bytes 1585160 | tf_op jit(solution)/shard_map/ppermute | solution.py:22
  23.7 12.8 %collective-permute-start.3 = (bf16[1440,128]{1,0:T(8,128)(2,1)}, bf16[1440,128]{1,0:T(8,128)(2,1)S(1)}, u32[]{:S(2)}, u32[]{:S(2)}) collective-permute-start(bf16[1440,128]{1,0:T(8,128)(2,1)} %dynamic-slice_bitcast_fusion.1), channel_id=1, source_target_pairs={{0,0},{2,10},{4,4},{6,14},{8,8},{10,2},{12,12},{14,6},{1,1},{3,11}... | collective-permute-start | bytes 1105928 | tf_op jit(solution)/shard_map/ppermute | solution.py:367
  25.4 2.3 %copy-start.9 = (bf16[1,1440,1440]{2,1,0:T(8,128)(2,1)S(1)}, bf16[1,1440,1440]{2,1,0:T(8,128)(2,1)}, u32[]{:S(2)}) copy-start(bf16[1,1440,1440]{2,1,0:T(8,128)(2,1)} %param.19) | copy-start | bytes 12441604
  32.4 2.2 %copy-start.3 = (bf16[1440,1440]{1,0:T(8,128)(2,1)}, bf16[1440,1440]{1,0:T(8,128)(2,1)S(1)}, u32[]{:S(2)}) copy-start(bf16[1440,1440]{1,0:T(8,128)(2,1)S(1)} %get-tuple-element.63.refs_3_.refs_7_) | copy-start | bytes 12441604
  34.5 2.0 %copy-start.5 = (bf16[1440,1440]{1,0:T(8,128)(2,1)}, bf16[1440,1440]{1,0:T(8,128)(2,1)S(1)}, u32[]{:S(2)}) copy-start(bf16[1440,1440]{1,0:T(8,128)(2,1)S(1)} %get-tuple-element.64.refs_4_.refs_8_) | copy-start | bytes 12441604
  36.6 19.1 %copy-start.22 = (bf16[1440,128]{1,0:T(8,128)(2,1)}, bf16[1440,128]{1,0:T(8,128)(2,1)S(1)}, u32[]{:S(2)}) copy-start(bf16[1440,128]{1,0:T(8,128)(2,1)S(1)} %collective-permute-done.3) | copy-start | bytes 1105924
  55.7 3.7 %collective-permute-start.5 = (bf16[720,1024]{1,0:T(8,128)(2,1)S(1)}, bf16[720,1024]{1,0:T(8,128)(2,1)}, u32[]{:S(2)}, u32[]{:S(2)}) collective-permute-start(bf16[720,1024]{1,0:T(8,128)(2,1)S(1)} %collective-permute-done.2.refs_2_), channel_id=1, source_target_pairs={{0,1},{1,0},{2,3},{3,2},{4,5},{5,4},{6,7},{7,6},{8,9},{9,8},{10,11... | collective-permute-start | bytes 4423688 | tf_op jit(solution)/shard_map/ppermute | solution.py:22
  55.9 1.8 copy-start.8
  57.8 71.1 %slice-start = ((s8[4423680]{0:T(1024)(128)(4,1)}), s8[229376]{0:T(1024)(128)(4,1)S(1)}, s32[]{:S(2)}) async-start(s8[4423680]{0:T(1024)(128)(4,1)} %bitcast.31), calls=%async_computation | async-start | bytes 458752
  59.3 21.2 %copy-start.23 = (bf16[1440,128]{1,0:T(8,128)(2,1)S(1)}, bf16[1440,128]{1,0:T(8,128)(2,1)}, u32[]{:S(2)}) copy-start(bf16[1440,128]{1,0:T(8,128)(2,1)} %copy-done.22) | copy-start | bytes 1105924
  61.8 18.7 %collective-permute-start.6 = (bf16[1440,128]{1,0:T(8,128)(2,1)S(1)}, bf16[1440,128]{1,0:T(8,128)(2,1)S(1)}, u32[]{:S(2)}, u32[]{:S(2)}) collective-permute-start(bf16[1440,128]{1,0:T(8,128)(2,1)S(1)} %pad_maximum_fusion.1), channel_id=1, source_target_pairs={{0,2},{2,0},{1,3},{3,1},{4,6},{6,4},{5,7},{7,5},{8,10},{10,8},{9,1... | collective-permute-start | bytes 1105928 | tf_op jit(solution)/shard_map/ppermute | solution.py:22
  80.8 21.6 %copy-start.20 = (bf16[1440,128]{1,0:T(8,128)(2,1)}, bf16[1440,128]{1,0:T(8,128)(2,1)S(1)}, u32[]{:S(2)}) copy-start(bf16[1440,128]{1,0:T(8,128)(2,1)S(1)} %fusion.2) | copy-start | bytes 1105924
  80.9 20.1 %collective-permute-start.7 = (bf16[1456,128]{1,0:T(8,128)(2,1)S(1)}, bf16[1456,128]{1,0:T(8,128)(2,1)S(1)}, u32[]{:S(2)}, u32[]{:S(2)}) collective-permute-start(bf16[1456,128]{1,0:T(8,128)(2,1)S(1)} %pad_maximum_fusion.refs_0_), channel_id=1, source_target_pairs={{0,8},{4,12},{8,0},{12,4},{1,9},{5,13},{9,1},{13,5},{2,10},{6,14},... | collective-permute-start | bytes 1118216 | tf_op jit(solution)/shard_map/ppermute | solution.py:22
  84.3 21.8 %collective-permute-start.10 = (bf16[1456,128]{1,0:T(8,128)(2,1)S(1)}, bf16[1456,128]{1,0:T(8,128)(2,1)S(1)}, u32[]{:S(2)}, u32[]{:S(2)}) collective-permute-start(bf16[1456,128]{1,0:T(8,128)(2,1)S(1)} %pad_maximum_fusion.refs_0_), channel_id=1, source_target_pairs={{0,2},{2,0},{1,3},{3,1},{4,6},{6,4},{5,7},{7,5},{8,10},{10,8},{9,1... | collective-permute-start | bytes 1118216 | tf_op jit(solution)/shard_map/ppermute | solution.py:22
  86.0 20.0 %collective-permute-start.8 = (bf16[1456,128]{1,0:T(8,128)(2,1)S(1)}, bf16[1456,128]{1,0:T(8,128)(2,1)S(1)}, u32[]{:S(2)}, u32[]{:S(2)}) collective-permute-start(bf16[1456,128]{1,0:T(8,128)(2,1)S(1)} %pad_maximum_fusion.refs_0_), channel_id=1, source_target_pairs={{0,4},{4,0},{8,12},{12,8},{1,5},{5,1},{9,13},{13,9},{2,6},{6,2},{1... | collective-permute-start | bytes 1118216 | tf_op jit(solution)/shard_map/ppermute | solution.py:22
  101.0 9.9 %collective-permute-start.11 = (bf16[1456,128]{1,0:T(8,128)(2,1)S(1)}, bf16[1456,128]{1,0:T(8,128)(2,1)S(1)}, u32[]{:S(2)}, u32[]{:S(2)}) collective-permute-start(bf16[1456,128]{1,0:T(8,128)(2,1)S(1)} %collective-permute-done.7.refs_1_), channel_id=1, source_target_pairs={{0,2},{2,0},{1,3},{3,1},{4,6},{6,4},{5,7},{7,5},{8,10},{10,8},{9,1... | collective-permute-start | bytes 1118216 | tf_op jit(solution)/shard_map/ppermute | solution.py:22
  102.4 9.5 %collective-permute-start.9 = (bf16[1456,128]{1,0:T(8,128)(2,1)S(1)}, bf16[1456,128]{1,0:T(8,128)(2,1)S(1)}, u32[]{:S(2)}, u32[]{:S(2)}) collective-permute-start(bf16[1456,128]{1,0:T(8,128)(2,1)S(1)} %collective-permute-done.7.refs_1_), channel_id=1, source_target_pairs={{0,4},{4,0},{8,12},{12,8},{1,5},{5,1},{9,13},{13,9},{2,6},{6,2},{1... | collective-permute-start | bytes 1118216 | tf_op jit(solution)/shard_map/ppermute | solution.py:22
  102.6 3.4 %copy-start.1 = (bf16[1,2,2880,720]{2,3,1,0:T(8,128)(2,1)S(1)}, bf16[1,2,2880,720]{2,3,1,0:T(8,128)(2,1)}, u32[]{:S(2)}) copy-start(bf16[1,2,2880,720]{2,3,1,0:T(8,128)(2,1)} %param.18) | copy-start | bytes 24883204
  106.0 22.9 %slice-start.1 = ((s8[4423680]{0:T(1024)(128)(4,1)}), s8[4194304]{0:T(1024)(128)(4,1)S(1)}, s32[]{:S(2)}) async-start(s8[4423680]{0:T(1024)(128)(4,1)} %bitcast.31), calls=%async_computation.1 | async-start | bytes 8388608
  106.0 22.9 %copy-start.6 = (bf16[1440,1440]{1,0:T(8,128)(2,1)S(1)}, bf16[1440,1440]{1,0:T(8,128)(2,1)}, u32[]{:S(2)}) copy-start(bf16[1440,1440]{1,0:T(8,128)(2,1)} %copy-done.5) | copy-start | bytes 12441604
  106.1 21.6 %copy-start.11 = (bf16[1456,128]{1,0:T(8,128)(2,1)}, bf16[1456,128]{1,0:T(8,128)(2,1)S(1)}, u32[]{:S(2)}) copy-start(bf16[1456,128]{1,0:T(8,128)(2,1)S(1)} %collective-permute-done.8.refs_0_) | copy-start | bytes 1118212
  111.9 15.7 %copy-start.13 = (bf16[1456,128]{1,0:T(8,128)(2,1)}, bf16[1456,128]{1,0:T(8,128)(2,1)S(1)}, u32[]{:S(2)}) copy-start(bf16[1456,128]{1,0:T(8,128)(2,1)S(1)} %collective-permute-done.9.refs_1_) | copy-start | bytes 1118212
  111.9 16.6 %collective-permute-start.15 = (bf16[1456,128]{1,0:T(8,128)(2,1)S(1)}, bf16[1456,128]{1,0:T(8,128)(2,1)S(1)}, u32[]{:S(2)}, u32[]{:S(2)}) collective-permute-start(bf16[1456,128]{1,0:T(8,128)(2,1)S(1)} %collective-permute-done.8.refs_0_), channel_id=1, source_target_pairs={{0,2},{2,0},{1,3},{3,1},{4,6},{6,4},{5,7},{7,5},{8,10},{10,8},{9,1... | collective-permute-start | bytes 1118216 | tf_op jit(solution)/shard_map/ppermute | solution.py:22
  112.7 16.2 %collective-permute-start.16 = (bf16[1456,128]{1,0:T(8,128)(2,1)S(1)}, bf16[1456,128]{1,0:T(8,128)(2,1)S(1)}, u32[]{:S(2)}, u32[]{:S(2)}) collective-permute-start(bf16[1456,128]{1,0:T(8,128)(2,1)S(1)} %collective-permute-done.9.refs_1_), channel_id=1, source_target_pairs={{0,2},{2,0},{1,3},{3,1},{4,6},{6,4},{5,7},{7,5},{8,10},{10,8},{9,1... | collective-permute-start | bytes 1118216 | tf_op jit(solution)/shard_map/ppermute | solution.py:22
  113.9 3.4 %copy-start.2 = (bf16[1,2,2880,720]{2,3,1,0:T(8,128)(2,1)S(1)}, bf16[1,2,2880,720]{2,3,1,0:T(8,128)(2,1)}, u32[]{:S(2)}) copy-start(bf16[1,2,2880,720]{2,3,1,0:T(8,128)(2,1)} %param.18) | copy-start | bytes 24883204
  127.6 19.8 %collective-permute-start.13 = (bf16[2,720,256]{2,1,0:T(8,128)(2,1)}, bf16[2,720,256]{2,1,0:T(8,128)(2,1)}, u32[]{:S(2)}, u32[]{:S(2)}) collective-permute-start(bf16[2,720,256]{2,1,0:T(8,128)(2,1)} %get-tuple-element.61.refs_0_), channel_id=1, source_target_pairs={{0,2},{2,0},{1,3},{3,1},{4,6},{6,4},{5,7},{7,5},{8,10},{10,8},{9,1... | collective-permute-start | bytes 2211848 | tf_op jit(solution)/shard_map/ppermute | solution.py:22
  128.9 1.0 copy-start.12
  129.9 1.0 copy-start.14
  138.5 21.6 %collective-permute-start.17 = (bf16[2,720,256]{2,1,0:T(8,128)(2,1)S(1)}, bf16[2,720,256]{2,1,0:T(8,128)(2,1)}, u32[]{:S(2)}, u32[]{:S(2)}) collective-permute-start(bf16[2,720,256]{2,1,0:T(8,128)(2,1)S(1)} %get-tuple-element.73.refs_0_), channel_id=1, source_target_pairs={{0,2},{2,0},{1,3},{3,1},{4,6},{6,4},{5,7},{7,5},{8,10},{10,8},{9,1... | collective-permute-start | bytes 2211848 | tf_op jit(solution)/shard_map/ppermute | solution.py:22
  147.4 2.3 %copy-start.4 = (bf16[1440,1440]{1,0:T(8,128)(2,1)S(1)}, bf16[1440,1440]{1,0:T(8,128)(2,1)}, u32[]{:S(2)}) copy-start(bf16[1440,1440]{1,0:T(8,128)(2,1)} %copy-done.3) | copy-start | bytes 12441604
  149.7 2.3 %copy-start.7 = (bf16[1440,1440]{1,0:T(8,128)(2,1)S(1)}, bf16[1440,1440]{1,0:T(8,128)(2,1)}, u32[]{:S(2)}) copy-start(bf16[1440,1440]{1,0:T(8,128)(2,1)} %copy-done.5) | copy-start | bytes 12441604
  155.9 20.2 %collective-permute-start.14 = (bf16[1440,128]{1,0:T(8,128)(2,1)S(1)}, bf16[1440,128]{1,0:T(8,128)(2,1)S(1)}, u32[]{:S(2)}, u32[]{:S(2)}) collective-permute-start(bf16[1440,128]{1,0:T(8,128)(2,1)S(1)} %get-tuple-element.66), channel_id=1, source_target_pairs={{0,8},{4,12},{8,0},{12,4},{1,9},{5,13},{9,1},{13,5},{2,10},{6,14},... | collective-permute-start | bytes 1105928 | tf_op jit(solution)/shard_map/ppermute | solution.py:22
  160.1 6.6 %copy-start.21 = (bf16[1440,128]{1,0:T(8,128)(2,1)S(1)}, bf16[1440,128]{1,0:T(8,128)(2,1)}, u32[]{:S(2)}) copy-start(bf16[1440,128]{1,0:T(8,128)(2,1)} %copy-done.20) | copy-start | bytes 1105924
  163.9 20.4 %collective-permute-start.18 = (bf16[1440,128]{1,0:T(8,128)(2,1)S(1)}, bf16[1440,128]{1,0:T(8,128)(2,1)S(1)}, u32[]{:S(2)}, u32[]{:S(2)}) collective-permute-start(bf16[1440,128]{1,0:T(8,128)(2,1)S(1)} %get-tuple-element.75), channel_id=1, source_target_pairs={{0,4},{4,0},{8,12},{12,8},{1,5},{5,1},{9,13},{13,9},{2,6},{6,2},{1... | collective-permute-start | bytes 1105928 | tf_op jit(solution)/shard_map/ppermute | solution.py:22
  164.5 19.8 %collective-permute-start.19 = (bf16[1440,128]{1,0:T(8,128)(2,1)S(1)}, bf16[1440,128]{1,0:T(8,128)(2,1)S(1)}, u32[]{:S(2)}, u32[]{:S(2)}) collective-permute-start(bf16[1440,128]{1,0:T(8,128)(2,1)S(1)} %get-tuple-element.76), channel_id=1, source_target_pairs={{0,12},{4,8},{8,4},{12,0},{1,13},{5,9},{9,5},{13,1},{2,14},{6,10},... | collective-permute-start | bytes 1105928 | tf_op jit(solution)/shard_map/ppermute | solution.py:22

commit v13 on v12

--- a/solution.py
+++ b/solution.py
@@ -9,7 +9,7 @@
 HD = 64
 WIN = 128
 TOP = 4
-VMEM_BYTES = 16 * 1024 * 1024
+MIB = 1024 * 1024
 
 
 def shifted(block, axis, distance):
@@ -58,15 +58,18 @@
     return [(*at, pl.ds(i * step, step)) for at in lead for i in range(count)]
 
 
-def params():
-    return pltpu.CompilerParams(vmem_limit_bytes=VMEM_BYTES)
-
-
-def attention_kernel(place_ref, sink_ref, q_ref, earlier_ref, k_ref, v_ref, routes_ref, scores_ref, out_ref):
+def params(mebibytes):
+    return pltpu.CompilerParams(vmem_limit_bytes=int(mebibytes * MIB))
+
+
+def attention_kernel(
+    place_ref, sink_ref, q_ref, earlier_ref, k_ref, v_ref, routes_ref, scores_ref, residual_ref, out_ref
+):
     width = q_ref.shape[1]
     numbers = [routes_ref[...], scores_ref[...] // 256, scores_ref[...] % 256]
-    numbers.append(jnp.zeros((out_ref.shape[0] - width - 3 * TOP, q_ref.shape[0]), jnp.int32))
-    out_ref[width:, :] = jnp.concatenate(numbers, axis=0).astype(jnp.float32).astype(jnp.bfloat16)
+    numbers.append(jnp.zeros((16 - 3 * TOP, q_ref.shape[0]), jnp.int32))
+    out_ref[width : width + 16, :] = jnp.concatenate(numbers, axis=0).astype(jnp.float32).astype(jnp.bfloat16)
+    out_ref[width + 16 :, :] = residual_ref[place_ref[1]]
     rows = q_ref.shape[0]
     kv_count = k_ref.shape[1] // HD
     pairs = q_ref.shape[1] // (2 * HD * kv_count)
@@ -120,17 +123,17 @@
             out_ref[start + HD : start + 2 * HD, :] = result[:, rows:]
 
 
-def attention(queries, earlier, key_rows, value_rows, sink_logits, first, routes, scores):
+def attention(queries, earlier, key_rows, value_rows, sink_logits, place, routes, scores, residual):
     rows, width = queries.shape
     return pl.pallas_call(
         attention_kernel,
-        out_shape=jax.ShapeDtypeStruct((width + 16, rows), jnp.bfloat16),
-        in_specs=[in_smem(), in_smem()] + in_vmem(6),
+        out_shape=jax.ShapeDtypeStruct((width + 16 + residual.shape[1], rows), jnp.bfloat16),
+        in_specs=[in_smem(), in_smem()] + in_vmem(7),
         out_specs=in_vmem(1)[0],
-        compiler_params=params(),
+        compiler_params=params(8),
         cost_estimate=cost(8 * rows * rows * width, 6 * rows * width),
         name="attention",
-    )(first, sink_logits, queries, earlier, key_rows, value_rows, routes, scores)
+    )(place, sink_logits, queries, earlier, key_rows, value_rows, routes, scores, residual)
 
 
 def flip(arrays):
@@ -143,13 +146,13 @@
         out_shape=tuple(jax.ShapeDtypeStruct(a.shape[::-1], a.dtype) for a in arrays),
         in_specs=in_vmem(len(arrays)),
         out_specs=tuple(in_vmem(len(arrays))),
-        compiler_params=params(),
+        compiler_params=params(12),
         cost_estimate=cost(0, 4 * sum(a.size for a in arrays)),
         name="flip",
     )(*arrays)
 
 
-def project(attended, weights, t, s, t_count):
+def project(attended, weights, residual, has_share, t, s, t_count):
     slots = len(attended)
     rows = attended[0].shape[1]
     columns, depth = weights[0].shape
@@ -159,7 +162,7 @@
     def kernel(place_ref, *refs):
         attended_refs = refs[:slots]
         weight_refs = refs[slots : slots + shares]
-        kept_ref, sent_ref, total = refs[slots + shares :]
+        residual_ref, kept_ref, sent_ref, total = refs[slots + shares :]
         t, s = place_ref[0], place_ref[1]
         result = 0.0
         for u in range(shares):
@@ -167,6 +170,14 @@
             block = jnp.concatenate([ref[span, :] for ref in attended_refs], axis=1)
             result = result + dot(weight_refs[u][...], block)
         total[...] = result
+
+        @pl.when(place_ref[2] == 1)
+        def _():
+            for j in range(slots):
+                share = attended_refs[j][width + 16 :, :] if j else residual_ref[...]
+                if share.shape[0] == columns:
+                    total[:, j * rows : (j + 1) * rows] += share.astype(jnp.float32)
+
         for m in range(t_count):
             block = total[:, pl.ds(pl.multiple_of((t ^ m) * rows, 128), rows)]
             if m == 0:
@@ -180,16 +191,16 @@
             jax.ShapeDtypeStruct((columns, rows), jnp.float32),
             jax.ShapeDtypeStruct((t_count - 1, columns, rows), jnp.bfloat16),
         ),
-        in_specs=[in_smem()] + in_vmem(slots + shares),
+        in_specs=[in_smem()] + in_vmem(slots + shares + 1),
         out_specs=tuple(in_vmem(2)),
         scratch_shapes=[pltpu.VMEM((columns, slots * rows), jnp.float32)],
-        compiler_params=params(),
+        compiler_params=params(8),
         cost_estimate=cost(2 * slots * rows * width * columns, 2 * width * columns),
         name="project",
-    )(jnp.stack([t, s]).astype(jnp.int32), *attended, *weights)
-
-
-def activate(pieces, gain_table, weights, pair, t, chosen, ahead):
+    )(jnp.stack([t, s, has_share]).astype(jnp.int32), *attended, *weights, residual)
+
+
+def activate(pieces, gain_table, weights, pair, t, chosen):
     slots = len(pieces)
     height, rows = pieces[0][0].shape
     depth = D // slots
@@ -203,7 +214,7 @@
         table_ref = refs[slots * slots]
         weight_refs = refs[slots * slots + 1 : slots * slots + 1 + experts]
         out_ref, share_ref, rows_ref, stage_ref, routes_ref, held_ref, arrived = refs[
-            slots * slots + 1 + experts + len(ahead) :
+            slots * slots + 1 + experts :
         ]
         copies = [
             fetches(weight_refs[e], held_ref.at[e - 1], arrived.at[e - 1], cuts) for e in range(1, experts)
@@ -252,8 +263,7 @@
         ),
         in_specs=[in_smem()]
         + in_vmem(len(flat) + 2)
-        + [pl.BlockSpec(memory_space=pl.ANY)] * (experts - 1)
-        + in_vmem(len(ahead)),
+        + [pl.BlockSpec(memory_space=pl.ANY)] * (experts - 1),
         out_specs=tuple(in_vmem(2)),
         scratch_shapes=[
             pltpu.VMEM((D, lanes), jnp.bfloat16),
@@ -262,10 +272,10 @@
             pltpu.VMEM((max(1, experts - 1), 2, units, D), jnp.bfloat16),
             pltpu.SemaphoreType.DMA((max(1, experts - 1), len(cuts))),
         ],
-        compiler_params=params(),
+        compiler_params=params(13 if aligned(depth) else 16),
         cost_estimate=cost(4 * experts * lanes * D * units, 4 * experts * D * units),
         name="activate",
-    )(jnp.stack([pair, t] + chosen).astype(jnp.int32), *flat, gain_table, *weights, *ahead)
+    )(jnp.stack([pair, t] + chosen).astype(jnp.int32), *flat, gain_table, *weights)
 
 
 def ready(table, ahead):
@@ -277,7 +287,7 @@
         out_shape=jax.ShapeDtypeStruct(table.shape, table.dtype),
         in_specs=in_vmem(2),
         out_specs=in_vmem(1)[0],
-        compiler_params=params(),
+        compiler_params=params(4),
         cost_estimate=cost(0, 4 * table.size),
         name="ready",
     )(table, ahead)
@@ -319,7 +329,7 @@
             pltpu.VMEM((experts, t_count * units, lanes), jnp.bfloat16),
             pltpu.VMEM((1, 1, 16, 128) if aligned(units) else (t_count, experts, units, lanes), jnp.bfloat16),
         ],
-        compiler_params=params(),
+        compiler_params=params(7 if aligned(units) else 16),
         cost_estimate=cost(
             2 * experts * lanes * t_count * units * width, 2 * experts * t_count * units * width
         ),
@@ -354,17 +364,18 @@
     out_weight = out_weight.T
     depth = out_weight.shape[1] // s_count
     near = lax.dynamic_slice_in_dim(out_weight, s * depth, depth, 1)
-    residual = picked(residual.T.reshape(slots, group * columns, rows), pair ^ t, 0)
-    earlier, near, residual, expert_in, expert_out = lax.optimization_barrier(
-        (earlier, near, residual, expert_in, expert_out)
-    )
+    shared = slots == 2 and group == t_count and aligned(columns)
+    residual = residual.T.reshape(slots * group, columns, rows)
+    kept_residual = picked(residual.reshape(slots, group * columns, rows), pair ^ t, 0)
+    earlier, near, expert_in, expert_out = lax.optimization_barrier((earlier, near, expert_in, expert_out))
 
     near = swapped(near, "ep", 1)
 
-    route = [
-        (i * t_count + k, (i ^ (group * k)) * t_count + k) for i in range(z_count) for k in range(t_count)
-    ]
-    residual = lax.ppermute(residual, ("ep", "tp"), route)
+    if not shared:
+        route = [
+            (i * t_count + k, (i ^ (group * k)) * t_count + k) for i in range(z_count) for k in range(t_count)
+        ]
+        kept_residual = lax.ppermute(kept_residual, ("ep", "tp"), route)
 
     expert_in = expert_in[0].transpose(0, 2, 1)
     expert_out = expert_out[0]
@@ -372,27 +383,34 @@
     experts_out = [expert_out] + [swapped(expert_out, "sub", e) for e in range(1, s_count)]
     chosen = [z * s_count + (s ^ e) for e in range(s_count)]
 
-    first = (lax.axis_index(("ep", "sub")) == 0).astype(jnp.int32).reshape(1)
+    first = (lax.axis_index(("ep", "sub")) == 0).astype(jnp.int32)
+    below = residual if shared else residual[:, :16]
+    place = jnp.stack([first, (pair ^ 1) * group + t if shared else first * 0])
     attended = attention(
-        queries, earlier, key_rows, value_rows, sink_logits, first, routes.T, route_scores.T
+        queries, earlier, key_rows, value_rows, sink_logits, place, routes.T, route_scores.T, below
     )
     gathered = [attended] + [swapped(attended, "ep", group * j) for j in range(1, slots)]
     experts_out, _ = lax.optimization_barrier((experts_out, attended))
     experts_out = flip(experts_out)
 
-    gathered, near, residual, experts_out = lax.optimization_barrier((gathered, near, residual, experts_out))
+    gathered, near, experts_out = lax.optimization_barrier((gathered, near, experts_out))
     near_weights = [near] + [swapped(near, "sub", u) for u in range(1, s_count)]
-    mine = project(gathered, [out_weight], t, s * 0, t_count)
-    other = project(gathered, near_weights, t, s, t_count)
+    own_share = picked(residual, pair * group + t, 0) if shared else below[0]
+    member = z % group
+    mine = project(gathered, [out_weight], own_share, (t == member) & shared, t, s * 0, t_count)
+    other = project(gathered, near_weights, own_share, (t == member ^ 1) & shared, t, s, t_count)
     first_member = z % group == 0
 
     def ordered(a, b):
         return jnp.concatenate([jnp.where(first_member, a, b), jnp.where(first_member, b, a)], axis=0)
 
-    kept_routes = gathered[0][queries.shape[1] :]
+    span = slice(queries.shape[1], queries.shape[1] + 16)
+    kept_routes = gathered[0][span]
     for j in range(1, slots):
-        kept_routes = jnp.where(t == j, gathered[j][queries.shape[1] :], kept_routes)
-    hidden = ordered(mine[0], other[0]) + residual.astype(jnp.float32)
+        kept_routes = jnp.where(t == j, gathered[j][span], kept_routes)
+    hidden = ordered(mine[0], other[0])
+    if not shared:
+        hidden = hidden + kept_residual.astype(jnp.float32)
     for m in range(1, t_count):
         received = swapped(ordered(mine[1][m - 1], other[1][m - 1]), "tp", m)
         hidden = hidden + received.astype(jnp.float32)
@@ -439,9 +457,7 @@
         part = [[pieces[m][group * r + p] for r in range(slots)] for m in range(t_count)]
         if p:
             part, after = lax.optimization_barrier((part, after))
-        activated, share = activate(
-            part, gain_table, experts_in, pair, t, chosen, experts_out if p == group - 1 else []
-        )
+        activated, share = activate(part, gain_table, experts_in, pair, t, chosen)
         after = activated
         activated = [activated] + [swapped(activated, "tp", m) for m in range(1, t_count)]
         for j, result in enumerate(combine(activated, share, experts_out, t, slots)):

time: 186 us -> 184 us (0.989)
  waiting for transfers between devices: 77.4 us -> 83.6 us
  starting transfers between devices: 34.8 us -> 28.9 us
  Pallas kernels: 39.7 us -> 36.6 us
    ppermute x18, waiting for transfers between devices: 77.4 us -> 83.6 us  [swapped(): lax.ppermute(block, axis, [(i, i ^ distance) for i in range(lax.axis_size...]
    ppermute x18, starting transfers between devices: 30.8 us -> 26.5 us  [swapped(): lax.ppermute(block, axis, [(i, i ^ distance) for i in range(lax.axis_size...]
    pallas_call x2, Pallas kernels: 17.9 us -> 15.4 us  [activate(): pl.pallas_call(kernel, out_shape=(jax.ShapeDtypeStruct((experts, units, l...]
    unnamed x54 -> x48, local copies, waits for them, and re-layouts: 26.4 us -> 26.7 us
  transfers between devices with their start and end apart: 20 -> 19, of which waited for: 11 -> 11; matrix products, arithmetic and copies ran while one was open for 3% -> 3% of each run, Pallas kernels for 21% -> 20%
where the time goes in v13:
time: 184 us; the launch traced here: 183 us
  waiting for transfers between devices  83.6 us (45%)
  Pallas kernels  36.6 us (20%)
  local copies, waits for them, and re-layouts  30.5 us (17%)
  starting transfers between devices  28.9 us (16%)
  other arithmetic  2.97 us (2%)
    ppermute x18, waiting for transfers between devices, swapped(): lax.ppermute(block, axis, [(i, i ^ distance) for i in range(lax.axis_size...  83.6 us
    unnamed x48, local copies, waits for them, and re-layouts  26.7 us
    ppermute x18, starting transfers between devices, swapped(): lax.ppermute(block, axis, [(i, i ^ distance) for i in range(lax.axis_size...  26.5 us
    pallas_call x2, Pallas kernels, activate(): pl.pallas_call(kernel, out_shape=(jax.ShapeDtypeStruct((experts, units, l...  15.4 us
    pallas_call x2, Pallas kernels, combine(): pl.pallas_call(kernel, out_shape=tuple((jax.ShapeDtypeStruct((width, rows...  6.33 us
    pallas_call x1, Pallas kernels, attention(): pl.pallas_call(attention_kernel, out_shape=jax.ShapeDtypeStruct((width +...  5.55 us
    pallas_call x1, Pallas kernels, flip(): pl.pallas_call(kernel, out_shape=tuple((jax.ShapeDtypeStruct(a.shape[::-1...  4.73 us
    pallas_call x2, Pallas kernels, project(): pl.pallas_call(kernel, out_shape=(jax.ShapeDtypeStruct((columns, rows), j...  4.58 us
  transfers between devices with their start and end apart: 19, of which 11 were waited for; matrix products, arithmetic and copies ran while one was open for 3% of the time, Pallas kernels for 20%

profile of v13, /device:TPU:0, one launch (start us, length us, event | category | flops | bytes accessed | tf_op | source)
XLA Modules:
  0.0 182.8 jit_solution(13709626970381016480)
XLA Ops:
  0.0 0.9 pad_maximum_fusion.2
  0.9 2.4 %collective-permute-start = (bf16[128,512]{1,0:T(8,128)(2,1)S(1)}, bf16[128,512]{1,0:T(8,128)(2,1)S(1)}, u32[]{:S(2)}, u32[]{:S(2)}) collective-permute-start(bf16[128,512]{1,0:T(8,128)(2,1)S(1)} %pad_maximum_fusion.2), channel_id=1, source_target_pairs={{0,1},{1,4},{4,5},{5,8},{8,9},{9,12},{12,13},{2,3},{3,6},{6,7},{7,... | collective-permute-start | bytes 393224 | tf_op jit(solution)/shard_map/ppermute | solution.py:18
  3.3 2.6 %dynamic-slice_bitcast_fusion = bf16[720,1024]{1,0:T(8,128)(2,1)} fusion(bf16[2048,720]{0,1:T(8,128)(2,1)} %param.15, s32[]{:T(128)S(6)} %select_n.95), kind=kLoop, calls=%fused_computation | loop fusion | bytes 2949124 | tf_op jit(solution)/shard_map/dynamic_slice | solution.py:366
  5.9 2.7 %collective-permute-start.3 = (bf16[1440,1440]{1,0:T(8,128)(2,1)}, bf16[1440,1440]{1,0:T(8,128)(2,1)}, u32[]{:S(2)}, u32[]{:S(2)}) collective-permute-start(bf16[1440,1440]{1,0:T(8,128)(2,1)} %bitcast.34), channel_id=1, source_target_pairs={{0,1},{1,0},{2,3},{3,2},{4,5},{5,4},{6,7},{7,6},{8,9},{9,8},{10,11... | collective-permute-start | bytes 12441608 | tf_op jit(solution)/shard_map/ppermute | solution.py:22
  8.6 2.2 %collective-permute-start.2 = (bf16[720,1024]{1,0:T(8,128)(2,1)}, bf16[720,1024]{1,0:T(8,128)(2,1)}, u32[]{:S(2)}, u32[]{:S(2)}) collective-permute-start(bf16[720,1024]{1,0:T(8,128)(2,1)} %dynamic-slice_bitcast_fusion), channel_id=1, source_target_pairs={{0,4},{4,0},{8,12},{12,8},{1,5},{5,1},{9,13},{13,9},{2,6},{6,2},{1... | collective-permute-start | bytes 4423688 | tf_op jit(solution)/shard_map/ppermute | solution.py:22
  10.8 1.1 copy-done.14
  11.9 1.0 copy-done.15
  12.9 0.8 copy-done.16
  16.6 5.5 %attention.1.refs_0_ = bf16[2784,128]{1,0:T(8,128)(2,1)S(1)} custom-call(s32[2]{0:T(128)S(1)} %pad_add_fusion.1.place_ref, f32[32]{0:T(128)S(1)} %copy-done.20, bf16[128,2048]{1,0:T(8,128)(2,1)S(1)} %copy-done.15, bf16[128,512]{1,0:T(8,128)(2,1)S(1)} %collective-permute-done.earlier_ref, bf16[128,256]{1,0:T(8,128)(2,1)S(1)} %copy-done.17, ...), custom_call_target="tpu_custom_call" | custom-call | flops 268435456 | bytes 1572864 | tf_op jit(solution)/shard_map/attention/pallas_call | solution.py:128
  22.2 2.7 %collective-permute-start.1 = (bf16[2784,128]{1,0:T(8,128)(2,1)S(1)}, bf16[2784,128]{1,0:T(8,128)(2,1)S(1)}, u32[]{:S(2)}, u32[]{:S(2)}) collective-permute-start(bf16[2784,128]{1,0:T(8,128)(2,1)S(1)} %attention.1.refs_0_), channel_id=1, source_target_pairs={{0,8},{4,12},{8,0},{12,4},{1,9},{5,13},{9,1},{13,5},{2,10},{6,14},... | collective-permute-start | bytes 2138120 | tf_op jit(solution)/shard_map/ppermute | solution.py:22
  24.9 2.3 %copy-done.10 = bf16[1,1440,1440]{2,1,0:T(8,128)(2,1)S(1)} copy-done((bf16[1,1440,1440]{2,1,0:T(8,128)(2,1)S(1)}, bf16[1,1440,1440]{2,1,0:T(8,128)(2,1)}, u32[]{:S(2)}) %copy-start.10) | copy-done | bytes 4147224
  27.1 4.7 %flip.1 = (bf16[1440,1440]{1,0:T(8,128)(2,1)S(1)}, bf16[1440,1440]{1,0:T(8,128)(2,1)S(1)}) custom-call(bf16[1440,1440]{1,0:T(8,128)(2,1)S(1)} %bitcast.35, bf16[1440,1440]{1,0:T(8,128)(2,1)} %collective-permute-done.3.refs_1_), custom_call_target="tpu_custom_call" | custom-call | bytes 16588800 | tf_op jit(solution)/shard_map/flip/pallas_call | solution.py:144
  31.9 2.1 %copy-done.2 = bf16[1440,1440]{1,0:T(8,128)(2,1)} copy-done((bf16[1440,1440]{1,0:T(8,128)(2,1)}, bf16[1440,1440]{1,0:T(8,128)(2,1)S(1)}, u32[]{:S(2)}) %copy-start.2) | copy-done | bytes 4147224
  34.0 2.0 %copy-done.4 = bf16[1440,1440]{1,0:T(8,128)(2,1)} copy-done((bf16[1440,1440]{1,0:T(8,128)(2,1)}, bf16[1440,1440]{1,0:T(8,128)(2,1)S(1)}, u32[]{:S(2)}) %copy-start.4) | copy-done | bytes 4147224
  36.0 21.9 %collective-permute-done.1.refs_1_ = bf16[2784,128]{1,0:T(8,128)(2,1)S(1)} collective-permute-done((bf16[2784,128]{1,0:T(8,128)(2,1)S(1)}, bf16[2784,128]{1,0:T(8,128)(2,1)S(1)}, u32[]{:S(2)}, u32[]{:S(2)}) %collective-permute-start.1) | collective-permute-done | bytes 712736 | tf_op jit(solution)/shard_map/ppermute | solution.py:22
  57.9 0.9 copy-done.11
  59.1 0.9 dynamic-slice_bitcast_fusion.1.refs_3_.refs_4_
  60.1 1.1 copy-done.8
  61.2 1.1 copy-done.12
  62.3 1.6 project.2
  63.9 3.0 %project.3 = (f32[720,128]{1,0:T(8,128)S(1)}, bf16[1,720,128]{2,1,0:T(8,128)(2,1)S(1)}) custom-call(s32[3]{0:T(128)S(1)} %pad_add_fusion.2.place_ref, bf16[2784,128]{1,0:T(8,128)(2,1)S(1)} %copy-done.9, bf16[2784,128]{1,0:T(8,128)(2,1)S(1)} %copy-done.13, bf16[720,1024]{1,0:T(8,128)(2,1)} %collective-permute-done.2.refs_2_, ...), custom_call_target="tpu_custom_call" | custom-call | flops 754974720 | bytes 2949120 | tf_op jit(solution)/shard_map/project/pallas_call | solution.py:188
  67.0 1.6 collective-permute-start.5
  68.6 9.4 %collective-permute-done.5 = bf16[1440,128]{1,0:T(8,128)(2,1)S(1)} collective-permute-done((bf16[1440,128]{1,0:T(8,128)(2,1)S(1)}, bf16[1440,128]{1,0:T(8,128)(2,1)S(1)}, u32[]{:S(2)}, u32[]{:S(2)}) %collective-permute-start.5) | collective-permute-done | bytes 368672 | tf_op jit(solution)/shard_map/ppermute | solution.py:22
  78.4 3.4 %collective-permute-start.6 = (bf16[1456,128]{1,0:T(8,128)(2,1)S(1)}, bf16[1456,128]{1,0:T(8,128)(2,1)S(1)}, u32[]{:S(2)}, u32[]{:S(2)}) collective-permute-start(bf16[1456,128]{1,0:T(8,128)(2,1)S(1)} %pad_maximum_fusion.refs_0_), channel_id=1, source_target_pairs={{0,8},{4,12},{8,0},{12,4},{1,9},{5,13},{9,1},{13,5},{2,10},{6,14},... | collective-permute-start | bytes 1118216 | tf_op jit(solution)/shard_map/ppermute | solution.py:22
  81.9 0.9 collective-permute-start.7
  82.8 1.5 collective-permute-start.9
  84.3 13.9 %collective-permute-done.6.refs_1_ = bf16[1456,128]{1,0:T(8,128)(2,1)S(1)} collective-permute-done((bf16[1456,128]{1,0:T(8,128)(2,1)S(1)}, bf16[1456,128]{1,0:T(8,128)(2,1)S(1)}, u32[]{:S(2)}, u32[]{:S(2)}) %collective-permute-start.6) | collective-permute-done | bytes 372768 | tf_op jit(solution)/shard_map/ppermute | solution.py:22
  98.3 1.5 collective-permute-start.10
  100.2 3.4 %copy-done = bf16[1,2,2880,720]{2,3,1,0:T(8,128)(2,1)S(1)} copy-done((bf16[1,2,2880,720]{2,3,1,0:T(8,128)(2,1)S(1)}, bf16[1,2,2880,720]{2,3,1,0:T(8,128)(2,1)}, u32[]{:S(2)}) %copy-start) | copy-done | bytes 8294424
  103.6 4.3 %collective-permute-done.10.refs_3_ = bf16[1456,128]{1,0:T(8,128)(2,1)S(1)} collective-permute-done((bf16[1456,128]{1,0:T(8,128)(2,1)S(1)}, bf16[1456,128]{1,0:T(8,128)(2,1)S(1)}, u32[]{:S(2)}, u32[]{:S(2)}) %collective-permute-start.10) | collective-permute-done | bytes 372768 | tf_op jit(solution)/shard_map/ppermute | solution.py:22
  107.9 1.3 collective-permute-done.8.refs_1_
  109.8 1.5 collective-permute-start.15
  111.3 3.4 %copy-done.1 = bf16[1,2,2880,720]{2,3,1,0:T(8,128)(2,1)S(1)} copy-done((bf16[1,2,2880,720]{2,3,1,0:T(8,128)(2,1)S(1)}, bf16[1,2,2880,720]{2,3,1,0:T(8,128)(2,1)}, u32[]{:S(2)}) %copy-start.1) | copy-done | bytes 8294424
  114.7 7.4 %activate.2 = (bf16[2,720,256]{2,1,0:T(8,128)(2,1)S(1)}, f32[2,256]{1,0:T(2,128)S(1)}) custom-call(s32[4]{0:T(128)S(1)} %pad_add_fusion.3.place_ref, bf16[1456,128]{1,0:T(8,128)(2,1)S(1)} %pad_maximum_fusion.refs_0_, bf16[1456,128]{1,0:T(8,128)(2,1)S(1)} %collective-permute-done.6.refs_1_, bf16[1456,128]{1,0:T(8,128)(2,1)S(1)} %collective-permute-done.9.refs_2_, ...), custom_call_target="tpu_custom_call" | custom-call | flops 4246732800 | bytes 16588800 | tf_op jit(solution)/shard_map/activate/pallas_call | solution.py:258
  122.7 6.4 %collective-permute-done.15.refs_3_ = bf16[1456,128]{1,0:T(8,128)(2,1)S(1)} collective-permute-done((bf16[1456,128]{1,0:T(8,128)(2,1)}, bf16[1456,128]{1,0:T(8,128)(2,1)S(1)}, u32[]{:S(2)}, u32[]{:S(2)}) %collective-permute-start.15) | collective-permute-done | bytes 372768 | tf_op jit(solution)/shard_map/ppermute | solution.py:22
  129.1 8.0 %activate.3 = (bf16[2,720,256]{2,1,0:T(8,128)(2,1)S(1)}, f32[2,256]{1,0:T(2,128)S(1)}) custom-call(s32[4]{0:T(128)S(1)} %pad_add_fusion.3.place_ref, bf16[1456,128]{1,0:T(8,128)(2,1)} %collective-permute-done.7.refs_0_, bf16[1456,128]{1,0:T(8,128)(2,1)} %collective-permute-done.8.refs_1_, bf16[1456,128]{1,0:T(8,128)(2,1)S(1)} %collective-permute-done.14.refs_2_, ...), custom_call_target="tpu_custom_call" | custom-call | flops 4246732800 | bytes 16588800 | tf_op jit(solution)/shard_map/activate/pallas_call | solution.py:258
  137.7 7.2 %collective-permute-done.12.refs_1_ = bf16[2,720,256]{2,1,0:T(8,128)(2,1)S(1)} collective-permute-done((bf16[2,720,256]{2,1,0:T(8,128)(2,1)S(1)}, bf16[2,720,256]{2,1,0:T(8,128)(2,1)S(1)}, u32[]{:S(2)}, u32[]{:S(2)}) %collective-permute-start.12) | collective-permute-done | bytes 737312 | tf_op jit(solution)/shard_map/ppermute | solution.py:22
  144.9 2.3 %copy-done.3 = bf16[1440,1440]{1,0:T(8,128)(2,1)S(1)} copy-done((bf16[1440,1440]{1,0:T(8,128)(2,1)S(1)}, bf16[1440,1440]{1,0:T(8,128)(2,1)}, u32[]{:S(2)}) %copy-start.3) | copy-done | bytes 4147224
  147.1 2.3 %copy-done.5 = bf16[1440,1440]{1,0:T(8,128)(2,1)S(1)} copy-done((bf16[1440,1440]{1,0:T(8,128)(2,1)S(1)}, bf16[1440,1440]{1,0:T(8,128)(2,1)}, u32[]{:S(2)}) %copy-start.5) | copy-done | bytes 4147224
  149.4 2.6 %combine.2 = (bf16[1440,128]{1,0:T(8,128)(2,1)S(1)}, bf16[1440,128]{1,0:T(8,128)(2,1)S(1)}) custom-call(s32[1]{0:T(128)} %bitcast.t_ref, bf16[2,720,256]{2,1,0:T(8,128)(2,1)S(1)} %get-tuple-element.57.refs_0_, bf16[2,720,256]{2,1,0:T(8,128)(2,1)S(1)} %collective-permute-done.12.refs_1_, f32[2,256]{1,0:T(2,128)S(1)} %get-tuple-element.58.refs_2_, ...), custom_call_target="tpu_custom_call" | custom-call | flops 2123366400 | bytes 8294400 | tf_op jit(solution)/shard_map/combine/pallas_call | solution.py:323
  152.0 2.3 %collective-permute-start.13 = (bf16[1440,128]{1,0:T(8,128)(2,1)S(1)}, bf16[1440,128]{1,0:T(8,128)(2,1)S(1)}, u32[]{:S(2)}, u32[]{:S(2)}) collective-permute-start(bf16[1440,128]{1,0:T(8,128)(2,1)S(1)} %get-tuple-element.62), channel_id=1, source_target_pairs={{0,8},{4,12},{8,0},{12,4},{1,9},{5,13},{9,1},{13,5},{2,10},{6,14},... | collective-permute-start | bytes 1105928 | tf_op jit(solution)/shard_map/ppermute | solution.py:22
  154.3 3.4 %collective-permute-done.16.refs_1_ = bf16[2,720,256]{2,1,0:T(8,128)(2,1)} collective-permute-done((bf16[2,720,256]{2,1,0:T(8,128)(2,1)S(1)}, bf16[2,720,256]{2,1,0:T(8,128)(2,1)}, u32[]{:S(2)}, u32[]{:S(2)}) %collective-permute-start.16) | collective-permute-done | bytes 737312 | tf_op jit(solution)/shard_map/ppermute | solution.py:22
  157.7 3.7 %combine.3 = (bf16[1440,128]{1,0:T(8,128)(2,1)S(1)}, bf16[1440,128]{1,0:T(8,128)(2,1)S(1)}) custom-call(s32[1]{0:T(128)} %bitcast.t_ref, bf16[2,720,256]{2,1,0:T(8,128)(2,1)S(1)} %get-tuple-element.69.refs_0_, bf16[2,720,256]{2,1,0:T(8,128)(2,1)} %collective-permute-done.16.refs_1_, f32[2,256]{1,0:T(2,128)S(1)} %get-tuple-element.70.refs_2_, ...), custom_call_target="tpu_custom_call" | custom-call | flops 2123366400 | bytes 8294400 | tf_op jit(solution)/shard_map/combine/pallas_call | solution.py:323
  161.4 1.0 collective-permute-start.17
  162.5 3.3 %collective-permute-start.18 = (bf16[1440,128]{1,0:T(8,128)(2,1)S(1)}, bf16[1440,128]{1,0:T(8,128)(2,1)S(1)}, u32[]{:S(2)}, u32[]{:S(2)}) collective-permute-start(bf16[1440,128]{1,0:T(8,128)(2,1)S(1)} %get-tuple-element.72), channel_id=1, source_target_pairs={{0,12},{4,8},{8,4},{12,0},{1,13},{5,9},{9,5},{13,1},{2,14},{6,10},... | collective-permute-start | bytes 1105928 | tf_op jit(solution)/shard_map/ppermute | solution.py:22
  166.1 2.2 %collective-permute-done.13 = bf16[1440,128]{1,0:T(8,128)(2,1)S(1)} collective-permute-done((bf16[1440,128]{1,0:T(8,128)(2,1)S(1)}, bf16[1440,128]{1,0:T(8,128)(2,1)S(1)}, u32[]{:S(2)}, u32[]{:S(2)}) %collective-permute-start.13) | collective-permute-done | bytes 368672 | tf_op jit(solution)/shard_map/ppermute | solution.py:22
  168.3 13.4 %collective-permute-done.17 = bf16[1440,128]{1,0:T(8,128)(2,1)S(1)} collective-permute-done((bf16[1440,128]{1,0:T(8,128)(2,1)S(1)}, bf16[1440,128]{1,0:T(8,128)(2,1)S(1)}, u32[]{:S(2)}, u32[]{:S(2)}) %collective-permute-start.17) | collective-permute-done | bytes 368672 | tf_op jit(solution)/shard_map/ppermute | solution.py:22
  181.8 1.0 fusion.2
  (71 shorter events, 6.3 us)
Async XLA Ops:
  0.9 5.0 %collective-permute-start = (bf16[128,512]{1,0:T(8,128)(2,1)S(1)}, bf16[128,512]{1,0:T(8,128)(2,1)S(1)}, u32[]{:S(2)}, u32[]{:S(2)}) collective-permute-start(bf16[128,512]{1,0:T(8,128)(2,1)S(1)} %pad_maximum_fusion.2), channel_id=1, source_target_pairs={{0,1},{1,4},{4,5},{5,8},{8,9},{9,12},{12,13},{2,3},{3,6},{6,7},{7,... | collective-permute-start | bytes 393224 | tf_op jit(solution)/shard_map/ppermute | solution.py:18
  5.9 19.0 %collective-permute-start.3 = (bf16[1440,1440]{1,0:T(8,128)(2,1)}, bf16[1440,1440]{1,0:T(8,128)(2,1)}, u32[]{:S(2)}, u32[]{:S(2)}) collective-permute-start(bf16[1440,1440]{1,0:T(8,128)(2,1)} %bitcast.34), channel_id=1, source_target_pairs={{0,1},{1,0},{2,3},{3,2},{4,5},{5,4},{6,7},{7,6},{8,9},{9,8},{10,11... | collective-permute-start | bytes 12441608 | tf_op jit(solution)/shard_map/ppermute | solution.py:22
  8.5 102.8 %collective-permute-start.11 = (bf16[2,720,2880]{2,1,0:T(8,128)(2,1)}, bf16[2,720,2880]{2,1,0:T(8,128)(2,1)}, u32[]{:S(2)}, u32[]{:S(2)}) collective-permute-start(bf16[2,720,2880]{2,1,0:T(8,128)(2,1)} %bitcast.29), channel_id=1, source_target_pairs={{0,1},{1,0},{2,3},{3,2},{4,5},{5,4},{6,7},{7,6},{8,9},{9,8},{10,11... | collective-permute-start | bytes 24883208 | tf_op jit(solution)/shard_map/ppermute | solution.py:22
  8.6 50.3 %collective-permute-start.2 = (bf16[720,1024]{1,0:T(8,128)(2,1)}, bf16[720,1024]{1,0:T(8,128)(2,1)}, u32[]{:S(2)}, u32[]{:S(2)}) collective-permute-start(bf16[720,1024]{1,0:T(8,128)(2,1)} %dynamic-slice_bitcast_fusion), channel_id=1, source_target_pairs={{0,4},{4,0},{8,12},{12,8},{1,5},{5,1},{9,13},{13,9},{2,6},{6,2},{1... | collective-permute-start | bytes 4423688 | tf_op jit(solution)/shard_map/ppermute | solution.py:22
  10.8 1.1 copy-start.14
  11.9 1.0 copy-start.15
  12.9 0.8 copy-start.16
  13.8 0.8 copy-start.17
  14.6 0.7 copy-start.18
  15.3 0.7 copy-start.19
  16.0 0.7 copy-start.20
  16.6 42.2 %copy-start.23 = (f32[2880]{0:T(1024)S(1)}, f32[2880]{0:T(1024)}, u32[]{:S(2)}) copy-start(f32[2880]{0:T(1024)} %param.17) | copy-start | bytes 34564
  22.2 36.6 %copy-start.7 = (bf16[2784,128]{1,0:T(8,128)(2,1)}, bf16[2784,128]{1,0:T(8,128)(2,1)S(1)}, u32[]{:S(2)}) copy-start(bf16[2784,128]{1,0:T(8,128)(2,1)S(1)} %attention.1.refs_0_) | copy-start | bytes 2138116
  22.2 37.9 %copy-start.6 = (bf16[2048,720]{0,1:T(8,128)(2,1)S(1)}, bf16[2048,720]{0,1:T(8,128)(2,1)}, u32[]{:S(2)}) copy-start(bf16[2048,720]{0,1:T(8,128)(2,1)} %param.15) | copy-start | bytes 8847364
  22.2 35.7 %collective-permute-start.1 = (bf16[2784,128]{1,0:T(8,128)(2,1)S(1)}, bf16[2784,128]{1,0:T(8,128)(2,1)S(1)}, u32[]{:S(2)}, u32[]{:S(2)}) collective-permute-start(bf16[2784,128]{1,0:T(8,128)(2,1)S(1)} %attention.1.refs_0_), channel_id=1, source_target_pairs={{0,8},{4,12},{8,0},{12,4},{1,9},{5,13},{9,1},{13,5},{2,10},{6,14},... | collective-permute-start | bytes 2138120 | tf_op jit(solution)/shard_map/ppermute | solution.py:22
  24.9 2.3 %copy-start.10 = (bf16[1,1440,1440]{2,1,0:T(8,128)(2,1)S(1)}, bf16[1,1440,1440]{2,1,0:T(8,128)(2,1)}, u32[]{:S(2)}) copy-start(bf16[1,1440,1440]{2,1,0:T(8,128)(2,1)} %param.19) | copy-start | bytes 12441604
  31.9 2.1 %copy-start.2 = (bf16[1440,1440]{1,0:T(8,128)(2,1)}, bf16[1440,1440]{1,0:T(8,128)(2,1)S(1)}, u32[]{:S(2)}) copy-start(bf16[1440,1440]{1,0:T(8,128)(2,1)S(1)} %get-tuple-element.59.refs_3_) | copy-start | bytes 12441604
  34.0 2.0 %copy-start.4 = (bf16[1440,1440]{1,0:T(8,128)(2,1)}, bf16[1440,1440]{1,0:T(8,128)(2,1)S(1)}, u32[]{:S(2)}) copy-start(bf16[1440,1440]{1,0:T(8,128)(2,1)S(1)} %get-tuple-element.60.refs_4_) | copy-start | bytes 12441604
  57.9 0.9 copy-start.11
  58.8 5.0 %collective-permute-start.4 = (bf16[720,1024]{1,0:T(8,128)(2,1)}, bf16[720,1024]{1,0:T(8,128)(2,1)}, u32[]{:S(2)}, u32[]{:S(2)}) collective-permute-start(bf16[720,1024]{1,0:T(8,128)(2,1)} %collective-permute-done.2.refs_2_), channel_id=1, source_target_pairs={{0,1},{1,0},{2,3},{3,2},{4,5},{5,4},{6,7},{7,6},{8,9},{9,8},{10,11... | collective-permute-start | bytes 4423688 | tf_op jit(solution)/shard_map/ppermute | solution.py:22
  60.1 1.1 copy-start.8
  61.2 1.1 copy-start.12
  62.3 1.6 copy-start.9
  62.3 1.6 copy-start.13
  67.0 11.1 %collective-permute-start.5 = (bf16[1440,128]{1,0:T(8,128)(2,1)S(1)}, bf16[1440,128]{1,0:T(8,128)(2,1)S(1)}, u32[]{:S(2)}, u32[]{:S(2)}) collective-permute-start(bf16[1440,128]{1,0:T(8,128)(2,1)S(1)} %pad_maximum_fusion.1), channel_id=1, source_target_pairs={{0,2},{2,0},{1,3},{3,1},{4,6},{6,4},{5,7},{7,5},{8,10},{10,8},{9,1... | collective-permute-start | bytes 1105928 | tf_op jit(solution)/shard_map/ppermute | solution.py:22
  78.3 21.4 %copy-start.21 = (bf16[1440,128]{1,0:T(8,128)(2,1)}, bf16[1440,128]{1,0:T(8,128)(2,1)S(1)}, u32[]{:S(2)}) copy-start(bf16[1440,128]{1,0:T(8,128)(2,1)S(1)} %fusion.1) | copy-start | bytes 1105924
  78.4 19.9 %collective-permute-start.6 = (bf16[1456,128]{1,0:T(8,128)(2,1)S(1)}, bf16[1456,128]{1,0:T(8,128)(2,1)S(1)}, u32[]{:S(2)}, u32[]{:S(2)}) collective-permute-start(bf16[1456,128]{1,0:T(8,128)(2,1)S(1)} %pad_maximum_fusion.refs_0_), channel_id=1, source_target_pairs={{0,8},{4,12},{8,0},{12,4},{1,9},{5,13},{9,1},{13,5},{2,10},{6,14},... | collective-permute-start | bytes 1118216 | tf_op jit(solution)/shard_map/ppermute | solution.py:22
  81.9 21.7 %collective-permute-start.7 = (bf16[1456,128]{1,0:T(8,128)(2,1)S(1)}, bf16[1456,128]{1,0:T(8,128)(2,1)}, u32[]{:S(2)}, u32[]{:S(2)}) collective-permute-start(bf16[1456,128]{1,0:T(8,128)(2,1)S(1)} %pad_maximum_fusion.refs_0_), channel_id=1, source_target_pairs={{0,4},{4,0},{8,12},{12,8},{1,5},{5,1},{9,13},{13,9},{2,6},{6,2},{1... | collective-permute-start | bytes 1118216 | tf_op jit(solution)/shard_map/ppermute | solution.py:22
  82.8 20.8 %collective-permute-start.9 = (bf16[1456,128]{1,0:T(8,128)(2,1)S(1)}, bf16[1456,128]{1,0:T(8,128)(2,1)S(1)}, u32[]{:S(2)}, u32[]{:S(2)}) collective-permute-start(bf16[1456,128]{1,0:T(8,128)(2,1)S(1)} %pad_maximum_fusion.refs_0_), channel_id=1, source_target_pairs={{0,2},{2,0},{1,3},{3,1},{4,6},{6,4},{5,7},{7,5},{8,10},{10,8},{9,1... | collective-permute-start | bytes 1118216 | tf_op jit(solution)/shard_map/ppermute | solution.py:22
  98.3 9.7 %collective-permute-start.10 = (bf16[1456,128]{1,0:T(8,128)(2,1)S(1)}, bf16[1456,128]{1,0:T(8,128)(2,1)S(1)}, u32[]{:S(2)}, u32[]{:S(2)}) collective-permute-start(bf16[1456,128]{1,0:T(8,128)(2,1)S(1)} %collective-permute-done.6.refs_1_), channel_id=1, source_target_pairs={{0,2},{2,0},{1,3},{3,1},{4,6},{6,4},{5,7},{7,5},{8,10},{10,8},{9,1... | collective-permute-start | bytes 1118216 | tf_op jit(solution)/shard_map/ppermute | solution.py:22
  99.8 9.5 %collective-permute-start.8 = (bf16[1456,128]{1,0:T(8,128)(2,1)S(1)}, bf16[1456,128]{1,0:T(8,128)(2,1)}, u32[]{:S(2)}, u32[]{:S(2)}) collective-permute-start(bf16[1456,128]{1,0:T(8,128)(2,1)S(1)} %collective-permute-done.6.refs_1_), channel_id=1, source_target_pairs={{0,4},{4,0},{8,12},{12,8},{1,5},{5,1},{9,13},{13,9},{2,6},{6,2},{1... | collective-permute-start | bytes 1118216 | tf_op jit(solution)/shard_map/ppermute | solution.py:22
  100.2 3.4 %copy-start = (bf16[1,2,2880,720]{2,3,1,0:T(8,128)(2,1)S(1)}, bf16[1,2,2880,720]{2,3,1,0:T(8,128)(2,1)}, u32[]{:S(2)}) copy-start(bf16[1,2,2880,720]{2,3,1,0:T(8,128)(2,1)} %param.18) | copy-start | bytes 24883204
  109.3 13.4 %collective-permute-start.14 = (bf16[1456,128]{1,0:T(8,128)(2,1)}, bf16[1456,128]{1,0:T(8,128)(2,1)S(1)}, u32[]{:S(2)}, u32[]{:S(2)}) collective-permute-start(bf16[1456,128]{1,0:T(8,128)(2,1)} %collective-permute-done.7.refs_0_), channel_id=1, source_target_pairs={{0,2},{2,0},{1,3},{3,1},{4,6},{6,4},{5,7},{7,5},{8,10},{10,8},{9,1... | collective-permute-start | bytes 1118216 | tf_op jit(solution)/shard_map/ppermute | solution.py:22
  109.8 19.3 %collective-permute-start.15 = (bf16[1456,128]{1,0:T(8,128)(2,1)}, bf16[1456,128]{1,0:T(8,128)(2,1)S(1)}, u32[]{:S(2)}, u32[]{:S(2)}) collective-permute-start(bf16[1456,128]{1,0:T(8,128)(2,1)} %collective-permute-done.8.refs_1_), channel_id=1, source_target_pairs={{0,2},{2,0},{1,3},{3,1},{4,6},{6,4},{5,7},{7,5},{8,10},{10,8},{9,1... | collective-permute-start | bytes 1118216 | tf_op jit(solution)/shard_map/ppermute | solution.py:22
  111.3 3.4 %copy-start.1 = (bf16[1,2,2880,720]{2,3,1,0:T(8,128)(2,1)S(1)}, bf16[1,2,2880,720]{2,3,1,0:T(8,128)(2,1)}, u32[]{:S(2)}) copy-start(bf16[1,2,2880,720]{2,3,1,0:T(8,128)(2,1)} %param.18) | copy-start | bytes 24883204
  122.1 22.8 %collective-permute-start.12 = (bf16[2,720,256]{2,1,0:T(8,128)(2,1)S(1)}, bf16[2,720,256]{2,1,0:T(8,128)(2,1)S(1)}, u32[]{:S(2)}, u32[]{:S(2)}) collective-permute-start(bf16[2,720,256]{2,1,0:T(8,128)(2,1)S(1)} %get-tuple-element.57.refs_0_), channel_id=1, source_target_pairs={{0,2},{2,0},{1,3},{3,1},{4,6},{6,4},{5,7},{7,5},{8,10},{10,8},{9,1... | collective-permute-start | bytes 2211848 | tf_op jit(solution)/shard_map/ppermute | solution.py:22
  137.1 20.6 %collective-permute-start.16 = (bf16[2,720,256]{2,1,0:T(8,128)(2,1)S(1)}, bf16[2,720,256]{2,1,0:T(8,128)(2,1)}, u32[]{:S(2)}, u32[]{:S(2)}) collective-permute-start(bf16[2,720,256]{2,1,0:T(8,128)(2,1)S(1)} %get-tuple-element.69.refs_0_), channel_id=1, source_target_pairs={{0,2},{2,0},{1,3},{3,1},{4,6},{6,4},{5,7},{7,5},{8,10},{10,8},{9,1... | collective-permute-start | bytes 2211848 | tf_op jit(solution)/shard_map/ppermute | solution.py:22
  144.9 2.3 %copy-start.3 = (bf16[1440,1440]{1,0:T(8,128)(2,1)S(1)}, bf16[1440,1440]{1,0:T(8,128)(2,1)}, u32[]{:S(2)}) copy-start(bf16[1440,1440]{1,0:T(8,128)(2,1)} %copy-done.2) | copy-start | bytes 12441604
  147.1 2.3 %copy-start.5 = (bf16[1440,1440]{1,0:T(8,128)(2,1)S(1)}, bf16[1440,1440]{1,0:T(8,128)(2,1)}, u32[]{:S(2)}) copy-start(bf16[1440,1440]{1,0:T(8,128)(2,1)} %copy-done.4) | copy-start | bytes 12441604
  152.0 16.4 %collective-permute-start.13 = (bf16[1440,128]{1,0:T(8,128)(2,1)S(1)}, bf16[1440,128]{1,0:T(8,128)(2,1)S(1)}, u32[]{:S(2)}, u32[]{:S(2)}) collective-permute-start(bf16[1440,128]{1,0:T(8,128)(2,1)S(1)} %get-tuple-element.62), channel_id=1, source_target_pairs={{0,8},{4,12},{8,0},{12,4},{1,9},{5,13},{9,1},{13,5},{2,10},{6,14},... | collective-permute-start | bytes 1105928 | tf_op jit(solution)/shard_map/ppermute | solution.py:22
  157.7 8.1 %copy-start.22 = (bf16[1440,128]{1,0:T(8,128)(2,1)S(1)}, bf16[1440,128]{1,0:T(8,128)(2,1)}, u32[]{:S(2)}) copy-start(bf16[1440,128]{1,0:T(8,128)(2,1)} %copy-done.21) | copy-start | bytes 1105924
  161.4 20.3 %collective-permute-start.17 = (bf16[1440,128]{1,0:T(8,128)(2,1)S(1)}, bf16[1440,128]{1,0:T(8,128)(2,1)S(1)}, u32[]{:S(2)}, u32[]{:S(2)}) collective-permute-start(bf16[1440,128]{1,0:T(8,128)(2,1)S(1)} %get-tuple-element.71), channel_id=1, source_target_pairs={{0,4},{4,0},{8,12},{12,8},{1,5},{5,1},{9,13},{13,9},{2,6},{6,2},{1... | collective-permute-start | bytes 1105928 | tf_op jit(solution)/shard_map/ppermute | solution.py:22
  162.5 19.3 %collective-permute-start.18 = (bf16[1440,128]{1,0:T(8,128)(2,1)S(1)}, bf16[1440,128]{1,0:T(8,128)(2,1)S(1)}, u32[]{:S(2)}, u32[]{:S(2)}) collective-permute-start(bf16[1440,128]{1,0:T(8,128)(2,1)S(1)} %get-tuple-element.72), channel_id=1, source_target_pairs={{0,12},{4,8},{8,4},{12,0},{1,13},{5,9},{9,5},{13,1},{2,14},{6,10},... | collective-permute-start | bytes 1105928 | tf_op jit(solution)/shard_map/ppermute | solution.py:22

commit v14 on v13

--- a/solution.py
+++ b/solution.py
@@ -278,21 +278,6 @@
     )(jnp.stack([pair, t] + chosen).astype(jnp.int32), *flat, gain_table, *weights)
 
 
-def ready(table, ahead):
-    def kernel(table_ref, ahead_ref, out_ref):
-        out_ref[...] = table_ref[...]
-
-    return pl.pallas_call(
-        kernel,
-        out_shape=jax.ShapeDtypeStruct(table.shape, table.dtype),
-        in_specs=in_vmem(2),
-        out_specs=in_vmem(1)[0],
-        compiler_params=params(4),
-        cost_estimate=cost(0, 4 * table.size),
-        name="ready",
-    )(table, ahead)
-
-
 def combine(activated, share, weights, t, slots):
     t_count = len(activated)
     experts, units, lanes = activated[0].shape
@@ -393,9 +378,10 @@
     experts_out, _ = lax.optimization_barrier((experts_out, attended))
     experts_out = flip(experts_out)
 
-    gathered, near, experts_out = lax.optimization_barrier((gathered, near, experts_out))
+    own_share = picked(residual, pair * group + t, 0) if shared else below[0]
+    own_share, _ = lax.optimization_barrier((own_share, attended))
+    gathered, near, experts_out, own_share = lax.optimization_barrier((gathered, near, experts_out, own_share))
     near_weights = [near] + [swapped(near, "sub", u) for u in range(1, s_count)]
-    own_share = picked(residual, pair * group + t, 0) if shared else below[0]
     member = z % group
     mine = project(gathered, [out_weight], own_share, (t == member) & shared, t, s * 0, t_count)
     other = project(gathered, near_weights, own_share, (t == member ^ 1) & shared, t, s, t_count)
@@ -418,31 +404,29 @@
     scaled = jnp.concatenate([(hidden * gain_part[:, None]).astype(jnp.bfloat16), kept_routes], axis=0)
 
     own = {0: scaled}
-    pieces = [own] + [{} for m in range(1, t_count)]
+    pieces = [own] + [{0: swapped(scaled, "tp", m)} for m in range(1, t_count)]
     distance = z_count // 2
-    while distance:
-        held = list(own)
-        if distance >= group:
-            for m in range(1, t_count):
-                pieces[m].update({d: swapped(own[d], "tp", m) for d in held if d not in pieces[m]})
-        for d in held:
-            own[d + distance] = swapped(own[d], "ep", distance)
+    while distance >= group:
+        own.update({d + distance: swapped(own[d], "ep", distance) for d in list(own)})
         distance //= 2
+    again, pieces[1:] = lax.optimization_barrier((scaled, pieces[1:]))
+    own[1] = swapped(again, "ep", 1)
+    own, pieces[1:] = lax.optimization_barrier((own, pieces[1:]))
+    pieces[0] = own
+    for d in range(group, z_count, group):
+        own[d + 1] = swapped(own[d], "ep", 1)
+        for m in range(1, t_count):
+            pieces[m][d] = swapped(own[d], "tp", m)
     for m in range(1, t_count):
-        pieces[m].update({d: swapped(own[d], "tp", m) for d in range(0, z_count, group) if d not in pieces[m]})
-    late = {d: own[d] for d in own if d % group}
-    late, pieces[1:] = lax.optimization_barrier((late, pieces[1:]))
-    for m in range(1, t_count):
-        pieces[m].update({d: swapped(late[d], "tp", m) for d in late})
+        pieces[m][1] = swapped(pieces[m][0], "ep", 1)
+        for d in range(group, z_count, group):
+            pieces[m][d + 1] = swapped(own[d + 1], "tp", m)
 
     inverse_gain = 1.0 / norm_gain
     inverse_square = inverse_gain * inverse_gain
     coarse = inverse_square.astype(jnp.bfloat16)
     fine = (inverse_square - coarse.astype(jnp.float32)).astype(jnp.bfloat16)
     gain_table = jnp.concatenate([coarse[None], fine[None], jnp.zeros((14, D), jnp.bfloat16)], axis=0)
-
-    gain_table, _ = lax.optimization_barrier((gain_table, scaled))
-    gain_table = ready(gain_table, expert_in)
 
     total = 0.0
     for m in range(t_count):

time: 184 us -> 185 us (level)
  starting transfers between devices: 28.9 us -> 34.8 us
  local copies, waits for them, and re-layouts: 30.5 us -> 25.1 us
  waiting for transfers between devices: 83.6 us -> 79.4 us
  Pallas kernels: 36.6 us -> 39.1 us
    ppermute x18, starting transfers between devices: 26.5 us -> 32.4 us  [swapped(): lax.ppermute(block, axis, [(i, i ^ distance) for i in range(lax.axis_size...]
    unnamed x48 -> x34, local copies, waits for them, and re-layouts: 26.7 us -> 21.3 us
    ppermute x18, waiting for transfers between devices: 83.6 us -> 79.4 us  [swapped(): lax.ppermute(block, axis, [(i, i ^ distance) for i in range(lax.axis_size...]
  transfers between devices with their start and end apart: 19 -> 19, of which waited for: 11 -> 12; matrix products, arithmetic and copies ran while one was open for 3% -> 3% of each run, Pallas kernels for 20% -> 21%
where the time goes in v14:
time: 185 us; the launch traced here: 182 us
  waiting for transfers between devices  79.4 us (43%)
  Pallas kernels  39.1 us (21%)
  starting transfers between devices  34.8 us (19%)
  local copies, waits for them, and re-layouts  25.1 us (14%)
  other arithmetic  3.65 us (2%)
    ppermute x18, waiting for transfers between devices, swapped(): lax.ppermute(block, axis, [(i, i ^ distance) for i in range(lax.axis_size...  79.4 us
    ppermute x18, starting transfers between devices, swapped(): lax.ppermute(block, axis, [(i, i ^ distance) for i in range(lax.axis_size...  32.4 us
    unnamed x34, local copies, waits for them, and re-layouts  21.3 us
    pallas_call x2, Pallas kernels, activate(): pl.pallas_call(kernel, out_shape=(jax.ShapeDtypeStruct((experts, units, l...  14.8 us
    pallas_call x2, Pallas kernels, combine(): pl.pallas_call(kernel, out_shape=tuple((jax.ShapeDtypeStruct((width, rows...  7.4 us
    pallas_call x1, Pallas kernels, attention(): pl.pallas_call(attention_kernel, out_shape=jax.ShapeDtypeStruct((width +...  6.42 us
    pallas_call x2, Pallas kernels, project(): pl.pallas_call(kernel, out_shape=(jax.ShapeDtypeStruct((columns, rows), j...  5.79 us
    pallas_call x1, Pallas kernels, flip(): pl.pallas_call(kernel, out_shape=tuple((jax.ShapeDtypeStruct(a.shape[::-1...  4.75 us
  transfers between devices with their start and end apart: 19, of which 12 were waited for; matrix products, arithmetic and copies ran while one was open for 3% of the time, Pallas kernels for 21%

profile of v14, /device:TPU:0, one launch (start us, length us, event | category | flops | bytes accessed | tf_op | source)
XLA Modules:
  0.0 182.3 jit_solution(15006083676860693703)
XLA Ops:
  0.0 0.9 pad_maximum_fusion.2
  0.9 2.4 %collective-permute-start = (bf16[128,512]{1,0:T(8,128)(2,1)S(1)}, bf16[128,512]{1,0:T(8,128)(2,1)S(1)}, u32[]{:S(2)}, u32[]{:S(2)}) collective-permute-start(bf16[128,512]{1,0:T(8,128)(2,1)S(1)} %pad_maximum_fusion.2), channel_id=1, source_target_pairs={{0,1},{1,4},{4,5},{5,8},{8,9},{9,12},{12,13},{2,3},{3,6},{6,7},{7,... | collective-permute-start | bytes 393224 | tf_op jit(solution)/shard_map/ppermute | solution.py:18
  3.3 2.6 %dynamic-slice_bitcast_fusion = bf16[720,1024]{1,0:T(8,128)(2,1)} fusion(bf16[2048,720]{0,1:T(8,128)(2,1)} %param.15, s32[]{:T(128)S(6)} %select_n.95), kind=kLoop, calls=%fused_computation | loop fusion | bytes 2949124 | tf_op jit(solution)/shard_map/dynamic_slice | solution.py:351
  5.9 2.7 %collective-permute-start.3 = (bf16[1440,1440]{1,0:T(8,128)(2,1)}, bf16[1440,1440]{1,0:T(8,128)(2,1)}, u32[]{:S(2)}, u32[]{:S(2)}) collective-permute-start(bf16[1440,1440]{1,0:T(8,128)(2,1)} %bitcast.33), channel_id=1, source_target_pairs={{0,1},{1,0},{2,3},{3,2},{4,5},{5,4},{6,7},{7,6},{8,9},{9,8},{10,11... | collective-permute-start | bytes 12441608 | tf_op jit(solution)/shard_map/ppermute | solution.py:22
  8.6 2.2 %collective-permute-start.2 = (bf16[720,1024]{1,0:T(8,128)(2,1)}, bf16[720,1024]{1,0:T(8,128)(2,1)}, u32[]{:S(2)}, u32[]{:S(2)}) collective-permute-start(bf16[720,1024]{1,0:T(8,128)(2,1)} %dynamic-slice_bitcast_fusion), channel_id=1, source_target_pairs={{0,4},{4,0},{8,12},{12,8},{1,5},{5,1},{9,13},{13,9},{2,6},{6,2},{1... | collective-permute-start | bytes 4423688 | tf_op jit(solution)/shard_map/ppermute | solution.py:22
  10.8 1.1 copy-done.7
  11.9 1.0 copy-done.8
  12.9 0.8 copy-done.11
  13.8 0.8 copy-done.12
  16.6 6.4 %attention.1.refs_0_ = bf16[2784,128]{1,0:T(8,128)(2,1)} custom-call(s32[2]{0:T(128)S(1)} %pad_add_fusion.1.place_ref, f32[32]{0:T(128)S(1)} %copy-done.15, bf16[128,2048]{1,0:T(8,128)(2,1)S(1)} %copy-done.8, bf16[128,512]{1,0:T(8,128)(2,1)S(1)} %collective-permute-done.earlier_ref, bf16[128,256]{1,0:T(8,128)(2,1)S(1)} %copy-done.12, ...), custom_call_target="tpu_custom_call" | custom-call | flops 268435456 | bytes 1572864 | tf_op jit(solution)/shard_map/attention/pallas_call | solution.py:128
  23.1 2.6 %collective-permute-start.1 = (bf16[2784,128]{1,0:T(8,128)(2,1)}, bf16[2784,128]{1,0:T(8,128)(2,1)}, u32[]{:S(2)}, u32[]{:S(2)}) collective-permute-start(bf16[2784,128]{1,0:T(8,128)(2,1)} %attention.1.refs_0_), channel_id=1, source_target_pairs={{0,8},{4,12},{8,0},{12,4},{1,9},{5,13},{9,1},{13,5},{2,10},{6,14},... | collective-permute-start | bytes 2138120 | tf_op jit(solution)/shard_map/ppermute | solution.py:22
  25.6 0.9 dynamic-slice_bitcast_fusion.1.refs_3_.refs_4_
  26.6 2.4 %copy-done.6 = bf16[1,1440,1440]{2,1,0:T(8,128)(2,1)S(1)} copy-done((bf16[1,1440,1440]{2,1,0:T(8,128)(2,1)S(1)}, bf16[1,1440,1440]{2,1,0:T(8,128)(2,1)}, u32[]{:S(2)}) %copy-start.6) | copy-done | bytes 4147224
  29.0 4.7 %flip.1 = (bf16[1440,1440]{1,0:T(8,128)(2,1)S(1)}, bf16[1440,1440]{1,0:T(8,128)(2,1)S(1)}) custom-call(bf16[1440,1440]{1,0:T(8,128)(2,1)S(1)} %bitcast.34, bf16[1440,1440]{1,0:T(8,128)(2,1)} %collective-permute-done.3.refs_1_), custom_call_target="tpu_custom_call" | custom-call | bytes 16588800 | tf_op jit(solution)/shard_map/flip/pallas_call | solution.py:144
  33.8 2.1 %copy-done.1 = bf16[1440,1440]{1,0:T(8,128)(2,1)} copy-done((bf16[1440,1440]{1,0:T(8,128)(2,1)}, bf16[1440,1440]{1,0:T(8,128)(2,1)S(1)}, u32[]{:S(2)}) %copy-start.1) | copy-done | bytes 4147224
  35.9 2.0 %copy-done.3 = bf16[1440,1440]{1,0:T(8,128)(2,1)} copy-done((bf16[1440,1440]{1,0:T(8,128)(2,1)}, bf16[1440,1440]{1,0:T(8,128)(2,1)S(1)}, u32[]{:S(2)}) %copy-start.3) | copy-done | bytes 4147224
  37.9 20.1 %collective-permute-done.1.refs_1_ = bf16[2784,128]{1,0:T(8,128)(2,1)} collective-permute-done((bf16[2784,128]{1,0:T(8,128)(2,1)}, bf16[2784,128]{1,0:T(8,128)(2,1)}, u32[]{:S(2)}, u32[]{:S(2)}) %collective-permute-start.1) | collective-permute-done | bytes 712736 | tf_op jit(solution)/shard_map/ppermute | solution.py:22
  59.1 2.4 %project.2 = (f32[720,128]{1,0:T(8,128)S(1)}, bf16[1,720,128]{2,1,0:T(8,128)(2,1)S(1)}) custom-call(s32[3]{0:T(128)S(1)} %pad_add_fusion.place_ref, bf16[2784,128]{1,0:T(8,128)(2,1)} %attention.1.refs_0_, bf16[2784,128]{1,0:T(8,128)(2,1)} %collective-permute-done.1.refs_1_, bf16[720,2048]{1,0:T(8,128)(2,1)S(1)} %bitcast.32, ...), custom_call_target="tpu_custom_call" | custom-call | flops 754974720 | bytes 2949120 | tf_op jit(solution)/shard_map/project/pallas_call | solution.py:188
  61.5 1.0 collective-permute-done.4.refs_3_
  62.5 3.4 %project.3 = (f32[720,128]{1,0:T(8,128)S(1)}, bf16[1,720,128]{2,1,0:T(8,128)(2,1)S(1)}) custom-call(s32[3]{0:T(128)S(1)} %pad_add_fusion.2.place_ref, bf16[2784,128]{1,0:T(8,128)(2,1)} %attention.1.refs_0_, bf16[2784,128]{1,0:T(8,128)(2,1)} %collective-permute-done.1.refs_1_, bf16[720,1024]{1,0:T(8,128)(2,1)} %collective-permute-done.2.refs_2_, ...), custom_call_target="tpu_custom_call" | custom-call | flops 754974720 | bytes 2949120 | tf_op jit(solution)/shard_map/project/pallas_call | solution.py:188
  66.0 1.6 collective-permute-start.5
  68.3 8.3 %collective-permute-done.5 = bf16[1440,128]{1,0:T(8,128)(2,1)S(1)} collective-permute-done((bf16[1440,128]{1,0:T(8,128)(2,1)S(1)}, bf16[1440,128]{1,0:T(8,128)(2,1)S(1)}, u32[]{:S(2)}, u32[]{:S(2)}) %collective-permute-start.5) | collective-permute-done | bytes 368672 | tf_op jit(solution)/shard_map/ppermute | solution.py:22
  77.0 1.6 collective-permute-start.6
  78.6 2.6 %collective-permute-start.8 = (bf16[1456,128]{1,0:T(8,128)(2,1)S(1)}, bf16[1456,128]{1,0:T(8,128)(2,1)S(1)}, u32[]{:S(2)}, u32[]{:S(2)}) collective-permute-start(bf16[1456,128]{1,0:T(8,128)(2,1)S(1)} %pad_maximum_fusion.refs_0_), channel_id=1, source_target_pairs={{0,8},{4,12},{8,0},{12,4},{1,9},{5,13},{9,1},{13,5},{2,10},{6,14},... | collective-permute-start | bytes 1118216 | tf_op jit(solution)/shard_map/ppermute | solution.py:22
  81.1 5.8 %collective-permute-done.6.refs_2_ = bf16[1456,128]{1,0:T(8,128)(2,1)S(1)} collective-permute-done((bf16[1456,128]{1,0:T(8,128)(2,1)S(1)}, bf16[1456,128]{1,0:T(8,128)(2,1)S(1)}, u32[]{:S(2)}, u32[]{:S(2)}) %collective-permute-start.6) | collective-permute-done | bytes 372768 | tf_op jit(solution)/shard_map/ppermute | solution.py:22
  86.9 2.7 %collective-permute-start.7 = (bf16[1456,128]{1,0:T(8,128)(2,1)S(1)}, bf16[1456,128]{1,0:T(8,128)(2,1)S(1)}, u32[]{:S(2)}, u32[]{:S(2)}) collective-permute-start(bf16[1456,128]{1,0:T(8,128)(2,1)S(1)} %pad_maximum_fusion.refs_0_), channel_id=1, source_target_pairs={{0,4},{4,0},{8,12},{12,8},{1,5},{5,1},{9,13},{13,9},{2,6},{6,2},{1... | collective-permute-start | bytes 1118216 | tf_op jit(solution)/shard_map/ppermute | solution.py:22
  89.8 7.4 %collective-permute-done.8.refs_1_ = bf16[1456,128]{1,0:T(8,128)(2,1)S(1)} collective-permute-done((bf16[1456,128]{1,0:T(8,128)(2,1)S(1)}, bf16[1456,128]{1,0:T(8,128)(2,1)S(1)}, u32[]{:S(2)}, u32[]{:S(2)}) %collective-permute-start.8) | collective-permute-done | bytes 372768 | tf_op jit(solution)/shard_map/ppermute | solution.py:22
  97.2 5.5 %collective-permute-done.7.refs_0_ = bf16[1456,128]{1,0:T(8,128)(2,1)S(1)} collective-permute-done((bf16[1456,128]{1,0:T(8,128)(2,1)S(1)}, bf16[1456,128]{1,0:T(8,128)(2,1)S(1)}, u32[]{:S(2)}, u32[]{:S(2)}) %collective-permute-start.7) | collective-permute-done | bytes 372768 | tf_op jit(solution)/shard_map/ppermute | solution.py:22
  102.7 1.3 collective-permute-start.9
  104.2 2.0 %collective-permute-start.14 = (bf16[1456,128]{1,0:T(8,128)(2,1)S(1)}, bf16[1456,128]{1,0:T(8,128)(2,1)S(1)}, u32[]{:S(2)}, u32[]{:S(2)}) collective-permute-start(bf16[1456,128]{1,0:T(8,128)(2,1)S(1)} %collective-permute-done.6.refs_2_), channel_id=1, source_target_pairs={{0,4},{4,0},{8,12},{12,8},{1,5},{5,1},{9,13},{13,9},{2,6},{6,2},{1... | collective-permute-start | bytes 1118216 | tf_op jit(solution)/shard_map/ppermute | solution.py:22
  106.2 9.4 %collective-permute-done.13.refs_1_ = bf16[1456,128]{1,0:T(8,128)(2,1)S(1)} collective-permute-done((bf16[1456,128]{1,0:T(8,128)(2,1)S(1)}, bf16[1456,128]{1,0:T(8,128)(2,1)S(1)}, u32[]{:S(2)}, u32[]{:S(2)}) %collective-permute-start.13) | collective-permute-done | bytes 372768 | tf_op jit(solution)/shard_map/ppermute | solution.py:22
  116.4 3.4 %copy-done = bf16[1,2,2880,720]{2,3,1,0:T(8,128)(2,1)S(1)} copy-done((bf16[1,2,2880,720]{2,3,1,0:T(8,128)(2,1)S(1)}, bf16[1,2,2880,720]{2,3,1,0:T(8,128)(2,1)}, u32[]{:S(2)}) %copy-start) | copy-done | bytes 8294424
  119.8 7.4 %activate.2 = (bf16[2,720,256]{2,1,0:T(8,128)(2,1)S(1)}, f32[2,256]{1,0:T(2,128)S(1)}) custom-call(s32[4]{0:T(128)S(1)} %pad_add_fusion.3.place_ref, bf16[1456,128]{1,0:T(8,128)(2,1)S(1)} %pad_maximum_fusion.refs_0_, bf16[1456,128]{1,0:T(8,128)(2,1)S(1)} %collective-permute-done.8.refs_1_, bf16[1456,128]{1,0:T(8,128)(2,1)S(1)} %collective-permute-done.6.refs_2_, ...), custom_call_target="tpu_custom_call" | custom-call | flops 4246732800 | bytes 16588800 | tf_op jit(solution)/shard_map/activate/pallas_call | solution.py:258
  127.2 1.4 collective-permute-start.11
  128.6 1.0 copy-done.10
  129.6 7.4 %activate.3 = (bf16[2,720,256]{2,1,0:T(8,128)(2,1)S(1)}, f32[2,256]{1,0:T(2,128)S(1)}) custom-call(s32[4]{0:T(128)S(1)} %pad_add_fusion.3.place_ref, bf16[1456,128]{1,0:T(8,128)(2,1)S(1)} %collective-permute-done.7.refs_0_, bf16[1456,128]{1,0:T(8,128)(2,1)S(1)} %copy-done.10, bf16[1456,128]{1,0:T(8,128)(2,1)S(1)} %collective-permute-done.14.refs_2_, ...), custom_call_target="tpu_custom_call" | custom-call | flops 4246732800 | bytes 16588800 | tf_op jit(solution)/shard_map/activate/pallas_call | solution.py:258
  137.8 7.7 %collective-permute-done.11.refs_1_ = bf16[2,720,256]{2,1,0:T(8,128)(2,1)} collective-permute-done((bf16[2,720,256]{2,1,0:T(8,128)(2,1)S(1)}, bf16[2,720,256]{2,1,0:T(8,128)(2,1)}, u32[]{:S(2)}, u32[]{:S(2)}) %collective-permute-start.11) | collective-permute-done | bytes 737312 | tf_op jit(solution)/shard_map/ppermute | solution.py:22
  145.5 2.3 %copy-done.2 = bf16[1440,1440]{1,0:T(8,128)(2,1)S(1)} copy-done((bf16[1440,1440]{1,0:T(8,128)(2,1)S(1)}, bf16[1440,1440]{1,0:T(8,128)(2,1)}, u32[]{:S(2)}) %copy-start.2) | copy-done | bytes 4147224
  147.8 2.3 %copy-done.4 = bf16[1440,1440]{1,0:T(8,128)(2,1)S(1)} copy-done((bf16[1440,1440]{1,0:T(8,128)(2,1)S(1)}, bf16[1440,1440]{1,0:T(8,128)(2,1)}, u32[]{:S(2)}) %copy-start.4) | copy-done | bytes 4147224
  150.0 3.7 %combine.2 = (bf16[1440,128]{1,0:T(8,128)(2,1)S(1)}, bf16[1440,128]{1,0:T(8,128)(2,1)S(1)}) custom-call(s32[1]{0:T(128)} %bitcast.t_ref, bf16[2,720,256]{2,1,0:T(8,128)(2,1)S(1)} %get-tuple-element.64.refs_0_, bf16[2,720,256]{2,1,0:T(8,128)(2,1)} %collective-permute-done.11.refs_1_, f32[2,256]{1,0:T(2,128)S(1)} %get-tuple-element.65.refs_2_, ...), custom_call_target="tpu_custom_call" | custom-call | flops 2123366400 | bytes 8294400 | tf_op jit(solution)/shard_map/combine/pallas_call | solution.py:308
  153.7 4.7 %collective-permute-start.12 = (bf16[1440,128]{1,0:T(8,128)(2,1)S(1)}, bf16[1440,128]{1,0:T(8,128)(2,1)S(1)}, u32[]{:S(2)}, u32[]{:S(2)}) collective-permute-start(bf16[1440,128]{1,0:T(8,128)(2,1)S(1)} %get-tuple-element.69), channel_id=1, source_target_pairs={{0,8},{4,12},{8,0},{12,4},{1,9},{5,13},{9,1},{13,5},{2,10},{6,14},... | collective-permute-start | bytes 1105928 | tf_op jit(solution)/shard_map/ppermute | solution.py:22
  158.4 3.7 %combine.3 = (bf16[1440,128]{1,0:T(8,128)(2,1)S(1)}, bf16[1440,128]{1,0:T(8,128)(2,1)S(1)}) custom-call(s32[1]{0:T(128)} %bitcast.t_ref, bf16[2,720,256]{2,1,0:T(8,128)(2,1)S(1)} %get-tuple-element.75.refs_0_, bf16[2,720,256]{2,1,0:T(8,128)(2,1)} %collective-permute-done.16.refs_1_, f32[2,256]{1,0:T(2,128)S(1)} %get-tuple-element.76.refs_2_, ...), custom_call_target="tpu_custom_call" | custom-call | flops 2123366400 | bytes 8294400 | tf_op jit(solution)/shard_map/combine/pallas_call | solution.py:308
  162.1 2.1 %collective-permute-start.17 = (bf16[1440,128]{1,0:T(8,128)(2,1)S(1)}, bf16[1440,128]{1,0:T(8,128)(2,1)S(1)}, u32[]{:S(2)}, u32[]{:S(2)}) collective-permute-start(bf16[1440,128]{1,0:T(8,128)(2,1)S(1)} %get-tuple-element.77), channel_id=1, source_target_pairs={{0,4},{4,0},{8,12},{12,8},{1,5},{5,1},{9,13},{13,9},{2,6},{6,2},{1... | collective-permute-start | bytes 1105928 | tf_op jit(solution)/shard_map/ppermute | solution.py:22
  164.2 3.5 %collective-permute-start.18 = (bf16[1440,128]{1,0:T(8,128)(2,1)S(1)}, bf16[1440,128]{1,0:T(8,128)(2,1)S(1)}, u32[]{:S(2)}, u32[]{:S(2)}) collective-permute-start(bf16[1440,128]{1,0:T(8,128)(2,1)S(1)} %get-tuple-element.78), channel_id=1, source_target_pairs={{0,12},{4,8},{8,4},{12,0},{1,13},{5,9},{9,5},{13,1},{2,14},{6,10},... | collective-permute-start | bytes 1105928 | tf_op jit(solution)/shard_map/ppermute | solution.py:22
  168.0 4.8 %collective-permute-done.12 = bf16[1440,128]{1,0:T(8,128)(2,1)S(1)} collective-permute-done((bf16[1440,128]{1,0:T(8,128)(2,1)S(1)}, bf16[1440,128]{1,0:T(8,128)(2,1)S(1)}, u32[]{:S(2)}, u32[]{:S(2)}) %collective-permute-start.12) | collective-permute-done | bytes 368672 | tf_op jit(solution)/shard_map/ppermute | solution.py:22
  172.8 2.5 %collective-permute-done.17 = bf16[1440,128]{1,0:T(8,128)(2,1)S(1)} collective-permute-done((bf16[1440,128]{1,0:T(8,128)(2,1)S(1)}, bf16[1440,128]{1,0:T(8,128)(2,1)S(1)}, u32[]{:S(2)}, u32[]{:S(2)}) %collective-permute-start.17) | collective-permute-done | bytes 368672 | tf_op jit(solution)/shard_map/ppermute | solution.py:22
  175.3 6.0 %collective-permute-done.18 = bf16[1440,128]{1,0:T(8,128)(2,1)S(1)} collective-permute-done((bf16[1440,128]{1,0:T(8,128)(2,1)S(1)}, bf16[1440,128]{1,0:T(8,128)(2,1)S(1)}, u32[]{:S(2)}, u32[]{:S(2)}) %collective-permute-start.18) | collective-permute-done | bytes 368672 | tf_op jit(solution)/shard_map/ppermute | solution.py:22
  181.3 1.0 fusion.2
  (56 shorter events, 6.5 us)
Async XLA Ops:
  0.9 5.0 %collective-permute-start = (bf16[128,512]{1,0:T(8,128)(2,1)S(1)}, bf16[128,512]{1,0:T(8,128)(2,1)S(1)}, u32[]{:S(2)}, u32[]{:S(2)}) collective-permute-start(bf16[128,512]{1,0:T(8,128)(2,1)S(1)} %pad_maximum_fusion.2), channel_id=1, source_target_pairs={{0,1},{1,4},{4,5},{5,8},{8,9},{9,12},{12,13},{2,3},{3,6},{6,7},{7,... | collective-permute-start | bytes 393224 | tf_op jit(solution)/shard_map/ppermute | solution.py:18
  5.9 20.7 %collective-permute-start.3 = (bf16[1440,1440]{1,0:T(8,128)(2,1)}, bf16[1440,1440]{1,0:T(8,128)(2,1)}, u32[]{:S(2)}, u32[]{:S(2)}) collective-permute-start(bf16[1440,1440]{1,0:T(8,128)(2,1)} %bitcast.33), channel_id=1, source_target_pairs={{0,1},{1,0},{2,3},{3,2},{4,5},{5,4},{6,7},{7,6},{8,9},{9,8},{10,11... | collective-permute-start | bytes 12441608 | tf_op jit(solution)/shard_map/ppermute | solution.py:22
  8.5 107.8 %collective-permute-start.10 = (bf16[2,720,2880]{2,1,0:T(8,128)(2,1)}, bf16[2,720,2880]{2,1,0:T(8,128)(2,1)}, u32[]{:S(2)}, u32[]{:S(2)}) collective-permute-start(bf16[2,720,2880]{2,1,0:T(8,128)(2,1)} %bitcast.29), channel_id=1, source_target_pairs={{0,1},{1,0},{2,3},{3,2},{4,5},{5,4},{6,7},{7,6},{8,9},{9,8},{10,11... | collective-permute-start | bytes 24883208 | tf_op jit(solution)/shard_map/ppermute | solution.py:22
  8.6 50.3 %collective-permute-start.2 = (bf16[720,1024]{1,0:T(8,128)(2,1)}, bf16[720,1024]{1,0:T(8,128)(2,1)}, u32[]{:S(2)}, u32[]{:S(2)}) collective-permute-start(bf16[720,1024]{1,0:T(8,128)(2,1)} %dynamic-slice_bitcast_fusion), channel_id=1, source_target_pairs={{0,4},{4,0},{8,12},{12,8},{1,5},{5,1},{9,13},{13,9},{2,6},{6,2},{1... | collective-permute-start | bytes 4423688 | tf_op jit(solution)/shard_map/ppermute | solution.py:22
  10.8 1.1 copy-start.7
  11.9 1.0 copy-start.8
  12.9 0.8 copy-start.11
  13.8 0.8 copy-start.12
  14.6 0.7 copy-start.13
  15.3 0.7 copy-start.14
  16.0 0.7 copy-start.15
  23.1 35.0 %collective-permute-start.1 = (bf16[2784,128]{1,0:T(8,128)(2,1)}, bf16[2784,128]{1,0:T(8,128)(2,1)}, u32[]{:S(2)}, u32[]{:S(2)}) collective-permute-start(bf16[2784,128]{1,0:T(8,128)(2,1)} %attention.1.refs_0_), channel_id=1, source_target_pairs={{0,8},{4,12},{8,0},{12,4},{1,9},{5,13},{9,1},{13,5},{2,10},{6,14},... | collective-permute-start | bytes 2138120 | tf_op jit(solution)/shard_map/ppermute | solution.py:22
  26.6 32.5 %copy-start.5 = (bf16[2048,720]{0,1:T(8,128)(2,1)S(1)}, bf16[2048,720]{0,1:T(8,128)(2,1)}, u32[]{:S(2)}) copy-start(bf16[2048,720]{0,1:T(8,128)(2,1)} %param.15) | copy-start | bytes 8847364
  26.6 2.4 %copy-start.6 = (bf16[1,1440,1440]{2,1,0:T(8,128)(2,1)S(1)}, bf16[1,1440,1440]{2,1,0:T(8,128)(2,1)}, u32[]{:S(2)}) copy-start(bf16[1,1440,1440]{2,1,0:T(8,128)(2,1)} %param.19) | copy-start | bytes 12441604
  29.0 29.8 %copy-start.16 = (f32[2880]{0:T(1024)S(1)}, f32[2880]{0:T(1024)}, u32[]{:S(2)}) copy-start(f32[2880]{0:T(1024)} %param.17) | copy-start | bytes 34564
  33.8 2.1 %copy-start.1 = (bf16[1440,1440]{1,0:T(8,128)(2,1)}, bf16[1440,1440]{1,0:T(8,128)(2,1)S(1)}, u32[]{:S(2)}) copy-start(bf16[1440,1440]{1,0:T(8,128)(2,1)S(1)} %get-tuple-element.66.refs_3_) | copy-start | bytes 12441604
  35.9 2.0 %copy-start.3 = (bf16[1440,1440]{1,0:T(8,128)(2,1)}, bf16[1440,1440]{1,0:T(8,128)(2,1)S(1)}, u32[]{:S(2)}) copy-start(bf16[1440,1440]{1,0:T(8,128)(2,1)S(1)} %get-tuple-element.67.refs_4_) | copy-start | bytes 12441604
  58.8 3.6 %collective-permute-start.4 = (bf16[720,1024]{1,0:T(8,128)(2,1)}, bf16[720,1024]{1,0:T(8,128)(2,1)}, u32[]{:S(2)}, u32[]{:S(2)}) collective-permute-start(bf16[720,1024]{1,0:T(8,128)(2,1)} %collective-permute-done.2.refs_2_), channel_id=1, source_target_pairs={{0,1},{1,0},{2,3},{3,2},{4,5},{5,4},{6,7},{7,6},{8,9},{9,8},{10,11... | collective-permute-start | bytes 4423688 | tf_op jit(solution)/shard_map/ppermute | solution.py:22
  66.0 10.7 %collective-permute-start.5 = (bf16[1440,128]{1,0:T(8,128)(2,1)S(1)}, bf16[1440,128]{1,0:T(8,128)(2,1)S(1)}, u32[]{:S(2)}, u32[]{:S(2)}) collective-permute-start(bf16[1440,128]{1,0:T(8,128)(2,1)S(1)} %pad_maximum_fusion.1), channel_id=1, source_target_pairs={{0,2},{2,0},{1,3},{3,1},{4,6},{6,4},{5,7},{7,5},{8,10},{10,8},{9,1... | collective-permute-start | bytes 1105928 | tf_op jit(solution)/shard_map/ppermute | solution.py:22
  77.0 9.9 %collective-permute-start.6 = (bf16[1456,128]{1,0:T(8,128)(2,1)S(1)}, bf16[1456,128]{1,0:T(8,128)(2,1)S(1)}, u32[]{:S(2)}, u32[]{:S(2)}) collective-permute-start(bf16[1456,128]{1,0:T(8,128)(2,1)S(1)} %pad_maximum_fusion.refs_0_), channel_id=1, source_target_pairs={{0,2},{2,0},{1,3},{3,1},{4,6},{6,4},{5,7},{7,5},{8,10},{10,8},{9,1... | collective-permute-start | bytes 1118216 | tf_op jit(solution)/shard_map/ppermute | solution.py:22
  78.6 18.6 %collective-permute-start.8 = (bf16[1456,128]{1,0:T(8,128)(2,1)S(1)}, bf16[1456,128]{1,0:T(8,128)(2,1)S(1)}, u32[]{:S(2)}, u32[]{:S(2)}) collective-permute-start(bf16[1456,128]{1,0:T(8,128)(2,1)S(1)} %pad_maximum_fusion.refs_0_), channel_id=1, source_target_pairs={{0,8},{4,12},{8,0},{12,4},{1,9},{5,13},{9,1},{13,5},{2,10},{6,14},... | collective-permute-start | bytes 1118216 | tf_op jit(solution)/shard_map/ppermute | solution.py:22
  86.9 15.8 %collective-permute-start.7 = (bf16[1456,128]{1,0:T(8,128)(2,1)S(1)}, bf16[1456,128]{1,0:T(8,128)(2,1)S(1)}, u32[]{:S(2)}, u32[]{:S(2)}) collective-permute-start(bf16[1456,128]{1,0:T(8,128)(2,1)S(1)} %pad_maximum_fusion.refs_0_), channel_id=1, source_target_pairs={{0,4},{4,0},{8,12},{12,8},{1,5},{5,1},{9,13},{13,9},{2,6},{6,2},{1... | collective-permute-start | bytes 1118216 | tf_op jit(solution)/shard_map/ppermute | solution.py:22
  102.7 13.6 %collective-permute-start.9 = (bf16[1456,128]{1,0:T(8,128)(2,1)S(1)}, bf16[1456,128]{1,0:T(8,128)(2,1)S(1)}, u32[]{:S(2)}, u32[]{:S(2)}) collective-permute-start(bf16[1456,128]{1,0:T(8,128)(2,1)S(1)} %collective-permute-done.8.refs_1_), channel_id=1, source_target_pairs={{0,2},{2,0},{1,3},{3,1},{4,6},{6,4},{5,7},{7,5},{8,10},{10,8},{9,1... | collective-permute-start | bytes 1118216 | tf_op jit(solution)/shard_map/ppermute | solution.py:22
  104.0 11.6 %collective-permute-start.13 = (bf16[1456,128]{1,0:T(8,128)(2,1)S(1)}, bf16[1456,128]{1,0:T(8,128)(2,1)S(1)}, u32[]{:S(2)}, u32[]{:S(2)}) collective-permute-start(bf16[1456,128]{1,0:T(8,128)(2,1)S(1)} %collective-permute-done.8.refs_1_), channel_id=1, source_target_pairs={{0,4},{4,0},{8,12},{12,8},{1,5},{5,1},{9,13},{13,9},{2,6},{6,2},{1... | collective-permute-start | bytes 1118216 | tf_op jit(solution)/shard_map/ppermute | solution.py:22
  104.2 24.4 %collective-permute-start.14 = (bf16[1456,128]{1,0:T(8,128)(2,1)S(1)}, bf16[1456,128]{1,0:T(8,128)(2,1)S(1)}, u32[]{:S(2)}, u32[]{:S(2)}) collective-permute-start(bf16[1456,128]{1,0:T(8,128)(2,1)S(1)} %collective-permute-done.6.refs_2_), channel_id=1, source_target_pairs={{0,4},{4,0},{8,12},{12,8},{1,5},{5,1},{9,13},{13,9},{2,6},{6,2},{1... | collective-permute-start | bytes 1118216 | tf_op jit(solution)/shard_map/ppermute | solution.py:22
  115.6 11.5 %copy-start.9 = (bf16[1456,128]{1,0:T(8,128)(2,1)}, bf16[1456,128]{1,0:T(8,128)(2,1)S(1)}, u32[]{:S(2)}) copy-start(bf16[1456,128]{1,0:T(8,128)(2,1)S(1)} %collective-permute-done.13.refs_1_) | copy-start | bytes 1118212
  115.6 12.9 %collective-permute-start.15 = (bf16[1456,128]{1,0:T(8,128)(2,1)S(1)}, bf16[1456,128]{1,0:T(8,128)(2,1)S(1)}, u32[]{:S(2)}, u32[]{:S(2)}) collective-permute-start(bf16[1456,128]{1,0:T(8,128)(2,1)S(1)} %collective-permute-done.13.refs_1_), channel_id=1, source_target_pairs={{0,2},{2,0},{1,3},{3,1},{4,6},{6,4},{5,7},{7,5},{8,10},{10,8},{9,1... | collective-permute-start | bytes 1118216 | tf_op jit(solution)/shard_map/ppermute | solution.py:22
  116.4 3.4 %copy-start = (bf16[1,2,2880,720]{2,3,1,0:T(8,128)(2,1)S(1)}, bf16[1,2,2880,720]{2,3,1,0:T(8,128)(2,1)}, u32[]{:S(2)}) copy-start(bf16[1,2,2880,720]{2,3,1,0:T(8,128)(2,1)} %param.18) | copy-start | bytes 24883204
  127.2 18.3 %collective-permute-start.11 = (bf16[2,720,256]{2,1,0:T(8,128)(2,1)S(1)}, bf16[2,720,256]{2,1,0:T(8,128)(2,1)}, u32[]{:S(2)}, u32[]{:S(2)}) collective-permute-start(bf16[2,720,256]{2,1,0:T(8,128)(2,1)S(1)} %get-tuple-element.64.refs_0_), channel_id=1, source_target_pairs={{0,2},{2,0},{1,3},{3,1},{4,6},{6,4},{5,7},{7,5},{8,10},{10,8},{9,1... | collective-permute-start | bytes 2211848 | tf_op jit(solution)/shard_map/ppermute | solution.py:22
  128.6 1.0 copy-start.10
  137.0 21.4 %collective-permute-start.16 = (bf16[2,720,256]{2,1,0:T(8,128)(2,1)S(1)}, bf16[2,720,256]{2,1,0:T(8,128)(2,1)}, u32[]{:S(2)}, u32[]{:S(2)}) collective-permute-start(bf16[2,720,256]{2,1,0:T(8,128)(2,1)S(1)} %get-tuple-element.75.refs_0_), channel_id=1, source_target_pairs={{0,2},{2,0},{1,3},{3,1},{4,6},{6,4},{5,7},{7,5},{8,10},{10,8},{9,1... | collective-permute-start | bytes 2211848 | tf_op jit(solution)/shard_map/ppermute | solution.py:22
  145.5 2.3 %copy-start.2 = (bf16[1440,1440]{1,0:T(8,128)(2,1)S(1)}, bf16[1440,1440]{1,0:T(8,128)(2,1)}, u32[]{:S(2)}) copy-start(bf16[1440,1440]{1,0:T(8,128)(2,1)} %copy-done.1) | copy-start | bytes 12441604
  147.8 2.3 %copy-start.4 = (bf16[1440,1440]{1,0:T(8,128)(2,1)S(1)}, bf16[1440,1440]{1,0:T(8,128)(2,1)}, u32[]{:S(2)}) copy-start(bf16[1440,1440]{1,0:T(8,128)(2,1)} %copy-done.3) | copy-start | bytes 12441604
  153.7 19.1 %collective-permute-start.12 = (bf16[1440,128]{1,0:T(8,128)(2,1)S(1)}, bf16[1440,128]{1,0:T(8,128)(2,1)S(1)}, u32[]{:S(2)}, u32[]{:S(2)}) collective-permute-start(bf16[1440,128]{1,0:T(8,128)(2,1)S(1)} %get-tuple-element.69), channel_id=1, source_target_pairs={{0,8},{4,12},{8,0},{12,4},{1,9},{5,13},{9,1},{13,5},{2,10},{6,14},... | collective-permute-start | bytes 1105928 | tf_op jit(solution)/shard_map/ppermute | solution.py:22
  162.1 13.2 %collective-permute-start.17 = (bf16[1440,128]{1,0:T(8,128)(2,1)S(1)}, bf16[1440,128]{1,0:T(8,128)(2,1)S(1)}, u32[]{:S(2)}, u32[]{:S(2)}) collective-permute-start(bf16[1440,128]{1,0:T(8,128)(2,1)S(1)} %get-tuple-element.77), channel_id=1, source_target_pairs={{0,4},{4,0},{8,12},{12,8},{1,5},{5,1},{9,13},{13,9},{2,6},{6,2},{1... | collective-permute-start | bytes 1105928 | tf_op jit(solution)/shard_map/ppermute | solution.py:22
  164.2 17.1 %collective-permute-start.18 = (bf16[1440,128]{1,0:T(8,128)(2,1)S(1)}, bf16[1440,128]{1,0:T(8,128)(2,1)S(1)}, u32[]{:S(2)}, u32[]{:S(2)}) collective-permute-start(bf16[1440,128]{1,0:T(8,128)(2,1)S(1)} %get-tuple-element.78), channel_id=1, source_target_pairs={{0,12},{4,8},{8,4},{12,0},{1,13},{5,9},{9,5},{13,1},{2,14},{6,10},... | collective-permute-start | bytes 1105928 | tf_op jit(solution)/shard_map/ppermute | solution.py:22

commit v15 on v13

--- a/solution.py
+++ b/solution.py
@@ -278,21 +278,6 @@
     )(jnp.stack([pair, t] + chosen).astype(jnp.int32), *flat, gain_table, *weights)
 
 
-def ready(table, ahead):
-    def kernel(table_ref, ahead_ref, out_ref):
-        out_ref[...] = table_ref[...]
-
-    return pl.pallas_call(
-        kernel,
-        out_shape=jax.ShapeDtypeStruct(table.shape, table.dtype),
-        in_specs=in_vmem(2),
-        out_specs=in_vmem(1)[0],
-        compiler_params=params(4),
-        cost_estimate=cost(0, 4 * table.size),
-        name="ready",
-    )(table, ahead)
-
-
 def combine(activated, share, weights, t, slots):
     t_count = len(activated)
     experts, units, lanes = activated[0].shape
@@ -390,12 +375,10 @@
         queries, earlier, key_rows, value_rows, sink_logits, place, routes.T, route_scores.T, below
     )
     gathered = [attended] + [swapped(attended, "ep", group * j) for j in range(1, slots)]
-    experts_out, _ = lax.optimization_barrier((experts_out, attended))
-    experts_out = flip(experts_out)
-
-    gathered, near, experts_out = lax.optimization_barrier((gathered, near, experts_out))
+    own_share = picked(residual, pair * group + t, 0) if shared else below[0]
+    own_share, _ = lax.optimization_barrier((own_share, attended))
+    gathered, near, own_share, experts_out = lax.optimization_barrier((gathered, near, own_share, experts_out))
     near_weights = [near] + [swapped(near, "sub", u) for u in range(1, s_count)]
-    own_share = picked(residual, pair * group + t, 0) if shared else below[0]
     member = z % group
     mine = project(gathered, [out_weight], own_share, (t == member) & shared, t, s * 0, t_count)
     other = project(gathered, near_weights, own_share, (t == member ^ 1) & shared, t, s, t_count)
@@ -441,9 +424,6 @@
     fine = (inverse_square - coarse.astype(jnp.float32)).astype(jnp.bfloat16)
     gain_table = jnp.concatenate([coarse[None], fine[None], jnp.zeros((14, D), jnp.bfloat16)], axis=0)
 
-    gain_table, _ = lax.optimization_barrier((gain_table, scaled))
-    gain_table = ready(gain_table, expert_in)
-
     total = 0.0
     for m in range(t_count):
         for r in range(slots):
@@ -452,14 +432,18 @@
     total = total * lax.dynamic_slice_in_dim(inverse_gain, t * width, width, 0)[:, None]
     total = lax.optimization_barrier(total)
 
-    after = None
+    units = []
     for p in range(group):
         part = [[pieces[m][group * r + p] for r in range(slots)] for m in range(t_count)]
-        if p:
-            part, after = lax.optimization_barrier((part, after))
+        if units:
+            part, _ = lax.optimization_barrier((part, units[-1][0][0]))
         activated, share = activate(part, gain_table, experts_in, pair, t, chosen)
-        after = activated
-        activated = [activated] + [swapped(activated, "tp", m) for m in range(1, t_count)]
+        units.append(([activated] + [swapped(activated, "tp", m) for m in range(1, t_count)], share))
+
+    experts_out, _ = lax.optimization_barrier((experts_out, units[-1][0][0]))
+    experts_out = flip(experts_out)
+    for p in range(group):
+        activated, share = units[p]
         for j, result in enumerate(combine(activated, share, experts_out, t, slots)):
             distance = group * j + p
             result = swapped(result, "ep", distance) if distance else result

time: 184 us -> 181 us (0.984)
  local copies, waits for them, and re-layouts: 30.5 us -> 16.4 us
  waiting for transfers between devices: 83.6 us -> 88.7 us
  starting transfers between devices: 28.9 us -> 31.8 us
  Pallas kernels: 36.6 us -> 39.4 us
    unnamed x48 -> x30, local copies, waits for them, and re-layouts: 26.7 us -> 12.5 us
    ppermute x18, waiting for transfers between devices: 83.6 us -> 88.7 us  [swapped(): lax.ppermute(block, axis, [(i, i ^ distance) for i in range(lax.axis_size...]
    ppermute x18, starting transfers between devices: 26.5 us -> 29.4 us  [swapped(): lax.ppermute(block, axis, [(i, i ^ distance) for i in range(lax.axis_size...]
  transfers between devices with their start and end apart: 19 -> 19, of which waited for: 11 -> 11; matrix products, arithmetic and copies ran while one was open for 3% -> 3% of each run, Pallas kernels for 20% -> 22%
where the time goes in v15:
time: 181 us; the launch traced here: 180 us
  waiting for transfers between devices  88.7 us (49%)
  Pallas kernels  39.4 us (22%)
  starting transfers between devices  31.8 us (18%)
  local copies, waits for them, and re-layouts  16.4 us (9%)
  other arithmetic  3.78 us (2%)
    ppermute x18, waiting for transfers between devices, swapped(): lax.ppermute(block, axis, [(i, i ^ distance) for i in range(lax.axis_size...  88.7 us
    ppermute x18, starting transfers between devices, swapped(): lax.ppermute(block, axis, [(i, i ^ distance) for i in range(lax.axis_size...  29.4 us
    pallas_call x2, Pallas kernels, activate(): pl.pallas_call(kernel, out_shape=(jax.ShapeDtypeStruct((experts, units, l...  14.8 us
    unnamed x30, local copies, waits for them, and re-layouts  12.5 us
    pallas_call x2, Pallas kernels, combine(): pl.pallas_call(kernel, out_shape=tuple((jax.ShapeDtypeStruct((width, rows...  7.66 us
    pallas_call x1, Pallas kernels, attention(): pl.pallas_call(attention_kernel, out_shape=jax.ShapeDtypeStruct((width +...  6.44 us
    pallas_call x2, Pallas kernels, project(): pl.pallas_call(kernel, out_shape=(jax.ShapeDtypeStruct((columns, rows), j...  5.79 us
    pallas_call x1, Pallas kernels, flip(): pl.pallas_call(kernel, out_shape=tuple((jax.ShapeDtypeStruct(a.shape[::-1...  4.73 us
  transfers between devices with their start and end apart: 19, of which 11 were waited for; matrix products, arithmetic and copies ran while one was open for 3% of the time, Pallas kernels for 22%

profile of v15, /device:TPU:0, one launch (start us, length us, event | category | flops | bytes accessed | tf_op | source)
XLA Modules:
  0.0 180.3 jit_solution(14635908474351296031)
XLA Ops:
  0.0 1.0 pad_maximum_fusion.2
  1.1 2.4 %collective-permute-start = (bf16[128,512]{1,0:T(8,128)(2,1)S(1)}, bf16[128,512]{1,0:T(8,128)(2,1)S(1)}, u32[]{:S(2)}, u32[]{:S(2)}) collective-permute-start(bf16[128,512]{1,0:T(8,128)(2,1)S(1)} %pad_maximum_fusion.2), channel_id=1, source_target_pairs={{0,1},{1,4},{4,5},{5,8},{8,9},{9,12},{12,13},{2,3},{3,6},{6,7},{7,... | collective-permute-start | bytes 393224 | tf_op jit(solution)/shard_map/ppermute | solution.py:18
  3.4 2.6 %dynamic-slice_bitcast_fusion = bf16[720,1024]{1,0:T(8,128)(2,1)} fusion(bf16[2048,720]{0,1:T(8,128)(2,1)} %param.15, s32[]{:T(128)S(6)} %select_n.95), kind=kLoop, calls=%fused_computation | loop fusion | bytes 2949124 | tf_op jit(solution)/shard_map/dynamic_slice | solution.py:351
  6.1 2.7 %collective-permute-start.3 = (bf16[1440,1440]{1,0:T(8,128)(2,1)}, bf16[1440,1440]{1,0:T(8,128)(2,1)}, u32[]{:S(2)}, u32[]{:S(2)}) collective-permute-start(bf16[1440,1440]{1,0:T(8,128)(2,1)} %bitcast.33), channel_id=1, source_target_pairs={{0,1},{1,0},{2,3},{3,2},{4,5},{5,4},{6,7},{7,6},{8,9},{9,8},{10,11... | collective-permute-start | bytes 12441608 | tf_op jit(solution)/shard_map/ppermute | solution.py:22
  8.7 2.1 %collective-permute-start.2 = (bf16[720,1024]{1,0:T(8,128)(2,1)}, bf16[720,1024]{1,0:T(8,128)(2,1)}, u32[]{:S(2)}, u32[]{:S(2)}) collective-permute-start(bf16[720,1024]{1,0:T(8,128)(2,1)} %dynamic-slice_bitcast_fusion), channel_id=1, source_target_pairs={{0,4},{4,0},{8,12},{12,8},{1,5},{5,1},{9,13},{13,9},{2,6},{6,2},{1... | collective-permute-start | bytes 4423688 | tf_op jit(solution)/shard_map/ppermute | solution.py:22
  11.0 1.1 copy-done.3
  12.1 1.0 copy-done.4
  13.1 0.8 copy-done.7
  13.9 0.8 copy-done.8
  14.8 0.7 copy-done.9
  15.5 0.7 copy-done.10
  16.2 0.7 copy-done.11
  16.8 6.4 %attention.1.refs_0_ = bf16[2784,128]{1,0:T(8,128)(2,1)} custom-call(s32[2]{0:T(128)S(1)} %pad_add_fusion.1.place_ref, f32[32]{0:T(128)S(1)} %copy-done.11, bf16[128,2048]{1,0:T(8,128)(2,1)S(1)} %copy-done.4, bf16[128,512]{1,0:T(8,128)(2,1)S(1)} %collective-permute-done.earlier_ref, bf16[128,256]{1,0:T(8,128)(2,1)S(1)} %copy-done.8, ...), custom_call_target="tpu_custom_call" | custom-call | flops 268435456 | bytes 1572864 | tf_op jit(solution)/shard_map/attention/pallas_call | solution.py:128
  23.2 2.6 %collective-permute-start.1 = (bf16[2784,128]{1,0:T(8,128)(2,1)}, bf16[2784,128]{1,0:T(8,128)(2,1)}, u32[]{:S(2)}, u32[]{:S(2)}) collective-permute-start(bf16[2784,128]{1,0:T(8,128)(2,1)} %attention.1.refs_0_), channel_id=1, source_target_pairs={{0,8},{4,12},{8,0},{12,4},{1,9},{5,13},{9,1},{13,5},{2,10},{6,14},... | collective-permute-start | bytes 2138120 | tf_op jit(solution)/shard_map/ppermute | solution.py:22
  25.8 0.9 dynamic-slice_bitcast_fusion.1.refs_3_.refs_4_
  26.8 31.4 %collective-permute-done.1.refs_1_ = bf16[2784,128]{1,0:T(8,128)(2,1)} collective-permute-done((bf16[2784,128]{1,0:T(8,128)(2,1)}, bf16[2784,128]{1,0:T(8,128)(2,1)}, u32[]{:S(2)}, u32[]{:S(2)}) %collective-permute-start.1) | collective-permute-done | bytes 712736 | tf_op jit(solution)/shard_map/ppermute | solution.py:22
  58.2 0.9 collective-permute-done.2.refs_2_
  59.3 2.4 %project.2 = (f32[720,128]{1,0:T(8,128)S(1)}, bf16[1,720,128]{2,1,0:T(8,128)(2,1)S(1)}) custom-call(s32[3]{0:T(128)S(1)} %pad_add_fusion.place_ref, bf16[2784,128]{1,0:T(8,128)(2,1)} %attention.1.refs_0_, bf16[2784,128]{1,0:T(8,128)(2,1)} %collective-permute-done.1.refs_1_, bf16[720,2048]{1,0:T(8,128)(2,1)S(1)} %bitcast.32, ...), custom_call_target="tpu_custom_call" | custom-call | flops 754974720 | bytes 2949120 | tf_op jit(solution)/shard_map/project/pallas_call | solution.py:188
  61.7 1.0 collective-permute-done.4.refs_3_
  62.7 3.4 %project.3 = (f32[720,128]{1,0:T(8,128)S(1)}, bf16[1,720,128]{2,1,0:T(8,128)(2,1)S(1)}) custom-call(s32[3]{0:T(128)S(1)} %pad_add_fusion.2.place_ref, bf16[2784,128]{1,0:T(8,128)(2,1)} %attention.1.refs_0_, bf16[2784,128]{1,0:T(8,128)(2,1)} %collective-permute-done.1.refs_1_, bf16[720,1024]{1,0:T(8,128)(2,1)} %collective-permute-done.2.refs_2_, ...), custom_call_target="tpu_custom_call" | custom-call | flops 754974720 | bytes 2949120 | tf_op jit(solution)/shard_map/project/pallas_call | solution.py:188
  66.2 1.6 collective-permute-start.5
  67.8 0.7 slice_select_fusion
  68.5 8.4 %collective-permute-done.5 = bf16[1440,128]{1,0:T(8,128)(2,1)S(1)} collective-permute-done((bf16[1440,128]{1,0:T(8,128)(2,1)S(1)}, bf16[1440,128]{1,0:T(8,128)(2,1)S(1)}, u32[]{:S(2)}, u32[]{:S(2)}) %collective-permute-start.5) | collective-permute-done | bytes 368672 | tf_op jit(solution)/shard_map/ppermute | solution.py:22
  77.2 2.6 %collective-permute-start.6 = (bf16[1456,128]{1,0:T(8,128)(2,1)S(1)}, bf16[1456,128]{1,0:T(8,128)(2,1)S(1)}, u32[]{:S(2)}, u32[]{:S(2)}) collective-permute-start(bf16[1456,128]{1,0:T(8,128)(2,1)S(1)} %pad_maximum_fusion.refs_0_), channel_id=1, source_target_pairs={{0,8},{4,12},{8,0},{12,4},{1,9},{5,13},{9,1},{13,5},{2,10},{6,14},... | collective-permute-start | bytes 1118216 | tf_op jit(solution)/shard_map/ppermute | solution.py:22
  79.9 1.7 collective-permute-start.7
  81.6 1.4 collective-permute-start.9
  83.1 12.9 %collective-permute-done.6.refs_1_ = bf16[1456,128]{1,0:T(8,128)(2,1)S(1)} collective-permute-done((bf16[1456,128]{1,0:T(8,128)(2,1)S(1)}, bf16[1456,128]{1,0:T(8,128)(2,1)S(1)}, u32[]{:S(2)}, u32[]{:S(2)}) %collective-permute-start.6) | collective-permute-done | bytes 372768 | tf_op jit(solution)/shard_map/ppermute | solution.py:22
  96.0 1.5 collective-permute-start.10
  97.6 0.6 collective-permute-start.8
  98.4 6.6 %collective-permute-done.10.refs_3_ = bf16[1456,128]{1,0:T(8,128)(2,1)S(1)} collective-permute-done((bf16[1456,128]{1,0:T(8,128)(2,1)S(1)}, bf16[1456,128]{1,0:T(8,128)(2,1)S(1)}, u32[]{:S(2)}, u32[]{:S(2)}) %collective-permute-start.10) | collective-permute-done | bytes 372768 | tf_op jit(solution)/shard_map/ppermute | solution.py:22
  105.0 1.8 %collective-permute-done.8.refs_1_ = bf16[1456,128]{1,0:T(8,128)(2,1)S(1)} collective-permute-done((bf16[1456,128]{1,0:T(8,128)(2,1)S(1)}, bf16[1456,128]{1,0:T(8,128)(2,1)S(1)}, u32[]{:S(2)}, u32[]{:S(2)}) %collective-permute-start.8) | collective-permute-done | bytes 372768 | tf_op jit(solution)/shard_map/ppermute | solution.py:22
  107.3 1.5 collective-permute-start.14
  108.8 3.4 %copy-done = bf16[1,2,2880,720]{2,3,1,0:T(8,128)(2,1)S(1)} copy-done((bf16[1,2,2880,720]{2,3,1,0:T(8,128)(2,1)S(1)}, bf16[1,2,2880,720]{2,3,1,0:T(8,128)(2,1)}, u32[]{:S(2)}) %copy-start) | copy-done | bytes 8294424
  112.2 7.4 %activate.2 = (bf16[2,720,256]{2,1,0:T(8,128)(2,1)S(1)}, f32[2,256]{1,0:T(2,128)S(1)}) custom-call(s32[4]{0:T(128)S(1)} %pad_add_fusion.3.place_ref, bf16[1456,128]{1,0:T(8,128)(2,1)S(1)} %pad_maximum_fusion.refs_0_, bf16[1456,128]{1,0:T(8,128)(2,1)S(1)} %collective-permute-done.6.refs_1_, bf16[1456,128]{1,0:T(8,128)(2,1)S(1)} %collective-permute-done.9.refs_2_, ...), custom_call_target="tpu_custom_call" | custom-call | flops 4246732800 | bytes 16588800 | tf_op jit(solution)/shard_map/activate/pallas_call | solution.py:258
  120.2 6.2 %collective-permute-done.14.refs_3_ = bf16[1456,128]{1,0:T(8,128)(2,1)S(1)} collective-permute-done((bf16[1456,128]{1,0:T(8,128)(2,1)S(1)}, bf16[1456,128]{1,0:T(8,128)(2,1)S(1)}, u32[]{:S(2)}, u32[]{:S(2)}) %collective-permute-start.14) | collective-permute-done | bytes 372768 | tf_op jit(solution)/shard_map/ppermute | solution.py:22
  126.4 1.0 copy-done.6
  127.4 7.4 %activate.3 = (bf16[2,720,256]{2,1,0:T(8,128)(2,1)S(1)}, f32[2,256]{1,0:T(2,128)S(1)}) custom-call(s32[4]{0:T(128)S(1)} %pad_add_fusion.3.place_ref, bf16[1456,128]{1,0:T(8,128)(2,1)S(1)} %collective-permute-done.7.refs_0_, bf16[1456,128]{1,0:T(8,128)(2,1)S(1)} %copy-done.6, bf16[1456,128]{1,0:T(8,128)(2,1)S(1)} %collective-permute-done.13.refs_2_, ...), custom_call_target="tpu_custom_call" | custom-call | flops 4246732800 | bytes 16588800 | tf_op jit(solution)/shard_map/activate/pallas_call | solution.py:258
  135.4 2.3 %copy-done.2 = bf16[1,1440,1440]{2,1,0:T(8,128)(2,1)S(1)} copy-done((bf16[1,1440,1440]{2,1,0:T(8,128)(2,1)S(1)}, bf16[1,1440,1440]{2,1,0:T(8,128)(2,1)}, u32[]{:S(2)}) %copy-start.2) | copy-done | bytes 4147224
  137.7 4.7 %flip.1 = (bf16[1440,1440]{1,0:T(8,128)(2,1)S(1)}, bf16[1440,1440]{1,0:T(8,128)(2,1)S(1)}) custom-call(bf16[1440,1440]{1,0:T(8,128)(2,1)S(1)} %bitcast.34, bf16[1440,1440]{1,0:T(8,128)(2,1)} %collective-permute-done.3.refs_1_), custom_call_target="tpu_custom_call" | custom-call | bytes 16588800 | tf_op jit(solution)/shard_map/flip/pallas_call | solution.py:144
  142.4 3.9 %combine.2 = (bf16[1440,128]{1,0:T(8,128)(2,1)S(1)}, bf16[1440,128]{1,0:T(8,128)(2,1)S(1)}) custom-call(s32[1]{0:T(128)} %bitcast.t_ref, bf16[2,720,256]{2,1,0:T(8,128)(2,1)S(1)} %get-tuple-element.55.refs_0_, bf16[2,720,256]{2,1,0:T(8,128)(2,1)} %collective-permute-done.12.refs_1_, f32[2,256]{1,0:T(2,128)S(1)} %get-tuple-element.56.refs_2_, ...), custom_call_target="tpu_custom_call" | custom-call | flops 2123366400 | bytes 8294400 | tf_op jit(solution)/shard_map/combine/pallas_call | solution.py:308
  146.3 3.5 %collective-permute-start.15 = (bf16[1440,128]{1,0:T(8,128)(2,1)S(1)}, bf16[1440,128]{1,0:T(8,128)(2,1)S(1)}, u32[]{:S(2)}, u32[]{:S(2)}) collective-permute-start(bf16[1440,128]{1,0:T(8,128)(2,1)S(1)} %get-tuple-element.71), channel_id=1, source_target_pairs={{0,8},{4,12},{8,0},{12,4},{1,9},{5,13},{9,1},{13,5},{2,10},{6,14},... | collective-permute-start | bytes 1105928 | tf_op jit(solution)/shard_map/ppermute | solution.py:22
  149.8 5.4 %collective-permute-done.16.refs_1_ = bf16[2,720,256]{2,1,0:T(8,128)(2,1)} collective-permute-done((bf16[2,720,256]{2,1,0:T(8,128)(2,1)S(1)}, bf16[2,720,256]{2,1,0:T(8,128)(2,1)}, u32[]{:S(2)}, u32[]{:S(2)}) %collective-permute-start.16) | collective-permute-done | bytes 737312 | tf_op jit(solution)/shard_map/ppermute | solution.py:22
  155.2 3.7 %combine.3 = (bf16[1440,128]{1,0:T(8,128)(2,1)S(1)}, bf16[1440,128]{1,0:T(8,128)(2,1)S(1)}) custom-call(s32[1]{0:T(128)} %bitcast.t_ref, bf16[2,720,256]{2,1,0:T(8,128)(2,1)S(1)} %get-tuple-element.65.refs_0_, bf16[2,720,256]{2,1,0:T(8,128)(2,1)} %collective-permute-done.16.refs_1_, f32[2,256]{1,0:T(2,128)S(1)} %get-tuple-element.72.refs_2_, ...), custom_call_target="tpu_custom_call" | custom-call | flops 2123366400 | bytes 8294400 | tf_op jit(solution)/shard_map/combine/pallas_call | solution.py:308
  158.9 2.5 %collective-permute-start.17 = (bf16[1440,128]{1,0:T(8,128)(2,1)S(1)}, bf16[1440,128]{1,0:T(8,128)(2,1)S(1)}, u32[]{:S(2)}, u32[]{:S(2)}) collective-permute-start(bf16[1440,128]{1,0:T(8,128)(2,1)S(1)} %get-tuple-element.73), channel_id=1, source_target_pairs={{0,4},{4,0},{8,12},{12,8},{1,5},{5,1},{9,13},{13,9},{2,6},{6,2},{1... | collective-permute-start | bytes 1105928 | tf_op jit(solution)/shard_map/ppermute | solution.py:22
  161.5 3.4 %collective-permute-start.18 = (bf16[1440,128]{1,0:T(8,128)(2,1)S(1)}, bf16[1440,128]{1,0:T(8,128)(2,1)S(1)}, u32[]{:S(2)}, u32[]{:S(2)}) collective-permute-start(bf16[1440,128]{1,0:T(8,128)(2,1)S(1)} %get-tuple-element.74), channel_id=1, source_target_pairs={{0,12},{4,8},{8,4},{12,0},{1,13},{5,9},{9,5},{13,1},{2,14},{6,10},... | collective-permute-start | bytes 1105928 | tf_op jit(solution)/shard_map/ppermute | solution.py:22
  165.1 7.2 %collective-permute-done.17 = bf16[1440,128]{1,0:T(8,128)(2,1)S(1)} collective-permute-done((bf16[1440,128]{1,0:T(8,128)(2,1)S(1)}, bf16[1440,128]{1,0:T(8,128)(2,1)S(1)}, u32[]{:S(2)}, u32[]{:S(2)}) %collective-permute-start.17) | collective-permute-done | bytes 368672 | tf_op jit(solution)/shard_map/ppermute | solution.py:22
  172.3 7.1 %collective-permute-done.18 = bf16[1440,128]{1,0:T(8,128)(2,1)S(1)} collective-permute-done((bf16[1440,128]{1,0:T(8,128)(2,1)S(1)}, bf16[1440,128]{1,0:T(8,128)(2,1)S(1)}, u32[]{:S(2)}, u32[]{:S(2)}) %collective-permute-start.18) | collective-permute-done | bytes 368672 | tf_op jit(solution)/shard_map/ppermute | solution.py:22
  179.4 1.0 fusion.2
  (52 shorter events, 3.0 us)
Async XLA Ops:
  0.0 59.3 %copy-start.1 = (bf16[2048,720]{0,1:T(8,128)(2,1)S(1)}, bf16[2048,720]{0,1:T(8,128)(2,1)}, u32[]{:S(2)}) copy-start(bf16[2048,720]{0,1:T(8,128)(2,1)} %param.15) | copy-start | bytes 8847364
  0.0 59.0 %copy-start.14 = (f32[2880]{0:T(1024)S(1)}, f32[2880]{0:T(1024)}, u32[]{:S(2)}) copy-start(f32[2880]{0:T(1024)} %param.17) | copy-start | bytes 34564
  1.1 5.0 %collective-permute-start = (bf16[128,512]{1,0:T(8,128)(2,1)S(1)}, bf16[128,512]{1,0:T(8,128)(2,1)S(1)}, u32[]{:S(2)}, u32[]{:S(2)}) collective-permute-start(bf16[128,512]{1,0:T(8,128)(2,1)S(1)} %pad_maximum_fusion.2), channel_id=1, source_target_pairs={{0,1},{1,4},{4,5},{5,8},{8,9},{9,12},{12,13},{2,3},{3,6},{6,7},{7,... | collective-permute-start | bytes 393224 | tf_op jit(solution)/shard_map/ppermute | solution.py:18
  6.1 53.0 %collective-permute-start.3 = (bf16[1440,1440]{1,0:T(8,128)(2,1)}, bf16[1440,1440]{1,0:T(8,128)(2,1)}, u32[]{:S(2)}, u32[]{:S(2)}) collective-permute-start(bf16[1440,1440]{1,0:T(8,128)(2,1)} %bitcast.33), channel_id=1, source_target_pairs={{0,1},{1,0},{2,3},{3,2},{4,5},{5,4},{6,7},{7,6},{8,9},{9,8},{10,11... | collective-permute-start | bytes 12441608 | tf_op jit(solution)/shard_map/ppermute | solution.py:22
  8.7 100.1 %collective-permute-start.11 = (bf16[2,720,2880]{2,1,0:T(8,128)(2,1)}, bf16[2,720,2880]{2,1,0:T(8,128)(2,1)}, u32[]{:S(2)}, u32[]{:S(2)}) collective-permute-start(bf16[2,720,2880]{2,1,0:T(8,128)(2,1)} %bitcast.29), channel_id=1, source_target_pairs={{0,1},{1,0},{2,3},{3,2},{4,5},{5,4},{6,7},{7,6},{8,9},{9,8},{10,11... | collective-permute-start | bytes 24883208 | tf_op jit(solution)/shard_map/ppermute | solution.py:22
  8.7 50.3 %collective-permute-start.2 = (bf16[720,1024]{1,0:T(8,128)(2,1)}, bf16[720,1024]{1,0:T(8,128)(2,1)}, u32[]{:S(2)}, u32[]{:S(2)}) collective-permute-start(bf16[720,1024]{1,0:T(8,128)(2,1)} %dynamic-slice_bitcast_fusion), channel_id=1, source_target_pairs={{0,4},{4,0},{8,12},{12,8},{1,5},{5,1},{9,13},{13,9},{2,6},{6,2},{1... | collective-permute-start | bytes 4423688 | tf_op jit(solution)/shard_map/ppermute | solution.py:22
  10.9 1.1 copy-start.3
  12.1 1.0 copy-start.4
  13.1 0.8 copy-start.7
  13.9 0.8 copy-start.8
  14.8 0.7 copy-start.9
  15.5 0.7 copy-start.10
  16.2 0.7 copy-start.11
  23.2 34.9 %collective-permute-start.1 = (bf16[2784,128]{1,0:T(8,128)(2,1)}, bf16[2784,128]{1,0:T(8,128)(2,1)}, u32[]{:S(2)}, u32[]{:S(2)}) collective-permute-start(bf16[2784,128]{1,0:T(8,128)(2,1)} %attention.1.refs_0_), channel_id=1, source_target_pairs={{0,8},{4,12},{8,0},{12,4},{1,9},{5,13},{9,1},{13,5},{2,10},{6,14},... | collective-permute-start | bytes 2138120 | tf_op jit(solution)/shard_map/ppermute | solution.py:22
  59.0 3.6 %collective-permute-start.4 = (bf16[720,1024]{1,0:T(8,128)(2,1)}, bf16[720,1024]{1,0:T(8,128)(2,1)}, u32[]{:S(2)}, u32[]{:S(2)}) collective-permute-start(bf16[720,1024]{1,0:T(8,128)(2,1)} %collective-permute-done.2.refs_2_), channel_id=1, source_target_pairs={{0,1},{1,0},{2,3},{3,2},{4,5},{5,4},{6,7},{7,6},{8,9},{9,8},{10,11... | collective-permute-start | bytes 4423688 | tf_op jit(solution)/shard_map/ppermute | solution.py:22
  66.2 10.7 %collective-permute-start.5 = (bf16[1440,128]{1,0:T(8,128)(2,1)S(1)}, bf16[1440,128]{1,0:T(8,128)(2,1)S(1)}, u32[]{:S(2)}, u32[]{:S(2)}) collective-permute-start(bf16[1440,128]{1,0:T(8,128)(2,1)S(1)} %pad_maximum_fusion.1), channel_id=1, source_target_pairs={{0,2},{2,0},{1,3},{3,1},{4,6},{6,4},{5,7},{7,5},{8,10},{10,8},{9,1... | collective-permute-start | bytes 1105928 | tf_op jit(solution)/shard_map/ppermute | solution.py:22
  77.1 20.4 %copy-start.12 = (bf16[1440,128]{1,0:T(8,128)(2,1)}, bf16[1440,128]{1,0:T(8,128)(2,1)S(1)}, u32[]{:S(2)}) copy-start(bf16[1440,128]{1,0:T(8,128)(2,1)S(1)} %fusion.1) | copy-start | bytes 1105924
  77.2 18.8 %collective-permute-start.6 = (bf16[1456,128]{1,0:T(8,128)(2,1)S(1)}, bf16[1456,128]{1,0:T(8,128)(2,1)S(1)}, u32[]{:S(2)}, u32[]{:S(2)}) collective-permute-start(bf16[1456,128]{1,0:T(8,128)(2,1)S(1)} %pad_maximum_fusion.refs_0_), channel_id=1, source_target_pairs={{0,8},{4,12},{8,0},{12,4},{1,9},{5,13},{9,1},{13,5},{2,10},{6,14},... | collective-permute-start | bytes 1118216 | tf_op jit(solution)/shard_map/ppermute | solution.py:22
  79.9 18.5 %collective-permute-start.7 = (bf16[1456,128]{1,0:T(8,128)(2,1)S(1)}, bf16[1456,128]{1,0:T(8,128)(2,1)S(1)}, u32[]{:S(2)}, u32[]{:S(2)}) collective-permute-start(bf16[1456,128]{1,0:T(8,128)(2,1)S(1)} %pad_maximum_fusion.refs_0_), channel_id=1, source_target_pairs={{0,4},{4,0},{8,12},{12,8},{1,5},{5,1},{9,13},{13,9},{2,6},{6,2},{1... | collective-permute-start | bytes 1118216 | tf_op jit(solution)/shard_map/ppermute | solution.py:22
  81.6 16.8 %collective-permute-start.9 = (bf16[1456,128]{1,0:T(8,128)(2,1)S(1)}, bf16[1456,128]{1,0:T(8,128)(2,1)S(1)}, u32[]{:S(2)}, u32[]{:S(2)}) collective-permute-start(bf16[1456,128]{1,0:T(8,128)(2,1)S(1)} %pad_maximum_fusion.refs_0_), channel_id=1, source_target_pairs={{0,2},{2,0},{1,3},{3,1},{4,6},{6,4},{5,7},{7,5},{8,10},{10,8},{9,1... | collective-permute-start | bytes 1118216 | tf_op jit(solution)/shard_map/ppermute | solution.py:22
  96.0 9.0 %collective-permute-start.10 = (bf16[1456,128]{1,0:T(8,128)(2,1)S(1)}, bf16[1456,128]{1,0:T(8,128)(2,1)S(1)}, u32[]{:S(2)}, u32[]{:S(2)}) collective-permute-start(bf16[1456,128]{1,0:T(8,128)(2,1)S(1)} %collective-permute-done.6.refs_1_), channel_id=1, source_target_pairs={{0,2},{2,0},{1,3},{3,1},{4,6},{6,4},{5,7},{7,5},{8,10},{10,8},{9,1... | collective-permute-start | bytes 1118216 | tf_op jit(solution)/shard_map/ppermute | solution.py:22
  97.6 9.2 %collective-permute-start.8 = (bf16[1456,128]{1,0:T(8,128)(2,1)S(1)}, bf16[1456,128]{1,0:T(8,128)(2,1)S(1)}, u32[]{:S(2)}, u32[]{:S(2)}) collective-permute-start(bf16[1456,128]{1,0:T(8,128)(2,1)S(1)} %collective-permute-done.6.refs_1_), channel_id=1, source_target_pairs={{0,4},{4,0},{8,12},{12,8},{1,5},{5,1},{9,13},{13,9},{2,6},{6,2},{1... | collective-permute-start | bytes 1118216 | tf_op jit(solution)/shard_map/ppermute | solution.py:22
  106.8 12.8 %copy-start.5 = (bf16[1456,128]{1,0:T(8,128)(2,1)}, bf16[1456,128]{1,0:T(8,128)(2,1)S(1)}, u32[]{:S(2)}) copy-start(bf16[1456,128]{1,0:T(8,128)(2,1)S(1)} %collective-permute-done.8.refs_1_) | copy-start | bytes 1118212
  106.8 13.4 %collective-permute-start.13 = (bf16[1456,128]{1,0:T(8,128)(2,1)S(1)}, bf16[1456,128]{1,0:T(8,128)(2,1)S(1)}, u32[]{:S(2)}, u32[]{:S(2)}) collective-permute-start(bf16[1456,128]{1,0:T(8,128)(2,1)S(1)} %collective-permute-done.7.refs_0_), channel_id=1, source_target_pairs={{0,2},{2,0},{1,3},{3,1},{4,6},{6,4},{5,7},{7,5},{8,10},{10,8},{9,1... | collective-permute-start | bytes 1118216 | tf_op jit(solution)/shard_map/ppermute | solution.py:22
  107.3 19.1 %collective-permute-start.14 = (bf16[1456,128]{1,0:T(8,128)(2,1)S(1)}, bf16[1456,128]{1,0:T(8,128)(2,1)S(1)}, u32[]{:S(2)}, u32[]{:S(2)}) collective-permute-start(bf16[1456,128]{1,0:T(8,128)(2,1)S(1)} %collective-permute-done.8.refs_1_), channel_id=1, source_target_pairs={{0,2},{2,0},{1,3},{3,1},{4,6},{6,4},{5,7},{7,5},{8,10},{10,8},{9,1... | collective-permute-start | bytes 1118216 | tf_op jit(solution)/shard_map/ppermute | solution.py:22
  108.8 3.4 %copy-start = (bf16[1,2,2880,720]{2,3,1,0:T(8,128)(2,1)S(1)}, bf16[1,2,2880,720]{2,3,1,0:T(8,128)(2,1)}, u32[]{:S(2)}) copy-start(bf16[1,2,2880,720]{2,3,1,0:T(8,128)(2,1)} %param.18) | copy-start | bytes 24883204
  119.6 22.8 %collective-permute-start.12 = (bf16[2,720,256]{2,1,0:T(8,128)(2,1)S(1)}, bf16[2,720,256]{2,1,0:T(8,128)(2,1)}, u32[]{:S(2)}, u32[]{:S(2)}) collective-permute-start(bf16[2,720,256]{2,1,0:T(8,128)(2,1)S(1)} %get-tuple-element.55.refs_0_), channel_id=1, source_target_pairs={{0,2},{2,0},{1,3},{3,1},{4,6},{6,4},{5,7},{7,5},{8,10},{10,8},{9,1... | collective-permute-start | bytes 2211848 | tf_op jit(solution)/shard_map/ppermute | solution.py:22
  126.4 1.0 copy-start.6
  134.8 20.4 %collective-permute-start.16 = (bf16[2,720,256]{2,1,0:T(8,128)(2,1)S(1)}, bf16[2,720,256]{2,1,0:T(8,128)(2,1)}, u32[]{:S(2)}, u32[]{:S(2)}) collective-permute-start(bf16[2,720,256]{2,1,0:T(8,128)(2,1)S(1)} %get-tuple-element.65.refs_0_), channel_id=1, source_target_pairs={{0,2},{2,0},{1,3},{3,1},{4,6},{6,4},{5,7},{7,5},{8,10},{10,8},{9,1... | collective-permute-start | bytes 2211848 | tf_op jit(solution)/shard_map/ppermute | solution.py:22
  135.4 2.3 %copy-start.2 = (bf16[1,1440,1440]{2,1,0:T(8,128)(2,1)S(1)}, bf16[1,1440,1440]{2,1,0:T(8,128)(2,1)}, u32[]{:S(2)}) copy-start(bf16[1,1440,1440]{2,1,0:T(8,128)(2,1)} %param.19) | copy-start | bytes 12441604
  146.3 18.8 %collective-permute-start.15 = (bf16[1440,128]{1,0:T(8,128)(2,1)S(1)}, bf16[1440,128]{1,0:T(8,128)(2,1)S(1)}, u32[]{:S(2)}, u32[]{:S(2)}) collective-permute-start(bf16[1440,128]{1,0:T(8,128)(2,1)S(1)} %get-tuple-element.71), channel_id=1, source_target_pairs={{0,8},{4,12},{8,0},{12,4},{1,9},{5,13},{9,1},{13,5},{2,10},{6,14},... | collective-permute-start | bytes 1105928 | tf_op jit(solution)/shard_map/ppermute | solution.py:22
  155.2 9.7 %copy-start.13 = (bf16[1440,128]{1,0:T(8,128)(2,1)S(1)}, bf16[1440,128]{1,0:T(8,128)(2,1)}, u32[]{:S(2)}) copy-start(bf16[1440,128]{1,0:T(8,128)(2,1)} %copy-done.12) | copy-start | bytes 1105924
  158.9 13.4 %collective-permute-start.17 = (bf16[1440,128]{1,0:T(8,128)(2,1)S(1)}, bf16[1440,128]{1,0:T(8,128)(2,1)S(1)}, u32[]{:S(2)}, u32[]{:S(2)}) collective-permute-start(bf16[1440,128]{1,0:T(8,128)(2,1)S(1)} %get-tuple-element.73), channel_id=1, source_target_pairs={{0,4},{4,0},{8,12},{12,8},{1,5},{5,1},{9,13},{13,9},{2,6},{6,2},{1... | collective-permute-start | bytes 1105928 | tf_op jit(solution)/shard_map/ppermute | solution.py:22
  161.5 17.9 %collective-permute-start.18 = (bf16[1440,128]{1,0:T(8,128)(2,1)S(1)}, bf16[1440,128]{1,0:T(8,128)(2,1)S(1)}, u32[]{:S(2)}, u32[]{:S(2)}) collective-permute-start(bf16[1440,128]{1,0:T(8,128)(2,1)S(1)} %get-tuple-element.74), channel_id=1, source_target_pairs={{0,12},{4,8},{8,4},{12,0},{1,13},{5,9},{9,5},{13,1},{2,14},{6,10},... | collective-permute-start | bytes 1105928 | tf_op jit(solution)/shard_map/ppermute | solution.py:22

commit v16 on v15

--- a/solution.py
+++ b/solution.py
@@ -152,6 +152,28 @@
     )(*arrays)
 
 
+def fetched(weight):
+    cuts = cuts_of([(k,) for k in range(weight.shape[0])], weight.shape[1], 3)
+
+    def kernel(weight_ref, out_ref, arrived):
+        copies = fetches(weight_ref, out_ref, arrived, cuts)
+        for copy in copies:
+            copy.start()
+        for copy in copies:
+            copy.wait()
+
+    return pl.pallas_call(
+        kernel,
+        out_shape=jax.ShapeDtypeStruct(weight.shape, weight.dtype),
+        in_specs=[pl.BlockSpec(memory_space=pl.ANY)],
+        out_specs=in_vmem(1)[0],
+        scratch_shapes=[pltpu.SemaphoreType.DMA((len(cuts),))],
+        compiler_params=params(2),
+        cost_estimate=cost(0, 4 * weight.size),
+        name="fetched",
+    )(weight)
+
+
 def project(attended, weights, residual, has_share, t, s, t_count):
     slots = len(attended)
     rows = attended[0].shape[1]
@@ -413,10 +435,16 @@
         distance //= 2
     for m in range(1, t_count):
         pieces[m].update({d: swapped(own[d], "tp", m) for d in range(0, z_count, group) if d not in pieces[m]})
-    late = {d: own[d] for d in own if d % group}
+    late = {d: own[d] for d in own if d % group and d != 1}
     late, pieces[1:] = lax.optimization_barrier((late, pieces[1:]))
     for m in range(1, t_count):
         pieces[m].update({d: swapped(late[d], "tp", m) for d in late})
+
+    weight, _ = lax.optimization_barrier((experts_in[0], own[group]))
+    experts_in[0] = fetched(weight)
+    odd, _ = lax.optimization_barrier((own[1], experts_in[0]))
+    for m in range(1, t_count):
+        pieces[m][1] = swapped(odd, "tp", m)
 
     inverse_gain = 1.0 / norm_gain
     inverse_square = inverse_gain * inverse_gain

time: 181 us -> 180 us (level)
  waiting for transfers between devices: 88.7 us -> 86.4 us
    ppermute x18, waiting for transfers between devices: 88.7 us -> 86.4 us  [swapped(): lax.ppermute(block, axis, [(i, i ^ distance) for i in range(lax.axis_size...]
  transfers between devices with their start and end apart: 19 -> 19, of which waited for: 11 -> 11; matrix products, arithmetic and copies ran while one was open for 3% -> 3% of each run, Pallas kernels for 22% -> 23%
where the time goes in v16:
time: 180 us; the launch traced here: 179 us
  waiting for transfers between devices  86.4 us (48%)
  Pallas kernels  40.6 us (23%)
  starting transfers between devices  31.9 us (18%)
  local copies, waits for them, and re-layouts  16.4 us (9%)
  other arithmetic  3.78 us (2%)
    ppermute x18, waiting for transfers between devices, swapped(): lax.ppermute(block, axis, [(i, i ^ distance) for i in range(lax.axis_size...  86.4 us
    ppermute x18, starting transfers between devices, swapped(): lax.ppermute(block, axis, [(i, i ^ distance) for i in range(lax.axis_size...  29.5 us
    pallas_call x2, Pallas kernels, activate(): pl.pallas_call(kernel, out_shape=(jax.ShapeDtypeStruct((experts, units, l...  14.8 us
    unnamed x30, local copies, waits for them, and re-layouts  12.5 us
    pallas_call x2, Pallas kernels, combine(): pl.pallas_call(kernel, out_shape=tuple((jax.ShapeDtypeStruct((width, rows...  7.44 us
    pallas_call x1, Pallas kernels, attention(): pl.pallas_call(attention_kernel, out_shape=jax.ShapeDtypeStruct((width +...  6.44 us
    pallas_call x2, Pallas kernels, project(): pl.pallas_call(kernel, out_shape=(jax.ShapeDtypeStruct((columns, rows), j...  5.61 us
    pallas_call x1, Pallas kernels, flip(): pl.pallas_call(kernel, out_shape=tuple((jax.ShapeDtypeStruct(a.shape[::-1...  4.73 us
  transfers between devices with their start and end apart: 19, of which 11 were waited for; matrix products, arithmetic and copies ran while one was open for 3% of the time, Pallas kernels for 23%

profile of v16, /device:TPU:0, one launch (start us, length us, event | category | flops | bytes accessed | tf_op | source)
XLA Modules:
  0.0 179.3 jit_solution(5338417747740218278)
XLA Ops:
  0.0 1.0 pad_maximum_fusion.2
  1.1 2.4 %collective-permute-start = (bf16[128,512]{1,0:T(8,128)(2,1)S(1)}, bf16[128,512]{1,0:T(8,128)(2,1)S(1)}, u32[]{:S(2)}, u32[]{:S(2)}) collective-permute-start(bf16[128,512]{1,0:T(8,128)(2,1)S(1)} %pad_maximum_fusion.2), channel_id=1, source_target_pairs={{0,1},{1,4},{4,5},{5,8},{8,9},{9,12},{12,13},{2,3},{3,6},{6,7},{7,... | collective-permute-start | bytes 393224 | tf_op jit(solution)/shard_map/ppermute | solution.py:18
  3.4 2.6 %dynamic-slice_bitcast_fusion = bf16[720,1024]{1,0:T(8,128)(2,1)} fusion(bf16[2048,720]{0,1:T(8,128)(2,1)} %param.15, s32[]{:T(128)S(6)} %select_n.95), kind=kLoop, calls=%fused_computation | loop fusion | bytes 2949124 | tf_op jit(solution)/shard_map/dynamic_slice | solution.py:373
  6.1 2.7 %collective-permute-start.3 = (bf16[1440,1440]{1,0:T(8,128)(2,1)}, bf16[1440,1440]{1,0:T(8,128)(2,1)}, u32[]{:S(2)}, u32[]{:S(2)}) collective-permute-start(bf16[1440,1440]{1,0:T(8,128)(2,1)} %bitcast.32), channel_id=1, source_target_pairs={{0,1},{1,0},{2,3},{3,2},{4,5},{5,4},{6,7},{7,6},{8,9},{9,8},{10,11... | collective-permute-start | bytes 12441608 | tf_op jit(solution)/shard_map/ppermute | solution.py:22
  8.7 2.1 %collective-permute-start.2 = (bf16[720,1024]{1,0:T(8,128)(2,1)}, bf16[720,1024]{1,0:T(8,128)(2,1)}, u32[]{:S(2)}, u32[]{:S(2)}) collective-permute-start(bf16[720,1024]{1,0:T(8,128)(2,1)} %dynamic-slice_bitcast_fusion), channel_id=1, source_target_pairs={{0,4},{4,0},{8,12},{12,8},{1,5},{5,1},{9,13},{13,9},{2,6},{6,2},{1... | collective-permute-start | bytes 4423688 | tf_op jit(solution)/shard_map/ppermute | solution.py:22
  11.0 1.1 copy-done.3
  12.1 1.0 copy-done.4
  13.1 0.8 copy-done.7
  13.9 0.8 copy-done.8
  14.8 0.7 copy-done.9
  15.5 0.7 copy-done.10
  16.2 0.7 copy-done.11
  16.8 6.4 %attention.1.refs_0_ = bf16[2784,128]{1,0:T(8,128)(2,1)} custom-call(s32[2]{0:T(128)S(1)} %pad_add_fusion.1.place_ref, f32[32]{0:T(128)S(1)} %copy-done.11, bf16[128,2048]{1,0:T(8,128)(2,1)S(1)} %copy-done.4, bf16[128,512]{1,0:T(8,128)(2,1)S(1)} %collective-permute-done.earlier_ref, bf16[128,256]{1,0:T(8,128)(2,1)S(1)} %copy-done.8, ...), custom_call_target="tpu_custom_call" | custom-call | flops 268435456 | bytes 1572864 | tf_op jit(solution)/shard_map/attention/pallas_call | solution.py:128
  23.2 2.6 %collective-permute-start.1 = (bf16[2784,128]{1,0:T(8,128)(2,1)}, bf16[2784,128]{1,0:T(8,128)(2,1)}, u32[]{:S(2)}, u32[]{:S(2)}) collective-permute-start(bf16[2784,128]{1,0:T(8,128)(2,1)} %attention.1.refs_0_), channel_id=1, source_target_pairs={{0,8},{4,12},{8,0},{12,4},{1,9},{5,13},{9,1},{13,5},{2,10},{6,14},... | collective-permute-start | bytes 2138120 | tf_op jit(solution)/shard_map/ppermute | solution.py:22
  25.8 0.9 dynamic-slice_bitcast_fusion.1.refs_3_.refs_4_
  26.8 31.4 %collective-permute-done.1.refs_1_ = bf16[2784,128]{1,0:T(8,128)(2,1)} collective-permute-done((bf16[2784,128]{1,0:T(8,128)(2,1)}, bf16[2784,128]{1,0:T(8,128)(2,1)}, u32[]{:S(2)}, u32[]{:S(2)}) %collective-permute-start.1) | collective-permute-done | bytes 712736 | tf_op jit(solution)/shard_map/ppermute | solution.py:22
  58.2 0.9 collective-permute-done.2.refs_2_
  59.3 2.4 %project.2 = (f32[720,128]{1,0:T(8,128)S(1)}, bf16[1,720,128]{2,1,0:T(8,128)(2,1)S(1)}) custom-call(s32[3]{0:T(128)S(1)} %pad_add_fusion.place_ref, bf16[2784,128]{1,0:T(8,128)(2,1)} %attention.1.refs_0_, bf16[2784,128]{1,0:T(8,128)(2,1)} %collective-permute-done.1.refs_1_, bf16[720,2048]{1,0:T(8,128)(2,1)S(1)} %bitcast.31, ...), custom_call_target="tpu_custom_call" | custom-call | flops 754974720 | bytes 2949120 | tf_op jit(solution)/shard_map/project/pallas_call | solution.py:210
  61.7 1.0 collective-permute-done.4.refs_3_
  62.7 3.2 %project.3 = (f32[720,128]{1,0:T(8,128)S(1)}, bf16[1,720,128]{2,1,0:T(8,128)(2,1)S(1)}) custom-call(s32[3]{0:T(128)S(1)} %pad_add_fusion.2.place_ref, bf16[2784,128]{1,0:T(8,128)(2,1)} %attention.1.refs_0_, bf16[2784,128]{1,0:T(8,128)(2,1)} %collective-permute-done.1.refs_1_, bf16[720,1024]{1,0:T(8,128)(2,1)} %collective-permute-done.2.refs_2_, ...), custom_call_target="tpu_custom_call" | custom-call | flops 754974720 | bytes 2949120 | tf_op jit(solution)/shard_map/project/pallas_call | solution.py:210
  66.0 1.6 collective-permute-start.5
  67.6 0.7 slice_select_fusion
  68.3 8.4 %collective-permute-done.5 = bf16[1440,128]{1,0:T(8,128)(2,1)S(1)} collective-permute-done((bf16[1440,128]{1,0:T(8,128)(2,1)S(1)}, bf16[1440,128]{1,0:T(8,128)(2,1)S(1)}, u32[]{:S(2)}, u32[]{:S(2)}) %collective-permute-start.5) | collective-permute-done | bytes 368672 | tf_op jit(solution)/shard_map/ppermute | solution.py:22
  77.0 2.6 %collective-permute-start.6 = (bf16[1456,128]{1,0:T(8,128)(2,1)S(1)}, bf16[1456,128]{1,0:T(8,128)(2,1)S(1)}, u32[]{:S(2)}, u32[]{:S(2)}) collective-permute-start(bf16[1456,128]{1,0:T(8,128)(2,1)S(1)} %pad_maximum_fusion.refs_0_), channel_id=1, source_target_pairs={{0,8},{4,12},{8,0},{12,4},{1,9},{5,13},{9,1},{13,5},{2,10},{6,14},... | collective-permute-start | bytes 1118216 | tf_op jit(solution)/shard_map/ppermute | solution.py:22
  79.7 1.5 collective-permute-start.8
  81.3 1.6 collective-permute-start.12
  82.9 13.0 %collective-permute-done.6.refs_1_ = bf16[1456,128]{1,0:T(8,128)(2,1)S(1)} collective-permute-done((bf16[1456,128]{1,0:T(8,128)(2,1)S(1)}, bf16[1456,128]{1,0:T(8,128)(2,1)S(1)}, u32[]{:S(2)}, u32[]{:S(2)}) %collective-permute-start.6) | collective-permute-done | bytes 372768 | tf_op jit(solution)/shard_map/ppermute | solution.py:22
  96.5 1.5 collective-permute-start.9
  98.2 3.4 %copy-done = bf16[1,2,2880,720]{2,3,1,0:T(8,128)(2,1)S(1)} copy-done((bf16[1,2,2880,720]{2,3,1,0:T(8,128)(2,1)S(1)}, bf16[1,2,2880,720]{2,3,1,0:T(8,128)(2,1)}, u32[]{:S(2)}) %copy-start) | copy-done | bytes 8294424
  101.6 1.6 fetched.1.refs_5_
  103.7 1.6 collective-permute-done.7.refs_1_
  105.3 2.7 %collective-permute-done.9.refs_3_ = bf16[1456,128]{1,0:T(8,128)(2,1)S(1)} collective-permute-done((bf16[1456,128]{1,0:T(8,128)(2,1)S(1)}, bf16[1456,128]{1,0:T(8,128)(2,1)S(1)}, u32[]{:S(2)}, u32[]{:S(2)}) %collective-permute-start.9) | collective-permute-done | bytes 372768 | tf_op jit(solution)/shard_map/ppermute | solution.py:22
  108.1 1.5 collective-permute-start.14
  109.6 7.4 %activate.2 = (bf16[2,720,256]{2,1,0:T(8,128)(2,1)S(1)}, f32[2,256]{1,0:T(2,128)S(1)}) custom-call(s32[4]{0:T(128)S(1)} %pad_add_fusion.3.place_ref, bf16[1456,128]{1,0:T(8,128)(2,1)S(1)} %pad_maximum_fusion.refs_0_, bf16[1456,128]{1,0:T(8,128)(2,1)S(1)} %collective-permute-done.6.refs_1_, bf16[1456,128]{1,0:T(8,128)(2,1)S(1)} %collective-permute-done.8.refs_2_, ...), custom_call_target="tpu_custom_call" | custom-call | flops 4246732800 | bytes 16588800 | tf_op jit(solution)/shard_map/activate/pallas_call | solution.py:280
  117.6 6.5 %collective-permute-done.14.refs_3_ = bf16[1456,128]{1,0:T(8,128)(2,1)S(1)} collective-permute-done((bf16[1456,128]{1,0:T(8,128)(2,1)S(1)}, bf16[1456,128]{1,0:T(8,128)(2,1)S(1)}, u32[]{:S(2)}, u32[]{:S(2)}) %collective-permute-start.14) | collective-permute-done | bytes 372768 | tf_op jit(solution)/shard_map/ppermute | solution.py:22
  124.0 1.0 copy-done.6
  125.0 7.4 %activate.3 = (bf16[2,720,256]{2,1,0:T(8,128)(2,1)S(1)}, f32[2,256]{1,0:T(2,128)S(1)}) custom-call(s32[4]{0:T(128)S(1)} %pad_add_fusion.3.place_ref, bf16[1456,128]{1,0:T(8,128)(2,1)S(1)} %collective-permute-done.12.refs_0_, bf16[1456,128]{1,0:T(8,128)(2,1)S(1)} %copy-done.6, bf16[1456,128]{1,0:T(8,128)(2,1)S(1)} %collective-permute-done.13.refs_2_, ...), custom_call_target="tpu_custom_call" | custom-call | flops 4246732800 | bytes 16588800 | tf_op jit(solution)/shard_map/activate/pallas_call | solution.py:280
  132.4 1.6 collective-permute-start.16
  134.1 2.3 %copy-done.2 = bf16[1,1440,1440]{2,1,0:T(8,128)(2,1)S(1)} copy-done((bf16[1,1440,1440]{2,1,0:T(8,128)(2,1)S(1)}, bf16[1,1440,1440]{2,1,0:T(8,128)(2,1)}, u32[]{:S(2)}) %copy-start.2) | copy-done | bytes 4147224
  136.4 4.7 %flip.1 = (bf16[1440,1440]{1,0:T(8,128)(2,1)S(1)}, bf16[1440,1440]{1,0:T(8,128)(2,1)S(1)}) custom-call(bf16[1440,1440]{1,0:T(8,128)(2,1)S(1)} %bitcast.33, bf16[1440,1440]{1,0:T(8,128)(2,1)} %collective-permute-done.3.refs_1_), custom_call_target="tpu_custom_call" | custom-call | bytes 16588800 | tf_op jit(solution)/shard_map/flip/pallas_call | solution.py:144
  141.1 3.7 %combine.2 = (bf16[1440,128]{1,0:T(8,128)(2,1)S(1)}, bf16[1440,128]{1,0:T(8,128)(2,1)S(1)}) custom-call(s32[1]{0:T(128)} %bitcast.t_ref, bf16[2,720,256]{2,1,0:T(8,128)(2,1)S(1)} %get-tuple-element.57.refs_0_, bf16[2,720,256]{2,1,0:T(8,128)(2,1)} %collective-permute-done.11.refs_1_, f32[2,256]{1,0:T(2,128)S(1)} %get-tuple-element.58.refs_2_, ...), custom_call_target="tpu_custom_call" | custom-call | flops 2123366400 | bytes 8294400 | tf_op jit(solution)/shard_map/combine/pallas_call | solution.py:330
  144.8 3.5 %collective-permute-start.15 = (bf16[1440,128]{1,0:T(8,128)(2,1)S(1)}, bf16[1440,128]{1,0:T(8,128)(2,1)S(1)}, u32[]{:S(2)}, u32[]{:S(2)}) collective-permute-start(bf16[1440,128]{1,0:T(8,128)(2,1)S(1)} %get-tuple-element.73), channel_id=1, source_target_pairs={{0,8},{4,12},{8,0},{12,4},{1,9},{5,13},{9,1},{13,5},{2,10},{6,14},... | collective-permute-start | bytes 1105928 | tf_op jit(solution)/shard_map/ppermute | solution.py:22
  148.3 6.1 %collective-permute-done.16.refs_1_ = bf16[2,720,256]{2,1,0:T(8,128)(2,1)} collective-permute-done((bf16[2,720,256]{2,1,0:T(8,128)(2,1)S(1)}, bf16[2,720,256]{2,1,0:T(8,128)(2,1)}, u32[]{:S(2)}, u32[]{:S(2)}) %collective-permute-start.16) | collective-permute-done | bytes 737312 | tf_op jit(solution)/shard_map/ppermute | solution.py:22
  154.5 3.7 %combine.3 = (bf16[1440,128]{1,0:T(8,128)(2,1)S(1)}, bf16[1440,128]{1,0:T(8,128)(2,1)S(1)}) custom-call(s32[1]{0:T(128)} %bitcast.t_ref, bf16[2,720,256]{2,1,0:T(8,128)(2,1)S(1)} %get-tuple-element.67.refs_0_, bf16[2,720,256]{2,1,0:T(8,128)(2,1)} %collective-permute-done.16.refs_1_, f32[2,256]{1,0:T(2,128)S(1)} %get-tuple-element.74.refs_2_, ...), custom_call_target="tpu_custom_call" | custom-call | flops 2123366400 | bytes 8294400 | tf_op jit(solution)/shard_map/combine/pallas_call | solution.py:330
  158.6 4.6 %collective-permute-start.18 = (bf16[1440,128]{1,0:T(8,128)(2,1)S(1)}, bf16[1440,128]{1,0:T(8,128)(2,1)S(1)}, u32[]{:S(2)}, u32[]{:S(2)}) collective-permute-start(bf16[1440,128]{1,0:T(8,128)(2,1)S(1)} %get-tuple-element.76), channel_id=1, source_target_pairs={{0,12},{4,8},{8,4},{12,0},{1,13},{5,9},{9,5},{13,1},{2,14},{6,10},... | collective-permute-start | bytes 1105928 | tf_op jit(solution)/shard_map/ppermute | solution.py:22
  163.5 8.5 %collective-permute-done.17 = bf16[1440,128]{1,0:T(8,128)(2,1)S(1)} collective-permute-done((bf16[1440,128]{1,0:T(8,128)(2,1)S(1)}, bf16[1440,128]{1,0:T(8,128)(2,1)S(1)}, u32[]{:S(2)}, u32[]{:S(2)}) %collective-permute-start.17) | collective-permute-done | bytes 368672 | tf_op jit(solution)/shard_map/ppermute | solution.py:22
  172.0 6.3 %collective-permute-done.18 = bf16[1440,128]{1,0:T(8,128)(2,1)S(1)} collective-permute-done((bf16[1440,128]{1,0:T(8,128)(2,1)S(1)}, bf16[1440,128]{1,0:T(8,128)(2,1)S(1)}, u32[]{:S(2)}, u32[]{:S(2)}) %collective-permute-start.18) | collective-permute-done | bytes 368672 | tf_op jit(solution)/shard_map/ppermute | solution.py:22
  178.3 1.0 fusion.2
  (53 shorter events, 3.4 us)
Async XLA Ops:
  0.0 59.3 %copy-start.1 = (bf16[2048,720]{0,1:T(8,128)(2,1)S(1)}, bf16[2048,720]{0,1:T(8,128)(2,1)}, u32[]{:S(2)}) copy-start(bf16[2048,720]{0,1:T(8,128)(2,1)} %param.15) | copy-start | bytes 8847364
  0.0 59.0 %copy-start.14 = (f32[2880]{0:T(1024)S(1)}, f32[2880]{0:T(1024)}, u32[]{:S(2)}) copy-start(f32[2880]{0:T(1024)} %param.17) | copy-start | bytes 34564
  1.1 5.0 %collective-permute-start = (bf16[128,512]{1,0:T(8,128)(2,1)S(1)}, bf16[128,512]{1,0:T(8,128)(2,1)S(1)}, u32[]{:S(2)}, u32[]{:S(2)}) collective-permute-start(bf16[128,512]{1,0:T(8,128)(2,1)S(1)} %pad_maximum_fusion.2), channel_id=1, source_target_pairs={{0,1},{1,4},{4,5},{5,8},{8,9},{9,12},{12,13},{2,3},{3,6},{6,7},{7,... | collective-permute-start | bytes 393224 | tf_op jit(solution)/shard_map/ppermute | solution.py:18
  6.1 53.0 %collective-permute-start.3 = (bf16[1440,1440]{1,0:T(8,128)(2,1)}, bf16[1440,1440]{1,0:T(8,128)(2,1)}, u32[]{:S(2)}, u32[]{:S(2)}) collective-permute-start(bf16[1440,1440]{1,0:T(8,128)(2,1)} %bitcast.32), channel_id=1, source_target_pairs={{0,1},{1,0},{2,3},{3,2},{4,5},{5,4},{6,7},{7,6},{8,9},{9,8},{10,11... | collective-permute-start | bytes 12441608 | tf_op jit(solution)/shard_map/ppermute | solution.py:22
  8.7 100.9 %collective-permute-start.10 = (bf16[2,720,2880]{2,1,0:T(8,128)(2,1)}, bf16[2,720,2880]{2,1,0:T(8,128)(2,1)}, u32[]{:S(2)}, u32[]{:S(2)}) collective-permute-start(bf16[2,720,2880]{2,1,0:T(8,128)(2,1)} %bitcast.29), channel_id=1, source_target_pairs={{0,1},{1,0},{2,3},{3,2},{4,5},{5,4},{6,7},{7,6},{8,9},{9,8},{10,11... | collective-permute-start | bytes 24883208 | tf_op jit(solution)/shard_map/ppermute | solution.py:22
  8.7 50.3 %collective-permute-start.2 = (bf16[720,1024]{1,0:T(8,128)(2,1)}, bf16[720,1024]{1,0:T(8,128)(2,1)}, u32[]{:S(2)}, u32[]{:S(2)}) collective-permute-start(bf16[720,1024]{1,0:T(8,128)(2,1)} %dynamic-slice_bitcast_fusion), channel_id=1, source_target_pairs={{0,4},{4,0},{8,12},{12,8},{1,5},{5,1},{9,13},{13,9},{2,6},{6,2},{1... | collective-permute-start | bytes 4423688 | tf_op jit(solution)/shard_map/ppermute | solution.py:22
  10.9 1.1 copy-start.3
  12.1 1.0 copy-start.4
  13.1 0.8 copy-start.7
  13.9 0.8 copy-start.8
  14.8 0.7 copy-start.9
  15.5 0.7 copy-start.10
  16.2 0.7 copy-start.11
  23.2 34.9 %collective-permute-start.1 = (bf16[2784,128]{1,0:T(8,128)(2,1)}, bf16[2784,128]{1,0:T(8,128)(2,1)}, u32[]{:S(2)}, u32[]{:S(2)}) collective-permute-start(bf16[2784,128]{1,0:T(8,128)(2,1)} %attention.1.refs_0_), channel_id=1, source_target_pairs={{0,8},{4,12},{8,0},{12,4},{1,9},{5,13},{9,1},{13,5},{2,10},{6,14},... | collective-permute-start | bytes 2138120 | tf_op jit(solution)/shard_map/ppermute | solution.py:22
  59.0 3.6 %collective-permute-start.4 = (bf16[720,1024]{1,0:T(8,128)(2,1)}, bf16[720,1024]{1,0:T(8,128)(2,1)}, u32[]{:S(2)}, u32[]{:S(2)}) collective-permute-start(bf16[720,1024]{1,0:T(8,128)(2,1)} %collective-permute-done.2.refs_2_), channel_id=1, source_target_pairs={{0,1},{1,0},{2,3},{3,2},{4,5},{5,4},{6,7},{7,6},{8,9},{9,8},{10,11... | collective-permute-start | bytes 4423688 | tf_op jit(solution)/shard_map/ppermute | solution.py:22
  66.0 10.7 %collective-permute-start.5 = (bf16[1440,128]{1,0:T(8,128)(2,1)S(1)}, bf16[1440,128]{1,0:T(8,128)(2,1)S(1)}, u32[]{:S(2)}, u32[]{:S(2)}) collective-permute-start(bf16[1440,128]{1,0:T(8,128)(2,1)S(1)} %pad_maximum_fusion.1), channel_id=1, source_target_pairs={{0,2},{2,0},{1,3},{3,1},{4,6},{6,4},{5,7},{7,5},{8,10},{10,8},{9,1... | collective-permute-start | bytes 1105928 | tf_op jit(solution)/shard_map/ppermute | solution.py:22
  76.9 19.5 %copy-start.12 = (bf16[1440,128]{1,0:T(8,128)(2,1)}, bf16[1440,128]{1,0:T(8,128)(2,1)S(1)}, u32[]{:S(2)}) copy-start(bf16[1440,128]{1,0:T(8,128)(2,1)S(1)} %fusion.1) | copy-start | bytes 1105924
  77.0 18.9 %collective-permute-start.6 = (bf16[1456,128]{1,0:T(8,128)(2,1)S(1)}, bf16[1456,128]{1,0:T(8,128)(2,1)S(1)}, u32[]{:S(2)}, u32[]{:S(2)}) collective-permute-start(bf16[1456,128]{1,0:T(8,128)(2,1)S(1)} %pad_maximum_fusion.refs_0_), channel_id=1, source_target_pairs={{0,8},{4,12},{8,0},{12,4},{1,9},{5,13},{9,1},{13,5},{2,10},{6,14},... | collective-permute-start | bytes 1118216 | tf_op jit(solution)/shard_map/ppermute | solution.py:22
  79.7 24.0 %collective-permute-start.8 = (bf16[1456,128]{1,0:T(8,128)(2,1)S(1)}, bf16[1456,128]{1,0:T(8,128)(2,1)S(1)}, u32[]{:S(2)}, u32[]{:S(2)}) collective-permute-start(bf16[1456,128]{1,0:T(8,128)(2,1)S(1)} %pad_maximum_fusion.refs_0_), channel_id=1, source_target_pairs={{0,2},{2,0},{1,3},{3,1},{4,6},{6,4},{5,7},{7,5},{8,10},{10,8},{9,1... | collective-permute-start | bytes 1118216 | tf_op jit(solution)/shard_map/ppermute | solution.py:22
  81.3 21.9 %collective-permute-start.12 = (bf16[1456,128]{1,0:T(8,128)(2,1)S(1)}, bf16[1456,128]{1,0:T(8,128)(2,1)S(1)}, u32[]{:S(2)}, u32[]{:S(2)}) collective-permute-start(bf16[1456,128]{1,0:T(8,128)(2,1)S(1)} %pad_maximum_fusion.refs_0_), channel_id=1, source_target_pairs={{0,4},{4,0},{8,12},{12,8},{1,5},{5,1},{9,13},{13,9},{2,6},{6,2},{1... | collective-permute-start | bytes 1118216 | tf_op jit(solution)/shard_map/ppermute | solution.py:22
  95.9 9.4 %collective-permute-start.7 = (bf16[1456,128]{1,0:T(8,128)(2,1)S(1)}, bf16[1456,128]{1,0:T(8,128)(2,1)S(1)}, u32[]{:S(2)}, u32[]{:S(2)}) collective-permute-start(bf16[1456,128]{1,0:T(8,128)(2,1)S(1)} %collective-permute-done.6.refs_1_), channel_id=1, source_target_pairs={{0,4},{4,0},{8,12},{12,8},{1,5},{5,1},{9,13},{13,9},{2,6},{6,2},{1... | collective-permute-start | bytes 1118216 | tf_op jit(solution)/shard_map/ppermute | solution.py:22
  96.5 11.6 %collective-permute-start.9 = (bf16[1456,128]{1,0:T(8,128)(2,1)S(1)}, bf16[1456,128]{1,0:T(8,128)(2,1)S(1)}, u32[]{:S(2)}, u32[]{:S(2)}) collective-permute-start(bf16[1456,128]{1,0:T(8,128)(2,1)S(1)} %collective-permute-done.6.refs_1_), channel_id=1, source_target_pairs={{0,2},{2,0},{1,3},{3,1},{4,6},{6,4},{5,7},{7,5},{8,10},{10,8},{9,1... | collective-permute-start | bytes 1118216 | tf_op jit(solution)/shard_map/ppermute | solution.py:22
  98.2 3.4 %copy-start = (bf16[1,2,2880,720]{2,3,1,0:T(8,128)(2,1)S(1)}, bf16[1,2,2880,720]{2,3,1,0:T(8,128)(2,1)}, u32[]{:S(2)}) copy-start(bf16[1,2,2880,720]{2,3,1,0:T(8,128)(2,1)} %param.18) | copy-start | bytes 24883204
  103.2 14.4 %collective-permute-start.13 = (bf16[1456,128]{1,0:T(8,128)(2,1)S(1)}, bf16[1456,128]{1,0:T(8,128)(2,1)S(1)}, u32[]{:S(2)}, u32[]{:S(2)}) collective-permute-start(bf16[1456,128]{1,0:T(8,128)(2,1)S(1)} %collective-permute-done.12.refs_0_), channel_id=1, source_target_pairs={{0,2},{2,0},{1,3},{3,1},{4,6},{6,4},{5,7},{7,5},{8,10},{10,8},{9,1... | collective-permute-start | bytes 1118216 | tf_op jit(solution)/shard_map/ppermute | solution.py:22
  105.3 11.7 %copy-start.5 = (bf16[1456,128]{1,0:T(8,128)(2,1)}, bf16[1456,128]{1,0:T(8,128)(2,1)S(1)}, u32[]{:S(2)}) copy-start(bf16[1456,128]{1,0:T(8,128)(2,1)S(1)} %collective-permute-done.7.refs_1_) | copy-start | bytes 1118212
  108.1 16.0 %collective-permute-start.14 = (bf16[1456,128]{1,0:T(8,128)(2,1)S(1)}, bf16[1456,128]{1,0:T(8,128)(2,1)S(1)}, u32[]{:S(2)}, u32[]{:S(2)}) collective-permute-start(bf16[1456,128]{1,0:T(8,128)(2,1)S(1)} %collective-permute-done.7.refs_1_), channel_id=1, source_target_pairs={{0,2},{2,0},{1,3},{3,1},{4,6},{6,4},{5,7},{7,5},{8,10},{10,8},{9,1... | collective-permute-start | bytes 1118216 | tf_op jit(solution)/shard_map/ppermute | solution.py:22
  117.0 24.1 %collective-permute-start.11 = (bf16[2,720,256]{2,1,0:T(8,128)(2,1)S(1)}, bf16[2,720,256]{2,1,0:T(8,128)(2,1)}, u32[]{:S(2)}, u32[]{:S(2)}) collective-permute-start(bf16[2,720,256]{2,1,0:T(8,128)(2,1)S(1)} %get-tuple-element.57.refs_0_), channel_id=1, source_target_pairs={{0,2},{2,0},{1,3},{3,1},{4,6},{6,4},{5,7},{7,5},{8,10},{10,8},{9,1... | collective-permute-start | bytes 2211848 | tf_op jit(solution)/shard_map/ppermute | solution.py:22
  124.0 1.0 copy-start.6
  132.4 22.1 %collective-permute-start.16 = (bf16[2,720,256]{2,1,0:T(8,128)(2,1)S(1)}, bf16[2,720,256]{2,1,0:T(8,128)(2,1)}, u32[]{:S(2)}, u32[]{:S(2)}) collective-permute-start(bf16[2,720,256]{2,1,0:T(8,128)(2,1)S(1)} %get-tuple-element.67.refs_0_), channel_id=1, source_target_pairs={{0,2},{2,0},{1,3},{3,1},{4,6},{6,4},{5,7},{7,5},{8,10},{10,8},{9,1... | collective-permute-start | bytes 2211848 | tf_op jit(solution)/shard_map/ppermute | solution.py:22
  134.1 2.3 %copy-start.2 = (bf16[1,1440,1440]{2,1,0:T(8,128)(2,1)S(1)}, bf16[1,1440,1440]{2,1,0:T(8,128)(2,1)}, u32[]{:S(2)}) copy-start(bf16[1,1440,1440]{2,1,0:T(8,128)(2,1)} %param.19) | copy-start | bytes 12441604
  144.8 18.6 %collective-permute-start.15 = (bf16[1440,128]{1,0:T(8,128)(2,1)S(1)}, bf16[1440,128]{1,0:T(8,128)(2,1)S(1)}, u32[]{:S(2)}, u32[]{:S(2)}) collective-permute-start(bf16[1440,128]{1,0:T(8,128)(2,1)S(1)} %get-tuple-element.73), channel_id=1, source_target_pairs={{0,8},{4,12},{8,0},{12,4},{1,9},{5,13},{9,1},{13,5},{2,10},{6,14},... | collective-permute-start | bytes 1105928 | tf_op jit(solution)/shard_map/ppermute | solution.py:22
  154.5 8.7 %copy-start.13 = (bf16[1440,128]{1,0:T(8,128)(2,1)S(1)}, bf16[1440,128]{1,0:T(8,128)(2,1)}, u32[]{:S(2)}) copy-start(bf16[1440,128]{1,0:T(8,128)(2,1)} %copy-done.12) | copy-start | bytes 1105924
  158.2 13.8 %collective-permute-start.17 = (bf16[1440,128]{1,0:T(8,128)(2,1)S(1)}, bf16[1440,128]{1,0:T(8,128)(2,1)S(1)}, u32[]{:S(2)}, u32[]{:S(2)}) collective-permute-start(bf16[1440,128]{1,0:T(8,128)(2,1)S(1)} %get-tuple-element.75), channel_id=1, source_target_pairs={{0,4},{4,0},{8,12},{12,8},{1,5},{5,1},{9,13},{13,9},{2,6},{6,2},{1... | collective-permute-start | bytes 1105928 | tf_op jit(solution)/shard_map/ppermute | solution.py:22
  158.6 19.7 %collective-permute-start.18 = (bf16[1440,128]{1,0:T(8,128)(2,1)S(1)}, bf16[1440,128]{1,0:T(8,128)(2,1)S(1)}, u32[]{:S(2)}, u32[]{:S(2)}) collective-permute-start(bf16[1440,128]{1,0:T(8,128)(2,1)S(1)} %get-tuple-element.76), channel_id=1, source_target_pairs={{0,12},{4,8},{8,4},{12,0},{1,13},{5,9},{9,5},{13,1},{2,14},{6,10},... | collective-permute-start | bytes 1105928 | tf_op jit(solution)/shard_map/ppermute | solution.py:22

commit v17 on v16

--- a/solution.py
+++ b/solution.py
@@ -435,16 +435,13 @@
         distance //= 2
     for m in range(1, t_count):
         pieces[m].update({d: swapped(own[d], "tp", m) for d in range(0, z_count, group) if d not in pieces[m]})
-    late = {d: own[d] for d in own if d % group and d != 1}
-    late, pieces[1:] = lax.optimization_barrier((late, pieces[1:]))
-    for m in range(1, t_count):
-        pieces[m].update({d: swapped(late[d], "tp", m) for d in late})
+        pieces[m].update({d: swapped(own[d], "tp", m) for d in own if d % group and d != 1})
 
     weight, _ = lax.optimization_barrier((experts_in[0], own[group]))
     experts_in[0] = fetched(weight)
-    odd, _ = lax.optimization_barrier((own[1], experts_in[0]))
+    handed, _ = lax.optimization_barrier(([part[0] for part in pieces[1:]], [experts_in[0], own[1]]))
     for m in range(1, t_count):
-        pieces[m][1] = swapped(odd, "tp", m)
+        pieces[m][1] = swapped(handed[m - 1], "ep", 1)
 
     inverse_gain = 1.0 / norm_gain
     inverse_square = inverse_gain * inverse_gain

time: 180 us -> 172 us (0.956)
  waiting for transfers between devices: 86.4 us -> 77.9 us
    ppermute x18, waiting for transfers between devices: 86.4 us -> 77.9 us  [swapped(): lax.ppermute(block, axis, [(i, i ^ distance) for i in range(lax.axis_size...]
  transfers between devices with their start and end apart: 19 -> 19, of which waited for: 11 -> 10; matrix products, arithmetic and copies ran while one was open for 3% -> 3% of each run, Pallas kernels for 23% -> 24%
where the time goes in v17:
time: 172 us; the launch traced here: 171 us
  waiting for transfers between devices  77.9 us (45%)
  Pallas kernels  40.6 us (24%)
  starting transfers between devices  32.4 us (19%)
  local copies, waits for them, and re-layouts  16.4 us (10%)
  other arithmetic  3.78 us (2%)
    ppermute x18, waiting for transfers between devices, swapped(): lax.ppermute(block, axis, [(i, i ^ distance) for i in range(lax.axis_size...  77.9 us
    ppermute x18, starting transfers between devices, swapped(): lax.ppermute(block, axis, [(i, i ^ distance) for i in range(lax.axis_size...  30 us
    pallas_call x2, Pallas kernels, activate(): pl.pallas_call(kernel, out_shape=(jax.ShapeDtypeStruct((experts, units, l...  14.8 us
    unnamed x30, local copies, waits for them, and re-layouts  12.5 us
    pallas_call x2, Pallas kernels, combine(): pl.pallas_call(kernel, out_shape=tuple((jax.ShapeDtypeStruct((width, rows...  7.44 us
    pallas_call x1, Pallas kernels, attention(): pl.pallas_call(attention_kernel, out_shape=jax.ShapeDtypeStruct((width +...  6.44 us
    pallas_call x2, Pallas kernels, project(): pl.pallas_call(kernel, out_shape=(jax.ShapeDtypeStruct((columns, rows), j...  5.61 us
    pallas_call x1, Pallas kernels, flip(): pl.pallas_call(kernel, out_shape=tuple((jax.ShapeDtypeStruct(a.shape[::-1...  4.73 us
  transfers between devices with their start and end apart: 19, of which 10 were waited for; matrix products, arithmetic and copies ran while one was open for 3% of the time, Pallas kernels for 24%

profile of v17, /device:TPU:0, one launch (start us, length us, event | category | flops | bytes accessed | tf_op | source)
XLA Modules:
  0.0 171.2 jit_solution(4207621312511431511)
XLA Ops:
  0.0 1.0 pad_maximum_fusion.2
  1.1 2.4 %collective-permute-start = (bf16[128,512]{1,0:T(8,128)(2,1)S(1)}, bf16[128,512]{1,0:T(8,128)(2,1)S(1)}, u32[]{:S(2)}, u32[]{:S(2)}) collective-permute-start(bf16[128,512]{1,0:T(8,128)(2,1)S(1)} %pad_maximum_fusion.2), channel_id=1, source_target_pairs={{0,1},{1,4},{4,5},{5,8},{8,9},{9,12},{12,13},{2,3},{3,6},{6,7},{7,... | collective-permute-start | bytes 393224 | tf_op jit(solution)/shard_map/ppermute | solution.py:18
  3.4 2.6 %dynamic-slice_bitcast_fusion = bf16[720,1024]{1,0:T(8,128)(2,1)} fusion(bf16[2048,720]{0,1:T(8,128)(2,1)} %param.15, s32[]{:T(128)S(6)} %select_n.95), kind=kLoop, calls=%fused_computation | loop fusion | bytes 2949124 | tf_op jit(solution)/shard_map/dynamic_slice | solution.py:373
  6.1 2.7 %collective-permute-start.3 = (bf16[1440,1440]{1,0:T(8,128)(2,1)}, bf16[1440,1440]{1,0:T(8,128)(2,1)}, u32[]{:S(2)}, u32[]{:S(2)}) collective-permute-start(bf16[1440,1440]{1,0:T(8,128)(2,1)} %bitcast.32), channel_id=1, source_target_pairs={{0,1},{1,0},{2,3},{3,2},{4,5},{5,4},{6,7},{7,6},{8,9},{9,8},{10,11... | collective-permute-start | bytes 12441608 | tf_op jit(solution)/shard_map/ppermute | solution.py:22
  8.7 2.1 %collective-permute-start.2 = (bf16[720,1024]{1,0:T(8,128)(2,1)}, bf16[720,1024]{1,0:T(8,128)(2,1)}, u32[]{:S(2)}, u32[]{:S(2)}) collective-permute-start(bf16[720,1024]{1,0:T(8,128)(2,1)} %dynamic-slice_bitcast_fusion), channel_id=1, source_target_pairs={{0,4},{4,0},{8,12},{12,8},{1,5},{5,1},{9,13},{13,9},{2,6},{6,2},{1... | collective-permute-start | bytes 4423688 | tf_op jit(solution)/shard_map/ppermute | solution.py:22
  11.0 1.1 copy-done.3
  12.1 1.0 copy-done.4
  13.1 0.8 copy-done.7
  13.9 0.8 copy-done.8
  14.8 0.7 copy-done.9
  15.5 0.7 copy-done.10
  16.2 0.7 copy-done.11
  16.8 6.4 %attention.1.refs_0_ = bf16[2784,128]{1,0:T(8,128)(2,1)} custom-call(s32[2]{0:T(128)S(1)} %pad_add_fusion.1.place_ref, f32[32]{0:T(128)S(1)} %copy-done.11, bf16[128,2048]{1,0:T(8,128)(2,1)S(1)} %copy-done.4, bf16[128,512]{1,0:T(8,128)(2,1)S(1)} %collective-permute-done.earlier_ref, bf16[128,256]{1,0:T(8,128)(2,1)S(1)} %copy-done.8, ...), custom_call_target="tpu_custom_call" | custom-call | flops 268435456 | bytes 1572864 | tf_op jit(solution)/shard_map/attention/pallas_call | solution.py:128
  23.2 2.6 %collective-permute-start.1 = (bf16[2784,128]{1,0:T(8,128)(2,1)}, bf16[2784,128]{1,0:T(8,128)(2,1)}, u32[]{:S(2)}, u32[]{:S(2)}) collective-permute-start(bf16[2784,128]{1,0:T(8,128)(2,1)} %attention.1.refs_0_), channel_id=1, source_target_pairs={{0,8},{4,12},{8,0},{12,4},{1,9},{5,13},{9,1},{13,5},{2,10},{6,14},... | collective-permute-start | bytes 2138120 | tf_op jit(solution)/shard_map/ppermute | solution.py:22
  25.8 0.9 dynamic-slice_bitcast_fusion.1.refs_3_.refs_4_
  26.8 31.4 %collective-permute-done.1.refs_1_ = bf16[2784,128]{1,0:T(8,128)(2,1)} collective-permute-done((bf16[2784,128]{1,0:T(8,128)(2,1)}, bf16[2784,128]{1,0:T(8,128)(2,1)}, u32[]{:S(2)}, u32[]{:S(2)}) %collective-permute-start.1) | collective-permute-done | bytes 712736 | tf_op jit(solution)/shard_map/ppermute | solution.py:22
  58.2 0.9 collective-permute-done.2.refs_2_
  59.3 2.4 %project.2 = (f32[720,128]{1,0:T(8,128)S(1)}, bf16[1,720,128]{2,1,0:T(8,128)(2,1)S(1)}) custom-call(s32[3]{0:T(128)S(1)} %pad_add_fusion.place_ref, bf16[2784,128]{1,0:T(8,128)(2,1)} %attention.1.refs_0_, bf16[2784,128]{1,0:T(8,128)(2,1)} %collective-permute-done.1.refs_1_, bf16[720,2048]{1,0:T(8,128)(2,1)S(1)} %bitcast.31, ...), custom_call_target="tpu_custom_call" | custom-call | flops 754974720 | bytes 2949120 | tf_op jit(solution)/shard_map/project/pallas_call | solution.py:210
  61.7 1.0 collective-permute-done.4.refs_3_
  62.7 3.2 %project.3 = (f32[720,128]{1,0:T(8,128)S(1)}, bf16[1,720,128]{2,1,0:T(8,128)(2,1)S(1)}) custom-call(s32[3]{0:T(128)S(1)} %pad_add_fusion.2.place_ref, bf16[2784,128]{1,0:T(8,128)(2,1)} %attention.1.refs_0_, bf16[2784,128]{1,0:T(8,128)(2,1)} %collective-permute-done.1.refs_1_, bf16[720,1024]{1,0:T(8,128)(2,1)} %collective-permute-done.2.refs_2_, ...), custom_call_target="tpu_custom_call" | custom-call | flops 754974720 | bytes 2949120 | tf_op jit(solution)/shard_map/project/pallas_call | solution.py:210
  66.0 1.6 collective-permute-start.5
  67.6 0.7 slice_select_fusion
  68.3 8.4 %collective-permute-done.5 = bf16[1440,128]{1,0:T(8,128)(2,1)S(1)} collective-permute-done((bf16[1440,128]{1,0:T(8,128)(2,1)S(1)}, bf16[1440,128]{1,0:T(8,128)(2,1)S(1)}, u32[]{:S(2)}, u32[]{:S(2)}) %collective-permute-start.5) | collective-permute-done | bytes 368672 | tf_op jit(solution)/shard_map/ppermute | solution.py:22
  77.0 2.6 %collective-permute-start.6 = (bf16[1456,128]{1,0:T(8,128)(2,1)S(1)}, bf16[1456,128]{1,0:T(8,128)(2,1)S(1)}, u32[]{:S(2)}, u32[]{:S(2)}) collective-permute-start(bf16[1456,128]{1,0:T(8,128)(2,1)S(1)} %pad_maximum_fusion.refs_0_), channel_id=1, source_target_pairs={{0,8},{4,12},{8,0},{12,4},{1,9},{5,13},{9,1},{13,5},{2,10},{6,14},... | collective-permute-start | bytes 1118216 | tf_op jit(solution)/shard_map/ppermute | solution.py:22
  79.7 1.5 collective-permute-start.7
  81.3 1.6 collective-permute-start.11
  82.9 13.0 %collective-permute-done.6.refs_1_ = bf16[1456,128]{1,0:T(8,128)(2,1)S(1)} collective-permute-done((bf16[1456,128]{1,0:T(8,128)(2,1)S(1)}, bf16[1456,128]{1,0:T(8,128)(2,1)S(1)}, u32[]{:S(2)}, u32[]{:S(2)}) %collective-permute-start.6) | collective-permute-done | bytes 372768 | tf_op jit(solution)/shard_map/ppermute | solution.py:22
  95.9 1.4 collective-permute-start.8
  98.2 3.4 %copy-done = bf16[1,2,2880,720]{2,3,1,0:T(8,128)(2,1)S(1)} copy-done((bf16[1,2,2880,720]{2,3,1,0:T(8,128)(2,1)S(1)}, bf16[1,2,2880,720]{2,3,1,0:T(8,128)(2,1)}, u32[]{:S(2)}) %copy-start) | copy-done | bytes 8294424
  101.6 1.6 fetched.1.refs_5_
  103.2 1.4 collective-permute-start.13
  104.6 3.2 %collective-permute-done.12.refs_1_ = bf16[1456,128]{1,0:T(8,128)(2,1)S(1)} collective-permute-done((bf16[1456,128]{1,0:T(8,128)(2,1)S(1)}, bf16[1456,128]{1,0:T(8,128)(2,1)S(1)}, u32[]{:S(2)}, u32[]{:S(2)}) %collective-permute-start.12) | collective-permute-done | bytes 372768 | tf_op jit(solution)/shard_map/ppermute | solution.py:22
  108.3 7.4 %activate.2 = (bf16[2,720,256]{2,1,0:T(8,128)(2,1)S(1)}, f32[2,256]{1,0:T(2,128)S(1)}) custom-call(s32[4]{0:T(128)S(1)} %pad_add_fusion.3.place_ref, bf16[1456,128]{1,0:T(8,128)(2,1)S(1)} %pad_maximum_fusion.refs_0_, bf16[1456,128]{1,0:T(8,128)(2,1)S(1)} %collective-permute-done.6.refs_1_, bf16[1456,128]{1,0:T(8,128)(2,1)S(1)} %collective-permute-done.7.refs_2_, ...), custom_call_target="tpu_custom_call" | custom-call | flops 4246732800 | bytes 16588800 | tf_op jit(solution)/shard_map/activate/pallas_call | solution.py:280
  115.7 1.6 collective-permute-start.10
  117.3 1.0 copy-done.6
  118.3 7.4 %activate.3 = (bf16[2,720,256]{2,1,0:T(8,128)(2,1)S(1)}, f32[2,256]{1,0:T(2,128)S(1)}) custom-call(s32[4]{0:T(128)S(1)} %pad_add_fusion.3.place_ref, bf16[1456,128]{1,0:T(8,128)(2,1)S(1)} %collective-permute-done.11.refs_0_, bf16[1456,128]{1,0:T(8,128)(2,1)S(1)} %copy-done.6, bf16[1456,128]{1,0:T(8,128)(2,1)S(1)} %collective-permute-done.13.refs_2_, ...), custom_call_target="tpu_custom_call" | custom-call | flops 4246732800 | bytes 16588800 | tf_op jit(solution)/shard_map/activate/pallas_call | solution.py:280
  126.4 2.3 %copy-done.2 = bf16[1,1440,1440]{2,1,0:T(8,128)(2,1)S(1)} copy-done((bf16[1,1440,1440]{2,1,0:T(8,128)(2,1)S(1)}, bf16[1,1440,1440]{2,1,0:T(8,128)(2,1)}, u32[]{:S(2)}) %copy-start.2) | copy-done | bytes 4147224
  128.6 4.7 %flip.1 = (bf16[1440,1440]{1,0:T(8,128)(2,1)S(1)}, bf16[1440,1440]{1,0:T(8,128)(2,1)S(1)}) custom-call(bf16[1440,1440]{1,0:T(8,128)(2,1)S(1)} %bitcast.33, bf16[1440,1440]{1,0:T(8,128)(2,1)} %collective-permute-done.3.refs_1_), custom_call_target="tpu_custom_call" | custom-call | bytes 16588800 | tf_op jit(solution)/shard_map/flip/pallas_call | solution.py:144
  133.4 2.0 %collective-permute-done.10.refs_1_ = bf16[2,720,256]{2,1,0:T(8,128)(2,1)} collective-permute-done((bf16[2,720,256]{2,1,0:T(8,128)(2,1)S(1)}, bf16[2,720,256]{2,1,0:T(8,128)(2,1)}, u32[]{:S(2)}, u32[]{:S(2)}) %collective-permute-start.10) | collective-permute-done | bytes 737312 | tf_op jit(solution)/shard_map/ppermute | solution.py:22
  135.3 3.7 %combine.2 = (bf16[1440,128]{1,0:T(8,128)(2,1)S(1)}, bf16[1440,128]{1,0:T(8,128)(2,1)S(1)}) custom-call(s32[1]{0:T(128)} %bitcast.t_ref, bf16[2,720,256]{2,1,0:T(8,128)(2,1)S(1)} %get-tuple-element.52.refs_0_, bf16[2,720,256]{2,1,0:T(8,128)(2,1)} %collective-permute-done.10.refs_1_, f32[2,256]{1,0:T(2,128)S(1)} %get-tuple-element.53.refs_2_, ...), custom_call_target="tpu_custom_call" | custom-call | flops 2123366400 | bytes 8294400 | tf_op jit(solution)/shard_map/combine/pallas_call | solution.py:330
  139.0 3.2 %collective-permute-start.15 = (bf16[1440,128]{1,0:T(8,128)(2,1)S(1)}, bf16[1440,128]{1,0:T(8,128)(2,1)S(1)}, u32[]{:S(2)}, u32[]{:S(2)}) collective-permute-start(bf16[1440,128]{1,0:T(8,128)(2,1)S(1)} %get-tuple-element.67), channel_id=1, source_target_pairs={{0,8},{4,12},{8,0},{12,4},{1,9},{5,13},{9,1},{13,5},{2,10},{6,14},... | collective-permute-start | bytes 1105928 | tf_op jit(solution)/shard_map/ppermute | solution.py:22
  142.3 4.8 %collective-permute-done.16.refs_1_ = bf16[2,720,256]{2,1,0:T(8,128)(2,1)} collective-permute-done((bf16[2,720,256]{2,1,0:T(8,128)(2,1)S(1)}, bf16[2,720,256]{2,1,0:T(8,128)(2,1)}, u32[]{:S(2)}, u32[]{:S(2)}) %collective-permute-start.16) | collective-permute-done | bytes 737312 | tf_op jit(solution)/shard_map/ppermute | solution.py:22
  147.1 3.7 %combine.3 = (bf16[1440,128]{1,0:T(8,128)(2,1)S(1)}, bf16[1440,128]{1,0:T(8,128)(2,1)S(1)}) custom-call(s32[1]{0:T(128)} %bitcast.t_ref, bf16[2,720,256]{2,1,0:T(8,128)(2,1)S(1)} %get-tuple-element.61.refs_0_, bf16[2,720,256]{2,1,0:T(8,128)(2,1)} %collective-permute-done.16.refs_1_, f32[2,256]{1,0:T(2,128)S(1)} %get-tuple-element.68.refs_2_, ...), custom_call_target="tpu_custom_call" | custom-call | flops 2123366400 | bytes 8294400 | tf_op jit(solution)/shard_map/combine/pallas_call | solution.py:330
  150.8 2.5 %collective-permute-start.17 = (bf16[1440,128]{1,0:T(8,128)(2,1)S(1)}, bf16[1440,128]{1,0:T(8,128)(2,1)S(1)}, u32[]{:S(2)}, u32[]{:S(2)}) collective-permute-start(bf16[1440,128]{1,0:T(8,128)(2,1)S(1)} %get-tuple-element.69), channel_id=1, source_target_pairs={{0,4},{4,0},{8,12},{12,8},{1,5},{5,1},{9,13},{13,9},{2,6},{6,2},{1... | collective-permute-start | bytes 1105928 | tf_op jit(solution)/shard_map/ppermute | solution.py:22
  153.3 3.4 %collective-permute-start.18 = (bf16[1440,128]{1,0:T(8,128)(2,1)S(1)}, bf16[1440,128]{1,0:T(8,128)(2,1)S(1)}, u32[]{:S(2)}, u32[]{:S(2)}) collective-permute-start(bf16[1440,128]{1,0:T(8,128)(2,1)S(1)} %get-tuple-element.70), channel_id=1, source_target_pairs={{0,12},{4,8},{8,4},{12,0},{1,13},{5,9},{9,5},{13,1},{2,14},{6,10},... | collective-permute-start | bytes 1105928 | tf_op jit(solution)/shard_map/ppermute | solution.py:22
  157.0 8.8 %collective-permute-done.17 = bf16[1440,128]{1,0:T(8,128)(2,1)S(1)} collective-permute-done((bf16[1440,128]{1,0:T(8,128)(2,1)S(1)}, bf16[1440,128]{1,0:T(8,128)(2,1)S(1)}, u32[]{:S(2)}, u32[]{:S(2)}) %collective-permute-start.17) | collective-permute-done | bytes 368672 | tf_op jit(solution)/shard_map/ppermute | solution.py:22
  165.7 4.5 %collective-permute-done.18 = bf16[1440,128]{1,0:T(8,128)(2,1)S(1)} collective-permute-done((bf16[1440,128]{1,0:T(8,128)(2,1)S(1)}, bf16[1440,128]{1,0:T(8,128)(2,1)S(1)}, u32[]{:S(2)}, u32[]{:S(2)}) %collective-permute-start.18) | collective-permute-done | bytes 368672 | tf_op jit(solution)/shard_map/ppermute | solution.py:22
  170.2 1.0 fusion.2
  (53 shorter events, 3.1 us)
Async XLA Ops:
  0.0 59.3 %copy-start.1 = (bf16[2048,720]{0,1:T(8,128)(2,1)S(1)}, bf16[2048,720]{0,1:T(8,128)(2,1)}, u32[]{:S(2)}) copy-start(bf16[2048,720]{0,1:T(8,128)(2,1)} %param.15) | copy-start | bytes 8847364
  0.0 59.0 %copy-start.14 = (f32[2880]{0:T(1024)S(1)}, f32[2880]{0:T(1024)}, u32[]{:S(2)}) copy-start(f32[2880]{0:T(1024)} %param.17) | copy-start | bytes 34564
  1.1 5.0 %collective-permute-start = (bf16[128,512]{1,0:T(8,128)(2,1)S(1)}, bf16[128,512]{1,0:T(8,128)(2,1)S(1)}, u32[]{:S(2)}, u32[]{:S(2)}) collective-permute-start(bf16[128,512]{1,0:T(8,128)(2,1)S(1)} %pad_maximum_fusion.2), channel_id=1, source_target_pairs={{0,1},{1,4},{4,5},{5,8},{8,9},{9,12},{12,13},{2,3},{3,6},{6,7},{7,... | collective-permute-start | bytes 393224 | tf_op jit(solution)/shard_map/ppermute | solution.py:18
  6.1 53.0 %collective-permute-start.3 = (bf16[1440,1440]{1,0:T(8,128)(2,1)}, bf16[1440,1440]{1,0:T(8,128)(2,1)}, u32[]{:S(2)}, u32[]{:S(2)}) collective-permute-start(bf16[1440,1440]{1,0:T(8,128)(2,1)} %bitcast.32), channel_id=1, source_target_pairs={{0,1},{1,0},{2,3},{3,2},{4,5},{5,4},{6,7},{7,6},{8,9},{9,8},{10,11... | collective-permute-start | bytes 12441608 | tf_op jit(solution)/shard_map/ppermute | solution.py:22
  8.7 99.6 %collective-permute-start.9 = (bf16[2,720,2880]{2,1,0:T(8,128)(2,1)}, bf16[2,720,2880]{2,1,0:T(8,128)(2,1)}, u32[]{:S(2)}, u32[]{:S(2)}) collective-permute-start(bf16[2,720,2880]{2,1,0:T(8,128)(2,1)} %bitcast.29), channel_id=1, source_target_pairs={{0,1},{1,0},{2,3},{3,2},{4,5},{5,4},{6,7},{7,6},{8,9},{9,8},{10,11... | collective-permute-start | bytes 24883208 | tf_op jit(solution)/shard_map/ppermute | solution.py:22
  8.7 50.3 %collective-permute-start.2 = (bf16[720,1024]{1,0:T(8,128)(2,1)}, bf16[720,1024]{1,0:T(8,128)(2,1)}, u32[]{:S(2)}, u32[]{:S(2)}) collective-permute-start(bf16[720,1024]{1,0:T(8,128)(2,1)} %dynamic-slice_bitcast_fusion), channel_id=1, source_target_pairs={{0,4},{4,0},{8,12},{12,8},{1,5},{5,1},{9,13},{13,9},{2,6},{6,2},{1... | collective-permute-start | bytes 4423688 | tf_op jit(solution)/shard_map/ppermute | solution.py:22
  10.9 1.1 copy-start.3
  12.1 1.0 copy-start.4
  13.1 0.8 copy-start.7
  13.9 0.8 copy-start.8
  14.8 0.7 copy-start.9
  15.5 0.7 copy-start.10
  16.2 0.7 copy-start.11
  23.2 34.9 %collective-permute-start.1 = (bf16[2784,128]{1,0:T(8,128)(2,1)}, bf16[2784,128]{1,0:T(8,128)(2,1)}, u32[]{:S(2)}, u32[]{:S(2)}) collective-permute-start(bf16[2784,128]{1,0:T(8,128)(2,1)} %attention.1.refs_0_), channel_id=1, source_target_pairs={{0,8},{4,12},{8,0},{12,4},{1,9},{5,13},{9,1},{13,5},{2,10},{6,14},... | collective-permute-start | bytes 2138120 | tf_op jit(solution)/shard_map/ppermute | solution.py:22
  59.0 3.6 %collective-permute-start.4 = (bf16[720,1024]{1,0:T(8,128)(2,1)}, bf16[720,1024]{1,0:T(8,128)(2,1)}, u32[]{:S(2)}, u32[]{:S(2)}) collective-permute-start(bf16[720,1024]{1,0:T(8,128)(2,1)} %collective-permute-done.2.refs_2_), channel_id=1, source_target_pairs={{0,1},{1,0},{2,3},{3,2},{4,5},{5,4},{6,7},{7,6},{8,9},{9,8},{10,11... | collective-permute-start | bytes 4423688 | tf_op jit(solution)/shard_map/ppermute | solution.py:22
  66.0 10.7 %collective-permute-start.5 = (bf16[1440,128]{1,0:T(8,128)(2,1)S(1)}, bf16[1440,128]{1,0:T(8,128)(2,1)S(1)}, u32[]{:S(2)}, u32[]{:S(2)}) collective-permute-start(bf16[1440,128]{1,0:T(8,128)(2,1)S(1)} %pad_maximum_fusion.1), channel_id=1, source_target_pairs={{0,2},{2,0},{1,3},{3,1},{4,6},{6,4},{5,7},{7,5},{8,10},{10,8},{9,1... | collective-permute-start | bytes 1105928 | tf_op jit(solution)/shard_map/ppermute | solution.py:22
  76.9 20.4 %copy-start.12 = (bf16[1440,128]{1,0:T(8,128)(2,1)}, bf16[1440,128]{1,0:T(8,128)(2,1)S(1)}, u32[]{:S(2)}) copy-start(bf16[1440,128]{1,0:T(8,128)(2,1)S(1)} %fusion.1) | copy-start | bytes 1105924
  77.0 18.9 %collective-permute-start.6 = (bf16[1456,128]{1,0:T(8,128)(2,1)S(1)}, bf16[1456,128]{1,0:T(8,128)(2,1)S(1)}, u32[]{:S(2)}, u32[]{:S(2)}) collective-permute-start(bf16[1456,128]{1,0:T(8,128)(2,1)S(1)} %pad_maximum_fusion.refs_0_), channel_id=1, source_target_pairs={{0,8},{4,12},{8,0},{12,4},{1,9},{5,13},{9,1},{13,5},{2,10},{6,14},... | collective-permute-start | bytes 1118216 | tf_op jit(solution)/shard_map/ppermute | solution.py:22
  79.7 23.5 %collective-permute-start.7 = (bf16[1456,128]{1,0:T(8,128)(2,1)S(1)}, bf16[1456,128]{1,0:T(8,128)(2,1)S(1)}, u32[]{:S(2)}, u32[]{:S(2)}) collective-permute-start(bf16[1456,128]{1,0:T(8,128)(2,1)S(1)} %pad_maximum_fusion.refs_0_), channel_id=1, source_target_pairs={{0,2},{2,0},{1,3},{3,1},{4,6},{6,4},{5,7},{7,5},{8,10},{10,8},{9,1... | collective-permute-start | bytes 1118216 | tf_op jit(solution)/shard_map/ppermute | solution.py:22
  81.3 21.9 %collective-permute-start.11 = (bf16[1456,128]{1,0:T(8,128)(2,1)S(1)}, bf16[1456,128]{1,0:T(8,128)(2,1)S(1)}, u32[]{:S(2)}, u32[]{:S(2)}) collective-permute-start(bf16[1456,128]{1,0:T(8,128)(2,1)S(1)} %pad_maximum_fusion.refs_0_), channel_id=1, source_target_pairs={{0,4},{4,0},{8,12},{12,8},{1,5},{5,1},{9,13},{13,9},{2,6},{6,2},{1... | collective-permute-start | bytes 1118216 | tf_op jit(solution)/shard_map/ppermute | solution.py:22
  95.9 12.4 %collective-permute-start.8 = (bf16[1456,128]{1,0:T(8,128)(2,1)S(1)}, bf16[1456,128]{1,0:T(8,128)(2,1)S(1)}, u32[]{:S(2)}, u32[]{:S(2)}) collective-permute-start(bf16[1456,128]{1,0:T(8,128)(2,1)S(1)} %collective-permute-done.6.refs_1_), channel_id=1, source_target_pairs={{0,2},{2,0},{1,3},{3,1},{4,6},{6,4},{5,7},{7,5},{8,10},{10,8},{9,1... | collective-permute-start | bytes 1118216 | tf_op jit(solution)/shard_map/ppermute | solution.py:22
  97.4 10.4 %collective-permute-start.12 = (bf16[1456,128]{1,0:T(8,128)(2,1)S(1)}, bf16[1456,128]{1,0:T(8,128)(2,1)S(1)}, u32[]{:S(2)}, u32[]{:S(2)}) collective-permute-start(bf16[1456,128]{1,0:T(8,128)(2,1)S(1)} %collective-permute-done.6.refs_1_), channel_id=1, source_target_pairs={{0,4},{4,0},{8,12},{12,8},{1,5},{5,1},{9,13},{13,9},{2,6},{6,2},{1... | collective-permute-start | bytes 1118216 | tf_op jit(solution)/shard_map/ppermute | solution.py:22
  98.2 3.4 %copy-start = (bf16[1,2,2880,720]{2,3,1,0:T(8,128)(2,1)S(1)}, bf16[1,2,2880,720]{2,3,1,0:T(8,128)(2,1)}, u32[]{:S(2)}) copy-start(bf16[1,2,2880,720]{2,3,1,0:T(8,128)(2,1)} %param.18) | copy-start | bytes 24883204
  103.2 14.1 %collective-permute-start.13 = (bf16[1456,128]{1,0:T(8,128)(2,1)S(1)}, bf16[1456,128]{1,0:T(8,128)(2,1)S(1)}, u32[]{:S(2)}, u32[]{:S(2)}) collective-permute-start(bf16[1456,128]{1,0:T(8,128)(2,1)S(1)} %collective-permute-done.7.refs_2_), channel_id=1, source_target_pairs={{0,4},{4,0},{8,12},{12,8},{1,5},{5,1},{9,13},{13,9},{2,6},{6,2},{1... | collective-permute-start | bytes 1118216 | tf_op jit(solution)/shard_map/ppermute | solution.py:22
  107.8 7.9 %copy-start.5 = (bf16[1456,128]{1,0:T(8,128)(2,1)}, bf16[1456,128]{1,0:T(8,128)(2,1)S(1)}, u32[]{:S(2)}) copy-start(bf16[1456,128]{1,0:T(8,128)(2,1)S(1)} %collective-permute-done.12.refs_1_) | copy-start | bytes 1118212
  107.8 9.5 %collective-permute-start.14 = (bf16[1456,128]{1,0:T(8,128)(2,1)S(1)}, bf16[1456,128]{1,0:T(8,128)(2,1)S(1)}, u32[]{:S(2)}, u32[]{:S(2)}) collective-permute-start(bf16[1456,128]{1,0:T(8,128)(2,1)S(1)} %collective-permute-done.12.refs_1_), channel_id=1, source_target_pairs={{0,2},{2,0},{1,3},{3,1},{4,6},{6,4},{5,7},{7,5},{8,10},{10,8},{9,1... | collective-permute-start | bytes 1118216 | tf_op jit(solution)/shard_map/ppermute | solution.py:22
  115.7 19.6 %collective-permute-start.10 = (bf16[2,720,256]{2,1,0:T(8,128)(2,1)S(1)}, bf16[2,720,256]{2,1,0:T(8,128)(2,1)}, u32[]{:S(2)}, u32[]{:S(2)}) collective-permute-start(bf16[2,720,256]{2,1,0:T(8,128)(2,1)S(1)} %get-tuple-element.52.refs_0_), channel_id=1, source_target_pairs={{0,2},{2,0},{1,3},{3,1},{4,6},{6,4},{5,7},{7,5},{8,10},{10,8},{9,1... | collective-permute-start | bytes 2211848 | tf_op jit(solution)/shard_map/ppermute | solution.py:22
  117.3 1.0 copy-start.6
  125.7 21.3 %collective-permute-start.16 = (bf16[2,720,256]{2,1,0:T(8,128)(2,1)S(1)}, bf16[2,720,256]{2,1,0:T(8,128)(2,1)}, u32[]{:S(2)}, u32[]{:S(2)}) collective-permute-start(bf16[2,720,256]{2,1,0:T(8,128)(2,1)S(1)} %get-tuple-element.61.refs_0_), channel_id=1, source_target_pairs={{0,2},{2,0},{1,3},{3,1},{4,6},{6,4},{5,7},{7,5},{8,10},{10,8},{9,1... | collective-permute-start | bytes 2211848 | tf_op jit(solution)/shard_map/ppermute | solution.py:22
  126.4 2.3 %copy-start.2 = (bf16[1,1440,1440]{2,1,0:T(8,128)(2,1)S(1)}, bf16[1,1440,1440]{2,1,0:T(8,128)(2,1)}, u32[]{:S(2)}) copy-start(bf16[1,1440,1440]{2,1,0:T(8,128)(2,1)} %param.19) | copy-start | bytes 12441604
  139.0 17.9 %collective-permute-start.15 = (bf16[1440,128]{1,0:T(8,128)(2,1)S(1)}, bf16[1440,128]{1,0:T(8,128)(2,1)S(1)}, u32[]{:S(2)}, u32[]{:S(2)}) collective-permute-start(bf16[1440,128]{1,0:T(8,128)(2,1)S(1)} %get-tuple-element.67), channel_id=1, source_target_pairs={{0,8},{4,12},{8,0},{12,4},{1,9},{5,13},{9,1},{13,5},{2,10},{6,14},... | collective-permute-start | bytes 1105928 | tf_op jit(solution)/shard_map/ppermute | solution.py:22
  147.1 9.6 %copy-start.13 = (bf16[1440,128]{1,0:T(8,128)(2,1)S(1)}, bf16[1440,128]{1,0:T(8,128)(2,1)}, u32[]{:S(2)}) copy-start(bf16[1440,128]{1,0:T(8,128)(2,1)} %copy-done.12) | copy-start | bytes 1105924
  150.8 14.9 %collective-permute-start.17 = (bf16[1440,128]{1,0:T(8,128)(2,1)S(1)}, bf16[1440,128]{1,0:T(8,128)(2,1)S(1)}, u32[]{:S(2)}, u32[]{:S(2)}) collective-permute-start(bf16[1440,128]{1,0:T(8,128)(2,1)S(1)} %get-tuple-element.69), channel_id=1, source_target_pairs={{0,4},{4,0},{8,12},{12,8},{1,5},{5,1},{9,13},{13,9},{2,6},{6,2},{1... | collective-permute-start | bytes 1105928 | tf_op jit(solution)/shard_map/ppermute | solution.py:22
  153.3 16.9 %collective-permute-start.18 = (bf16[1440,128]{1,0:T(8,128)(2,1)S(1)}, bf16[1440,128]{1,0:T(8,128)(2,1)S(1)}, u32[]{:S(2)}, u32[]{:S(2)}) collective-permute-start(bf16[1440,128]{1,0:T(8,128)(2,1)S(1)} %get-tuple-element.70), channel_id=1, source_target_pairs={{0,12},{4,8},{8,4},{12,0},{1,13},{5,9},{9,5},{13,1},{2,14},{6,10},... | collective-permute-start | bytes 1105928 | tf_op jit(solution)/shard_map/ppermute | solution.py:22

commit v18 on v17

--- a/solution.py
+++ b/solution.py
@@ -136,20 +136,25 @@
     )(place, sink_logits, queries, earlier, key_rows, value_rows, routes, scores, residual)
 
 
-def flip(arrays):
-    def kernel(*refs):
-        for i in range(len(arrays)):
-            refs[len(arrays) + i][...] = refs[i][...].T
-
-    return pl.pallas_call(
+def flip(arrays, t, t_count):
+    units, width = arrays[0].shape[0] // t_count, arrays[0].shape[1]
+    count = len(arrays)
+
+    def kernel(t_ref, *refs):
+        for i in range(count):
+            for u in range(t_count):
+                refs[count + i * t_count + u][...] = refs[i][t_ref[0] ^ u].T
+
+    out = pl.pallas_call(
         kernel,
-        out_shape=tuple(jax.ShapeDtypeStruct(a.shape[::-1], a.dtype) for a in arrays),
-        in_specs=in_vmem(len(arrays)),
-        out_specs=tuple(in_vmem(len(arrays))),
+        out_shape=tuple(jax.ShapeDtypeStruct((width, units), arrays[0].dtype) for _ in range(count * t_count)),
+        in_specs=[in_smem()] + in_vmem(count),
+        out_specs=tuple(in_vmem(count * t_count)),
         compiler_params=params(12),
         cost_estimate=cost(0, 4 * sum(a.size for a in arrays)),
         name="flip",
-    )(*arrays)
+    )(t.reshape(1), *[a.reshape(t_count, units, width) for a in arrays])
+    return [out[i * t_count : (i + 1) * t_count] for i in range(count)]
 
 
 def fetched(weight):
@@ -300,48 +305,52 @@
     )(jnp.stack([pair, t] + chosen).astype(jnp.int32), *flat, gain_table, *weights)
 
 
-def combine(activated, share, weights, t, slots):
-    t_count = len(activated)
+def own_part(activated, weights):
+    experts, units, lanes = activated.shape
+    width = weights[0].shape[0]
+
+    def kernel(activated_ref, *refs):
+        for e in range(experts):
+            refs[experts][e] = dot(refs[e][...], activated_ref[e])
+
+    return pl.pallas_call(
+        kernel,
+        out_shape=jax.ShapeDtypeStruct((experts, width, lanes), jnp.float32),
+        in_specs=in_vmem(1 + experts),
+        out_specs=in_vmem(1)[0],
+        compiler_params=params(7 if aligned(units) else 16),
+        cost_estimate=cost(2 * experts * lanes * units * width, 2 * experts * units * width),
+        name="own_part",
+    )(activated, *weights)
+
+
+def combine(part, activated, share, weights, slots):
+    others = len(activated)
     experts, units, lanes = activated[0].shape
-    width = weights[0].shape[0]
+    width = part.shape[1]
     rows = lanes // slots
 
-    def kernel(t_ref, *refs):
-        activated_refs = refs[:t_count]
-        share_ref = refs[t_count]
-        weight_refs = refs[t_count + 1 : t_count + 1 + experts]
-        *out_refs, all_ref, stage_ref = refs[t_count + 1 + experts :]
-        for u in range(t_count):
-            index = t_ref[0] ^ u
-            if aligned(units):
-                all_ref[:, pl.ds(pl.multiple_of(index * units, 16), units), :] = activated_refs[u][...]
-            else:
-                stage_ref[index] = activated_refs[u][...]
-        if not aligned(units):
-            for index in range(t_count):
-                all_ref[:, index * units : (index + 1) * units, :] = stage_ref[index]
+    def kernel(part_ref, share_ref, *refs):
+        activated_refs, weight_refs = refs[:others], refs[others : others + others * experts]
+        out_refs = refs[others + others * experts :]
         total = 0.0
         for e in range(experts):
-            result = dot(weight_refs[e][...], all_ref[e]).astype(jnp.bfloat16).astype(jnp.float32)
-            total = total + share_ref[e : e + 1, :] * result
+            result = part_ref[e]
+            for u in range(others):
+                result = result + dot(weight_refs[u * experts + e][...], activated_refs[u][e])
+            total = total + share_ref[e : e + 1, :] * result.astype(jnp.bfloat16).astype(jnp.float32)
         for j in range(slots):
             out_refs[j][...] = total[:, j * rows : (j + 1) * rows].astype(jnp.bfloat16)
 
     return pl.pallas_call(
         kernel,
         out_shape=tuple(jax.ShapeDtypeStruct((width, rows), jnp.bfloat16) for _ in range(slots)),
-        in_specs=[in_smem()] + in_vmem(t_count + 1 + experts),
+        in_specs=in_vmem(2 + others + others * experts),
         out_specs=tuple(in_vmem(slots)),
-        scratch_shapes=[
-            pltpu.VMEM((experts, t_count * units, lanes), jnp.bfloat16),
-            pltpu.VMEM((1, 1, 16, 128) if aligned(units) else (t_count, experts, units, lanes), jnp.bfloat16),
-        ],
-        compiler_params=params(7 if aligned(units) else 16),
-        cost_estimate=cost(
-            2 * experts * lanes * t_count * units * width, 2 * experts * t_count * units * width
-        ),
+        compiler_params=params(8 if aligned(units) else 16),
+        cost_estimate=cost(4 * experts * lanes * others * units * width, 4 * experts * others * units * width),
         name="combine",
-    )(t.reshape(1), *activated, share, *weights)
+    )(part, share, *activated, *[w for unit in weights for w in unit])
 
 
 def local(
@@ -466,13 +475,21 @@
         units.append(([activated] + [swapped(activated, "tp", m) for m in range(1, t_count)], share))
 
     experts_out, _ = lax.optimization_barrier((experts_out, units[-1][0][0]))
-    experts_out = flip(experts_out)
+    flipped = flip(experts_out, t, t_count)
+    others = [[weight[u] for weight in flipped] for u in range(1, t_count)]
+    results = None
     for p in range(group):
         activated, share = units[p]
-        for j, result in enumerate(combine(activated, share, experts_out, t, slots)):
+        mine = activated[0]
+        if results is not None:
+            mine, _ = lax.optimization_barrier((mine, results[0]))
+        part = own_part(mine, [weight[0] for weight in flipped])
+        results = combine(part, activated[1:], share, others, slots)
+        for j, result in enumerate(results):
             distance = group * j + p
             result = swapped(result, "ep", distance) if distance else result
             total = total + result.astype(jnp.float32)
+        total = lax.optimization_barrier(total) if p < group - 1 else total
     return total.astype(jnp.bfloat16).T
 
 

time: 172 us -> 173 us (level)
  waiting for transfers between devices: 77.9 us -> 81.5 us
    pallas_call x2, Pallas kernels: 7.44 us -> 2.86 us  [combine(): pl.pallas_call(kernel, out_shape=tuple((jax.ShapeDtypeStruct((width, rows...]
    ppermute x18, waiting for transfers between devices: 77.9 us -> 81.5 us  [swapped(): lax.ppermute(block, axis, [(i, i ^ distance) for i in range(lax.axis_size...]
    pallas_call x1 -> x3, Pallas kernels: 4.73 us -> 7.34 us  [the longest x1 4.73 us: flip(): pl.pallas_call(kernel, out_shape=tuple((jax.ShapeDtypeStruct((width, unit...]
  transfers between devices with their start and end apart: 19 -> 19, of which waited for: 10 -> 9; matrix products, arithmetic and copies ran while one was open for 3% -> 3% of each run, Pallas kernels for 24% -> 23%
where the time goes in v18:
time: 173 us
  waiting for transfers between devices  81.5 us (47%)
  Pallas kernels  39.3 us (23%)
  starting transfers between devices  32.4 us (19%)
  local copies, waits for them, and re-layouts  15.1 us (9%)
  other arithmetic  3.99 us (2%)
    ppermute x18, waiting for transfers between devices, swapped(): lax.ppermute(block, axis, [(i, i ^ distance) for i in range(lax.axis_size...  81.5 us
    ppermute x18, starting transfers between devices, swapped(): lax.ppermute(block, axis, [(i, i ^ distance) for i in range(lax.axis_size...  30.1 us
    pallas_call x2, Pallas kernels, activate(): pl.pallas_call(kernel, out_shape=(jax.ShapeDtypeStruct((experts, units, l...  15.5 us
    unnamed x30, local copies, waits for them, and re-layouts  11.3 us
    pallas_call x1, Pallas kernels, attention(): pl.pallas_call(attention_kernel, out_shape=jax.ShapeDtypeStruct((width +...  6.42 us
    pallas_call x2, Pallas kernels, project(): pl.pallas_call(kernel, out_shape=(jax.ShapeDtypeStruct((columns, rows), j...  5.61 us
    pallas_call x1, Pallas kernels, flip(): pl.pallas_call(kernel, out_shape=tuple((jax.ShapeDtypeStruct((width, unit...  4.73 us
  transfers between devices with their start and end apart: 19, of which 9 were waited for; matrix products, arithmetic and copies ran while one was open for 3% of the time, Pallas kernels for 23%

profile of v18, /device:TPU:0, one launch (start us, length us, event | category | flops | bytes accessed | tf_op | source)
XLA Modules:
  0.0 172.6 jit_solution(15607850937052451556)
XLA Ops:
  0.0 1.0 pad_maximum_fusion.2
  1.1 2.4 %collective-permute-start = (bf16[128,512]{1,0:T(8,128)(2,1)S(1)}, bf16[128,512]{1,0:T(8,128)(2,1)S(1)}, u32[]{:S(2)}, u32[]{:S(2)}) collective-permute-start(bf16[128,512]{1,0:T(8,128)(2,1)S(1)} %pad_maximum_fusion.2), channel_id=1, source_target_pairs={{0,1},{1,4},{4,5},{5,8},{8,9},{9,12},{12,13},{2,3},{3,6},{6,7},{7,... | collective-permute-start | bytes 393224 | tf_op jit(solution)/shard_map/ppermute | solution.py:18
  3.5 2.6 %dynamic-slice_bitcast_fusion = bf16[720,1024]{1,0:T(8,128)(2,1)} fusion(bf16[2048,720]{0,1:T(8,128)(2,1)} %param.15, s32[]{:T(128)S(6)} %select_n.95), kind=kLoop, calls=%fused_computation | loop fusion | bytes 2949124 | tf_op jit(solution)/shard_map/dynamic_slice | solution.py:382
  6.1 2.7 %collective-permute-start.3 = (bf16[1440,1440]{1,0:T(8,128)(2,1)}, bf16[1440,1440]{1,0:T(8,128)(2,1)}, u32[]{:S(2)}, u32[]{:S(2)}) collective-permute-start(bf16[1440,1440]{1,0:T(8,128)(2,1)} %bitcast.34), channel_id=1, source_target_pairs={{0,1},{1,0},{2,3},{3,2},{4,5},{5,4},{6,7},{7,6},{8,9},{9,8},{10,11... | collective-permute-start | bytes 12441608 | tf_op jit(solution)/shard_map/ppermute | solution.py:22
  8.8 2.1 %collective-permute-start.2 = (bf16[720,1024]{1,0:T(8,128)(2,1)}, bf16[720,1024]{1,0:T(8,128)(2,1)}, u32[]{:S(2)}, u32[]{:S(2)}) collective-permute-start(bf16[720,1024]{1,0:T(8,128)(2,1)} %dynamic-slice_bitcast_fusion), channel_id=1, source_target_pairs={{0,4},{4,0},{8,12},{12,8},{1,5},{5,1},{9,13},{13,9},{2,6},{6,2},{1... | collective-permute-start | bytes 4423688 | tf_op jit(solution)/shard_map/ppermute | solution.py:22
  11.0 1.1 copy-done.5
  12.1 1.0 copy-done.6
  13.2 6.4 %attention.1.refs_0_ = bf16[2784,128]{1,0:T(8,128)(2,1)} custom-call(s32[2]{0:T(128)S(1)} %pad_add_fusion.1.place_ref, f32[32]{0:T(128)S(1)} %copy-done.11, bf16[128,2048]{1,0:T(8,128)(2,1)S(1)} %copy-done.6, bf16[128,512]{1,0:T(8,128)(2,1)S(1)} %collective-permute-done.earlier_ref, bf16[128,256]{1,0:T(8,128)(2,1)S(1)} %copy-done.8, ...), custom_call_target="tpu_custom_call" | custom-call | flops 268435456 | bytes 1572864 | tf_op jit(solution)/shard_map/attention/pallas_call | solution.py:128
  19.6 2.6 %collective-permute-start.1 = (bf16[2784,128]{1,0:T(8,128)(2,1)}, bf16[2784,128]{1,0:T(8,128)(2,1)}, u32[]{:S(2)}, u32[]{:S(2)}) collective-permute-start(bf16[2784,128]{1,0:T(8,128)(2,1)} %attention.1.refs_0_), channel_id=1, source_target_pairs={{0,8},{4,12},{8,0},{12,4},{1,9},{5,13},{9,1},{13,5},{2,10},{6,14},... | collective-permute-start | bytes 2138120 | tf_op jit(solution)/shard_map/ppermute | solution.py:22
  22.2 0.9 dynamic-slice_bitcast_fusion.1.refs_3_.refs_4_
  23.1 35.1 %collective-permute-done.1.refs_1_ = bf16[2784,128]{1,0:T(8,128)(2,1)} collective-permute-done((bf16[2784,128]{1,0:T(8,128)(2,1)}, bf16[2784,128]{1,0:T(8,128)(2,1)}, u32[]{:S(2)}, u32[]{:S(2)}) %collective-permute-start.1) | collective-permute-done | bytes 712736 | tf_op jit(solution)/shard_map/ppermute | solution.py:22
  58.2 0.8 collective-permute-done.2.refs_2_
  59.3 2.4 %project.2 = (f32[720,128]{1,0:T(8,128)S(1)}, bf16[1,720,128]{2,1,0:T(8,128)(2,1)S(1)}) custom-call(s32[3]{0:T(128)S(1)} %pad_add_fusion.place_ref, bf16[2784,128]{1,0:T(8,128)(2,1)} %attention.1.refs_0_, bf16[2784,128]{1,0:T(8,128)(2,1)} %collective-permute-done.1.refs_1_, bf16[720,2048]{1,0:T(8,128)(2,1)S(1)} %bitcast.33, ...), custom_call_target="tpu_custom_call" | custom-call | flops 754974720 | bytes 2949120 | tf_op jit(solution)/shard_map/project/pallas_call | solution.py:215
  61.7 1.0 collective-permute-done.4.refs_3_
  62.7 3.2 %project.3 = (f32[720,128]{1,0:T(8,128)S(1)}, bf16[1,720,128]{2,1,0:T(8,128)(2,1)S(1)}) custom-call(s32[3]{0:T(128)S(1)} %pad_add_fusion.2.place_ref, bf16[2784,128]{1,0:T(8,128)(2,1)} %attention.1.refs_0_, bf16[2784,128]{1,0:T(8,128)(2,1)} %collective-permute-done.1.refs_1_, bf16[720,1024]{1,0:T(8,128)(2,1)} %collective-permute-done.2.refs_2_, ...), custom_call_target="tpu_custom_call" | custom-call | flops 754974720 | bytes 2949120 | tf_op jit(solution)/shard_map/project/pallas_call | solution.py:215
  66.0 1.6 collective-permute-start.5
  67.6 0.7 slice_select_fusion
  68.3 8.4 %collective-permute-done.5 = bf16[1440,128]{1,0:T(8,128)(2,1)S(1)} collective-permute-done((bf16[1440,128]{1,0:T(8,128)(2,1)S(1)}, bf16[1440,128]{1,0:T(8,128)(2,1)S(1)}, u32[]{:S(2)}, u32[]{:S(2)}) %collective-permute-start.5) | collective-permute-done | bytes 368672 | tf_op jit(solution)/shard_map/ppermute | solution.py:22
  77.0 2.6 %collective-permute-start.6 = (bf16[1456,128]{1,0:T(8,128)(2,1)S(1)}, bf16[1456,128]{1,0:T(8,128)(2,1)S(1)}, u32[]{:S(2)}, u32[]{:S(2)}) collective-permute-start(bf16[1456,128]{1,0:T(8,128)(2,1)S(1)} %pad_maximum_fusion.refs_0_), channel_id=1, source_target_pairs={{0,8},{4,12},{8,0},{12,4},{1,9},{5,13},{9,1},{13,5},{2,10},{6,14},... | collective-permute-start | bytes 1118216 | tf_op jit(solution)/shard_map/ppermute | solution.py:22
  79.7 1.5 collective-permute-start.7
  81.3 1.6 collective-permute-start.10
  82.9 13.0 %collective-permute-done.6.refs_1_ = bf16[1456,128]{1,0:T(8,128)(2,1)S(1)} collective-permute-done((bf16[1456,128]{1,0:T(8,128)(2,1)S(1)}, bf16[1456,128]{1,0:T(8,128)(2,1)S(1)}, u32[]{:S(2)}, u32[]{:S(2)}) %collective-permute-start.6) | collective-permute-done | bytes 372768 | tf_op jit(solution)/shard_map/ppermute | solution.py:22
  96.0 1.4 collective-permute-start.8
  97.4 0.7 collective-permute-start.11
  98.2 3.4 %copy-done.2 = bf16[1,2,2880,720]{2,3,1,0:T(8,128)(2,1)S(1)} copy-done((bf16[1,2,2880,720]{2,3,1,0:T(8,128)(2,1)S(1)}, bf16[1,2,2880,720]{2,3,1,0:T(8,128)(2,1)}, u32[]{:S(2)}) %copy-start.2) | copy-done | bytes 8294424
  101.6 1.6 fetched.1.refs_5_
  103.2 1.4 collective-permute-start.12
  104.7 3.3 %collective-permute-done.11.refs_1_ = bf16[1456,128]{1,0:T(8,128)(2,1)} collective-permute-done((bf16[1456,128]{1,0:T(8,128)(2,1)S(1)}, bf16[1456,128]{1,0:T(8,128)(2,1)}, u32[]{:S(2)}, u32[]{:S(2)}) %collective-permute-start.11) | collective-permute-done | bytes 372768 | tf_op jit(solution)/shard_map/ppermute | solution.py:22
  107.9 0.5 collective-permute-start.13
  108.4 7.4 %activate.2 = (bf16[2,720,256]{2,1,0:T(8,128)(2,1)S(1)}, f32[2,256]{1,0:T(2,128)S(1)}) custom-call(s32[4]{0:T(128)S(1)} %pad_add_fusion.3.place_ref, bf16[1456,128]{1,0:T(8,128)(2,1)S(1)} %pad_maximum_fusion.refs_0_, bf16[1456,128]{1,0:T(8,128)(2,1)S(1)} %collective-permute-done.6.refs_1_, bf16[1456,128]{1,0:T(8,128)(2,1)S(1)} %collective-permute-done.7.refs_2_, ...), custom_call_target="tpu_custom_call" | custom-call | flops 4246732800 | bytes 16588800 | tf_op jit(solution)/shard_map/activate/pallas_call | solution.py:285
  115.8 1.6 collective-permute-start.14
  117.5 3.4 %copy-done.1 = bf16[2,720,2880]{2,1,0:T(8,128)(2,1)S(1)} copy-done((bf16[2,720,2880]{2,1,0:T(8,128)(2,1)S(1)}, bf16[2,720,2880]{2,1,0:T(8,128)(2,1)}, u32[]{:S(2)}) %copy-start.1) | copy-done | bytes 8294424
  121.0 8.1 %activate.3 = (bf16[2,720,256]{2,1,0:T(8,128)(2,1)S(1)}, f32[2,256]{1,0:T(2,128)S(1)}) custom-call(s32[4]{0:T(128)S(1)} %pad_add_fusion.3.place_ref, bf16[1456,128]{1,0:T(8,128)(2,1)S(1)} %collective-permute-done.10.refs_0_, bf16[1456,128]{1,0:T(8,128)(2,1)} %collective-permute-done.11.refs_1_, bf16[1456,128]{1,0:T(8,128)(2,1)} %collective-permute-done.12.refs_2_, ...), custom_call_target="tpu_custom_call" | custom-call | flops 4246732800 | bytes 16588800 | tf_op jit(solution)/shard_map/activate/pallas_call | solution.py:285
  129.1 0.5 collective-permute-start.16
  129.6 2.3 %copy-done.4 = bf16[1,1440,1440]{2,1,0:T(8,128)(2,1)S(1)} copy-done((bf16[1,1440,1440]{2,1,0:T(8,128)(2,1)S(1)}, bf16[1,1440,1440]{2,1,0:T(8,128)(2,1)}, u32[]{:S(2)}) %copy-start.4) | copy-done | bytes 4147224
  131.9 4.7 %flip.1 = (bf16[1440,720]{1,0:T(8,128)(2,1)S(1)}, bf16[1440,720]{1,0:T(8,128)(2,1)S(1)}, bf16[1440,720]{1,0:T(8,128)(2,1)S(1)}, bf16[1440,720]{1,0:T(8,128)(2,1)S(1)}) custom-call(s32[1]{0:T(128)} %bitcast.t_ref, bf16[2,720,1440]{2,1,0:T(8,128)(2,1)S(1)} %bitcast.35, bf16[2,720,1440]{2,1,0:T(8,128)(2,1)} %bitcast.24.refs_1_), custom_call_target="tpu_custom_call" | custom-call | bytes 16588800 | tf_op jit(solution)/shard_map/flip/pallas_call | solution.py:148
  136.6 1.3 own_part.2.part_ref
  137.9 1.4 combine.2
  139.4 3.2 %collective-permute-start.15 = (bf16[1440,128]{1,0:T(8,128)(2,1)S(1)}, bf16[1440,128]{1,0:T(8,128)(2,1)S(1)}, u32[]{:S(2)}, u32[]{:S(2)}) collective-permute-start(bf16[1440,128]{1,0:T(8,128)(2,1)S(1)} %get-tuple-element.72), channel_id=1, source_target_pairs={{0,8},{4,12},{8,0},{12,4},{1,9},{5,13},{9,1},{13,5},{2,10},{6,14},... | collective-permute-start | bytes 1105928 | tf_op jit(solution)/shard_map/ppermute | solution.py:22
  142.6 0.5 add_multiply_fusion
  143.1 1.3 own_part.3.part_ref
  144.4 2.9 %collective-permute-done.16.refs_0_ = bf16[2,720,256]{2,1,0:T(8,128)(2,1)S(1)} collective-permute-done((bf16[2,720,256]{2,1,0:T(8,128)(2,1)S(1)}, bf16[2,720,256]{2,1,0:T(8,128)(2,1)S(1)}, u32[]{:S(2)}, u32[]{:S(2)}) %collective-permute-start.16) | collective-permute-done | bytes 737312 | tf_op jit(solution)/shard_map/ppermute | solution.py:22
  147.3 1.4 combine.3
  148.8 2.5 %collective-permute-start.17 = (bf16[1440,128]{1,0:T(8,128)(2,1)S(1)}, bf16[1440,128]{1,0:T(8,128)(2,1)S(1)}, u32[]{:S(2)}, u32[]{:S(2)}) collective-permute-start(bf16[1440,128]{1,0:T(8,128)(2,1)S(1)} %get-tuple-element.75), channel_id=1, source_target_pairs={{0,4},{4,0},{8,12},{12,8},{1,5},{5,1},{9,13},{13,9},{2,6},{6,2},{1... | collective-permute-start | bytes 1105928 | tf_op jit(solution)/shard_map/ppermute | solution.py:22
  151.2 3.3 %collective-permute-start.18 = (bf16[1440,128]{1,0:T(8,128)(2,1)S(1)}, bf16[1440,128]{1,0:T(8,128)(2,1)S(1)}, u32[]{:S(2)}, u32[]{:S(2)}) collective-permute-start(bf16[1440,128]{1,0:T(8,128)(2,1)S(1)} %get-tuple-element.76), channel_id=1, source_target_pairs={{0,12},{4,8},{8,4},{12,0},{1,13},{5,9},{9,5},{13,1},{2,14},{6,10},... | collective-permute-start | bytes 1105928 | tf_op jit(solution)/shard_map/ppermute | solution.py:22
  154.6 3.8 %collective-permute-done.15 = bf16[1440,128]{1,0:T(8,128)(2,1)S(1)} collective-permute-done((bf16[1440,128]{1,0:T(8,128)(2,1)S(1)}, bf16[1440,128]{1,0:T(8,128)(2,1)S(1)}, u32[]{:S(2)}, u32[]{:S(2)}) %collective-permute-start.15) | collective-permute-done | bytes 368672 | tf_op jit(solution)/shard_map/ppermute | solution.py:22
  158.5 13.2 %collective-permute-done.17 = bf16[1440,128]{1,0:T(8,128)(2,1)S(1)} collective-permute-done((bf16[1440,128]{1,0:T(8,128)(2,1)S(1)}, bf16[1440,128]{1,0:T(8,128)(2,1)S(1)}, u32[]{:S(2)}, u32[]{:S(2)}) %collective-permute-start.17) | collective-permute-done | bytes 368672 | tf_op jit(solution)/shard_map/ppermute | solution.py:22
  171.7 0.9 fusion.2
  (56 shorter events, 1.3 us)
Async XLA Ops:
  0.0 11.0 %copy-start.8 = (bf16[128,256]{1,0:T(8,128)(2,1)S(1)}, bf16[128,256]{1,0:T(8,128)(2,1)}, u32[]{:S(2)}) copy-start(bf16[128,256]{1,0:T(8,128)(2,1)} %k_ref.1) | copy-start | bytes 196612
  0.0 11.0 %copy-start.7 = (bf16[128,256]{1,0:T(8,128)(2,1)S(1)}, bf16[128,256]{1,0:T(8,128)(2,1)}, u32[]{:S(2)}) copy-start(bf16[128,256]{1,0:T(8,128)(2,1)} %v_ref.1) | copy-start | bytes 196612
  0.0 59.3 %copy-start.3 = (bf16[2048,720]{0,1:T(8,128)(2,1)S(1)}, bf16[2048,720]{0,1:T(8,128)(2,1)}, u32[]{:S(2)}) copy-start(bf16[2048,720]{0,1:T(8,128)(2,1)} %param.15) | copy-start | bytes 8847364
  0.0 11.0 %copy-start.9 = (s32[128,4]{0,1:T(4,128)S(1)}, s32[128,4]{0,1:T(4,128)}, u32[]{:S(2)}) copy-start(s32[128,4]{0,1:T(4,128)} %param.20) | copy-start | bytes 6148
  0.0 11.0 %copy-start.10 = (s32[128,4]{0,1:T(4,128)S(1)}, s32[128,4]{0,1:T(4,128)}, u32[]{:S(2)}) copy-start(s32[128,4]{0,1:T(4,128)} %param.21) | copy-start | bytes 6148
  0.0 11.0 %copy-start.11 = (f32[32]{0:T(128)S(1)}, f32[32]{0:T(128)}, u32[]{:S(2)}) copy-start(f32[32]{0:T(128)} %sink_ref.1) | copy-start | bytes 388
  0.0 59.0 %copy-start.14 = (f32[2880]{0:T(1024)S(1)}, f32[2880]{0:T(1024)}, u32[]{:S(2)}) copy-start(f32[2880]{0:T(1024)} %param.17) | copy-start | bytes 34564
  1.1 5.0 %collective-permute-start = (bf16[128,512]{1,0:T(8,128)(2,1)S(1)}, bf16[128,512]{1,0:T(8,128)(2,1)S(1)}, u32[]{:S(2)}, u32[]{:S(2)}) collective-permute-start(bf16[128,512]{1,0:T(8,128)(2,1)S(1)} %pad_maximum_fusion.2), channel_id=1, source_target_pairs={{0,1},{1,4},{4,5},{5,8},{8,9},{9,12},{12,13},{2,3},{3,6},{6,7},{7,... | collective-permute-start | bytes 393224 | tf_op jit(solution)/shard_map/ppermute | solution.py:18
  6.1 53.0 %collective-permute-start.3 = (bf16[1440,1440]{1,0:T(8,128)(2,1)}, bf16[1440,1440]{1,0:T(8,128)(2,1)}, u32[]{:S(2)}, u32[]{:S(2)}) collective-permute-start(bf16[1440,1440]{1,0:T(8,128)(2,1)} %bitcast.34), channel_id=1, source_target_pairs={{0,1},{1,0},{2,3},{3,2},{4,5},{5,4},{6,7},{7,6},{8,9},{9,8},{10,11... | collective-permute-start | bytes 12441608 | tf_op jit(solution)/shard_map/ppermute | solution.py:22
  8.8 99.7 %collective-permute-start.9 = (bf16[2,720,2880]{2,1,0:T(8,128)(2,1)}, bf16[2,720,2880]{2,1,0:T(8,128)(2,1)}, u32[]{:S(2)}, u32[]{:S(2)}) collective-permute-start(bf16[2,720,2880]{2,1,0:T(8,128)(2,1)} %bitcast.31), channel_id=1, source_target_pairs={{0,1},{1,0},{2,3},{3,2},{4,5},{5,4},{6,7},{7,6},{8,9},{9,8},{10,11... | collective-permute-start | bytes 24883208 | tf_op jit(solution)/shard_map/ppermute | solution.py:22
  8.8 50.3 %collective-permute-start.2 = (bf16[720,1024]{1,0:T(8,128)(2,1)}, bf16[720,1024]{1,0:T(8,128)(2,1)}, u32[]{:S(2)}, u32[]{:S(2)}) collective-permute-start(bf16[720,1024]{1,0:T(8,128)(2,1)} %dynamic-slice_bitcast_fusion), channel_id=1, source_target_pairs={{0,4},{4,0},{8,12},{12,8},{1,5},{5,1},{9,13},{13,9},{2,6},{6,2},{1... | collective-permute-start | bytes 4423688 | tf_op jit(solution)/shard_map/ppermute | solution.py:22
  11.0 1.1 copy-start.5
  12.1 1.0 copy-start.6
  19.6 38.6 %collective-permute-start.1 = (bf16[2784,128]{1,0:T(8,128)(2,1)}, bf16[2784,128]{1,0:T(8,128)(2,1)}, u32[]{:S(2)}, u32[]{:S(2)}) collective-permute-start(bf16[2784,128]{1,0:T(8,128)(2,1)} %attention.1.refs_0_), channel_id=1, source_target_pairs={{0,8},{4,12},{8,0},{12,4},{1,9},{5,13},{9,1},{13,5},{2,10},{6,14},... | collective-permute-start | bytes 2138120 | tf_op jit(solution)/shard_map/ppermute | solution.py:22
  59.1 3.6 %collective-permute-start.4 = (bf16[720,1024]{1,0:T(8,128)(2,1)}, bf16[720,1024]{1,0:T(8,128)(2,1)}, u32[]{:S(2)}, u32[]{:S(2)}) collective-permute-start(bf16[720,1024]{1,0:T(8,128)(2,1)} %collective-permute-done.2.refs_2_), channel_id=1, source_target_pairs={{0,1},{1,0},{2,3},{3,2},{4,5},{5,4},{6,7},{7,6},{8,9},{9,8},{10,11... | collective-permute-start | bytes 4423688 | tf_op jit(solution)/shard_map/ppermute | solution.py:22
  66.0 10.7 %collective-permute-start.5 = (bf16[1440,128]{1,0:T(8,128)(2,1)S(1)}, bf16[1440,128]{1,0:T(8,128)(2,1)S(1)}, u32[]{:S(2)}, u32[]{:S(2)}) collective-permute-start(bf16[1440,128]{1,0:T(8,128)(2,1)S(1)} %pad_maximum_fusion.1), channel_id=1, source_target_pairs={{0,2},{2,0},{1,3},{3,1},{4,6},{6,4},{5,7},{7,5},{8,10},{10,8},{9,1... | collective-permute-start | bytes 1105928 | tf_op jit(solution)/shard_map/ppermute | solution.py:22
  77.0 20.4 %copy-start.12 = (bf16[1440,128]{1,0:T(8,128)(2,1)}, bf16[1440,128]{1,0:T(8,128)(2,1)S(1)}, u32[]{:S(2)}) copy-start(bf16[1440,128]{1,0:T(8,128)(2,1)S(1)} %fusion.1) | copy-start | bytes 1105924
  77.0 18.9 %collective-permute-start.6 = (bf16[1456,128]{1,0:T(8,128)(2,1)S(1)}, bf16[1456,128]{1,0:T(8,128)(2,1)S(1)}, u32[]{:S(2)}, u32[]{:S(2)}) collective-permute-start(bf16[1456,128]{1,0:T(8,128)(2,1)S(1)} %pad_maximum_fusion.refs_0_), channel_id=1, source_target_pairs={{0,8},{4,12},{8,0},{12,4},{1,9},{5,13},{9,1},{13,5},{2,10},{6,14},... | collective-permute-start | bytes 1118216 | tf_op jit(solution)/shard_map/ppermute | solution.py:22
  79.7 23.5 %collective-permute-start.7 = (bf16[1456,128]{1,0:T(8,128)(2,1)S(1)}, bf16[1456,128]{1,0:T(8,128)(2,1)S(1)}, u32[]{:S(2)}, u32[]{:S(2)}) collective-permute-start(bf16[1456,128]{1,0:T(8,128)(2,1)S(1)} %pad_maximum_fusion.refs_0_), channel_id=1, source_target_pairs={{0,2},{2,0},{1,3},{3,1},{4,6},{6,4},{5,7},{7,5},{8,10},{10,8},{9,1... | collective-permute-start | bytes 1118216 | tf_op jit(solution)/shard_map/ppermute | solution.py:22
  81.3 21.9 %collective-permute-start.10 = (bf16[1456,128]{1,0:T(8,128)(2,1)S(1)}, bf16[1456,128]{1,0:T(8,128)(2,1)S(1)}, u32[]{:S(2)}, u32[]{:S(2)}) collective-permute-start(bf16[1456,128]{1,0:T(8,128)(2,1)S(1)} %pad_maximum_fusion.refs_0_), channel_id=1, source_target_pairs={{0,4},{4,0},{8,12},{12,8},{1,5},{5,1},{9,13},{13,9},{2,6},{6,2},{1... | collective-permute-start | bytes 1118216 | tf_op jit(solution)/shard_map/ppermute | solution.py:22
  96.0 12.5 %collective-permute-start.8 = (bf16[1456,128]{1,0:T(8,128)(2,1)S(1)}, bf16[1456,128]{1,0:T(8,128)(2,1)S(1)}, u32[]{:S(2)}, u32[]{:S(2)}) collective-permute-start(bf16[1456,128]{1,0:T(8,128)(2,1)S(1)} %collective-permute-done.6.refs_1_), channel_id=1, source_target_pairs={{0,2},{2,0},{1,3},{3,1},{4,6},{6,4},{5,7},{7,5},{8,10},{10,8},{9,1... | collective-permute-start | bytes 1118216 | tf_op jit(solution)/shard_map/ppermute | solution.py:22
  97.4 10.6 %collective-permute-start.11 = (bf16[1456,128]{1,0:T(8,128)(2,1)S(1)}, bf16[1456,128]{1,0:T(8,128)(2,1)}, u32[]{:S(2)}, u32[]{:S(2)}) collective-permute-start(bf16[1456,128]{1,0:T(8,128)(2,1)S(1)} %collective-permute-done.6.refs_1_), channel_id=1, source_target_pairs={{0,4},{4,0},{8,12},{12,8},{1,5},{5,1},{9,13},{13,9},{2,6},{6,2},{1... | collective-permute-start | bytes 1118216 | tf_op jit(solution)/shard_map/ppermute | solution.py:22
  98.2 3.4 %copy-start.2 = (bf16[1,2,2880,720]{2,3,1,0:T(8,128)(2,1)S(1)}, bf16[1,2,2880,720]{2,3,1,0:T(8,128)(2,1)}, u32[]{:S(2)}) copy-start(bf16[1,2,2880,720]{2,3,1,0:T(8,128)(2,1)} %param.18) | copy-start | bytes 24883204
  103.2 12.6 %copy-start = (bf16[2,720,2880]{2,1,0:T(8,128)(2,1)}, bf16[2,720,2880]{2,1,0:T(8,128)(2,1)S(1)}, u32[]{:S(2)}) copy-start(bf16[2,720,2880]{2,1,0:T(8,128)(2,1)S(1)} %fetched.1.refs_5_) | copy-start | bytes 24883204
  103.2 14.3 %collective-permute-start.12 = (bf16[1456,128]{1,0:T(8,128)(2,1)S(1)}, bf16[1456,128]{1,0:T(8,128)(2,1)}, u32[]{:S(2)}, u32[]{:S(2)}) collective-permute-start(bf16[1456,128]{1,0:T(8,128)(2,1)S(1)} %collective-permute-done.7.refs_2_), channel_id=1, source_target_pairs={{0,4},{4,0},{8,12},{12,8},{1,5},{5,1},{9,13},{13,9},{2,6},{6,2},{1... | collective-permute-start | bytes 1118216 | tf_op jit(solution)/shard_map/ppermute | solution.py:22
  107.9 9.6 %collective-permute-start.13 = (bf16[1456,128]{1,0:T(8,128)(2,1)}, bf16[1456,128]{1,0:T(8,128)(2,1)}, u32[]{:S(2)}, u32[]{:S(2)}) collective-permute-start(bf16[1456,128]{1,0:T(8,128)(2,1)} %collective-permute-done.11.refs_1_), channel_id=1, source_target_pairs={{0,2},{2,0},{1,3},{3,1},{4,6},{6,4},{5,7},{7,5},{8,10},{10,8},{9,1... | collective-permute-start | bytes 1118216 | tf_op jit(solution)/shard_map/ppermute | solution.py:22
  115.8 22.1 %collective-permute-start.14 = (bf16[2,720,256]{2,1,0:T(8,128)(2,1)S(1)}, bf16[2,720,256]{2,1,0:T(8,128)(2,1)S(1)}, u32[]{:S(2)}, u32[]{:S(2)}) collective-permute-start(bf16[2,720,256]{2,1,0:T(8,128)(2,1)S(1)} %get-tuple-element.55.activated_ref), channel_id=1, source_target_pairs={{0,2},{2,0},{1,3},{3,1},{4,6},{6,4},{5,7},{7,5},{8,10},{10,8},{9,1... | collective-permute-start | bytes 2211848 | tf_op jit(solution)/shard_map/ppermute | solution.py:22
  117.5 3.4 %copy-start.1 = (bf16[2,720,2880]{2,1,0:T(8,128)(2,1)S(1)}, bf16[2,720,2880]{2,1,0:T(8,128)(2,1)}, u32[]{:S(2)}) copy-start(bf16[2,720,2880]{2,1,0:T(8,128)(2,1)} %copy-done) | copy-start | bytes 24883204
  129.1 18.3 %collective-permute-start.16 = (bf16[2,720,256]{2,1,0:T(8,128)(2,1)S(1)}, bf16[2,720,256]{2,1,0:T(8,128)(2,1)S(1)}, u32[]{:S(2)}, u32[]{:S(2)}) collective-permute-start(bf16[2,720,256]{2,1,0:T(8,128)(2,1)S(1)} %get-tuple-element.73.activated_ref), channel_id=1, source_target_pairs={{0,2},{2,0},{1,3},{3,1},{4,6},{6,4},{5,7},{7,5},{8,10},{10,8},{9,1... | collective-permute-start | bytes 2211848 | tf_op jit(solution)/shard_map/ppermute | solution.py:22
  129.6 2.3 %copy-start.4 = (bf16[1,1440,1440]{2,1,0:T(8,128)(2,1)S(1)}, bf16[1,1440,1440]{2,1,0:T(8,128)(2,1)}, u32[]{:S(2)}) copy-start(bf16[1,1440,1440]{2,1,0:T(8,128)(2,1)} %param.19) | copy-start | bytes 12441604
  137.9 4.7 %copy-start.13 = (bf16[1440,128]{1,0:T(8,128)(2,1)S(1)}, bf16[1440,128]{1,0:T(8,128)(2,1)}, u32[]{:S(2)}) copy-start(bf16[1440,128]{1,0:T(8,128)(2,1)} %copy-done.12) | copy-start | bytes 1105924
  139.4 19.0 %collective-permute-start.15 = (bf16[1440,128]{1,0:T(8,128)(2,1)S(1)}, bf16[1440,128]{1,0:T(8,128)(2,1)S(1)}, u32[]{:S(2)}, u32[]{:S(2)}) collective-permute-start(bf16[1440,128]{1,0:T(8,128)(2,1)S(1)} %get-tuple-element.72), channel_id=1, source_target_pairs={{0,8},{4,12},{8,0},{12,4},{1,9},{5,13},{9,1},{13,5},{2,10},{6,14},... | collective-permute-start | bytes 1105928 | tf_op jit(solution)/shard_map/ppermute | solution.py:22
  148.8 22.9 %collective-permute-start.17 = (bf16[1440,128]{1,0:T(8,128)(2,1)S(1)}, bf16[1440,128]{1,0:T(8,128)(2,1)S(1)}, u32[]{:S(2)}, u32[]{:S(2)}) collective-permute-start(bf16[1440,128]{1,0:T(8,128)(2,1)S(1)} %get-tuple-element.75), channel_id=1, source_target_pairs={{0,4},{4,0},{8,12},{12,8},{1,5},{5,1},{9,13},{13,9},{2,6},{6,2},{1... | collective-permute-start | bytes 1105928 | tf_op jit(solution)/shard_map/ppermute | solution.py:22
  151.2 20.5 %collective-permute-start.18 = (bf16[1440,128]{1,0:T(8,128)(2,1)S(1)}, bf16[1440,128]{1,0:T(8,128)(2,1)S(1)}, u32[]{:S(2)}, u32[]{:S(2)}) collective-permute-start(bf16[1440,128]{1,0:T(8,128)(2,1)S(1)} %get-tuple-element.76), channel_id=1, source_target_pairs={{0,12},{4,8},{8,4},{12,0},{1,13},{5,9},{9,5},{13,1},{2,14},{6,10},... | collective-permute-start | bytes 1105928 | tf_op jit(solution)/shard_map/ppermute | solution.py:22

commit v19 on v18

--- a/solution.py
+++ b/solution.py
@@ -150,7 +150,7 @@
         out_shape=tuple(jax.ShapeDtypeStruct((width, units), arrays[0].dtype) for _ in range(count * t_count)),
         in_specs=[in_smem()] + in_vmem(count),
         out_specs=tuple(in_vmem(count * t_count)),
-        compiler_params=params(12),
+        compiler_params=params(8),
         cost_estimate=cost(0, 4 * sum(a.size for a in arrays)),
         name="flip",
     )(t.reshape(1), *[a.reshape(t_count, units, width) for a in arrays])
@@ -299,7 +299,7 @@
             pltpu.VMEM((max(1, experts - 1), 2, units, D), jnp.bfloat16),
             pltpu.SemaphoreType.DMA((max(1, experts - 1), len(cuts))),
         ],
-        compiler_params=params(13 if aligned(depth) else 16),
+        compiler_params=params(12 if aligned(depth) else 16),
         cost_estimate=cost(4 * experts * lanes * D * units, 4 * experts * D * units),
         name="activate",
     )(jnp.stack([pair, t] + chosen).astype(jnp.int32), *flat, gain_table, *weights)
@@ -318,7 +318,7 @@
         out_shape=jax.ShapeDtypeStruct((experts, width, lanes), jnp.float32),
         in_specs=in_vmem(1 + experts),
         out_specs=in_vmem(1)[0],
-        compiler_params=params(7 if aligned(units) else 16),
+        compiler_params=params(4 if aligned(units) else 16),
         cost_estimate=cost(2 * experts * lanes * units * width, 2 * experts * units * width),
         name="own_part",
     )(activated, *weights)
@@ -347,7 +347,7 @@
         out_shape=tuple(jax.ShapeDtypeStruct((width, rows), jnp.bfloat16) for _ in range(slots)),
         in_specs=in_vmem(2 + others + others * experts),
         out_specs=tuple(in_vmem(slots)),
-        compiler_params=params(8 if aligned(units) else 16),
+        compiler_params=params(6 if aligned(units) else 16),
         cost_estimate=cost(4 * experts * lanes * others * units * width, 4 * experts * others * units * width),
         name="combine",
     )(part, share, *activated, *[w for unit in weights for w in unit])

time: 173 us -> 173 us (level)
  no operation moved by 1% of the time
where the time goes in v19:
time: 173 us
  waiting for transfers between devices  81.5 us (47%)
  Pallas kernels  39.3 us (23%)
  starting transfers between devices  32.4 us (19%)
  local copies, waits for them, and re-layouts  15.1 us (9%)
  other arithmetic  3.99 us (2%)
    ppermute x18, waiting for transfers between devices, swapped(): lax.ppermute(block, axis, [(i, i ^ distance) for i in range(lax.axis_size...  81.4 us
    ppermute x18, starting transfers between devices, swapped(): lax.ppermute(block, axis, [(i, i ^ distance) for i in range(lax.axis_size...  30.1 us
    pallas_call x2, Pallas kernels, activate(): pl.pallas_call(kernel, out_shape=(jax.ShapeDtypeStruct((experts, units, l...  15.5 us
    unnamed x30, local copies, waits for them, and re-layouts  11.3 us
    pallas_call x1, Pallas kernels, attention(): pl.pallas_call(attention_kernel, out_shape=jax.ShapeDtypeStruct((width +...  6.42 us
    pallas_call x2, Pallas kernels, project(): pl.pallas_call(kernel, out_shape=(jax.ShapeDtypeStruct((columns, rows), j...  5.61 us
    pallas_call x1, Pallas kernels, flip(): pl.pallas_call(kernel, out_shape=tuple((jax.ShapeDtypeStruct((width, unit...  4.73 us
  transfers between devices with their start and end apart: 19, of which 9 were waited for; matrix products, arithmetic and copies ran while one was open for 3% of the time, Pallas kernels for 23%

profile of v19, /device:TPU:0, one launch (start us, length us, event | category | flops | bytes accessed | tf_op | source)
XLA Modules:
  0.0 172.6 jit_solution(1900098276311896664)
XLA Ops:
  0.0 1.0 pad_maximum_fusion.2
  1.1 2.4 %collective-permute-start = (bf16[128,512]{1,0:T(8,128)(2,1)S(1)}, bf16[128,512]{1,0:T(8,128)(2,1)S(1)}, u32[]{:S(2)}, u32[]{:S(2)}) collective-permute-start(bf16[128,512]{1,0:T(8,128)(2,1)S(1)} %pad_maximum_fusion.2), channel_id=1, source_target_pairs={{0,1},{1,4},{4,5},{5,8},{8,9},{9,12},{12,13},{2,3},{3,6},{6,7},{7,... | collective-permute-start | bytes 393224 | tf_op jit(solution)/shard_map/ppermute | solution.py:18
  3.5 2.6 %dynamic-slice_bitcast_fusion = bf16[720,1024]{1,0:T(8,128)(2,1)} fusion(bf16[2048,720]{0,1:T(8,128)(2,1)} %param.15, s32[]{:T(128)S(6)} %select_n.95), kind=kLoop, calls=%fused_computation | loop fusion | bytes 2949124 | tf_op jit(solution)/shard_map/dynamic_slice | solution.py:382
  6.1 2.7 %collective-permute-start.3 = (bf16[1440,1440]{1,0:T(8,128)(2,1)}, bf16[1440,1440]{1,0:T(8,128)(2,1)}, u32[]{:S(2)}, u32[]{:S(2)}) collective-permute-start(bf16[1440,1440]{1,0:T(8,128)(2,1)} %bitcast.34), channel_id=1, source_target_pairs={{0,1},{1,0},{2,3},{3,2},{4,5},{5,4},{6,7},{7,6},{8,9},{9,8},{10,11... | collective-permute-start | bytes 12441608 | tf_op jit(solution)/shard_map/ppermute | solution.py:22
  8.8 2.1 %collective-permute-start.2 = (bf16[720,1024]{1,0:T(8,128)(2,1)}, bf16[720,1024]{1,0:T(8,128)(2,1)}, u32[]{:S(2)}, u32[]{:S(2)}) collective-permute-start(bf16[720,1024]{1,0:T(8,128)(2,1)} %dynamic-slice_bitcast_fusion), channel_id=1, source_target_pairs={{0,4},{4,0},{8,12},{12,8},{1,5},{5,1},{9,13},{13,9},{2,6},{6,2},{1... | collective-permute-start | bytes 4423688 | tf_op jit(solution)/shard_map/ppermute | solution.py:22
  11.0 1.1 copy-done.5
  12.1 1.0 copy-done.6
  13.2 6.4 %attention.1.refs_0_ = bf16[2784,128]{1,0:T(8,128)(2,1)} custom-call(s32[2]{0:T(128)S(1)} %pad_add_fusion.1.place_ref, f32[32]{0:T(128)S(1)} %copy-done.11, bf16[128,2048]{1,0:T(8,128)(2,1)S(1)} %copy-done.6, bf16[128,512]{1,0:T(8,128)(2,1)S(1)} %collective-permute-done.earlier_ref, bf16[128,256]{1,0:T(8,128)(2,1)S(1)} %copy-done.8, ...), custom_call_target="tpu_custom_call" | custom-call | flops 268435456 | bytes 1572864 | tf_op jit(solution)/shard_map/attention/pallas_call | solution.py:128
  19.6 2.6 %collective-permute-start.1 = (bf16[2784,128]{1,0:T(8,128)(2,1)}, bf16[2784,128]{1,0:T(8,128)(2,1)}, u32[]{:S(2)}, u32[]{:S(2)}) collective-permute-start(bf16[2784,128]{1,0:T(8,128)(2,1)} %attention.1.refs_0_), channel_id=1, source_target_pairs={{0,8},{4,12},{8,0},{12,4},{1,9},{5,13},{9,1},{13,5},{2,10},{6,14},... | collective-permute-start | bytes 2138120 | tf_op jit(solution)/shard_map/ppermute | solution.py:22
  22.2 0.9 dynamic-slice_bitcast_fusion.1.refs_3_.refs_4_
  23.1 35.1 %collective-permute-done.1.refs_1_ = bf16[2784,128]{1,0:T(8,128)(2,1)} collective-permute-done((bf16[2784,128]{1,0:T(8,128)(2,1)}, bf16[2784,128]{1,0:T(8,128)(2,1)}, u32[]{:S(2)}, u32[]{:S(2)}) %collective-permute-start.1) | collective-permute-done | bytes 712736 | tf_op jit(solution)/shard_map/ppermute | solution.py:22
  58.2 0.8 collective-permute-done.2.refs_2_
  59.3 2.4 %project.2 = (f32[720,128]{1,0:T(8,128)S(1)}, bf16[1,720,128]{2,1,0:T(8,128)(2,1)S(1)}) custom-call(s32[3]{0:T(128)S(1)} %pad_add_fusion.place_ref, bf16[2784,128]{1,0:T(8,128)(2,1)} %attention.1.refs_0_, bf16[2784,128]{1,0:T(8,128)(2,1)} %collective-permute-done.1.refs_1_, bf16[720,2048]{1,0:T(8,128)(2,1)S(1)} %bitcast.33, ...), custom_call_target="tpu_custom_call" | custom-call | flops 754974720 | bytes 2949120 | tf_op jit(solution)/shard_map/project/pallas_call | solution.py:215
  61.7 1.0 collective-permute-done.4.refs_3_
  62.7 3.2 %project.3 = (f32[720,128]{1,0:T(8,128)S(1)}, bf16[1,720,128]{2,1,0:T(8,128)(2,1)S(1)}) custom-call(s32[3]{0:T(128)S(1)} %pad_add_fusion.2.place_ref, bf16[2784,128]{1,0:T(8,128)(2,1)} %attention.1.refs_0_, bf16[2784,128]{1,0:T(8,128)(2,1)} %collective-permute-done.1.refs_1_, bf16[720,1024]{1,0:T(8,128)(2,1)} %collective-permute-done.2.refs_2_, ...), custom_call_target="tpu_custom_call" | custom-call | flops 754974720 | bytes 2949120 | tf_op jit(solution)/shard_map/project/pallas_call | solution.py:215
  66.0 1.6 collective-permute-start.5
  67.6 0.7 slice_select_fusion
  68.3 8.4 %collective-permute-done.5 = bf16[1440,128]{1,0:T(8,128)(2,1)S(1)} collective-permute-done((bf16[1440,128]{1,0:T(8,128)(2,1)S(1)}, bf16[1440,128]{1,0:T(8,128)(2,1)S(1)}, u32[]{:S(2)}, u32[]{:S(2)}) %collective-permute-start.5) | collective-permute-done | bytes 368672 | tf_op jit(solution)/shard_map/ppermute | solution.py:22
  77.0 2.6 %collective-permute-start.6 = (bf16[1456,128]{1,0:T(8,128)(2,1)S(1)}, bf16[1456,128]{1,0:T(8,128)(2,1)S(1)}, u32[]{:S(2)}, u32[]{:S(2)}) collective-permute-start(bf16[1456,128]{1,0:T(8,128)(2,1)S(1)} %pad_maximum_fusion.refs_0_), channel_id=1, source_target_pairs={{0,8},{4,12},{8,0},{12,4},{1,9},{5,13},{9,1},{13,5},{2,10},{6,14},... | collective-permute-start | bytes 1118216 | tf_op jit(solution)/shard_map/ppermute | solution.py:22
  79.7 1.5 collective-permute-start.7
  81.3 1.6 collective-permute-start.10
  82.9 13.0 %collective-permute-done.6.refs_1_ = bf16[1456,128]{1,0:T(8,128)(2,1)S(1)} collective-permute-done((bf16[1456,128]{1,0:T(8,128)(2,1)S(1)}, bf16[1456,128]{1,0:T(8,128)(2,1)S(1)}, u32[]{:S(2)}, u32[]{:S(2)}) %collective-permute-start.6) | collective-permute-done | bytes 372768 | tf_op jit(solution)/shard_map/ppermute | solution.py:22
  96.0 1.4 collective-permute-start.8
  97.4 0.7 collective-permute-start.11
  98.2 3.4 %copy-done.2 = bf16[1,2,2880,720]{2,3,1,0:T(8,128)(2,1)S(1)} copy-done((bf16[1,2,2880,720]{2,3,1,0:T(8,128)(2,1)S(1)}, bf16[1,2,2880,720]{2,3,1,0:T(8,128)(2,1)}, u32[]{:S(2)}) %copy-start.2) | copy-done | bytes 8294424
  101.6 1.6 fetched.1.refs_5_
  103.2 1.4 collective-permute-start.12
  104.7 3.3 %collective-permute-done.11.refs_1_ = bf16[1456,128]{1,0:T(8,128)(2,1)} collective-permute-done((bf16[1456,128]{1,0:T(8,128)(2,1)S(1)}, bf16[1456,128]{1,0:T(8,128)(2,1)}, u32[]{:S(2)}, u32[]{:S(2)}) %collective-permute-start.11) | collective-permute-done | bytes 372768 | tf_op jit(solution)/shard_map/ppermute | solution.py:22
  107.9 0.5 collective-permute-start.13
  108.4 7.4 %activate.2 = (bf16[2,720,256]{2,1,0:T(8,128)(2,1)S(1)}, f32[2,256]{1,0:T(2,128)S(1)}) custom-call(s32[4]{0:T(128)S(1)} %pad_add_fusion.3.place_ref, bf16[1456,128]{1,0:T(8,128)(2,1)S(1)} %pad_maximum_fusion.refs_0_, bf16[1456,128]{1,0:T(8,128)(2,1)S(1)} %collective-permute-done.6.refs_1_, bf16[1456,128]{1,0:T(8,128)(2,1)S(1)} %collective-permute-done.7.refs_2_, ...), custom_call_target="tpu_custom_call" | custom-call | flops 4246732800 | bytes 16588800 | tf_op jit(solution)/shard_map/activate/pallas_call | solution.py:285
  115.8 1.6 collective-permute-start.14
  117.5 3.4 %copy-done.1 = bf16[2,720,2880]{2,1,0:T(8,128)(2,1)S(1)} copy-done((bf16[2,720,2880]{2,1,0:T(8,128)(2,1)S(1)}, bf16[2,720,2880]{2,1,0:T(8,128)(2,1)}, u32[]{:S(2)}) %copy-start.1) | copy-done | bytes 8294424
  121.0 8.1 %activate.3 = (bf16[2,720,256]{2,1,0:T(8,128)(2,1)S(1)}, f32[2,256]{1,0:T(2,128)S(1)}) custom-call(s32[4]{0:T(128)S(1)} %pad_add_fusion.3.place_ref, bf16[1456,128]{1,0:T(8,128)(2,1)S(1)} %collective-permute-done.10.refs_0_, bf16[1456,128]{1,0:T(8,128)(2,1)} %collective-permute-done.11.refs_1_, bf16[1456,128]{1,0:T(8,128)(2,1)} %collective-permute-done.12.refs_2_, ...), custom_call_target="tpu_custom_call" | custom-call | flops 4246732800 | bytes 16588800 | tf_op jit(solution)/shard_map/activate/pallas_call | solution.py:285
  129.1 0.5 collective-permute-start.16
  129.6 2.3 %copy-done.4 = bf16[1,1440,1440]{2,1,0:T(8,128)(2,1)S(1)} copy-done((bf16[1,1440,1440]{2,1,0:T(8,128)(2,1)S(1)}, bf16[1,1440,1440]{2,1,0:T(8,128)(2,1)}, u32[]{:S(2)}) %copy-start.4) | copy-done | bytes 4147224
  131.9 4.7 %flip.1 = (bf16[1440,720]{1,0:T(8,128)(2,1)S(1)}, bf16[1440,720]{1,0:T(8,128)(2,1)S(1)}, bf16[1440,720]{1,0:T(8,128)(2,1)S(1)}, bf16[1440,720]{1,0:T(8,128)(2,1)S(1)}) custom-call(s32[1]{0:T(128)} %bitcast.t_ref, bf16[2,720,1440]{2,1,0:T(8,128)(2,1)S(1)} %bitcast.35, bf16[2,720,1440]{2,1,0:T(8,128)(2,1)} %bitcast.24.refs_1_), custom_call_target="tpu_custom_call" | custom-call | bytes 16588800 | tf_op jit(solution)/shard_map/flip/pallas_call | solution.py:148
  136.6 1.3 own_part.2.part_ref
  137.9 1.4 combine.2
  139.4 3.2 %collective-permute-start.15 = (bf16[1440,128]{1,0:T(8,128)(2,1)S(1)}, bf16[1440,128]{1,0:T(8,128)(2,1)S(1)}, u32[]{:S(2)}, u32[]{:S(2)}) collective-permute-start(bf16[1440,128]{1,0:T(8,128)(2,1)S(1)} %get-tuple-element.72), channel_id=1, source_target_pairs={{0,8},{4,12},{8,0},{12,4},{1,9},{5,13},{9,1},{13,5},{2,10},{6,14},... | collective-permute-start | bytes 1105928 | tf_op jit(solution)/shard_map/ppermute | solution.py:22
  142.6 0.5 add_multiply_fusion
  143.1 1.3 own_part.3.part_ref
  144.4 2.9 %collective-permute-done.16.refs_0_ = bf16[2,720,256]{2,1,0:T(8,128)(2,1)S(1)} collective-permute-done((bf16[2,720,256]{2,1,0:T(8,128)(2,1)S(1)}, bf16[2,720,256]{2,1,0:T(8,128)(2,1)S(1)}, u32[]{:S(2)}, u32[]{:S(2)}) %collective-permute-start.16) | collective-permute-done | bytes 737312 | tf_op jit(solution)/shard_map/ppermute | solution.py:22
  147.3 1.4 combine.3
  148.8 2.5 %collective-permute-start.17 = (bf16[1440,128]{1,0:T(8,128)(2,1)S(1)}, bf16[1440,128]{1,0:T(8,128)(2,1)S(1)}, u32[]{:S(2)}, u32[]{:S(2)}) collective-permute-start(bf16[1440,128]{1,0:T(8,128)(2,1)S(1)} %get-tuple-element.75), channel_id=1, source_target_pairs={{0,4},{4,0},{8,12},{12,8},{1,5},{5,1},{9,13},{13,9},{2,6},{6,2},{1... | collective-permute-start | bytes 1105928 | tf_op jit(solution)/shard_map/ppermute | solution.py:22
  151.2 3.3 %collective-permute-start.18 = (bf16[1440,128]{1,0:T(8,128)(2,1)S(1)}, bf16[1440,128]{1,0:T(8,128)(2,1)S(1)}, u32[]{:S(2)}, u32[]{:S(2)}) collective-permute-start(bf16[1440,128]{1,0:T(8,128)(2,1)S(1)} %get-tuple-element.76), channel_id=1, source_target_pairs={{0,12},{4,8},{8,4},{12,0},{1,13},{5,9},{9,5},{13,1},{2,14},{6,10},... | collective-permute-start | bytes 1105928 | tf_op jit(solution)/shard_map/ppermute | solution.py:22
  154.6 3.8 %collective-permute-done.15 = bf16[1440,128]{1,0:T(8,128)(2,1)S(1)} collective-permute-done((bf16[1440,128]{1,0:T(8,128)(2,1)S(1)}, bf16[1440,128]{1,0:T(8,128)(2,1)S(1)}, u32[]{:S(2)}, u32[]{:S(2)}) %collective-permute-start.15) | collective-permute-done | bytes 368672 | tf_op jit(solution)/shard_map/ppermute | solution.py:22
  158.5 13.2 %collective-permute-done.17 = bf16[1440,128]{1,0:T(8,128)(2,1)S(1)} collective-permute-done((bf16[1440,128]{1,0:T(8,128)(2,1)S(1)}, bf16[1440,128]{1,0:T(8,128)(2,1)S(1)}, u32[]{:S(2)}, u32[]{:S(2)}) %collective-permute-start.17) | collective-permute-done | bytes 368672 | tf_op jit(solution)/shard_map/ppermute | solution.py:22
  171.7 0.9 fusion.2
  (56 shorter events, 1.3 us)
Async XLA Ops:
  0.0 11.0 %copy-start.8 = (bf16[128,256]{1,0:T(8,128)(2,1)S(1)}, bf16[128,256]{1,0:T(8,128)(2,1)}, u32[]{:S(2)}) copy-start(bf16[128,256]{1,0:T(8,128)(2,1)} %k_ref.1) | copy-start | bytes 196612
  0.0 11.0 %copy-start.7 = (bf16[128,256]{1,0:T(8,128)(2,1)S(1)}, bf16[128,256]{1,0:T(8,128)(2,1)}, u32[]{:S(2)}) copy-start(bf16[128,256]{1,0:T(8,128)(2,1)} %v_ref.1) | copy-start | bytes 196612
  0.0 59.3 %copy-start.3 = (bf16[2048,720]{0,1:T(8,128)(2,1)S(1)}, bf16[2048,720]{0,1:T(8,128)(2,1)}, u32[]{:S(2)}) copy-start(bf16[2048,720]{0,1:T(8,128)(2,1)} %param.15) | copy-start | bytes 8847364
  0.0 11.0 %copy-start.9 = (s32[128,4]{0,1:T(4,128)S(1)}, s32[128,4]{0,1:T(4,128)}, u32[]{:S(2)}) copy-start(s32[128,4]{0,1:T(4,128)} %param.20) | copy-start | bytes 6148
  0.0 11.0 %copy-start.10 = (s32[128,4]{0,1:T(4,128)S(1)}, s32[128,4]{0,1:T(4,128)}, u32[]{:S(2)}) copy-start(s32[128,4]{0,1:T(4,128)} %param.21) | copy-start | bytes 6148
  0.0 11.0 %copy-start.11 = (f32[32]{0:T(128)S(1)}, f32[32]{0:T(128)}, u32[]{:S(2)}) copy-start(f32[32]{0:T(128)} %sink_ref.1) | copy-start | bytes 388
  0.0 59.0 %copy-start.14 = (f32[2880]{0:T(1024)S(1)}, f32[2880]{0:T(1024)}, u32[]{:S(2)}) copy-start(f32[2880]{0:T(1024)} %param.17) | copy-start | bytes 34564
  1.1 5.0 %collective-permute-start = (bf16[128,512]{1,0:T(8,128)(2,1)S(1)}, bf16[128,512]{1,0:T(8,128)(2,1)S(1)}, u32[]{:S(2)}, u32[]{:S(2)}) collective-permute-start(bf16[128,512]{1,0:T(8,128)(2,1)S(1)} %pad_maximum_fusion.2), channel_id=1, source_target_pairs={{0,1},{1,4},{4,5},{5,8},{8,9},{9,12},{12,13},{2,3},{3,6},{6,7},{7,... | collective-permute-start | bytes 393224 | tf_op jit(solution)/shard_map/ppermute | solution.py:18
  6.1 53.0 %collective-permute-start.3 = (bf16[1440,1440]{1,0:T(8,128)(2,1)}, bf16[1440,1440]{1,0:T(8,128)(2,1)}, u32[]{:S(2)}, u32[]{:S(2)}) collective-permute-start(bf16[1440,1440]{1,0:T(8,128)(2,1)} %bitcast.34), channel_id=1, source_target_pairs={{0,1},{1,0},{2,3},{3,2},{4,5},{5,4},{6,7},{7,6},{8,9},{9,8},{10,11... | collective-permute-start | bytes 12441608 | tf_op jit(solution)/shard_map/ppermute | solution.py:22
  8.8 99.7 %collective-permute-start.9 = (bf16[2,720,2880]{2,1,0:T(8,128)(2,1)}, bf16[2,720,2880]{2,1,0:T(8,128)(2,1)}, u32[]{:S(2)}, u32[]{:S(2)}) collective-permute-start(bf16[2,720,2880]{2,1,0:T(8,128)(2,1)} %bitcast.31), channel_id=1, source_target_pairs={{0,1},{1,0},{2,3},{3,2},{4,5},{5,4},{6,7},{7,6},{8,9},{9,8},{10,11... | collective-permute-start | bytes 24883208 | tf_op jit(solution)/shard_map/ppermute | solution.py:22
  8.8 50.3 %collective-permute-start.2 = (bf16[720,1024]{1,0:T(8,128)(2,1)}, bf16[720,1024]{1,0:T(8,128)(2,1)}, u32[]{:S(2)}, u32[]{:S(2)}) collective-permute-start(bf16[720,1024]{1,0:T(8,128)(2,1)} %dynamic-slice_bitcast_fusion), channel_id=1, source_target_pairs={{0,4},{4,0},{8,12},{12,8},{1,5},{5,1},{9,13},{13,9},{2,6},{6,2},{1... | collective-permute-start | bytes 4423688 | tf_op jit(solution)/shard_map/ppermute | solution.py:22
  11.0 1.1 copy-start.5
  12.1 1.0 copy-start.6
  19.6 38.6 %collective-permute-start.1 = (bf16[2784,128]{1,0:T(8,128)(2,1)}, bf16[2784,128]{1,0:T(8,128)(2,1)}, u32[]{:S(2)}, u32[]{:S(2)}) collective-permute-start(bf16[2784,128]{1,0:T(8,128)(2,1)} %attention.1.refs_0_), channel_id=1, source_target_pairs={{0,8},{4,12},{8,0},{12,4},{1,9},{5,13},{9,1},{13,5},{2,10},{6,14},... | collective-permute-start | bytes 2138120 | tf_op jit(solution)/shard_map/ppermute | solution.py:22
  59.1 3.6 %collective-permute-start.4 = (bf16[720,1024]{1,0:T(8,128)(2,1)}, bf16[720,1024]{1,0:T(8,128)(2,1)}, u32[]{:S(2)}, u32[]{:S(2)}) collective-permute-start(bf16[720,1024]{1,0:T(8,128)(2,1)} %collective-permute-done.2.refs_2_), channel_id=1, source_target_pairs={{0,1},{1,0},{2,3},{3,2},{4,5},{5,4},{6,7},{7,6},{8,9},{9,8},{10,11... | collective-permute-start | bytes 4423688 | tf_op jit(solution)/shard_map/ppermute | solution.py:22
  66.0 10.7 %collective-permute-start.5 = (bf16[1440,128]{1,0:T(8,128)(2,1)S(1)}, bf16[1440,128]{1,0:T(8,128)(2,1)S(1)}, u32[]{:S(2)}, u32[]{:S(2)}) collective-permute-start(bf16[1440,128]{1,0:T(8,128)(2,1)S(1)} %pad_maximum_fusion.1), channel_id=1, source_target_pairs={{0,2},{2,0},{1,3},{3,1},{4,6},{6,4},{5,7},{7,5},{8,10},{10,8},{9,1... | collective-permute-start | bytes 1105928 | tf_op jit(solution)/shard_map/ppermute | solution.py:22
  77.0 20.4 %copy-start.12 = (bf16[1440,128]{1,0:T(8,128)(2,1)}, bf16[1440,128]{1,0:T(8,128)(2,1)S(1)}, u32[]{:S(2)}) copy-start(bf16[1440,128]{1,0:T(8,128)(2,1)S(1)} %fusion.1) | copy-start | bytes 1105924
  77.0 18.9 %collective-permute-start.6 = (bf16[1456,128]{1,0:T(8,128)(2,1)S(1)}, bf16[1456,128]{1,0:T(8,128)(2,1)S(1)}, u32[]{:S(2)}, u32[]{:S(2)}) collective-permute-start(bf16[1456,128]{1,0:T(8,128)(2,1)S(1)} %pad_maximum_fusion.refs_0_), channel_id=1, source_target_pairs={{0,8},{4,12},{8,0},{12,4},{1,9},{5,13},{9,1},{13,5},{2,10},{6,14},... | collective-permute-start | bytes 1118216 | tf_op jit(solution)/shard_map/ppermute | solution.py:22
  79.7 23.5 %collective-permute-start.7 = (bf16[1456,128]{1,0:T(8,128)(2,1)S(1)}, bf16[1456,128]{1,0:T(8,128)(2,1)S(1)}, u32[]{:S(2)}, u32[]{:S(2)}) collective-permute-start(bf16[1456,128]{1,0:T(8,128)(2,1)S(1)} %pad_maximum_fusion.refs_0_), channel_id=1, source_target_pairs={{0,2},{2,0},{1,3},{3,1},{4,6},{6,4},{5,7},{7,5},{8,10},{10,8},{9,1... | collective-permute-start | bytes 1118216 | tf_op jit(solution)/shard_map/ppermute | solution.py:22
  81.3 21.9 %collective-permute-start.10 = (bf16[1456,128]{1,0:T(8,128)(2,1)S(1)}, bf16[1456,128]{1,0:T(8,128)(2,1)S(1)}, u32[]{:S(2)}, u32[]{:S(2)}) collective-permute-start(bf16[1456,128]{1,0:T(8,128)(2,1)S(1)} %pad_maximum_fusion.refs_0_), channel_id=1, source_target_pairs={{0,4},{4,0},{8,12},{12,8},{1,5},{5,1},{9,13},{13,9},{2,6},{6,2},{1... | collective-permute-start | bytes 1118216 | tf_op jit(solution)/shard_map/ppermute | solution.py:22
  96.0 12.5 %collective-permute-start.8 = (bf16[1456,128]{1,0:T(8,128)(2,1)S(1)}, bf16[1456,128]{1,0:T(8,128)(2,1)S(1)}, u32[]{:S(2)}, u32[]{:S(2)}) collective-permute-start(bf16[1456,128]{1,0:T(8,128)(2,1)S(1)} %collective-permute-done.6.refs_1_), channel_id=1, source_target_pairs={{0,2},{2,0},{1,3},{3,1},{4,6},{6,4},{5,7},{7,5},{8,10},{10,8},{9,1... | collective-permute-start | bytes 1118216 | tf_op jit(solution)/shard_map/ppermute | solution.py:22
  97.4 10.6 %collective-permute-start.11 = (bf16[1456,128]{1,0:T(8,128)(2,1)S(1)}, bf16[1456,128]{1,0:T(8,128)(2,1)}, u32[]{:S(2)}, u32[]{:S(2)}) collective-permute-start(bf16[1456,128]{1,0:T(8,128)(2,1)S(1)} %collective-permute-done.6.refs_1_), channel_id=1, source_target_pairs={{0,4},{4,0},{8,12},{12,8},{1,5},{5,1},{9,13},{13,9},{2,6},{6,2},{1... | collective-permute-start | bytes 1118216 | tf_op jit(solution)/shard_map/ppermute | solution.py:22
  98.2 3.4 %copy-start.2 = (bf16[1,2,2880,720]{2,3,1,0:T(8,128)(2,1)S(1)}, bf16[1,2,2880,720]{2,3,1,0:T(8,128)(2,1)}, u32[]{:S(2)}) copy-start(bf16[1,2,2880,720]{2,3,1,0:T(8,128)(2,1)} %param.18) | copy-start | bytes 24883204
  103.2 12.6 %copy-start = (bf16[2,720,2880]{2,1,0:T(8,128)(2,1)}, bf16[2,720,2880]{2,1,0:T(8,128)(2,1)S(1)}, u32[]{:S(2)}) copy-start(bf16[2,720,2880]{2,1,0:T(8,128)(2,1)S(1)} %fetched.1.refs_5_) | copy-start | bytes 24883204
  103.2 14.3 %collective-permute-start.12 = (bf16[1456,128]{1,0:T(8,128)(2,1)S(1)}, bf16[1456,128]{1,0:T(8,128)(2,1)}, u32[]{:S(2)}, u32[]{:S(2)}) collective-permute-start(bf16[1456,128]{1,0:T(8,128)(2,1)S(1)} %collective-permute-done.7.refs_2_), channel_id=1, source_target_pairs={{0,4},{4,0},{8,12},{12,8},{1,5},{5,1},{9,13},{13,9},{2,6},{6,2},{1... | collective-permute-start | bytes 1118216 | tf_op jit(solution)/shard_map/ppermute | solution.py:22
  107.9 9.6 %collective-permute-start.13 = (bf16[1456,128]{1,0:T(8,128)(2,1)}, bf16[1456,128]{1,0:T(8,128)(2,1)}, u32[]{:S(2)}, u32[]{:S(2)}) collective-permute-start(bf16[1456,128]{1,0:T(8,128)(2,1)} %collective-permute-done.11.refs_1_), channel_id=1, source_target_pairs={{0,2},{2,0},{1,3},{3,1},{4,6},{6,4},{5,7},{7,5},{8,10},{10,8},{9,1... | collective-permute-start | bytes 1118216 | tf_op jit(solution)/shard_map/ppermute | solution.py:22
  115.8 22.1 %collective-permute-start.14 = (bf16[2,720,256]{2,1,0:T(8,128)(2,1)S(1)}, bf16[2,720,256]{2,1,0:T(8,128)(2,1)S(1)}, u32[]{:S(2)}, u32[]{:S(2)}) collective-permute-start(bf16[2,720,256]{2,1,0:T(8,128)(2,1)S(1)} %get-tuple-element.55.activated_ref), channel_id=1, source_target_pairs={{0,2},{2,0},{1,3},{3,1},{4,6},{6,4},{5,7},{7,5},{8,10},{10,8},{9,1... | collective-permute-start | bytes 2211848 | tf_op jit(solution)/shard_map/ppermute | solution.py:22
  117.5 3.4 %copy-start.1 = (bf16[2,720,2880]{2,1,0:T(8,128)(2,1)S(1)}, bf16[2,720,2880]{2,1,0:T(8,128)(2,1)}, u32[]{:S(2)}) copy-start(bf16[2,720,2880]{2,1,0:T(8,128)(2,1)} %copy-done) | copy-start | bytes 24883204
  129.1 18.3 %collective-permute-start.16 = (bf16[2,720,256]{2,1,0:T(8,128)(2,1)S(1)}, bf16[2,720,256]{2,1,0:T(8,128)(2,1)S(1)}, u32[]{:S(2)}, u32[]{:S(2)}) collective-permute-start(bf16[2,720,256]{2,1,0:T(8,128)(2,1)S(1)} %get-tuple-element.73.activated_ref), channel_id=1, source_target_pairs={{0,2},{2,0},{1,3},{3,1},{4,6},{6,4},{5,7},{7,5},{8,10},{10,8},{9,1... | collective-permute-start | bytes 2211848 | tf_op jit(solution)/shard_map/ppermute | solution.py:22
  129.6 2.3 %copy-start.4 = (bf16[1,1440,1440]{2,1,0:T(8,128)(2,1)S(1)}, bf16[1,1440,1440]{2,1,0:T(8,128)(2,1)}, u32[]{:S(2)}) copy-start(bf16[1,1440,1440]{2,1,0:T(8,128)(2,1)} %param.19) | copy-start | bytes 12441604
  137.9 4.7 %copy-start.13 = (bf16[1440,128]{1,0:T(8,128)(2,1)S(1)}, bf16[1440,128]{1,0:T(8,128)(2,1)}, u32[]{:S(2)}) copy-start(bf16[1440,128]{1,0:T(8,128)(2,1)} %copy-done.12) | copy-start | bytes 1105924
  139.4 19.0 %collective-permute-start.15 = (bf16[1440,128]{1,0:T(8,128)(2,1)S(1)}, bf16[1440,128]{1,0:T(8,128)(2,1)S(1)}, u32[]{:S(2)}, u32[]{:S(2)}) collective-permute-start(bf16[1440,128]{1,0:T(8,128)(2,1)S(1)} %get-tuple-element.72), channel_id=1, source_target_pairs={{0,8},{4,12},{8,0},{12,4},{1,9},{5,13},{9,1},{13,5},{2,10},{6,14},... | collective-permute-start | bytes 1105928 | tf_op jit(solution)/shard_map/ppermute | solution.py:22
  148.8 22.9 %collective-permute-start.17 = (bf16[1440,128]{1,0:T(8,128)(2,1)S(1)}, bf16[1440,128]{1,0:T(8,128)(2,1)S(1)}, u32[]{:S(2)}, u32[]{:S(2)}) collective-permute-start(bf16[1440,128]{1,0:T(8,128)(2,1)S(1)} %get-tuple-element.75), channel_id=1, source_target_pairs={{0,4},{4,0},{8,12},{12,8},{1,5},{5,1},{9,13},{13,9},{2,6},{6,2},{1... | collective-permute-start | bytes 1105928 | tf_op jit(solution)/shard_map/ppermute | solution.py:22
  151.2 20.5 %collective-permute-start.18 = (bf16[1440,128]{1,0:T(8,128)(2,1)S(1)}, bf16[1440,128]{1,0:T(8,128)(2,1)S(1)}, u32[]{:S(2)}, u32[]{:S(2)}) collective-permute-start(bf16[1440,128]{1,0:T(8,128)(2,1)S(1)} %get-tuple-element.76), channel_id=1, source_target_pairs={{0,12},{4,8},{8,4},{12,0},{1,13},{5,9},{9,5},{13,1},{2,14},{6,10},... | collective-permute-start | bytes 1105928 | tf_op jit(solution)/shard_map/ppermute | solution.py:22
